TPU v7x, 32 devices: a whole 2x2x4 slice. The times are simulated.
32 devices in a mesh: shots: 2 (over x), xline: 8 (over z, y), inline: 2 (over core).
Axes of the slice: x: 2, y: 2, z: 4, core: 2. Of those that a mesh axis runs over, the one named last changes fastest.
Arguments:
- fwd_now: float32 [128, 64, 256], P(('shots', 'inline'), 'xline'), parts along dimension 0, may hold values from -6 to 6
- fwd_before: float32 [128, 64, 256], P(('shots', 'inline'), 'xline'), parts along dimension 0, may hold values from -6 to 6
- adj_now: float32 [128, 64, 256], P(('shots', 'inline'), 'xline'), parts along dimension 0, may hold values from -6 to 6
- adj_before: float32 [128, 64, 256], P(('shots', 'inline'), 'xline'), parts along dimension 0, may hold values from -6 to 6
- velocity: float32 [64, 64, 256], P('inline', 'xline'), may hold values from 0.2 to 0.4
- log_density: float32 [64, 64, 256], P('inline', 'xline'), may hold values from -0.3 to 0.3
- observed: float32 [16, 2048], P('shots', ('xline', 'inline')), parts along dimension 0, may hold values from -48 to 48
- rec_cells: int32 [16, 128], P(('xline', 'inline')), may hold values from 0 to 65535
- rec_counts: int32 [16, 16], P(('xline', 'inline')), may hold values from 0 to 8, as said below
- src_cell: int32 [32], P('shots'), parts along dimension 0, may hold values from 0 to 1048575
- wavelet: float32 [16, 16], P('shots'), parts along dimension 0, may hold values from -144 to 144
Outputs:
- gradient: float32 [512, 64, 64], P(('shots', 'xline'), 'inline'), parts along dimension 0
- adjoint_state: float32 [128, 64, 256], P(('shots', 'inline'), 'xline'), parts along dimension 0
- adjoint_previous: float32 [128, 64, 256], P(('shots', 'inline'), 'xline'), parts along dimension 0
There are 2 independent parts, one for each index of `shots`. A program takes and returns all parts, laid end to end along the dimension named above; an argument that names none is the same for every part. Nothing has to cross between parts.
Inputs may be any that keep to these rules, and one draw needn't show every extreme that they name: rec_counts[o, s] live slots of the 8 that device s sends to subdomain o; in every draw one subdomain receives 8 live slots from every device.
All inputs are finite; a program needn't handle non-finite values.
Results may differ from a plain program's by a relative error of at most 0.04.
Values sent between devices are 32-bit elements; how exact they have to be, the bound alone decides.
No kernel may reach another device: no remote copies, remote signals or barrier semaphores. Data moves between devices by JAX's collectives and lax.ppermute only.
A program may use at most 64 MiB of HBM per device.

v0:
```python
import functools

import jax
import jax.numpy as jnp
import numpy as np
from jax import lax
from jax.experimental import pallas as pl
from jax.experimental.pallas import tpu as pltpu
from jax.sharding import PartitionSpec as P

CAP = 8
SMOOTH = 16
SECOND = (-205.0 / 72.0, 8.0 / 5.0, -1.0 / 5.0, 8.0 / 315.0, -1.0 / 560.0)
FIRST = (4.0 / 5.0, -1.0 / 5.0, 4.0 / 105.0, -1.0 / 280.0)
ALL = ("shots", "xline", "inline")
F32 = jnp.float32
BF16 = jnp.bfloat16


class Plan:
    def __init__(self, mesh):
        self.shots = mesh.shape["shots"]
        self.nx = mesh.shape["xline"]
        self.nq = self.nx // 2

    def index(self, s, q, y, c):
        return (s * self.nx + 2 * q + y) * 2 + c

    def perm(self, partner):
        pairs = []
        for s in range(self.shots):
            for q in range(self.nq):
                for y in range(2):
                    for c in range(2):
                        t = partner(q, y, c)
                        dst = self.index(s ^ 1, q, y, c) if t is None else self.index(s, *t)
                        pairs.append((self.index(s, q, y, c), dst))
        return pairs

    def swap(self):
        return self.perm(lambda q, y, c: None if y == c else (q, c, y))

    def z(self):
        def partner(q, y, c):
            other = q + 1 if c == 1 else q - 1
            return (other, y, 1 - c) if 0 <= other < self.nq else None

        return self.perm(partner)

    def core(self):
        return self.perm(lambda q, y, c: (q, y, 1 - c))

    def y(self):
        return self.perm(lambda q, y, c: (q, 1 - y, c))

    def spread(self, shift):
        return self.perm(lambda q, y, c: ((q + shift) % self.nq, c, y))


def send(value, pairs):
    return lax.ppermute(value, ALL, pairs)


def depth_matrix(n):
    m = np.zeros((n, 2 * n), np.float32)
    for k in range(1, 5):
        for j in range(n):
            for i, sign in ((j + k, 1.0), (j - k, -1.0)):
                if 0 <= i < n:
                    m[i, j] = round(SECOND[k] * 5040)
                    m[i, n + j] = sign * round(FIRST[k - 1] * 840)
    return m


def split(value):
    high = value.astype(BF16)
    return high, (value - high.astype(F32)).astype(BF16)


def mm(a, b):
    return jnp.dot(a, b, preferred_element_type=F32)


def fill(flags, cur, zm, cm, ym, g):
    rows, cols, depth = cur.shape
    c, y, inside = flags[0], flags[1], flags[2]
    from_z = jnp.where(inside == 1, zm[...], 0.0)
    from_c = cm[...]
    low = jnp.where(c == 0, from_z, from_c)
    high = jnp.where(c == 0, from_c, from_z)
    edge = ym[...]
    top = jnp.where(y == 1, edge, 0.0)
    bottom = jnp.where(y == 0, edge, 0.0)
    own = cur[...]
    for h in range(depth // 128):
        lanes = slice(h * 128, h * 128 + 128)
        g[h, 4 : 4 + rows, 0:4, :] = low[:, :, lanes]
        g[h, 4 : 4 + rows, 4 : 4 + cols, :] = own[:, :, lanes]
        g[h, 4 : 4 + rows, 4 + cols : 8 + cols, :] = high[:, :, lanes]
        g[h, 0:4, 4 : 4 + cols, :] = top[:, :, lanes]
        g[h, 4 + rows : 8 + rows, 4 : 4 + cols, :] = bottom[:, :, lanes]


def depth_part(cur, mat, zz):
    rows, cols, depth = cur.shape
    high, low = split(cur[...].reshape(rows * cols, depth))
    zz[...] = mm(high, mat[...]) + mm(low, mat[...])


def stencil(g, zz, depth, cols, h, r):
    def at(di, dx):
        return g[h, r + 4 + di, 4 + dx : 4 + dx + cols, :]

    row = pl.ds(pl.multiple_of(r * cols, cols), cols)
    center = at(0, 0)
    lap = 3.0 * SECOND[0] * center + zz[row, h * 128 : h * 128 + 128] * (1.0 / 5040)
    slope_z = zz[row, depth + h * 128 : depth + h * 128 + 128] * (1.0 / 840)
    slope_i = slope_x = None
    for k in range(1, 5):
        pi, mi, px, mx = at(k, 0), at(-k, 0), at(0, k), at(0, -k)
        lap = lap + SECOND[k] * ((pi + mi) + (px + mx))
        si, sx = FIRST[k - 1] * (pi - mi), FIRST[k - 1] * (px - mx)
        slope_i = si if slope_i is None else slope_i + si
        slope_x = sx if slope_x is None else slope_x + sx
    return center, lap, slope_i, slope_x, slope_z


def rims(flags, new, zo, co, yo):
    rows, cols, depth = new.shape
    c, y = flags[0], flags[1]
    first, last = new[:, 0:4, :], new[:, cols - 4 : cols, :]
    zo[...] = jnp.where(c == 0, first, last)
    co[...] = jnp.where(c == 0, last, first)
    yo[...] = jnp.where(y == 0, new[rows - 4 : rows], new[0:4])


def settle_kernel(flags, a, b, recv, a_out, b_out, zo, co, yo):
    keep = flags[0] == flags[1]
    for n, (own, out) in enumerate(((a, a_out), (b, b_out))):
        out[...] = jnp.where(keep, own[...], recv[n])
        rims(flags, out, zo.at[n], co.at[n], yo.at[n])


def slope_kernel(flags, lr, zm, cm, ym, mat, gi, gx, gz, g, zz):
    rows, cols, depth = lr.shape
    fill(flags, lr, zm.at[0], cm.at[0], ym.at[0], g)
    depth_part(lr, mat, zz)

    def body(r, carry):
        for h in range(depth // 128):
            lanes = slice(h * 128, h * 128 + 128)
            spare, lap, si, sx, sz = stencil(g, zz, depth, cols, h, r)
            gi[r, :, lanes] = si
            gx[r, :, lanes] = sx
            gz[r, :, lanes] = sz
        return carry

    lax.fori_loop(0, rows, body, 0, unroll=2)


def advance(cur, prev, vel, gi, gx, gz, g, zz, inj, finish):
    rows, cols, depth = cur.shape

    def body(r, carry):
        row = pl.ds(pl.multiple_of(r * cols, cols), cols)
        for h in range(depth // 128):
            lanes = slice(h * 128, h * 128 + 128)
            center, lap, si, sx, sz = stencil(g, zz, depth, cols, h, r)
            coupling = gi[r, :, lanes] * si + gx[r, :, lanes] * sx + gz[r, :, lanes] * sz
            v = vel[r, :, lanes]
            change = (v * v) * (lap - coupling) + inj[row, lanes]
            finish(r, lanes, 2.0 * center - prev[r, :, lanes] + change, change, v)
        return carry

    lax.fori_loop(0, rows, body, 0, unroll=2)


def forward_kernel(step, flags, cur, prev, vel, gi, gx, gz, zm, cm, ym, mat, srow, sz, wave,
                   new, change_out, zo, co, yo, g, zz, inj):
    rows, cols, depth = cur.shape
    fill(flags, cur, zm, cm, ym, g)
    depth_part(cur, mat, zz)
    n = srow.shape[1]
    spot = lax.broadcasted_iota(jnp.int32, (rows * cols, n), 0) == srow[...]
    spot = spot.astype(F32).astype(BF16)
    high, low = split(jnp.where(
        lax.broadcasted_iota(jnp.int32, (n, depth), 1) == sz[...], wave[:, step : step + 1], 0.0))
    inj[...] = mm(spot, high) + mm(spot, low)

    def finish(r, lanes, value, change, v):
        new[r, :, lanes] = value
        change_out[r, :, lanes] = change

    advance(cur, prev, vel, gi, gx, gz, g, zz, inj, finish)
    rims(flags, new, zo, co, yo)


def adjoint_kernel(t, last, flags, cur, prev, vel, gi, gx, gz, zm, cm, ym, mat, pnext, change_in,
                   image, rrow, rrow_c, rz, obs, new, image_out, *rest):
    rows, cols, depth = cur.shape
    g, zz, inj = rest[-3:]
    fill(flags, cur, zm, cm, ym, g)
    depth_part(cur, mat, zz)
    n = rrow.shape[1]
    spot = lax.broadcasted_iota(jnp.int32, (rows * cols, n), 0) == rrow[...]
    spot = spot.astype(F32).astype(BF16)
    pick = lax.broadcasted_iota(jnp.int32, (n, rows * cols), 1) == rrow_c[...]
    pick = pick.astype(F32).astype(BF16)
    high, low = split(pnext[...].reshape(rows * cols, depth))
    deep = lax.broadcasted_iota(jnp.int32, (n, depth), 1) == rz[...]
    seen = jnp.where(deep, mm(pick, high) + mm(pick, low), 0.0)
    residual = jnp.sum(seen, axis=1, keepdims=True) - obs[:, t : t + 1]
    high, low = split(jnp.where(deep, residual, 0.0))
    inj[...] = mm(spot, high) + mm(spot, low)
    scale = 2.0 / obs.shape[1]

    def finish(r, lanes, value, change, v):
        new[r, :, lanes] = value
        total = value * change_in[r, :, lanes]
        if image is not None:
            total = total + image[r, :, lanes]
        if last:
            total = total * scale / v
        image_out[r, :, lanes] = total

    advance(cur, prev, vel, gi, gx, gz, g, zz, inj, finish)
    if not last:
        rims(flags, new, *rest[:3])


def first_adjoint_kernel(t, last, *refs):
    adjoint_kernel(t, last, *refs[:13], None, *refs[13:])


def shaped(*shape):
    return jax.ShapeDtypeStruct(shape, F32)


def call(kernel, name, outs, scratch, *args):
    specs = [pl.BlockSpec(memory_space=pltpu.SMEM)]
    specs += [pl.BlockSpec(memory_space=pltpu.VMEM)] * (len(args) - 1)
    return pl.pallas_call(
        kernel,
        name=name,
        out_shape=outs,
        in_specs=specs,
        out_specs=[pl.BlockSpec(memory_space=pltpu.VMEM)] * len(outs),
        scratch_shapes=scratch,
        compiler_params=pltpu.CompilerParams(vmem_limit_bytes=16 * 1024 * 1024),
        cost_estimate=pl.CostEstimate(flops=5_000_000, bytes_accessed=2_000_000, transcendentals=0),
    )(*args)


def per_device(plan, fwd_now, fwd_before, adj_now, adj_before, velocity, log_density, observed,
               rec_cells, rec_counts, src_cell, wavelet):
    block = fwd_now.shape
    rows, cols, depth = block
    steps = wavelet.shape[0]
    nx, nq = plan.nx, plan.nq
    subs = 2 * nx
    xline, c = lax.axis_index("xline"), lax.axis_index("inline")
    q, y = xline // 2, xline % 2
    z_perm, c_perm, y_perm, swap_perm = plan.z(), plan.core(), plan.y(), plan.swap()
    inside = jnp.where(c == 0, q > 0, q < nq - 1).astype(jnp.int32)
    flags = jnp.stack([c, y, inside]).astype(jnp.int32)
    mat = jnp.asarray(depth_matrix(depth), BF16)
    rims_of = [shaped(rows, 4, depth), shaped(rows, 4, depth), shaped(4, cols, depth)]
    pair_rims = [shaped(2, rows, 4, depth), shaped(2, rows, 4, depth), shaped(2, 4, cols, depth)]
    scratch = [
        pltpu.VMEM((depth // 128, rows + 8, cols + 8, 128), F32),
        pltpu.VMEM((rows * cols, 2 * depth), F32),
    ]
    full_scratch = scratch + [pltpu.VMEM((rows * cols, depth), F32)]

    def halo(zo, co, yo):
        return send(zo, z_perm), send(co, c_perm), send(yo, y_perm)

    live = jnp.arange(CAP)[None, :] < rec_counts[0][:, None]
    cells = jnp.where(live.reshape(-1), rec_cells[0], -1)
    packed = jnp.concatenate([observed, cells[None, :].astype(F32)], axis=0)
    gathered = lax.all_gather(packed, ("xline", "inline"))

    first = send(jnp.stack([log_density, fwd_now]), swap_perm)
    second = send(jnp.stack([velocity, fwd_before]), swap_perm)
    third = send(jnp.stack([adj_now, adj_before]), swap_perm)
    settle = functools.partial(call, settle_kernel, "settle", [shaped(*block)] * 2 + pair_rims, [])
    density, p_now, zo, co, yo = settle(flags, log_density, fwd_now, first)
    zm, cm, ym = halo(zo, co, yo)
    keep = y == c
    vel = jnp.where(keep, velocity, second[0])
    p_before = jnp.where(keep, fwd_before, second[1])
    u_now, u_before, zo, co, yo = settle(flags, adj_now, adj_before, third)
    u_halo = halo(zo[0], co[0], yo[0])

    gi, gx, gz = call(slope_kernel, "slopes", [shaped(*block)] * 3, scratch,
                      flags, density, zm, cm, ym, mat)

    plane = nx * cols * depth
    src_i = src_cell // plane - y * rows
    src_x = src_cell // depth % (nx * cols) - (2 * q + c) * cols
    ok = (src_i >= 0) & (src_i < rows) & (src_x >= 0) & (src_x < cols)
    srow = jnp.where(ok, src_i * cols + src_x, -1)[None, :]
    sz = (src_cell % depth)[:, None]
    wave = wavelet.T

    model = (vel, gi, gx, gz)
    halos = (zm[1], cm[1], ym[1])
    states, changes = [], []
    for t in range(steps):
        p_next, change, zo, co, yo = call(
            functools.partial(forward_kernel, t), "forward",
            [shaped(*block)] * 2 + rims_of, full_scratch,
            flags, p_now, p_before, *model, *halos, mat, srow, sz, wave)
        if t < steps - 1:
            halos = halo(zo, co, yo)
        p_before, p_now = p_now, p_next
        states.append(p_next)
        changes.append(change)

    sub = (2 * q + c) * 2 + y
    mine = lax.dynamic_index_in_dim(gathered, sub, 0, keepdims=False)[steps].astype(jnp.int32)
    traces = gathered[:, :steps].reshape(subs, steps, subs, CAP)
    traces = lax.dynamic_index_in_dim(traces, sub, 2, keepdims=False)
    obs = traces.transpose(0, 2, 1).reshape(subs * CAP, steps)
    rrow = jnp.where(mine < 0, -1, mine // depth)
    rz = (mine % depth)[:, None]

    halos = u_halo
    image = []
    for j in range(steps):
        t = steps - 1 - j
        last = j == steps - 1
        kernel = functools.partial(adjoint_kernel if image else first_adjoint_kernel, t, last)
        outs = call(
            kernel, "adjoint",
            [shaped(*block)] * 2 + ([] if last else rims_of), full_scratch,
            flags, u_now, u_before, *model, *halos, mat, states[t], changes[t], *image,
            rrow[None, :], rrow[:, None], rz, obs)
        u_before, u_now = u_now, outs[0]
        image = [outs[1]]
        if not last:
            halos = halo(*outs[2:])

    chunk = depth // nx
    raw = image[0].reshape(rows * cols, depth).T.reshape(nq, 2, chunk, rows * cols)
    own = lax.dynamic_index_in_dim(raw, c, 1, keepdims=False)
    other = send(lax.dynamic_index_in_dim(raw, 1 - c, 1, keepdims=False), c_perm)
    both = jnp.where(c == 0, jnp.stack([own, other], 1), jnp.stack([other, own], 1))
    pieces = [
        send(lax.dynamic_index_in_dim(both, (q + s) % nq, 0, keepdims=False), plan.spread(s))
        for s in range(nq)
    ]
    adj_out = send(u_now, swap_perm)
    adj_prev = send(u_before, swap_perm)
    adj_out = jnp.where(keep, u_now, adj_out)
    adj_prev = jnp.where(keep, u_before, adj_prev)

    pieces = jnp.stack(pieces).reshape(2 * nq, chunk, rows, cols)
    lines = jnp.arange(nx * cols)
    from_q = (q - jnp.arange(nq)) % nq
    places = (from_q[:, None] * (2 * cols) + jnp.arange(2 * cols)[None, :]).reshape(-1)
    weights = jnp.exp(-jnp.abs(lines[:, None] - places[None, :]).astype(F32) / SMOOTH)
    weights = weights / jnp.sum(weights, axis=1, keepdims=True)
    gradient = jnp.einsum("jzix,yjx->ziy", pieces, weights.reshape(-1, 2 * nq, cols),
                          precision=lax.Precision.HIGHEST)
    return gradient, adj_out, adj_prev


def solution(mesh):
    field = P(("shots", "inline"), "xline", None)
    model = P("inline", "xline", None)
    lists = P(("xline", "inline"), None)
    return jax.shard_map(
        functools.partial(per_device, Plan(mesh)),
        mesh=mesh,
        in_specs=(field, field, field, field, model, model, P("shots", ("xline", "inline")),
                  lists, lists, P("shots"), P("shots", None)),
        out_specs=(P(("shots", "xline"), "inline", None), field, field),
        check_vma=False,
    )
```

profile of v0, /device:TPU:1, one launch (start us, length us, event | category | flops | bytes accessed | tf_op | source)
XLA Modules:
  0.0 191.4 jit_solution(16670770514656430994)
XLA Ops:
  1.8 2.7 %collective-permute-start.2 = (f32[2,32,8,256]{3,2,1,0:T(8,128)S(1)}, f32[2,32,8,256]{3,2,1,0:T(8,128)S(1)}, u32[]{:S(2)}, u32[]{:S(2)}) collective-permute-start(f32[2,32,8,256]{3,2,1,0:T(8,128)S(1)} %pad_maximum_fusion.2), channel_id=1, source_target_pairs={{0,16},{1,2},{2,1},{3,19},{4,20},{5,6},{6,5},{7,23},{8,24},{9,10},... | collective-permute-start | bytes 1572872 | tf_op jit(solution)/shard_map/ppermute | solution.py:61
  6.5 1.4 collective-permute-start
  9.4 2.3 %collective-permute-done.2.recv = f32[2,32,8,256]{3,2,1,0:T(8,128)S(1)} collective-permute-done((f32[2,32,8,256]{3,2,1,0:T(8,128)S(1)}, f32[2,32,8,256]{3,2,1,0:T(8,128)S(1)}, u32[]{:S(2)}, u32[]{:S(2)}) %collective-permute-start.2) | collective-permute-done | bytes 524320 | tf_op jit(solution)/shard_map/ppermute | solution.py:61
  12.5 2.0 %collective-permute-start.3 = (f32[2,32,4,256]{3,2,1,0:T(4,128)S(1)}, f32[2,32,4,256]{3,2,1,0:T(4,128)S(1)}, u32[]{:S(2)}, u32[]{:S(2)}) collective-permute-start(f32[2,32,4,256]{3,2,1,0:T(4,128)S(1)} %get-tuple-element.93), channel_id=1, source_target_pairs={{0,16},{1,4},{2,18},{3,6},{4,1},{5,8},{6,3},{7,10},{8,5},{9,12},{1... | collective-permute-start | bytes 786440 | tf_op jit(solution)/shard_map/ppermute | solution.py:61
  15.5 1.8 collective-permute-done.1
  18.5 4.8 %collective-permute-done.5.ym = f32[2,4,8,256]{3,2,1,0:T(8,128)S(1)} collective-permute-done((f32[2,4,8,256]{3,2,1,0:T(8,128)S(1)}, f32[2,4,8,256]{3,2,1,0:T(8,128)S(1)}, u32[]{:S(2)}, u32[]{:S(2)}) %collective-permute-start.5) | collective-permute-done | bytes 65568 | tf_op jit(solution)/shard_map/ppermute | solution.py:61
  25.4 1.7 forward.8
  27.9 1.9 collective-permute-start.10
  31.7 1.9 collective-permute-done.11.ym
  34.3 2.4 %forward.9 = (f32[32,8,256]{2,1,0:T(8,128)S(1)}, f32[32,8,256]{2,1,0:T(8,128)S(1)}, f32[32,4,256]{2,1,0:T(4,128)}, f32[32,4,256]{2,1,0:T(4,128)S(1)}, f32[4,8,256]{2,1,0:T(8,128)S(1)}) custom-call(s32[3]{0:T(128)S(1)} %pad_add_fusion.flags.refs_0_, f32[32,8,256]{2,1,0:T(8,128)S(1)} %get-tuple-element.103.cur.prev.pnext, ...), custom_call_target="tpu_custom_call" | custom-call | flops 5000000 | bytes 2000000 | tf_op jit(solution)/shard_map/forward/pallas_call | solution.py:242
  37.9 1.2 collective-permute-start.13
  39.2 3.0 %collective-permute-done.14.ym = f32[4,8,256]{2,1,0:T(8,128)S(1)} collective-permute-done((f32[4,8,256]{2,1,0:T(8,128)S(1)}, f32[4,8,256]{2,1,0:T(8,128)S(1)}, u32[]{:S(2)}, u32[]{:S(2)}) %collective-permute-start.14) | collective-permute-done | bytes 32800 | tf_op jit(solution)/shard_map/ppermute | solution.py:61
  42.2 2.4 %forward.10 = (f32[32,8,256]{2,1,0:T(8,128)S(1)}, f32[32,8,256]{2,1,0:T(8,128)S(1)}, f32[32,4,256]{2,1,0:T(4,128)}, f32[32,4,256]{2,1,0:T(4,128)}, f32[4,8,256]{2,1,0:T(8,128)S(1)}) custom-call(s32[3]{0:T(128)S(1)} %pad_add_fusion.flags.refs_0_, f32[32,8,256]{2,1,0:T(8,128)S(1)} %get-tuple-element.107.cur.prev.pnext, ...), custom_call_target="tpu_custom_call" | custom-call | flops 5000000 | bytes 2000000 | tf_op jit(solution)/shard_map/forward/pallas_call | solution.py:242
  46.7 20.2 %all-gather.1 = f32[16,9,128]{2,1,0:T(8,128)} all-gather(f32[1,9,128]{2,1,0:T(8,128)S(1)} %maximum_bitcast_fusion), channel_id=2, replica_groups=mesh['shots'=2,'xline'=8,'inline'=2] {'xline','inline'}, dimensions={0}, use_global_device_ids=true | all-gather | bytes 78336 | tf_op jit(solution)/shard_map/all_gather | solution.py:281
  69.7 2.4 %forward.11 = (f32[32,8,256]{2,1,0:T(8,128)S(1)}, f32[32,8,256]{2,1,0:T(8,128)S(1)}, f32[32,4,256]{2,1,0:T(4,128)}, f32[32,4,256]{2,1,0:T(4,128)}, f32[4,8,256]{2,1,0:T(8,128)S(1)}) custom-call(s32[3]{0:T(128)S(1)} %pad_add_fusion.flags.refs_0_, f32[32,8,256]{2,1,0:T(8,128)S(1)} %get-tuple-element.111.cur.prev.pnext, ...), custom_call_target="tpu_custom_call" | custom-call | flops 5000000 | bytes 2000000 | tf_op jit(solution)/shard_map/forward/pallas_call | solution.py:242
  72.8 2.3 %collective-permute-start.19 = (f32[32,4,256]{2,1,0:T(4,128)}, f32[32,4,256]{2,1,0:T(4,128)}, u32[]{:S(2)}, u32[]{:S(2)}) collective-permute-start(f32[32,4,256]{2,1,0:T(4,128)} %get-tuple-element.117), channel_id=1, source_target_pairs={{0,1},{1,0},{2,3},{3,2},{4,5},{5,4},{6,7},{7,6},{8,9},{9,8},{10,11... | collective-permute-start | bytes 393224 | tf_op jit(solution)/shard_map/ppermute | solution.py:61
  75.2 1.5 slice.46
  76.7 1.8 copy.99
  78.9 1.4 dynamic-slice_bitcast_fusion.5
  80.3 1.3 settle.2
  81.6 2.2 %forward.12 = (f32[32,8,256]{2,1,0:T(8,128)S(1)}, f32[32,8,256]{2,1,0:T(8,128)S(1)}, f32[32,4,256]{2,1,0:T(4,128)S(1)}, f32[32,4,256]{2,1,0:T(4,128)S(1)}, f32[4,8,256]{2,1,0:T(8,128)S(1)}) custom-call(s32[3]{0:T(128)S(1)} %pad_add_fusion.flags.refs_0_, f32[32,8,256]{2,1,0:T(8,128)S(1)} %get-tuple-element.115.cur.prev.pnext, ...), custom_call_target="tpu_custom_call" | custom-call | flops 5000000 | bytes 2000000 | tf_op jit(solution)/shard_map/forward/pallas_call | solution.py:242
  84.0 1.6 collective-permute-start.22
  88.7 1.7 forward.13
  93.9 1.5 collective-permute-done.26.ym
  95.5 2.4 %forward.14 = (f32[32,8,256]{2,1,0:T(8,128)S(1)}, f32[32,8,256]{2,1,0:T(8,128)S(1)}, f32[32,4,256]{2,1,0:T(4,128)}, f32[32,4,256]{2,1,0:T(4,128)}, f32[4,8,256]{2,1,0:T(8,128)S(1)}) custom-call(s32[3]{0:T(128)S(1)} %pad_add_fusion.flags.refs_0_, f32[32,8,256]{2,1,0:T(8,128)S(1)} %get-tuple-element.123.cur.prev.pnext, ...), custom_call_target="tpu_custom_call" | custom-call | flops 5000000 | bytes 2000000 | tf_op jit(solution)/shard_map/forward/pallas_call | solution.py:242
  102.4 1.9 %collective-permute-done.29.ym = f32[4,8,256]{2,1,0:T(8,128)S(1)} collective-permute-done((f32[4,8,256]{2,1,0:T(8,128)S(1)}, f32[4,8,256]{2,1,0:T(8,128)S(1)}, u32[]{:S(2)}, u32[]{:S(2)}) %collective-permute-start.29) | collective-permute-done | bytes 32800 | tf_op jit(solution)/shard_map/ppermute | solution.py:61
  107.5 2.9 %forward.15 = (f32[32,8,256]{2,1,0:T(8,128)S(1)}, f32[32,8,256]{2,1,0:T(8,128)S(1)}, f32[32,4,256]{2,1,0:T(4,128)}, f32[32,4,256]{2,1,0:T(4,128)}, f32[4,8,256]{2,1,0:T(8,128)}) custom-call(s32[3]{0:T(128)S(1)} %pad_add_fusion.flags.refs_0_, f32[32,8,256]{2,1,0:T(8,128)S(1)} %copy-done.6, f32[32,8,256]{2,1,0:T(8,128)S(1)} %get-tuple-element.123.cur.prev.pnext, ...), custom_call_target="tpu_custom_call" | custom-call | flops 5000000 | bytes 2000000 | tf_op jit(solution)/shard_map/forward/pallas_call | solution.py:242
  110.4 2.6 %adjoint.8 = (f32[32,8,256]{2,1,0:T(8,128)S(1)}, f32[32,8,256]{2,1,0:T(8,128)S(1)}, f32[32,4,256]{2,1,0:T(4,128)S(1)}, f32[32,4,256]{2,1,0:T(4,128)S(1)}, f32[4,8,256]{2,1,0:T(8,128)S(1)}) custom-call(s32[3]{0:T(128)S(1)} %pad_add_fusion.flags.refs_0_, f32[32,8,256]{2,1,0:T(8,128)S(1)} %get-tuple-element.90.refs_1_.prev, f32[32,8,256]{2,1,0:T(8,128)S(1)} %copy-done.26, ...), custom_call_target="tpu_custom_call" | custom-call | flops 5000000 | bytes 2000000 | tf_op jit(solution)/shard_map/adjoint/pallas_call | solution.py:242
  116.0 2.2 %collective-permute-done.32.ym = f32[4,8,256]{2,1,0:T(8,128)S(1)} collective-permute-done((f32[4,8,256]{2,1,0:T(8,128)S(1)}, f32[4,8,256]{2,1,0:T(8,128)S(1)}, u32[]{:S(2)}, u32[]{:S(2)}) %collective-permute-start.32) | collective-permute-done | bytes 32800 | tf_op jit(solution)/shard_map/ppermute | solution.py:61
  118.2 2.2 %adjoint.9 = (f32[32,8,256]{2,1,0:T(8,128)S(1)}, f32[32,8,256]{2,1,0:T(8,128)S(1)}, f32[32,4,256]{2,1,0:T(4,128)S(1)}, f32[32,4,256]{2,1,0:T(4,128)S(1)}, f32[4,8,256]{2,1,0:T(8,128)S(1)}) custom-call(s32[3]{0:T(128)S(1)} %pad_add_fusion.flags.refs_0_, f32[32,8,256]{2,1,0:T(8,128)S(1)} %get-tuple-element.133.cur.prev, ...), custom_call_target="tpu_custom_call" | custom-call | flops 5000000 | bytes 2000000 | tf_op jit(solution)/shard_map/adjoint/pallas_call | solution.py:242
  121.1 1.3 collective-permute-start.34
  123.3 2.2 %collective-permute-done.35.ym = f32[4,8,256]{2,1,0:T(8,128)S(1)} collective-permute-done((f32[4,8,256]{2,1,0:T(8,128)S(1)}, f32[4,8,256]{2,1,0:T(8,128)S(1)}, u32[]{:S(2)}, u32[]{:S(2)}) %collective-permute-start.35) | collective-permute-done | bytes 32800 | tf_op jit(solution)/shard_map/ppermute | solution.py:61
  125.5 2.2 %adjoint.10 = (f32[32,8,256]{2,1,0:T(8,128)S(1)}, f32[32,8,256]{2,1,0:T(8,128)S(1)}, f32[32,4,256]{2,1,0:T(4,128)S(1)}, f32[32,4,256]{2,1,0:T(4,128)S(1)}, f32[4,8,256]{2,1,0:T(8,128)S(1)}) custom-call(s32[3]{0:T(128)S(1)} %pad_add_fusion.flags.refs_0_, f32[32,8,256]{2,1,0:T(8,128)S(1)} %get-tuple-element.139.cur.prev, ...), custom_call_target="tpu_custom_call" | custom-call | flops 5000000 | bytes 2000000 | tf_op jit(solution)/shard_map/adjoint/pallas_call | solution.py:242
  130.6 2.2 %collective-permute-done.38.ym = f32[4,8,256]{2,1,0:T(8,128)S(1)} collective-permute-done((f32[4,8,256]{2,1,0:T(8,128)S(1)}, f32[4,8,256]{2,1,0:T(8,128)S(1)}, u32[]{:S(2)}, u32[]{:S(2)}) %collective-permute-start.38) | collective-permute-done | bytes 32800 | tf_op jit(solution)/shard_map/ppermute | solution.py:61
  132.8 2.2 %adjoint.11 = (f32[32,8,256]{2,1,0:T(8,128)S(1)}, f32[32,8,256]{2,1,0:T(8,128)S(1)}, f32[32,4,256]{2,1,0:T(4,128)S(1)}, f32[32,4,256]{2,1,0:T(4,128)S(1)}, f32[4,8,256]{2,1,0:T(8,128)S(1)}) custom-call(s32[3]{0:T(128)S(1)} %pad_add_fusion.flags.refs_0_, f32[32,8,256]{2,1,0:T(8,128)S(1)} %get-tuple-element.145.cur.prev, ...), custom_call_target="tpu_custom_call" | custom-call | flops 5000000 | bytes 2000000 | tf_op jit(solution)/shard_map/adjoint/pallas_call | solution.py:242
  137.8 2.2 %collective-permute-done.41.ym = f32[4,8,256]{2,1,0:T(8,128)S(1)} collective-permute-done((f32[4,8,256]{2,1,0:T(8,128)S(1)}, f32[4,8,256]{2,1,0:T(8,128)S(1)}, u32[]{:S(2)}, u32[]{:S(2)}) %collective-permute-start.41) | collective-permute-done | bytes 32800 | tf_op jit(solution)/shard_map/ppermute | solution.py:61
  140.0 2.2 %adjoint.12 = (f32[32,8,256]{2,1,0:T(8,128)S(1)}, f32[32,8,256]{2,1,0:T(8,128)S(1)}, f32[32,4,256]{2,1,0:T(4,128)S(1)}, f32[32,4,256]{2,1,0:T(4,128)S(1)}, f32[4,8,256]{2,1,0:T(8,128)S(1)}) custom-call(s32[3]{0:T(128)S(1)} %pad_add_fusion.flags.refs_0_, f32[32,8,256]{2,1,0:T(8,128)S(1)} %get-tuple-element.151.cur.prev, ...), custom_call_target="tpu_custom_call" | custom-call | flops 5000000 | bytes 2000000 | tf_op jit(solution)/shard_map/adjoint/pallas_call | solution.py:242
  145.1 2.2 %collective-permute-done.44.ym = f32[4,8,256]{2,1,0:T(8,128)S(1)} collective-permute-done((f32[4,8,256]{2,1,0:T(8,128)S(1)}, f32[4,8,256]{2,1,0:T(8,128)S(1)}, u32[]{:S(2)}, u32[]{:S(2)}) %collective-permute-start.44) | collective-permute-done | bytes 32800 | tf_op jit(solution)/shard_map/ppermute | solution.py:61
  147.3 2.8 %adjoint.13 = (f32[32,8,256]{2,1,0:T(8,128)S(1)}, f32[32,8,256]{2,1,0:T(8,128)S(1)}, f32[32,4,256]{2,1,0:T(4,128)S(1)}, f32[32,4,256]{2,1,0:T(4,128)S(1)}, f32[4,8,256]{2,1,0:T(8,128)}) custom-call(s32[3]{0:T(128)S(1)} %pad_add_fusion.flags.refs_0_, f32[32,8,256]{2,1,0:T(8,128)S(1)} %get-tuple-element.157.cur.prev, ...), custom_call_target="tpu_custom_call" | custom-call | flops 5000000 | bytes 2000000 | tf_op jit(solution)/shard_map/adjoint/pallas_call | solution.py:242
  153.9 2.1 %collective-permute-done.47.ym = f32[4,8,256]{2,1,0:T(8,128)S(1)} collective-permute-done((f32[4,8,256]{2,1,0:T(8,128)}, f32[4,8,256]{2,1,0:T(8,128)S(1)}, u32[]{:S(2)}, u32[]{:S(2)}) %collective-permute-start.47) | collective-permute-done | bytes 32800 | tf_op jit(solution)/shard_map/ppermute | solution.py:61
  158.5 2.9 %adjoint.14 = (f32[32,8,256]{2,1,0:T(8,128)S(1)}, f32[32,8,256]{2,1,0:T(8,128)S(1)}, f32[32,4,256]{2,1,0:T(4,128)}, f32[32,4,256]{2,1,0:T(4,128)}, f32[4,8,256]{2,1,0:T(8,128)}) custom-call(s32[3]{0:T(128)S(1)} %pad_add_fusion.flags.refs_0_, f32[32,8,256]{2,1,0:T(8,128)S(1)} %get-tuple-element.163.cur.prev, f32[32,8,256]{2,1,0:T(8,128)S(1)} %get-tuple-element.157.cur.prev, ...), custom_call_target="tpu_custom_call" | custom-call | flops 5000000 | bytes 2000000 | tf_op jit(solution)/shard_map/adjoint/pallas_call | solution.py:242
  164.9 2.3 %collective-permute-done.50.ym = f32[4,8,256]{2,1,0:T(8,128)S(1)} collective-permute-done((f32[4,8,256]{2,1,0:T(8,128)}, f32[4,8,256]{2,1,0:T(8,128)S(1)}, u32[]{:S(2)}, u32[]{:S(2)}) %collective-permute-start.50) | collective-permute-done | bytes 32800 | tf_op jit(solution)/shard_map/ppermute | solution.py:61
  169.8 2.2 %adjoint.15 = (f32[32,8,256]{2,1,0:T(8,128)S(1)}, f32[32,8,256]{2,1,0:T(8,128)S(1)}) custom-call(s32[3]{0:T(128)S(1)} %pad_add_fusion.flags.refs_0_, f32[32,8,256]{2,1,0:T(8,128)S(1)} %get-tuple-element.169.cur, f32[32,8,256]{2,1,0:T(8,128)S(1)} %get-tuple-element.163.cur.prev, f32[32,8,256]{2,1,0:T(8,128)S(1)} %get-tuple-element.178.vel.refs_3_, ...), custom_call_target="tpu_custom_call" | custom-call | flops 5000000 | bytes 2000000 | tf_op jit(solution)/shard_map/adjoint/pallas_call | solution.py:242
  175.3 2.7 %collective-permute-start.52 = (f32[2,32,256]{2,1,0:T(8,128)S(1)}, f32[2,32,256]{2,1,0:T(8,128)S(1)}, u32[]{:S(2)}, u32[]{:S(2)}) collective-permute-start(f32[2,32,256]{2,1,0:T(8,128)S(1)} %get-tuple-element.179), channel_id=1, source_target_pairs={{0,0},{1,2},{2,1},{3,3},{4,4},{5,6},{6,5},{7,7},{8,8},{9,10},{10,9... | collective-permute-start | bytes 196616 | tf_op jit(solution)/shard_map/ppermute | solution.py:61
  179.4 3.1 %collective-permute-start.55 = (f32[2,32,256]{2,1,0:T(8,128)S(1)}, f32[2,32,256]{2,1,0:T(8,128)S(1)}, u32[]{:S(2)}, u32[]{:S(2)}) collective-permute-start(f32[2,32,256]{2,1,0:T(8,128)S(1)} %get-tuple-element.180), channel_id=1, source_target_pairs={{0,12},{1,14},{2,13},{3,15},{4,0},{5,2},{6,1},{7,3},{8,4},{9,6},{1... | collective-permute-start | bytes 196616 | tf_op jit(solution)/shard_map/ppermute | solution.py:61
  183.2 1.3 collective-permute-done.53
  187.1 2.6 %convolution_bitcast_fusion = f32[32,32,64]{2,1,0:T(8,128)} fusion(f32[8,32,32,8]{2,3,0,1:T(8,128)S(1)} %copy.97, f32[64]{0:T(128)S(1)} %exponential_reduce_fusion, s32[8,8]{1,0:T(8,128)S(1)} %broadcast_add_fusion), kind=kOutput, calls=%fused_computation | convolution fusion | flops 50356224 | bytes 524800 | tf_op jit(solution)/shard_map/jzix,yjx->ziy/dot_general | solution.py:364
  189.7 1.7 broadcast_select_fusion.1
  (211 shorter events, 68.0 us)
Async XLA Ops:
  1.8 10.0 %collective-permute-start.2 = (f32[2,32,8,256]{3,2,1,0:T(8,128)S(1)}, f32[2,32,8,256]{3,2,1,0:T(8,128)S(1)}, u32[]{:S(2)}, u32[]{:S(2)}) collective-permute-start(f32[2,32,8,256]{3,2,1,0:T(8,128)S(1)} %pad_maximum_fusion.2), channel_id=1, source_target_pairs={{0,16},{1,2},{2,1},{3,19},{4,20},{5,6},{6,5},{7,23},{8,24},{9,10},... | collective-permute-start | bytes 1572872 | tf_op jit(solution)/shard_map/ppermute | solution.py:61
  5.3 12.0 %collective-permute-start.1 = (f32[2,32,8,256]{3,2,1,0:T(8,128)}, f32[2,32,8,256]{3,2,1,0:T(8,128)}, u32[]{:S(2)}, u32[]{:S(2)}) collective-permute-start(f32[2,32,8,256]{3,2,1,0:T(8,128)} %pad_maximum_fusion.1), channel_id=1, source_target_pairs={{0,16},{1,2},{2,1},{3,19},{4,20},{5,6},{6,5},{7,23},{8,24},{9,10},... | collective-permute-start | bytes 1572872 | tf_op jit(solution)/shard_map/ppermute | solution.py:61
  6.5 73.7 %collective-permute-start = (f32[2,32,8,256]{3,2,1,0:T(8,128)}, f32[2,32,8,256]{3,2,1,0:T(8,128)}, u32[]{:S(2)}, u32[]{:S(2)}) collective-permute-start(f32[2,32,8,256]{3,2,1,0:T(8,128)} %pad_maximum_fusion), channel_id=1, source_target_pairs={{0,16},{1,2},{2,1},{3,19},{4,20},{5,6},{6,5},{7,23},{8,24},{9,10},... | collective-permute-start | bytes 1572872 | tf_op jit(solution)/shard_map/ppermute | solution.py:61
  12.5 10.8 %collective-permute-start.3 = (f32[2,32,4,256]{3,2,1,0:T(4,128)S(1)}, f32[2,32,4,256]{3,2,1,0:T(4,128)S(1)}, u32[]{:S(2)}, u32[]{:S(2)}) collective-permute-start(f32[2,32,4,256]{3,2,1,0:T(4,128)S(1)} %get-tuple-element.93), channel_id=1, source_target_pairs={{0,16},{1,4},{2,18},{3,6},{4,1},{5,8},{6,3},{7,10},{8,5},{9,12},{1... | collective-permute-start | bytes 786440 | tf_op jit(solution)/shard_map/ppermute | solution.py:61
  14.5 8.7 %collective-permute-start.4 = (f32[2,32,4,256]{3,2,1,0:T(4,128)S(1)}, f32[2,32,4,256]{3,2,1,0:T(4,128)S(1)}, u32[]{:S(2)}, u32[]{:S(2)}) collective-permute-start(f32[2,32,4,256]{3,2,1,0:T(4,128)S(1)} %get-tuple-element.94), channel_id=1, source_target_pairs={{0,1},{1,0},{2,3},{3,2},{4,5},{5,4},{6,7},{7,6},{8,9},{9,8},{10,11... | collective-permute-start | bytes 786440 | tf_op jit(solution)/shard_map/ppermute | solution.py:61
  14.9 8.4 %collective-permute-start.5 = (f32[2,4,8,256]{3,2,1,0:T(8,128)S(1)}, f32[2,4,8,256]{3,2,1,0:T(8,128)S(1)}, u32[]{:S(2)}, u32[]{:S(2)}) collective-permute-start(f32[2,4,8,256]{3,2,1,0:T(8,128)S(1)} %get-tuple-element.95), channel_id=1, source_target_pairs={{0,2},{1,3},{2,0},{3,1},{4,6},{5,7},{6,4},{7,5},{8,10},{9,11},{10,... | collective-permute-start | bytes 196616 | tf_op jit(solution)/shard_map/ppermute | solution.py:61
  27.9 5.7 %collective-permute-start.10 = (f32[32,4,256]{2,1,0:T(4,128)S(1)}, f32[32,4,256]{2,1,0:T(4,128)S(1)}, u32[]{:S(2)}, u32[]{:S(2)}) collective-permute-start(f32[32,4,256]{2,1,0:T(4,128)S(1)} %get-tuple-element.105), channel_id=1, source_target_pairs={{0,1},{1,0},{2,3},{3,2},{4,5},{5,4},{6,7},{7,6},{8,9},{9,8},{10,11... | collective-permute-start | bytes 393224 | tf_op jit(solution)/shard_map/ppermute | solution.py:61
  29.8 4.6 %collective-permute-start.9 = (f32[32,4,256]{2,1,0:T(4,128)S(1)}, f32[32,4,256]{2,1,0:T(4,128)S(1)}, u32[]{:S(2)}, u32[]{:S(2)}) collective-permute-start(f32[32,4,256]{2,1,0:T(4,128)S(1)} %get-tuple-element.104), channel_id=1, source_target_pairs={{0,16},{1,4},{2,18},{3,6},{4,1},{5,8},{6,3},{7,10},{8,5},{9,12},{1... | collective-permute-start | bytes 393224 | tf_op jit(solution)/shard_map/ppermute | solution.py:61
  30.5 3.1 %collective-permute-start.11 = (f32[4,8,256]{2,1,0:T(8,128)S(1)}, f32[4,8,256]{2,1,0:T(8,128)S(1)}, u32[]{:S(2)}, u32[]{:S(2)}) collective-permute-start(f32[4,8,256]{2,1,0:T(8,128)S(1)} %get-tuple-element.106), channel_id=1, source_target_pairs={{0,2},{1,3},{2,0},{3,1},{4,6},{5,7},{6,4},{7,5},{8,10},{9,11},{10,... | collective-permute-start | bytes 98312 | tf_op jit(solution)/shard_map/ppermute | solution.py:61
  36.7 5.5 %collective-permute-start.12 = (f32[32,4,256]{2,1,0:T(4,128)}, f32[32,4,256]{2,1,0:T(4,128)S(1)}, u32[]{:S(2)}, u32[]{:S(2)}) collective-permute-start(f32[32,4,256]{2,1,0:T(4,128)} %get-tuple-element.108), channel_id=1, source_target_pairs={{0,16},{1,4},{2,18},{3,6},{4,1},{5,8},{6,3},{7,10},{8,5},{9,12},{1... | collective-permute-start | bytes 393224 | tf_op jit(solution)/shard_map/ppermute | solution.py:61
  37.9 4.3 %collective-permute-start.13 = (f32[32,4,256]{2,1,0:T(4,128)S(1)}, f32[32,4,256]{2,1,0:T(4,128)S(1)}, u32[]{:S(2)}, u32[]{:S(2)}) collective-permute-start(f32[32,4,256]{2,1,0:T(4,128)S(1)} %get-tuple-element.109), channel_id=1, source_target_pairs={{0,1},{1,0},{2,3},{3,2},{4,5},{5,4},{6,7},{7,6},{8,9},{9,8},{10,11... | collective-permute-start | bytes 393224 | tf_op jit(solution)/shard_map/ppermute | solution.py:61
  44.6 25.0 %collective-permute-start.15 = (f32[32,4,256]{2,1,0:T(4,128)}, f32[32,4,256]{2,1,0:T(4,128)S(1)}, u32[]{:S(2)}, u32[]{:S(2)}) collective-permute-start(f32[32,4,256]{2,1,0:T(4,128)} %get-tuple-element.112), channel_id=1, source_target_pairs={{0,16},{1,4},{2,18},{3,6},{4,1},{5,8},{6,3},{7,10},{8,5},{9,12},{1... | collective-permute-start | bytes 393224 | tf_op jit(solution)/shard_map/ppermute | solution.py:61
  45.6 24.1 %collective-permute-start.16 = (f32[32,4,256]{2,1,0:T(4,128)}, f32[32,4,256]{2,1,0:T(4,128)S(1)}, u32[]{:S(2)}, u32[]{:S(2)}) collective-permute-start(f32[32,4,256]{2,1,0:T(4,128)} %get-tuple-element.113), channel_id=1, source_target_pairs={{0,1},{1,0},{2,3},{3,2},{4,5},{5,4},{6,7},{7,6},{8,9},{9,8},{10,11... | collective-permute-start | bytes 393224 | tf_op jit(solution)/shard_map/ppermute | solution.py:61
  72.8 8.8 %collective-permute-start.18 = (f32[32,4,256]{2,1,0:T(4,128)}, f32[32,4,256]{2,1,0:T(4,128)S(1)}, u32[]{:S(2)}, u32[]{:S(2)}) collective-permute-start(f32[32,4,256]{2,1,0:T(4,128)} %get-tuple-element.116), channel_id=1, source_target_pairs={{0,16},{1,4},{2,18},{3,6},{4,1},{5,8},{6,3},{7,10},{8,5},{9,12},{1... | collective-permute-start | bytes 393224 | tf_op jit(solution)/shard_map/ppermute | solution.py:61
  72.8 8.8 %collective-permute-start.19 = (f32[32,4,256]{2,1,0:T(4,128)}, f32[32,4,256]{2,1,0:T(4,128)}, u32[]{:S(2)}, u32[]{:S(2)}) collective-permute-start(f32[32,4,256]{2,1,0:T(4,128)} %get-tuple-element.117), channel_id=1, source_target_pairs={{0,1},{1,0},{2,3},{3,2},{4,5},{5,4},{6,7},{7,6},{8,9},{9,8},{10,11... | collective-permute-start | bytes 393224 | tf_op jit(solution)/shard_map/ppermute | solution.py:61
  83.8 4.9 %collective-permute-start.21 = (f32[32,4,256]{2,1,0:T(4,128)S(1)}, f32[32,4,256]{2,1,0:T(4,128)S(1)}, u32[]{:S(2)}, u32[]{:S(2)}) collective-permute-start(f32[32,4,256]{2,1,0:T(4,128)S(1)} %get-tuple-element.120), channel_id=1, source_target_pairs={{0,16},{1,4},{2,18},{3,6},{4,1},{5,8},{6,3},{7,10},{8,5},{9,12},{1... | collective-permute-start | bytes 393224 | tf_op jit(solution)/shard_map/ppermute | solution.py:61
  84.0 4.7 %collective-permute-start.22 = (f32[32,4,256]{2,1,0:T(4,128)S(1)}, f32[32,4,256]{2,1,0:T(4,128)S(1)}, u32[]{:S(2)}, u32[]{:S(2)}) collective-permute-start(f32[32,4,256]{2,1,0:T(4,128)S(1)} %get-tuple-element.121), channel_id=1, source_target_pairs={{0,1},{1,0},{2,3},{3,2},{4,5},{5,4},{6,7},{7,6},{8,9},{9,8},{10,11... | collective-permute-start | bytes 393224 | tf_op jit(solution)/shard_map/ppermute | solution.py:61
  86.9 23.5 %collective-permute-start.6 = (f32[32,4,256]{2,1,0:T(4,128)}, f32[32,4,256]{2,1,0:T(4,128)S(1)}, u32[]{:S(2)}, u32[]{:S(2)}) collective-permute-start(f32[32,4,256]{2,1,0:T(4,128)} %slice_bitcast_fusion.5), channel_id=1, source_target_pairs={{0,16},{1,4},{2,18},{3,6},{4,1},{5,8},{6,3},{7,10},{8,5},{9,12},{1... | collective-permute-start | bytes 393224 | tf_op jit(solution)/shard_map/ppermute | solution.py:61
  90.4 5.0 %collective-permute-start.24 = (f32[32,4,256]{2,1,0:T(4,128)S(1)}, f32[32,4,256]{2,1,0:T(4,128)S(1)}, u32[]{:S(2)}, u32[]{:S(2)}) collective-permute-start(f32[32,4,256]{2,1,0:T(4,128)S(1)} %get-tuple-element.124), channel_id=1, source_target_pairs={{0,16},{1,4},{2,18},{3,6},{4,1},{5,8},{6,3},{7,10},{8,5},{9,12},{1... | collective-permute-start | bytes 393224 | tf_op jit(solution)/shard_map/ppermute | solution.py:61
  91.3 4.1 %collective-permute-start.25 = (f32[32,4,256]{2,1,0:T(4,128)S(1)}, f32[32,4,256]{2,1,0:T(4,128)S(1)}, u32[]{:S(2)}, u32[]{:S(2)}) collective-permute-start(f32[32,4,256]{2,1,0:T(4,128)S(1)} %get-tuple-element.125), channel_id=1, source_target_pairs={{0,1},{1,0},{2,3},{3,2},{4,5},{5,4},{6,7},{7,6},{8,9},{9,8},{10,11... | collective-permute-start | bytes 393224 | tf_op jit(solution)/shard_map/ppermute | solution.py:61
  93.6 16.7 %collective-permute-start.7 = (f32[32,4,256]{2,1,0:T(4,128)}, f32[32,4,256]{2,1,0:T(4,128)}, u32[]{:S(2)}, u32[]{:S(2)}) collective-permute-start(f32[32,4,256]{2,1,0:T(4,128)} %slice_bitcast_fusion.4), channel_id=1, source_target_pairs={{0,1},{1,0},{2,3},{3,2},{4,5},{5,4},{6,7},{7,6},{8,9},{9,8},{10,11... | collective-permute-start | bytes 393224 | tf_op jit(solution)/shard_map/ppermute | solution.py:61
  99.3 7.2 %collective-permute-start.27 = (f32[32,4,256]{2,1,0:T(4,128)}, f32[32,4,256]{2,1,0:T(4,128)}, u32[]{:S(2)}, u32[]{:S(2)}) collective-permute-start(f32[32,4,256]{2,1,0:T(4,128)} %get-tuple-element.128), channel_id=1, source_target_pairs={{0,16},{1,4},{2,18},{3,6},{4,1},{5,8},{6,3},{7,10},{8,5},{9,12},{1... | collective-permute-start | bytes 393224 | tf_op jit(solution)/shard_map/ppermute | solution.py:61
  100.0 6.5 %collective-permute-start.28 = (f32[32,4,256]{2,1,0:T(4,128)}, f32[32,4,256]{2,1,0:T(4,128)}, u32[]{:S(2)}, u32[]{:S(2)}) collective-permute-start(f32[32,4,256]{2,1,0:T(4,128)} %get-tuple-element.129), channel_id=1, source_target_pairs={{0,1},{1,0},{2,3},{3,2},{4,5},{5,4},{6,7},{7,6},{8,9},{9,8},{10,11... | collective-permute-start | bytes 393224 | tf_op jit(solution)/shard_map/ppermute | solution.py:61
  101.2 3.2 %collective-permute-start.29 = (f32[4,8,256]{2,1,0:T(8,128)S(1)}, f32[4,8,256]{2,1,0:T(8,128)S(1)}, u32[]{:S(2)}, u32[]{:S(2)}) collective-permute-start(f32[4,8,256]{2,1,0:T(8,128)S(1)} %get-tuple-element.130), channel_id=1, source_target_pairs={{0,2},{1,3},{2,0},{3,1},{4,6},{5,7},{6,4},{7,5},{8,10},{9,11},{10,... | collective-permute-start | bytes 98312 | tf_op jit(solution)/shard_map/ppermute | solution.py:61
  104.4 6.0 %collective-permute-start.8 = (f32[4,8,256]{2,1,0:T(8,128)}, f32[4,8,256]{2,1,0:T(8,128)}, u32[]{:S(2)}, u32[]{:S(2)}) collective-permute-start(f32[4,8,256]{2,1,0:T(8,128)} %slice_bitcast_fusion.7), channel_id=1, source_target_pairs={{0,2},{1,3},{2,0},{3,1},{4,6},{5,7},{6,4},{7,5},{8,10},{9,11},{10,... | collective-permute-start | bytes 98312 | tf_op jit(solution)/shard_map/ppermute | solution.py:61
  113.0 5.2 %collective-permute-start.30 = (f32[32,4,256]{2,1,0:T(4,128)S(1)}, f32[32,4,256]{2,1,0:T(4,128)S(1)}, u32[]{:S(2)}, u32[]{:S(2)}) collective-permute-start(f32[32,4,256]{2,1,0:T(4,128)S(1)} %get-tuple-element.134), channel_id=1, source_target_pairs={{0,16},{1,4},{2,18},{3,6},{4,1},{5,8},{6,3},{7,10},{8,5},{9,12},{1... | collective-permute-start | bytes 393224 | tf_op jit(solution)/shard_map/ppermute | solution.py:61
  114.0 4.2 %collective-permute-start.31 = (f32[32,4,256]{2,1,0:T(4,128)S(1)}, f32[32,4,256]{2,1,0:T(4,128)S(1)}, u32[]{:S(2)}, u32[]{:S(2)}) collective-permute-start(f32[32,4,256]{2,1,0:T(4,128)S(1)} %get-tuple-element.135), channel_id=1, source_target_pairs={{0,1},{1,0},{2,3},{3,2},{4,5},{5,4},{6,7},{7,6},{8,9},{9,8},{10,11... | collective-permute-start | bytes 393224 | tf_op jit(solution)/shard_map/ppermute | solution.py:61
  120.4 5.0 %collective-permute-start.33 = (f32[32,4,256]{2,1,0:T(4,128)S(1)}, f32[32,4,256]{2,1,0:T(4,128)S(1)}, u32[]{:S(2)}, u32[]{:S(2)}) collective-permute-start(f32[32,4,256]{2,1,0:T(4,128)S(1)} %get-tuple-element.140), channel_id=1, source_target_pairs={{0,16},{1,4},{2,18},{3,6},{4,1},{5,8},{6,3},{7,10},{8,5},{9,12},{1... | collective-permute-start | bytes 393224 | tf_op jit(solution)/shard_map/ppermute | solution.py:61
  121.1 4.4 %collective-permute-start.34 = (f32[32,4,256]{2,1,0:T(4,128)S(1)}, f32[32,4,256]{2,1,0:T(4,128)S(1)}, u32[]{:S(2)}, u32[]{:S(2)}) collective-permute-start(f32[32,4,256]{2,1,0:T(4,128)S(1)} %get-tuple-element.141), channel_id=1, source_target_pairs={{0,1},{1,0},{2,3},{3,2},{4,5},{5,4},{6,7},{7,6},{8,9},{9,8},{10,11... | collective-permute-start | bytes 393224 | tf_op jit(solution)/shard_map/ppermute | solution.py:61
  127.7 5.0 %collective-permute-start.36 = (f32[32,4,256]{2,1,0:T(4,128)S(1)}, f32[32,4,256]{2,1,0:T(4,128)S(1)}, u32[]{:S(2)}, u32[]{:S(2)}) collective-permute-start(f32[32,4,256]{2,1,0:T(4,128)S(1)} %get-tuple-element.146), channel_id=1, source_target_pairs={{0,16},{1,4},{2,18},{3,6},{4,1},{5,8},{6,3},{7,10},{8,5},{9,12},{1... | collective-permute-start | bytes 393224 | tf_op jit(solution)/shard_map/ppermute | solution.py:61
  128.5 4.3 %collective-permute-start.37 = (f32[32,4,256]{2,1,0:T(4,128)S(1)}, f32[32,4,256]{2,1,0:T(4,128)S(1)}, u32[]{:S(2)}, u32[]{:S(2)}) collective-permute-start(f32[32,4,256]{2,1,0:T(4,128)S(1)} %get-tuple-element.147), channel_id=1, source_target_pairs={{0,1},{1,0},{2,3},{3,2},{4,5},{5,4},{6,7},{7,6},{8,9},{9,8},{10,11... | collective-permute-start | bytes 393224 | tf_op jit(solution)/shard_map/ppermute | solution.py:61
  135.0 5.0 %collective-permute-start.39 = (f32[32,4,256]{2,1,0:T(4,128)S(1)}, f32[32,4,256]{2,1,0:T(4,128)S(1)}, u32[]{:S(2)}, u32[]{:S(2)}) collective-permute-start(f32[32,4,256]{2,1,0:T(4,128)S(1)} %get-tuple-element.152), channel_id=1, source_target_pairs={{0,16},{1,4},{2,18},{3,6},{4,1},{5,8},{6,3},{7,10},{8,5},{9,12},{1... | collective-permute-start | bytes 393224 | tf_op jit(solution)/shard_map/ppermute | solution.py:61
  135.8 4.2 %collective-permute-start.40 = (f32[32,4,256]{2,1,0:T(4,128)S(1)}, f32[32,4,256]{2,1,0:T(4,128)S(1)}, u32[]{:S(2)}, u32[]{:S(2)}) collective-permute-start(f32[32,4,256]{2,1,0:T(4,128)S(1)} %get-tuple-element.153), channel_id=1, source_target_pairs={{0,1},{1,0},{2,3},{3,2},{4,5},{5,4},{6,7},{7,6},{8,9},{9,8},{10,11... | collective-permute-start | bytes 393224 | tf_op jit(solution)/shard_map/ppermute | solution.py:61
  142.3 5.0 %collective-permute-start.42 = (f32[32,4,256]{2,1,0:T(4,128)S(1)}, f32[32,4,256]{2,1,0:T(4,128)S(1)}, u32[]{:S(2)}, u32[]{:S(2)}) collective-permute-start(f32[32,4,256]{2,1,0:T(4,128)S(1)} %get-tuple-element.158), channel_id=1, source_target_pairs={{0,16},{1,4},{2,18},{3,6},{4,1},{5,8},{6,3},{7,10},{8,5},{9,12},{1... | collective-permute-start | bytes 393224 | tf_op jit(solution)/shard_map/ppermute | solution.py:61
  143.0 4.2 %collective-permute-start.43 = (f32[32,4,256]{2,1,0:T(4,128)S(1)}, f32[32,4,256]{2,1,0:T(4,128)S(1)}, u32[]{:S(2)}, u32[]{:S(2)}) collective-permute-start(f32[32,4,256]{2,1,0:T(4,128)S(1)} %get-tuple-element.159), channel_id=1, source_target_pairs={{0,1},{1,0},{2,3},{3,2},{4,5},{5,4},{6,7},{7,6},{8,9},{9,8},{10,11... | collective-permute-start | bytes 393224 | tf_op jit(solution)/shard_map/ppermute | solution.py:61
  150.8 5.2 %collective-permute-start.45 = (f32[32,4,256]{2,1,0:T(4,128)S(1)}, f32[32,4,256]{2,1,0:T(4,128)S(1)}, u32[]{:S(2)}, u32[]{:S(2)}) collective-permute-start(f32[32,4,256]{2,1,0:T(4,128)S(1)} %get-tuple-element.164), channel_id=1, source_target_pairs={{0,16},{1,4},{2,18},{3,6},{4,1},{5,8},{6,3},{7,10},{8,5},{9,12},{1... | collective-permute-start | bytes 393224 | tf_op jit(solution)/shard_map/ppermute | solution.py:61
  151.5 4.5 %collective-permute-start.46 = (f32[32,4,256]{2,1,0:T(4,128)S(1)}, f32[32,4,256]{2,1,0:T(4,128)S(1)}, u32[]{:S(2)}, u32[]{:S(2)}) collective-permute-start(f32[32,4,256]{2,1,0:T(4,128)S(1)} %get-tuple-element.165), channel_id=1, source_target_pairs={{0,1},{1,0},{2,3},{3,2},{4,5},{5,4},{6,7},{7,6},{8,9},{9,8},{10,11... | collective-permute-start | bytes 393224 | tf_op jit(solution)/shard_map/ppermute | solution.py:61
  152.7 3.3 %collective-permute-start.47 = (f32[4,8,256]{2,1,0:T(8,128)}, f32[4,8,256]{2,1,0:T(8,128)S(1)}, u32[]{:S(2)}, u32[]{:S(2)}) collective-permute-start(f32[4,8,256]{2,1,0:T(8,128)} %get-tuple-element.166), channel_id=1, source_target_pairs={{0,2},{1,3},{2,0},{3,1},{4,6},{5,7},{6,4},{7,5},{8,10},{9,11},{10,... | collective-permute-start | bytes 98312 | tf_op jit(solution)/shard_map/ppermute | solution.py:61
  162.1 5.1 %collective-permute-start.48 = (f32[32,4,256]{2,1,0:T(4,128)}, f32[32,4,256]{2,1,0:T(4,128)S(1)}, u32[]{:S(2)}, u32[]{:S(2)}) collective-permute-start(f32[32,4,256]{2,1,0:T(4,128)} %get-tuple-element.170), channel_id=1, source_target_pairs={{0,16},{1,4},{2,18},{3,6},{4,1},{5,8},{6,3},{7,10},{8,5},{9,12},{1... | collective-permute-start | bytes 393224 | tf_op jit(solution)/shard_map/ppermute | solution.py:61
  162.8 4.4 %collective-permute-start.49 = (f32[32,4,256]{2,1,0:T(4,128)}, f32[32,4,256]{2,1,0:T(4,128)S(1)}, u32[]{:S(2)}, u32[]{:S(2)}) collective-permute-start(f32[32,4,256]{2,1,0:T(4,128)} %get-tuple-element.171), channel_id=1, source_target_pairs={{0,1},{1,0},{2,3},{3,2},{4,5},{5,4},{6,7},{7,6},{8,9},{9,8},{10,11... | collective-permute-start | bytes 393224 | tf_op jit(solution)/shard_map/ppermute | solution.py:61
  164.0 3.3 %collective-permute-start.50 = (f32[4,8,256]{2,1,0:T(8,128)}, f32[4,8,256]{2,1,0:T(8,128)S(1)}, u32[]{:S(2)}, u32[]{:S(2)}) collective-permute-start(f32[4,8,256]{2,1,0:T(8,128)} %get-tuple-element.172), channel_id=1, source_target_pairs={{0,2},{1,3},{2,0},{3,1},{4,6},{5,7},{6,4},{7,5},{8,10},{9,11},{10,... | collective-permute-start | bytes 98312 | tf_op jit(solution)/shard_map/ppermute | solution.py:61
  172.1 3.1 %collective-permute-start.51 = (f32[4,32,256]{2,1,0:T(8,128)S(1)}, f32[4,32,256]{2,1,0:T(8,128)S(1)}, u32[]{:S(2)}, u32[]{:S(2)}) collective-permute-start(f32[4,32,256]{2,1,0:T(8,128)S(1)} %get-tuple-element.184), channel_id=1, source_target_pairs={{0,1},{1,0},{2,3},{3,2},{4,5},{5,4},{6,7},{7,6},{8,9},{9,8},{10,11... | collective-permute-start | bytes 393224 | tf_op jit(solution)/shard_map/ppermute | solution.py:61
  173.2 6.2 %collective-permute-start.57 = (f32[32,8,256]{2,1,0:T(8,128)S(1)}, f32[32,8,256]{2,1,0:T(8,128)S(1)}, u32[]{:S(2)}, u32[]{:S(2)}) collective-permute-start(f32[32,8,256]{2,1,0:T(8,128)S(1)} %get-tuple-element.169.cur), channel_id=1, source_target_pairs={{0,16},{1,2},{2,1},{3,19},{4,20},{5,6},{6,5},{7,23},{8,24},{9,10},... | collective-permute-start | bytes 786440 | tf_op jit(solution)/shard_map/ppermute | solution.py:61
  174.2 15.5 %collective-permute-start.56 = (f32[32,8,256]{2,1,0:T(8,128)S(1)}, f32[32,8,256]{2,1,0:T(8,128)}, u32[]{:S(2)}, u32[]{:S(2)}) collective-permute-start(f32[32,8,256]{2,1,0:T(8,128)S(1)} %get-tuple-element.176), channel_id=1, source_target_pairs={{0,16},{1,2},{2,1},{3,19},{4,20},{5,6},{6,5},{7,23},{8,24},{9,10},... | collective-permute-start | bytes 786440 | tf_op jit(solution)/shard_map/ppermute | solution.py:61
  175.3 8.0 %collective-permute-start.52 = (f32[2,32,256]{2,1,0:T(8,128)S(1)}, f32[2,32,256]{2,1,0:T(8,128)S(1)}, u32[]{:S(2)}, u32[]{:S(2)}) collective-permute-start(f32[2,32,256]{2,1,0:T(8,128)S(1)} %get-tuple-element.179), channel_id=1, source_target_pairs={{0,0},{1,2},{2,1},{3,3},{4,4},{5,6},{6,5},{7,7},{8,8},{9,10},{10,9... | collective-permute-start | bytes 196616 | tf_op jit(solution)/shard_map/ppermute | solution.py:61
  178.0 6.5 %collective-permute-start.53 = (f32[2,32,256]{2,1,0:T(8,128)S(1)}, f32[2,32,256]{2,1,0:T(8,128)S(1)}, u32[]{:S(2)}, u32[]{:S(2)}) collective-permute-start(f32[2,32,256]{2,1,0:T(8,128)S(1)} %get-tuple-element.182), channel_id=1, source_target_pairs={{0,4},{1,6},{2,5},{3,7},{4,8},{5,10},{6,9},{7,11},{8,12},{9,14},{1... | collective-permute-start | bytes 196616 | tf_op jit(solution)/shard_map/ppermute | solution.py:61
  178.7 7.0 %collective-permute-start.54 = (f32[2,32,256]{2,1,0:T(8,128)S(1)}, f32[2,32,256]{2,1,0:T(8,128)S(1)}, u32[]{:S(2)}, u32[]{:S(2)}) collective-permute-start(f32[2,32,256]{2,1,0:T(8,128)S(1)} %get-tuple-element.181), channel_id=1, source_target_pairs={{0,8},{1,10},{2,9},{3,11},{4,12},{5,14},{6,13},{7,15},{8,0},{9,2},... | collective-permute-start | bytes 196616 | tf_op jit(solution)/shard_map/ppermute | solution.py:61
  179.4 6.3 %collective-permute-start.55 = (f32[2,32,256]{2,1,0:T(8,128)S(1)}, f32[2,32,256]{2,1,0:T(8,128)S(1)}, u32[]{:S(2)}, u32[]{:S(2)}) collective-permute-start(f32[2,32,256]{2,1,0:T(8,128)S(1)} %get-tuple-element.180), channel_id=1, source_target_pairs={{0,12},{1,14},{2,13},{3,15},{4,0},{5,2},{6,1},{7,3},{8,4},{9,6},{1... | collective-permute-start | bytes 196616 | tf_op jit(solution)/shard_map/ppermute | solution.py:61
  (49 other events, 184.6 us)
where the time goes:
time: 192 us; the launch traced here: 191 us
  starting transfers between devices  56.6 us (29%)
  Pallas kernels  40.8 us (21%)
  waiting for transfers between devices  38.7 us (20%)
  local copies, waits for them, and re-layouts  23 us (12%)
  blocking collectives  20.2 us (11%)
  other arithmetic  8.22 us (4%)
  matrix products  2.62 us (1%)
    ppermute x58, starting transfers between devices, send(): return lax.ppermute(value, ALL, pairs)  56.6 us
    pallas_call x19, Pallas kernels, call(): pl.pallas_call(kernel, name=name, out_shape=outs, in_specs=specs, out_spe...  40.8 us
    ppermute x58, waiting for transfers between devices, send(): return lax.ppermute(value, ALL, pairs)  38.7 us
    all_gather x1, blocking collectives, per_device(): gathered = lax.all_gather(packed, ('xline', 'inline'))  20.2 us
    unnamed x80, local copies, waits for them, and re-layouts  14.7 us
  transfers between devices with their start and end apart: 58, of which 21 were waited for; matrix products, arithmetic and copies ran while one was open for 9% of the time, Pallas kernels for 10%

commit v1 on v0

v1 whole, which is shorter than its diff:
```python
import functools

import jax
import jax.numpy as jnp
import numpy as np
from jax import lax
from jax.experimental import pallas as pl
from jax.experimental.pallas import tpu as pltpu
from jax.sharding import PartitionSpec as P

CAP = 8
SMOOTH = 16
SECOND = (-205.0 / 72.0, 8.0 / 5.0, -1.0 / 5.0, 8.0 / 315.0, -1.0 / 560.0)
FIRST = (4.0 / 5.0, -1.0 / 5.0, 4.0 / 105.0, -1.0 / 280.0)
ALL = ("shots", "xline", "inline")
COLS = 8
GROUP = 8
VMEM_BYTES = 8 * 1024 * 1024
F32 = jnp.float32
BF16 = jnp.bfloat16


class Plan:
    def __init__(self, mesh):
        self.shots = mesh.shape["shots"]
        self.nx = mesh.shape["xline"]
        self.nq = self.nx // 2

    def index(self, s, q, y, c):
        return (s * self.nx + 2 * q + y) * 2 + c

    def perm(self, partner):
        pairs = []
        for s in range(self.shots):
            for q in range(self.nq):
                for y in range(2):
                    for c in range(2):
                        t = partner(q, y, c)
                        dst = self.index(s ^ 1, q, y, c) if t is None else self.index(s, *t)
                        pairs.append((self.index(s, q, y, c), dst))
        return pairs

    def swap(self):
        return self.perm(lambda q, y, c: None if y == c else (q, c, y))

    def z(self):
        def partner(q, y, c):
            other = q + 1 if c == 1 else q - 1
            return (other, y, 1 - c) if 0 <= other < self.nq else None

        return self.perm(partner)

    def core(self):
        return self.perm(lambda q, y, c: (q, y, 1 - c))

    def y(self):
        return self.perm(lambda q, y, c: (q, 1 - y, c))

    def flip(self, bit):
        return self.perm(lambda q, y, c: (q ^ bit, y, c) if (q ^ bit) < self.nq else None)

    def spread(self, shift):
        return self.perm(lambda q, y, c: ((q + shift) % self.nq, c, y))


def send(value, pairs):
    return lax.ppermute(value, ALL, pairs)


def depth_matrix(n):
    m = np.zeros((n, 2 * n), np.float32)
    for k in range(1, 5):
        for j in range(n):
            for i, sign in ((j + k, 1.0), (j - k, -1.0)):
                if 0 <= i < n:
                    m[i, j] = round(SECOND[k] * 5040)
                    m[i, n + j] = sign * round(FIRST[k - 1] * 840)
    return m


def stencil_matrix(rows, cols):
    own = (rows + 8) * cols
    m = np.zeros((3, rows, cols, own + rows * 8), np.float32)
    for i in range(rows):
        for x in range(cols):
            for k in range(1, 5):
                total = round(SECOND[k] * 5040)
                slope = round(FIRST[k - 1] * 840)
                for sign in (1, -1):
                    at = (i + 4 + sign * k) * cols + x
                    m[0, i, x, at] += total
                    m[1, i, x, at] += sign * slope
                    to = x + sign * k
                    if to < 0:
                        at = own + i * 4 + to + 4
                    elif to >= cols:
                        at = own + rows * 4 + i * 4 + to - cols
                    else:
                        at = (i + 4) * cols + to
                    m[0, i, x, at] += total
                    m[2, i, x, at] += sign * slope
    return m.reshape(3 * rows * cols, own + rows * 8)


def split(value):
    high = value.astype(BF16)
    return high, (value - high.astype(F32)).astype(BF16)


def mm(a, b):
    return jnp.dot(a, b, preferred_element_type=F32)


def differences(flags, cur, zm, cm, ym, near, deep):
    depth = cur.shape[1]
    size = GROUP * COLS
    own = split(cur[...])
    along = mm(jnp.concatenate(own, axis=1), deep[...])
    edge = ym[...]
    top = split(jnp.where(flags[1] == 1, edge, 0.0))
    bottom = split(jnp.where(flags[1] == 0, edge, 0.0))
    from_z, from_c = split(zm[...]), split(cm[...])
    ext = [jnp.concatenate(parts, axis=0) for parts in zip(top, own, bottom)]
    for n in range(cur.shape[0] // size):
        here = slice(n * size, n * size + size)
        sides = slice(n * GROUP * 4, n * GROUP * 4 + GROUP * 4)
        rhs = []
        for p in range(2):
            rhs += [ext[p][n * size : n * size + size + 8 * COLS], from_z[p][sides], from_c[p][sides]]
        out = mm(near[...], jnp.concatenate(rhs, axis=0))
        yield (here, out[0:size], along[here, 0:depth], out[size : 2 * size], out[2 * size :],
               along[here, depth:])


def halves(value):
    rows, depth = value.shape
    pairs = value.reshape(rows // (2 * COLS), 2, COLS, depth)
    a, b = pairs[:, 0], pairs[:, 1]
    low = lax.broadcasted_iota(jnp.int32, a.shape, 1) < 4
    first = jnp.where(low, a, pltpu.roll(b, 4, axis=1))
    last = jnp.where(low, pltpu.roll(a, 4, axis=1), b)
    return first.reshape(rows // 2, depth), last.reshape(rows // 2, depth)


def rims(flags, new, zo, co, yo):
    first, last = halves(new[...])
    zo[...] = jnp.where(flags[0] == 0, first, last)
    co[...] = jnp.where(flags[0] == 0, last, first)
    size = new.shape[0]
    yo[...] = jnp.where(flags[1] == 0, new[size - 4 * COLS :], new[0 : 4 * COLS])


def settle_kernel(rim_count, flags, a, b, recv, a_out, b_out, *outs):
    keep = flags[0] == flags[1]
    for n, (own, out) in enumerate(((a, a_out), (b, b_out))):
        out[...] = jnp.where(keep, own[...], recv[n])
        if n < rim_count:
            rims(flags, out, *(ref.at[n] for ref in outs))


def settle_one(with_rims, flags, own, recv, out, *outs):
    out[...] = jnp.where(flags[0] == flags[1], own[...], recv[...])
    if with_rims:
        rims(flags, out, *outs)


def model_kernel(flags, lr, zm, cm, ym, near, deep, vel, k0, ki, kx, kz):
    for here, spare, spare_z, di, dx, dz in differences(flags, lr, zm.at[0], cm.at[0], ym.at[0], near, deep):
        v = vel[here]
        square = v * v
        k0[here] = square * (1.0 / 5040)
        scaled = square * (1.0 / (840 * 840))
        ki[here] = scaled * di
        kx[here] = scaled * dx
        kz[here] = scaled * dz


def advance(flags, cur, prev, k0, ki, kx, kz, zm, cm, ym, near, deep, inj, finish):
    for here, sums, sums_z, di, dx, dz in differences(flags, cur, zm, cm, ym, near, deep):
        center = cur[here]
        change = k0[here] * ((sums + sums_z) + (3.0 * SECOND[0] * 5040) * center)
        change = change - (ki[here] * di + kx[here] * dx + kz[here] * dz) + inj[here]
        finish(here, (center - prev[here]) + (center + change), change)


def forward_kernel(step, flags, cur, prev, k0, ki, kx, kz, zm, cm, ym, near, deep, srow, sz, wave,
                   new, change_out, zo, co, yo):
    size, depth = cur.shape
    n = srow.shape[1]
    spot = lax.broadcasted_iota(jnp.int32, (size, n), 0) == srow[...]
    spot = spot.astype(F32).astype(BF16)
    high, low = split(jnp.where(
        lax.broadcasted_iota(jnp.int32, (n, depth), 1) == sz[...], wave[:, step : step + 1], 0.0))
    inj = mm(spot, high) + mm(spot, low)

    def finish(here, value, change):
        new[here] = value
        change_out[here] = change

    advance(flags, cur, prev, k0, ki, kx, kz, zm, cm, ym, near, deep, inj, finish)
    rims(flags, new, zo, co, yo)


def adjoint_kernel(t, last, flags, cur, prev, k0, ki, kx, kz, zm, cm, ym, near, deep, pnext,
                   change_in, image, rrow, rrow_c, rz, obs, extra, new, image_out, *outs):
    size, depth = cur.shape
    n = rrow.shape[1]
    spot = lax.broadcasted_iota(jnp.int32, (size, n), 0) == rrow[...]
    spot = spot.astype(F32).astype(BF16)
    pick = lax.broadcasted_iota(jnp.int32, (n, size), 1) == rrow_c[...]
    pick = pick.astype(F32).astype(BF16)
    high, low = split(pnext[...])
    at = lax.broadcasted_iota(jnp.int32, (n, depth), 1) == rz[...]
    seen = jnp.where(at, mm(pick, high) + mm(pick, low), 0.0)
    residual = jnp.sum(seen, axis=1, keepdims=True) - obs[:, t : t + 1]
    high, low = split(jnp.where(at, residual, 0.0))
    inj = mm(spot, high) + mm(spot, low)
    scale = 2.0 / obs.shape[1]

    def finish(here, value, change):
        new[here] = value
        total = value * change_in[here]
        if image is not None:
            total = total + image[here]
        if last:
            total = total * scale / extra[here]
        image_out[here] = total

    advance(flags, cur, prev, k0, ki, kx, kz, zm, cm, ym, near, deep, inj, finish)
    if not last:
        rims(flags, new, *outs)


def first_adjoint_kernel(t, last, *refs):
    adjoint_kernel(t, last, *refs[:14], None, *refs[14:])


def middle(kernel):
    def run(t, last, *refs):
        n = 18 if kernel is first_adjoint_kernel else 19
        kernel(t, last, *refs[:n], None, *refs[n:])

    return run


def shaped(*shape):
    return jax.ShapeDtypeStruct(shape, F32)


def call(kernel, name, outs, *args):
    specs = [pl.BlockSpec(memory_space=pltpu.SMEM)]
    specs += [pl.BlockSpec(memory_space=pltpu.VMEM)] * (len(args) - 1)
    return pl.pallas_call(
        kernel,
        name=name,
        out_shape=outs,
        in_specs=specs,
        out_specs=[pl.BlockSpec(memory_space=pltpu.VMEM)] * len(outs),
        compiler_params=pltpu.CompilerParams(vmem_limit_bytes=VMEM_BYTES),
        cost_estimate=pl.CostEstimate(flops=5_000_000, bytes_accessed=2_000_000, transcendentals=0),
    )(*args)


def per_device(plan, fwd_now, fwd_before, adj_now, adj_before, velocity, log_density, observed,
               rec_cells, rec_counts, src_cell, wavelet):
    rows, cols, depth = fwd_now.shape
    size = rows * cols
    steps = wavelet.shape[0]
    nx, nq = plan.nx, plan.nq
    subs = 2 * nx
    xline, c = lax.axis_index("xline"), lax.axis_index("inline")
    q, y = xline // 2, xline % 2
    keep = y == c
    z_perm, c_perm, y_perm, swap_perm = plan.z(), plan.core(), plan.y(), plan.swap()
    flags = jnp.stack([c, y]).astype(jnp.int32)
    field = shaped(size, depth)
    side, edge = (size // 2, depth), (4 * cols, depth)
    rim = [shaped(*side), shaped(*side), shaped(*edge)]

    deep = depth_matrix(depth)
    deep = jnp.asarray(np.concatenate([deep, deep]), BF16)
    near = stencil_matrix(GROUP, cols)
    own, half = near.shape[1] - GROUP * 8, GROUP * 4
    from_z = np.where(np.arange(near.shape[1]) // half == own // half, 0.0, 1.0)
    other = np.concatenate([near[:, :own], near[:, own + half :], near[:, own : own + half]], axis=1)
    inside = jnp.where(c == 0, q > 0, q < nq - 1)
    near = jnp.where(c == 0, jnp.asarray(near, F32), jnp.asarray(other, F32))
    near = jnp.where(inside, near, near * jnp.asarray(from_z, F32)[None, :]).astype(BF16)
    near = jnp.concatenate([near, near], axis=1)

    def halo(zo, co, yo):
        return send(zo, z_perm), send(co, c_perm), send(yo, y_perm)

    def after(value, *deps):
        return lax.optimization_barrier((value,) + deps)[0]

    def flat(value):
        return value.reshape(size, depth)

    log_density, fwd_now, velocity = flat(log_density), flat(fwd_now), flat(velocity)
    fwd_before, adj_now, adj_before = flat(fwd_before), flat(adj_now), flat(adj_before)
    first = send(jnp.stack([log_density, fwd_now]), swap_perm)
    second = send(jnp.stack([velocity, fwd_before]), swap_perm)
    density, p_now, *out = call(
        functools.partial(settle_kernel, 2), "settle",
        [field, field] + [shaped(2, *r.shape) for r in rim], flags, log_density, fwd_now, first)
    zm, cm, ym = halo(*out)
    vel, p_before = call(functools.partial(settle_kernel, 0), "settle_model", [field, field],
                         flags, velocity, fwd_before, second)
    model = call(model_kernel, "model", [field] * 4, flags, density, zm, cm, ym, near, deep, vel)
    halos = (zm[1], cm[1], ym[1])

    plane = nx * cols * depth
    src_i = src_cell // plane - y * rows
    src_x = src_cell // depth % (nx * cols) - (2 * q + c) * cols
    ok = (src_i >= 0) & (src_i < rows) & (src_x >= 0) & (src_x < cols)
    srow = jnp.where(ok, src_i * cols + src_x, -1)[None, :]
    sz = (src_cell % depth)[:, None]
    wave = wavelet.T

    live = jnp.arange(CAP)[None, :] < rec_counts[0][:, None]
    cells = jnp.where(live.reshape(-1), rec_cells[0], -1)
    lists = jnp.concatenate([observed, cells[None, :].astype(F32)], axis=0)[None]
    stages = [(c_perm, c), (y_perm, y)]
    stages += [(plan.flip(1 << b), (q >> b) & 1) for b in range((nq - 1).bit_length())]

    states, changes = [], []
    for t in range(steps):
        p_next, change, *out = call(
            functools.partial(forward_kernel, t), "forward", [field, field] + rim,
            flags, p_now, p_before, *model, *halos, near, deep, srow, sz, wave)
        if t < steps - 1:
            halos = halo(*out)
        share = -(-len(stages) // (steps - 2))
        for pairs, bit in stages[t * share : t * share + share]:
            got = send(after(lists, out[0]), pairs)
            lists = jnp.where(bit == 0, jnp.concatenate([lists, got]), jnp.concatenate([got, lists]))
        if t == 1:
            got_now = send(after(adj_now, out[0]), swap_perm)
        if t == 3:
            got_before = send(after(adj_before, out[0]), swap_perm)
            u_now, *out = call(functools.partial(settle_one, True), "settle_adjoint", [field] + rim,
                               flags, adj_now, after(got_now, out[0]))
            u_rim = out
        if t == 4:
            u_halos = halo(*(after(r, out[0]) for r in u_rim))
        if t == 5:
            u_before, = call(functools.partial(settle_one, False), "settle_before", [field],
                             flags, adj_before, after(got_before, out[0]))
        p_before, p_now = p_now, p_next
        states.append(p_next)
        changes.append(change)

    sub = (2 * q + c) * 2 + y
    mine = lax.dynamic_index_in_dim(lists, sub, 0, keepdims=False)[steps].astype(jnp.int32)
    traces = lax.dynamic_slice(lists, (0, 0, sub * CAP), (subs, steps, CAP))
    obs = traces.transpose(0, 2, 1).reshape(subs * CAP, steps)
    rrow = jnp.where(mine < 0, -1, mine // depth)
    rz = (mine % depth)[:, None]

    halos = u_halos
    image = None
    for j in range(steps):
        t = steps - 1 - j
        last = j == steps - 1
        args = [flags, u_now, u_before, *model, *halos, near, deep, states[t], changes[t]]
        kernel = adjoint_kernel
        if j == 0:
            kernel = first_adjoint_kernel
        else:
            args.append(image)
        args += [rrow[None, :], rrow[:, None], rz, obs]
        if last:
            args.append(vel)
        else:
            kernel = middle(kernel)
        outs = call(functools.partial(kernel, t, last), "adjoint",
                    [field, field] + ([] if last else rim), *args)
        u_before, u_now = u_now, outs[0]
        image = outs[1]
        if not last:
            halos = halo(*outs[2:])

    chunk = depth // nx
    raw = image.T.reshape(nq, 2, chunk, size)
    own = lax.dynamic_index_in_dim(raw, c, 1, keepdims=False)
    other = send(lax.dynamic_index_in_dim(raw, 1 - c, 1, keepdims=False), c_perm)
    both = jnp.where(c == 0, jnp.stack([own, other], 1), jnp.stack([other, own], 1))
    pieces = [
        send(lax.dynamic_index_in_dim(both, (q + s) % nq, 0, keepdims=False), plan.spread(s))
        for s in range(nq)
    ]
    block = (rows, cols, depth)
    adj_out = jnp.where(keep, u_now, send(u_now, swap_perm)).reshape(block)
    adj_prev = jnp.where(keep, u_before, send(u_before, swap_perm)).reshape(block)

    pieces = jnp.stack(pieces).reshape(2 * nq, chunk, rows, cols)
    lines = jnp.arange(nx * cols)
    from_q = (q - jnp.arange(nq)) % nq
    places = (from_q[:, None] * (2 * cols) + jnp.arange(2 * cols)[None, :]).reshape(-1)
    weights = jnp.exp(-jnp.abs(lines[:, None] - places[None, :]).astype(F32) / SMOOTH)
    weights = weights / jnp.sum(weights, axis=1, keepdims=True)
    gradient = jnp.einsum("jzix,yjx->ziy", pieces, weights.reshape(-1, 2 * nq, cols),
                          precision=lax.Precision.HIGHEST)
    return gradient, adj_out, adj_prev


def solution(mesh):
    field = P(("shots", "inline"), "xline", None)
    model = P("inline", "xline", None)
    lists = P(("xline", "inline"), None)
    return jax.shard_map(
        functools.partial(per_device, Plan(mesh)),
        mesh=mesh,
        in_specs=(field, field, field, field, model, model, P("shots", ("xline", "inline")),
                  lists, lists, P("shots"), P("shots", None)),
        out_specs=(P(("shots", "xline"), "inline", None), field, field),
        check_vma=False,
    )
```

time: 192 us -> 178 us (0.927)
  blocking collectives: 20.2 us -> 0 us
  starting transfers between devices: 56.6 us -> 63.8 us
  local copies, waits for them, and re-layouts: 23 us -> 29.3 us
  Pallas kernels: 40.8 us -> 35 us
    all_gather x1 -> x0, blocking collectives: 20.2 us -> none  [per_device(): gathered = lax.all_gather(packed, ('xline', 'inline'))]
    unnamed x80 -> x119, local copies, waits for them, and re-layouts: 14.7 us -> 24.1 us
    ppermute x58 -> x63, starting transfers between devices: 56.6 us -> 63.8 us  [send(): return lax.ppermute(value, ALL, pairs)]
    pallas_call x19 -> x21, Pallas kernels: 40.8 us -> 35 us  [call(): pl.pallas_call(kernel, name=name, out_shape=outs, in_specs=specs, out_spe...]
    squeeze x3 -> x0, local copies, waits for them, and re-layouts: 1.94 us -> none  [per_device(): u_halo = halo(zo[0], co[0], yo[0])]
    ppermute x58 -> x63, waiting for transfers between devices: 38.7 us -> 36.8 us  [send(): return lax.ppermute(value, ALL, pairs)]
  transfers between devices with their start and end apart: 58 -> 63, of which waited for: 21 -> 22; matrix products, arithmetic and copies ran while one was open for 9% -> 8% of each run, Pallas kernels for 10% -> 9%
where the time goes in v1:
time: 178 us; the launch traced here: 177 us
  starting transfers between devices  63.8 us (36%)
  waiting for transfers between devices  36.8 us (21%)
  Pallas kernels  35 us (20%)
  local copies, waits for them, and re-layouts  29.3 us (16%)
  other arithmetic  7.34 us (4%)
  matrix products  3.84 us (2%)
    ppermute x63, starting transfers between devices, send(): return lax.ppermute(value, ALL, pairs)  63.8 us
    ppermute x63, waiting for transfers between devices, send(): return lax.ppermute(value, ALL, pairs)  36.8 us
    pallas_call x21, Pallas kernels, call(): pl.pallas_call(kernel, name=name, out_shape=outs, in_specs=specs, out_spe...  35 us
    unnamed x119, local copies, waits for them, and re-layouts  24.1 us
    dot_general x1, matrix products, per_device(): jnp.einsum('jzix,yjx->ziy', pieces, weights.reshape(-1, 2 * nq, cols), pr...  3.84 us
  transfers between devices with their start and end apart: 63, of which 22 were waited for; matrix products, arithmetic and copies ran while one was open for 8% of the time, Pallas kernels for 9%

profile of v1, /device:TPU:1, one launch (start us, length us, event | category | flops | bytes accessed | tf_op | source)
XLA Modules:
  0.0 177.4 jit_solution(1217187985902739699)
XLA Ops:
  1.8 2.7 %collective-permute-start = (f32[2,256,256]{2,1,0:T(8,128)S(1)}, f32[2,256,256]{2,1,0:T(8,128)S(1)}, u32[]{:S(2)}, u32[]{:S(2)}) collective-permute-start(f32[2,256,256]{2,1,0:T(8,128)S(1)} %pad_maximum_fusion), channel_id=1, source_target_pairs={{0,16},{1,2},{2,1},{3,19},{4,20},{5,6},{6,5},{7,23},{8,24},{9,10},... | collective-permute-start | bytes 1572872 | tf_op jit(solution)/shard_map/ppermute | solution.py:67
  6.3 5.4 %collective-permute-done.recv = f32[2,256,256]{2,1,0:T(8,128)S(1)} collective-permute-done((f32[2,256,256]{2,1,0:T(8,128)S(1)}, f32[2,256,256]{2,1,0:T(8,128)S(1)}, u32[]{:S(2)}, u32[]{:S(2)}) %collective-permute-start) | collective-permute-done | bytes 524320 | tf_op jit(solution)/shard_map/ppermute | solution.py:67
  11.6 1.4 settle.1
  15.5 1.5 collective-permute-start.2
  18.3 3.4 %collective-permute-done.2.zm = f32[2,128,256]{2,1,0:T(8,128)S(1)} collective-permute-done((f32[2,128,256]{2,1,0:T(8,128)S(1)}, f32[2,128,256]{2,1,0:T(8,128)S(1)}, u32[]{:S(2)}, u32[]{:S(2)}) %collective-permute-start.2) | collective-permute-done | bytes 262176 | tf_op jit(solution)/shard_map/ppermute | solution.py:67
  27.5 2.3 %collective-permute-done.7.ym = f32[32,256]{1,0:T(8,128)S(1)} collective-permute-done((f32[32,256]{1,0:T(8,128)S(1)}, f32[32,256]{1,0:T(8,128)S(1)}, u32[]{:S(2)}, u32[]{:S(2)}) %collective-permute-start.7) | collective-permute-done | bytes 32800 | tf_op jit(solution)/shard_map/ppermute | solution.py:67
  29.8 1.9 %forward.9 = (f32[256,256]{1,0:T(8,128)S(1)}, f32[256,256]{1,0:T(8,128)S(1)}, f32[128,256]{1,0:T(8,128)S(1)}, f32[128,256]{1,0:T(8,128)}, f32[32,256]{1,0:T(8,128)S(1)}) custom-call(s32[2]{0:T(128)S(1)} %pad_add_fusion.flags.refs_0_, f32[256,256]{1,0:T(8,128)S(1)} %get-tuple-element.114.cur.prev.pnext, f32[256,256]{1,0:T(8,128)S(1)} %get-tuple-element.103.cur.prev, ...), custom_call_target="tpu_custom_call" | custom-call | flops 5000000 | bytes 2000000 | tf_op jit(solution)/shard_map/forward/pallas_call | solution.py:253
  36.1 1.3 collective-permute-done.11.ym
  38.0 1.9 %forward.10 = (f32[256,256]{1,0:T(8,128)S(1)}, f32[256,256]{1,0:T(8,128)S(1)}, f32[128,256]{1,0:T(8,128)}, f32[128,256]{1,0:T(8,128)}, f32[32,256]{1,0:T(8,128)S(1)}) custom-call(s32[2]{0:T(128)S(1)} %pad_add_fusion.flags.refs_0_, f32[256,256]{1,0:T(8,128)S(1)} %get-tuple-element.120.cur.prev.refs_12_, f32[256,256]{1,0:T(8,128)S(1)} %get-tuple-element.114.cur.prev.pnext, ...), custom_call_target="tpu_custom_call" | custom-call | flops 5000000 | bytes 2000000 | tf_op jit(solution)/shard_map/forward/pallas_call | solution.py:253
  40.6 1.8 %collective-permute-start.12 = (f32[128,256]{1,0:T(8,128)}, f32[128,256]{1,0:T(8,128)S(1)}, u32[]{:S(2)}, u32[]{:S(2)}) collective-permute-start(f32[128,256]{1,0:T(8,128)} %get-tuple-element.124), channel_id=1, source_target_pairs={{0,16},{1,4},{2,18},{3,6},{4,1},{5,8},{6,3},{7,10},{8,5},{9,12},{1... | collective-permute-start | bytes 393224 | tf_op jit(solution)/shard_map/ppermute | solution.py:67
  45.5 2.1 %collective-permute-done.14.ym = f32[32,256]{1,0:T(8,128)S(1)} collective-permute-done((f32[32,256]{1,0:T(8,128)S(1)}, f32[32,256]{1,0:T(8,128)S(1)}, u32[]{:S(2)}, u32[]{:S(2)}) %collective-permute-start.14) | collective-permute-done | bytes 32800 | tf_op jit(solution)/shard_map/ppermute | solution.py:67
  49.2 1.9 %forward.11 = (f32[256,256]{1,0:T(8,128)S(1)}, f32[256,256]{1,0:T(8,128)S(1)}, f32[128,256]{1,0:T(8,128)}, f32[128,256]{1,0:T(8,128)}, f32[32,256]{1,0:T(8,128)S(1)}) custom-call(s32[2]{0:T(128)S(1)} %pad_add_fusion.flags.refs_0_, f32[256,256]{1,0:T(8,128)S(1)} %get-tuple-element.123.cur.prev.refs_12_, f32[256,256]{1,0:T(8,128)S(1)} %get-tuple-element.120.cur.prev.refs_12_, ...), custom_call_target="tpu_custom_call" | custom-call | flops 5000000 | bytes 2000000 | tf_op jit(solution)/shard_map/forward/pallas_call | solution.py:253
  51.8 2.6 %collective-permute-start.16 = (f32[128,256]{1,0:T(8,128)}, f32[128,256]{1,0:T(8,128)S(1)}, u32[]{:S(2)}, u32[]{:S(2)}) collective-permute-start(f32[128,256]{1,0:T(8,128)} %get-tuple-element.127), channel_id=1, source_target_pairs={{0,16},{1,4},{2,18},{3,6},{4,1},{5,8},{6,3},{7,10},{8,5},{9,12},{1... | collective-permute-start | bytes 393224 | tf_op jit(solution)/shard_map/ppermute | solution.py:67
  55.3 1.5 maximum_select_fusion.2
  57.9 1.6 collective-permute-start.15
  59.5 1.3 settle_adjoint.1
  60.9 2.4 %forward.12 = (f32[256,256]{1,0:T(8,128)S(1)}, f32[256,256]{1,0:T(8,128)S(1)}, f32[128,256]{1,0:T(8,128)}, f32[128,256]{1,0:T(8,128)}, f32[32,256]{1,0:T(8,128)S(1)}) custom-call(s32[2]{0:T(128)S(1)} %pad_add_fusion.flags.refs_0_, f32[256,256]{1,0:T(8,128)S(1)} %get-tuple-element.131.cur.prev.refs_12_, f32[256,256]{1,0:T(8,128)S(1)} %get-tuple-element.123.cur.prev.refs_12_, ...), custom_call_target="tpu_custom_call" | custom-call | flops 5000000 | bytes 2000000 | tf_op jit(solution)/shard_map/forward/pallas_call | solution.py:253
  68.3 1.5 collective-permute-done.21.ym
  73.3 2.0 %collective-permute-start.25 = (f32[128,256]{1,0:T(8,128)S(1)}, f32[128,256]{1,0:T(8,128)S(1)}, u32[]{:S(2)}, u32[]{:S(2)}) collective-permute-start(f32[128,256]{1,0:T(8,128)S(1)} %get-tuple-element.138), channel_id=1, source_target_pairs={{0,16},{1,4},{2,18},{3,6},{4,1},{5,8},{6,3},{7,10},{8,5},{9,12},{1... | collective-permute-start | bytes 393224 | tf_op jit(solution)/shard_map/ppermute | solution.py:67
  76.7 1.7 collective-permute-done.27.ym
  78.4 1.6 collective-permute-start.22
  80.0 1.9 %forward.14 = (f32[256,256]{1,0:T(8,128)S(1)}, f32[256,256]{1,0:T(8,128)S(1)}, f32[128,256]{1,0:T(8,128)}, f32[128,256]{1,0:T(8,128)}, f32[32,256]{1,0:T(8,128)S(1)}) custom-call(s32[2]{0:T(128)S(1)} %pad_add_fusion.flags.refs_0_, f32[256,256]{1,0:T(8,128)S(1)} %get-tuple-element.146.cur.prev.refs_12_, f32[256,256]{1,0:T(8,128)S(1)} %get-tuple-element.134.cur.prev.refs_12_, ...), custom_call_target="tpu_custom_call" | custom-call | flops 5000000 | bytes 2000000 | tf_op jit(solution)/shard_map/forward/pallas_call | solution.py:253
  83.5 1.6 collective-permute-start.29
  86.3 2.0 %collective-permute-done.30.ym = f32[32,256]{1,0:T(8,128)S(1)} collective-permute-done((f32[32,256]{1,0:T(8,128)S(1)}, f32[32,256]{1,0:T(8,128)S(1)}, u32[]{:S(2)}, u32[]{:S(2)}) %collective-permute-start.30) | collective-permute-done | bytes 32800 | tf_op jit(solution)/shard_map/ppermute | solution.py:67
  92.3 2.4 %forward.15 = (f32[256,256]{1,0:T(8,128)S(1)}, f32[256,256]{1,0:T(8,128)S(1)}, f32[128,256]{1,0:T(8,128)}, f32[128,256]{1,0:T(8,128)}, f32[32,256]{1,0:T(8,128)}) custom-call(s32[2]{0:T(128)S(1)} %pad_add_fusion.flags.refs_0_, f32[256,256]{1,0:T(8,128)S(1)} %copy-done.10, f32[256,256]{1,0:T(8,128)S(1)} %get-tuple-element.146.cur.prev.refs_12_, ...), custom_call_target="tpu_custom_call" | custom-call | flops 5000000 | bytes 2000000 | tf_op jit(solution)/shard_map/forward/pallas_call | solution.py:253
  94.8 2.1 %adjoint.8 = (f32[256,256]{1,0:T(8,128)S(1)}, f32[256,256]{1,0:T(8,128)S(1)}, f32[128,256]{1,0:T(8,128)S(1)}, f32[128,256]{1,0:T(8,128)S(1)}, f32[32,256]{1,0:T(8,128)S(1)}) custom-call(s32[2]{0:T(128)S(1)} %pad_add_fusion.flags.refs_0_, f32[256,256]{1,0:T(8,128)S(1)} %copy-done.8, f32[256,256]{1,0:T(8,128)S(1)} %settle_before.1.refs_2_, ...), custom_call_target="tpu_custom_call" | custom-call | flops 5000000 | bytes 2000000 | tf_op jit(solution)/shard_map/adjoint/pallas_call | solution.py:253
  98.4 1.4 collective-permute-start.37
  99.8 1.7 collective-permute-done.37.refs_9_
  101.6 1.6 adjoint.9
  104.3 1.3 collective-permute-start.39
  106.6 2.0 %collective-permute-done.40.refs_9_ = f32[32,256]{1,0:T(8,128)S(1)} collective-permute-done((f32[32,256]{1,0:T(8,128)S(1)}, f32[32,256]{1,0:T(8,128)S(1)}, u32[]{:S(2)}, u32[]{:S(2)}) %collective-permute-start.40) | collective-permute-done | bytes 32800 | tf_op jit(solution)/shard_map/ppermute | solution.py:67
  108.7 1.8 %adjoint.10 = (f32[256,256]{1,0:T(8,128)S(1)}, f32[256,256]{1,0:T(8,128)S(1)}, f32[128,256]{1,0:T(8,128)S(1)}, f32[128,256]{1,0:T(8,128)S(1)}, f32[32,256]{1,0:T(8,128)S(1)}) custom-call(s32[2]{0:T(128)S(1)} %pad_add_fusion.flags.refs_0_, f32[256,256]{1,0:T(8,128)S(1)} %get-tuple-element.165.refs_1_.refs_2_, ...), custom_call_target="tpu_custom_call" | custom-call | flops 5000000 | bytes 2000000 | tf_op jit(solution)/shard_map/adjoint/pallas_call | solution.py:253
  110.9 1.6 collective-permute-start.42
  113.5 2.0 %collective-permute-done.43.refs_9_ = f32[32,256]{1,0:T(8,128)S(1)} collective-permute-done((f32[32,256]{1,0:T(8,128)S(1)}, f32[32,256]{1,0:T(8,128)S(1)}, u32[]{:S(2)}, u32[]{:S(2)}) %collective-permute-start.43) | collective-permute-done | bytes 32800 | tf_op jit(solution)/shard_map/ppermute | solution.py:67
  115.5 1.6 adjoint.11
  120.1 2.0 %collective-permute-done.46.refs_9_ = f32[32,256]{1,0:T(8,128)S(1)} collective-permute-done((f32[32,256]{1,0:T(8,128)S(1)}, f32[32,256]{1,0:T(8,128)S(1)}, u32[]{:S(2)}, u32[]{:S(2)}) %collective-permute-start.46) | collective-permute-done | bytes 32800 | tf_op jit(solution)/shard_map/ppermute | solution.py:67
  122.2 1.6 adjoint.12
  126.8 2.0 %collective-permute-done.49.refs_9_ = f32[32,256]{1,0:T(8,128)S(1)} collective-permute-done((f32[32,256]{1,0:T(8,128)S(1)}, f32[32,256]{1,0:T(8,128)S(1)}, u32[]{:S(2)}, u32[]{:S(2)}) %collective-permute-start.49) | collective-permute-done | bytes 32800 | tf_op jit(solution)/shard_map/ppermute | solution.py:67
  128.9 2.2 %adjoint.13 = (f32[256,256]{1,0:T(8,128)S(1)}, f32[256,256]{1,0:T(8,128)S(1)}, f32[128,256]{1,0:T(8,128)S(1)}, f32[128,256]{1,0:T(8,128)S(1)}, f32[32,256]{1,0:T(8,128)}) custom-call(s32[2]{0:T(128)S(1)} %pad_add_fusion.flags.refs_0_, f32[256,256]{1,0:T(8,128)S(1)} %get-tuple-element.183.refs_1_.refs_2_, f32[256,256]{1,0:T(8,128)S(1)} %get-tuple-element.177.refs_1_.refs_2_, ...), custom_call_target="tpu_custom_call" | custom-call | flops 5000000 | bytes 2000000 | tf_op jit(solution)/shard_map/adjoint/pallas_call | solution.py:253
  135.4 1.6 collective-permute-done.52.refs_9_
  142.0 2.3 %adjoint.14 = (f32[256,256]{1,0:T(8,128)S(1)}, f32[256,256]{1,0:T(8,128)S(1)}, f32[128,256]{1,0:T(8,128)}, f32[128,256]{1,0:T(8,128)}, f32[32,256]{1,0:T(8,128)}) custom-call(s32[2]{0:T(128)S(1)} %pad_add_fusion.flags.refs_0_, f32[256,256]{1,0:T(8,128)S(1)} %get-tuple-element.189.refs_1_.prev, f32[256,256]{1,0:T(8,128)S(1)} %get-tuple-element.183.refs_1_.refs_2_, ...), custom_call_target="tpu_custom_call" | custom-call | flops 5000000 | bytes 2000000 | tf_op jit(solution)/shard_map/adjoint/pallas_call | solution.py:253
  148.0 2.2 %collective-permute-done.55.ym = f32[32,256]{1,0:T(8,128)S(1)} collective-permute-done((f32[32,256]{1,0:T(8,128)}, f32[32,256]{1,0:T(8,128)S(1)}, u32[]{:S(2)}, u32[]{:S(2)}) %collective-permute-start.55) | collective-permute-done | bytes 32800 | tf_op jit(solution)/shard_map/ppermute | solution.py:67
  155.2 1.6 adjoint.15
  158.1 1.4 collective-permute-start.62
  160.1 3.3 %collective-permute-start.57 = (f32[2,32,256]{2,1,0:T(8,128)S(1)}, f32[2,32,256]{2,1,0:T(8,128)S(1)}, u32[]{:S(2)}, u32[]{:S(2)}) collective-permute-start(f32[2,32,256]{2,1,0:T(8,128)S(1)} %get-tuple-element.203), channel_id=1, source_target_pairs={{0,0},{1,2},{2,1},{3,3},{4,4},{5,6},{6,5},{7,7},{8,8},{9,10},{10,9... | collective-permute-start | bytes 196616 | tf_op jit(solution)/shard_map/ppermute | solution.py:67
  164.1 3.8 %collective-permute-start.60 = (f32[2,32,256]{2,1,0:T(8,128)S(1)}, f32[2,32,256]{2,1,0:T(8,128)S(1)}, u32[]{:S(2)}, u32[]{:S(2)}) collective-permute-start(f32[2,32,256]{2,1,0:T(8,128)S(1)} %get-tuple-element.204), channel_id=1, source_target_pairs={{0,12},{1,14},{2,13},{3,15},{4,0},{5,2},{6,1},{7,3},{8,4},{9,6},{1... | collective-permute-start | bytes 196616 | tf_op jit(solution)/shard_map/ppermute | solution.py:67
  170.9 1.8 %copy.81 = f32[8,32,32,8]{2,3,0,1:T(8,128)} copy(f32[8,32,32,8]{1,3,2,0:T(8,128)S(1)} %bitcast.98) | data formatting | bytes 524288 | tf_op jit(solution)/shard_map/reshape | solution.py:397
  172.8 3.8 %convolution_bitcast_fusion = f32[32,32,64]{2,1,0:T(8,128)} fusion(f32[8,32,32,8]{2,3,0,1:T(8,128)} %copy.81, f32[64]{0:T(128)S(1)} %exponential_reduce_fusion, s32[8,8]{1,0:T(8,128)S(1)} %broadcast_add_fusion), kind=kOutput, calls=%fused_computation | convolution fusion | flops 50356224 | bytes 524800 | tf_op jit(solution)/shard_map/jzix,yjx->ziy/dot_general | solution.py:403
  (261 shorter events, 77.4 us)
Async XLA Ops:
  1.8 9.9 %collective-permute-start = (f32[2,256,256]{2,1,0:T(8,128)S(1)}, f32[2,256,256]{2,1,0:T(8,128)S(1)}, u32[]{:S(2)}, u32[]{:S(2)}) collective-permute-start(f32[2,256,256]{2,1,0:T(8,128)S(1)} %pad_maximum_fusion), channel_id=1, source_target_pairs={{0,16},{1,2},{2,1},{3,19},{4,20},{5,6},{6,5},{7,23},{8,24},{9,10},... | collective-permute-start | bytes 1572872 | tf_op jit(solution)/shard_map/ppermute | solution.py:67
  5.3 12.3 %collective-permute-start.1 = (f32[2,256,256]{2,1,0:T(8,128)}, f32[2,256,256]{2,1,0:T(8,128)S(1)}, u32[]{:S(2)}, u32[]{:S(2)}) collective-permute-start(f32[2,256,256]{2,1,0:T(8,128)} %pad_maximum_fusion.1), channel_id=1, source_target_pairs={{0,16},{1,2},{2,1},{3,19},{4,20},{5,6},{6,5},{7,23},{8,24},{9,10},... | collective-permute-start | bytes 1572872 | tf_op jit(solution)/shard_map/ppermute | solution.py:67
  13.0 5.3 %collective-permute-start.3 = (f32[2,128,256]{2,1,0:T(8,128)}, f32[2,128,256]{2,1,0:T(8,128)S(1)}, u32[]{:S(2)}, u32[]{:S(2)}) collective-permute-start(f32[2,128,256]{2,1,0:T(8,128)} %get-tuple-element.107), channel_id=1, source_target_pairs={{0,1},{1,0},{2,3},{3,2},{4,5},{5,4},{6,7},{7,6},{8,9},{9,8},{10,11... | collective-permute-start | bytes 786440 | tf_op jit(solution)/shard_map/ppermute | solution.py:67
  13.4 4.9 %collective-permute-start.4 = (f32[2,32,256]{2,1,0:T(8,128)S(1)}, f32[2,32,256]{2,1,0:T(8,128)S(1)}, u32[]{:S(2)}, u32[]{:S(2)}) collective-permute-start(f32[2,32,256]{2,1,0:T(8,128)S(1)} %get-tuple-element.108), channel_id=1, source_target_pairs={{0,2},{1,3},{2,0},{3,1},{4,6},{5,7},{6,4},{7,5},{8,10},{9,11},{10,... | collective-permute-start | bytes 196616 | tf_op jit(solution)/shard_map/ppermute | solution.py:67
  15.5 6.2 %collective-permute-start.2 = (f32[2,128,256]{2,1,0:T(8,128)S(1)}, f32[2,128,256]{2,1,0:T(8,128)S(1)}, u32[]{:S(2)}, u32[]{:S(2)}) collective-permute-start(f32[2,128,256]{2,1,0:T(8,128)S(1)} %get-tuple-element.106), channel_id=1, source_target_pairs={{0,16},{1,4},{2,18},{3,6},{4,1},{5,8},{6,3},{7,10},{8,5},{9,12},{1... | collective-permute-start | bytes 786440 | tf_op jit(solution)/shard_map/ppermute | solution.py:67
  24.7 5.1 %collective-permute-start.5 = (f32[128,256]{1,0:T(8,128)S(1)}, f32[128,256]{1,0:T(8,128)S(1)}, u32[]{:S(2)}, u32[]{:S(2)}) collective-permute-start(f32[128,256]{1,0:T(8,128)S(1)} %get-tuple-element.115), channel_id=1, source_target_pairs={{0,16},{1,4},{2,18},{3,6},{4,1},{5,8},{6,3},{7,10},{8,5},{9,12},{1... | collective-permute-start | bytes 393224 | tf_op jit(solution)/shard_map/ppermute | solution.py:67
  25.9 3.9 %collective-permute-start.6 = (f32[128,256]{1,0:T(8,128)S(1)}, f32[128,256]{1,0:T(8,128)S(1)}, u32[]{:S(2)}, u32[]{:S(2)}) collective-permute-start(f32[128,256]{1,0:T(8,128)S(1)} %get-tuple-element.116), channel_id=1, source_target_pairs={{0,1},{1,0},{2,3},{3,2},{4,5},{5,4},{6,7},{7,6},{8,9},{9,8},{10,11... | collective-permute-start | bytes 393224 | tf_op jit(solution)/shard_map/ppermute | solution.py:67
  32.4 5.1 %collective-permute-start.10 = (f32[128,256]{1,0:T(8,128)}, f32[128,256]{1,0:T(8,128)S(1)}, u32[]{:S(2)}, u32[]{:S(2)}) collective-permute-start(f32[128,256]{1,0:T(8,128)} %get-tuple-element.121), channel_id=1, source_target_pairs={{0,1},{1,0},{2,3},{3,2},{4,5},{5,4},{6,7},{7,6},{8,9},{9,8},{10,11... | collective-permute-start | bytes 393224 | tf_op jit(solution)/shard_map/ppermute | solution.py:67
  33.3 4.7 %collective-permute-start.9 = (f32[128,256]{1,0:T(8,128)S(1)}, f32[128,256]{1,0:T(8,128)S(1)}, u32[]{:S(2)}, u32[]{:S(2)}) collective-permute-start(f32[128,256]{1,0:T(8,128)S(1)} %get-tuple-element.118), channel_id=1, source_target_pairs={{0,16},{1,4},{2,18},{3,6},{4,1},{5,8},{6,3},{7,10},{8,5},{9,12},{1... | collective-permute-start | bytes 393224 | tf_op jit(solution)/shard_map/ppermute | solution.py:67
  35.3 9.2 %collective-permute-start.32 = (f32[2,9,128]{2,1,0:T(8,128)S(1)}, f32[2,9,128]{2,1,0:T(8,128)}, u32[]{:S(2)}, u32[]{:S(2)}) collective-permute-start(f32[2,9,128]{2,1,0:T(8,128)S(1)} %maximum_select_fusion.4), channel_id=1, source_target_pairs={{0,2},{1,3},{2,0},{3,1},{4,6},{5,7},{6,4},{7,5},{8,10},{9,11},{10,... | collective-permute-start | bytes 27656 | tf_op jit(solution)/shard_map/ppermute | solution.py:67
  40.6 7.1 %collective-permute-start.12 = (f32[128,256]{1,0:T(8,128)}, f32[128,256]{1,0:T(8,128)S(1)}, u32[]{:S(2)}, u32[]{:S(2)}) collective-permute-start(f32[128,256]{1,0:T(8,128)} %get-tuple-element.124), channel_id=1, source_target_pairs={{0,16},{1,4},{2,18},{3,6},{4,1},{5,8},{6,3},{7,10},{8,5},{9,12},{1... | collective-permute-start | bytes 393224 | tf_op jit(solution)/shard_map/ppermute | solution.py:67
  42.4 5.2 %collective-permute-start.13 = (f32[128,256]{1,0:T(8,128)}, f32[128,256]{1,0:T(8,128)S(1)}, u32[]{:S(2)}, u32[]{:S(2)}) collective-permute-start(f32[128,256]{1,0:T(8,128)} %get-tuple-element.125), channel_id=1, source_target_pairs={{0,1},{1,0},{2,3},{3,2},{4,5},{5,4},{6,7},{7,6},{8,9},{9,8},{10,11... | collective-permute-start | bytes 393224 | tf_op jit(solution)/shard_map/ppermute | solution.py:67
  42.7 15.2 %collective-permute-start.8 = (f32[256,256]{1,0:T(8,128)S(1)}, f32[256,256]{1,0:T(8,128)S(1)}, u32[]{:S(2)}, u32[]{:S(2)}) collective-permute-start(f32[256,256]{1,0:T(8,128)S(1)} %bitcast.93), channel_id=1, source_target_pairs={{0,16},{1,2},{2,1},{3,19},{4,20},{5,6},{6,5},{7,23},{8,24},{9,10},... | collective-permute-start | bytes 786440 | tf_op jit(solution)/shard_map/ppermute | solution.py:67
  43.6 4.0 %collective-permute-start.14 = (f32[32,256]{1,0:T(8,128)S(1)}, f32[32,256]{1,0:T(8,128)S(1)}, u32[]{:S(2)}, u32[]{:S(2)}) collective-permute-start(f32[32,256]{1,0:T(8,128)S(1)} %get-tuple-element.126), channel_id=1, source_target_pairs={{0,2},{1,3},{2,0},{3,1},{4,6},{5,7},{6,4},{7,5},{8,10},{9,11},{10,... | collective-permute-start | bytes 98312 | tf_op jit(solution)/shard_map/ppermute | solution.py:67
  45.2 10.1 %collective-permute-start.33 = (f32[4,9,128]{2,1,0:T(8,128)S(1)}, f32[4,9,128]{2,1,0:T(8,128)}, u32[]{:S(2)}, u32[]{:S(2)}) collective-permute-start(f32[4,9,128]{2,1,0:T(8,128)S(1)} %maximum_select_fusion.3), channel_id=1, source_target_pairs={{0,4},{1,5},{2,6},{3,7},{4,0},{5,1},{6,2},{7,3},{8,12},{9,13},{10,... | collective-permute-start | bytes 55304 | tf_op jit(solution)/shard_map/ppermute | solution.py:67
  51.8 9.0 %collective-permute-start.16 = (f32[128,256]{1,0:T(8,128)}, f32[128,256]{1,0:T(8,128)S(1)}, u32[]{:S(2)}, u32[]{:S(2)}) collective-permute-start(f32[128,256]{1,0:T(8,128)} %get-tuple-element.127), channel_id=1, source_target_pairs={{0,16},{1,4},{2,18},{3,6},{4,1},{5,8},{6,3},{7,10},{8,5},{9,12},{1... | collective-permute-start | bytes 393224 | tf_op jit(solution)/shard_map/ppermute | solution.py:67
  54.5 6.4 %collective-permute-start.17 = (f32[128,256]{1,0:T(8,128)}, f32[128,256]{1,0:T(8,128)}, u32[]{:S(2)}, u32[]{:S(2)}) collective-permute-start(f32[128,256]{1,0:T(8,128)} %get-tuple-element.132), channel_id=1, source_target_pairs={{0,1},{1,0},{2,3},{3,2},{4,5},{5,4},{6,7},{7,6},{8,9},{9,8},{10,11... | collective-permute-start | bytes 393224 | tf_op jit(solution)/shard_map/ppermute | solution.py:67
  56.8 9.3 %collective-permute-start.34 = (f32[8,9,128]{2,1,0:T(8,128)}, f32[8,9,128]{2,1,0:T(8,128)}, u32[]{:S(2)}, u32[]{:S(2)}) collective-permute-start(f32[8,9,128]{2,1,0:T(8,128)} %maximum_select_fusion.2), channel_id=1, source_target_pairs={{0,8},{1,9},{2,10},{3,11},{4,12},{5,13},{6,14},{7,15},{8,0},{9,1},... | collective-permute-start | bytes 110600 | tf_op jit(solution)/shard_map/ppermute | solution.py:67
  57.9 27.2 %collective-permute-start.15 = (f32[256,256]{1,0:T(8,128)}, f32[256,256]{1,0:T(8,128)}, u32[]{:S(2)}, u32[]{:S(2)}) collective-permute-start(f32[256,256]{1,0:T(8,128)} %bitcast.96), channel_id=1, source_target_pairs={{0,16},{1,2},{2,1},{3,19},{4,20},{5,6},{6,5},{7,23},{8,24},{9,10},... | collective-permute-start | bytes 786440 | tf_op jit(solution)/shard_map/ppermute | solution.py:67
  64.0 5.9 %collective-permute-start.19 = (f32[128,256]{1,0:T(8,128)}, f32[128,256]{1,0:T(8,128)S(1)}, u32[]{:S(2)}, u32[]{:S(2)}) collective-permute-start(f32[128,256]{1,0:T(8,128)} %get-tuple-element.135), channel_id=1, source_target_pairs={{0,16},{1,4},{2,18},{3,6},{4,1},{5,8},{6,3},{7,10},{8,5},{9,12},{1... | collective-permute-start | bytes 393224 | tf_op jit(solution)/shard_map/ppermute | solution.py:67
  64.8 5.1 %collective-permute-start.20 = (f32[128,256]{1,0:T(8,128)}, f32[128,256]{1,0:T(8,128)S(1)}, u32[]{:S(2)}, u32[]{:S(2)}) collective-permute-start(f32[128,256]{1,0:T(8,128)} %get-tuple-element.136), channel_id=1, source_target_pairs={{0,1},{1,0},{2,3},{3,2},{4,5},{5,4},{6,7},{7,6},{8,9},{9,8},{10,11... | collective-permute-start | bytes 393224 | tf_op jit(solution)/shard_map/ppermute | solution.py:67
  73.3 6.7 %collective-permute-start.25 = (f32[128,256]{1,0:T(8,128)S(1)}, f32[128,256]{1,0:T(8,128)S(1)}, u32[]{:S(2)}, u32[]{:S(2)}) collective-permute-start(f32[128,256]{1,0:T(8,128)S(1)} %get-tuple-element.138), channel_id=1, source_target_pairs={{0,16},{1,4},{2,18},{3,6},{4,1},{5,8},{6,3},{7,10},{8,5},{9,12},{1... | collective-permute-start | bytes 393224 | tf_op jit(solution)/shard_map/ppermute | solution.py:67
  75.3 4.7 %collective-permute-start.26 = (f32[128,256]{1,0:T(8,128)S(1)}, f32[128,256]{1,0:T(8,128)S(1)}, u32[]{:S(2)}, u32[]{:S(2)}) collective-permute-start(f32[128,256]{1,0:T(8,128)S(1)} %get-tuple-element.147), channel_id=1, source_target_pairs={{0,1},{1,0},{2,3},{3,2},{4,5},{5,4},{6,7},{7,6},{8,9},{9,8},{10,11... | collective-permute-start | bytes 393224 | tf_op jit(solution)/shard_map/ppermute | solution.py:67
  76.4 18.4 %collective-permute-start.23 = (f32[128,256]{1,0:T(8,128)}, f32[128,256]{1,0:T(8,128)}, u32[]{:S(2)}, u32[]{:S(2)}) collective-permute-start(f32[128,256]{1,0:T(8,128)} %get-tuple-element.143), channel_id=1, source_target_pairs={{0,1},{1,0},{2,3},{3,2},{4,5},{5,4},{6,7},{7,6},{8,9},{9,8},{10,11... | collective-permute-start | bytes 393224 | tf_op jit(solution)/shard_map/ppermute | solution.py:67
  78.4 16.3 %collective-permute-start.22 = (f32[128,256]{1,0:T(8,128)}, f32[128,256]{1,0:T(8,128)}, u32[]{:S(2)}, u32[]{:S(2)}) collective-permute-start(f32[128,256]{1,0:T(8,128)} %get-tuple-element.141), channel_id=1, source_target_pairs={{0,16},{1,4},{2,18},{3,6},{4,1},{5,8},{6,3},{7,10},{8,5},{9,12},{1... | collective-permute-start | bytes 393224 | tf_op jit(solution)/shard_map/ppermute | solution.py:67
  83.4 8.9 %collective-permute-start.28 = (f32[128,256]{1,0:T(8,128)}, f32[128,256]{1,0:T(8,128)}, u32[]{:S(2)}, u32[]{:S(2)}) collective-permute-start(f32[128,256]{1,0:T(8,128)} %get-tuple-element.150), channel_id=1, source_target_pairs={{0,16},{1,4},{2,18},{3,6},{4,1},{5,8},{6,3},{7,10},{8,5},{9,12},{1... | collective-permute-start | bytes 393224 | tf_op jit(solution)/shard_map/ppermute | solution.py:67
  83.5 8.8 %collective-permute-start.29 = (f32[128,256]{1,0:T(8,128)}, f32[128,256]{1,0:T(8,128)}, u32[]{:S(2)}, u32[]{:S(2)}) collective-permute-start(f32[128,256]{1,0:T(8,128)} %get-tuple-element.151), channel_id=1, source_target_pairs={{0,1},{1,0},{2,3},{3,2},{4,5},{5,4},{6,7},{7,6},{8,9},{9,8},{10,11... | collective-permute-start | bytes 393224 | tf_op jit(solution)/shard_map/ppermute | solution.py:67
  88.9 5.8 %collective-permute-start.24 = (f32[32,256]{1,0:T(8,128)}, f32[32,256]{1,0:T(8,128)S(1)}, u32[]{:S(2)}, u32[]{:S(2)}) collective-permute-start(f32[32,256]{1,0:T(8,128)} %get-tuple-element.145), channel_id=1, source_target_pairs={{0,2},{1,3},{2,0},{3,1},{4,6},{5,7},{6,4},{7,5},{8,10},{9,11},{10,... | collective-permute-start | bytes 98312 | tf_op jit(solution)/shard_map/ppermute | solution.py:67
  96.9 4.8 %collective-permute-start.35 = (f32[128,256]{1,0:T(8,128)S(1)}, f32[128,256]{1,0:T(8,128)S(1)}, u32[]{:S(2)}, u32[]{:S(2)}) collective-permute-start(f32[128,256]{1,0:T(8,128)S(1)} %get-tuple-element.160), channel_id=1, source_target_pairs={{0,16},{1,4},{2,18},{3,6},{4,1},{5,8},{6,3},{7,10},{8,5},{9,12},{1... | collective-permute-start | bytes 393224 | tf_op jit(solution)/shard_map/ppermute | solution.py:67
  97.4 4.2 %collective-permute-start.36 = (f32[128,256]{1,0:T(8,128)S(1)}, f32[128,256]{1,0:T(8,128)S(1)}, u32[]{:S(2)}, u32[]{:S(2)}) collective-permute-start(f32[128,256]{1,0:T(8,128)S(1)} %get-tuple-element.161), channel_id=1, source_target_pairs={{0,1},{1,0},{2,3},{3,2},{4,5},{5,4},{6,7},{7,6},{8,9},{9,8},{10,11... | collective-permute-start | bytes 393224 | tf_op jit(solution)/shard_map/ppermute | solution.py:67
  103.3 5.4 %collective-permute-start.38 = (f32[128,256]{1,0:T(8,128)S(1)}, f32[128,256]{1,0:T(8,128)S(1)}, u32[]{:S(2)}, u32[]{:S(2)}) collective-permute-start(f32[128,256]{1,0:T(8,128)S(1)} %get-tuple-element.166), channel_id=1, source_target_pairs={{0,16},{1,4},{2,18},{3,6},{4,1},{5,8},{6,3},{7,10},{8,5},{9,12},{1... | collective-permute-start | bytes 393224 | tf_op jit(solution)/shard_map/ppermute | solution.py:67
  104.3 4.4 %collective-permute-start.39 = (f32[128,256]{1,0:T(8,128)S(1)}, f32[128,256]{1,0:T(8,128)S(1)}, u32[]{:S(2)}, u32[]{:S(2)}) collective-permute-start(f32[128,256]{1,0:T(8,128)S(1)} %get-tuple-element.167), channel_id=1, source_target_pairs={{0,1},{1,0},{2,3},{3,2},{4,5},{5,4},{6,7},{7,6},{8,9},{9,8},{10,11... | collective-permute-start | bytes 393224 | tf_op jit(solution)/shard_map/ppermute | solution.py:67
  110.5 5.0 %collective-permute-start.41 = (f32[128,256]{1,0:T(8,128)S(1)}, f32[128,256]{1,0:T(8,128)S(1)}, u32[]{:S(2)}, u32[]{:S(2)}) collective-permute-start(f32[128,256]{1,0:T(8,128)S(1)} %get-tuple-element.172), channel_id=1, source_target_pairs={{0,16},{1,4},{2,18},{3,6},{4,1},{5,8},{6,3},{7,10},{8,5},{9,12},{1... | collective-permute-start | bytes 393224 | tf_op jit(solution)/shard_map/ppermute | solution.py:67
  110.9 4.7 %collective-permute-start.42 = (f32[128,256]{1,0:T(8,128)S(1)}, f32[128,256]{1,0:T(8,128)S(1)}, u32[]{:S(2)}, u32[]{:S(2)}) collective-permute-start(f32[128,256]{1,0:T(8,128)S(1)} %get-tuple-element.173), channel_id=1, source_target_pairs={{0,1},{1,0},{2,3},{3,2},{4,5},{5,4},{6,7},{7,6},{8,9},{9,8},{10,11... | collective-permute-start | bytes 393224 | tf_op jit(solution)/shard_map/ppermute | solution.py:67
  117.2 5.0 %collective-permute-start.44 = (f32[128,256]{1,0:T(8,128)S(1)}, f32[128,256]{1,0:T(8,128)S(1)}, u32[]{:S(2)}, u32[]{:S(2)}) collective-permute-start(f32[128,256]{1,0:T(8,128)S(1)} %get-tuple-element.178), channel_id=1, source_target_pairs={{0,16},{1,4},{2,18},{3,6},{4,1},{5,8},{6,3},{7,10},{8,5},{9,12},{1... | collective-permute-start | bytes 393224 | tf_op jit(solution)/shard_map/ppermute | solution.py:67
  117.9 4.3 %collective-permute-start.45 = (f32[128,256]{1,0:T(8,128)S(1)}, f32[128,256]{1,0:T(8,128)S(1)}, u32[]{:S(2)}, u32[]{:S(2)}) collective-permute-start(f32[128,256]{1,0:T(8,128)S(1)} %get-tuple-element.179), channel_id=1, source_target_pairs={{0,1},{1,0},{2,3},{3,2},{4,5},{5,4},{6,7},{7,6},{8,9},{9,8},{10,11... | collective-permute-start | bytes 393224 | tf_op jit(solution)/shard_map/ppermute | solution.py:67
  123.8 5.0 %collective-permute-start.47 = (f32[128,256]{1,0:T(8,128)S(1)}, f32[128,256]{1,0:T(8,128)S(1)}, u32[]{:S(2)}, u32[]{:S(2)}) collective-permute-start(f32[128,256]{1,0:T(8,128)S(1)} %get-tuple-element.184), channel_id=1, source_target_pairs={{0,16},{1,4},{2,18},{3,6},{4,1},{5,8},{6,3},{7,10},{8,5},{9,12},{1... | collective-permute-start | bytes 393224 | tf_op jit(solution)/shard_map/ppermute | solution.py:67
  124.6 4.3 %collective-permute-start.48 = (f32[128,256]{1,0:T(8,128)S(1)}, f32[128,256]{1,0:T(8,128)S(1)}, u32[]{:S(2)}, u32[]{:S(2)}) collective-permute-start(f32[128,256]{1,0:T(8,128)S(1)} %get-tuple-element.185), channel_id=1, source_target_pairs={{0,1},{1,0},{2,3},{3,2},{4,5},{5,4},{6,7},{7,6},{8,9},{9,8},{10,11... | collective-permute-start | bytes 393224 | tf_op jit(solution)/shard_map/ppermute | solution.py:67
  131.8 5.2 %collective-permute-start.50 = (f32[128,256]{1,0:T(8,128)S(1)}, f32[128,256]{1,0:T(8,128)S(1)}, u32[]{:S(2)}, u32[]{:S(2)}) collective-permute-start(f32[128,256]{1,0:T(8,128)S(1)} %get-tuple-element.190), channel_id=1, source_target_pairs={{0,16},{1,4},{2,18},{3,6},{4,1},{5,8},{6,3},{7,10},{8,5},{9,12},{1... | collective-permute-start | bytes 393224 | tf_op jit(solution)/shard_map/ppermute | solution.py:67
  132.5 5.1 %collective-permute-start.51 = (f32[128,256]{1,0:T(8,128)S(1)}, f32[128,256]{1,0:T(8,128)S(1)}, u32[]{:S(2)}, u32[]{:S(2)}) collective-permute-start(f32[128,256]{1,0:T(8,128)S(1)} %get-tuple-element.191), channel_id=1, source_target_pairs={{0,1},{1,0},{2,3},{3,2},{4,5},{5,4},{6,7},{7,6},{8,9},{9,8},{10,11... | collective-permute-start | bytes 393224 | tf_op jit(solution)/shard_map/ppermute | solution.py:67
  145.0 5.2 %collective-permute-start.53 = (f32[128,256]{1,0:T(8,128)}, f32[128,256]{1,0:T(8,128)S(1)}, u32[]{:S(2)}, u32[]{:S(2)}) collective-permute-start(f32[128,256]{1,0:T(8,128)} %get-tuple-element.196), channel_id=1, source_target_pairs={{0,16},{1,4},{2,18},{3,6},{4,1},{5,8},{6,3},{7,10},{8,5},{9,12},{1... | collective-permute-start | bytes 393224 | tf_op jit(solution)/shard_map/ppermute | solution.py:67
  145.7 5.1 %collective-permute-start.54 = (f32[128,256]{1,0:T(8,128)}, f32[128,256]{1,0:T(8,128)S(1)}, u32[]{:S(2)}, u32[]{:S(2)}) collective-permute-start(f32[128,256]{1,0:T(8,128)} %get-tuple-element.197), channel_id=1, source_target_pairs={{0,1},{1,0},{2,3},{3,2},{4,5},{5,4},{6,7},{7,6},{8,9},{9,8},{10,11... | collective-permute-start | bytes 393224 | tf_op jit(solution)/shard_map/ppermute | solution.py:67
  158.1 6.1 %collective-permute-start.62 = (f32[256,256]{1,0:T(8,128)S(1)}, f32[256,256]{1,0:T(8,128)S(1)}, u32[]{:S(2)}, u32[]{:S(2)}) collective-permute-start(f32[256,256]{1,0:T(8,128)S(1)} %get-tuple-element.195.cur), channel_id=1, source_target_pairs={{0,16},{1,2},{2,1},{3,19},{4,20},{5,6},{6,5},{7,23},{8,24},{9,10},... | collective-permute-start | bytes 786440 | tf_op jit(solution)/shard_map/ppermute | solution.py:67
  159.7 17.0 %collective-permute-start.61 = (f32[256,256]{1,0:T(8,128)S(1)}, f32[256,256]{1,0:T(8,128)S(1)}, u32[]{:S(2)}, u32[]{:S(2)}) collective-permute-start(f32[256,256]{1,0:T(8,128)S(1)} %get-tuple-element.202), channel_id=1, source_target_pairs={{0,16},{1,2},{2,1},{3,19},{4,20},{5,6},{6,5},{7,23},{8,24},{9,10},... | collective-permute-start | bytes 786440 | tf_op jit(solution)/shard_map/ppermute | solution.py:67
  160.1 8.5 %collective-permute-start.57 = (f32[2,32,256]{2,1,0:T(8,128)S(1)}, f32[2,32,256]{2,1,0:T(8,128)S(1)}, u32[]{:S(2)}, u32[]{:S(2)}) collective-permute-start(f32[2,32,256]{2,1,0:T(8,128)S(1)} %get-tuple-element.203), channel_id=1, source_target_pairs={{0,0},{1,2},{2,1},{3,3},{4,4},{5,6},{6,5},{7,7},{8,8},{9,10},{10,9... | collective-permute-start | bytes 196616 | tf_op jit(solution)/shard_map/ppermute | solution.py:67
  163.4 6.5 %collective-permute-start.58 = (f32[2,32,256]{2,1,0:T(8,128)S(1)}, f32[2,32,256]{2,1,0:T(8,128)S(1)}, u32[]{:S(2)}, u32[]{:S(2)}) collective-permute-start(f32[2,32,256]{2,1,0:T(8,128)S(1)} %get-tuple-element.206), channel_id=1, source_target_pairs={{0,4},{1,6},{2,5},{3,7},{4,8},{5,10},{6,9},{7,11},{8,12},{9,14},{1... | collective-permute-start | bytes 196616 | tf_op jit(solution)/shard_map/ppermute | solution.py:67
  163.5 6.4 %collective-permute-start.59 = (f32[2,32,256]{2,1,0:T(8,128)S(1)}, f32[2,32,256]{2,1,0:T(8,128)S(1)}, u32[]{:S(2)}, u32[]{:S(2)}) collective-permute-start(f32[2,32,256]{2,1,0:T(8,128)S(1)} %get-tuple-element.205), channel_id=1, source_target_pairs={{0,8},{1,10},{2,9},{3,11},{4,12},{5,14},{6,13},{7,15},{8,0},{9,2},... | collective-permute-start | bytes 196616 | tf_op jit(solution)/shard_map/ppermute | solution.py:67
  164.1 6.4 %collective-permute-start.60 = (f32[2,32,256]{2,1,0:T(8,128)S(1)}, f32[2,32,256]{2,1,0:T(8,128)S(1)}, u32[]{:S(2)}, u32[]{:S(2)}) collective-permute-start(f32[2,32,256]{2,1,0:T(8,128)S(1)} %get-tuple-element.204), channel_id=1, source_target_pairs={{0,12},{1,14},{2,13},{3,15},{4,0},{5,2},{6,1},{7,3},{8,4},{9,6},{1... | collective-permute-start | bytes 196616 | tf_op jit(solution)/shard_map/ppermute | solution.py:67
  (74 other events, 178.9 us)

commit v2 on v1

--- a/solution.py
+++ b/solution.py
@@ -150,10 +150,10 @@
     yo[...] = jnp.where(flags[1] == 0, new[size - 4 * COLS :], new[0 : 4 * COLS])
 
 
-def settle_kernel(rim_count, flags, a, b, recv, a_out, b_out, *outs):
+def settle_kernel(rim_count, flags, a, b, recv_a, recv_b, a_out, b_out, *outs):
     keep = flags[0] == flags[1]
-    for n, (own, out) in enumerate(((a, a_out), (b, b_out))):
-        out[...] = jnp.where(keep, own[...], recv[n])
+    for n, (own, recv, out) in enumerate(((a, recv_a, a_out), (b, recv_b, b_out))):
+        out[...] = jnp.where(keep, own[...], recv[...])
         if n < rim_count:
             rims(flags, out, *(ref.at[n] for ref in outs))
 
@@ -201,46 +201,120 @@
     rims(flags, new, zo, co, yo)
 
 
-def adjoint_kernel(t, last, flags, cur, prev, k0, ki, kx, kz, zm, cm, ym, near, deep, pnext,
-                   change_in, image, rrow, rrow_c, rz, obs, extra, new, image_out, *outs):
-    size, depth = cur.shape
-    n = rrow.shape[1]
-    spot = lax.broadcasted_iota(jnp.int32, (size, n), 0) == rrow[...]
-    spot = spot.astype(F32).astype(BF16)
-    pick = lax.broadcasted_iota(jnp.int32, (n, size), 1) == rrow_c[...]
-    pick = pick.astype(F32).astype(BF16)
+def merge_kernel(stage, flags, mine, got, out):
+    n = mine.shape[0]
+    bit = flags[4 + stage]
+    out[pl.ds(bit * n, n)] = mine[...]
+    out[pl.ds((1 - bit) * n, n)] = got[...]
+
+
+def lists_kernel(flags, lists, spot, pick, at, obs):
+    size, n = spot.shape
+    depth = at.shape[1]
+    steps = obs.shape[1]
+    sub = flags[2]
+    cell = lists[sub, steps : steps + 1, :]
+    along = jnp.floor((cell + 0.5) * (1.0 / depth))
+    same = lax.broadcasted_iota(jnp.int32, (n, n), 0) == lax.broadcasted_iota(jnp.int32, (n, n), 1)
+
+    def column(row):
+        return jnp.sum(jnp.where(same, row, 0.0), axis=1, keepdims=True).astype(jnp.int32)
+
+    hot = lax.broadcasted_iota(jnp.int32, (size, n), 0) == along.astype(jnp.int32)
+    spot[...] = hot.astype(F32).astype(BF16)
+    hot = lax.broadcasted_iota(jnp.int32, (n, size), 1) == column(along)
+    pick[...] = hot.astype(F32).astype(BF16)
+    hot = lax.broadcasted_iota(jnp.int32, (n, depth), 1) == column(cell - along * depth)
+    at[...] = hot.astype(F32)
+    subs = lists.shape[0]
+    chosen = lax.broadcasted_iota(jnp.int32, (CAP, n), 1) == (
+        sub * CAP + lax.broadcasted_iota(jnp.int32, (CAP, n), 0))
+    chosen = chosen.astype(F32).astype(BF16)
+    traces = lists[:, 0:steps, :].reshape(subs * steps, n)
+    high, mid = split(traces)
+    low = (traces - high.astype(F32) - mid.astype(F32)).astype(BF16)
+    sent = sum(
+        lax.dot_general(chosen, part, (((1,), (1,)), ((), ())), preferred_element_type=F32)
+        for part in (low, mid, high))
+    for s in range(subs):
+        obs[s * CAP : s * CAP + CAP, :] = sent[:, s * steps : s * steps + steps]
+
+
+def adjoint_kernel(t, first, last, flags, cur, prev, k0, ki, kx, kz, zm, cm, ym, near, deep, pnext,
+                   change_in, spot, pick, at, obs, *rest):
+    rest = list(rest)
+    image = None if first else rest.pop(0)
+    vel, recv = (rest.pop(0), rest.pop(0)) if last else (None, None)
+    new, image_out, *outs = rest
     high, low = split(pnext[...])
-    at = lax.broadcasted_iota(jnp.int32, (n, depth), 1) == rz[...]
-    seen = jnp.where(at, mm(pick, high) + mm(pick, low), 0.0)
+    seen = at[...] * (mm(pick[...], high) + mm(pick[...], low))
     residual = jnp.sum(seen, axis=1, keepdims=True) - obs[:, t : t + 1]
-    high, low = split(jnp.where(at, residual, 0.0))
-    inj = mm(spot, high) + mm(spot, low)
+    high, low = split(at[...] * residual)
+    inj = mm(spot[...], high) + mm(spot[...], low)
     scale = 2.0 / obs.shape[1]
+    raw = []
 
     def finish(here, value, change):
         new[here] = value
         total = value * change_in[here]
-        if image is not None:
+        if not first:
             total = total + image[here]
         if last:
-            total = total * scale / extra[here]
-        image_out[here] = total
+            raw.append(total * scale / vel[here])
+        else:
+            image_out[here] = total
 
     advance(flags, cur, prev, k0, ki, kx, kz, zm, cm, ym, near, deep, inj, finish)
     if not last:
         rims(flags, new, *outs)
-
-
-def first_adjoint_kernel(t, last, *refs):
-    adjoint_kernel(t, last, *refs[:14], None, *refs[14:])
-
-
-def middle(kernel):
-    def run(t, last, *refs):
-        n = 18 if kernel is first_adjoint_kernel else 19
-        kernel(t, last, *refs[:n], None, *refs[n:])
-
-    return run
+        return
+    raw = jnp.concatenate(raw, axis=0)
+    parts, height, lanes = image_out.shape
+    chunk = cur.shape[1] // parts
+    for n in range(parts):
+        image_out[n] = jnp.concatenate(
+            [raw[g * height : g * height + height, n * chunk : n * chunk + chunk]
+             for g in range(lanes // chunk)], axis=1)
+    outs[0][...] = jnp.where(flags[0] == flags[1], cur[...], recv[...])
+
+
+def pair_kernel(flags, parts, mine, other):
+    for n in range(mine.shape[0]):
+        mine[n] = parts[2 * n + flags[0]]
+        other[n] = parts[2 * n + 1 - flags[0]]
+
+
+def join_kernel(flags, mine, got, *outs):
+    count = len(outs)
+    for s, out in enumerate(outs):
+        to = flags[3] + s
+        to = jnp.where(to >= count, to - count, to)
+        a, b = mine[to], got[to]
+        out[0] = jnp.where(flags[0] == 0, a, b)
+        out[1] = jnp.where(flags[0] == 0, b, a)
+
+
+def filter_kernel(flags, *refs):
+    pieces, out = refs[:-1], refs[-1]
+    height, lanes = pieces[0].shape[1:]
+    chunk, rows, full = out.shape
+    groups = lanes // chunk
+    q = flags[3]
+    shape = (full, full)
+    y = lax.broadcasted_iota(jnp.int32, shape, 1)
+    at = lax.broadcasted_iota(jnp.int32, shape, 0)
+    within = jnp.bitwise_and(at, 2 * COLS - 1)
+    place = q * (2 * COLS) - (at - within)
+    place = jnp.where(place < 0, place + full, place) + within
+    weights = jnp.exp(jnp.abs(y - place).astype(F32) * (-1.0 / SMOOTH))
+    weights = split(weights / jnp.sum(weights, axis=0, keepdims=True))
+    for n in range(height // COLS):
+        here = slice(n * COLS, n * COLS + COLS)
+        lines = jnp.concatenate([piece[b, here, :] for piece in pieces for b in range(2)], axis=0)
+        high, low = split(lines.T)
+        done = mm(high, weights[0]) + mm(low, weights[0]) + mm(high, weights[1])
+        for g in range(groups):
+            out[:, g * (rows // groups) + n, :] = done[g * chunk : g * chunk + chunk]
 
 
 def shaped(*shape):
@@ -272,7 +346,10 @@
     q, y = xline // 2, xline % 2
     keep = y == c
     z_perm, c_perm, y_perm, swap_perm = plan.z(), plan.core(), plan.y(), plan.swap()
-    flags = jnp.stack([c, y]).astype(jnp.int32)
+    stages = [(c_perm, c), (y_perm, y)]
+    stages += [(plan.flip(1 << b), (q >> b) & 1) for b in range((nq - 1).bit_length())]
+    sub = (2 * q + c) * 2 + y
+    flags = jnp.stack([c, y, sub, q] + [bit for pairs, bit in stages]).astype(jnp.int32)
     field = shaped(size, depth)
     side, edge = (size // 2, depth), (4 * cols, depth)
     rim = [shaped(*side), shaped(*side), shaped(*edge)]
@@ -299,14 +376,13 @@
 
     log_density, fwd_now, velocity = flat(log_density), flat(fwd_now), flat(velocity)
     fwd_before, adj_now, adj_before = flat(fwd_before), flat(adj_now), flat(adj_before)
-    first = send(jnp.stack([log_density, fwd_now]), swap_perm)
-    second = send(jnp.stack([velocity, fwd_before]), swap_perm)
+    got = [send(v, swap_perm) for v in (log_density, fwd_now, velocity, fwd_before)]
     density, p_now, *out = call(
         functools.partial(settle_kernel, 2), "settle",
-        [field, field] + [shaped(2, *r.shape) for r in rim], flags, log_density, fwd_now, first)
+        [field, field] + [shaped(2, *r.shape) for r in rim], flags, log_density, fwd_now, *got[:2])
     zm, cm, ym = halo(*out)
     vel, p_before = call(functools.partial(settle_kernel, 0), "settle_model", [field, field],
-                         flags, velocity, fwd_before, second)
+                         flags, velocity, fwd_before, *got[2:])
     model = call(model_kernel, "model", [field] * 4, flags, density, zm, cm, ym, near, deep, vel)
     halos = (zm[1], cm[1], ym[1])
 
@@ -321,8 +397,7 @@
     live = jnp.arange(CAP)[None, :] < rec_counts[0][:, None]
     cells = jnp.where(live.reshape(-1), rec_cells[0], -1)
     lists = jnp.concatenate([observed, cells[None, :].astype(F32)], axis=0)[None]
-    stages = [(c_perm, c), (y_perm, y)]
-    stages += [(plan.flip(1 << b), (q >> b) & 1) for b in range((nq - 1).bit_length())]
+    share = -(-len(stages) // (steps - 2))
 
     states, changes = [], []
     for t in range(steps):
@@ -331,10 +406,10 @@
             flags, p_now, p_before, *model, *halos, near, deep, srow, sz, wave)
         if t < steps - 1:
             halos = halo(*out)
-        share = -(-len(stages) // (steps - 2))
-        for pairs, bit in stages[t * share : t * share + share]:
-            got = send(after(lists, out[0]), pairs)
-            lists = jnp.where(bit == 0, jnp.concatenate([lists, got]), jnp.concatenate([got, lists]))
+        for n in range(t * share, min(t * share + share, len(stages))):
+            moved = send(after(lists, out[0]) if n else lists, stages[n][0])
+            lists, = call(functools.partial(merge_kernel, n), "merge",
+                          [shaped(2 * lists.shape[0], *lists.shape[1:])], flags, lists, moved)
         if t == 1:
             got_now = send(after(adj_now, out[0]), swap_perm)
         if t == 3:
@@ -351,58 +426,42 @@
         states.append(p_next)
         changes.append(change)
 
-    sub = (2 * q + c) * 2 + y
-    mine = lax.dynamic_index_in_dim(lists, sub, 0, keepdims=False)[steps].astype(jnp.int32)
-    traces = lax.dynamic_slice(lists, (0, 0, sub * CAP), (subs, steps, CAP))
-    obs = traces.transpose(0, 2, 1).reshape(subs * CAP, steps)
-    rrow = jnp.where(mine < 0, -1, mine // depth)
-    rz = (mine % depth)[:, None]
+    slots = subs * CAP
+    receivers = call(
+        lists_kernel, "lists",
+        [jax.ShapeDtypeStruct((size, slots), BF16), jax.ShapeDtypeStruct((slots, size), BF16),
+         shaped(slots, depth), shaped(slots, steps)], flags, lists)
 
     halos = u_halos
-    image = None
+    image = ()
+    chunk = depth // nx
+    packed = shaped(nx, size * chunk // 128, 128)
     for j in range(steps):
         t = steps - 1 - j
         last = j == steps - 1
-        args = [flags, u_now, u_before, *model, *halos, near, deep, states[t], changes[t]]
-        kernel = adjoint_kernel
-        if j == 0:
-            kernel = first_adjoint_kernel
-        else:
-            args.append(image)
-        args += [rrow[None, :], rrow[:, None], rz, obs]
+        args = [flags, u_now, u_before, *model, *halos, near, deep, states[t], changes[t],
+                *receivers, *image]
+        outs = [field, field] + rim
         if last:
-            args.append(vel)
-        else:
-            kernel = middle(kernel)
-        outs = call(functools.partial(kernel, t, last), "adjoint",
-                    [field, field] + ([] if last else rim), *args)
-        u_before, u_now = u_now, outs[0]
-        image = outs[1]
+            args += [vel, send(u_now, swap_perm)]
+            outs = [field, packed, field]
+        u_before = u_now
+        u_now, *outs = call(functools.partial(adjoint_kernel, t, j == 0, last), "adjoint", outs, *args)
+        image = outs[:1]
         if not last:
-            halos = halo(*outs[2:])
-
-    chunk = depth // nx
-    raw = image.T.reshape(nq, 2, chunk, size)
-    own = lax.dynamic_index_in_dim(raw, c, 1, keepdims=False)
-    other = send(lax.dynamic_index_in_dim(raw, 1 - c, 1, keepdims=False), c_perm)
-    both = jnp.where(c == 0, jnp.stack([own, other], 1), jnp.stack([other, own], 1))
-    pieces = [
-        send(lax.dynamic_index_in_dim(both, (q + s) % nq, 0, keepdims=False), plan.spread(s))
-        for s in range(nq)
-    ]
+            halos = halo(*outs[1:])
+    raw, adj_prev = outs
+
+    half = shaped(nq, *packed.shape[1:])
+    mine, other = call(pair_kernel, "pair", [half, half], flags, raw)
+    piece = shaped(2, *packed.shape[1:])
+    pieces = call(join_kernel, "join", [piece] * nq, flags, mine, send(other, c_perm))
+    got = send(after(u_now, pieces[0]), swap_perm)
+    pieces = [send(value, plan.spread(s)) for s, value in enumerate(pieces)]
+    gradient, = call(filter_kernel, "filter", [shaped(chunk, rows, nx * cols)], flags, *pieces)
+    adj_out = jnp.where(keep, u_now, got)
     block = (rows, cols, depth)
-    adj_out = jnp.where(keep, u_now, send(u_now, swap_perm)).reshape(block)
-    adj_prev = jnp.where(keep, u_before, send(u_before, swap_perm)).reshape(block)
-
-    pieces = jnp.stack(pieces).reshape(2 * nq, chunk, rows, cols)
-    lines = jnp.arange(nx * cols)
-    from_q = (q - jnp.arange(nq)) % nq
-    places = (from_q[:, None] * (2 * cols) + jnp.arange(2 * cols)[None, :]).reshape(-1)
-    weights = jnp.exp(-jnp.abs(lines[:, None] - places[None, :]).astype(F32) / SMOOTH)
-    weights = weights / jnp.sum(weights, axis=1, keepdims=True)
-    gradient = jnp.einsum("jzix,yjx->ziy", pieces, weights.reshape(-1, 2 * nq, cols),
-                          precision=lax.Precision.HIGHEST)
-    return gradient, adj_out, adj_prev
+    return gradient, adj_out.reshape(block), adj_prev.reshape(block)
 
 
 def solution(mesh):

time: 178 us -> 163 us (0.916)
  local copies, waits for them, and re-layouts: 29.3 us -> 2.49 us
  waiting for transfers between devices: 36.8 us -> 54.1 us
  other arithmetic: 7.34 us -> 1.96 us
  matrix products: 3.84 us -> 0 us
  starting transfers between devices: 63.8 us -> 67.4 us
    unnamed x119 -> x39, local copies, waits for them, and re-layouts: 24.1 us -> 2.2 us
    ppermute x63 -> x65, waiting for transfers between devices: 36.8 us -> 54.1 us  [send(): return lax.ppermute(value, ALL, pairs)]
    dot_general x1 -> x0, matrix products: 3.84 us -> none  [per_device(): jnp.einsum('jzix,yjx->ziy', pieces, weights.reshape(-1, 2 * nq, cols), pr...]
    ppermute x63 -> x65, starting transfers between devices: 63.8 us -> 67.4 us  [send(): return lax.ppermute(value, ALL, pairs)]
    select_n x7 -> x0, other arithmetic: 3.31 us -> none  [the longest x4 3.22 us: per_device(): jnp.where(bit == 0, jnp.concatenate([lists, got]), jnp.concatenate([got,...]
    another operation x4 -> x0, other arithmetic: 2.04 us -> none  [the longest x1 1.12 us: per_device(): first = send(jnp.stack([log_density, fwd_now]), swap_perm)]
    reshape x1 -> x0, local copies, waits for them, and re-layouts: 1.83 us -> none  [per_device(): pieces = jnp.stack(pieces).reshape(2 * nq, chunk, rows, cols)]
    pallas_call x21 -> x29, Pallas kernels: 35 us -> 35.7 us  [call(): pl.pallas_call(kernel, name=name, out_shape=outs, in_specs=specs, out_spe...]
  transfers between devices with their start and end apart: 63 -> 65, of which waited for: 22 -> 27; matrix products, arithmetic and copies ran while one was open for 8% -> 1% of each run, Pallas kernels for 9% -> 9%
where the time goes in v2:
time: 163 us
  starting transfers between devices  67.4 us (41%)
  waiting for transfers between devices  54.1 us (33%)
  Pallas kernels  35.7 us (22%)
  local copies, waits for them, and re-layouts  2.49 us (2%)
  other arithmetic  1.96 us (1%)
    ppermute x65, starting transfers between devices, send(): return lax.ppermute(value, ALL, pairs)  67.4 us
    ppermute x65, waiting for transfers between devices, send(): return lax.ppermute(value, ALL, pairs)  54.1 us
    pallas_call x29, Pallas kernels, call(): pl.pallas_call(kernel, name=name, out_shape=outs, in_specs=specs, out_spe...  35.7 us
  transfers between devices with their start and end apart: 65, of which 27 were waited for; matrix products, arithmetic and copies ran while one was open for 1% of the time, Pallas kernels for 9%

profile of v2, /device:TPU:1, one launch (start us, length us, event | category | flops | bytes accessed | tf_op | source)
XLA Modules:
  0.0 162.8 jit_solution(16435441325537426258)
XLA Ops:
  0.6 2.7 %collective-permute-start.1 = (f32[256,256]{1,0:T(8,128)}, f32[256,256]{1,0:T(8,128)S(1)}, u32[]{:S(2)}, u32[]{:S(2)}) collective-permute-start(f32[256,256]{1,0:T(8,128)} %bitcast.41), channel_id=1, source_target_pairs={{0,16},{1,2},{2,1},{3,19},{4,20},{5,6},{6,5},{7,23},{8,24},{9,10},... | collective-permute-start | bytes 786440 | tf_op jit(solution)/shard_map/ppermute | solution.py:67
  3.4 1.7 %collective-permute-start.2 = (f32[256,256]{1,0:T(8,128)}, f32[256,256]{1,0:T(8,128)S(1)}, u32[]{:S(2)}, u32[]{:S(2)}) collective-permute-start(f32[256,256]{1,0:T(8,128)} %bitcast.43), channel_id=1, source_target_pairs={{0,16},{1,2},{2,1},{3,19},{4,20},{5,6},{6,5},{7,23},{8,24},{9,10},... | collective-permute-start | bytes 786440 | tf_op jit(solution)/shard_map/ppermute | solution.py:67
  7.9 8.4 %collective-permute-done.recv_a = f32[256,256]{1,0:T(8,128)S(1)} collective-permute-done((f32[256,256]{1,0:T(8,128)}, f32[256,256]{1,0:T(8,128)S(1)}, u32[]{:S(2)}, u32[]{:S(2)}) %collective-permute-start) | collective-permute-done | bytes 262176 | tf_op jit(solution)/shard_map/ppermute | solution.py:67
  18.3 2.4 %collective-permute-start.4 = (f32[2,128,256]{2,1,0:T(8,128)}, f32[2,128,256]{2,1,0:T(8,128)S(1)}, u32[]{:S(2)}, u32[]{:S(2)}) collective-permute-start(f32[2,128,256]{2,1,0:T(8,128)} %get-tuple-element.117), channel_id=1, source_target_pairs={{0,16},{1,4},{2,18},{3,6},{4,1},{5,8},{6,3},{7,10},{8,5},{9,12},{1... | collective-permute-start | bytes 786440 | tf_op jit(solution)/shard_map/ppermute | solution.py:67
  22.0 3.3 %collective-permute-done.4.zm = f32[2,128,256]{2,1,0:T(8,128)S(1)} collective-permute-done((f32[2,128,256]{2,1,0:T(8,128)}, f32[2,128,256]{2,1,0:T(8,128)S(1)}, u32[]{:S(2)}, u32[]{:S(2)}) %collective-permute-start.4) | collective-permute-done | bytes 262176 | tf_op jit(solution)/shard_map/ppermute | solution.py:67
  27.6 1.5 collective-permute-start.7
  30.8 2.3 %collective-permute-done.9.ym = f32[32,256]{1,0:T(8,128)S(1)} collective-permute-done((f32[32,256]{1,0:T(8,128)S(1)}, f32[32,256]{1,0:T(8,128)S(1)}, u32[]{:S(2)}, u32[]{:S(2)}) %collective-permute-start.9) | collective-permute-done | bytes 32800 | tf_op jit(solution)/shard_map/ppermute | solution.py:67
  36.9 2.3 %collective-permute-done.13.ym = f32[32,256]{1,0:T(8,128)S(1)} collective-permute-done((f32[32,256]{1,0:T(8,128)S(1)}, f32[32,256]{1,0:T(8,128)S(1)}, u32[]{:S(2)}, u32[]{:S(2)}) %collective-permute-start.13) | collective-permute-done | bytes 32800 | tf_op jit(solution)/shard_map/ppermute | solution.py:67
  43.3 2.3 %collective-permute-done.16.ym = f32[32,256]{1,0:T(8,128)S(1)} collective-permute-done((f32[32,256]{1,0:T(8,128)S(1)}, f32[32,256]{1,0:T(8,128)S(1)}, u32[]{:S(2)}, u32[]{:S(2)}) %collective-permute-start.16) | collective-permute-done | bytes 32800 | tf_op jit(solution)/shard_map/ppermute | solution.py:67
  46.3 1.9 %forward.11 = (f32[256,256]{1,0:T(8,128)S(1)}, f32[256,256]{1,0:T(8,128)S(1)}, f32[128,256]{1,0:T(8,128)}, f32[128,256]{1,0:T(8,128)}, f32[32,256]{1,0:T(8,128)S(1)}) custom-call(s32[8]{0:T(128)S(1)} %stack.29.flags, f32[256,256]{1,0:T(8,128)S(1)} %get-tuple-element.134.cur.prev.pnext, f32[256,256]{1,0:T(8,128)S(1)} %get-tuple-element.131.cur.prev.pnext, ...), custom_call_target="tpu_custom_call" | custom-call | flops 5000000 | bytes 2000000 | tf_op jit(solution)/shard_map/forward/pallas_call | solution.py:327
  53.1 2.3 %collective-permute-done.18.zm = f32[128,256]{1,0:T(8,128)} collective-permute-done((f32[128,256]{1,0:T(8,128)}, f32[128,256]{1,0:T(8,128)}, u32[]{:S(2)}, u32[]{:S(2)}) %collective-permute-start.18) | collective-permute-done | bytes 131104 | tf_op jit(solution)/shard_map/ppermute | solution.py:67
  55.3 1.6 forward.12
  57.8 1.6 collective-permute-start.22
  60.5 3.5 %collective-permute-done.21.zm = f32[128,256]{1,0:T(8,128)S(1)} collective-permute-done((f32[128,256]{1,0:T(8,128)S(1)}, f32[128,256]{1,0:T(8,128)S(1)}, u32[]{:S(2)}, u32[]{:S(2)}) %collective-permute-start.21) | collective-permute-done | bytes 131104 | tf_op jit(solution)/shard_map/ppermute | solution.py:67
  68.0 2.5 %collective-permute-done.34.got = f32[2,9,128]{2,1,0:T(8,128)S(1)} collective-permute-done((f32[2,9,128]{2,1,0:T(8,128)S(1)}, f32[2,9,128]{2,1,0:T(8,128)S(1)}, u32[]{:S(2)}, u32[]{:S(2)}) %collective-permute-start.34) | collective-permute-done | bytes 9248 | tf_op jit(solution)/shard_map/ppermute | solution.py:67
  72.2 1.7 %collective-permute-done.35.got = f32[4,9,128]{2,1,0:T(8,128)S(1)} collective-permute-done((f32[4,9,128]{2,1,0:T(8,128)S(1)}, f32[4,9,128]{2,1,0:T(8,128)S(1)}, u32[]{:S(2)}, u32[]{:S(2)}) %collective-permute-start.35) | collective-permute-done | bytes 18464 | tf_op jit(solution)/shard_map/ppermute | solution.py:67
  75.0 2.6 %collective-permute-done.29.ym = f32[32,256]{1,0:T(8,128)S(1)} collective-permute-done((f32[32,256]{1,0:T(8,128)S(1)}, f32[32,256]{1,0:T(8,128)S(1)}, u32[]{:S(2)}, u32[]{:S(2)}) %collective-permute-start.29) | collective-permute-done | bytes 32800 | tf_op jit(solution)/shard_map/ppermute | solution.py:67
  78.9 4.6 %collective-permute-start.30 = (f32[128,256]{1,0:T(8,128)S(1)}, f32[128,256]{1,0:T(8,128)S(1)}, u32[]{:S(2)}, u32[]{:S(2)}) collective-permute-start(f32[128,256]{1,0:T(8,128)S(1)} %get-tuple-element.161), channel_id=1, source_target_pairs={{0,16},{1,4},{2,18},{3,6},{4,1},{5,8},{6,3},{7,10},{8,5},{9,12},{1... | collective-permute-start | bytes 393224 | tf_op jit(solution)/shard_map/ppermute | solution.py:67
  84.5 1.9 %collective-permute-start.24 = (f32[128,256]{1,0:T(8,128)S(1)}, f32[128,256]{1,0:T(8,128)S(1)}, u32[]{:S(2)}, u32[]{:S(2)}) collective-permute-start(f32[128,256]{1,0:T(8,128)S(1)} %get-tuple-element.152), channel_id=1, source_target_pairs={{0,16},{1,4},{2,18},{3,6},{4,1},{5,8},{6,3},{7,10},{8,5},{9,12},{1... | collective-permute-start | bytes 393224 | tf_op jit(solution)/shard_map/ppermute | solution.py:67
  86.5 2.7 %collective-permute-done.32.ym = f32[32,256]{1,0:T(8,128)S(1)} collective-permute-done((f32[32,256]{1,0:T(8,128)S(1)}, f32[32,256]{1,0:T(8,128)S(1)}, u32[]{:S(2)}, u32[]{:S(2)}) %collective-permute-start.32) | collective-permute-done | bytes 32800 | tf_op jit(solution)/shard_map/ppermute | solution.py:67
  91.6 2.0 %forward.15 = (f32[256,256]{1,0:T(8,128)S(1)}, f32[256,256]{1,0:T(8,128)S(1)}, f32[128,256]{1,0:T(8,128)}, f32[128,256]{1,0:T(8,128)}, f32[32,256]{1,0:T(8,128)}) custom-call(s32[8]{0:T(128)S(1)} %stack.29.flags, f32[256,256]{1,0:T(8,128)S(1)} %get-tuple-element.160.cur.pnext, f32[256,256]{1,0:T(8,128)S(1)} %get-tuple-element.157.cur.prev.pnext, ...), custom_call_target="tpu_custom_call" | custom-call | flops 5000000 | bytes 2000000 | tf_op jit(solution)/shard_map/forward/pallas_call | solution.py:327
  93.5 1.6 adjoint.8
  95.1 2.4 %collective-permute-start.37 = (f32[128,256]{1,0:T(8,128)S(1)}, f32[128,256]{1,0:T(8,128)S(1)}, u32[]{:S(2)}, u32[]{:S(2)}) collective-permute-start(f32[128,256]{1,0:T(8,128)S(1)} %get-tuple-element.174), channel_id=1, source_target_pairs={{0,16},{1,4},{2,18},{3,6},{4,1},{5,8},{6,3},{7,10},{8,5},{9,12},{1... | collective-permute-start | bytes 393224 | tf_op jit(solution)/shard_map/ppermute | solution.py:67
  97.9 1.6 collective-permute-start.39
  99.5 1.6 collective-permute-done.39.ym
  101.1 1.6 adjoint.9
  104.5 1.6 collective-permute-start.42
  106.1 1.6 collective-permute-done.42.ym
  107.7 1.8 %adjoint.10 = (f32[256,256]{1,0:T(8,128)S(1)}, f32[256,256]{1,0:T(8,128)S(1)}, f32[128,256]{1,0:T(8,128)S(1)}, f32[128,256]{1,0:T(8,128)S(1)}, f32[32,256]{1,0:T(8,128)S(1)}) custom-call(s32[8]{0:T(128)S(1)} %stack.29.flags, f32[256,256]{1,0:T(8,128)S(1)} %get-tuple-element.179.cur.prev, f32[256,256]{1,0:T(8,128)S(1)} %get-tuple-element.173.cur.prev, ...), custom_call_target="tpu_custom_call" | custom-call | flops 5000000 | bytes 2000000 | tf_op jit(solution)/shard_map/adjoint/pallas_call | solution.py:327
  111.5 1.6 collective-permute-start.45
  113.0 1.6 collective-permute-done.45.ym
  114.6 1.6 adjoint.11
  118.1 1.6 collective-permute-start.48
  119.7 1.6 collective-permute-done.48.ym
  121.3 1.6 adjoint.12
  124.8 1.6 collective-permute-start.51
  126.4 1.6 collective-permute-done.51.ym
  128.0 1.6 adjoint.13
  131.5 1.6 collective-permute-start.54
  133.0 1.6 collective-permute-done.54.ym
  134.6 1.6 adjoint.14
  136.3 2.3 %collective-permute-start.58 = (f32[256,256]{1,0:T(8,128)S(1)}, f32[256,256]{1,0:T(8,128)S(1)}, u32[]{:S(2)}, u32[]{:S(2)}) collective-permute-start(f32[256,256]{1,0:T(8,128)S(1)} %get-tuple-element.209.cur), channel_id=1, source_target_pairs={{0,16},{1,2},{2,1},{3,19},{4,20},{5,6},{6,5},{7,23},{8,24},{9,10},... | collective-permute-start | bytes 786440 | tf_op jit(solution)/shard_map/ppermute | solution.py:67
  139.8 2.8 %collective-permute-done.57.ym = f32[32,256]{1,0:T(8,128)S(1)} collective-permute-done((f32[32,256]{1,0:T(8,128)S(1)}, f32[32,256]{1,0:T(8,128)S(1)}, u32[]{:S(2)}, u32[]{:S(2)}) %collective-permute-start.57) | collective-permute-done | bytes 32800 | tf_op jit(solution)/shard_map/ppermute | solution.py:67
  143.3 2.5 %adjoint.15 = (f32[256,256]{1,0:T(8,128)}, f32[8,64,128]{2,1,0:T(8,128)S(1)}, f32[256,256]{1,0:T(8,128)}) custom-call(s32[8]{0:T(128)S(1)} %stack.29.flags, f32[256,256]{1,0:T(8,128)S(1)} %get-tuple-element.209.cur, f32[256,256]{1,0:T(8,128)S(1)} %get-tuple-element.203.cur.prev, f32[256,256]{1,0:T(8,128)S(1)} %get-tuple-element.121.k0, ...), custom_call_target="tpu_custom_call" | custom-call | flops 5000000 | bytes 2000000 | tf_op jit(solution)/shard_map/adjoint/pallas_call | solution.py:327
  146.3 1.7 %collective-permute-start.59 = (f32[4,64,128]{2,1,0:T(8,128)S(1)}, f32[4,64,128]{2,1,0:T(8,128)S(1)}, u32[]{:S(2)}, u32[]{:S(2)}) collective-permute-start(f32[4,64,128]{2,1,0:T(8,128)S(1)} %get-tuple-element.217), channel_id=1, source_target_pairs={{0,1},{1,0},{2,3},{3,2},{4,5},{5,4},{6,7},{7,6},{8,9},{9,8},{10,11... | collective-permute-start | bytes 393224 | tf_op jit(solution)/shard_map/ppermute | solution.py:67
  150.6 4.0 %collective-permute-start.63 = (f32[2,64,128]{2,1,0:T(8,128)S(1)}, f32[2,64,128]{2,1,0:T(8,128)S(1)}, u32[]{:S(2)}, u32[]{:S(2)}) collective-permute-start(f32[2,64,128]{2,1,0:T(8,128)S(1)} %get-tuple-element.221), channel_id=1, source_target_pairs={{0,12},{1,14},{2,13},{3,15},{4,0},{5,2},{6,1},{7,3},{8,4},{9,6},{1... | collective-permute-start | bytes 196616 | tf_op jit(solution)/shard_map/ppermute | solution.py:67
  154.5 3.2 %collective-permute-start.60 = (f32[2,64,128]{2,1,0:T(8,128)S(1)}, f32[2,64,128]{2,1,0:T(8,128)S(1)}, u32[]{:S(2)}, u32[]{:S(2)}) collective-permute-start(f32[2,64,128]{2,1,0:T(8,128)S(1)} %get-tuple-element.218), channel_id=1, source_target_pairs={{0,0},{1,2},{2,1},{3,3},{4,4},{5,6},{6,5},{7,7},{8,8},{9,10},{10,9... | collective-permute-start | bytes 196616 | tf_op jit(solution)/shard_map/ppermute | solution.py:67
  160.1 2.0 %filter.1 = f32[32,32,64]{2,1,0:T(8,128)} custom-call(s32[8]{0:T(128)S(1)} %stack.29.flags, f32[2,64,128]{2,1,0:T(8,128)S(1)} %collective-permute-done.60.refs_0_, f32[2,64,128]{2,1,0:T(8,128)S(1)} %collective-permute-done.61.refs_1_, f32[2,64,128]{2,1,0:T(8,128)S(1)} %collective-permute-done.62.refs_2_, f32[2,64,128]{2,1,0:T(8,128)S(1)} %collective-permute-done.63.refs_3_), custom_call_target="tpu_custom_call" | custom-call | flops 5000000 | bytes 2000000 | tf_op jit(solution)/shard_map/filter/pallas_call | solution.py:327
  (163 shorter events, 54.8 us)
Async XLA Ops:
  0.6 7.3 %collective-permute-start.1 = (f32[256,256]{1,0:T(8,128)}, f32[256,256]{1,0:T(8,128)S(1)}, u32[]{:S(2)}, u32[]{:S(2)}) collective-permute-start(f32[256,256]{1,0:T(8,128)} %bitcast.41), channel_id=1, source_target_pairs={{0,16},{1,2},{2,1},{3,19},{4,20},{5,6},{6,5},{7,23},{8,24},{9,10},... | collective-permute-start | bytes 786440 | tf_op jit(solution)/shard_map/ppermute | solution.py:67
  3.3 18.0 %collective-permute-start.3 = (f32[256,256]{1,0:T(8,128)}, f32[256,256]{1,0:T(8,128)S(1)}, u32[]{:S(2)}, u32[]{:S(2)}) collective-permute-start(f32[256,256]{1,0:T(8,128)} %bitcast.45), channel_id=1, source_target_pairs={{0,16},{1,2},{2,1},{3,19},{4,20},{5,6},{6,5},{7,23},{8,24},{9,10},... | collective-permute-start | bytes 786440 | tf_op jit(solution)/shard_map/ppermute | solution.py:67
  3.4 17.9 %collective-permute-start.2 = (f32[256,256]{1,0:T(8,128)}, f32[256,256]{1,0:T(8,128)S(1)}, u32[]{:S(2)}, u32[]{:S(2)}) collective-permute-start(f32[256,256]{1,0:T(8,128)} %bitcast.43), channel_id=1, source_target_pairs={{0,16},{1,2},{2,1},{3,19},{4,20},{5,6},{6,5},{7,23},{8,24},{9,10},... | collective-permute-start | bytes 786440 | tf_op jit(solution)/shard_map/ppermute | solution.py:67
  5.1 11.2 %collective-permute-start = (f32[256,256]{1,0:T(8,128)}, f32[256,256]{1,0:T(8,128)S(1)}, u32[]{:S(2)}, u32[]{:S(2)}) collective-permute-start(f32[256,256]{1,0:T(8,128)} %bitcast.39), channel_id=1, source_target_pairs={{0,16},{1,2},{2,1},{3,19},{4,20},{5,6},{6,5},{7,23},{8,24},{9,10},... | collective-permute-start | bytes 786440 | tf_op jit(solution)/shard_map/ppermute | solution.py:67
  17.7 4.3 %collective-permute-start.6 = (f32[2,32,256]{2,1,0:T(8,128)S(1)}, f32[2,32,256]{2,1,0:T(8,128)S(1)}, u32[]{:S(2)}, u32[]{:S(2)}) collective-permute-start(f32[2,32,256]{2,1,0:T(8,128)S(1)} %get-tuple-element.119), channel_id=1, source_target_pairs={{0,2},{1,3},{2,0},{3,1},{4,6},{5,7},{6,4},{7,5},{8,10},{9,11},{10,... | collective-permute-start | bytes 196616 | tf_op jit(solution)/shard_map/ppermute | solution.py:67
  18.3 7.0 %collective-permute-start.4 = (f32[2,128,256]{2,1,0:T(8,128)}, f32[2,128,256]{2,1,0:T(8,128)S(1)}, u32[]{:S(2)}, u32[]{:S(2)}) collective-permute-start(f32[2,128,256]{2,1,0:T(8,128)} %get-tuple-element.117), channel_id=1, source_target_pairs={{0,16},{1,4},{2,18},{3,6},{4,1},{5,8},{6,3},{7,10},{8,5},{9,12},{1... | collective-permute-start | bytes 786440 | tf_op jit(solution)/shard_map/ppermute | solution.py:67
  21.0 4.3 %collective-permute-start.5 = (f32[2,128,256]{2,1,0:T(8,128)S(1)}, f32[2,128,256]{2,1,0:T(8,128)S(1)}, u32[]{:S(2)}, u32[]{:S(2)}) collective-permute-start(f32[2,128,256]{2,1,0:T(8,128)S(1)} %get-tuple-element.118), channel_id=1, source_target_pairs={{0,1},{1,0},{2,3},{3,2},{4,5},{5,4},{6,7},{7,6},{8,9},{9,8},{10,11... | collective-permute-start | bytes 786440 | tf_op jit(solution)/shard_map/ppermute | solution.py:67
  27.6 5.5 %collective-permute-start.7 = (f32[128,256]{1,0:T(8,128)S(1)}, f32[128,256]{1,0:T(8,128)S(1)}, u32[]{:S(2)}, u32[]{:S(2)}) collective-permute-start(f32[128,256]{1,0:T(8,128)S(1)} %get-tuple-element.126), channel_id=1, source_target_pairs={{0,16},{1,4},{2,18},{3,6},{4,1},{5,8},{6,3},{7,10},{8,5},{9,12},{1... | collective-permute-start | bytes 393224 | tf_op jit(solution)/shard_map/ppermute | solution.py:67
  29.1 3.9 %collective-permute-start.8 = (f32[128,256]{1,0:T(8,128)S(1)}, f32[128,256]{1,0:T(8,128)S(1)}, u32[]{:S(2)}, u32[]{:S(2)}) collective-permute-start(f32[128,256]{1,0:T(8,128)S(1)} %get-tuple-element.127), channel_id=1, source_target_pairs={{0,1},{1,0},{2,3},{3,2},{4,5},{5,4},{6,7},{7,6},{8,9},{9,8},{10,11... | collective-permute-start | bytes 393224 | tf_op jit(solution)/shard_map/ppermute | solution.py:67
  34.3 4.9 %collective-permute-start.12 = (f32[128,256]{1,0:T(8,128)S(1)}, f32[128,256]{1,0:T(8,128)S(1)}, u32[]{:S(2)}, u32[]{:S(2)}) collective-permute-start(f32[128,256]{1,0:T(8,128)S(1)} %get-tuple-element.132), channel_id=1, source_target_pairs={{0,1},{1,0},{2,3},{3,2},{4,5},{5,4},{6,7},{7,6},{8,9},{9,8},{10,11... | collective-permute-start | bytes 393224 | tf_op jit(solution)/shard_map/ppermute | solution.py:67
  35.2 4.7 %collective-permute-start.11 = (f32[128,256]{1,0:T(8,128)S(1)}, f32[128,256]{1,0:T(8,128)S(1)}, u32[]{:S(2)}, u32[]{:S(2)}) collective-permute-start(f32[128,256]{1,0:T(8,128)S(1)} %get-tuple-element.129), channel_id=1, source_target_pairs={{0,16},{1,4},{2,18},{3,6},{4,1},{5,8},{6,3},{7,10},{8,5},{9,12},{1... | collective-permute-start | bytes 393224 | tf_op jit(solution)/shard_map/ppermute | solution.py:67
  41.1 4.4 %collective-permute-start.15 = (f32[128,256]{1,0:T(8,128)S(1)}, f32[128,256]{1,0:T(8,128)S(1)}, u32[]{:S(2)}, u32[]{:S(2)}) collective-permute-start(f32[128,256]{1,0:T(8,128)S(1)} %get-tuple-element.136), channel_id=1, source_target_pairs={{0,1},{1,0},{2,3},{3,2},{4,5},{5,4},{6,7},{7,6},{8,9},{9,8},{10,11... | collective-permute-start | bytes 393224 | tf_op jit(solution)/shard_map/ppermute | solution.py:67
  41.6 4.7 %collective-permute-start.14 = (f32[128,256]{1,0:T(8,128)S(1)}, f32[128,256]{1,0:T(8,128)S(1)}, u32[]{:S(2)}, u32[]{:S(2)}) collective-permute-start(f32[128,256]{1,0:T(8,128)S(1)} %get-tuple-element.135), channel_id=1, source_target_pairs={{0,16},{1,4},{2,18},{3,6},{4,1},{5,8},{6,3},{7,10},{8,5},{9,12},{1... | collective-permute-start | bytes 393224 | tf_op jit(solution)/shard_map/ppermute | solution.py:67
  48.9 4.1 %collective-permute-start.20 = (f32[32,256]{1,0:T(8,128)S(1)}, f32[32,256]{1,0:T(8,128)S(1)}, u32[]{:S(2)}, u32[]{:S(2)}) collective-permute-start(f32[32,256]{1,0:T(8,128)S(1)} %get-tuple-element.144), channel_id=1, source_target_pairs={{0,2},{1,3},{2,0},{3,1},{4,6},{5,7},{6,4},{7,5},{8,10},{9,11},{10,... | collective-permute-start | bytes 98312 | tf_op jit(solution)/shard_map/ppermute | solution.py:67
  50.5 4.9 %collective-permute-start.18 = (f32[128,256]{1,0:T(8,128)}, f32[128,256]{1,0:T(8,128)}, u32[]{:S(2)}, u32[]{:S(2)}) collective-permute-start(f32[128,256]{1,0:T(8,128)} %get-tuple-element.138), channel_id=1, source_target_pairs={{0,16},{1,4},{2,18},{3,6},{4,1},{5,8},{6,3},{7,10},{8,5},{9,12},{1... | collective-permute-start | bytes 393224 | tf_op jit(solution)/shard_map/ppermute | solution.py:67
  51.3 23.6 %collective-permute-start.10 = (f32[256,256]{1,0:T(8,128)}, f32[256,256]{1,0:T(8,128)S(1)}, u32[]{:S(2)}, u32[]{:S(2)}) collective-permute-start(f32[256,256]{1,0:T(8,128)} %bitcast.37), channel_id=1, source_target_pairs={{0,16},{1,2},{2,1},{3,19},{4,20},{5,6},{6,5},{7,23},{8,24},{9,10},... | collective-permute-start | bytes 786440 | tf_op jit(solution)/shard_map/ppermute | solution.py:67
  52.3 34.1 %collective-permute-start.17 = (f32[256,256]{1,0:T(8,128)}, f32[256,256]{1,0:T(8,128)S(1)}, u32[]{:S(2)}, u32[]{:S(2)}) collective-permute-start(f32[256,256]{1,0:T(8,128)} %bitcast.47), channel_id=1, source_target_pairs={{0,16},{1,2},{2,1},{3,19},{4,20},{5,6},{6,5},{7,23},{8,24},{9,10},... | collective-permute-start | bytes 786440 | tf_op jit(solution)/shard_map/ppermute | solution.py:67
  56.9 3.5 %collective-permute-start.23 = (f32[32,256]{1,0:T(8,128)S(1)}, f32[32,256]{1,0:T(8,128)S(1)}, u32[]{:S(2)}, u32[]{:S(2)}) collective-permute-start(f32[32,256]{1,0:T(8,128)S(1)} %get-tuple-element.148), channel_id=1, source_target_pairs={{0,2},{1,3},{2,0},{3,1},{4,6},{5,7},{6,4},{7,5},{8,10},{9,11},{10,... | collective-permute-start | bytes 98312 | tf_op jit(solution)/shard_map/ppermute | solution.py:67
  59.4 4.6 %collective-permute-start.21 = (f32[128,256]{1,0:T(8,128)S(1)}, f32[128,256]{1,0:T(8,128)S(1)}, u32[]{:S(2)}, u32[]{:S(2)}) collective-permute-start(f32[128,256]{1,0:T(8,128)S(1)} %get-tuple-element.146), channel_id=1, source_target_pairs={{0,16},{1,4},{2,18},{3,6},{4,1},{5,8},{6,3},{7,10},{8,5},{9,12},{1... | collective-permute-start | bytes 393224 | tf_op jit(solution)/shard_map/ppermute | solution.py:67
  65.2 12.4 %collective-permute-start.28 = (f32[128,256]{1,0:T(8,128)S(1)}, f32[128,256]{1,0:T(8,128)S(1)}, u32[]{:S(2)}, u32[]{:S(2)}) collective-permute-start(f32[128,256]{1,0:T(8,128)S(1)} %get-tuple-element.158), channel_id=1, source_target_pairs={{0,1},{1,0},{2,3},{3,2},{4,5},{5,4},{6,7},{7,6},{8,9},{9,8},{10,11... | collective-permute-start | bytes 393224 | tf_op jit(solution)/shard_map/ppermute | solution.py:67
  65.7 11.9 %collective-permute-start.27 = (f32[128,256]{1,0:T(8,128)S(1)}, f32[128,256]{1,0:T(8,128)S(1)}, u32[]{:S(2)}, u32[]{:S(2)}) collective-permute-start(f32[128,256]{1,0:T(8,128)S(1)} %get-tuple-element.149), channel_id=1, source_target_pairs={{0,16},{1,4},{2,18},{3,6},{4,1},{5,8},{6,3},{7,10},{8,5},{9,12},{1... | collective-permute-start | bytes 393224 | tf_op jit(solution)/shard_map/ppermute | solution.py:67
  74.5 11.9 %collective-permute-start.36 = (f32[8,9,128]{2,1,0:T(8,128)S(1)}, f32[8,9,128]{2,1,0:T(8,128)S(1)}, u32[]{:S(2)}, u32[]{:S(2)}) collective-permute-start(f32[8,9,128]{2,1,0:T(8,128)S(1)} %merge.6.mine), channel_id=1, source_target_pairs={{0,8},{1,9},{2,10},{3,11},{4,12},{5,13},{6,14},{7,15},{8,0},{9,1},... | collective-permute-start | bytes 110600 | tf_op jit(solution)/shard_map/ppermute | solution.py:67
  78.9 12.6 %collective-permute-start.30 = (f32[128,256]{1,0:T(8,128)S(1)}, f32[128,256]{1,0:T(8,128)S(1)}, u32[]{:S(2)}, u32[]{:S(2)}) collective-permute-start(f32[128,256]{1,0:T(8,128)S(1)} %get-tuple-element.161), channel_id=1, source_target_pairs={{0,16},{1,4},{2,18},{3,6},{4,1},{5,8},{6,3},{7,10},{8,5},{9,12},{1... | collective-permute-start | bytes 393224 | tf_op jit(solution)/shard_map/ppermute | solution.py:67
  83.5 8.1 %collective-permute-start.31 = (f32[128,256]{1,0:T(8,128)S(1)}, f32[128,256]{1,0:T(8,128)S(1)}, u32[]{:S(2)}, u32[]{:S(2)}) collective-permute-start(f32[128,256]{1,0:T(8,128)S(1)} %get-tuple-element.162), channel_id=1, source_target_pairs={{0,1},{1,0},{2,3},{3,2},{4,5},{5,4},{6,7},{7,6},{8,9},{9,8},{10,11... | collective-permute-start | bytes 393224 | tf_op jit(solution)/shard_map/ppermute | solution.py:67
  84.5 9.0 %collective-permute-start.24 = (f32[128,256]{1,0:T(8,128)S(1)}, f32[128,256]{1,0:T(8,128)S(1)}, u32[]{:S(2)}, u32[]{:S(2)}) collective-permute-start(f32[128,256]{1,0:T(8,128)S(1)} %get-tuple-element.152), channel_id=1, source_target_pairs={{0,16},{1,4},{2,18},{3,6},{4,1},{5,8},{6,3},{7,10},{8,5},{9,12},{1... | collective-permute-start | bytes 393224 | tf_op jit(solution)/shard_map/ppermute | solution.py:67
  86.4 7.1 %collective-permute-start.25 = (f32[128,256]{1,0:T(8,128)S(1)}, f32[128,256]{1,0:T(8,128)S(1)}, u32[]{:S(2)}, u32[]{:S(2)}) collective-permute-start(f32[128,256]{1,0:T(8,128)S(1)} %get-tuple-element.154), channel_id=1, source_target_pairs={{0,1},{1,0},{2,3},{3,2},{4,5},{5,4},{6,7},{7,6},{8,9},{9,8},{10,11... | collective-permute-start | bytes 393224 | tf_op jit(solution)/shard_map/ppermute | solution.py:67
  89.2 4.3 %collective-permute-start.26 = (f32[32,256]{1,0:T(8,128)S(1)}, f32[32,256]{1,0:T(8,128)S(1)}, u32[]{:S(2)}, u32[]{:S(2)}) collective-permute-start(f32[32,256]{1,0:T(8,128)S(1)} %get-tuple-element.156), channel_id=1, source_target_pairs={{0,2},{1,3},{2,0},{3,1},{4,6},{5,7},{6,4},{7,5},{8,10},{9,11},{10,... | collective-permute-start | bytes 98312 | tf_op jit(solution)/shard_map/ppermute | solution.py:67
  95.1 6.0 %collective-permute-start.37 = (f32[128,256]{1,0:T(8,128)S(1)}, f32[128,256]{1,0:T(8,128)S(1)}, u32[]{:S(2)}, u32[]{:S(2)}) collective-permute-start(f32[128,256]{1,0:T(8,128)S(1)} %get-tuple-element.174), channel_id=1, source_target_pairs={{0,16},{1,4},{2,18},{3,6},{4,1},{5,8},{6,3},{7,10},{8,5},{9,12},{1... | collective-permute-start | bytes 393224 | tf_op jit(solution)/shard_map/ppermute | solution.py:67
  97.5 3.6 %collective-permute-start.38 = (f32[128,256]{1,0:T(8,128)S(1)}, f32[128,256]{1,0:T(8,128)S(1)}, u32[]{:S(2)}, u32[]{:S(2)}) collective-permute-start(f32[128,256]{1,0:T(8,128)S(1)} %get-tuple-element.175), channel_id=1, source_target_pairs={{0,1},{1,0},{2,3},{3,2},{4,5},{5,4},{6,7},{7,6},{8,9},{9,8},{10,11... | collective-permute-start | bytes 393224 | tf_op jit(solution)/shard_map/ppermute | solution.py:67
  102.7 5.0 %collective-permute-start.40 = (f32[128,256]{1,0:T(8,128)S(1)}, f32[128,256]{1,0:T(8,128)S(1)}, u32[]{:S(2)}, u32[]{:S(2)}) collective-permute-start(f32[128,256]{1,0:T(8,128)S(1)} %get-tuple-element.180), channel_id=1, source_target_pairs={{0,16},{1,4},{2,18},{3,6},{4,1},{5,8},{6,3},{7,10},{8,5},{9,12},{1... | collective-permute-start | bytes 393224 | tf_op jit(solution)/shard_map/ppermute | solution.py:67
  103.7 4.1 %collective-permute-start.41 = (f32[128,256]{1,0:T(8,128)S(1)}, f32[128,256]{1,0:T(8,128)S(1)}, u32[]{:S(2)}, u32[]{:S(2)}) collective-permute-start(f32[128,256]{1,0:T(8,128)S(1)} %get-tuple-element.181), channel_id=1, source_target_pairs={{0,1},{1,0},{2,3},{3,2},{4,5},{5,4},{6,7},{7,6},{8,9},{9,8},{10,11... | collective-permute-start | bytes 393224 | tf_op jit(solution)/shard_map/ppermute | solution.py:67
  109.5 5.1 %collective-permute-start.43 = (f32[128,256]{1,0:T(8,128)S(1)}, f32[128,256]{1,0:T(8,128)S(1)}, u32[]{:S(2)}, u32[]{:S(2)}) collective-permute-start(f32[128,256]{1,0:T(8,128)S(1)} %get-tuple-element.186), channel_id=1, source_target_pairs={{0,16},{1,4},{2,18},{3,6},{4,1},{5,8},{6,3},{7,10},{8,5},{9,12},{1... | collective-permute-start | bytes 393224 | tf_op jit(solution)/shard_map/ppermute | solution.py:67
  110.7 3.9 %collective-permute-start.44 = (f32[128,256]{1,0:T(8,128)S(1)}, f32[128,256]{1,0:T(8,128)S(1)}, u32[]{:S(2)}, u32[]{:S(2)}) collective-permute-start(f32[128,256]{1,0:T(8,128)S(1)} %get-tuple-element.187), channel_id=1, source_target_pairs={{0,1},{1,0},{2,3},{3,2},{4,5},{5,4},{6,7},{7,6},{8,9},{9,8},{10,11... | collective-permute-start | bytes 393224 | tf_op jit(solution)/shard_map/ppermute | solution.py:67
  116.3 5.0 %collective-permute-start.46 = (f32[128,256]{1,0:T(8,128)S(1)}, f32[128,256]{1,0:T(8,128)S(1)}, u32[]{:S(2)}, u32[]{:S(2)}) collective-permute-start(f32[128,256]{1,0:T(8,128)S(1)} %get-tuple-element.192), channel_id=1, source_target_pairs={{0,16},{1,4},{2,18},{3,6},{4,1},{5,8},{6,3},{7,10},{8,5},{9,12},{1... | collective-permute-start | bytes 393224 | tf_op jit(solution)/shard_map/ppermute | solution.py:67
  117.0 4.3 %collective-permute-start.47 = (f32[128,256]{1,0:T(8,128)S(1)}, f32[128,256]{1,0:T(8,128)S(1)}, u32[]{:S(2)}, u32[]{:S(2)}) collective-permute-start(f32[128,256]{1,0:T(8,128)S(1)} %get-tuple-element.193), channel_id=1, source_target_pairs={{0,1},{1,0},{2,3},{3,2},{4,5},{5,4},{6,7},{7,6},{8,9},{9,8},{10,11... | collective-permute-start | bytes 393224 | tf_op jit(solution)/shard_map/ppermute | solution.py:67
  122.9 5.0 %collective-permute-start.49 = (f32[128,256]{1,0:T(8,128)S(1)}, f32[128,256]{1,0:T(8,128)S(1)}, u32[]{:S(2)}, u32[]{:S(2)}) collective-permute-start(f32[128,256]{1,0:T(8,128)S(1)} %get-tuple-element.198), channel_id=1, source_target_pairs={{0,16},{1,4},{2,18},{3,6},{4,1},{5,8},{6,3},{7,10},{8,5},{9,12},{1... | collective-permute-start | bytes 393224 | tf_op jit(solution)/shard_map/ppermute | solution.py:67
  123.7 4.3 %collective-permute-start.50 = (f32[128,256]{1,0:T(8,128)S(1)}, f32[128,256]{1,0:T(8,128)S(1)}, u32[]{:S(2)}, u32[]{:S(2)}) collective-permute-start(f32[128,256]{1,0:T(8,128)S(1)} %get-tuple-element.199), channel_id=1, source_target_pairs={{0,1},{1,0},{2,3},{3,2},{4,5},{5,4},{6,7},{7,6},{8,9},{9,8},{10,11... | collective-permute-start | bytes 393224 | tf_op jit(solution)/shard_map/ppermute | solution.py:67
  129.6 5.0 %collective-permute-start.52 = (f32[128,256]{1,0:T(8,128)S(1)}, f32[128,256]{1,0:T(8,128)S(1)}, u32[]{:S(2)}, u32[]{:S(2)}) collective-permute-start(f32[128,256]{1,0:T(8,128)S(1)} %get-tuple-element.204), channel_id=1, source_target_pairs={{0,16},{1,4},{2,18},{3,6},{4,1},{5,8},{6,3},{7,10},{8,5},{9,12},{1... | collective-permute-start | bytes 393224 | tf_op jit(solution)/shard_map/ppermute | solution.py:67
  130.4 4.3 %collective-permute-start.53 = (f32[128,256]{1,0:T(8,128)S(1)}, f32[128,256]{1,0:T(8,128)S(1)}, u32[]{:S(2)}, u32[]{:S(2)}) collective-permute-start(f32[128,256]{1,0:T(8,128)S(1)} %get-tuple-element.205), channel_id=1, source_target_pairs={{0,1},{1,0},{2,3},{3,2},{4,5},{5,4},{6,7},{7,6},{8,9},{9,8},{10,11... | collective-permute-start | bytes 393224 | tf_op jit(solution)/shard_map/ppermute | solution.py:67
  136.3 7.0 %collective-permute-start.58 = (f32[256,256]{1,0:T(8,128)S(1)}, f32[256,256]{1,0:T(8,128)S(1)}, u32[]{:S(2)}, u32[]{:S(2)}) collective-permute-start(f32[256,256]{1,0:T(8,128)S(1)} %get-tuple-element.209.cur), channel_id=1, source_target_pairs={{0,16},{1,2},{2,1},{3,19},{4,20},{5,6},{6,5},{7,23},{8,24},{9,10},... | collective-permute-start | bytes 786440 | tf_op jit(solution)/shard_map/ppermute | solution.py:67
  138.6 4.7 %collective-permute-start.55 = (f32[128,256]{1,0:T(8,128)S(1)}, f32[128,256]{1,0:T(8,128)S(1)}, u32[]{:S(2)}, u32[]{:S(2)}) collective-permute-start(f32[128,256]{1,0:T(8,128)S(1)} %get-tuple-element.210), channel_id=1, source_target_pairs={{0,16},{1,4},{2,18},{3,6},{4,1},{5,8},{6,3},{7,10},{8,5},{9,12},{1... | collective-permute-start | bytes 393224 | tf_op jit(solution)/shard_map/ppermute | solution.py:67
  138.6 4.7 %collective-permute-start.56 = (f32[128,256]{1,0:T(8,128)S(1)}, f32[128,256]{1,0:T(8,128)S(1)}, u32[]{:S(2)}, u32[]{:S(2)}) collective-permute-start(f32[128,256]{1,0:T(8,128)S(1)} %get-tuple-element.211), channel_id=1, source_target_pairs={{0,1},{1,0},{2,3},{3,2},{4,5},{5,4},{6,7},{7,6},{8,9},{9,8},{10,11... | collective-permute-start | bytes 393224 | tf_op jit(solution)/shard_map/ppermute | solution.py:67
  139.1 3.5 %collective-permute-start.57 = (f32[32,256]{1,0:T(8,128)S(1)}, f32[32,256]{1,0:T(8,128)S(1)}, u32[]{:S(2)}, u32[]{:S(2)}) collective-permute-start(f32[32,256]{1,0:T(8,128)S(1)} %get-tuple-element.212), channel_id=1, source_target_pairs={{0,2},{1,3},{2,0},{3,1},{4,6},{5,7},{6,4},{7,5},{8,10},{9,11},{10,... | collective-permute-start | bytes 98312 | tf_op jit(solution)/shard_map/ppermute | solution.py:67
  149.5 12.5 %collective-permute-start.64 = (f32[256,256]{1,0:T(8,128)}, f32[256,256]{1,0:T(8,128)S(1)}, u32[]{:S(2)}, u32[]{:S(2)}) collective-permute-start(f32[256,256]{1,0:T(8,128)} %get-tuple-element.223), channel_id=1, source_target_pairs={{0,16},{1,2},{2,1},{3,19},{4,20},{5,6},{6,5},{7,23},{8,24},{9,10},... | collective-permute-start | bytes 786440 | tf_op jit(solution)/shard_map/ppermute | solution.py:67
  150.1 7.6 %collective-permute-start.61 = (f32[2,64,128]{2,1,0:T(8,128)S(1)}, f32[2,64,128]{2,1,0:T(8,128)S(1)}, u32[]{:S(2)}, u32[]{:S(2)}) collective-permute-start(f32[2,64,128]{2,1,0:T(8,128)S(1)} %get-tuple-element.219), channel_id=1, source_target_pairs={{0,4},{1,6},{2,5},{3,7},{4,8},{5,10},{6,9},{7,11},{8,12},{9,14},{1... | collective-permute-start | bytes 196616 | tf_op jit(solution)/shard_map/ppermute | solution.py:67
  150.6 8.1 %collective-permute-start.62 = (f32[2,64,128]{2,1,0:T(8,128)S(1)}, f32[2,64,128]{2,1,0:T(8,128)S(1)}, u32[]{:S(2)}, u32[]{:S(2)}) collective-permute-start(f32[2,64,128]{2,1,0:T(8,128)S(1)} %get-tuple-element.220), channel_id=1, source_target_pairs={{0,8},{1,10},{2,9},{3,11},{4,12},{5,14},{6,13},{7,15},{8,0},{9,2},... | collective-permute-start | bytes 196616 | tf_op jit(solution)/shard_map/ppermute | solution.py:67
  150.6 8.1 %collective-permute-start.63 = (f32[2,64,128]{2,1,0:T(8,128)S(1)}, f32[2,64,128]{2,1,0:T(8,128)S(1)}, u32[]{:S(2)}, u32[]{:S(2)}) collective-permute-start(f32[2,64,128]{2,1,0:T(8,128)S(1)} %get-tuple-element.221), channel_id=1, source_target_pairs={{0,12},{1,14},{2,13},{3,15},{4,0},{5,2},{6,1},{7,3},{8,4},{9,6},{1... | collective-permute-start | bytes 196616 | tf_op jit(solution)/shard_map/ppermute | solution.py:67
  154.5 5.6 %collective-permute-start.60 = (f32[2,64,128]{2,1,0:T(8,128)S(1)}, f32[2,64,128]{2,1,0:T(8,128)S(1)}, u32[]{:S(2)}, u32[]{:S(2)}) collective-permute-start(f32[2,64,128]{2,1,0:T(8,128)S(1)} %get-tuple-element.218), channel_id=1, source_target_pairs={{0,0},{1,2},{2,1},{3,3},{4,4},{5,6},{6,5},{7,7},{8,8},{9,10},{10,9... | collective-permute-start | bytes 196616 | tf_op jit(solution)/shard_map/ppermute | solution.py:67
  (36 other events, 140.0 us)

commit v3 on v2

--- a/solution.py
+++ b/solution.py
@@ -111,25 +111,36 @@
     return jnp.dot(a, b, preferred_element_type=F32)
 
 
-def differences(flags, cur, zm, cm, ym, near, deep):
+def inner_differences(cur, near, deep):
     depth = cur.shape[1]
     size = GROUP * COLS
     own = split(cur[...])
     along = mm(jnp.concatenate(own, axis=1), deep[...])
-    edge = ym[...]
-    top = split(jnp.where(flags[1] == 1, edge, 0.0))
-    bottom = split(jnp.where(flags[1] == 0, edge, 0.0))
-    from_z, from_c = split(zm[...]), split(cm[...])
-    ext = [jnp.concatenate(parts, axis=0) for parts in zip(top, own, bottom)]
+    blank = jnp.zeros((4 * COLS, depth), BF16)
+    ext = [jnp.concatenate([blank, part, blank], axis=0) for part in own]
     for n in range(cur.shape[0] // size):
         here = slice(n * size, n * size + size)
-        sides = slice(n * GROUP * 4, n * GROUP * 4 + GROUP * 4)
-        rhs = []
-        for p in range(2):
-            rhs += [ext[p][n * size : n * size + size + 8 * COLS], from_z[p][sides], from_c[p][sides]]
+        rhs = [part[n * size : n * size + size + 8 * COLS] for part in ext]
         out = mm(near[...], jnp.concatenate(rhs, axis=0))
         yield (here, out[0:size], along[here, 0:depth], out[size : 2 * size], out[2 * size :],
                along[here, depth:])
+
+
+def side_differences(rows, zm, cm, side):
+    size = GROUP * COLS
+    from_z, from_c = split(zm[...]), split(cm[...])
+    for n in range(rows // size):
+        sides = slice(n * GROUP * 4, n * GROUP * 4 + GROUP * 4)
+        rhs = [part[p][sides] for p in range(2) for part in (from_z, from_c)]
+        out = mm(side[...], jnp.concatenate(rhs, axis=0))
+        yield slice(n * size, n * size + size), out[0:size], out[size:]
+
+
+def edge_differences(flags, rows, ym, edge):
+    size = GROUP * COLS
+    out = mm(edge[...], jnp.concatenate(split(ym[...]), axis=0))
+    start = jnp.where(flags[1] == 1, 0, rows - size)
+    return pl.ds(pl.multiple_of(start, size), size), out[0:size], out[size:]
 
 
 def halves(value):
@@ -164,27 +175,38 @@
         rims(flags, out, *outs)
 
 
-def model_kernel(flags, lr, zm, cm, ym, near, deep, vel, k0, ki, kx, kz):
-    for here, spare, spare_z, di, dx, dz in differences(flags, lr, zm.at[0], cm.at[0], ym.at[0], near, deep):
-        v = vel[here]
-        square = v * v
-        k0[here] = square * (1.0 / 5040)
-        scaled = square * (1.0 / (840 * 840))
-        ki[here] = scaled * di
-        kx[here] = scaled * dx
-        kz[here] = scaled * dz
-
-
-def advance(flags, cur, prev, k0, ki, kx, kz, zm, cm, ym, near, deep, inj, finish):
-    for here, sums, sums_z, di, dx, dz in differences(flags, cur, zm, cm, ym, near, deep):
+def model_kernel(flags, lr, zm, cm, ym, near, deep, side, edge, vel, k0, ki, kx, kz):
+    for here, spare, spare_z, di, dx, dz in inner_differences(lr, near, deep):
+        ki[here], kx[here], kz[here] = di, dx, dz
+    for here, spare, dx in side_differences(lr.shape[0], zm.at[0], cm.at[0], side):
+        kx[here] += dx
+    here, spare, di = edge_differences(flags, lr.shape[0], ym.at[0], edge)
+    ki[here] += di
+    square = vel[...] * vel[...]
+    k0[...] = square * (1.0 / 5040)
+    scaled = square * (1.0 / (840 * 840))
+    for factor in (ki, kx, kz):
+        factor[...] = scaled * factor[...]
+
+
+def inner(cur, prev, k0, ki, kx, kz, near, deep, inj, out):
+    for here, sums, sums_z, di, dx, dz in inner_differences(cur, near, deep):
         center = cur[here]
         change = k0[here] * ((sums + sums_z) + (3.0 * SECOND[0] * 5040) * center)
         change = change - (ki[here] * di + kx[here] * dx + kz[here] * dz) + inj[here]
-        finish(here, (center - prev[here]) + (center + change), change)
-
-
-def forward_kernel(step, flags, cur, prev, k0, ki, kx, kz, zm, cm, ym, near, deep, srow, sz, wave,
-                   new, change_out, zo, co, yo):
+        out[here] = (center - prev[here]) + (center + change)
+
+
+def outer(flags, part, k0, ki, kx, zm, cm, ym, side, edge, new):
+    rows = part.shape[0]
+    for here, sums, dx in side_differences(rows, zm, cm, side):
+        new[here] = part[here] + (k0[here] * sums - kx[here] * dx)
+    here, sums, di = edge_differences(flags, rows, ym, edge)
+    new[here] += k0[here] * sums - ki[here] * di
+
+
+def forward_inner_kernel(step, flags, cur, prev, k0, ki, kx, kz, near, deep, srow, sz, wave,
+                         *rest):
     size, depth = cur.shape
     n = srow.shape[1]
     spot = lax.broadcasted_iota(jnp.int32, (size, n), 0) == srow[...]
@@ -192,20 +214,25 @@
     high, low = split(jnp.where(
         lax.broadcasted_iota(jnp.int32, (n, depth), 1) == sz[...], wave[:, step : step + 1], 0.0))
     inj = mm(spot, high) + mm(spot, low)
-
-    def finish(here, value, change):
-        new[here] = value
-        change_out[here] = change
-
-    advance(flags, cur, prev, k0, ki, kx, kz, zm, cm, ym, near, deep, inj, finish)
+    if step > 0:
+        before, part, change = rest
+        change[...] = (cur[...] - prev[...]) - (prev[...] - before[...])
+    else:
+        part, = rest
+    inner(cur, prev, k0, ki, kx, kz, near, deep, inj, part)
+
+
+def outer_kernel(stage, flags, part, k0, ki, kx, zm, cm, ym, side, edge, *rest):
+    if stage is None:
+        new, zo, co, yo = rest
+    else:
+        mine, got, new, zo, co, yo, lists = rest
+        n = mine.shape[0]
+        bit = flags[4 + stage]
+        lists[pl.ds(bit * n, n)] = mine[...]
+        lists[pl.ds((1 - bit) * n, n)] = got[...]
+    outer(flags, part, k0, ki, kx, zm, cm, ym, side, edge, new)
     rims(flags, new, zo, co, yo)
-
-
-def merge_kernel(stage, flags, mine, got, out):
-    n = mine.shape[0]
-    bit = flags[4 + stage]
-    out[pl.ds(bit * n, n)] = mine[...]
-    out[pl.ds((1 - bit) * n, n)] = got[...]
 
 
 def lists_kernel(flags, lists, spot, pick, at, obs):
@@ -240,48 +267,39 @@
         obs[s * CAP : s * CAP + CAP, :] = sent[:, s * steps : s * steps + steps]
 
 
-def adjoint_kernel(t, first, last, flags, cur, prev, k0, ki, kx, kz, zm, cm, ym, near, deep, pnext,
-                   change_in, spot, pick, at, obs, *rest):
-    rest = list(rest)
-    image = None if first else rest.pop(0)
-    vel, recv = (rest.pop(0), rest.pop(0)) if last else (None, None)
-    new, image_out, *outs = rest
-    high, low = split(pnext[...])
+def adjoint_inner_kernel(t, flags, cur, prev, k0, ki, kx, kz, near, deep, seen_state, spot, pick,
+                         at, obs, *rest):
+    if len(rest) == 1:
+        part, = rest
+    elif len(rest) == 4:
+        change, image, part, image_out = rest
+        image_out[...] = cur[...] * change[...] + image[...]
+    else:
+        now, mid, before, part, image_out = rest
+        image_out[...] = cur[...] * ((now[...] - mid[...]) - (mid[...] - before[...]))
+    high, low = split(seen_state[...])
     seen = at[...] * (mm(pick[...], high) + mm(pick[...], low))
     residual = jnp.sum(seen, axis=1, keepdims=True) - obs[:, t : t + 1]
     high, low = split(at[...] * residual)
     inj = mm(spot[...], high) + mm(spot[...], low)
-    scale = 2.0 / obs.shape[1]
-    raw = []
-
-    def finish(here, value, change):
-        new[here] = value
-        total = value * change_in[here]
-        if not first:
-            total = total + image[here]
-        if last:
-            raw.append(total * scale / vel[here])
-        else:
-            image_out[here] = total
-
-    advance(flags, cur, prev, k0, ki, kx, kz, zm, cm, ym, near, deep, inj, finish)
-    if not last:
-        rims(flags, new, *outs)
-        return
-    raw = jnp.concatenate(raw, axis=0)
-    parts, height, lanes = image_out.shape
-    chunk = cur.shape[1] // parts
-    for n in range(parts):
-        image_out[n] = jnp.concatenate(
-            [raw[g * height : g * height + height, n * chunk : n * chunk + chunk]
-             for g in range(lanes // chunk)], axis=1)
-    outs[0][...] = jnp.where(flags[0] == flags[1], cur[...], recv[...])
-
-
-def pair_kernel(flags, parts, mine, other):
-    for n in range(mine.shape[0]):
-        mine[n] = parts[2 * n + flags[0]]
-        other[n] = parts[2 * n + 1 - flags[0]]
+    inner(cur, prev, k0, ki, kx, kz, near, deep, inj, part)
+
+
+def last_kernel(scale, flags, part, k0, ki, kx, zm, cm, ym, side, edge, image, change, vel, prev,
+                got, new, mine, other, prev_out):
+    outer(flags, part, k0, ki, kx, zm, cm, ym, side, edge, new)
+    raw = (image[...] + new[...] * change[...]) * scale / vel[...]
+    count, height, lanes = mine.shape
+    chunk = raw.shape[1] // (2 * count)
+    for n in range(count):
+        even, odd = (
+            jnp.concatenate(
+                [raw[g * height : g * height + height, m * chunk : m * chunk + chunk]
+                 for g in range(lanes // chunk)], axis=1)
+            for m in (2 * n, 2 * n + 1))
+        mine[n] = jnp.where(flags[0] == 0, even, odd)
+        other[n] = jnp.where(flags[0] == 0, odd, even)
+    prev_out[...] = jnp.where(flags[0] == flags[1], prev[...], got[...])
 
 
 def join_kernel(flags, mine, got, *outs):
@@ -295,7 +313,8 @@
 
 
 def filter_kernel(flags, *refs):
-    pieces, out = refs[:-1], refs[-1]
+    *pieces, own, got, out, state = refs
+    state[...] = jnp.where(flags[0] == flags[1], own[...], got[...])
     height, lanes = pieces[0].shape[1:]
     chunk, rows, full = out.shape
     groups = lanes // chunk
@@ -357,13 +376,18 @@
     deep = depth_matrix(depth)
     deep = jnp.asarray(np.concatenate([deep, deep]), BF16)
     near = stencil_matrix(GROUP, cols)
-    own, half = near.shape[1] - GROUP * 8, GROUP * 4
-    from_z = np.where(np.arange(near.shape[1]) // half == own // half, 0.0, 1.0)
-    other = np.concatenate([near[:, :own], near[:, own + half :], near[:, own : own + half]], axis=1)
+    group, own, half = GROUP * cols, near.shape[1] - GROUP * 8, GROUP * 4
+    side = np.concatenate([near[:group, own:], near[2 * group :, own:]])
+    other = np.concatenate([side[:, half:], side[:, :half]], axis=1)
+    from_z = np.arange(2 * half) < half
     inside = jnp.where(c == 0, q > 0, q < nq - 1)
-    near = jnp.where(c == 0, jnp.asarray(near, F32), jnp.asarray(other, F32))
-    near = jnp.where(inside, near, near * jnp.asarray(from_z, F32)[None, :]).astype(BF16)
-    near = jnp.concatenate([near, near], axis=1)
+    side = jnp.where(c == 0, jnp.asarray(side, F32), jnp.asarray(other, F32))
+    side = jnp.where(from_z[None, :] & ~inside, 0.0, side).astype(BF16)
+    side = jnp.concatenate([side, side], axis=1)
+    edge = jnp.where(y == 1, jnp.asarray(near[: 2 * group, : 4 * cols], F32),
+                     jnp.asarray(near[: 2 * group, own - 4 * cols : own], F32)).astype(BF16)
+    edge = jnp.concatenate([edge, edge], axis=1)
+    near = jnp.asarray(np.concatenate([near[:, :own], near[:, :own]], axis=1), BF16)
 
     def halo(zo, co, yo):
         return send(zo, z_perm), send(co, c_perm), send(yo, y_perm)
@@ -376,14 +400,16 @@
 
     log_density, fwd_now, velocity = flat(log_density), flat(fwd_now), flat(velocity)
     fwd_before, adj_now, adj_before = flat(fwd_before), flat(adj_now), flat(adj_before)
-    got = [send(v, swap_perm) for v in (log_density, fwd_now, velocity, fwd_before)]
+    got = [send(v, swap_perm) for v in (log_density, fwd_now)]
     density, p_now, *out = call(
         functools.partial(settle_kernel, 2), "settle",
-        [field, field] + [shaped(2, *r.shape) for r in rim], flags, log_density, fwd_now, *got[:2])
+        [field, field] + [shaped(2, *r.shape) for r in rim], flags, log_density, fwd_now, *got)
     zm, cm, ym = halo(*out)
+    got = [send(after(v, out[0]), swap_perm) for v in (velocity, fwd_before)]
     vel, p_before = call(functools.partial(settle_kernel, 0), "settle_model", [field, field],
-                         flags, velocity, fwd_before, *got[2:])
-    model = call(model_kernel, "model", [field] * 4, flags, density, zm, cm, ym, near, deep, vel)
+                         flags, velocity, fwd_before, *got)
+    k0, ki, kx, kz = call(model_kernel, "model", [field] * 4, flags, density, zm, cm, ym, near,
+                          deep, side, edge, vel)
     halos = (zm[1], cm[1], ym[1])
 
     plane = nx * cols * depth
@@ -397,34 +423,47 @@
     live = jnp.arange(CAP)[None, :] < rec_counts[0][:, None]
     cells = jnp.where(live.reshape(-1), rec_cells[0], -1)
     lists = jnp.concatenate([observed, cells[None, :].astype(F32)], axis=0)[None]
-    share = -(-len(stages) // (steps - 2))
-
-    states, changes = [], []
+
+    states = [p_before, p_now]
+    changes = []
     for t in range(steps):
-        p_next, change, *out = call(
-            functools.partial(forward_kernel, t), "forward", [field, field] + rim,
-            flags, p_now, p_before, *model, *halos, near, deep, srow, sz, wave)
+        args = states[:-3:-1] + [k0, ki, kx, kz, near, deep, srow, sz, wave]
+        outs = [field]
+        if t > 0:
+            args.append(states[-3])
+            outs = [field, field]
+        part, *change = call(functools.partial(forward_inner_kernel, t), "forward_inner", outs,
+                             flags, *args)
+        changes += change
+        if t == 1:
+            u_now, *u_rim = call(functools.partial(settle_one, True), "settle_adjoint", [field] + rim,
+                                 flags, adj_now, got_now)
+            part = after(part, u_now)
+        if t == 3:
+            u_before, = call(functools.partial(settle_one, False), "settle_before", [field],
+                             flags, adj_before, got_before)
+            part = after(part, u_before)
+        if t == 6:
+            part = after(part, *u_halos)
+        args = [part, k0, ki, kx, *halos, side, edge]
+        outs = [field] + rim
+        stage = t if t < len(stages) else None
+        if stage is not None:
+            args += [lists, send(after(lists, out[0]) if t else lists, stages[t][0])]
+            outs = outs + [shaped(2 * lists.shape[0], *lists.shape[1:])]
+        new, zo, co, yo, *merged = call(functools.partial(outer_kernel, stage), "forward_outer", outs,
+                                        flags, *args)
+        out = (zo, co, yo)
+        lists = merged[0] if merged else lists
+        states.append(new)
         if t < steps - 1:
             halos = halo(*out)
-        for n in range(t * share, min(t * share + share, len(stages))):
-            moved = send(after(lists, out[0]) if n else lists, stages[n][0])
-            lists, = call(functools.partial(merge_kernel, n), "merge",
-                          [shaped(2 * lists.shape[0], *lists.shape[1:])], flags, lists, moved)
-        if t == 1:
-            got_now = send(after(adj_now, out[0]), swap_perm)
-        if t == 3:
-            got_before = send(after(adj_before, out[0]), swap_perm)
-            u_now, *out = call(functools.partial(settle_one, True), "settle_adjoint", [field] + rim,
-                               flags, adj_now, after(got_now, out[0]))
-            u_rim = out
+        if t == 0:
+            got_now = send(after(adj_now, zo), swap_perm)
+        if t == 2:
+            got_before = send(after(adj_before, zo), swap_perm)
         if t == 4:
-            u_halos = halo(*(after(r, out[0]) for r in u_rim))
-        if t == 5:
-            u_before, = call(functools.partial(settle_one, False), "settle_before", [field],
-                             flags, adj_before, after(got_before, out[0]))
-        p_before, p_now = p_now, p_next
-        states.append(p_next)
-        changes.append(change)
+            u_halos = halo(*(after(r, zo) for r in u_rim))
 
     slots = subs * CAP
     receivers = call(
@@ -433,33 +472,36 @@
          shaped(slots, depth), shaped(slots, steps)], flags, lists)
 
     halos = u_halos
-    image = ()
+    image = []
     chunk = depth // nx
-    packed = shaped(nx, size * chunk // 128, 128)
+    half = shaped(nq, size * chunk // 128, 128)
     for j in range(steps):
         t = steps - 1 - j
-        last = j == steps - 1
-        args = [flags, u_now, u_before, *model, *halos, near, deep, states[t], changes[t],
-                *receivers, *image]
-        outs = [field, field] + rim
-        if last:
-            args += [vel, send(u_now, swap_perm)]
-            outs = [field, packed, field]
+        args = [u_now, u_before, k0, ki, kx, kz, near, deep, states[t + 2], *receivers]
+        outs = [field]
+        if j > 0:
+            args += [changes[t + 1], *image] if image else states[:-4:-1]
+            outs = [field, field]
+        part, *image = call(functools.partial(adjoint_inner_kernel, t), "adjoint_inner", outs,
+                            flags, *args)
+        args = [part, k0, ki, kx, *halos, side, edge]
+        if j == steps - 1:
+            args += [*image, changes[0], vel, u_now, send(u_now, swap_perm)]
+            u_last, mine, other, adj_prev = call(
+                functools.partial(last_kernel, 2.0 / steps), "last", [field, half, half, field],
+                flags, *args)
+            break
         u_before = u_now
-        u_now, *outs = call(functools.partial(adjoint_kernel, t, j == 0, last), "adjoint", outs, *args)
-        image = outs[:1]
-        if not last:
-            halos = halo(*outs[1:])
-    raw, adj_prev = outs
-
-    half = shaped(nq, *packed.shape[1:])
-    mine, other = call(pair_kernel, "pair", [half, half], flags, raw)
-    piece = shaped(2, *packed.shape[1:])
-    pieces = call(join_kernel, "join", [piece] * nq, flags, mine, send(other, c_perm))
-    got = send(after(u_now, pieces[0]), swap_perm)
+        u_now, *out = call(functools.partial(outer_kernel, None), "adjoint_outer", [field] + rim,
+                           flags, *args)
+        halos = halo(*out)
+
+    got = send(u_last, swap_perm)
+    pieces = call(join_kernel, "join", [shaped(2, *half.shape[1:])] * nq, flags, mine,
+                  send(other, c_perm))
     pieces = [send(value, plan.spread(s)) for s, value in enumerate(pieces)]
-    gradient, = call(filter_kernel, "filter", [shaped(chunk, rows, nx * cols)], flags, *pieces)
-    adj_out = jnp.where(keep, u_now, got)
+    gradient, adj_out = call(filter_kernel, "filter", [shaped(chunk, rows, nx * cols), field], flags,
+                             *pieces, u_last, got)
     block = (rows, cols, depth)
     return gradient, adj_out.reshape(block), adj_prev.reshape(block)
 

time: 163 us -> 148 us (0.908)
  waiting for transfers between devices: 54.1 us -> 35.5 us
  Pallas kernels: 35.7 us -> 43.2 us
  starting transfers between devices: 67.4 us -> 62.6 us
    ppermute x65, waiting for transfers between devices: 54.1 us -> 35.5 us  [send(): return lax.ppermute(value, ALL, pairs)]
    pallas_call x29 -> x40, Pallas kernels: 35.7 us -> 43.2 us  [call(): pl.pallas_call(kernel, name=name, out_shape=outs, in_specs=specs, out_spe...]
    ppermute x65, starting transfers between devices: 67.4 us -> 62.6 us  [send(): return lax.ppermute(value, ALL, pairs)]
  transfers between devices with their start and end apart: 65 -> 65, of which waited for: 27 -> 25; matrix products, arithmetic and copies ran while one was open for 1% -> 2% of each run, Pallas kernels for 9% -> 17%
where the time goes in v3:
time: 148 us; the launch traced here: 147 us
  starting transfers between devices  62.6 us (42%)
  Pallas kernels  43.2 us (29%)
  waiting for transfers between devices  35.5 us (24%)
  other arithmetic  2.96 us (2%)
  local copies, waits for them, and re-layouts  2.18 us (1%)
    ppermute x65, starting transfers between devices, send(): return lax.ppermute(value, ALL, pairs)  62.6 us
    pallas_call x40, Pallas kernels, call(): pl.pallas_call(kernel, name=name, out_shape=outs, in_specs=specs, out_spe...  43.2 us
    ppermute x65, waiting for transfers between devices, send(): return lax.ppermute(value, ALL, pairs)  35.5 us
  transfers between devices with their start and end apart: 65, of which 25 were waited for; matrix products, arithmetic and copies ran while one was open for 2% of the time, Pallas kernels for 17%

profile of v3, /device:TPU:1, one launch (start us, length us, event | category | flops | bytes accessed | tf_op | source)
XLA Modules:
  0.0 147.5 jit_solution(17705958441953444436)
XLA Ops:
  0.7 2.7 %collective-permute-start = (f32[256,256]{1,0:T(8,128)}, f32[256,256]{1,0:T(8,128)S(1)}, u32[]{:S(2)}, u32[]{:S(2)}) collective-permute-start(f32[256,256]{1,0:T(8,128)} %bitcast.40), channel_id=1, source_target_pairs={{0,16},{1,2},{2,1},{3,19},{4,20},{5,6},{6,5},{7,23},{8,24},{9,10},... | collective-permute-start | bytes 786440 | tf_op jit(solution)/shard_map/ppermute | solution.py:67
  8.0 2.8 %collective-permute-done.1.recv_b = f32[256,256]{1,0:T(8,128)S(1)} collective-permute-done((f32[256,256]{1,0:T(8,128)}, f32[256,256]{1,0:T(8,128)S(1)}, u32[]{:S(2)}, u32[]{:S(2)}) %collective-permute-start.1) | collective-permute-done | bytes 262176 | tf_op jit(solution)/shard_map/ppermute | solution.py:67
  12.8 1.2 collective-permute-start.6
  14.9 1.5 %collective-permute-start.4 = (f32[2,128,256]{2,1,0:T(8,128)S(1)}, f32[2,128,256]{2,1,0:T(8,128)S(1)}, u32[]{:S(2)}, u32[]{:S(2)}) collective-permute-start(f32[2,128,256]{2,1,0:T(8,128)S(1)} %get-tuple-element.135), channel_id=1, source_target_pairs={{0,16},{1,4},{2,18},{3,6},{4,1},{5,8},{6,3},{7,10},{8,5},{9,12},{1... | collective-permute-start | bytes 786440 | tf_op jit(solution)/shard_map/ppermute | solution.py:67
  18.5 2.5 %collective-permute-done.4.zm = f32[2,128,256]{2,1,0:T(8,128)S(1)} collective-permute-done((f32[2,128,256]{2,1,0:T(8,128)S(1)}, f32[2,128,256]{2,1,0:T(8,128)S(1)}, u32[]{:S(2)}, u32[]{:S(2)}) %collective-permute-start.4) | collective-permute-done | bytes 262176 | tf_op jit(solution)/shard_map/ppermute | solution.py:67
  21.0 1.5 %collective-permute-done.2.recv_a = f32[256,256]{1,0:T(8,128)S(1)} collective-permute-done((f32[256,256]{1,0:T(8,128)S(1)}, f32[256,256]{1,0:T(8,128)S(1)}, u32[]{:S(2)}, u32[]{:S(2)}) %collective-permute-start.2) | collective-permute-done | bytes 262176 | tf_op jit(solution)/shard_map/ppermute | solution.py:67
  22.5 2.8 %collective-permute-done.3.recv_b = f32[256,256]{1,0:T(8,128)S(1)} collective-permute-done((f32[256,256]{1,0:T(8,128)S(1)}, f32[256,256]{1,0:T(8,128)S(1)}, u32[]{:S(2)}, u32[]{:S(2)}) %collective-permute-start.3) | collective-permute-done | bytes 262176 | tf_op jit(solution)/shard_map/ppermute | solution.py:67
  29.8 2.7 %collective-permute-start.10 = (f32[128,256]{1,0:T(8,128)S(1)}, f32[128,256]{1,0:T(8,128)S(1)}, u32[]{:S(2)}, u32[]{:S(2)}) collective-permute-start(f32[128,256]{1,0:T(8,128)S(1)} %get-tuple-element.153), channel_id=1, source_target_pairs={{0,1},{1,0},{2,3},{3,2},{4,5},{5,4},{6,7},{7,6},{8,9},{9,8},{10,11... | collective-permute-start | bytes 393224 | tf_op jit(solution)/shard_map/ppermute | solution.py:67
  32.5 1.5 collective-permute-start.12
  35.8 1.3 collective-permute-done.9.zm
  38.0 1.2 collective-permute-start.13
  39.2 1.9 %collective-permute-start.14 = (f32[128,256]{1,0:T(8,128)S(1)}, f32[128,256]{1,0:T(8,128)S(1)}, u32[]{:S(2)}, u32[]{:S(2)}) collective-permute-start(f32[128,256]{1,0:T(8,128)S(1)} %get-tuple-element.160), channel_id=1, source_target_pairs={{0,1},{1,0},{2,3},{3,2},{4,5},{5,4},{6,7},{7,6},{8,9},{9,8},{10,11... | collective-permute-start | bytes 393224 | tf_op jit(solution)/shard_map/ppermute | solution.py:67
  42.3 1.9 %collective-permute-done.16.rest_1_ = f32[4,9,128]{2,1,0:T(8,128)S(1)} collective-permute-done((f32[4,9,128]{2,1,0:T(8,128)S(1)}, f32[4,9,128]{2,1,0:T(8,128)S(1)}, u32[]{:S(2)}, u32[]{:S(2)}) %collective-permute-start.16) | collective-permute-done | bytes 18464 | tf_op jit(solution)/shard_map/ppermute | solution.py:67
  45.2 2.5 %collective-permute-start.17 = (f32[256,256]{1,0:T(8,128)S(1)}, f32[256,256]{1,0:T(8,128)S(1)}, u32[]{:S(2)}, u32[]{:S(2)}) collective-permute-start(f32[256,256]{1,0:T(8,128)S(1)} %bitcast.48), channel_id=1, source_target_pairs={{0,16},{1,2},{2,1},{3,19},{4,20},{5,6},{6,5},{7,23},{8,24},{9,10},... | collective-permute-start | bytes 786440 | tf_op jit(solution)/shard_map/ppermute | solution.py:67
  48.3 1.9 %collective-permute-start.21 = (f32[8,9,128]{2,1,0:T(8,128)S(1)}, f32[8,9,128]{2,1,0:T(8,128)S(1)}, u32[]{:S(2)}, u32[]{:S(2)}) collective-permute-start(f32[8,9,128]{2,1,0:T(8,128)S(1)} %get-tuple-element.172.rest_0_), channel_id=1, source_target_pairs={{0,8},{1,9},{2,10},{3,11},{4,12},{5,13},{6,14},{7,15},{8,0},{9,1},... | collective-permute-start | bytes 110600 | tf_op jit(solution)/shard_map/ppermute | solution.py:67
  54.1 3.2 %collective-permute-start.22 = (f32[128,256]{1,0:T(8,128)S(1)}, f32[128,256]{1,0:T(8,128)S(1)}, u32[]{:S(2)}, u32[]{:S(2)}) collective-permute-start(f32[128,256]{1,0:T(8,128)S(1)} %get-tuple-element.175), channel_id=1, source_target_pairs={{0,16},{1,4},{2,18},{3,6},{4,1},{5,8},{6,3},{7,10},{8,5},{9,12},{1... | collective-permute-start | bytes 393224 | tf_op jit(solution)/shard_map/ppermute | solution.py:67
  57.3 1.3 collective-permute-start.24
  61.2 1.4 collective-permute-start.25
  62.6 1.4 collective-permute-start.26
  67.8 1.9 %collective-permute-start.31 = (f32[128,256]{1,0:T(8,128)S(1)}, f32[128,256]{1,0:T(8,128)S(1)}, u32[]{:S(2)}, u32[]{:S(2)}) collective-permute-start(f32[128,256]{1,0:T(8,128)S(1)} %get-tuple-element.192), channel_id=1, source_target_pairs={{0,16},{1,4},{2,18},{3,6},{4,1},{5,8},{6,3},{7,10},{8,5},{9,12},{1... | collective-permute-start | bytes 393224 | tf_op jit(solution)/shard_map/ppermute | solution.py:67
  70.3 2.6 %collective-permute-done.30.ym = f32[32,256]{1,0:T(8,128)S(1)} collective-permute-done((f32[32,256]{1,0:T(8,128)S(1)}, f32[32,256]{1,0:T(8,128)S(1)}, u32[]{:S(2)}, u32[]{:S(2)}) %collective-permute-start.30) | collective-permute-done | bytes 32800 | tf_op jit(solution)/shard_map/ppermute | solution.py:67
  76.5 2.8 %collective-permute-start.34 = (f32[128,256]{1,0:T(8,128)S(1)}, f32[128,256]{1,0:T(8,128)S(1)}, u32[]{:S(2)}, u32[]{:S(2)}) collective-permute-start(f32[128,256]{1,0:T(8,128)S(1)} %get-tuple-element.197), channel_id=1, source_target_pairs={{0,16},{1,4},{2,18},{3,6},{4,1},{5,8},{6,3},{7,10},{8,5},{9,12},{1... | collective-permute-start | bytes 393224 | tf_op jit(solution)/shard_map/ppermute | solution.py:67
  81.0 1.2 forward_inner.15
  83.3 1.5 %forward_outer.15 = (f32[256,256]{1,0:T(8,128)S(1)}, f32[128,256]{1,0:T(8,128)}, f32[128,256]{1,0:T(8,128)}, f32[32,256]{1,0:T(8,128)}) custom-call(s32[8]{0:T(128)S(1)} %stack.29.flags, f32[256,256]{1,0:T(8,128)S(1)} %get-tuple-element.196.part, f32[256,256]{1,0:T(8,128)S(1)} %get-tuple-element.143.k0, f32[256,256]{1,0:T(8,128)S(1)} %get-tuple-element.144.ki, ...), custom_call_target="tpu_custom_call" | custom-call | flops 5000000 | bytes 2000000 | tf_op jit(solution)/shard_map/forward_outer/pallas_call | solution.py:346
  84.9 1.4 adjoint_inner.8.part
  87.6 1.5 %collective-permute-start.38 = (f32[128,256]{1,0:T(8,128)S(1)}, f32[128,256]{1,0:T(8,128)S(1)}, u32[]{:S(2)}, u32[]{:S(2)}) collective-permute-start(f32[128,256]{1,0:T(8,128)S(1)} %get-tuple-element.209), channel_id=1, source_target_pairs={{0,1},{1,0},{2,3},{3,2},{4,5},{5,4},{6,7},{7,6},{8,9},{9,8},{10,11... | collective-permute-start | bytes 393224 | tf_op jit(solution)/shard_map/ppermute | solution.py:67
  89.3 1.7 %adjoint_inner.9 = (f32[256,256]{1,0:T(8,128)S(1)}, f32[256,256]{1,0:T(8,128)S(1)}) custom-call(s32[8]{0:T(128)S(1)} %stack.29.flags, f32[256,256]{1,0:T(8,128)S(1)} %get-tuple-element.206.cur.prev, f32[256,256]{1,0:T(8,128)S(1)} %get-tuple-element.149.cur.prev, f32[256,256]{1,0:T(8,128)S(1)} %get-tuple-element.143.k0, ...), custom_call_target="tpu_custom_call" | custom-call | flops 5000000 | bytes 2000000 | tf_op jit(solution)/shard_map/adjoint_inner/pallas_call | solution.py:346
  93.8 1.2 collective-permute-start.41
  95.2 1.5 adjoint_inner.10
  96.7 1.4 collective-permute-done.42.ym
  99.6 1.2 collective-permute-start.44
  101.1 1.5 adjoint_inner.11
  102.5 1.4 collective-permute-done.45.ym
  106.9 1.5 adjoint_inner.12
  108.4 1.4 collective-permute-done.48.ym
  112.8 1.5 %adjoint_inner.13 = (f32[256,256]{1,0:T(8,128)S(1)}, f32[256,256]{1,0:T(8,128)S(1)}) custom-call(s32[8]{0:T(128)S(1)} %stack.29.flags, f32[256,256]{1,0:T(8,128)S(1)} %get-tuple-element.232.cur.prev, f32[256,256]{1,0:T(8,128)S(1)} %get-tuple-element.225.cur.prev, f32[256,256]{1,0:T(8,128)S(1)} %get-tuple-element.143.k0, ...), custom_call_target="tpu_custom_call" | custom-call | flops 5000000 | bytes 2000000 | tf_op jit(solution)/shard_map/adjoint_inner/pallas_call | solution.py:346
  114.3 1.4 collective-permute-done.51.ym
  118.6 1.5 adjoint_inner.14
  120.1 1.4 collective-permute-done.54.ym
  125.3 1.5 %adjoint_inner.15 = (f32[256,256]{1,0:T(8,128)S(1)}, f32[256,256]{1,0:T(8,128)S(1)}) custom-call(s32[8]{0:T(128)S(1)} %stack.29.flags, f32[256,256]{1,0:T(8,128)S(1)} %get-tuple-element.246.cur.prev, f32[256,256]{1,0:T(8,128)S(1)} %get-tuple-element.239.cur.prev, f32[256,256]{1,0:T(8,128)S(1)} %get-tuple-element.143.k0, ...), custom_call_target="tpu_custom_call" | custom-call | flops 5000000 | bytes 2000000 | tf_op jit(solution)/shard_map/adjoint_inner/pallas_call | solution.py:346
  126.8 2.0 %collective-permute-done.57.ym = f32[32,256]{1,0:T(8,128)S(1)} collective-permute-done((f32[32,256]{1,0:T(8,128)S(1)}, f32[32,256]{1,0:T(8,128)S(1)}, u32[]{:S(2)}, u32[]{:S(2)}) %collective-permute-start.57) | collective-permute-done | bytes 32800 | tf_op jit(solution)/shard_map/ppermute | solution.py:67
  128.8 1.7 %last.1 = (f32[256,256]{1,0:T(8,128)S(1)}, f32[4,64,128]{2,1,0:T(8,128)S(1)}, f32[4,64,128]{2,1,0:T(8,128)S(1)}, f32[256,256]{1,0:T(8,128)}) custom-call(s32[8]{0:T(128)S(1)} %stack.29.flags, f32[256,256]{1,0:T(8,128)S(1)} %get-tuple-element.249.part, f32[256,256]{1,0:T(8,128)S(1)} %get-tuple-element.143.k0, f32[256,256]{1,0:T(8,128)S(1)} %get-tuple-element.144.ki, ...), custom_call_target="tpu_custom_call" | custom-call | flops 5000000 | bytes 2000000 | tf_op jit(solution)/shard_map/last/pallas_call | solution.py:346
  131.5 2.3 %collective-permute-start.59 = (f32[4,64,128]{2,1,0:T(8,128)S(1)}, f32[4,64,128]{2,1,0:T(8,128)S(1)}, u32[]{:S(2)}, u32[]{:S(2)}) collective-permute-start(f32[4,64,128]{2,1,0:T(8,128)S(1)} %get-tuple-element.256), channel_id=1, source_target_pairs={{0,1},{1,0},{2,3},{3,2},{4,5},{5,4},{6,7},{7,6},{8,9},{9,8},{10,11... | collective-permute-start | bytes 393224 | tf_op jit(solution)/shard_map/ppermute | solution.py:67
  135.3 1.9 %collective-permute-start.60 = (f32[2,64,128]{2,1,0:T(8,128)S(1)}, f32[2,64,128]{2,1,0:T(8,128)S(1)}, u32[]{:S(2)}, u32[]{:S(2)}) collective-permute-start(f32[2,64,128]{2,1,0:T(8,128)S(1)} %get-tuple-element.257), channel_id=1, source_target_pairs={{0,0},{1,2},{2,1},{3,3},{4,4},{5,6},{6,5},{7,7},{8,8},{9,10},{10,9... | collective-permute-start | bytes 196616 | tf_op jit(solution)/shard_map/ppermute | solution.py:67
  137.4 4.4 %collective-permute-start.63 = (f32[2,64,128]{2,1,0:T(8,128)S(1)}, f32[2,64,128]{2,1,0:T(8,128)S(1)}, u32[]{:S(2)}, u32[]{:S(2)}) collective-permute-start(f32[2,64,128]{2,1,0:T(8,128)S(1)} %get-tuple-element.260), channel_id=1, source_target_pairs={{0,12},{1,14},{2,13},{3,15},{4,0},{5,2},{6,1},{7,3},{8,4},{9,6},{1... | collective-permute-start | bytes 196616 | tf_op jit(solution)/shard_map/ppermute | solution.py:67
  141.8 1.9 %collective-permute-done.61.refs_1_ = f32[2,64,128]{2,1,0:T(8,128)S(1)} collective-permute-done((f32[2,64,128]{2,1,0:T(8,128)S(1)}, f32[2,64,128]{2,1,0:T(8,128)S(1)}, u32[]{:S(2)}, u32[]{:S(2)}) %collective-permute-start.61) | collective-permute-done | bytes 65568 | tf_op jit(solution)/shard_map/ppermute | solution.py:67
  143.7 1.7 %collective-permute-done.63.refs_3_ = f32[2,64,128]{2,1,0:T(8,128)S(1)} collective-permute-done((f32[2,64,128]{2,1,0:T(8,128)S(1)}, f32[2,64,128]{2,1,0:T(8,128)S(1)}, u32[]{:S(2)}, u32[]{:S(2)}) %collective-permute-start.63) | collective-permute-done | bytes 65568 | tf_op jit(solution)/shard_map/ppermute | solution.py:67
  145.5 2.0 %filter.1 = (f32[32,32,64]{2,1,0:T(8,128)}, f32[256,256]{1,0:T(8,128)}) custom-call(s32[8]{0:T(128)S(1)} %stack.29.flags, f32[2,64,128]{2,1,0:T(8,128)S(1)} %collective-permute-done.60.refs_0_, f32[2,64,128]{2,1,0:T(8,128)S(1)} %collective-permute-done.61.refs_1_, f32[2,64,128]{2,1,0:T(8,128)S(1)} %collective-permute-done.62.refs_2_, ...), custom_call_target="tpu_custom_call" | custom-call | flops 5000000 | bytes 2000000 | tf_op jit(solution)/shard_map/filter/pallas_call | solution.py:346
  (166 shorter events, 58.4 us)
Async XLA Ops:
  0.7 7.3 %collective-permute-start = (f32[256,256]{1,0:T(8,128)}, f32[256,256]{1,0:T(8,128)S(1)}, u32[]{:S(2)}, u32[]{:S(2)}) collective-permute-start(f32[256,256]{1,0:T(8,128)} %bitcast.40), channel_id=1, source_target_pairs={{0,16},{1,2},{2,1},{3,19},{4,20},{5,6},{6,5},{7,23},{8,24},{9,10},... | collective-permute-start | bytes 786440 | tf_op jit(solution)/shard_map/ppermute | solution.py:67
  3.4 7.3 %collective-permute-start.1 = (f32[256,256]{1,0:T(8,128)}, f32[256,256]{1,0:T(8,128)S(1)}, u32[]{:S(2)}, u32[]{:S(2)}) collective-permute-start(f32[256,256]{1,0:T(8,128)} %bitcast.42), channel_id=1, source_target_pairs={{0,16},{1,2},{2,1},{3,19},{4,20},{5,6},{6,5},{7,23},{8,24},{9,10},... | collective-permute-start | bytes 786440 | tf_op jit(solution)/shard_map/ppermute | solution.py:67
  5.7 22.5 %collective-permute-start.7 = (f32[1,9,128]{2,1,0:T(8,128)S(1)}, f32[1,9,128]{2,1,0:T(8,128)S(1)}, u32[]{:S(2)}, u32[]{:S(2)}) collective-permute-start(f32[1,9,128]{2,1,0:T(8,128)S(1)} %maximum_bitcast_fusion.rest_0_), channel_id=1, source_target_pairs={{0,1},{1,0},{2,3},{3,2},{4,5},{5,4},{6,7},{7,6},{8,9},{9,8},{10,11... | collective-permute-start | bytes 13832 | tf_op jit(solution)/shard_map/ppermute | solution.py:67
  12.4 6.1 %collective-permute-start.5 = (f32[2,128,256]{2,1,0:T(8,128)S(1)}, f32[2,128,256]{2,1,0:T(8,128)S(1)}, u32[]{:S(2)}, u32[]{:S(2)}) collective-permute-start(f32[2,128,256]{2,1,0:T(8,128)S(1)} %get-tuple-element.140), channel_id=1, source_target_pairs={{0,1},{1,0},{2,3},{3,2},{4,5},{5,4},{6,7},{7,6},{8,9},{9,8},{10,11... | collective-permute-start | bytes 786440 | tf_op jit(solution)/shard_map/ppermute | solution.py:67
  12.8 4.6 %collective-permute-start.6 = (f32[2,32,256]{2,1,0:T(8,128)S(1)}, f32[2,32,256]{2,1,0:T(8,128)S(1)}, u32[]{:S(2)}, u32[]{:S(2)}) collective-permute-start(f32[2,32,256]{2,1,0:T(8,128)S(1)} %get-tuple-element.141), channel_id=1, source_target_pairs={{0,2},{1,3},{2,0},{3,1},{4,6},{5,7},{6,4},{7,5},{8,10},{9,11},{10,... | collective-permute-start | bytes 196616 | tf_op jit(solution)/shard_map/ppermute | solution.py:67
  14.9 6.1 %collective-permute-start.4 = (f32[2,128,256]{2,1,0:T(8,128)S(1)}, f32[2,128,256]{2,1,0:T(8,128)S(1)}, u32[]{:S(2)}, u32[]{:S(2)}) collective-permute-start(f32[2,128,256]{2,1,0:T(8,128)S(1)} %get-tuple-element.135), channel_id=1, source_target_pairs={{0,16},{1,4},{2,18},{3,6},{4,1},{5,8},{6,3},{7,10},{8,5},{9,12},{1... | collective-permute-start | bytes 786440 | tf_op jit(solution)/shard_map/ppermute | solution.py:67
  16.4 6.1 %collective-permute-start.2 = (f32[256,256]{1,0:T(8,128)S(1)}, f32[256,256]{1,0:T(8,128)S(1)}, u32[]{:S(2)}, u32[]{:S(2)}) collective-permute-start(f32[256,256]{1,0:T(8,128)S(1)} %bitcast.44), channel_id=1, source_target_pairs={{0,16},{1,2},{2,1},{3,19},{4,20},{5,6},{6,5},{7,23},{8,24},{9,10},... | collective-permute-start | bytes 786440 | tf_op jit(solution)/shard_map/ppermute | solution.py:67
  17.4 7.9 %collective-permute-start.3 = (f32[256,256]{1,0:T(8,128)S(1)}, f32[256,256]{1,0:T(8,128)S(1)}, u32[]{:S(2)}, u32[]{:S(2)}) collective-permute-start(f32[256,256]{1,0:T(8,128)S(1)} %bitcast.46), channel_id=1, source_target_pairs={{0,16},{1,2},{2,1},{3,19},{4,20},{5,6},{6,5},{7,23},{8,24},{9,10},... | collective-permute-start | bytes 786440 | tf_op jit(solution)/shard_map/ppermute | solution.py:67
  29.1 6.1 %collective-permute-start.8 = (f32[256,256]{1,0:T(8,128)S(1)}, f32[256,256]{1,0:T(8,128)S(1)}, u32[]{:S(2)}, u32[]{:S(2)}) collective-permute-start(f32[256,256]{1,0:T(8,128)S(1)} %bitcast.38), channel_id=1, source_target_pairs={{0,16},{1,2},{2,1},{3,19},{4,20},{5,6},{6,5},{7,23},{8,24},{9,10},... | collective-permute-start | bytes 786440 | tf_op jit(solution)/shard_map/ppermute | solution.py:67
  29.8 6.0 %collective-permute-start.10 = (f32[128,256]{1,0:T(8,128)S(1)}, f32[128,256]{1,0:T(8,128)S(1)}, u32[]{:S(2)}, u32[]{:S(2)}) collective-permute-start(f32[128,256]{1,0:T(8,128)S(1)} %get-tuple-element.153), channel_id=1, source_target_pairs={{0,1},{1,0},{2,3},{3,2},{4,5},{5,4},{6,7},{7,6},{8,9},{9,8},{10,11... | collective-permute-start | bytes 393224 | tf_op jit(solution)/shard_map/ppermute | solution.py:67
  32.5 4.7 %collective-permute-start.9 = (f32[128,256]{1,0:T(8,128)S(1)}, f32[128,256]{1,0:T(8,128)S(1)}, u32[]{:S(2)}, u32[]{:S(2)}) collective-permute-start(f32[128,256]{1,0:T(8,128)S(1)} %get-tuple-element.147), channel_id=1, source_target_pairs={{0,16},{1,4},{2,18},{3,6},{4,1},{5,8},{6,3},{7,10},{8,5},{9,12},{1... | collective-permute-start | bytes 393224 | tf_op jit(solution)/shard_map/ppermute | solution.py:67
  32.5 3.3 %collective-permute-start.11 = (f32[32,256]{1,0:T(8,128)S(1)}, f32[32,256]{1,0:T(8,128)S(1)}, u32[]{:S(2)}, u32[]{:S(2)}) collective-permute-start(f32[32,256]{1,0:T(8,128)S(1)} %get-tuple-element.154), channel_id=1, source_target_pairs={{0,2},{1,3},{2,0},{3,1},{4,6},{5,7},{6,4},{7,5},{8,10},{9,11},{10,... | collective-permute-start | bytes 98312 | tf_op jit(solution)/shard_map/ppermute | solution.py:67
  38.0 6.2 %collective-permute-start.13 = (f32[128,256]{1,0:T(8,128)S(1)}, f32[128,256]{1,0:T(8,128)S(1)}, u32[]{:S(2)}, u32[]{:S(2)}) collective-permute-start(f32[128,256]{1,0:T(8,128)S(1)} %get-tuple-element.159), channel_id=1, source_target_pairs={{0,16},{1,4},{2,18},{3,6},{4,1},{5,8},{6,3},{7,10},{8,5},{9,12},{1... | collective-permute-start | bytes 393224 | tf_op jit(solution)/shard_map/ppermute | solution.py:67
  39.2 5.0 %collective-permute-start.14 = (f32[128,256]{1,0:T(8,128)S(1)}, f32[128,256]{1,0:T(8,128)S(1)}, u32[]{:S(2)}, u32[]{:S(2)}) collective-permute-start(f32[128,256]{1,0:T(8,128)S(1)} %get-tuple-element.160), channel_id=1, source_target_pairs={{0,1},{1,0},{2,3},{3,2},{4,5},{5,4},{6,7},{7,6},{8,9},{9,8},{10,11... | collective-permute-start | bytes 393224 | tf_op jit(solution)/shard_map/ppermute | solution.py:67
  45.2 6.8 %collective-permute-start.17 = (f32[256,256]{1,0:T(8,128)S(1)}, f32[256,256]{1,0:T(8,128)S(1)}, u32[]{:S(2)}, u32[]{:S(2)}) collective-permute-start(f32[256,256]{1,0:T(8,128)S(1)} %bitcast.48), channel_id=1, source_target_pairs={{0,16},{1,2},{2,1},{3,19},{4,20},{5,6},{6,5},{7,23},{8,24},{9,10},... | collective-permute-start | bytes 786440 | tf_op jit(solution)/shard_map/ppermute | solution.py:67
  47.6 5.6 %collective-permute-start.18 = (f32[128,256]{1,0:T(8,128)S(1)}, f32[128,256]{1,0:T(8,128)S(1)}, u32[]{:S(2)}, u32[]{:S(2)}) collective-permute-start(f32[128,256]{1,0:T(8,128)S(1)} %get-tuple-element.164), channel_id=1, source_target_pairs={{0,16},{1,4},{2,18},{3,6},{4,1},{5,8},{6,3},{7,10},{8,5},{9,12},{1... | collective-permute-start | bytes 393224 | tf_op jit(solution)/shard_map/ppermute | solution.py:67
  48.0 5.3 %collective-permute-start.19 = (f32[128,256]{1,0:T(8,128)S(1)}, f32[128,256]{1,0:T(8,128)S(1)}, u32[]{:S(2)}, u32[]{:S(2)}) collective-permute-start(f32[128,256]{1,0:T(8,128)S(1)} %get-tuple-element.169), channel_id=1, source_target_pairs={{0,1},{1,0},{2,3},{3,2},{4,5},{5,4},{6,7},{7,6},{8,9},{9,8},{10,11... | collective-permute-start | bytes 393224 | tf_op jit(solution)/shard_map/ppermute | solution.py:67
  48.3 5.0 %collective-permute-start.21 = (f32[8,9,128]{2,1,0:T(8,128)S(1)}, f32[8,9,128]{2,1,0:T(8,128)S(1)}, u32[]{:S(2)}, u32[]{:S(2)}) collective-permute-start(f32[8,9,128]{2,1,0:T(8,128)S(1)} %get-tuple-element.172.rest_0_), channel_id=1, source_target_pairs={{0,8},{1,9},{2,10},{3,11},{4,12},{5,13},{6,14},{7,15},{8,0},{9,1},... | collective-permute-start | bytes 110600 | tf_op jit(solution)/shard_map/ppermute | solution.py:67
  54.1 6.3 %collective-permute-start.22 = (f32[128,256]{1,0:T(8,128)S(1)}, f32[128,256]{1,0:T(8,128)S(1)}, u32[]{:S(2)}, u32[]{:S(2)}) collective-permute-start(f32[128,256]{1,0:T(8,128)S(1)} %get-tuple-element.175), channel_id=1, source_target_pairs={{0,16},{1,4},{2,18},{3,6},{4,1},{5,8},{6,3},{7,10},{8,5},{9,12},{1... | collective-permute-start | bytes 393224 | tf_op jit(solution)/shard_map/ppermute | solution.py:67
  61.2 5.8 %collective-permute-start.25 = (f32[128,256]{1,0:T(8,128)S(1)}, f32[128,256]{1,0:T(8,128)S(1)}, u32[]{:S(2)}, u32[]{:S(2)}) collective-permute-start(f32[128,256]{1,0:T(8,128)S(1)} %get-tuple-element.180), channel_id=1, source_target_pairs={{0,16},{1,4},{2,18},{3,6},{4,1},{5,8},{6,3},{7,10},{8,5},{9,12},{1... | collective-permute-start | bytes 393224 | tf_op jit(solution)/shard_map/ppermute | solution.py:67
  62.6 4.4 %collective-permute-start.26 = (f32[128,256]{1,0:T(8,128)S(1)}, f32[128,256]{1,0:T(8,128)S(1)}, u32[]{:S(2)}, u32[]{:S(2)}) collective-permute-start(f32[128,256]{1,0:T(8,128)S(1)} %get-tuple-element.181), channel_id=1, source_target_pairs={{0,1},{1,0},{2,3},{3,2},{4,5},{5,4},{6,7},{7,6},{8,9},{9,8},{10,11... | collective-permute-start | bytes 393224 | tf_op jit(solution)/shard_map/ppermute | solution.py:67
  64.5 10.1 %collective-permute-start.29 = (f32[128,256]{1,0:T(8,128)S(1)}, f32[128,256]{1,0:T(8,128)S(1)}, u32[]{:S(2)}, u32[]{:S(2)}) collective-permute-start(f32[128,256]{1,0:T(8,128)S(1)} %get-tuple-element.188), channel_id=1, source_target_pairs={{0,1},{1,0},{2,3},{3,2},{4,5},{5,4},{6,7},{7,6},{8,9},{9,8},{10,11... | collective-permute-start | bytes 393224 | tf_op jit(solution)/shard_map/ppermute | solution.py:67
  64.7 9.8 %collective-permute-start.28 = (f32[128,256]{1,0:T(8,128)S(1)}, f32[128,256]{1,0:T(8,128)S(1)}, u32[]{:S(2)}, u32[]{:S(2)}) collective-permute-start(f32[128,256]{1,0:T(8,128)S(1)} %get-tuple-element.186), channel_id=1, source_target_pairs={{0,16},{1,4},{2,18},{3,6},{4,1},{5,8},{6,3},{7,10},{8,5},{9,12},{1... | collective-permute-start | bytes 393224 | tf_op jit(solution)/shard_map/ppermute | solution.py:67
  67.8 7.8 %collective-permute-start.31 = (f32[128,256]{1,0:T(8,128)S(1)}, f32[128,256]{1,0:T(8,128)S(1)}, u32[]{:S(2)}, u32[]{:S(2)}) collective-permute-start(f32[128,256]{1,0:T(8,128)S(1)} %get-tuple-element.192), channel_id=1, source_target_pairs={{0,16},{1,4},{2,18},{3,6},{4,1},{5,8},{6,3},{7,10},{8,5},{9,12},{1... | collective-permute-start | bytes 393224 | tf_op jit(solution)/shard_map/ppermute | solution.py:67
  69.8 5.9 %collective-permute-start.32 = (f32[128,256]{1,0:T(8,128)S(1)}, f32[128,256]{1,0:T(8,128)S(1)}, u32[]{:S(2)}, u32[]{:S(2)}) collective-permute-start(f32[128,256]{1,0:T(8,128)S(1)} %get-tuple-element.193), channel_id=1, source_target_pairs={{0,1},{1,0},{2,3},{3,2},{4,5},{5,4},{6,7},{7,6},{8,9},{9,8},{10,11... | collective-permute-start | bytes 393224 | tf_op jit(solution)/shard_map/ppermute | solution.py:67
  76.5 6.8 %collective-permute-start.34 = (f32[128,256]{1,0:T(8,128)S(1)}, f32[128,256]{1,0:T(8,128)S(1)}, u32[]{:S(2)}, u32[]{:S(2)}) collective-permute-start(f32[128,256]{1,0:T(8,128)S(1)} %get-tuple-element.197), channel_id=1, source_target_pairs={{0,16},{1,4},{2,18},{3,6},{4,1},{5,8},{6,3},{7,10},{8,5},{9,12},{1... | collective-permute-start | bytes 393224 | tf_op jit(solution)/shard_map/ppermute | solution.py:67
  79.3 4.0 %collective-permute-start.35 = (f32[128,256]{1,0:T(8,128)S(1)}, f32[128,256]{1,0:T(8,128)S(1)}, u32[]{:S(2)}, u32[]{:S(2)}) collective-permute-start(f32[128,256]{1,0:T(8,128)S(1)} %get-tuple-element.198), channel_id=1, source_target_pairs={{0,1},{1,0},{2,3},{3,2},{4,5},{5,4},{6,7},{7,6},{8,9},{9,8},{10,11... | collective-permute-start | bytes 393224 | tf_op jit(solution)/shard_map/ppermute | solution.py:67
  87.1 5.0 %collective-permute-start.37 = (f32[128,256]{1,0:T(8,128)S(1)}, f32[128,256]{1,0:T(8,128)S(1)}, u32[]{:S(2)}, u32[]{:S(2)}) collective-permute-start(f32[128,256]{1,0:T(8,128)S(1)} %get-tuple-element.208), channel_id=1, source_target_pairs={{0,16},{1,4},{2,18},{3,6},{4,1},{5,8},{6,3},{7,10},{8,5},{9,12},{1... | collective-permute-start | bytes 393224 | tf_op jit(solution)/shard_map/ppermute | solution.py:67
  87.6 4.6 %collective-permute-start.38 = (f32[128,256]{1,0:T(8,128)S(1)}, f32[128,256]{1,0:T(8,128)S(1)}, u32[]{:S(2)}, u32[]{:S(2)}) collective-permute-start(f32[128,256]{1,0:T(8,128)S(1)} %get-tuple-element.209), channel_id=1, source_target_pairs={{0,1},{1,0},{2,3},{3,2},{4,5},{5,4},{6,7},{7,6},{8,9},{9,8},{10,11... | collective-permute-start | bytes 393224 | tf_op jit(solution)/shard_map/ppermute | solution.py:67
  93.0 5.0 %collective-permute-start.40 = (f32[128,256]{1,0:T(8,128)S(1)}, f32[128,256]{1,0:T(8,128)S(1)}, u32[]{:S(2)}, u32[]{:S(2)}) collective-permute-start(f32[128,256]{1,0:T(8,128)S(1)} %get-tuple-element.215), channel_id=1, source_target_pairs={{0,16},{1,4},{2,18},{3,6},{4,1},{5,8},{6,3},{7,10},{8,5},{9,12},{1... | collective-permute-start | bytes 393224 | tf_op jit(solution)/shard_map/ppermute | solution.py:67
  93.8 4.3 %collective-permute-start.41 = (f32[128,256]{1,0:T(8,128)S(1)}, f32[128,256]{1,0:T(8,128)S(1)}, u32[]{:S(2)}, u32[]{:S(2)}) collective-permute-start(f32[128,256]{1,0:T(8,128)S(1)} %get-tuple-element.216), channel_id=1, source_target_pairs={{0,1},{1,0},{2,3},{3,2},{4,5},{5,4},{6,7},{7,6},{8,9},{9,8},{10,11... | collective-permute-start | bytes 393224 | tf_op jit(solution)/shard_map/ppermute | solution.py:67
  98.9 5.0 %collective-permute-start.43 = (f32[128,256]{1,0:T(8,128)S(1)}, f32[128,256]{1,0:T(8,128)S(1)}, u32[]{:S(2)}, u32[]{:S(2)}) collective-permute-start(f32[128,256]{1,0:T(8,128)S(1)} %get-tuple-element.222), channel_id=1, source_target_pairs={{0,16},{1,4},{2,18},{3,6},{4,1},{5,8},{6,3},{7,10},{8,5},{9,12},{1... | collective-permute-start | bytes 393224 | tf_op jit(solution)/shard_map/ppermute | solution.py:67
  99.6 4.3 %collective-permute-start.44 = (f32[128,256]{1,0:T(8,128)S(1)}, f32[128,256]{1,0:T(8,128)S(1)}, u32[]{:S(2)}, u32[]{:S(2)}) collective-permute-start(f32[128,256]{1,0:T(8,128)S(1)} %get-tuple-element.223), channel_id=1, source_target_pairs={{0,1},{1,0},{2,3},{3,2},{4,5},{5,4},{6,7},{7,6},{8,9},{9,8},{10,11... | collective-permute-start | bytes 393224 | tf_op jit(solution)/shard_map/ppermute | solution.py:67
  104.7 5.0 %collective-permute-start.46 = (f32[128,256]{1,0:T(8,128)S(1)}, f32[128,256]{1,0:T(8,128)S(1)}, u32[]{:S(2)}, u32[]{:S(2)}) collective-permute-start(f32[128,256]{1,0:T(8,128)S(1)} %get-tuple-element.229), channel_id=1, source_target_pairs={{0,16},{1,4},{2,18},{3,6},{4,1},{5,8},{6,3},{7,10},{8,5},{9,12},{1... | collective-permute-start | bytes 393224 | tf_op jit(solution)/shard_map/ppermute | solution.py:67
  105.5 4.3 %collective-permute-start.47 = (f32[128,256]{1,0:T(8,128)S(1)}, f32[128,256]{1,0:T(8,128)S(1)}, u32[]{:S(2)}, u32[]{:S(2)}) collective-permute-start(f32[128,256]{1,0:T(8,128)S(1)} %get-tuple-element.230), channel_id=1, source_target_pairs={{0,1},{1,0},{2,3},{3,2},{4,5},{5,4},{6,7},{7,6},{8,9},{9,8},{10,11... | collective-permute-start | bytes 393224 | tf_op jit(solution)/shard_map/ppermute | solution.py:67
  110.6 5.0 %collective-permute-start.49 = (f32[128,256]{1,0:T(8,128)S(1)}, f32[128,256]{1,0:T(8,128)S(1)}, u32[]{:S(2)}, u32[]{:S(2)}) collective-permute-start(f32[128,256]{1,0:T(8,128)S(1)} %get-tuple-element.236), channel_id=1, source_target_pairs={{0,16},{1,4},{2,18},{3,6},{4,1},{5,8},{6,3},{7,10},{8,5},{9,12},{1... | collective-permute-start | bytes 393224 | tf_op jit(solution)/shard_map/ppermute | solution.py:67
  111.4 4.3 %collective-permute-start.50 = (f32[128,256]{1,0:T(8,128)S(1)}, f32[128,256]{1,0:T(8,128)S(1)}, u32[]{:S(2)}, u32[]{:S(2)}) collective-permute-start(f32[128,256]{1,0:T(8,128)S(1)} %get-tuple-element.237), channel_id=1, source_target_pairs={{0,1},{1,0},{2,3},{3,2},{4,5},{5,4},{6,7},{7,6},{8,9},{9,8},{10,11... | collective-permute-start | bytes 393224 | tf_op jit(solution)/shard_map/ppermute | solution.py:67
  116.4 5.0 %collective-permute-start.52 = (f32[128,256]{1,0:T(8,128)S(1)}, f32[128,256]{1,0:T(8,128)S(1)}, u32[]{:S(2)}, u32[]{:S(2)}) collective-permute-start(f32[128,256]{1,0:T(8,128)S(1)} %get-tuple-element.243), channel_id=1, source_target_pairs={{0,16},{1,4},{2,18},{3,6},{4,1},{5,8},{6,3},{7,10},{8,5},{9,12},{1... | collective-permute-start | bytes 393224 | tf_op jit(solution)/shard_map/ppermute | solution.py:67
  117.2 4.3 %collective-permute-start.53 = (f32[128,256]{1,0:T(8,128)S(1)}, f32[128,256]{1,0:T(8,128)S(1)}, u32[]{:S(2)}, u32[]{:S(2)}) collective-permute-start(f32[128,256]{1,0:T(8,128)S(1)} %get-tuple-element.244), channel_id=1, source_target_pairs={{0,1},{1,0},{2,3},{3,2},{4,5},{5,4},{6,7},{7,6},{8,9},{9,8},{10,11... | collective-permute-start | bytes 393224 | tf_op jit(solution)/shard_map/ppermute | solution.py:67
  122.3 6.5 %collective-permute-start.58 = (f32[256,256]{1,0:T(8,128)S(1)}, f32[256,256]{1,0:T(8,128)S(1)}, u32[]{:S(2)}, u32[]{:S(2)}) collective-permute-start(f32[256,256]{1,0:T(8,128)S(1)} %get-tuple-element.246.cur.prev), channel_id=1, source_target_pairs={{0,16},{1,2},{2,1},{3,19},{4,20},{5,6},{6,5},{7,23},{8,24},{9,10},... | collective-permute-start | bytes 786440 | tf_op jit(solution)/shard_map/ppermute | solution.py:67
  123.3 5.4 %collective-permute-start.55 = (f32[128,256]{1,0:T(8,128)S(1)}, f32[128,256]{1,0:T(8,128)S(1)}, u32[]{:S(2)}, u32[]{:S(2)}) collective-permute-start(f32[128,256]{1,0:T(8,128)S(1)} %get-tuple-element.250), channel_id=1, source_target_pairs={{0,16},{1,4},{2,18},{3,6},{4,1},{5,8},{6,3},{7,10},{8,5},{9,12},{1... | collective-permute-start | bytes 393224 | tf_op jit(solution)/shard_map/ppermute | solution.py:67
  124.1 4.7 %collective-permute-start.56 = (f32[128,256]{1,0:T(8,128)S(1)}, f32[128,256]{1,0:T(8,128)S(1)}, u32[]{:S(2)}, u32[]{:S(2)}) collective-permute-start(f32[128,256]{1,0:T(8,128)S(1)} %get-tuple-element.251), channel_id=1, source_target_pairs={{0,1},{1,0},{2,3},{3,2},{4,5},{5,4},{6,7},{7,6},{8,9},{9,8},{10,11... | collective-permute-start | bytes 393224 | tf_op jit(solution)/shard_map/ppermute | solution.py:67
  125.3 3.5 %collective-permute-start.57 = (f32[32,256]{1,0:T(8,128)S(1)}, f32[32,256]{1,0:T(8,128)S(1)}, u32[]{:S(2)}, u32[]{:S(2)}) collective-permute-start(f32[32,256]{1,0:T(8,128)S(1)} %get-tuple-element.252), channel_id=1, source_target_pairs={{0,2},{1,3},{2,0},{3,1},{4,6},{5,7},{6,4},{7,5},{8,10},{9,11},{10,... | collective-permute-start | bytes 98312 | tf_op jit(solution)/shard_map/ppermute | solution.py:67
  130.5 14.9 %collective-permute-start.64 = (f32[256,256]{1,0:T(8,128)S(1)}, f32[256,256]{1,0:T(8,128)S(1)}, u32[]{:S(2)}, u32[]{:S(2)}) collective-permute-start(f32[256,256]{1,0:T(8,128)S(1)} %get-tuple-element.261.refs_4_), channel_id=1, source_target_pairs={{0,16},{1,2},{2,1},{3,19},{4,20},{5,6},{6,5},{7,23},{8,24},{9,10},... | collective-permute-start | bytes 786440 | tf_op jit(solution)/shard_map/ppermute | solution.py:67
  135.3 6.4 %collective-permute-start.60 = (f32[2,64,128]{2,1,0:T(8,128)S(1)}, f32[2,64,128]{2,1,0:T(8,128)S(1)}, u32[]{:S(2)}, u32[]{:S(2)}) collective-permute-start(f32[2,64,128]{2,1,0:T(8,128)S(1)} %get-tuple-element.257), channel_id=1, source_target_pairs={{0,0},{1,2},{2,1},{3,3},{4,4},{5,6},{6,5},{7,7},{8,8},{9,10},{10,9... | collective-permute-start | bytes 196616 | tf_op jit(solution)/shard_map/ppermute | solution.py:67
  137.3 6.4 %collective-permute-start.61 = (f32[2,64,128]{2,1,0:T(8,128)S(1)}, f32[2,64,128]{2,1,0:T(8,128)S(1)}, u32[]{:S(2)}, u32[]{:S(2)}) collective-permute-start(f32[2,64,128]{2,1,0:T(8,128)S(1)} %get-tuple-element.258), channel_id=1, source_target_pairs={{0,4},{1,6},{2,5},{3,7},{4,8},{5,10},{6,9},{7,11},{8,12},{9,14},{1... | collective-permute-start | bytes 196616 | tf_op jit(solution)/shard_map/ppermute | solution.py:67
  137.3 6.4 %collective-permute-start.62 = (f32[2,64,128]{2,1,0:T(8,128)S(1)}, f32[2,64,128]{2,1,0:T(8,128)S(1)}, u32[]{:S(2)}, u32[]{:S(2)}) collective-permute-start(f32[2,64,128]{2,1,0:T(8,128)S(1)} %get-tuple-element.259), channel_id=1, source_target_pairs={{0,8},{1,10},{2,9},{3,11},{4,12},{5,14},{6,13},{7,15},{8,0},{9,2},... | collective-permute-start | bytes 196616 | tf_op jit(solution)/shard_map/ppermute | solution.py:67
  137.4 8.0 %collective-permute-start.63 = (f32[2,64,128]{2,1,0:T(8,128)S(1)}, f32[2,64,128]{2,1,0:T(8,128)S(1)}, u32[]{:S(2)}, u32[]{:S(2)}) collective-permute-start(f32[2,64,128]{2,1,0:T(8,128)S(1)} %get-tuple-element.260), channel_id=1, source_target_pairs={{0,12},{1,14},{2,13},{3,15},{4,0},{5,2},{6,1},{7,3},{8,4},{9,6},{1... | collective-permute-start | bytes 196616 | tf_op jit(solution)/shard_map/ppermute | solution.py:67
  (31 other events, 114.9 us)

commit v4 on v3

--- a/solution.py
+++ b/solution.py
@@ -60,7 +60,7 @@
         return self.perm(lambda q, y, c: (q ^ bit, y, c) if (q ^ bit) < self.nq else None)
 
     def spread(self, shift):
-        return self.perm(lambda q, y, c: ((q + shift) % self.nq, c, y))
+        return self.perm(lambda q, y, c: (q ^ shift, c, y))
 
 
 def send(value, pairs):
@@ -161,12 +161,23 @@
     yo[...] = jnp.where(flags[1] == 0, new[size - 4 * COLS :], new[0 : 4 * COLS])
 
 
-def settle_kernel(rim_count, flags, a, b, recv_a, recv_b, a_out, b_out, *outs):
+def load_kernel(flags, *refs):
+    half = len(refs) // 2
+    for source, out in zip(refs[:half], refs[half:]):
+        out[...] = source[...]
+
+
+def settle_kernel(flags, a, b, recv_a, recv_b, a_out, b_out, *outs):
     keep = flags[0] == flags[1]
     for n, (own, recv, out) in enumerate(((a, recv_a, a_out), (b, recv_b, b_out))):
         out[...] = jnp.where(keep, own[...], recv[...])
-        if n < rim_count:
-            rims(flags, out, *(ref.at[n] for ref in outs))
+        rims(flags, out, *(ref.at[n] for ref in outs))
+
+
+def settle_model_kernel(flags, a, b, recv, a_out, b_out):
+    keep = flags[0] == flags[1]
+    a_out[...] = jnp.where(keep, a[...], recv[0])
+    b_out[...] = jnp.where(keep, b[...], recv[1])
 
 
 def settle_one(with_rims, flags, own, recv, out, *outs):
@@ -193,7 +204,9 @@
     for here, sums, sums_z, di, dx, dz in inner_differences(cur, near, deep):
         center = cur[here]
         change = k0[here] * ((sums + sums_z) + (3.0 * SECOND[0] * 5040) * center)
-        change = change - (ki[here] * di + kx[here] * dx + kz[here] * dz) + inj[here]
+        change = change - (ki[here] * di + kx[here] * dx + kz[here] * dz)
+        if inj is not None:
+            change = change + inj[here]
         out[here] = (center - prev[here]) + (center + change)
 
 
@@ -267,26 +280,39 @@
         obs[s * CAP : s * CAP + CAP, :] = sent[:, s * steps : s * steps + steps]
 
 
-def adjoint_inner_kernel(t, flags, cur, prev, k0, ki, kx, kz, near, deep, seen_state, spot, pick,
+def injection(t, state, spot, pick, at, obs):
+    high, low = split(state[...])
+    seen = at[...] * (mm(pick[...], high) + mm(pick[...], low))
+    residual = jnp.sum(seen, axis=1, keepdims=True) - obs[:, t : t + 1]
+    high, low = split(at[...] * residual)
+    return mm(spot[...], high) + mm(spot[...], low)
+
+
+def adjoint_inner_kernel(t, flags, cur, prev, k0, ki, kx, kz, near, deep, state, spot, pick,
                          at, obs, *rest):
-    if len(rest) == 1:
-        part, = rest
-    elif len(rest) == 4:
+    if len(rest) == 4:
         change, image, part, image_out = rest
         image_out[...] = cur[...] * change[...] + image[...]
     else:
         now, mid, before, part, image_out = rest
         image_out[...] = cur[...] * ((now[...] - mid[...]) - (mid[...] - before[...]))
-    high, low = split(seen_state[...])
-    seen = at[...] * (mm(pick[...], high) + mm(pick[...], low))
-    residual = jnp.sum(seen, axis=1, keepdims=True) - obs[:, t : t + 1]
-    high, low = split(at[...] * residual)
-    inj = mm(spot[...], high) + mm(spot[...], low)
-    inner(cur, prev, k0, ki, kx, kz, near, deep, inj, part)
-
-
-def last_kernel(scale, flags, part, k0, ki, kx, zm, cm, ym, side, edge, image, change, vel, prev,
-                got, new, mine, other, prev_out):
+    inner(cur, prev, k0, ki, kx, kz, near, deep, injection(t, state, spot, pick, at, obs), part)
+
+
+def first_inner_kernel(flags, cur, prev, k0, ki, kx, kz, near, deep, part):
+    inner(cur, prev, k0, ki, kx, kz, near, deep, None, part)
+
+
+def turn_kernel(t, flags, part, k0, ki, kx, zm, cm, ym, side, edge, u_part, u_zm, u_cm, u_ym,
+                spot, pick, at, obs, new, u_new, zo, co, yo):
+    outer(flags, part, k0, ki, kx, zm, cm, ym, side, edge, new)
+    outer(flags, u_part, k0, ki, kx, u_zm, u_cm, u_ym, side, edge, u_new)
+    u_new[...] += injection(t, new, spot, pick, at, obs)
+    rims(flags, u_new, zo, co, yo)
+
+
+def last_kernel(scale, flags, part, k0, ki, kx, zm, cm, ym, side, edge, image, change, vel,
+                new, mine, other):
     outer(flags, part, k0, ki, kx, zm, cm, ym, side, edge, new)
     raw = (image[...] + new[...] * change[...]) * scale / vel[...]
     count, height, lanes = mine.shape
@@ -299,22 +325,21 @@
             for m in (2 * n, 2 * n + 1))
         mine[n] = jnp.where(flags[0] == 0, even, odd)
         other[n] = jnp.where(flags[0] == 0, odd, even)
-    prev_out[...] = jnp.where(flags[0] == flags[1], prev[...], got[...])
 
 
 def join_kernel(flags, mine, got, *outs):
-    count = len(outs)
     for s, out in enumerate(outs):
-        to = flags[3] + s
-        to = jnp.where(to >= count, to - count, to)
+        to = jnp.bitwise_xor(flags[3], s)
         a, b = mine[to], got[to]
         out[0] = jnp.where(flags[0] == 0, a, b)
         out[1] = jnp.where(flags[0] == 0, b, a)
 
 
 def filter_kernel(flags, *refs):
-    *pieces, own, got, out, state = refs
-    state[...] = jnp.where(flags[0] == flags[1], own[...], got[...])
+    *pieces, own, got, prev, prev_got, out, state, prev_state = refs
+    keep = flags[0] == flags[1]
+    state[...] = jnp.where(keep, own[...], got[...])
+    prev_state[...] = jnp.where(keep, prev[...], prev_got[...])
     height, lanes = pieces[0].shape[1:]
     chunk, rows, full = out.shape
     groups = lanes // chunk
@@ -323,8 +348,7 @@
     y = lax.broadcasted_iota(jnp.int32, shape, 1)
     at = lax.broadcasted_iota(jnp.int32, shape, 0)
     within = jnp.bitwise_and(at, 2 * COLS - 1)
-    place = q * (2 * COLS) - (at - within)
-    place = jnp.where(place < 0, place + full, place) + within
+    place = jnp.bitwise_xor(q * (2 * COLS), at - within) + within
     weights = jnp.exp(jnp.abs(y - place).astype(F32) * (-1.0 / SMOOTH))
     weights = split(weights / jnp.sum(weights, axis=0, keepdims=True))
     for n in range(height // COLS):
@@ -401,13 +425,16 @@
     log_density, fwd_now, velocity = flat(log_density), flat(fwd_now), flat(velocity)
     fwd_before, adj_now, adj_before = flat(fwd_before), flat(adj_now), flat(adj_before)
     got = [send(v, swap_perm) for v in (log_density, fwd_now)]
-    density, p_now, *out = call(
-        functools.partial(settle_kernel, 2), "settle",
-        [field, field] + [shaped(2, *r.shape) for r in rim], flags, log_density, fwd_now, *got)
+    got_model = send(jnp.stack([velocity, fwd_before]), swap_perm)
+    log_density, fwd_now, velocity, fwd_before, adj_now, adj_before = call(
+        load_kernel, "load", [field] * 6, flags, log_density, fwd_now, velocity, fwd_before,
+        adj_now, adj_before)
+    density, p_now, *out = call(settle_kernel, "settle",
+                                [field, field] + [shaped(2, *r.shape) for r in rim],
+                                flags, log_density, fwd_now, *got)
     zm, cm, ym = halo(*out)
-    got = [send(after(v, out[0]), swap_perm) for v in (velocity, fwd_before)]
-    vel, p_before = call(functools.partial(settle_kernel, 0), "settle_model", [field, field],
-                         flags, velocity, fwd_before, *got)
+    vel, p_before = call(settle_model_kernel, "settle_model", [field, field],
+                         flags, velocity, fwd_before, got_model)
     k0, ki, kx, kz = call(model_kernel, "model", [field] * 4, flags, density, zm, cm, ym, near,
                           deep, side, edge, vel)
     halos = (zm[1], cm[1], ym[1])
@@ -423,6 +450,9 @@
     live = jnp.arange(CAP)[None, :] < rec_counts[0][:, None]
     cells = jnp.where(live.reshape(-1), rec_cells[0], -1)
     lists = jnp.concatenate([observed, cells[None, :].astype(F32)], axis=0)[None]
+
+    lag = 2 if 2 * (len(stages) - 1) < steps - 1 else 1
+    moved = send(lists, stages[0][0])
 
     states = [p_before, p_now]
     changes = []
@@ -436,72 +466,77 @@
                              flags, *args)
         changes += change
         if t == 1:
-            u_now, *u_rim = call(functools.partial(settle_one, True), "settle_adjoint", [field] + rim,
-                                 flags, adj_now, got_now)
+            got_now = send(after(adj_now, part), swap_perm)
+        if t == 2:
+            u_now, *u_rim = call(functools.partial(settle_one, True), "settle_adjoint",
+                                 [field] + rim, flags, adj_now, after(got_now, part))
             part = after(part, u_now)
+            got_before = send(after(adj_before, part), swap_perm)
         if t == 3:
             u_before, = call(functools.partial(settle_one, False), "settle_before", [field],
-                             flags, adj_before, got_before)
+                             flags, adj_before, after(got_before, part))
             part = after(part, u_before)
-        if t == 6:
-            part = after(part, *u_halos)
+            u_halos = halo(*(after(r, part) for r in u_rim))
+        if t == steps - 1:
+            u_part, = call(first_inner_kernel, "adjoint_inner", [field], flags, u_now, u_before,
+                           k0, ki, kx, kz, near, deep)
+            slots = subs * CAP
+            receivers = call(
+                lists_kernel, "lists",
+                [jax.ShapeDtypeStruct((size, slots), BF16),
+                 jax.ShapeDtypeStruct((slots, size), BF16), shaped(slots, depth),
+                 shaped(slots, steps)], flags, lists)
+            new, u_new, *out = call(
+                functools.partial(turn_kernel, t), "turn", [field, field] + rim, flags, part,
+                k0, ki, kx, *halos, side, edge, u_part, *u_halos, *receivers)
+            states.append(new)
+            break
         args = [part, k0, ki, kx, *halos, side, edge]
         outs = [field] + rim
-        stage = t if t < len(stages) else None
+        stage = t // lag if t % lag == 0 and t // lag < len(stages) else None
         if stage is not None:
-            args += [lists, send(after(lists, out[0]) if t else lists, stages[t][0])]
+            args += [lists, moved]
             outs = outs + [shaped(2 * lists.shape[0], *lists.shape[1:])]
-        new, zo, co, yo, *merged = call(functools.partial(outer_kernel, stage), "forward_outer", outs,
-                                        flags, *args)
-        out = (zo, co, yo)
-        lists = merged[0] if merged else lists
+        elif t % lag == 1 and t // lag + 1 < len(stages):
+            moved = send(after(lists, part), stages[t // lag + 1][0])
+        new, *out = call(functools.partial(outer_kernel, stage), "forward_outer", outs, flags, *args)
+        if stage is not None:
+            lists = out.pop()
+            if lag == 1 and stage + 1 < len(stages):
+                moved = send(lists, stages[stage + 1][0])
         states.append(new)
-        if t < steps - 1:
-            halos = halo(*out)
-        if t == 0:
-            got_now = send(after(adj_now, zo), swap_perm)
-        if t == 2:
-            got_before = send(after(adj_before, zo), swap_perm)
-        if t == 4:
-            u_halos = halo(*(after(r, zo) for r in u_rim))
-
-    slots = subs * CAP
-    receivers = call(
-        lists_kernel, "lists",
-        [jax.ShapeDtypeStruct((size, slots), BF16), jax.ShapeDtypeStruct((slots, size), BF16),
-         shaped(slots, depth), shaped(slots, steps)], flags, lists)
-
-    halos = u_halos
+        halos = halo(*out)
+
+    halos = halo(*out)
+    u_before, u_now = u_now, u_new
     image = []
     chunk = depth // nx
     half = shaped(nq, size * chunk // 128, 128)
-    for j in range(steps):
+    for j in range(1, steps):
         t = steps - 1 - j
-        args = [u_now, u_before, k0, ki, kx, kz, near, deep, states[t + 2], *receivers]
-        outs = [field]
-        if j > 0:
-            args += [changes[t + 1], *image] if image else states[:-4:-1]
-            outs = [field, field]
-        part, *image = call(functools.partial(adjoint_inner_kernel, t), "adjoint_inner", outs,
-                            flags, *args)
+        terms = [changes[t + 1], *image] if image else states[:-4:-1]
+        part, *image = call(
+            functools.partial(adjoint_inner_kernel, t), "adjoint_inner", [field, field], flags,
+            u_now, u_before, k0, ki, kx, kz, near, deep, states[t + 2], *receivers, *terms)
         args = [part, k0, ki, kx, *halos, side, edge]
         if j == steps - 1:
-            args += [*image, changes[0], vel, u_now, send(u_now, swap_perm)]
-            u_last, mine, other, adj_prev = call(
-                functools.partial(last_kernel, 2.0 / steps), "last", [field, half, half, field],
-                flags, *args)
+            got_prev = send(after(u_now, part), swap_perm)
+            u_last, mine, other = call(
+                functools.partial(last_kernel, 2.0 / steps), "last", [field, half, half],
+                flags, *args, *image, changes[0], vel)
             break
         u_before = u_now
         u_now, *out = call(functools.partial(outer_kernel, None), "adjoint_outer", [field] + rim,
                            flags, *args)
         halos = halo(*out)
 
-    got = send(u_last, swap_perm)
     pieces = call(join_kernel, "join", [shaped(2, *half.shape[1:])] * nq, flags, mine,
                   send(other, c_perm))
+    got = send(after(u_last, pieces[0]), swap_perm)
     pieces = [send(value, plan.spread(s)) for s, value in enumerate(pieces)]
-    gradient, adj_out = call(filter_kernel, "filter", [shaped(chunk, rows, nx * cols), field], flags,
-                             *pieces, u_last, got)
+    gradient, adj_out, adj_prev = call(
+        filter_kernel, "filter", [shaped(chunk, rows, nx * cols), field, field], flags, *pieces,
+        u_last, got, u_now, got_prev)
     block = (rows, cols, depth)
     return gradient, adj_out.reshape(block), adj_prev.reshape(block)
 

time: 148 us -> 142 us (0.959)
  waiting for transfers between devices: 35.5 us -> 29.3 us
  local copies, waits for them, and re-layouts: 2.18 us -> 3.7 us
    ppermute x65 -> x64, waiting for transfers between devices: 35.5 us -> 29.3 us  [send(): return lax.ppermute(value, ALL, pairs)]
    another operation x0 -> x1, other arithmetic: none -> 1.95 us  [per_device(): got_model = send(jnp.stack([velocity, fwd_before]), swap_perm)]
    unnamed x29 -> x35, local copies, waits for them, and re-layouts: 1.89 us -> 3.41 us
    ppermute x65 -> x64, starting transfers between devices: 62.6 us -> 62.5 us  [send(): return lax.ppermute(value, ALL, pairs)]
  transfers between devices with their start and end apart: 65 -> 64, of which waited for: 25 -> 20; matrix products, arithmetic and copies ran while one was open for 2% -> 2% of each run, Pallas kernels for 17% -> 20%
where the time goes in v4:
time: 142 us
  starting transfers between devices  62.5 us (44%)
  Pallas kernels  42.8 us (30%)
  waiting for transfers between devices  29.3 us (21%)
  local copies, waits for them, and re-layouts  3.7 us (3%)
  other arithmetic  2.27 us (2%)
    ppermute x64, starting transfers between devices, send(): return lax.ppermute(value, ALL, pairs)  62.5 us
    pallas_call x40, Pallas kernels, call(): pl.pallas_call(kernel, name=name, out_shape=outs, in_specs=specs, out_spe...  42.8 us
    ppermute x64, waiting for transfers between devices, send(): return lax.ppermute(value, ALL, pairs)  29.3 us
    unnamed x35, local copies, waits for them, and re-layouts  3.41 us
  transfers between devices with their start and end apart: 64, of which 20 were waited for; matrix products, arithmetic and copies ran while one was open for 2% of the time, Pallas kernels for 20%

profile of v4, /device:TPU:1, one launch (start us, length us, event | category | flops | bytes accessed | tf_op | source)
XLA Modules:
  0.0 141.8 jit_solution(8306570669867020046)
XLA Ops:
  2.2 2.6 %collective-permute-start.1 = (f32[256,256]{1,0:T(8,128)}, f32[256,256]{1,0:T(8,128)S(1)}, u32[]{:S(2)}, u32[]{:S(2)}) collective-permute-start(f32[256,256]{1,0:T(8,128)} %bitcast.46), channel_id=1, source_target_pairs={{0,16},{1,2},{2,1},{3,19},{4,20},{5,6},{6,5},{7,23},{8,24},{9,10},... | collective-permute-start | bytes 786440 | tf_op jit(solution)/shard_map/ppermute | solution.py:67
  4.9 1.9 %pad_maximum_fusion = f32[2,256,256]{2,1,0:T(8,128)} fusion(f32[1,256,256]{2,1,0:T(8,128)} %bitcast.34, f32[1,256,256]{2,1,0:T(8,128)} %bitcast.32), kind=kLoop, calls=%fused_computation | loop fusion | flops 131072 | bytes 1048576 | tf_op jit(solution)/shard_map/stack | solution.py:428
  6.9 1.7 %collective-permute-start.2 = (f32[2,256,256]{2,1,0:T(8,128)}, f32[2,256,256]{2,1,0:T(8,128)S(1)}, u32[]{:S(2)}, u32[]{:S(2)}) collective-permute-start(f32[2,256,256]{2,1,0:T(8,128)} %pad_maximum_fusion), channel_id=1, source_target_pairs={{0,16},{1,2},{2,1},{3,19},{4,20},{5,6},{6,5},{7,23},{8,24},{9,10},... | collective-permute-start | bytes 1572872 | tf_op jit(solution)/shard_map/ppermute | solution.py:67
  10.6 1.6 %collective-permute-done.recv_a = f32[256,256]{1,0:T(8,128)S(1)} collective-permute-done((f32[256,256]{1,0:T(8,128)}, f32[256,256]{1,0:T(8,128)S(1)}, u32[]{:S(2)}, u32[]{:S(2)}) %collective-permute-start) | collective-permute-done | bytes 262176 | tf_op jit(solution)/shard_map/ppermute | solution.py:67
  12.2 1.5 %settle.1 = (f32[256,256]{1,0:T(8,128)S(1)}, f32[256,256]{1,0:T(8,128)S(1)}, f32[2,128,256]{2,1,0:T(8,128)}, f32[2,128,256]{2,1,0:T(8,128)}, f32[2,32,256]{2,1,0:T(8,128)S(1)}) custom-call(s32[8]{0:T(128)S(1)} %stack.32.flags, f32[256,256]{1,0:T(8,128)S(1)} %get-tuple-element.141.a, f32[256,256]{1,0:T(8,128)S(1)} %get-tuple-element.142.b, ...), custom_call_target="tpu_custom_call" | custom-call | flops 5000000 | bytes 2000000 | tf_op jit(solution)/shard_map/settle/pallas_call | solution.py:370
  13.7 1.2 collective-permute-start.5
  14.9 1.8 %collective-permute-start.3 = (f32[2,128,256]{2,1,0:T(8,128)}, f32[2,128,256]{2,1,0:T(8,128)S(1)}, u32[]{:S(2)}, u32[]{:S(2)}) collective-permute-start(f32[2,128,256]{2,1,0:T(8,128)} %get-tuple-element.148), channel_id=1, source_target_pairs={{0,16},{1,4},{2,18},{3,6},{4,1},{5,8},{6,3},{7,10},{8,5},{9,12},{1... | collective-permute-start | bytes 786440 | tf_op jit(solution)/shard_map/ppermute | solution.py:67
  18.2 3.1 %collective-permute-done.3.zm = f32[2,128,256]{2,1,0:T(8,128)S(1)} collective-permute-done((f32[2,128,256]{2,1,0:T(8,128)}, f32[2,128,256]{2,1,0:T(8,128)S(1)}, u32[]{:S(2)}, u32[]{:S(2)}) %collective-permute-start.3) | collective-permute-done | bytes 262176 | tf_op jit(solution)/shard_map/ppermute | solution.py:67
  25.4 1.2 forward_inner.9
  27.6 1.9 %collective-permute-start.7 = (f32[128,256]{1,0:T(8,128)S(1)}, f32[128,256]{1,0:T(8,128)S(1)}, u32[]{:S(2)}, u32[]{:S(2)}) collective-permute-start(f32[128,256]{1,0:T(8,128)S(1)} %get-tuple-element.158), channel_id=1, source_target_pairs={{0,16},{1,4},{2,18},{3,6},{4,1},{5,8},{6,3},{7,10},{8,5},{9,12},{1... | collective-permute-start | bytes 393224 | tf_op jit(solution)/shard_map/ppermute | solution.py:67
  30.0 3.0 %collective-permute-done.9.ym = f32[32,256]{1,0:T(8,128)S(1)} collective-permute-done((f32[32,256]{1,0:T(8,128)S(1)}, f32[32,256]{1,0:T(8,128)S(1)}, u32[]{:S(2)}, u32[]{:S(2)}) %collective-permute-start.9) | collective-permute-done | bytes 32800 | tf_op jit(solution)/shard_map/ppermute | solution.py:67
  33.9 1.2 forward_inner.10
  35.7 1.6 %collective-permute-start.15 = (f32[256,256]{1,0:T(8,128)S(1)}, f32[256,256]{1,0:T(8,128)S(1)}, u32[]{:S(2)}, u32[]{:S(2)}) collective-permute-start(f32[256,256]{1,0:T(8,128)S(1)} %get-tuple-element.176.own), channel_id=1, source_target_pairs={{0,16},{1,2},{2,1},{3,19},{4,20},{5,6},{6,5},{7,23},{8,24},{9,10},... | collective-permute-start | bytes 786440 | tf_op jit(solution)/shard_map/ppermute | solution.py:67
  37.2 1.8 %collective-permute-start.11 = (f32[128,256]{1,0:T(8,128)S(1)}, f32[128,256]{1,0:T(8,128)S(1)}, u32[]{:S(2)}, u32[]{:S(2)}) collective-permute-start(f32[128,256]{1,0:T(8,128)S(1)} %get-tuple-element.168), channel_id=1, source_target_pairs={{0,16},{1,4},{2,18},{3,6},{4,1},{5,8},{6,3},{7,10},{8,5},{9,12},{1... | collective-permute-start | bytes 393224 | tf_op jit(solution)/shard_map/ppermute | solution.py:67
  40.0 1.5 %collective-permute-start.14 = (f32[2,9,128]{2,1,0:T(8,128)S(1)}, f32[2,9,128]{2,1,0:T(8,128)S(1)}, u32[]{:S(2)}, u32[]{:S(2)}) collective-permute-start(f32[2,9,128]{2,1,0:T(8,128)S(1)} %get-tuple-element.172.rest_0_), channel_id=1, source_target_pairs={{0,2},{1,3},{2,0},{3,1},{4,6},{5,7},{6,4},{7,5},{8,10},{9,11},{10,... | collective-permute-start | bytes 27656 | tf_op jit(solution)/shard_map/ppermute | solution.py:67
  41.4 1.9 %collective-permute-done.14.rest_1_ = f32[2,9,128]{2,1,0:T(8,128)S(1)} collective-permute-done((f32[2,9,128]{2,1,0:T(8,128)S(1)}, f32[2,9,128]{2,1,0:T(8,128)S(1)}, u32[]{:S(2)}, u32[]{:S(2)}) %collective-permute-start.14) | collective-permute-done | bytes 9248 | tf_op jit(solution)/shard_map/ppermute | solution.py:67
  44.2 1.6 %collective-permute-start.16 = (f32[128,256]{1,0:T(8,128)S(1)}, f32[128,256]{1,0:T(8,128)S(1)}, u32[]{:S(2)}, u32[]{:S(2)}) collective-permute-start(f32[128,256]{1,0:T(8,128)S(1)} %get-tuple-element.179), channel_id=1, source_target_pairs={{0,16},{1,4},{2,18},{3,6},{4,1},{5,8},{6,3},{7,10},{8,5},{9,12},{1... | collective-permute-start | bytes 393224 | tf_op jit(solution)/shard_map/ppermute | solution.py:67
  45.8 2.3 %collective-permute-start.17 = (f32[128,256]{1,0:T(8,128)S(1)}, f32[128,256]{1,0:T(8,128)S(1)}, u32[]{:S(2)}, u32[]{:S(2)}) collective-permute-start(f32[128,256]{1,0:T(8,128)S(1)} %get-tuple-element.180), channel_id=1, source_target_pairs={{0,1},{1,0},{2,3},{3,2},{4,5},{5,4},{6,7},{7,6},{8,9},{9,8},{10,11... | collective-permute-start | bytes 393224 | tf_op jit(solution)/shard_map/ppermute | solution.py:67
  49.9 1.3 collective-permute-done.18.ym
  52.3 1.7 %collective-permute-start.20 = (f32[128,256]{1,0:T(8,128)S(1)}, f32[128,256]{1,0:T(8,128)S(1)}, u32[]{:S(2)}, u32[]{:S(2)}) collective-permute-start(f32[128,256]{1,0:T(8,128)S(1)} %get-tuple-element.185), channel_id=1, source_target_pairs={{0,1},{1,0},{2,3},{3,2},{4,5},{5,4},{6,7},{7,6},{8,9},{9,8},{10,11... | collective-permute-start | bytes 393224 | tf_op jit(solution)/shard_map/ppermute | solution.py:67
  55.3 1.8 %collective-permute-done.22.rest_1_ = f32[4,9,128]{2,1,0:T(8,128)S(1)} collective-permute-done((f32[4,9,128]{2,1,0:T(8,128)S(1)}, f32[4,9,128]{2,1,0:T(8,128)S(1)}, u32[]{:S(2)}, u32[]{:S(2)}) %collective-permute-start.22) | collective-permute-done | bytes 18464 | tf_op jit(solution)/shard_map/ppermute | solution.py:67
  58.0 1.3 collective-permute-start.23
  60.0 1.6 %collective-permute-start.25 = (f32[32,256]{1,0:T(8,128)S(1)}, f32[32,256]{1,0:T(8,128)S(1)}, u32[]{:S(2)}, u32[]{:S(2)}) collective-permute-start(f32[32,256]{1,0:T(8,128)S(1)} %get-tuple-element.193), channel_id=1, source_target_pairs={{0,2},{1,3},{2,0},{3,1},{4,6},{5,7},{6,4},{7,5},{8,10},{9,11},{10,... | collective-permute-start | bytes 98312 | tf_op jit(solution)/shard_map/ppermute | solution.py:67
  66.2 1.3 collective-permute-start.28
  68.7 3.3 %collective-permute-done.29.rest_1_ = f32[8,9,128]{2,1,0:T(8,128)S(1)} collective-permute-done((f32[8,9,128]{2,1,0:T(8,128)S(1)}, f32[8,9,128]{2,1,0:T(8,128)S(1)}, u32[]{:S(2)}, u32[]{:S(2)}) %collective-permute-start.29) | collective-permute-done | bytes 36896 | tf_op jit(solution)/shard_map/ppermute | solution.py:67
  73.5 1.2 collective-permute-start.31
  74.7 1.2 collective-permute-start.35
  76.0 1.8 %collective-permute-done.35.u_ym = f32[32,256]{1,0:T(8,128)S(1)} collective-permute-done((f32[32,256]{1,0:T(8,128)S(1)}, f32[32,256]{1,0:T(8,128)S(1)}, u32[]{:S(2)}, u32[]{:S(2)}) %collective-permute-start.35) | collective-permute-done | bytes 32800 | tf_op jit(solution)/shard_map/ppermute | solution.py:67
  77.8 1.2 collective-permute-start.32
  80.8 1.2 forward_inner.15
  82.1 1.5 %turn.1 = (f32[256,256]{1,0:T(8,128)S(1)}, f32[256,256]{1,0:T(8,128)S(1)}, f32[128,256]{1,0:T(8,128)S(1)}, f32[128,256]{1,0:T(8,128)S(1)}, f32[32,256]{1,0:T(8,128)S(1)}) custom-call(s32[8]{0:T(128)S(1)} %stack.32.flags, f32[256,256]{1,0:T(8,128)S(1)} %get-tuple-element.202.part, f32[256,256]{1,0:T(8,128)S(1)} %get-tuple-element.152.k0, ...), custom_call_target="tpu_custom_call" | custom-call | flops 5000000 | bytes 2000000 | tf_op jit(solution)/shard_map/turn/pallas_call | solution.py:370
  83.6 1.9 %collective-permute-start.36 = (f32[128,256]{1,0:T(8,128)S(1)}, f32[128,256]{1,0:T(8,128)S(1)}, u32[]{:S(2)}, u32[]{:S(2)}) collective-permute-start(f32[128,256]{1,0:T(8,128)S(1)} %get-tuple-element.220), channel_id=1, source_target_pairs={{0,16},{1,4},{2,18},{3,6},{4,1},{5,8},{6,3},{7,10},{8,5},{9,12},{1... | collective-permute-start | bytes 393224 | tf_op jit(solution)/shard_map/ppermute | solution.py:67
  86.4 1.7 %adjoint_inner.9 = (f32[256,256]{1,0:T(8,128)S(1)}, f32[256,256]{1,0:T(8,128)S(1)}) custom-call(s32[8]{0:T(128)S(1)} %stack.32.flags, f32[256,256]{1,0:T(8,128)S(1)} %get-tuple-element.217.cur.prev, f32[256,256]{1,0:T(8,128)S(1)} %get-tuple-element.166.cur.prev, f32[256,256]{1,0:T(8,128)S(1)} %get-tuple-element.152.k0, ...), custom_call_target="tpu_custom_call" | custom-call | flops 5000000 | bytes 2000000 | tf_op jit(solution)/shard_map/adjoint_inner/pallas_call | solution.py:370
  92.4 1.5 %adjoint_inner.10 = (f32[256,256]{1,0:T(8,128)S(1)}, f32[256,256]{1,0:T(8,128)S(1)}) custom-call(s32[8]{0:T(128)S(1)} %stack.32.flags, f32[256,256]{1,0:T(8,128)S(1)} %get-tuple-element.223.cur.prev, f32[256,256]{1,0:T(8,128)S(1)} %get-tuple-element.217.cur.prev, f32[256,256]{1,0:T(8,128)S(1)} %get-tuple-element.152.k0, ...), custom_call_target="tpu_custom_call" | custom-call | flops 5000000 | bytes 2000000 | tf_op jit(solution)/shard_map/adjoint_inner/pallas_call | solution.py:370
  96.4 1.4 collective-permute-start.43
  98.3 1.5 %adjoint_inner.11 = (f32[256,256]{1,0:T(8,128)S(1)}, f32[256,256]{1,0:T(8,128)S(1)}) custom-call(s32[8]{0:T(128)S(1)} %stack.32.flags, f32[256,256]{1,0:T(8,128)S(1)} %get-tuple-element.230.cur.prev, f32[256,256]{1,0:T(8,128)S(1)} %get-tuple-element.223.cur.prev, f32[256,256]{1,0:T(8,128)S(1)} %get-tuple-element.152.k0, ...), custom_call_target="tpu_custom_call" | custom-call | flops 5000000 | bytes 2000000 | tf_op jit(solution)/shard_map/adjoint_inner/pallas_call | solution.py:370
  102.4 1.2 collective-permute-start.46
  104.2 1.5 %adjoint_inner.12 = (f32[256,256]{1,0:T(8,128)S(1)}, f32[256,256]{1,0:T(8,128)S(1)}) custom-call(s32[8]{0:T(128)S(1)} %stack.32.flags, f32[256,256]{1,0:T(8,128)S(1)} %get-tuple-element.237.cur.prev, f32[256,256]{1,0:T(8,128)S(1)} %get-tuple-element.230.cur.prev, f32[256,256]{1,0:T(8,128)S(1)} %get-tuple-element.152.k0, ...), custom_call_target="tpu_custom_call" | custom-call | flops 5000000 | bytes 2000000 | tf_op jit(solution)/shard_map/adjoint_inner/pallas_call | solution.py:370
  108.3 1.2 collective-permute-start.49
  110.0 1.5 %adjoint_inner.13 = (f32[256,256]{1,0:T(8,128)S(1)}, f32[256,256]{1,0:T(8,128)S(1)}) custom-call(s32[8]{0:T(128)S(1)} %stack.32.flags, f32[256,256]{1,0:T(8,128)S(1)} %get-tuple-element.244.cur.prev, f32[256,256]{1,0:T(8,128)S(1)} %get-tuple-element.237.cur.prev, f32[256,256]{1,0:T(8,128)S(1)} %get-tuple-element.152.k0, ...), custom_call_target="tpu_custom_call" | custom-call | flops 5000000 | bytes 2000000 | tf_op jit(solution)/shard_map/adjoint_inner/pallas_call | solution.py:370
  114.2 1.2 collective-permute-start.52
  115.9 1.5 %adjoint_inner.14 = (f32[256,256]{1,0:T(8,128)S(1)}, f32[256,256]{1,0:T(8,128)S(1)}) custom-call(s32[8]{0:T(128)S(1)} %stack.32.flags, f32[256,256]{1,0:T(8,128)S(1)} %get-tuple-element.251.cur.prev, f32[256,256]{1,0:T(8,128)S(1)} %get-tuple-element.244.cur.prev, f32[256,256]{1,0:T(8,128)S(1)} %get-tuple-element.152.k0, ...), custom_call_target="tpu_custom_call" | custom-call | flops 5000000 | bytes 2000000 | tf_op jit(solution)/shard_map/adjoint_inner/pallas_call | solution.py:370
  120.0 1.2 collective-permute-start.55
  121.7 1.5 %adjoint_inner.15 = (f32[256,256]{1,0:T(8,128)S(1)}, f32[256,256]{1,0:T(8,128)S(1)}) custom-call(s32[8]{0:T(128)S(1)} %stack.32.flags, f32[256,256]{1,0:T(8,128)S(1)} %get-tuple-element.275.cur.refs_6_, f32[256,256]{1,0:T(8,128)S(1)} %get-tuple-element.251.cur.prev, f32[256,256]{1,0:T(8,128)S(1)} %get-tuple-element.152.k0, ...), custom_call_target="tpu_custom_call" | custom-call | flops 5000000 | bytes 2000000 | tf_op jit(solution)/shard_map/adjoint_inner/pallas_call | solution.py:370
  129.3 4.8 %collective-permute-start.61 = (f32[2,64,128]{2,1,0:T(8,128)S(1)}, f32[2,64,128]{2,1,0:T(8,128)S(1)}, u32[]{:S(2)}, u32[]{:S(2)}) collective-permute-start(f32[2,64,128]{2,1,0:T(8,128)S(1)} %get-tuple-element.272), channel_id=1, source_target_pairs={{0,12},{1,14},{2,13},{3,15},{4,8},{5,10},{6,9},{7,11},{8,4},{9,6},... | collective-permute-start | bytes 196616 | tf_op jit(solution)/shard_map/ppermute | solution.py:67
  134.1 2.7 %collective-permute-start.58 = (f32[2,64,128]{2,1,0:T(8,128)S(1)}, f32[2,64,128]{2,1,0:T(8,128)S(1)}, u32[]{:S(2)}, u32[]{:S(2)}) collective-permute-start(f32[2,64,128]{2,1,0:T(8,128)S(1)} %get-tuple-element.269), channel_id=1, source_target_pairs={{0,0},{1,2},{2,1},{3,3},{4,4},{5,6},{6,5},{7,7},{8,8},{9,10},{10,9... | collective-permute-start | bytes 196616 | tf_op jit(solution)/shard_map/ppermute | solution.py:67
  137.4 2.3 %collective-permute-done.58.refs_0_ = f32[2,64,128]{2,1,0:T(8,128)S(1)} collective-permute-done((f32[2,64,128]{2,1,0:T(8,128)S(1)}, f32[2,64,128]{2,1,0:T(8,128)S(1)}, u32[]{:S(2)}, u32[]{:S(2)}) %collective-permute-start.58) | collective-permute-done | bytes 65568 | tf_op jit(solution)/shard_map/ppermute | solution.py:67
  139.7 2.1 %filter.1 = (f32[32,32,64]{2,1,0:T(8,128)}, f32[256,256]{1,0:T(8,128)}, f32[256,256]{1,0:T(8,128)}) custom-call(s32[8]{0:T(128)S(1)} %stack.32.flags, f32[2,64,128]{2,1,0:T(8,128)S(1)} %collective-permute-done.58.refs_0_, f32[2,64,128]{2,1,0:T(8,128)S(1)} %collective-permute-done.59.refs_1_, f32[2,64,128]{2,1,0:T(8,128)S(1)} %collective-permute-done.60.refs_2_, ...), custom_call_target="tpu_custom_call" | custom-call | flops 5000000 | bytes 2000000 | tf_op jit(solution)/shard_map/filter/pallas_call | solution.py:370
  (171 shorter events, 56.1 us)
Async XLA Ops:
  2.1 22.4 %collective-permute-start.6 = (f32[1,9,128]{2,1,0:T(8,128)S(1)}, f32[1,9,128]{2,1,0:T(8,128)S(1)}, u32[]{:S(2)}, u32[]{:S(2)}) collective-permute-start(f32[1,9,128]{2,1,0:T(8,128)S(1)} %maximum_bitcast_fusion.rest_0_), channel_id=1, source_target_pairs={{0,1},{1,0},{2,3},{3,2},{4,5},{5,4},{6,7},{7,6},{8,9},{9,8},{10,11... | collective-permute-start | bytes 13832 | tf_op jit(solution)/shard_map/ppermute | solution.py:67
  2.2 8.4 %collective-permute-start.1 = (f32[256,256]{1,0:T(8,128)}, f32[256,256]{1,0:T(8,128)S(1)}, u32[]{:S(2)}, u32[]{:S(2)}) collective-permute-start(f32[256,256]{1,0:T(8,128)} %bitcast.46), channel_id=1, source_target_pairs={{0,16},{1,2},{2,1},{3,19},{4,20},{5,6},{6,5},{7,23},{8,24},{9,10},... | collective-permute-start | bytes 786440 | tf_op jit(solution)/shard_map/ppermute | solution.py:67
  4.8 7.4 %collective-permute-start = (f32[256,256]{1,0:T(8,128)}, f32[256,256]{1,0:T(8,128)S(1)}, u32[]{:S(2)}, u32[]{:S(2)}) collective-permute-start(f32[256,256]{1,0:T(8,128)} %bitcast.48), channel_id=1, source_target_pairs={{0,16},{1,2},{2,1},{3,19},{4,20},{5,6},{6,5},{7,23},{8,24},{9,10},... | collective-permute-start | bytes 786440 | tf_op jit(solution)/shard_map/ppermute | solution.py:67
  6.9 14.4 %collective-permute-start.2 = (f32[2,256,256]{2,1,0:T(8,128)}, f32[2,256,256]{2,1,0:T(8,128)S(1)}, u32[]{:S(2)}, u32[]{:S(2)}) collective-permute-start(f32[2,256,256]{2,1,0:T(8,128)} %pad_maximum_fusion), channel_id=1, source_target_pairs={{0,16},{1,2},{2,1},{3,19},{4,20},{5,6},{6,5},{7,23},{8,24},{9,10},... | collective-permute-start | bytes 1572872 | tf_op jit(solution)/shard_map/ppermute | solution.py:67
  13.7 4.5 %collective-permute-start.5 = (f32[2,32,256]{2,1,0:T(8,128)S(1)}, f32[2,32,256]{2,1,0:T(8,128)S(1)}, u32[]{:S(2)}, u32[]{:S(2)}) collective-permute-start(f32[2,32,256]{2,1,0:T(8,128)S(1)} %get-tuple-element.150), channel_id=1, source_target_pairs={{0,2},{1,3},{2,0},{3,1},{4,6},{5,7},{6,4},{7,5},{8,10},{9,11},{10,... | collective-permute-start | bytes 196616 | tf_op jit(solution)/shard_map/ppermute | solution.py:67
  14.9 6.4 %collective-permute-start.3 = (f32[2,128,256]{2,1,0:T(8,128)}, f32[2,128,256]{2,1,0:T(8,128)S(1)}, u32[]{:S(2)}, u32[]{:S(2)}) collective-permute-start(f32[2,128,256]{2,1,0:T(8,128)} %get-tuple-element.148), channel_id=1, source_target_pairs={{0,16},{1,4},{2,18},{3,6},{4,1},{5,8},{6,3},{7,10},{8,5},{9,12},{1... | collective-permute-start | bytes 786440 | tf_op jit(solution)/shard_map/ppermute | solution.py:67
  17.5 3.7 %collective-permute-start.4 = (f32[2,128,256]{2,1,0:T(8,128)}, f32[2,128,256]{2,1,0:T(8,128)S(1)}, u32[]{:S(2)}, u32[]{:S(2)}) collective-permute-start(f32[2,128,256]{2,1,0:T(8,128)} %get-tuple-element.149), channel_id=1, source_target_pairs={{0,1},{1,0},{2,3},{3,2},{4,5},{5,4},{6,7},{7,6},{8,9},{9,8},{10,11... | collective-permute-start | bytes 786440 | tf_op jit(solution)/shard_map/ppermute | solution.py:67
  26.6 8.5 %collective-permute-start.10 = (f32[256,256]{1,0:T(8,128)S(1)}, f32[256,256]{1,0:T(8,128)S(1)}, u32[]{:S(2)}, u32[]{:S(2)}) collective-permute-start(f32[256,256]{1,0:T(8,128)S(1)} %get-tuple-element.164.own), channel_id=1, source_target_pairs={{0,16},{1,2},{2,1},{3,19},{4,20},{5,6},{6,5},{7,23},{8,24},{9,10},... | collective-permute-start | bytes 786440 | tf_op jit(solution)/shard_map/ppermute | solution.py:67
  27.6 5.4 %collective-permute-start.7 = (f32[128,256]{1,0:T(8,128)S(1)}, f32[128,256]{1,0:T(8,128)S(1)}, u32[]{:S(2)}, u32[]{:S(2)}) collective-permute-start(f32[128,256]{1,0:T(8,128)S(1)} %get-tuple-element.158), channel_id=1, source_target_pairs={{0,16},{1,4},{2,18},{3,6},{4,1},{5,8},{6,3},{7,10},{8,5},{9,12},{1... | collective-permute-start | bytes 393224 | tf_op jit(solution)/shard_map/ppermute | solution.py:67
  29.6 3.5 %collective-permute-start.8 = (f32[128,256]{1,0:T(8,128)S(1)}, f32[128,256]{1,0:T(8,128)S(1)}, u32[]{:S(2)}, u32[]{:S(2)}) collective-permute-start(f32[128,256]{1,0:T(8,128)S(1)} %get-tuple-element.159), channel_id=1, source_target_pairs={{0,1},{1,0},{2,3},{3,2},{4,5},{5,4},{6,7},{7,6},{8,9},{9,8},{10,11... | collective-permute-start | bytes 393224 | tf_op jit(solution)/shard_map/ppermute | solution.py:67
  29.6 3.5 %collective-permute-start.9 = (f32[32,256]{1,0:T(8,128)S(1)}, f32[32,256]{1,0:T(8,128)S(1)}, u32[]{:S(2)}, u32[]{:S(2)}) collective-permute-start(f32[32,256]{1,0:T(8,128)S(1)} %get-tuple-element.160), channel_id=1, source_target_pairs={{0,2},{1,3},{2,0},{3,1},{4,6},{5,7},{6,4},{7,5},{8,10},{9,11},{10,... | collective-permute-start | bytes 98312 | tf_op jit(solution)/shard_map/ppermute | solution.py:67
  35.7 13.6 %collective-permute-start.15 = (f32[256,256]{1,0:T(8,128)S(1)}, f32[256,256]{1,0:T(8,128)S(1)}, u32[]{:S(2)}, u32[]{:S(2)}) collective-permute-start(f32[256,256]{1,0:T(8,128)S(1)} %get-tuple-element.176.own), channel_id=1, source_target_pairs={{0,16},{1,2},{2,1},{3,19},{4,20},{5,6},{6,5},{7,23},{8,24},{9,10},... | collective-permute-start | bytes 786440 | tf_op jit(solution)/shard_map/ppermute | solution.py:67
  37.2 6.1 %collective-permute-start.11 = (f32[128,256]{1,0:T(8,128)S(1)}, f32[128,256]{1,0:T(8,128)S(1)}, u32[]{:S(2)}, u32[]{:S(2)}) collective-permute-start(f32[128,256]{1,0:T(8,128)S(1)} %get-tuple-element.168), channel_id=1, source_target_pairs={{0,16},{1,4},{2,18},{3,6},{4,1},{5,8},{6,3},{7,10},{8,5},{9,12},{1... | collective-permute-start | bytes 393224 | tf_op jit(solution)/shard_map/ppermute | solution.py:67
  39.1 4.3 %collective-permute-start.12 = (f32[128,256]{1,0:T(8,128)S(1)}, f32[128,256]{1,0:T(8,128)S(1)}, u32[]{:S(2)}, u32[]{:S(2)}) collective-permute-start(f32[128,256]{1,0:T(8,128)S(1)} %get-tuple-element.169), channel_id=1, source_target_pairs={{0,1},{1,0},{2,3},{3,2},{4,5},{5,4},{6,7},{7,6},{8,9},{9,8},{10,11... | collective-permute-start | bytes 393224 | tf_op jit(solution)/shard_map/ppermute | solution.py:67
  44.2 7.0 %collective-permute-start.16 = (f32[128,256]{1,0:T(8,128)S(1)}, f32[128,256]{1,0:T(8,128)S(1)}, u32[]{:S(2)}, u32[]{:S(2)}) collective-permute-start(f32[128,256]{1,0:T(8,128)S(1)} %get-tuple-element.179), channel_id=1, source_target_pairs={{0,16},{1,4},{2,18},{3,6},{4,1},{5,8},{6,3},{7,10},{8,5},{9,12},{1... | collective-permute-start | bytes 393224 | tf_op jit(solution)/shard_map/ppermute | solution.py:67
  45.8 5.4 %collective-permute-start.17 = (f32[128,256]{1,0:T(8,128)S(1)}, f32[128,256]{1,0:T(8,128)S(1)}, u32[]{:S(2)}, u32[]{:S(2)}) collective-permute-start(f32[128,256]{1,0:T(8,128)S(1)} %get-tuple-element.180), channel_id=1, source_target_pairs={{0,1},{1,0},{2,3},{3,2},{4,5},{5,4},{6,7},{7,6},{8,9},{9,8},{10,11... | collective-permute-start | bytes 393224 | tf_op jit(solution)/shard_map/ppermute | solution.py:67
  52.0 5.1 %collective-permute-start.19 = (f32[128,256]{1,0:T(8,128)S(1)}, f32[128,256]{1,0:T(8,128)S(1)}, u32[]{:S(2)}, u32[]{:S(2)}) collective-permute-start(f32[128,256]{1,0:T(8,128)S(1)} %get-tuple-element.184), channel_id=1, source_target_pairs={{0,16},{1,4},{2,18},{3,6},{4,1},{5,8},{6,3},{7,10},{8,5},{9,12},{1... | collective-permute-start | bytes 393224 | tf_op jit(solution)/shard_map/ppermute | solution.py:67
  52.3 4.8 %collective-permute-start.20 = (f32[128,256]{1,0:T(8,128)S(1)}, f32[128,256]{1,0:T(8,128)S(1)}, u32[]{:S(2)}, u32[]{:S(2)}) collective-permute-start(f32[128,256]{1,0:T(8,128)S(1)} %get-tuple-element.185), channel_id=1, source_target_pairs={{0,1},{1,0},{2,3},{3,2},{4,5},{5,4},{6,7},{7,6},{8,9},{9,8},{10,11... | collective-permute-start | bytes 393224 | tf_op jit(solution)/shard_map/ppermute | solution.py:67
  58.0 5.2 %collective-permute-start.23 = (f32[128,256]{1,0:T(8,128)S(1)}, f32[128,256]{1,0:T(8,128)S(1)}, u32[]{:S(2)}, u32[]{:S(2)}) collective-permute-start(f32[128,256]{1,0:T(8,128)S(1)} %get-tuple-element.191), channel_id=1, source_target_pairs={{0,16},{1,4},{2,18},{3,6},{4,1},{5,8},{6,3},{7,10},{8,5},{9,12},{1... | collective-permute-start | bytes 393224 | tf_op jit(solution)/shard_map/ppermute | solution.py:67
  59.3 3.8 %collective-permute-start.24 = (f32[128,256]{1,0:T(8,128)S(1)}, f32[128,256]{1,0:T(8,128)S(1)}, u32[]{:S(2)}, u32[]{:S(2)}) collective-permute-start(f32[128,256]{1,0:T(8,128)S(1)} %get-tuple-element.192), channel_id=1, source_target_pairs={{0,1},{1,0},{2,3},{3,2},{4,5},{5,4},{6,7},{7,6},{8,9},{9,8},{10,11... | collective-permute-start | bytes 393224 | tf_op jit(solution)/shard_map/ppermute | solution.py:67
  64.0 8.6 %collective-permute-start.26 = (f32[128,256]{1,0:T(8,128)S(1)}, f32[128,256]{1,0:T(8,128)S(1)}, u32[]{:S(2)}, u32[]{:S(2)}) collective-permute-start(f32[128,256]{1,0:T(8,128)S(1)} %get-tuple-element.196), channel_id=1, source_target_pairs={{0,16},{1,4},{2,18},{3,6},{4,1},{5,8},{6,3},{7,10},{8,5},{9,12},{1... | collective-permute-start | bytes 393224 | tf_op jit(solution)/shard_map/ppermute | solution.py:67
  65.1 7.5 %collective-permute-start.27 = (f32[128,256]{1,0:T(8,128)S(1)}, f32[128,256]{1,0:T(8,128)S(1)}, u32[]{:S(2)}, u32[]{:S(2)}) collective-permute-start(f32[128,256]{1,0:T(8,128)S(1)} %get-tuple-element.197), channel_id=1, source_target_pairs={{0,1},{1,0},{2,3},{3,2},{4,5},{5,4},{6,7},{7,6},{8,9},{9,8},{10,11... | collective-permute-start | bytes 393224 | tf_op jit(solution)/shard_map/ppermute | solution.py:67
  66.1 5.9 %collective-permute-start.29 = (f32[8,9,128]{2,1,0:T(8,128)S(1)}, f32[8,9,128]{2,1,0:T(8,128)S(1)}, u32[]{:S(2)}, u32[]{:S(2)}) collective-permute-start(f32[8,9,128]{2,1,0:T(8,128)S(1)} %get-tuple-element.200.rest_0_), channel_id=1, source_target_pairs={{0,8},{1,9},{2,10},{3,11},{4,12},{5,13},{6,14},{7,15},{8,0},{9,1},... | collective-permute-start | bytes 110600 | tf_op jit(solution)/shard_map/ppermute | solution.py:67
  66.2 6.4 %collective-permute-start.28 = (f32[32,256]{1,0:T(8,128)S(1)}, f32[32,256]{1,0:T(8,128)S(1)}, u32[]{:S(2)}, u32[]{:S(2)}) collective-permute-start(f32[32,256]{1,0:T(8,128)S(1)} %get-tuple-element.198), channel_id=1, source_target_pairs={{0,2},{1,3},{2,0},{3,1},{4,6},{5,7},{6,4},{7,5},{8,10},{9,11},{10,... | collective-permute-start | bytes 98312 | tf_op jit(solution)/shard_map/ppermute | solution.py:67
  67.4 14.7 %collective-permute-start.33 = (f32[128,256]{1,0:T(8,128)S(1)}, f32[128,256]{1,0:T(8,128)S(1)}, u32[]{:S(2)}, u32[]{:S(2)}) collective-permute-start(f32[128,256]{1,0:T(8,128)S(1)} %get-tuple-element.207), channel_id=1, source_target_pairs={{0,16},{1,4},{2,18},{3,6},{4,1},{5,8},{6,3},{7,10},{8,5},{9,12},{1... | collective-permute-start | bytes 393224 | tf_op jit(solution)/shard_map/ppermute | solution.py:67
  72.0 10.0 %collective-permute-start.34 = (f32[128,256]{1,0:T(8,128)S(1)}, f32[128,256]{1,0:T(8,128)S(1)}, u32[]{:S(2)}, u32[]{:S(2)}) collective-permute-start(f32[128,256]{1,0:T(8,128)S(1)} %get-tuple-element.209), channel_id=1, source_target_pairs={{0,1},{1,0},{2,3},{3,2},{4,5},{5,4},{6,7},{7,6},{8,9},{9,8},{10,11... | collective-permute-start | bytes 393224 | tf_op jit(solution)/shard_map/ppermute | solution.py:67
  73.4 8.7 %collective-permute-start.30 = (f32[128,256]{1,0:T(8,128)S(1)}, f32[128,256]{1,0:T(8,128)S(1)}, u32[]{:S(2)}, u32[]{:S(2)}) collective-permute-start(f32[128,256]{1,0:T(8,128)S(1)} %get-tuple-element.203), channel_id=1, source_target_pairs={{0,16},{1,4},{2,18},{3,6},{4,1},{5,8},{6,3},{7,10},{8,5},{9,12},{1... | collective-permute-start | bytes 393224 | tf_op jit(solution)/shard_map/ppermute | solution.py:67
  73.5 8.6 %collective-permute-start.31 = (f32[128,256]{1,0:T(8,128)S(1)}, f32[128,256]{1,0:T(8,128)S(1)}, u32[]{:S(2)}, u32[]{:S(2)}) collective-permute-start(f32[128,256]{1,0:T(8,128)S(1)} %get-tuple-element.204), channel_id=1, source_target_pairs={{0,1},{1,0},{2,3},{3,2},{4,5},{5,4},{6,7},{7,6},{8,9},{9,8},{10,11... | collective-permute-start | bytes 393224 | tf_op jit(solution)/shard_map/ppermute | solution.py:67
  77.8 4.3 %collective-permute-start.32 = (f32[32,256]{1,0:T(8,128)S(1)}, f32[32,256]{1,0:T(8,128)S(1)}, u32[]{:S(2)}, u32[]{:S(2)}) collective-permute-start(f32[32,256]{1,0:T(8,128)S(1)} %get-tuple-element.205), channel_id=1, source_target_pairs={{0,2},{1,3},{2,0},{3,1},{4,6},{5,7},{6,4},{7,5},{8,10},{9,11},{10,... | collective-permute-start | bytes 98312 | tf_op jit(solution)/shard_map/ppermute | solution.py:67
  83.6 5.2 %collective-permute-start.36 = (f32[128,256]{1,0:T(8,128)S(1)}, f32[128,256]{1,0:T(8,128)S(1)}, u32[]{:S(2)}, u32[]{:S(2)}) collective-permute-start(f32[128,256]{1,0:T(8,128)S(1)} %get-tuple-element.220), channel_id=1, source_target_pairs={{0,16},{1,4},{2,18},{3,6},{4,1},{5,8},{6,3},{7,10},{8,5},{9,12},{1... | collective-permute-start | bytes 393224 | tf_op jit(solution)/shard_map/ppermute | solution.py:67
  89.7 5.2 %collective-permute-start.39 = (f32[128,256]{1,0:T(8,128)S(1)}, f32[128,256]{1,0:T(8,128)S(1)}, u32[]{:S(2)}, u32[]{:S(2)}) collective-permute-start(f32[128,256]{1,0:T(8,128)S(1)} %get-tuple-element.227), channel_id=1, source_target_pairs={{0,16},{1,4},{2,18},{3,6},{4,1},{5,8},{6,3},{7,10},{8,5},{9,12},{1... | collective-permute-start | bytes 393224 | tf_op jit(solution)/shard_map/ppermute | solution.py:67
  90.8 4.1 %collective-permute-start.40 = (f32[128,256]{1,0:T(8,128)S(1)}, f32[128,256]{1,0:T(8,128)S(1)}, u32[]{:S(2)}, u32[]{:S(2)}) collective-permute-start(f32[128,256]{1,0:T(8,128)S(1)} %get-tuple-element.228), channel_id=1, source_target_pairs={{0,1},{1,0},{2,3},{3,2},{4,5},{5,4},{6,7},{7,6},{8,9},{9,8},{10,11... | collective-permute-start | bytes 393224 | tf_op jit(solution)/shard_map/ppermute | solution.py:67
  95.8 5.0 %collective-permute-start.42 = (f32[128,256]{1,0:T(8,128)S(1)}, f32[128,256]{1,0:T(8,128)S(1)}, u32[]{:S(2)}, u32[]{:S(2)}) collective-permute-start(f32[128,256]{1,0:T(8,128)S(1)} %get-tuple-element.234), channel_id=1, source_target_pairs={{0,16},{1,4},{2,18},{3,6},{4,1},{5,8},{6,3},{7,10},{8,5},{9,12},{1... | collective-permute-start | bytes 393224 | tf_op jit(solution)/shard_map/ppermute | solution.py:67
  96.4 4.5 %collective-permute-start.43 = (f32[128,256]{1,0:T(8,128)S(1)}, f32[128,256]{1,0:T(8,128)S(1)}, u32[]{:S(2)}, u32[]{:S(2)}) collective-permute-start(f32[128,256]{1,0:T(8,128)S(1)} %get-tuple-element.235), channel_id=1, source_target_pairs={{0,1},{1,0},{2,3},{3,2},{4,5},{5,4},{6,7},{7,6},{8,9},{9,8},{10,11... | collective-permute-start | bytes 393224 | tf_op jit(solution)/shard_map/ppermute | solution.py:67
  101.7 5.0 %collective-permute-start.45 = (f32[128,256]{1,0:T(8,128)S(1)}, f32[128,256]{1,0:T(8,128)S(1)}, u32[]{:S(2)}, u32[]{:S(2)}) collective-permute-start(f32[128,256]{1,0:T(8,128)S(1)} %get-tuple-element.241), channel_id=1, source_target_pairs={{0,16},{1,4},{2,18},{3,6},{4,1},{5,8},{6,3},{7,10},{8,5},{9,12},{1... | collective-permute-start | bytes 393224 | tf_op jit(solution)/shard_map/ppermute | solution.py:67
  102.4 4.3 %collective-permute-start.46 = (f32[128,256]{1,0:T(8,128)S(1)}, f32[128,256]{1,0:T(8,128)S(1)}, u32[]{:S(2)}, u32[]{:S(2)}) collective-permute-start(f32[128,256]{1,0:T(8,128)S(1)} %get-tuple-element.242), channel_id=1, source_target_pairs={{0,1},{1,0},{2,3},{3,2},{4,5},{5,4},{6,7},{7,6},{8,9},{9,8},{10,11... | collective-permute-start | bytes 393224 | tf_op jit(solution)/shard_map/ppermute | solution.py:67
  107.5 5.0 %collective-permute-start.48 = (f32[128,256]{1,0:T(8,128)S(1)}, f32[128,256]{1,0:T(8,128)S(1)}, u32[]{:S(2)}, u32[]{:S(2)}) collective-permute-start(f32[128,256]{1,0:T(8,128)S(1)} %get-tuple-element.248), channel_id=1, source_target_pairs={{0,16},{1,4},{2,18},{3,6},{4,1},{5,8},{6,3},{7,10},{8,5},{9,12},{1... | collective-permute-start | bytes 393224 | tf_op jit(solution)/shard_map/ppermute | solution.py:67
  108.3 4.3 %collective-permute-start.49 = (f32[128,256]{1,0:T(8,128)S(1)}, f32[128,256]{1,0:T(8,128)S(1)}, u32[]{:S(2)}, u32[]{:S(2)}) collective-permute-start(f32[128,256]{1,0:T(8,128)S(1)} %get-tuple-element.249), channel_id=1, source_target_pairs={{0,1},{1,0},{2,3},{3,2},{4,5},{5,4},{6,7},{7,6},{8,9},{9,8},{10,11... | collective-permute-start | bytes 393224 | tf_op jit(solution)/shard_map/ppermute | solution.py:67
  113.4 5.0 %collective-permute-start.51 = (f32[128,256]{1,0:T(8,128)S(1)}, f32[128,256]{1,0:T(8,128)S(1)}, u32[]{:S(2)}, u32[]{:S(2)}) collective-permute-start(f32[128,256]{1,0:T(8,128)S(1)} %get-tuple-element.255), channel_id=1, source_target_pairs={{0,16},{1,4},{2,18},{3,6},{4,1},{5,8},{6,3},{7,10},{8,5},{9,12},{1... | collective-permute-start | bytes 393224 | tf_op jit(solution)/shard_map/ppermute | solution.py:67
  114.2 4.3 %collective-permute-start.52 = (f32[128,256]{1,0:T(8,128)S(1)}, f32[128,256]{1,0:T(8,128)S(1)}, u32[]{:S(2)}, u32[]{:S(2)}) collective-permute-start(f32[128,256]{1,0:T(8,128)S(1)} %get-tuple-element.256), channel_id=1, source_target_pairs={{0,1},{1,0},{2,3},{3,2},{4,5},{5,4},{6,7},{7,6},{8,9},{9,8},{10,11... | collective-permute-start | bytes 393224 | tf_op jit(solution)/shard_map/ppermute | solution.py:67
  119.3 5.0 %collective-permute-start.54 = (f32[128,256]{1,0:T(8,128)S(1)}, f32[128,256]{1,0:T(8,128)S(1)}, u32[]{:S(2)}, u32[]{:S(2)}) collective-permute-start(f32[128,256]{1,0:T(8,128)S(1)} %get-tuple-element.262), channel_id=1, source_target_pairs={{0,16},{1,4},{2,18},{3,6},{4,1},{5,8},{6,3},{7,10},{8,5},{9,12},{1... | collective-permute-start | bytes 393224 | tf_op jit(solution)/shard_map/ppermute | solution.py:67
  120.0 4.3 %collective-permute-start.55 = (f32[128,256]{1,0:T(8,128)S(1)}, f32[128,256]{1,0:T(8,128)S(1)}, u32[]{:S(2)}, u32[]{:S(2)}) collective-permute-start(f32[128,256]{1,0:T(8,128)S(1)} %get-tuple-element.263), channel_id=1, source_target_pairs={{0,1},{1,0},{2,3},{3,2},{4,5},{5,4},{6,7},{7,6},{8,9},{9,8},{10,11... | collective-permute-start | bytes 393224 | tf_op jit(solution)/shard_map/ppermute | solution.py:67
  126.3 7.8 %collective-permute-start.63 = (f32[256,256]{1,0:T(8,128)S(1)}, f32[256,256]{1,0:T(8,128)S(1)}, u32[]{:S(2)}, u32[]{:S(2)}) collective-permute-start(f32[256,256]{1,0:T(8,128)S(1)} %get-tuple-element.275.cur.refs_6_), channel_id=1, source_target_pairs={{0,16},{1,2},{2,1},{3,19},{4,20},{5,6},{6,5},{7,23},{8,24},{9,10},... | collective-permute-start | bytes 786440 | tf_op jit(solution)/shard_map/ppermute | solution.py:67
  127.8 11.8 %collective-permute-start.62 = (f32[256,256]{1,0:T(8,128)S(1)}, f32[256,256]{1,0:T(8,128)S(1)}, u32[]{:S(2)}, u32[]{:S(2)}) collective-permute-start(f32[256,256]{1,0:T(8,128)S(1)} %get-tuple-element.274.refs_4_), channel_id=1, source_target_pairs={{0,16},{1,2},{2,1},{3,19},{4,20},{5,6},{6,5},{7,23},{8,24},{9,10},... | collective-permute-start | bytes 786440 | tf_op jit(solution)/shard_map/ppermute | solution.py:67
  128.7 8.1 %collective-permute-start.59 = (f32[2,64,128]{2,1,0:T(8,128)S(1)}, f32[2,64,128]{2,1,0:T(8,128)S(1)}, u32[]{:S(2)}, u32[]{:S(2)}) collective-permute-start(f32[2,64,128]{2,1,0:T(8,128)S(1)} %get-tuple-element.270), channel_id=1, source_target_pairs={{0,4},{1,6},{2,5},{3,7},{4,0},{5,2},{6,1},{7,3},{8,12},{9,14},{10,... | collective-permute-start | bytes 196616 | tf_op jit(solution)/shard_map/ppermute | solution.py:67
  129.3 8.1 %collective-permute-start.60 = (f32[2,64,128]{2,1,0:T(8,128)S(1)}, f32[2,64,128]{2,1,0:T(8,128)S(1)}, u32[]{:S(2)}, u32[]{:S(2)}) collective-permute-start(f32[2,64,128]{2,1,0:T(8,128)S(1)} %get-tuple-element.271), channel_id=1, source_target_pairs={{0,8},{1,10},{2,9},{3,11},{4,12},{5,14},{6,13},{7,15},{8,0},{9,2},... | collective-permute-start | bytes 196616 | tf_op jit(solution)/shard_map/ppermute | solution.py:67
  129.3 8.1 %collective-permute-start.61 = (f32[2,64,128]{2,1,0:T(8,128)S(1)}, f32[2,64,128]{2,1,0:T(8,128)S(1)}, u32[]{:S(2)}, u32[]{:S(2)}) collective-permute-start(f32[2,64,128]{2,1,0:T(8,128)S(1)} %get-tuple-element.272), channel_id=1, source_target_pairs={{0,12},{1,14},{2,13},{3,15},{4,8},{5,10},{6,9},{7,11},{8,4},{9,6},... | collective-permute-start | bytes 196616 | tf_op jit(solution)/shard_map/ppermute | solution.py:67
  134.1 5.6 %collective-permute-start.58 = (f32[2,64,128]{2,1,0:T(8,128)S(1)}, f32[2,64,128]{2,1,0:T(8,128)S(1)}, u32[]{:S(2)}, u32[]{:S(2)}) collective-permute-start(f32[2,64,128]{2,1,0:T(8,128)S(1)} %get-tuple-element.269), channel_id=1, source_target_pairs={{0,0},{1,2},{2,1},{3,3},{4,4},{5,6},{6,5},{7,7},{8,8},{9,10},{10,9... | collective-permute-start | bytes 196616 | tf_op jit(solution)/shard_map/ppermute | solution.py:67
  (33 other events, 92.7 us)

commit v5 on v4

--- a/solution.py
+++ b/solution.py
@@ -111,28 +111,30 @@
     return jnp.dot(a, b, preferred_element_type=F32)
 
 
-def inner_differences(cur, near, deep):
+def inner_differences(cur, cm, near, deep):
     depth = cur.shape[1]
     size = GROUP * COLS
     own = split(cur[...])
     along = mm(jnp.concatenate(own, axis=1), deep[...])
     blank = jnp.zeros((4 * COLS, depth), BF16)
     ext = [jnp.concatenate([blank, part, blank], axis=0) for part in own]
+    from_c = split(cm[...])
     for n in range(cur.shape[0] // size):
         here = slice(n * size, n * size + size)
+        sides = slice(n * GROUP * 4, n * GROUP * 4 + GROUP * 4)
         rhs = [part[n * size : n * size + size + 8 * COLS] for part in ext]
+        rhs += [part[sides] for part in from_c]
         out = mm(near[...], jnp.concatenate(rhs, axis=0))
         yield (here, out[0:size], along[here, 0:depth], out[size : 2 * size], out[2 * size :],
                along[here, depth:])
 
 
-def side_differences(rows, zm, cm, side):
+def side_differences(rows, zm, side):
     size = GROUP * COLS
-    from_z, from_c = split(zm[...]), split(cm[...])
+    from_z = split(zm[...])
     for n in range(rows // size):
         sides = slice(n * GROUP * 4, n * GROUP * 4 + GROUP * 4)
-        rhs = [part[p][sides] for p in range(2) for part in (from_z, from_c)]
-        out = mm(side[...], jnp.concatenate(rhs, axis=0))
+        out = mm(side[...], jnp.concatenate([part[sides] for part in from_z], axis=0))
         yield slice(n * size, n * size + size), out[0:size], out[size:]
 
 
@@ -186,22 +188,44 @@
         rims(flags, out, *outs)
 
 
-def model_kernel(flags, lr, zm, cm, ym, near, deep, side, edge, vel, k0, ki, kx, kz):
-    for here, spare, spare_z, di, dx, dz in inner_differences(lr, near, deep):
-        ki[here], kx[here], kz[here] = di, dx, dz
-    for here, spare, dx in side_differences(lr.shape[0], zm.at[0], cm.at[0], side):
-        kx[here] += dx
-    here, spare, di = edge_differences(flags, lr.shape[0], ym.at[0], edge)
-    ki[here] += di
-    square = vel[...] * vel[...]
-    k0[...] = square * (1.0 / 5040)
-    scaled = square * (1.0 / (840 * 840))
-    for factor in (ki, kx, kz):
-        factor[...] = scaled * factor[...]
-
-
-def inner(cur, prev, k0, ki, kx, kz, near, deep, inj, out):
-    for here, sums, sums_z, di, dx, dz in inner_differences(cur, near, deep):
+def first_inner_kernel(flags, lr, cur, lr_cm, cm, near, deep, *outs):
+    ri, rx, rz, sums_out, di_out, dx_out, dz_out = outs
+    for here, spare, spare_z, di, dx, dz in inner_differences(lr, lr_cm, near, deep):
+        ri[here], rx[here], rz[here] = di, dx, dz
+    for here, sums, sums_z, di, dx, dz in inner_differences(cur, cm, near, deep):
+        sums_out[here] = sums + sums_z + (3.0 * SECOND[0] * 5040) * cur[here]
+        di_out[here], dx_out[here], dz_out[here] = di, dx, dz
+
+
+def first_outer_kernel(flags, cur, prev, vel, ri, rx, rz, sums, di, dx, dz, inj, lr_zm, lr_ym, zm,
+                       ym, side, edge, mine, got, new, zo, co, yo, lists, k0, ki, kx, kz):
+    rows = cur.shape[0]
+    merge(0, flags, mine, got, lists)
+    kz[...] = sums[...]
+    ki[...] = di[...]
+    here, more, more_i = edge_differences(flags, rows, ym, edge)
+    kz[here] += more
+    ki[here] += more_i
+    lr_here, spare, lr_more_i = edge_differences(flags, rows, lr_ym, edge)
+    k0[...] = ri[...]
+    k0[lr_here] += lr_more_i
+    first = side_differences(rows, lr_zm, side)
+    second = side_differences(rows, zm, side)
+    for (here, spare, more_r), (spare_here, more, more_x) in zip(first, second):
+        square = vel[here] * vel[here]
+        scaled = square * (1.0 / (840 * 840))
+        factor = square * (1.0 / 5040)
+        along_i, along_x, along_z = scaled * k0[here], scaled * (rx[here] + more_r), scaled * rz[here]
+        change = factor * (kz[here] + more) - (
+            along_i * ki[here] + along_x * (dx[here] + more_x) + along_z * dz[here])
+        k0[here], ki[here], kx[here], kz[here] = factor, along_i, along_x, along_z
+        center = cur[here]
+        new[here] = (center - prev[here]) + (center + (change + inj[here]))
+    rims(flags, new, zo, co, yo)
+
+
+def inner(cur, prev, k0, ki, kx, kz, cm, near, deep, inj, out):
+    for here, sums, sums_z, di, dx, dz in inner_differences(cur, cm, near, deep):
         center = cur[here]
         change = k0[here] * ((sums + sums_z) + (3.0 * SECOND[0] * 5040) * center)
         change = change - (ki[here] * di + kx[here] * dx + kz[here] * dz)
@@ -210,41 +234,45 @@
         out[here] = (center - prev[here]) + (center + change)
 
 
-def outer(flags, part, k0, ki, kx, zm, cm, ym, side, edge, new):
+def outer(flags, part, k0, ki, kx, zm, ym, side, edge, new):
     rows = part.shape[0]
-    for here, sums, dx in side_differences(rows, zm, cm, side):
+    for here, sums, dx in side_differences(rows, zm, side):
         new[here] = part[here] + (k0[here] * sums - kx[here] * dx)
     here, sums, di = edge_differences(flags, rows, ym, edge)
     new[here] += k0[here] * sums - ki[here] * di
 
 
-def forward_inner_kernel(step, flags, cur, prev, k0, ki, kx, kz, near, deep, srow, sz, wave,
-                         *rest):
-    size, depth = cur.shape
+def merge(stage, flags, mine, got, out):
+    n = mine.shape[0]
+    bit = flags[4 + stage]
+    out[pl.ds(bit * n, n)] = mine[...]
+    out[pl.ds((1 - bit) * n, n)] = got[...]
+
+
+def source_kernel(step, flags, srow, sz, wave, out):
+    size, depth = out.shape
     n = srow.shape[1]
     spot = lax.broadcasted_iota(jnp.int32, (size, n), 0) == srow[...]
     spot = spot.astype(F32).astype(BF16)
     high, low = split(jnp.where(
         lax.broadcasted_iota(jnp.int32, (n, depth), 1) == sz[...], wave[:, step : step + 1], 0.0))
-    inj = mm(spot, high) + mm(spot, low)
-    if step > 0:
-        before, part, change = rest
-        change[...] = (cur[...] - prev[...]) - (prev[...] - before[...])
-    else:
-        part, = rest
-    inner(cur, prev, k0, ki, kx, kz, near, deep, inj, part)
-
-
-def outer_kernel(stage, flags, part, k0, ki, kx, zm, cm, ym, side, edge, *rest):
+    out[...] = mm(spot, high) + mm(spot, low)
+
+
+def forward_inner_kernel(step, flags, cur, prev, k0, ki, kx, kz, cm, near, deep, srow, sz, wave,
+                         before, part, change):
+    source_kernel(step, flags, srow, sz, wave, change)
+    inner(cur, prev, k0, ki, kx, kz, cm, near, deep, change, part)
+    change[...] = (cur[...] - prev[...]) - (prev[...] - before[...])
+
+
+def outer_kernel(stage, flags, part, k0, ki, kx, zm, ym, side, edge, *rest):
     if stage is None:
         new, zo, co, yo = rest
     else:
         mine, got, new, zo, co, yo, lists = rest
-        n = mine.shape[0]
-        bit = flags[4 + stage]
-        lists[pl.ds(bit * n, n)] = mine[...]
-        lists[pl.ds((1 - bit) * n, n)] = got[...]
-    outer(flags, part, k0, ki, kx, zm, cm, ym, side, edge, new)
+        merge(stage, flags, mine, got, lists)
+    outer(flags, part, k0, ki, kx, zm, ym, side, edge, new)
     rims(flags, new, zo, co, yo)
 
 
@@ -288,7 +316,7 @@
     return mm(spot[...], high) + mm(spot[...], low)
 
 
-def adjoint_inner_kernel(t, flags, cur, prev, k0, ki, kx, kz, near, deep, state, spot, pick,
+def adjoint_inner_kernel(t, flags, cur, prev, k0, ki, kx, kz, cm, near, deep, state, spot, pick,
                          at, obs, *rest):
     if len(rest) == 4:
         change, image, part, image_out = rest
@@ -296,24 +324,24 @@
     else:
         now, mid, before, part, image_out = rest
         image_out[...] = cur[...] * ((now[...] - mid[...]) - (mid[...] - before[...]))
-    inner(cur, prev, k0, ki, kx, kz, near, deep, injection(t, state, spot, pick, at, obs), part)
-
-
-def first_inner_kernel(flags, cur, prev, k0, ki, kx, kz, near, deep, part):
-    inner(cur, prev, k0, ki, kx, kz, near, deep, None, part)
-
-
-def turn_kernel(t, flags, part, k0, ki, kx, zm, cm, ym, side, edge, u_part, u_zm, u_cm, u_ym,
-                spot, pick, at, obs, new, u_new, zo, co, yo):
-    outer(flags, part, k0, ki, kx, zm, cm, ym, side, edge, new)
-    outer(flags, u_part, k0, ki, kx, u_zm, u_cm, u_ym, side, edge, u_new)
+    inj = injection(t, state, spot, pick, at, obs)
+    inner(cur, prev, k0, ki, kx, kz, cm, near, deep, inj, part)
+
+
+def adjoint_first_kernel(flags, cur, prev, k0, ki, kx, kz, cm, near, deep, part):
+    inner(cur, prev, k0, ki, kx, kz, cm, near, deep, None, part)
+
+
+def turn_kernel(t, flags, part, k0, ki, kx, zm, ym, side, edge, u_part, u_zm, u_ym, spot, pick, at, obs, new, u_new, zo, co, yo):
+    outer(flags, part, k0, ki, kx, zm, ym, side, edge, new)
+    outer(flags, u_part, k0, ki, kx, u_zm, u_ym, side, edge, u_new)
     u_new[...] += injection(t, new, spot, pick, at, obs)
     rims(flags, u_new, zo, co, yo)
 
 
-def last_kernel(scale, flags, part, k0, ki, kx, zm, cm, ym, side, edge, image, change, vel,
+def last_kernel(scale, flags, part, k0, ki, kx, zm, ym, side, edge, image, change, vel,
                 new, mine, other):
-    outer(flags, part, k0, ki, kx, zm, cm, ym, side, edge, new)
+    outer(flags, part, k0, ki, kx, zm, ym, side, edge, new)
     raw = (image[...] + new[...] * change[...]) * scale / vel[...]
     count, height, lanes = mine.shape
     chunk = raw.shape[1] // (2 * count)
@@ -374,7 +402,7 @@
         in_specs=specs,
         out_specs=[pl.BlockSpec(memory_space=pltpu.VMEM)] * len(outs),
         compiler_params=pltpu.CompilerParams(vmem_limit_bytes=VMEM_BYTES),
-        cost_estimate=pl.CostEstimate(flops=5_000_000, bytes_accessed=2_000_000, transcendentals=0),
+        cost_estimate=pl.CostEstimate(flops=1000, bytes_accessed=1000, transcendentals=0),
     )(*args)
 
 
@@ -401,17 +429,18 @@
     deep = jnp.asarray(np.concatenate([deep, deep]), BF16)
     near = stencil_matrix(GROUP, cols)
     group, own, half = GROUP * cols, near.shape[1] - GROUP * 8, GROUP * 4
-    side = np.concatenate([near[:group, own:], near[2 * group :, own:]])
-    other = np.concatenate([side[:, half:], side[:, :half]], axis=1)
-    from_z = np.arange(2 * half) < half
+    both = [near[:, own : own + half], near[:, own + half :]]
+    from_z = [np.concatenate([part[:group], part[2 * group :]]) for part in both]
     inside = jnp.where(c == 0, q > 0, q < nq - 1)
-    side = jnp.where(c == 0, jnp.asarray(side, F32), jnp.asarray(other, F32))
-    side = jnp.where(from_z[None, :] & ~inside, 0.0, side).astype(BF16)
+    side = jnp.where(c == 0, jnp.asarray(from_z[0], F32), jnp.asarray(from_z[1], F32))
+    side = jnp.where(inside, side, 0.0).astype(BF16)
     side = jnp.concatenate([side, side], axis=1)
+    core = jnp.where(c == 0, jnp.asarray(both[1], F32), jnp.asarray(both[0], F32)).astype(BF16)
     edge = jnp.where(y == 1, jnp.asarray(near[: 2 * group, : 4 * cols], F32),
                      jnp.asarray(near[: 2 * group, own - 4 * cols : own], F32)).astype(BF16)
     edge = jnp.concatenate([edge, edge], axis=1)
     near = jnp.asarray(np.concatenate([near[:, :own], near[:, :own]], axis=1), BF16)
+    near = jnp.concatenate([near, core, core], axis=1)
 
     def halo(zo, co, yo):
         return send(zo, z_perm), send(co, c_perm), send(yo, y_perm)
@@ -433,11 +462,10 @@
                                 [field, field] + [shaped(2, *r.shape) for r in rim],
                                 flags, log_density, fwd_now, *got)
     zm, cm, ym = halo(*out)
+    parts = call(first_inner_kernel, "first_inner", [field] * 7, flags, density, p_now, cm[0], cm[1],
+                 near, deep)
     vel, p_before = call(settle_model_kernel, "settle_model", [field, field],
                          flags, velocity, fwd_before, got_model)
-    k0, ki, kx, kz = call(model_kernel, "model", [field] * 4, flags, density, zm, cm, ym, near,
-                          deep, side, edge, vel)
-    halos = (zm[1], cm[1], ym[1])
 
     plane = nx * cols * depth
     src_i = src_cell // plane - y * rows
@@ -447,6 +475,8 @@
     sz = (src_cell % depth)[:, None]
     wave = wavelet.T
 
+    rec_counts, rec_cells, observed = lax.optimization_barrier(
+        (rec_counts, rec_cells, observed, density))[:3]
     live = jnp.arange(CAP)[None, :] < rec_counts[0][:, None]
     cells = jnp.where(live.reshape(-1), rec_cells[0], -1)
     lists = jnp.concatenate([observed, cells[None, :].astype(F32)], axis=0)[None]
@@ -454,17 +484,23 @@
     lag = 2 if 2 * (len(stages) - 1) < steps - 1 else 1
     moved = send(lists, stages[0][0])
 
-    states = [p_before, p_now]
+    inj, = call(functools.partial(source_kernel, 0), "source", [field], flags, srow, sz, wave)
+    grown = shaped(2, *lists.shape[1:])
+    new, zo, co, yo, lists, *model = call(
+        first_outer_kernel, "first_outer", [field] + rim + [grown] + [field] * 4, flags, p_now,
+        p_before, vel, *parts, inj, zm[0], ym[0], zm[1], ym[1], side, edge, lists, moved)
+    k0, ki, kx, kz = model
+    states = [p_before, p_now, new]
     changes = []
-    for t in range(steps):
-        args = states[:-3:-1] + [k0, ki, kx, kz, near, deep, srow, sz, wave]
-        outs = [field]
-        if t > 0:
-            args.append(states[-3])
-            outs = [field, field]
-        part, *change = call(functools.partial(forward_inner_kernel, t), "forward_inner", outs,
-                             flags, *args)
-        changes += change
+    zm, cm, ym = halo(zo, co, yo)
+    if lag == 1:
+        moved = send(lists, stages[1][0])
+    for t in range(1, steps):
+        cur, prev, before = states[:-4:-1]
+        part, change = call(
+            functools.partial(forward_inner_kernel, t), "forward_inner", [field, field], flags, cur,
+            prev, *model, cm, near, deep, srow, sz, wave, before)
+        changes.append(change)
         if t == 1:
             got_now = send(after(adj_now, part), swap_perm)
         if t == 2:
@@ -476,10 +512,14 @@
             u_before, = call(functools.partial(settle_one, False), "settle_before", [field],
                              flags, adj_before, after(got_before, part))
             part = after(part, u_before)
-            u_halos = halo(*(after(r, part) for r in u_rim))
+            u_zm, u_cm, u_ym = halo(*(after(r, part) for r in u_rim))
+        if t == 4:
+            u_part, = call(adjoint_first_kernel, "adjoint_inner", [field], flags, u_now, u_before,
+                           *model, u_cm, near, deep)
+            part = after(part, u_part)
+        if t == 5:
+            part = after(part, u_zm, u_ym)
         if t == steps - 1:
-            u_part, = call(first_inner_kernel, "adjoint_inner", [field], flags, u_now, u_before,
-                           k0, ki, kx, kz, near, deep)
             slots = subs * CAP
             receivers = call(
                 lists_kernel, "lists",
@@ -488,10 +528,10 @@
                  shaped(slots, steps)], flags, lists)
             new, u_new, *out = call(
                 functools.partial(turn_kernel, t), "turn", [field, field] + rim, flags, part,
-                k0, ki, kx, *halos, side, edge, u_part, *u_halos, *receivers)
+                k0, ki, kx, zm, ym, side, edge, u_part, u_zm, u_ym, *receivers)
             states.append(new)
             break
-        args = [part, k0, ki, kx, *halos, side, edge]
+        args = [part, k0, ki, kx, zm, ym, side, edge]
         outs = [field] + rim
         stage = t // lag if t % lag == 0 and t // lag < len(stages) else None
         if stage is not None:
@@ -505,9 +545,9 @@
             if lag == 1 and stage + 1 < len(stages):
                 moved = send(lists, stages[stage + 1][0])
         states.append(new)
-        halos = halo(*out)
-
-    halos = halo(*out)
+        zm, cm, ym = halo(*out)
+
+    zm, cm, ym = halo(*out)
     u_before, u_now = u_now, u_new
     image = []
     chunk = depth // nx
@@ -517,8 +557,8 @@
         terms = [changes[t + 1], *image] if image else states[:-4:-1]
         part, *image = call(
             functools.partial(adjoint_inner_kernel, t), "adjoint_inner", [field, field], flags,
-            u_now, u_before, k0, ki, kx, kz, near, deep, states[t + 2], *receivers, *terms)
-        args = [part, k0, ki, kx, *halos, side, edge]
+            u_now, u_before, *model, cm, near, deep, states[t + 2], *receivers, *terms)
+        args = [part, k0, ki, kx, zm, ym, side, edge]
         if j == steps - 1:
             got_prev = send(after(u_now, part), swap_perm)
             u_last, mine, other = call(
@@ -528,11 +568,11 @@
         u_before = u_now
         u_now, *out = call(functools.partial(outer_kernel, None), "adjoint_outer", [field] + rim,
                            flags, *args)
-        halos = halo(*out)
+        zm, cm, ym = halo(*out)
 
     pieces = call(join_kernel, "join", [shaped(2, *half.shape[1:])] * nq, flags, mine,
                   send(other, c_perm))
-    got = send(after(u_last, pieces[0]), swap_perm)
+    got = send(u_last, swap_perm)
     pieces = [send(value, plan.spread(s)) for s, value in enumerate(pieces)]
     gradient, adj_out, adj_prev = call(
         filter_kernel, "filter", [shaped(chunk, rows, nx * cols), field, field], flags, *pieces,

time: 142 us -> 144 us (1.014)
  waiting for transfers between devices: 29.3 us -> 42.5 us
  starting transfers between devices: 62.5 us -> 50.8 us
    ppermute x64, waiting for transfers between devices: 29.3 us -> 42.5 us  [send(): return lax.ppermute(value, ALL, pairs)]
    ppermute x64, starting transfers between devices: 62.5 us -> 50.8 us  [send(): return lax.ppermute(value, ALL, pairs)]
    unnamed x35 -> x45, local copies, waits for them, and re-layouts: 3.41 us -> 3.7 us
  transfers between devices with their start and end apart: 64 -> 64, of which waited for: 20 -> 39; matrix products, arithmetic and copies ran while one was open for 2% -> 2% of each run, Pallas kernels for 20% -> 21%
where the time goes in v5:
time: 144 us
  starting transfers between devices  50.8 us (35%)
  Pallas kernels  43.2 us (30%)
  waiting for transfers between devices  42.5 us (30%)
  local copies, waits for them, and re-layouts  4 us (3%)
  other arithmetic  2.28 us (2%)
    ppermute x64, starting transfers between devices, send(): return lax.ppermute(value, ALL, pairs)  50.8 us
    pallas_call x40, Pallas kernels, call(): pl.pallas_call(kernel, name=name, out_shape=outs, in_specs=specs, out_spe...  43.2 us
    ppermute x64, waiting for transfers between devices, send(): return lax.ppermute(value, ALL, pairs)  42.5 us
    unnamed x45, local copies, waits for them, and re-layouts  3.7 us
  transfers between devices with their start and end apart: 64, of which 39 were waited for; matrix products, arithmetic and copies ran while one was open for 2% of the time, Pallas kernels for 21%

profile of v5, /device:TPU:1, one launch (start us, length us, event | category | flops | bytes accessed | tf_op | source)
XLA Modules:
  0.0 144.0 jit_solution(10211610497304586860)
XLA Ops:
  0.6 2.7 %collective-permute-start.1 = (f32[256,256]{1,0:T(8,128)}, f32[256,256]{1,0:T(8,128)S(1)}, u32[]{:S(2)}, u32[]{:S(2)}) collective-permute-start(f32[256,256]{1,0:T(8,128)} %bitcast.50), channel_id=1, source_target_pairs={{0,16},{1,2},{2,1},{3,19},{4,20},{5,6},{6,5},{7,23},{8,24},{9,10},... | collective-permute-start | bytes 786440 | tf_op jit(solution)/shard_map/ppermute | solution.py:67
  3.4 1.9 %pad_maximum_fusion = f32[2,256,256]{2,1,0:T(8,128)} fusion(f32[1,256,256]{2,1,0:T(8,128)} %bitcast.38, f32[1,256,256]{2,1,0:T(8,128)} %bitcast.36), kind=kLoop, calls=%fused_computation | loop fusion | flops 131072 | bytes 1048576 | tf_op jit(solution)/shard_map/stack | solution.py:457
  5.4 1.7 %collective-permute-start.2 = (f32[2,256,256]{2,1,0:T(8,128)}, f32[2,256,256]{2,1,0:T(8,128)S(1)}, u32[]{:S(2)}, u32[]{:S(2)}) collective-permute-start(f32[2,256,256]{2,1,0:T(8,128)} %pad_maximum_fusion), channel_id=1, source_target_pairs={{0,16},{1,2},{2,1},{3,19},{4,20},{5,6},{6,5},{7,23},{8,24},{9,10},... | collective-permute-start | bytes 1572872 | tf_op jit(solution)/shard_map/ppermute | solution.py:67
  15.2 1.7 %collective-permute-start.4 = (f32[2,128,256]{2,1,0:T(8,128)S(1)}, f32[2,128,256]{2,1,0:T(8,128)S(1)}, u32[]{:S(2)}, u32[]{:S(2)}) collective-permute-start(f32[2,128,256]{2,1,0:T(8,128)S(1)} %get-tuple-element.168), channel_id=1, source_target_pairs={{0,16},{1,4},{2,18},{3,6},{4,1},{5,8},{6,3},{7,10},{8,5},{9,12},{1... | collective-permute-start | bytes 786440 | tf_op jit(solution)/shard_map/ppermute | solution.py:67
  16.9 4.4 %collective-permute-done.4 = f32[2,128,256]{2,1,0:T(8,128)S(1)} collective-permute-done((f32[2,128,256]{2,1,0:T(8,128)S(1)}, f32[2,128,256]{2,1,0:T(8,128)S(1)}, u32[]{:S(2)}, u32[]{:S(2)}) %collective-permute-start.4) | collective-permute-done | bytes 262176 | tf_op jit(solution)/shard_map/ppermute | solution.py:67
  21.4 1.3 first_inner.1
  26.2 1.2 forward_inner.7
  27.5 1.5 %collective-permute-start.11 = (f32[256,256]{1,0:T(8,128)S(1)}, f32[256,256]{1,0:T(8,128)S(1)}, u32[]{:S(2)}, u32[]{:S(2)}) collective-permute-start(f32[256,256]{1,0:T(8,128)S(1)} %get-tuple-element.186.own), channel_id=1, source_target_pairs={{0,16},{1,2},{2,1},{3,19},{4,20},{5,6},{6,5},{7,23},{8,24},{9,10},... | collective-permute-start | bytes 786440 | tf_op jit(solution)/shard_map/ppermute | solution.py:67
  29.3 3.7 %collective-permute-done.9.ym = f32[32,256]{1,0:T(8,128)S(1)} collective-permute-done((f32[32,256]{1,0:T(8,128)S(1)}, f32[32,256]{1,0:T(8,128)S(1)}, u32[]{:S(2)}, u32[]{:S(2)}) %collective-permute-start.9) | collective-permute-done | bytes 32800 | tf_op jit(solution)/shard_map/ppermute | solution.py:67
  33.8 1.8 %collective-permute-start.10 = (f32[128,256]{1,0:T(8,128)S(1)}, f32[128,256]{1,0:T(8,128)S(1)}, u32[]{:S(2)}, u32[]{:S(2)}) collective-permute-start(f32[128,256]{1,0:T(8,128)S(1)} %get-tuple-element.183), channel_id=1, source_target_pairs={{0,1},{1,0},{2,3},{3,2},{4,5},{5,4},{6,7},{7,6},{8,9},{9,8},{10,11... | collective-permute-start | bytes 393224 | tf_op jit(solution)/shard_map/ppermute | solution.py:67
  36.6 1.2 forward_inner.8
  40.6 2.7 %collective-permute-done.14.rest_1_ = f32[2,9,128]{2,1,0:T(8,128)S(1)} collective-permute-done((f32[2,9,128]{2,1,0:T(8,128)S(1)}, f32[2,9,128]{2,1,0:T(8,128)S(1)}, u32[]{:S(2)}, u32[]{:S(2)}) %collective-permute-start.14) | collective-permute-done | bytes 9248 | tf_op jit(solution)/shard_map/ppermute | solution.py:67
  44.2 2.8 %collective-permute-start.15 = (f32[128,256]{1,0:T(8,128)S(1)}, f32[128,256]{1,0:T(8,128)S(1)}, u32[]{:S(2)}, u32[]{:S(2)}) collective-permute-start(f32[128,256]{1,0:T(8,128)S(1)} %get-tuple-element.195), channel_id=1, source_target_pairs={{0,1},{1,0},{2,3},{3,2},{4,5},{5,4},{6,7},{7,6},{8,9},{9,8},{10,11... | collective-permute-start | bytes 393224 | tf_op jit(solution)/shard_map/ppermute | solution.py:67
  48.0 1.2 forward_inner.9
  53.8 1.2 collective-permute-start.23
  56.1 1.2 forward_inner.10
  58.6 1.1 collective-permute-start.24
  59.9 1.6 %collective-permute-start.27 = (f32[128,256]{1,0:T(8,128)S(1)}, f32[128,256]{1,0:T(8,128)S(1)}, u32[]{:S(2)}, u32[]{:S(2)}) collective-permute-start(f32[128,256]{1,0:T(8,128)S(1)} %get-tuple-element.221), channel_id=1, source_target_pairs={{0,16},{1,4},{2,18},{3,6},{4,1},{5,8},{6,3},{7,10},{8,5},{9,12},{1... | collective-permute-start | bytes 393224 | tf_op jit(solution)/shard_map/ppermute | solution.py:67
  62.9 1.2 forward_inner.11
  64.5 1.2 collective-permute-done.28.ym
  66.6 1.3 collective-permute-start.29
  68.3 1.6 %collective-permute-start.32 = (f32[8,9,128]{2,1,0:T(8,128)S(1)}, f32[8,9,128]{2,1,0:T(8,128)S(1)}, u32[]{:S(2)}, u32[]{:S(2)}) collective-permute-start(f32[8,9,128]{2,1,0:T(8,128)S(1)} %get-tuple-element.229.rest_0_), channel_id=1, source_target_pairs={{0,8},{1,9},{2,10},{3,11},{4,12},{5,13},{6,14},{7,15},{8,0},{9,1},... | collective-permute-start | bytes 110600 | tf_op jit(solution)/shard_map/ppermute | solution.py:67
  70.0 1.2 forward_inner.12
  71.3 1.4 collective-permute-done.31.ym
  74.5 2.4 %collective-permute-start.33 = (f32[128,256]{1,0:T(8,128)S(1)}, f32[128,256]{1,0:T(8,128)S(1)}, u32[]{:S(2)}, u32[]{:S(2)}) collective-permute-start(f32[128,256]{1,0:T(8,128)S(1)} %get-tuple-element.231), channel_id=1, source_target_pairs={{0,1},{1,0},{2,3},{3,2},{4,5},{5,4},{6,7},{7,6},{8,9},{9,8},{10,11... | collective-permute-start | bytes 393224 | tf_op jit(solution)/shard_map/ppermute | solution.py:67
  77.9 1.2 forward_inner.13
  79.6 1.9 %collective-permute-done.34.zm = f32[128,256]{1,0:T(8,128)S(1)} collective-permute-done((f32[128,256]{1,0:T(8,128)S(1)}, f32[128,256]{1,0:T(8,128)S(1)}, u32[]{:S(2)}, u32[]{:S(2)}) %collective-permute-start.34) | collective-permute-done | bytes 131104 | tf_op jit(solution)/shard_map/ppermute | solution.py:67
  81.5 1.5 %turn.1 = (f32[256,256]{1,0:T(8,128)S(1)}, f32[256,256]{1,0:T(8,128)S(1)}, f32[128,256]{1,0:T(8,128)S(1)}, f32[128,256]{1,0:T(8,128)S(1)}, f32[32,256]{1,0:T(8,128)S(1)}) custom-call(s32[8]{0:T(128)S(1)} %stack.32.flags, f32[256,256]{1,0:T(8,128)S(1)} %get-tuple-element.232.part, f32[256,256]{1,0:T(8,128)S(1)} %get-tuple-element.174.k0, ...), custom_call_target="tpu_custom_call" | custom-call | flops 1000 | bytes 1000 | tf_op jit(solution)/shard_map/turn/pallas_call | solution.py:398
  84.4 1.8 %adjoint_inner.9 = (f32[256,256]{1,0:T(8,128)S(1)}, f32[256,256]{1,0:T(8,128)S(1)}) custom-call(s32[8]{0:T(128)S(1)} %stack.32.flags, f32[256,256]{1,0:T(8,128)S(1)} %get-tuple-element.240.cur.prev, f32[256,256]{1,0:T(8,128)S(1)} %get-tuple-element.188.cur.prev, f32[256,256]{1,0:T(8,128)S(1)} %get-tuple-element.174.k0, ...), custom_call_target="tpu_custom_call" | custom-call | flops 1000 | bytes 1000 | tf_op jit(solution)/shard_map/adjoint_inner/pallas_call | solution.py:398
  90.4 1.6 %adjoint_inner.10 = (f32[256,256]{1,0:T(8,128)S(1)}, f32[256,256]{1,0:T(8,128)S(1)}) custom-call(s32[8]{0:T(128)S(1)} %stack.32.flags, f32[256,256]{1,0:T(8,128)S(1)} %get-tuple-element.246.cur.prev, f32[256,256]{1,0:T(8,128)S(1)} %get-tuple-element.240.cur.prev, f32[256,256]{1,0:T(8,128)S(1)} %get-tuple-element.174.k0, ...), custom_call_target="tpu_custom_call" | custom-call | flops 1000 | bytes 1000 | tf_op jit(solution)/shard_map/adjoint_inner/pallas_call | solution.py:398
  92.0 1.2 collective-permute-done.41.ym
  96.4 1.6 %adjoint_inner.11 = (f32[256,256]{1,0:T(8,128)S(1)}, f32[256,256]{1,0:T(8,128)S(1)}) custom-call(s32[8]{0:T(128)S(1)} %stack.32.flags, f32[256,256]{1,0:T(8,128)S(1)} %get-tuple-element.253.cur.prev, f32[256,256]{1,0:T(8,128)S(1)} %get-tuple-element.246.cur.prev, f32[256,256]{1,0:T(8,128)S(1)} %get-tuple-element.174.k0, ...), custom_call_target="tpu_custom_call" | custom-call | flops 1000 | bytes 1000 | tf_op jit(solution)/shard_map/adjoint_inner/pallas_call | solution.py:398
  97.9 1.2 collective-permute-done.44.ym
  102.3 1.6 %adjoint_inner.12 = (f32[256,256]{1,0:T(8,128)S(1)}, f32[256,256]{1,0:T(8,128)S(1)}) custom-call(s32[8]{0:T(128)S(1)} %stack.32.flags, f32[256,256]{1,0:T(8,128)S(1)} %get-tuple-element.260.cur.prev, f32[256,256]{1,0:T(8,128)S(1)} %get-tuple-element.253.cur.prev, f32[256,256]{1,0:T(8,128)S(1)} %get-tuple-element.174.k0, ...), custom_call_target="tpu_custom_call" | custom-call | flops 1000 | bytes 1000 | tf_op jit(solution)/shard_map/adjoint_inner/pallas_call | solution.py:398
  103.9 1.2 collective-permute-done.47.ym
  108.3 1.6 %adjoint_inner.13 = (f32[256,256]{1,0:T(8,128)S(1)}, f32[256,256]{1,0:T(8,128)S(1)}) custom-call(s32[8]{0:T(128)S(1)} %stack.32.flags, f32[256,256]{1,0:T(8,128)S(1)} %get-tuple-element.267.cur.prev, f32[256,256]{1,0:T(8,128)S(1)} %get-tuple-element.260.cur.prev, f32[256,256]{1,0:T(8,128)S(1)} %get-tuple-element.174.k0, ...), custom_call_target="tpu_custom_call" | custom-call | flops 1000 | bytes 1000 | tf_op jit(solution)/shard_map/adjoint_inner/pallas_call | solution.py:398
  109.9 1.2 collective-permute-done.50.ym
  114.3 1.6 %adjoint_inner.14 = (f32[256,256]{1,0:T(8,128)S(1)}, f32[256,256]{1,0:T(8,128)S(1)}) custom-call(s32[8]{0:T(128)S(1)} %stack.32.flags, f32[256,256]{1,0:T(8,128)S(1)} %get-tuple-element.274.cur.prev, f32[256,256]{1,0:T(8,128)S(1)} %get-tuple-element.267.cur.prev, f32[256,256]{1,0:T(8,128)S(1)} %get-tuple-element.174.k0, ...), custom_call_target="tpu_custom_call" | custom-call | flops 1000 | bytes 1000 | tf_op jit(solution)/shard_map/adjoint_inner/pallas_call | solution.py:398
  115.8 1.2 collective-permute-done.53.ym
  120.2 1.6 %adjoint_inner.15 = (f32[256,256]{1,0:T(8,128)S(1)}, f32[256,256]{1,0:T(8,128)S(1)}) custom-call(s32[8]{0:T(128)S(1)} %stack.32.flags, f32[256,256]{1,0:T(8,128)S(1)} %get-tuple-element.297.cur.refs_6_, f32[256,256]{1,0:T(8,128)S(1)} %get-tuple-element.274.cur.prev, f32[256,256]{1,0:T(8,128)S(1)} %get-tuple-element.174.k0, ...), custom_call_target="tpu_custom_call" | custom-call | flops 1000 | bytes 1000 | tf_op jit(solution)/shard_map/adjoint_inner/pallas_call | solution.py:398
  121.8 1.2 collective-permute-done.56.ym
  125.6 1.6 %collective-permute-start.63 = (f32[256,256]{1,0:T(8,128)S(1)}, f32[256,256]{1,0:T(8,128)S(1)}, u32[]{:S(2)}, u32[]{:S(2)}) collective-permute-start(f32[256,256]{1,0:T(8,128)S(1)} %get-tuple-element.297.cur.refs_6_), channel_id=1, source_target_pairs={{0,16},{1,2},{2,1},{3,19},{4,20},{5,6},{6,5},{7,23},{8,24},{9,10},... | collective-permute-start | bytes 786440 | tf_op jit(solution)/shard_map/ppermute | solution.py:67
  127.7 2.1 %collective-permute-start.58 = (f32[2,64,128]{2,1,0:T(8,128)S(1)}, f32[2,64,128]{2,1,0:T(8,128)S(1)}, u32[]{:S(2)}, u32[]{:S(2)}) collective-permute-start(f32[2,64,128]{2,1,0:T(8,128)S(1)} %get-tuple-element.292), channel_id=1, source_target_pairs={{0,0},{1,2},{2,1},{3,3},{4,4},{5,6},{6,5},{7,7},{8,8},{9,10},{10,9... | collective-permute-start | bytes 196616 | tf_op jit(solution)/shard_map/ppermute | solution.py:67
  129.8 2.1 %collective-permute-start.59 = (f32[2,64,128]{2,1,0:T(8,128)S(1)}, f32[2,64,128]{2,1,0:T(8,128)S(1)}, u32[]{:S(2)}, u32[]{:S(2)}) collective-permute-start(f32[2,64,128]{2,1,0:T(8,128)S(1)} %get-tuple-element.293), channel_id=1, source_target_pairs={{0,4},{1,6},{2,5},{3,7},{4,0},{5,2},{6,1},{7,3},{8,12},{9,14},{10,... | collective-permute-start | bytes 196616 | tf_op jit(solution)/shard_map/ppermute | solution.py:67
  132.8 2.6 %collective-permute-done.58.refs_0_ = f32[2,64,128]{2,1,0:T(8,128)S(1)} collective-permute-done((f32[2,64,128]{2,1,0:T(8,128)S(1)}, f32[2,64,128]{2,1,0:T(8,128)S(1)}, u32[]{:S(2)}, u32[]{:S(2)}) %collective-permute-start.58) | collective-permute-done | bytes 65568 | tf_op jit(solution)/shard_map/ppermute | solution.py:67
  136.5 1.5 %collective-permute-done.60.refs_2_ = f32[2,64,128]{2,1,0:T(8,128)S(1)} collective-permute-done((f32[2,64,128]{2,1,0:T(8,128)S(1)}, f32[2,64,128]{2,1,0:T(8,128)S(1)}, u32[]{:S(2)}, u32[]{:S(2)}) %collective-permute-start.60) | collective-permute-done | bytes 65568 | tf_op jit(solution)/shard_map/ppermute | solution.py:67
  138.1 3.7 %collective-permute-done.61.refs_3_ = f32[2,64,128]{2,1,0:T(8,128)S(1)} collective-permute-done((f32[2,64,128]{2,1,0:T(8,128)S(1)}, f32[2,64,128]{2,1,0:T(8,128)S(1)}, u32[]{:S(2)}, u32[]{:S(2)}) %collective-permute-start.61) | collective-permute-done | bytes 65568 | tf_op jit(solution)/shard_map/ppermute | solution.py:67
  141.8 2.1 %filter.1 = (f32[32,32,64]{2,1,0:T(8,128)}, f32[256,256]{1,0:T(8,128)}, f32[256,256]{1,0:T(8,128)}) custom-call(s32[8]{0:T(128)S(1)} %stack.32.flags, f32[2,64,128]{2,1,0:T(8,128)S(1)} %collective-permute-done.58.refs_0_, f32[2,64,128]{2,1,0:T(8,128)S(1)} %collective-permute-done.59.refs_1_, f32[2,64,128]{2,1,0:T(8,128)S(1)} %collective-permute-done.60.refs_2_, ...), custom_call_target="tpu_custom_call" | custom-call | flops 1000 | bytes 1000 | tf_op jit(solution)/shard_map/filter/pallas_call | solution.py:398
  (181 shorter events, 58.6 us)
Async XLA Ops:
  0.6 11.5 %collective-permute-start.1 = (f32[256,256]{1,0:T(8,128)}, f32[256,256]{1,0:T(8,128)S(1)}, u32[]{:S(2)}, u32[]{:S(2)}) collective-permute-start(f32[256,256]{1,0:T(8,128)} %bitcast.50), channel_id=1, source_target_pairs={{0,16},{1,2},{2,1},{3,19},{4,20},{5,6},{6,5},{7,23},{8,24},{9,10},... | collective-permute-start | bytes 786440 | tf_op jit(solution)/shard_map/ppermute | solution.py:67
  3.3 8.8 %collective-permute-start = (f32[256,256]{1,0:T(8,128)}, f32[256,256]{1,0:T(8,128)S(1)}, u32[]{:S(2)}, u32[]{:S(2)}) collective-permute-start(f32[256,256]{1,0:T(8,128)} %bitcast.52), channel_id=1, source_target_pairs={{0,16},{1,2},{2,1},{3,19},{4,20},{5,6},{6,5},{7,23},{8,24},{9,10},... | collective-permute-start | bytes 786440 | tf_op jit(solution)/shard_map/ppermute | solution.py:67
  5.4 17.4 %collective-permute-start.2 = (f32[2,256,256]{2,1,0:T(8,128)}, f32[2,256,256]{2,1,0:T(8,128)S(1)}, u32[]{:S(2)}, u32[]{:S(2)}) collective-permute-start(f32[2,256,256]{2,1,0:T(8,128)} %pad_maximum_fusion), channel_id=1, source_target_pairs={{0,16},{1,2},{2,1},{3,19},{4,20},{5,6},{6,5},{7,23},{8,24},{9,10},... | collective-permute-start | bytes 1572872 | tf_op jit(solution)/shard_map/ppermute | solution.py:67
  13.6 3.2 %collective-permute-start.5 = (f32[2,32,256]{2,1,0:T(8,128)S(1)}, f32[2,32,256]{2,1,0:T(8,128)S(1)}, u32[]{:S(2)}, u32[]{:S(2)}) collective-permute-start(f32[2,32,256]{2,1,0:T(8,128)S(1)} %get-tuple-element.169), channel_id=1, source_target_pairs={{0,2},{1,3},{2,0},{3,1},{4,6},{5,7},{6,4},{7,5},{8,10},{9,11},{10,... | collective-permute-start | bytes 196616 | tf_op jit(solution)/shard_map/ppermute | solution.py:67
  15.1 8.3 %collective-permute-start.6 = (f32[1,9,128]{2,1,0:T(8,128)S(1)}, f32[1,9,128]{2,1,0:T(8,128)S(1)}, u32[]{:S(2)}, u32[]{:S(2)}) collective-permute-start(f32[1,9,128]{2,1,0:T(8,128)S(1)} %maximum_bitcast_fusion.mine), channel_id=1, source_target_pairs={{0,1},{1,0},{2,3},{3,2},{4,5},{5,4},{6,7},{7,6},{8,9},{9,8},{10,11... | collective-permute-start | bytes 13832 | tf_op jit(solution)/shard_map/ppermute | solution.py:67
  15.2 6.1 %collective-permute-start.4 = (f32[2,128,256]{2,1,0:T(8,128)S(1)}, f32[2,128,256]{2,1,0:T(8,128)S(1)}, u32[]{:S(2)}, u32[]{:S(2)}) collective-permute-start(f32[2,128,256]{2,1,0:T(8,128)S(1)} %get-tuple-element.168), channel_id=1, source_target_pairs={{0,16},{1,4},{2,18},{3,6},{4,1},{5,8},{6,3},{7,10},{8,5},{9,12},{1... | collective-permute-start | bytes 786440 | tf_op jit(solution)/shard_map/ppermute | solution.py:67
  25.2 7.8 %collective-permute-start.8 = (f32[128,256]{1,0:T(8,128)S(1)}, f32[128,256]{1,0:T(8,128)S(1)}, u32[]{:S(2)}, u32[]{:S(2)}) collective-permute-start(f32[128,256]{1,0:T(8,128)S(1)} %get-tuple-element.180), channel_id=1, source_target_pairs={{0,16},{1,4},{2,18},{3,6},{4,1},{5,8},{6,3},{7,10},{8,5},{9,12},{1... | collective-permute-start | bytes 393224 | tf_op jit(solution)/shard_map/ppermute | solution.py:67
  27.5 10.4 %collective-permute-start.11 = (f32[256,256]{1,0:T(8,128)S(1)}, f32[256,256]{1,0:T(8,128)S(1)}, u32[]{:S(2)}, u32[]{:S(2)}) collective-permute-start(f32[256,256]{1,0:T(8,128)S(1)} %get-tuple-element.186.own), channel_id=1, source_target_pairs={{0,16},{1,2},{2,1},{3,19},{4,20},{5,6},{6,5},{7,23},{8,24},{9,10},... | collective-permute-start | bytes 786440 | tf_op jit(solution)/shard_map/ppermute | solution.py:67
  29.0 4.0 %collective-permute-start.9 = (f32[32,256]{1,0:T(8,128)S(1)}, f32[32,256]{1,0:T(8,128)S(1)}, u32[]{:S(2)}, u32[]{:S(2)}) collective-permute-start(f32[32,256]{1,0:T(8,128)S(1)} %get-tuple-element.181), channel_id=1, source_target_pairs={{0,2},{1,3},{2,0},{3,1},{4,6},{5,7},{6,4},{7,5},{8,10},{9,11},{10,... | collective-permute-start | bytes 98312 | tf_op jit(solution)/shard_map/ppermute | solution.py:67
  35.6 7.7 %collective-permute-start.12 = (f32[128,256]{1,0:T(8,128)S(1)}, f32[128,256]{1,0:T(8,128)S(1)}, u32[]{:S(2)}, u32[]{:S(2)}) collective-permute-start(f32[128,256]{1,0:T(8,128)S(1)} %get-tuple-element.190), channel_id=1, source_target_pairs={{0,16},{1,4},{2,18},{3,6},{4,1},{5,8},{6,3},{7,10},{8,5},{9,12},{1... | collective-permute-start | bytes 393224 | tf_op jit(solution)/shard_map/ppermute | solution.py:67
  38.5 10.7 %collective-permute-start.16 = (f32[256,256]{1,0:T(8,128)S(1)}, f32[256,256]{1,0:T(8,128)S(1)}, u32[]{:S(2)}, u32[]{:S(2)}) collective-permute-start(f32[256,256]{1,0:T(8,128)S(1)} %get-tuple-element.198.own), channel_id=1, source_target_pairs={{0,16},{1,2},{2,1},{3,19},{4,20},{5,6},{6,5},{7,23},{8,24},{9,10},... | collective-permute-start | bytes 786440 | tf_op jit(solution)/shard_map/ppermute | solution.py:67
  39.1 4.2 %collective-permute-start.13 = (f32[32,256]{1,0:T(8,128)S(1)}, f32[32,256]{1,0:T(8,128)S(1)}, u32[]{:S(2)}, u32[]{:S(2)}) collective-permute-start(f32[32,256]{1,0:T(8,128)S(1)} %get-tuple-element.191), channel_id=1, source_target_pairs={{0,2},{1,3},{2,0},{3,1},{4,6},{5,7},{6,4},{7,5},{8,10},{9,11},{10,... | collective-permute-start | bytes 98312 | tf_op jit(solution)/shard_map/ppermute | solution.py:67
  39.6 3.7 %collective-permute-start.14 = (f32[2,9,128]{2,1,0:T(8,128)S(1)}, f32[2,9,128]{2,1,0:T(8,128)S(1)}, u32[]{:S(2)}, u32[]{:S(2)}) collective-permute-start(f32[2,9,128]{2,1,0:T(8,128)S(1)} %get-tuple-element.193.rest_0_), channel_id=1, source_target_pairs={{0,2},{1,3},{2,0},{3,1},{4,6},{5,7},{6,4},{7,5},{8,10},{9,11},{10,... | collective-permute-start | bytes 27656 | tf_op jit(solution)/shard_map/ppermute | solution.py:67
  44.2 3.8 %collective-permute-start.15 = (f32[128,256]{1,0:T(8,128)S(1)}, f32[128,256]{1,0:T(8,128)S(1)}, u32[]{:S(2)}, u32[]{:S(2)}) collective-permute-start(f32[128,256]{1,0:T(8,128)S(1)} %get-tuple-element.195), channel_id=1, source_target_pairs={{0,1},{1,0},{2,3},{3,2},{4,5},{5,4},{6,7},{7,6},{8,9},{9,8},{10,11... | collective-permute-start | bytes 393224 | tf_op jit(solution)/shard_map/ppermute | solution.py:67
  47.0 4.7 %collective-permute-start.17 = (f32[128,256]{1,0:T(8,128)S(1)}, f32[128,256]{1,0:T(8,128)S(1)}, u32[]{:S(2)}, u32[]{:S(2)}) collective-permute-start(f32[128,256]{1,0:T(8,128)S(1)} %get-tuple-element.201), channel_id=1, source_target_pairs={{0,16},{1,4},{2,18},{3,6},{4,1},{5,8},{6,3},{7,10},{8,5},{9,12},{1... | collective-permute-start | bytes 393224 | tf_op jit(solution)/shard_map/ppermute | solution.py:67
  47.9 3.1 %collective-permute-start.18 = (f32[32,256]{1,0:T(8,128)S(1)}, f32[32,256]{1,0:T(8,128)S(1)}, u32[]{:S(2)}, u32[]{:S(2)}) collective-permute-start(f32[32,256]{1,0:T(8,128)S(1)} %get-tuple-element.202), channel_id=1, source_target_pairs={{0,2},{1,3},{2,0},{3,1},{4,6},{5,7},{6,4},{7,5},{8,10},{9,11},{10,... | collective-permute-start | bytes 98312 | tf_op jit(solution)/shard_map/ppermute | solution.py:67
  49.8 5.2 %collective-permute-start.20 = (f32[128,256]{1,0:T(8,128)S(1)}, f32[128,256]{1,0:T(8,128)S(1)}, u32[]{:S(2)}, u32[]{:S(2)}) collective-permute-start(f32[128,256]{1,0:T(8,128)S(1)} %get-tuple-element.207), channel_id=1, source_target_pairs={{0,1},{1,0},{2,3},{3,2},{4,5},{5,4},{6,7},{7,6},{8,9},{9,8},{10,11... | collective-permute-start | bytes 393224 | tf_op jit(solution)/shard_map/ppermute | solution.py:67
  52.5 3.6 %collective-permute-start.19 = (f32[128,256]{1,0:T(8,128)S(1)}, f32[128,256]{1,0:T(8,128)S(1)}, u32[]{:S(2)}, u32[]{:S(2)}) collective-permute-start(f32[128,256]{1,0:T(8,128)S(1)} %get-tuple-element.204), channel_id=1, source_target_pairs={{0,1},{1,0},{2,3},{3,2},{4,5},{5,4},{6,7},{7,6},{8,9},{9,8},{10,11... | collective-permute-start | bytes 393224 | tf_op jit(solution)/shard_map/ppermute | solution.py:67
  53.0 4.7 %collective-permute-start.21 = (f32[128,256]{1,0:T(8,128)S(1)}, f32[128,256]{1,0:T(8,128)S(1)}, u32[]{:S(2)}, u32[]{:S(2)}) collective-permute-start(f32[128,256]{1,0:T(8,128)S(1)} %get-tuple-element.209), channel_id=1, source_target_pairs={{0,16},{1,4},{2,18},{3,6},{4,1},{5,8},{6,3},{7,10},{8,5},{9,12},{1... | collective-permute-start | bytes 393224 | tf_op jit(solution)/shard_map/ppermute | solution.py:67
  53.8 3.6 %collective-permute-start.22 = (f32[32,256]{1,0:T(8,128)S(1)}, f32[32,256]{1,0:T(8,128)S(1)}, u32[]{:S(2)}, u32[]{:S(2)}) collective-permute-start(f32[32,256]{1,0:T(8,128)S(1)} %get-tuple-element.210), channel_id=1, source_target_pairs={{0,2},{1,3},{2,0},{3,1},{4,6},{5,7},{6,4},{7,5},{8,10},{9,11},{10,... | collective-permute-start | bytes 98312 | tf_op jit(solution)/shard_map/ppermute | solution.py:67
  53.8 3.5 %collective-permute-start.23 = (f32[4,9,128]{2,1,0:T(8,128)S(1)}, f32[4,9,128]{2,1,0:T(8,128)S(1)}, u32[]{:S(2)}, u32[]{:S(2)}) collective-permute-start(f32[4,9,128]{2,1,0:T(8,128)S(1)} %get-tuple-element.212.rest_0_), channel_id=1, source_target_pairs={{0,4},{1,5},{2,6},{3,7},{4,0},{5,1},{6,2},{7,3},{8,12},{9,13},{10,... | collective-permute-start | bytes 55304 | tf_op jit(solution)/shard_map/ppermute | solution.py:67
  58.6 4.3 %collective-permute-start.24 = (f32[128,256]{1,0:T(8,128)S(1)}, f32[128,256]{1,0:T(8,128)S(1)}, u32[]{:S(2)}, u32[]{:S(2)}) collective-permute-start(f32[128,256]{1,0:T(8,128)S(1)} %get-tuple-element.214), channel_id=1, source_target_pairs={{0,1},{1,0},{2,3},{3,2},{4,5},{5,4},{6,7},{7,6},{8,9},{9,8},{10,11... | collective-permute-start | bytes 393224 | tf_op jit(solution)/shard_map/ppermute | solution.py:67
  59.7 4.8 %collective-permute-start.25 = (f32[128,256]{1,0:T(8,128)S(1)}, f32[128,256]{1,0:T(8,128)S(1)}, u32[]{:S(2)}, u32[]{:S(2)}) collective-permute-start(f32[128,256]{1,0:T(8,128)S(1)} %get-tuple-element.217), channel_id=1, source_target_pairs={{0,16},{1,4},{2,18},{3,6},{4,1},{5,8},{6,3},{7,10},{8,5},{9,12},{1... | collective-permute-start | bytes 393224 | tf_op jit(solution)/shard_map/ppermute | solution.py:67
  59.9 5.9 %collective-permute-start.27 = (f32[128,256]{1,0:T(8,128)S(1)}, f32[128,256]{1,0:T(8,128)S(1)}, u32[]{:S(2)}, u32[]{:S(2)}) collective-permute-start(f32[128,256]{1,0:T(8,128)S(1)} %get-tuple-element.221), channel_id=1, source_target_pairs={{0,16},{1,4},{2,18},{3,6},{4,1},{5,8},{6,3},{7,10},{8,5},{9,12},{1... | collective-permute-start | bytes 393224 | tf_op jit(solution)/shard_map/ppermute | solution.py:67
  61.4 3.1 %collective-permute-start.26 = (f32[32,256]{1,0:T(8,128)S(1)}, f32[32,256]{1,0:T(8,128)S(1)}, u32[]{:S(2)}, u32[]{:S(2)}) collective-permute-start(f32[32,256]{1,0:T(8,128)S(1)} %get-tuple-element.219), channel_id=1, source_target_pairs={{0,2},{1,3},{2,0},{3,1},{4,6},{5,7},{6,4},{7,5},{8,10},{9,11},{10,... | collective-permute-start | bytes 98312 | tf_op jit(solution)/shard_map/ppermute | solution.py:67
  62.5 3.2 %collective-permute-start.28 = (f32[32,256]{1,0:T(8,128)S(1)}, f32[32,256]{1,0:T(8,128)S(1)}, u32[]{:S(2)}, u32[]{:S(2)}) collective-permute-start(f32[32,256]{1,0:T(8,128)S(1)} %get-tuple-element.222), channel_id=1, source_target_pairs={{0,2},{1,3},{2,0},{3,1},{4,6},{5,7},{6,4},{7,5},{8,10},{9,11},{10,... | collective-permute-start | bytes 98312 | tf_op jit(solution)/shard_map/ppermute | solution.py:67
  66.6 3.5 %collective-permute-start.29 = (f32[128,256]{1,0:T(8,128)S(1)}, f32[128,256]{1,0:T(8,128)S(1)}, u32[]{:S(2)}, u32[]{:S(2)}) collective-permute-start(f32[128,256]{1,0:T(8,128)S(1)} %get-tuple-element.224), channel_id=1, source_target_pairs={{0,1},{1,0},{2,3},{3,2},{4,5},{5,4},{6,7},{7,6},{8,9},{9,8},{10,11... | collective-permute-start | bytes 393224 | tf_op jit(solution)/shard_map/ppermute | solution.py:67
  67.9 5.8 %collective-permute-start.30 = (f32[128,256]{1,0:T(8,128)S(1)}, f32[128,256]{1,0:T(8,128)S(1)}, u32[]{:S(2)}, u32[]{:S(2)}) collective-permute-start(f32[128,256]{1,0:T(8,128)S(1)} %get-tuple-element.226), channel_id=1, source_target_pairs={{0,16},{1,4},{2,18},{3,6},{4,1},{5,8},{6,3},{7,10},{8,5},{9,12},{1... | collective-permute-start | bytes 393224 | tf_op jit(solution)/shard_map/ppermute | solution.py:67
  68.3 5.4 %collective-permute-start.32 = (f32[8,9,128]{2,1,0:T(8,128)S(1)}, f32[8,9,128]{2,1,0:T(8,128)S(1)}, u32[]{:S(2)}, u32[]{:S(2)}) collective-permute-start(f32[8,9,128]{2,1,0:T(8,128)S(1)} %get-tuple-element.229.rest_0_), channel_id=1, source_target_pairs={{0,8},{1,9},{2,10},{3,11},{4,12},{5,13},{6,14},{7,15},{8,0},{9,1},... | collective-permute-start | bytes 110600 | tf_op jit(solution)/shard_map/ppermute | solution.py:67
  74.5 3.4 %collective-permute-start.33 = (f32[128,256]{1,0:T(8,128)S(1)}, f32[128,256]{1,0:T(8,128)S(1)}, u32[]{:S(2)}, u32[]{:S(2)}) collective-permute-start(f32[128,256]{1,0:T(8,128)S(1)} %get-tuple-element.231), channel_id=1, source_target_pairs={{0,1},{1,0},{2,3},{3,2},{4,5},{5,4},{6,7},{7,6},{8,9},{9,8},{10,11... | collective-permute-start | bytes 393224 | tf_op jit(solution)/shard_map/ppermute | solution.py:67
  76.8 4.7 %collective-permute-start.34 = (f32[128,256]{1,0:T(8,128)S(1)}, f32[128,256]{1,0:T(8,128)S(1)}, u32[]{:S(2)}, u32[]{:S(2)}) collective-permute-start(f32[128,256]{1,0:T(8,128)S(1)} %get-tuple-element.233), channel_id=1, source_target_pairs={{0,16},{1,4},{2,18},{3,6},{4,1},{5,8},{6,3},{7,10},{8,5},{9,12},{1... | collective-permute-start | bytes 393224 | tf_op jit(solution)/shard_map/ppermute | solution.py:67
  83.4 4.7 %collective-permute-start.37 = (f32[128,256]{1,0:T(8,128)S(1)}, f32[128,256]{1,0:T(8,128)S(1)}, u32[]{:S(2)}, u32[]{:S(2)}) collective-permute-start(f32[128,256]{1,0:T(8,128)S(1)} %get-tuple-element.244), channel_id=1, source_target_pairs={{0,16},{1,4},{2,18},{3,6},{4,1},{5,8},{6,3},{7,10},{8,5},{9,12},{1... | collective-permute-start | bytes 393224 | tf_op jit(solution)/shard_map/ppermute | solution.py:67
  84.1 3.1 %collective-permute-start.38 = (f32[32,256]{1,0:T(8,128)S(1)}, f32[32,256]{1,0:T(8,128)S(1)}, u32[]{:S(2)}, u32[]{:S(2)}) collective-permute-start(f32[32,256]{1,0:T(8,128)S(1)} %get-tuple-element.245), channel_id=1, source_target_pairs={{0,2},{1,3},{2,0},{3,1},{4,6},{5,7},{6,4},{7,5},{8,10},{9,11},{10,... | collective-permute-start | bytes 98312 | tf_op jit(solution)/shard_map/ppermute | solution.py:67
  89.4 4.7 %collective-permute-start.40 = (f32[128,256]{1,0:T(8,128)S(1)}, f32[128,256]{1,0:T(8,128)S(1)}, u32[]{:S(2)}, u32[]{:S(2)}) collective-permute-start(f32[128,256]{1,0:T(8,128)S(1)} %get-tuple-element.251), channel_id=1, source_target_pairs={{0,16},{1,4},{2,18},{3,6},{4,1},{5,8},{6,3},{7,10},{8,5},{9,12},{1... | collective-permute-start | bytes 393224 | tf_op jit(solution)/shard_map/ppermute | solution.py:67
  90.1 3.1 %collective-permute-start.41 = (f32[32,256]{1,0:T(8,128)S(1)}, f32[32,256]{1,0:T(8,128)S(1)}, u32[]{:S(2)}, u32[]{:S(2)}) collective-permute-start(f32[32,256]{1,0:T(8,128)S(1)} %get-tuple-element.252), channel_id=1, source_target_pairs={{0,2},{1,3},{2,0},{3,1},{4,6},{5,7},{6,4},{7,5},{8,10},{9,11},{10,... | collective-permute-start | bytes 98312 | tf_op jit(solution)/shard_map/ppermute | solution.py:67
  95.4 4.7 %collective-permute-start.43 = (f32[128,256]{1,0:T(8,128)S(1)}, f32[128,256]{1,0:T(8,128)S(1)}, u32[]{:S(2)}, u32[]{:S(2)}) collective-permute-start(f32[128,256]{1,0:T(8,128)S(1)} %get-tuple-element.258), channel_id=1, source_target_pairs={{0,16},{1,4},{2,18},{3,6},{4,1},{5,8},{6,3},{7,10},{8,5},{9,12},{1... | collective-permute-start | bytes 393224 | tf_op jit(solution)/shard_map/ppermute | solution.py:67
  96.1 3.1 %collective-permute-start.44 = (f32[32,256]{1,0:T(8,128)S(1)}, f32[32,256]{1,0:T(8,128)S(1)}, u32[]{:S(2)}, u32[]{:S(2)}) collective-permute-start(f32[32,256]{1,0:T(8,128)S(1)} %get-tuple-element.259), channel_id=1, source_target_pairs={{0,2},{1,3},{2,0},{3,1},{4,6},{5,7},{6,4},{7,5},{8,10},{9,11},{10,... | collective-permute-start | bytes 98312 | tf_op jit(solution)/shard_map/ppermute | solution.py:67
  101.3 4.7 %collective-permute-start.46 = (f32[128,256]{1,0:T(8,128)S(1)}, f32[128,256]{1,0:T(8,128)S(1)}, u32[]{:S(2)}, u32[]{:S(2)}) collective-permute-start(f32[128,256]{1,0:T(8,128)S(1)} %get-tuple-element.265), channel_id=1, source_target_pairs={{0,16},{1,4},{2,18},{3,6},{4,1},{5,8},{6,3},{7,10},{8,5},{9,12},{1... | collective-permute-start | bytes 393224 | tf_op jit(solution)/shard_map/ppermute | solution.py:67
  102.0 3.1 %collective-permute-start.47 = (f32[32,256]{1,0:T(8,128)S(1)}, f32[32,256]{1,0:T(8,128)S(1)}, u32[]{:S(2)}, u32[]{:S(2)}) collective-permute-start(f32[32,256]{1,0:T(8,128)S(1)} %get-tuple-element.266), channel_id=1, source_target_pairs={{0,2},{1,3},{2,0},{3,1},{4,6},{5,7},{6,4},{7,5},{8,10},{9,11},{10,... | collective-permute-start | bytes 98312 | tf_op jit(solution)/shard_map/ppermute | solution.py:67
  107.3 4.7 %collective-permute-start.49 = (f32[128,256]{1,0:T(8,128)S(1)}, f32[128,256]{1,0:T(8,128)S(1)}, u32[]{:S(2)}, u32[]{:S(2)}) collective-permute-start(f32[128,256]{1,0:T(8,128)S(1)} %get-tuple-element.272), channel_id=1, source_target_pairs={{0,16},{1,4},{2,18},{3,6},{4,1},{5,8},{6,3},{7,10},{8,5},{9,12},{1... | collective-permute-start | bytes 393224 | tf_op jit(solution)/shard_map/ppermute | solution.py:67
  113.3 4.7 %collective-permute-start.52 = (f32[128,256]{1,0:T(8,128)S(1)}, f32[128,256]{1,0:T(8,128)S(1)}, u32[]{:S(2)}, u32[]{:S(2)}) collective-permute-start(f32[128,256]{1,0:T(8,128)S(1)} %get-tuple-element.279), channel_id=1, source_target_pairs={{0,16},{1,4},{2,18},{3,6},{4,1},{5,8},{6,3},{7,10},{8,5},{9,12},{1... | collective-permute-start | bytes 393224 | tf_op jit(solution)/shard_map/ppermute | solution.py:67
  119.2 4.7 %collective-permute-start.55 = (f32[128,256]{1,0:T(8,128)S(1)}, f32[128,256]{1,0:T(8,128)S(1)}, u32[]{:S(2)}, u32[]{:S(2)}) collective-permute-start(f32[128,256]{1,0:T(8,128)S(1)} %get-tuple-element.286), channel_id=1, source_target_pairs={{0,16},{1,4},{2,18},{3,6},{4,1},{5,8},{6,3},{7,10},{8,5},{9,12},{1... | collective-permute-start | bytes 393224 | tf_op jit(solution)/shard_map/ppermute | solution.py:67
  125.4 16.4 %collective-permute-start.62 = (f32[256,256]{1,0:T(8,128)S(1)}, f32[256,256]{1,0:T(8,128)S(1)}, u32[]{:S(2)}, u32[]{:S(2)}) collective-permute-start(f32[256,256]{1,0:T(8,128)S(1)} %get-tuple-element.296.refs_4_), channel_id=1, source_target_pairs={{0,16},{1,2},{2,1},{3,19},{4,20},{5,6},{6,5},{7,23},{8,24},{9,10},... | collective-permute-start | bytes 786440 | tf_op jit(solution)/shard_map/ppermute | solution.py:67
  125.6 16.2 %collective-permute-start.63 = (f32[256,256]{1,0:T(8,128)S(1)}, f32[256,256]{1,0:T(8,128)S(1)}, u32[]{:S(2)}, u32[]{:S(2)}) collective-permute-start(f32[256,256]{1,0:T(8,128)S(1)} %get-tuple-element.297.cur.refs_6_), channel_id=1, source_target_pairs={{0,16},{1,2},{2,1},{3,19},{4,20},{5,6},{6,5},{7,23},{8,24},{9,10},... | collective-permute-start | bytes 786440 | tf_op jit(solution)/shard_map/ppermute | solution.py:67
  127.7 7.7 %collective-permute-start.58 = (f32[2,64,128]{2,1,0:T(8,128)S(1)}, f32[2,64,128]{2,1,0:T(8,128)S(1)}, u32[]{:S(2)}, u32[]{:S(2)}) collective-permute-start(f32[2,64,128]{2,1,0:T(8,128)S(1)} %get-tuple-element.292), channel_id=1, source_target_pairs={{0,0},{1,2},{2,1},{3,3},{4,4},{5,6},{6,5},{7,7},{8,8},{9,10},{10,9... | collective-permute-start | bytes 196616 | tf_op jit(solution)/shard_map/ppermute | solution.py:67
  129.8 6.7 %collective-permute-start.59 = (f32[2,64,128]{2,1,0:T(8,128)S(1)}, f32[2,64,128]{2,1,0:T(8,128)S(1)}, u32[]{:S(2)}, u32[]{:S(2)}) collective-permute-start(f32[2,64,128]{2,1,0:T(8,128)S(1)} %get-tuple-element.293), channel_id=1, source_target_pairs={{0,4},{1,6},{2,5},{3,7},{4,0},{5,2},{6,1},{7,3},{8,12},{9,14},{10,... | collective-permute-start | bytes 196616 | tf_op jit(solution)/shard_map/ppermute | solution.py:67
  131.9 6.2 %collective-permute-start.60 = (f32[2,64,128]{2,1,0:T(8,128)S(1)}, f32[2,64,128]{2,1,0:T(8,128)S(1)}, u32[]{:S(2)}, u32[]{:S(2)}) collective-permute-start(f32[2,64,128]{2,1,0:T(8,128)S(1)} %get-tuple-element.294), channel_id=1, source_target_pairs={{0,8},{1,10},{2,9},{3,11},{4,12},{5,14},{6,13},{7,15},{8,0},{9,2},... | collective-permute-start | bytes 196616 | tf_op jit(solution)/shard_map/ppermute | solution.py:67
  135.4 6.4 %collective-permute-start.61 = (f32[2,64,128]{2,1,0:T(8,128)S(1)}, f32[2,64,128]{2,1,0:T(8,128)S(1)}, u32[]{:S(2)}, u32[]{:S(2)}) collective-permute-start(f32[2,64,128]{2,1,0:T(8,128)S(1)} %get-tuple-element.295), channel_id=1, source_target_pairs={{0,12},{1,14},{2,13},{3,15},{4,8},{5,10},{6,9},{7,11},{8,4},{9,6},... | collective-permute-start | bytes 196616 | tf_op jit(solution)/shard_map/ppermute | solution.py:67
  (38 other events, 78.9 us)

commit v6 on v5

--- a/solution.py
+++ b/solution.py
@@ -114,6 +114,7 @@
 def inner_differences(cur, cm, near, deep):
     depth = cur.shape[1]
     size = GROUP * COLS
+    cm = cm.at[0] if len(cm.shape) == 3 else cm
     own = split(cur[...])
     along = mm(jnp.concatenate(own, axis=1), deep[...])
     blank = jnp.zeros((4 * COLS, depth), BF16)
@@ -131,6 +132,7 @@
 
 def side_differences(rows, zm, side):
     size = GROUP * COLS
+    zm = zm.at[0] if len(zm.shape) == 3 else zm
     from_z = split(zm[...])
     for n in range(rows // size):
         sides = slice(n * GROUP * 4, n * GROUP * 4 + GROUP * 4)
@@ -140,6 +142,7 @@
 
 def edge_differences(flags, rows, ym, edge):
     size = GROUP * COLS
+    ym = ym.at[0] if len(ym.shape) == 3 else ym
     out = mm(edge[...], jnp.concatenate(split(ym[...]), axis=0))
     start = jnp.where(flags[1] == 1, 0, rows - size)
     return pl.ds(pl.multiple_of(start, size), size), out[0:size], out[size:]
@@ -163,54 +166,64 @@
     yo[...] = jnp.where(flags[1] == 0, new[size - 4 * COLS :], new[0 : 4 * COLS])
 
 
-def load_kernel(flags, *refs):
-    half = len(refs) // 2
-    for source, out in zip(refs[:half], refs[half:]):
-        out[...] = source[...]
-
-
-def settle_kernel(flags, a, b, recv_a, recv_b, a_out, b_out, *outs):
+def choose(flags, pairs, sems):
     keep = flags[0] == flags[1]
-    for n, (own, recv, out) in enumerate(((a, recv_a, a_out), (b, recv_b, b_out))):
-        out[...] = jnp.where(keep, own[...], recv[...])
-        rims(flags, out, *(ref.at[n] for ref in outs))
-
-
-def settle_model_kernel(flags, a, b, recv, a_out, b_out):
-    keep = flags[0] == flags[1]
-    a_out[...] = jnp.where(keep, a[...], recv[0])
-    b_out[...] = jnp.where(keep, b[...], recv[1])
-
-
-def settle_one(with_rims, flags, own, recv, out, *outs):
+
+    @pl.when(keep)
+    def _():
+        copies = [pltpu.make_async_copy(own, out, sems.at[n])
+                  for n, (own, recv, out) in enumerate(pairs)]
+        for copy in copies:
+            copy.start()
+        for copy in copies:
+            copy.wait()
+
+    @pl.when(jnp.logical_not(keep))
+    def _():
+        for own, recv, out in pairs:
+            out[...] = recv[...]
+
+
+def settle_kernel(flags, a, b, recv_a, recv_b, a_out, b_out, zo, co, yo, sems):
+    choose(flags, [(a, recv_a, a_out), (b, recv_b, b_out)], sems)
+    for n, out in enumerate((a_out, b_out)):
+        rims(flags, out, zo.at[n], co.at[n], yo.at[n])
+
+
+def settle_model_kernel(flags, a, b, recv, a_out, b_out, sems):
+    choose(flags, [(a, recv.at[0], a_out), (b, recv.at[1], b_out)], sems)
+
+
+def settle_adjoint_kernel(flags, a, b, recv_a, recv_b, a_out, b_out, sems):
+    choose(flags, [(a, recv_a, a_out), (b, recv_b, b_out)], sems)
+
+
+def select_kernel(flags, own, recv, out):
     out[...] = jnp.where(flags[0] == flags[1], own[...], recv[...])
-    if with_rims:
-        rims(flags, out, *outs)
-
-
-def first_inner_kernel(flags, lr, cur, lr_cm, cm, near, deep, *outs):
+
+
+def first_inner_kernel(flags, lr, cur, cm, near, deep, *outs):
     ri, rx, rz, sums_out, di_out, dx_out, dz_out = outs
-    for here, spare, spare_z, di, dx, dz in inner_differences(lr, lr_cm, near, deep):
+    for here, spare, spare_z, di, dx, dz in inner_differences(lr, cm.at[0], near, deep):
         ri[here], rx[here], rz[here] = di, dx, dz
-    for here, sums, sums_z, di, dx, dz in inner_differences(cur, cm, near, deep):
+    for here, sums, sums_z, di, dx, dz in inner_differences(cur, cm.at[1], near, deep):
         sums_out[here] = sums + sums_z + (3.0 * SECOND[0] * 5040) * cur[here]
         di_out[here], dx_out[here], dz_out[here] = di, dx, dz
 
 
-def first_outer_kernel(flags, cur, prev, vel, ri, rx, rz, sums, di, dx, dz, inj, lr_zm, lr_ym, zm,
-                       ym, side, edge, mine, got, new, zo, co, yo, lists, k0, ki, kx, kz):
+def first_outer_kernel(flags, cur, prev, vel, ri, rx, rz, sums, di, dx, dz, inj, zm, ym, side, edge, mine, got, new, zo, co, yo, lists, k0, ki, kx, kz):
     rows = cur.shape[0]
     merge(0, flags, mine, got, lists)
     kz[...] = sums[...]
     ki[...] = di[...]
-    here, more, more_i = edge_differences(flags, rows, ym, edge)
+    here, more, more_i = edge_differences(flags, rows, ym.at[1], edge)
     kz[here] += more
     ki[here] += more_i
-    lr_here, spare, lr_more_i = edge_differences(flags, rows, lr_ym, edge)
+    lr_here, spare, lr_more_i = edge_differences(flags, rows, ym.at[0], edge)
     k0[...] = ri[...]
     k0[lr_here] += lr_more_i
-    first = side_differences(rows, lr_zm, side)
-    second = side_differences(rows, zm, side)
+    first = side_differences(rows, zm.at[0], side)
+    second = side_differences(rows, zm.at[1], side)
     for (here, spare, more_r), (spare_here, more, more_x) in zip(first, second):
         square = vel[here] * vel[here]
         scaled = square * (1.0 / (840 * 840))
@@ -266,14 +279,18 @@
     change[...] = (cur[...] - prev[...]) - (prev[...] - before[...])
 
 
-def outer_kernel(stage, flags, part, k0, ki, kx, zm, ym, side, edge, *rest):
-    if stage is None:
-        new, zo, co, yo = rest
+def outer_kernel(stage, double, flags, part, k0, ki, kx, zm, ym, side, edge, *rest):
+    rest = list(rest)
+    other = rest.pop(0) if double else None
+    if stage is not None:
+        merge(stage, flags, rest.pop(0), rest.pop(0), rest.pop())
+    new, zo, co, yo = rest
+    outer(flags, part, k0, ki, kx, zm, ym, side, edge, new)
+    if double:
+        for n, field in enumerate((new, other)):
+            rims(flags, field, zo.at[n], co.at[n], yo.at[n])
     else:
-        mine, got, new, zo, co, yo, lists = rest
-        merge(stage, flags, mine, got, lists)
-    outer(flags, part, k0, ki, kx, zm, ym, side, edge, new)
-    rims(flags, new, zo, co, yo)
+        rims(flags, new, zo, co, yo)
 
 
 def lists_kernel(flags, lists, spot, pick, at, obs):
@@ -329,12 +346,12 @@
 
 
 def adjoint_first_kernel(flags, cur, prev, k0, ki, kx, kz, cm, near, deep, part):
-    inner(cur, prev, k0, ki, kx, kz, cm, near, deep, None, part)
+    inner(cur, prev, k0, ki, kx, kz, cm.at[1], near, deep, None, part)
 
 
 def turn_kernel(t, flags, part, k0, ki, kx, zm, ym, side, edge, u_part, u_zm, u_ym, spot, pick, at, obs, new, u_new, zo, co, yo):
     outer(flags, part, k0, ki, kx, zm, ym, side, edge, new)
-    outer(flags, u_part, k0, ki, kx, u_zm, u_ym, side, edge, u_new)
+    outer(flags, u_part, k0, ki, kx, u_zm.at[1], u_ym.at[1], side, edge, u_new)
     u_new[...] += injection(t, new, spot, pick, at, obs)
     rims(flags, u_new, zo, co, yo)
 
@@ -364,10 +381,7 @@
 
 
 def filter_kernel(flags, *refs):
-    *pieces, own, got, prev, prev_got, out, state, prev_state = refs
-    keep = flags[0] == flags[1]
-    state[...] = jnp.where(keep, own[...], got[...])
-    prev_state[...] = jnp.where(keep, prev[...], prev_got[...])
+    *pieces, out = refs
     height, lanes = pieces[0].shape[1:]
     chunk, rows, full = out.shape
     groups = lanes // chunk
@@ -392,17 +406,20 @@
     return jax.ShapeDtypeStruct(shape, F32)
 
 
-def call(kernel, name, outs, *args):
+def call(kernel, name, outs, *args, weight=0, far=0):
     specs = [pl.BlockSpec(memory_space=pltpu.SMEM)]
-    specs += [pl.BlockSpec(memory_space=pltpu.VMEM)] * (len(args) - 1)
+    specs += [pl.BlockSpec(memory_space=pl.ANY)] * far
+    specs += [pl.BlockSpec(memory_space=pltpu.VMEM)] * (len(args) - 1 - far)
     return pl.pallas_call(
         kernel,
         name=name,
         out_shape=outs,
         in_specs=specs,
         out_specs=[pl.BlockSpec(memory_space=pltpu.VMEM)] * len(outs),
+        scratch_shapes=[pltpu.SemaphoreType.DMA((far,))] if far else [],
         compiler_params=pltpu.CompilerParams(vmem_limit_bytes=VMEM_BYTES),
-        cost_estimate=pl.CostEstimate(flops=1000, bytes_accessed=1000, transcendentals=0),
+        cost_estimate=pl.CostEstimate(
+            flops=1000, bytes_accessed=1000 + int(weight * 3_600_000), transcendentals=0),
     )(*args)
 
 
@@ -455,17 +472,15 @@
     fwd_before, adj_now, adj_before = flat(fwd_before), flat(adj_now), flat(adj_before)
     got = [send(v, swap_perm) for v in (log_density, fwd_now)]
     got_model = send(jnp.stack([velocity, fwd_before]), swap_perm)
-    log_density, fwd_now, velocity, fwd_before, adj_now, adj_before = call(
-        load_kernel, "load", [field] * 6, flags, log_density, fwd_now, velocity, fwd_before,
-        adj_now, adj_before)
     density, p_now, *out = call(settle_kernel, "settle",
                                 [field, field] + [shaped(2, *r.shape) for r in rim],
-                                flags, log_density, fwd_now, *got)
+                                flags, log_density, fwd_now, *got, far=2)
     zm, cm, ym = halo(*out)
-    parts = call(first_inner_kernel, "first_inner", [field] * 7, flags, density, p_now, cm[0], cm[1],
-                 near, deep)
+    got_adjoint = [send(after(v, density), swap_perm) for v in (adj_now, adj_before)]
     vel, p_before = call(settle_model_kernel, "settle_model", [field, field],
-                         flags, velocity, fwd_before, got_model)
+                         flags, velocity, fwd_before, got_model, weight=0.6, far=2)
+    parts = call(first_inner_kernel, "first_inner", [field] * 7, flags, density, p_now, cm,
+                 near, deep, weight=1.3)
 
     plane = nx * cols * depth
     src_i = src_cell // plane - y * rows
@@ -481,71 +496,57 @@
     cells = jnp.where(live.reshape(-1), rec_cells[0], -1)
     lists = jnp.concatenate([observed, cells[None, :].astype(F32)], axis=0)[None]
 
-    lag = 2 if 2 * (len(stages) - 1) < steps - 1 else 1
     moved = send(lists, stages[0][0])
 
-    inj, = call(functools.partial(source_kernel, 0), "source", [field], flags, srow, sz, wave)
+    inj, = call(functools.partial(source_kernel, 0), "source", [field], flags, srow, sz, wave,
+                weight=0.6)
     grown = shaped(2, *lists.shape[1:])
     new, zo, co, yo, lists, *model = call(
         first_outer_kernel, "first_outer", [field] + rim + [grown] + [field] * 4, flags, p_now,
-        p_before, vel, *parts, inj, zm[0], ym[0], zm[1], ym[1], side, edge, lists, moved)
+        p_before, vel, *parts, inj, zm, ym, side, edge, lists, moved)
     k0, ki, kx, kz = model
     states = [p_before, p_now, new]
     changes = []
     zm, cm, ym = halo(zo, co, yo)
-    if lag == 1:
-        moved = send(lists, stages[1][0])
+    u_now, u_before = call(settle_adjoint_kernel, "settle_adjoint", [field, field], flags, adj_now,
+                           adj_before, *got_adjoint, weight=0.6, far=2)
+    double = 2
     for t in range(1, steps):
         cur, prev, before = states[:-4:-1]
+        stage = t if t < len(stages) else None
+        extra = [lists, send(lists, stages[t][0])] if stage is not None else []
         part, change = call(
             functools.partial(forward_inner_kernel, t), "forward_inner", [field, field], flags, cur,
-            prev, *model, cm, near, deep, srow, sz, wave, before)
+            prev, *model, cm, near, deep, srow, sz, wave, before, weight=1.2)
         changes.append(change)
-        if t == 1:
-            got_now = send(after(adj_now, part), swap_perm)
-        if t == 2:
-            u_now, *u_rim = call(functools.partial(settle_one, True), "settle_adjoint",
-                                 [field] + rim, flags, adj_now, after(got_now, part))
-            part = after(part, u_now)
-            got_before = send(after(adj_before, part), swap_perm)
-        if t == 3:
-            u_before, = call(functools.partial(settle_one, False), "settle_before", [field],
-                             flags, adj_before, after(got_before, part))
-            part = after(part, u_before)
-            u_zm, u_cm, u_ym = halo(*(after(r, part) for r in u_rim))
-        if t == 4:
-            u_part, = call(adjoint_first_kernel, "adjoint_inner", [field], flags, u_now, u_before,
-                           *model, u_cm, near, deep)
-            part = after(part, u_part)
-        if t == 5:
-            part = after(part, u_zm, u_ym)
+        args = [flags, part, k0, ki, kx, zm, ym, side, edge]
         if t == steps - 1:
+            u_part, = call(adjoint_first_kernel, "adjoint_first", [field], flags, u_now, u_before,
+                           *model, u_cm, near, deep, weight=1.1)
             slots = subs * CAP
             receivers = call(
                 lists_kernel, "lists",
                 [jax.ShapeDtypeStruct((size, slots), BF16),
                  jax.ShapeDtypeStruct((slots, size), BF16), shaped(slots, depth),
-                 shaped(slots, steps)], flags, lists)
+                 shaped(slots, steps)], flags, lists, weight=0.8)
             new, u_new, *out = call(
-                functools.partial(turn_kernel, t), "turn", [field, field] + rim, flags, part,
-                k0, ki, kx, zm, ym, side, edge, u_part, u_zm, u_ym, *receivers)
+                functools.partial(turn_kernel, t), "turn", [field, field] + rim, *args, u_part,
+                u_zm, u_ym, *receivers)
             states.append(new)
             break
-        args = [part, k0, ki, kx, zm, ym, side, edge]
-        outs = [field] + rim
-        stage = t // lag if t % lag == 0 and t // lag < len(stages) else None
-        if stage is not None:
-            args += [lists, moved]
+        if t == double:
+            args.append(u_now)
+        outs = [field] + ([shaped(2, *r.shape) for r in rim] if t == double else rim)
+        if extra:
             outs = outs + [shaped(2 * lists.shape[0], *lists.shape[1:])]
-        elif t % lag == 1 and t // lag + 1 < len(stages):
-            moved = send(after(lists, part), stages[t // lag + 1][0])
-        new, *out = call(functools.partial(outer_kernel, stage), "forward_outer", outs, flags, *args)
-        if stage is not None:
+        new, *out = call(functools.partial(outer_kernel, stage, t == double), "forward_outer", outs,
+                         *args, *extra)
+        if extra:
             lists = out.pop()
-            if lag == 1 and stage + 1 < len(stages):
-                moved = send(lists, stages[stage + 1][0])
         states.append(new)
         zm, cm, ym = halo(*out)
+        if t == double:
+            u_zm, u_cm, u_ym = zm, cm, ym
 
     zm, cm, ym = halo(*out)
     u_before, u_now = u_now, u_new
@@ -557,7 +558,7 @@
         terms = [changes[t + 1], *image] if image else states[:-4:-1]
         part, *image = call(
             functools.partial(adjoint_inner_kernel, t), "adjoint_inner", [field, field], flags,
-            u_now, u_before, *model, cm, near, deep, states[t + 2], *receivers, *terms)
+            u_now, u_before, *model, cm, near, deep, states[t + 2], *receivers, *terms, weight=1.5)
         args = [part, k0, ki, kx, zm, ym, side, edge]
         if j == steps - 1:
             got_prev = send(after(u_now, part), swap_perm)
@@ -566,17 +567,17 @@
                 flags, *args, *image, changes[0], vel)
             break
         u_before = u_now
-        u_now, *out = call(functools.partial(outer_kernel, None), "adjoint_outer", [field] + rim,
+        u_now, *out = call(functools.partial(outer_kernel, None, False), "adjoint_outer", [field] + rim,
                            flags, *args)
         zm, cm, ym = halo(*out)
 
-    pieces = call(join_kernel, "join", [shaped(2, *half.shape[1:])] * nq, flags, mine,
-                  send(other, c_perm))
     got = send(u_last, swap_perm)
+    pieces = call(join_kernel, "join", [shaped(2, *half.shape[1:])] * nq, flags,
+                  after(mine, got_prev), send(other, c_perm))
     pieces = [send(value, plan.spread(s)) for s, value in enumerate(pieces)]
-    gradient, adj_out, adj_prev = call(
-        filter_kernel, "filter", [shaped(chunk, rows, nx * cols), field, field], flags, *pieces,
-        u_last, got, u_now, got_prev)
+    adj_prev, = call(select_kernel, "select_previous", [field], flags, u_now, got_prev, weight=0.6)
+    adj_out, = call(select_kernel, "select_state", [field], flags, u_last, got, weight=0.6)
+    gradient, = call(filter_kernel, "filter", [shaped(chunk, rows, nx * cols)], flags, *pieces)
     block = (rows, cols, depth)
     return gradient, adj_out.reshape(block), adj_prev.reshape(block)
 

time: 144 us -> 139 us (0.965)
  waiting for transfers between devices: 42.5 us -> 27.8 us
  starting transfers between devices: 50.8 us -> 59.4 us
  local copies, waits for them, and re-layouts: 4 us -> 1.45 us
  other arithmetic: 2.28 us -> 4.26 us
    ppermute x64 -> x61, waiting for transfers between devices: 42.5 us -> 27.8 us  [send(): return lax.ppermute(value, ALL, pairs)]
    ppermute x64 -> x61, starting transfers between devices: 50.8 us -> 59.4 us  [send(): return lax.ppermute(value, ALL, pairs)]
    unnamed x45 -> x39, local copies, waits for them, and re-layouts: 3.7 us -> 1.18 us
  transfers between devices with their start and end apart: 64 -> 61, of which waited for: 39 -> 27; matrix products, arithmetic and copies ran while one was open for 2% -> 3% of each run, Pallas kernels for 21% -> 23%
where the time goes in v6:
time: 139 us
  starting transfers between devices  59.4 us (43%)
  Pallas kernels  44.6 us (32%)
  waiting for transfers between devices  27.8 us (20%)
  other arithmetic  4.26 us (3%)
  local copies, waits for them, and re-layouts  1.45 us (1%)
    ppermute x61, starting transfers between devices, send(): return lax.ppermute(value, ALL, pairs)  59.4 us
    pallas_call x40, Pallas kernels, call(): pl.pallas_call(kernel, name=name, out_shape=outs, in_specs=specs, out_spe...  44.6 us
    ppermute x61, waiting for transfers between devices, send(): return lax.ppermute(value, ALL, pairs)  27.8 us
  transfers between devices with their start and end apart: 61, of which 27 were waited for; matrix products, arithmetic and copies ran while one was open for 3% of the time, Pallas kernels for 23%

profile of v6, /device:TPU:1, one launch (start us, length us, event | category | flops | bytes accessed | tf_op | source)
XLA Modules:
  0.0 138.7 jit_solution(9702393537195571772)
XLA Ops:
  0.6 2.7 %collective-permute-start.1 = (f32[256,256]{1,0:T(8,128)}, f32[256,256]{1,0:T(8,128)S(1)}, u32[]{:S(2)}, u32[]{:S(2)}) collective-permute-start(f32[256,256]{1,0:T(8,128)} %bitcast.38), channel_id=1, source_target_pairs={{0,16},{1,2},{2,1},{3,19},{4,20},{5,6},{6,5},{7,23},{8,24},{9,10},... | collective-permute-start | bytes 786440 | tf_op jit(solution)/shard_map/ppermute | solution.py:67
  3.4 1.9 %pad_maximum_fusion = f32[2,256,256]{2,1,0:T(8,128)} fusion(f32[1,256,256]{2,1,0:T(8,128)} %bitcast.26, f32[1,256,256]{2,1,0:T(8,128)} %bitcast.24), kind=kLoop, calls=%fused_computation | loop fusion | flops 131072 | bytes 1048576 | tf_op jit(solution)/shard_map/stack | solution.py:474
  5.3 1.7 %collective-permute-start.2 = (f32[2,256,256]{2,1,0:T(8,128)}, f32[2,256,256]{2,1,0:T(8,128)S(1)}, u32[]{:S(2)}, u32[]{:S(2)}) collective-permute-start(f32[2,256,256]{2,1,0:T(8,128)} %pad_maximum_fusion), channel_id=1, source_target_pairs={{0,16},{1,2},{2,1},{3,19},{4,20},{5,6},{6,5},{7,23},{8,24},{9,10},... | collective-permute-start | bytes 1572872 | tf_op jit(solution)/shard_map/ppermute | solution.py:67
  9.1 1.6 %collective-permute-done.recv_a = f32[256,256]{1,0:T(8,128)S(1)} collective-permute-done((f32[256,256]{1,0:T(8,128)}, f32[256,256]{1,0:T(8,128)S(1)}, u32[]{:S(2)}, u32[]{:S(2)}) %collective-permute-start) | collective-permute-done | bytes 262176 | tf_op jit(solution)/shard_map/ppermute | solution.py:67
  12.1 1.8 %collective-permute-start.4 = (f32[2,128,256]{2,1,0:T(8,128)S(1)}, f32[2,128,256]{2,1,0:T(8,128)S(1)}, u32[]{:S(2)}, u32[]{:S(2)}) collective-permute-start(f32[2,128,256]{2,1,0:T(8,128)S(1)} %get-tuple-element.142), channel_id=1, source_target_pairs={{0,16},{1,4},{2,18},{3,6},{4,1},{5,8},{6,3},{7,10},{8,5},{9,12},{1... | collective-permute-start | bytes 786440 | tf_op jit(solution)/shard_map/ppermute | solution.py:67
  14.9 1.4 %collective-permute-done.2.recv = f32[2,256,256]{2,1,0:T(8,128)S(1)} collective-permute-done((f32[2,256,256]{2,1,0:T(8,128)}, f32[2,256,256]{2,1,0:T(8,128)S(1)}, u32[]{:S(2)}, u32[]{:S(2)}) %collective-permute-start.2) | collective-permute-done | bytes 524320 | tf_op jit(solution)/shard_map/ppermute | solution.py:67
  16.3 1.4 %collective-permute-start.14 = (f32[256,256]{1,0:T(8,128)S(1)}, f32[256,256]{1,0:T(8,128)S(1)}, u32[]{:S(2)}, u32[]{:S(2)}) collective-permute-start(f32[256,256]{1,0:T(8,128)S(1)} %bitcast.40), channel_id=1, source_target_pairs={{0,16},{1,2},{2,1},{3,19},{4,20},{5,6},{6,5},{7,23},{8,24},{9,10},... | collective-permute-start | bytes 786440 | tf_op jit(solution)/shard_map/ppermute | solution.py:67
  20.7 1.3 first_inner.1
  22.1 1.1 first_outer.1
  24.3 1.3 collective-permute-start.8
  27.0 1.3 forward_inner.7
  28.3 1.6 %collective-permute-done.10.rest_1_ = f32[2,9,128]{2,1,0:T(8,128)S(1)} collective-permute-done((f32[2,9,128]{2,1,0:T(8,128)S(1)}, f32[2,9,128]{2,1,0:T(8,128)S(1)}, u32[]{:S(2)}, u32[]{:S(2)}) %collective-permute-start.10) | collective-permute-done | bytes 9248 | tf_op jit(solution)/shard_map/ppermute | solution.py:67
  30.7 2.9 %collective-permute-start.11 = (f32[128,256]{1,0:T(8,128)S(1)}, f32[128,256]{1,0:T(8,128)S(1)}, u32[]{:S(2)}, u32[]{:S(2)}) collective-permute-start(f32[128,256]{1,0:T(8,128)S(1)} %get-tuple-element.158), channel_id=1, source_target_pairs={{0,1},{1,0},{2,3},{3,2},{4,5},{5,4},{6,7},{7,6},{8,9},{9,8},{10,11... | collective-permute-start | bytes 393224 | tf_op jit(solution)/shard_map/ppermute | solution.py:67
  33.6 1.3 collective-permute-start.12
  34.9 2.6 %collective-permute-start.16 = (f32[4,9,128]{2,1,0:T(8,128)S(1)}, f32[4,9,128]{2,1,0:T(8,128)S(1)}, u32[]{:S(2)}, u32[]{:S(2)}) collective-permute-start(f32[4,9,128]{2,1,0:T(8,128)S(1)} %get-tuple-element.165.rest_1_), channel_id=1, source_target_pairs={{0,4},{1,5},{2,6},{3,7},{4,0},{5,1},{6,2},{7,3},{8,12},{9,13},{10,... | collective-permute-start | bytes 55304 | tf_op jit(solution)/shard_map/ppermute | solution.py:67
  38.2 1.2 forward_inner.8
  40.5 1.1 collective-permute-start.18
  41.5 1.5 %collective-permute-start.19 = (f32[2,32,256]{2,1,0:T(8,128)S(1)}, f32[2,32,256]{2,1,0:T(8,128)S(1)}, u32[]{:S(2)}, u32[]{:S(2)}) collective-permute-start(f32[2,32,256]{2,1,0:T(8,128)S(1)} %get-tuple-element.170), channel_id=1, source_target_pairs={{0,2},{1,3},{2,0},{3,1},{4,6},{5,7},{6,4},{7,5},{8,10},{9,11},{10,... | collective-permute-start | bytes 196616 | tf_op jit(solution)/shard_map/ppermute | solution.py:67
  43.0 2.6 %collective-permute-start.20 = (f32[8,9,128]{2,1,0:T(8,128)S(1)}, f32[8,9,128]{2,1,0:T(8,128)S(1)}, u32[]{:S(2)}, u32[]{:S(2)}) collective-permute-start(f32[8,9,128]{2,1,0:T(8,128)S(1)} %get-tuple-element.171.rest_0_), channel_id=1, source_target_pairs={{0,8},{1,9},{2,10},{3,11},{4,12},{5,13},{6,14},{7,15},{8,0},{9,1},... | collective-permute-start | bytes 110600 | tf_op jit(solution)/shard_map/ppermute | solution.py:67
  45.6 1.2 forward_inner.9
  46.9 1.8 %collective-permute-done.20.rest_1_ = f32[8,9,128]{2,1,0:T(8,128)S(1)} collective-permute-done((f32[8,9,128]{2,1,0:T(8,128)S(1)}, f32[8,9,128]{2,1,0:T(8,128)S(1)}, u32[]{:S(2)}, u32[]{:S(2)}) %collective-permute-start.20) | collective-permute-done | bytes 36896 | tf_op jit(solution)/shard_map/ppermute | solution.py:67
  49.5 2.0 %collective-permute-start.21 = (f32[128,256]{1,0:T(8,128)S(1)}, f32[128,256]{1,0:T(8,128)S(1)}, u32[]{:S(2)}, u32[]{:S(2)}) collective-permute-start(f32[128,256]{1,0:T(8,128)S(1)} %get-tuple-element.173), channel_id=1, source_target_pairs={{0,1},{1,0},{2,3},{3,2},{4,5},{5,4},{6,7},{7,6},{8,9},{9,8},{10,11... | collective-permute-start | bytes 393224 | tf_op jit(solution)/shard_map/ppermute | solution.py:67
  52.8 1.2 forward_inner.10
  54.1 1.7 %collective-permute-done.23.ym = f32[32,256]{1,0:T(8,128)S(1)} collective-permute-done((f32[32,256]{1,0:T(8,128)S(1)}, f32[32,256]{1,0:T(8,128)S(1)}, u32[]{:S(2)}, u32[]{:S(2)}) %collective-permute-start.23) | collective-permute-done | bytes 32800 | tf_op jit(solution)/shard_map/ppermute | solution.py:67
  58.5 1.2 forward_inner.11
  59.8 1.5 %collective-permute-done.26.ym = f32[32,256]{1,0:T(8,128)S(1)} collective-permute-done((f32[32,256]{1,0:T(8,128)S(1)}, f32[32,256]{1,0:T(8,128)S(1)}, u32[]{:S(2)}, u32[]{:S(2)}) %collective-permute-start.26) | collective-permute-done | bytes 32800 | tf_op jit(solution)/shard_map/ppermute | solution.py:67
  64.5 1.2 forward_inner.12
  65.7 1.4 %collective-permute-done.29.ym = f32[32,256]{1,0:T(8,128)S(1)} collective-permute-done((f32[32,256]{1,0:T(8,128)S(1)}, f32[32,256]{1,0:T(8,128)S(1)}, u32[]{:S(2)}, u32[]{:S(2)}) %collective-permute-start.29) | collective-permute-done | bytes 32800 | tf_op jit(solution)/shard_map/ppermute | solution.py:67
  71.2 1.1 adjoint_first.1.u_part
  72.3 1.2 forward_inner.13
  74.0 1.5 %turn.1 = (f32[256,256]{1,0:T(8,128)S(1)}, f32[256,256]{1,0:T(8,128)S(1)}, f32[128,256]{1,0:T(8,128)S(1)}, f32[128,256]{1,0:T(8,128)S(1)}, f32[32,256]{1,0:T(8,128)S(1)}) custom-call(s32[8]{0:T(128)S(1)} %stack.32.flags, f32[256,256]{1,0:T(8,128)S(1)} %get-tuple-element.189.part, f32[256,256]{1,0:T(8,128)S(1)} %get-tuple-element.148.k0, ...), custom_call_target="tpu_custom_call" | custom-call | flops 1000 | bytes 1000 | tf_op jit(solution)/shard_map/turn/pallas_call | solution.py:413
  77.7 1.6 %adjoint_inner.7 = (f32[256,256]{1,0:T(8,128)S(1)}, f32[256,256]{1,0:T(8,128)S(1)}) custom-call(s32[8]{0:T(128)S(1)} %stack.32.flags, f32[256,256]{1,0:T(8,128)S(1)} %get-tuple-element.198.cur.prev, f32[256,256]{1,0:T(8,128)S(1)} %get-tuple-element.164.rest_0_.cur.prev, f32[256,256]{1,0:T(8,128)S(1)} %get-tuple-element.148.k0, ...), custom_call_target="tpu_custom_call" | custom-call | flops 1000 | bytes 5401000 | tf_op jit(solution)/shard_map/adjoint_inner/pallas_call | solution.py:413
  83.6 1.6 %adjoint_inner.8 = (f32[256,256]{1,0:T(8,128)S(1)}, f32[256,256]{1,0:T(8,128)S(1)}) custom-call(s32[8]{0:T(128)S(1)} %stack.32.flags, f32[256,256]{1,0:T(8,128)S(1)} %get-tuple-element.204.cur.prev, f32[256,256]{1,0:T(8,128)S(1)} %get-tuple-element.198.cur.prev, f32[256,256]{1,0:T(8,128)S(1)} %get-tuple-element.148.k0, ...), custom_call_target="tpu_custom_call" | custom-call | flops 1000 | bytes 5401000 | tf_op jit(solution)/shard_map/adjoint_inner/pallas_call | solution.py:413
  89.5 1.6 %adjoint_inner.9 = (f32[256,256]{1,0:T(8,128)S(1)}, f32[256,256]{1,0:T(8,128)S(1)}) custom-call(s32[8]{0:T(128)S(1)} %stack.32.flags, f32[256,256]{1,0:T(8,128)S(1)} %get-tuple-element.211.cur.prev, f32[256,256]{1,0:T(8,128)S(1)} %get-tuple-element.204.cur.prev, f32[256,256]{1,0:T(8,128)S(1)} %get-tuple-element.148.k0, ...), custom_call_target="tpu_custom_call" | custom-call | flops 1000 | bytes 5401000 | tf_op jit(solution)/shard_map/adjoint_inner/pallas_call | solution.py:413
  95.5 1.6 %adjoint_inner.10 = (f32[256,256]{1,0:T(8,128)S(1)}, f32[256,256]{1,0:T(8,128)S(1)}) custom-call(s32[8]{0:T(128)S(1)} %stack.32.flags, f32[256,256]{1,0:T(8,128)S(1)} %get-tuple-element.218.cur.prev, f32[256,256]{1,0:T(8,128)S(1)} %get-tuple-element.211.cur.prev, f32[256,256]{1,0:T(8,128)S(1)} %get-tuple-element.148.k0, ...), custom_call_target="tpu_custom_call" | custom-call | flops 1000 | bytes 5401000 | tf_op jit(solution)/shard_map/adjoint_inner/pallas_call | solution.py:413
  101.4 1.8 %adjoint_inner.11 = (f32[256,256]{1,0:T(8,128)S(1)}, f32[256,256]{1,0:T(8,128)S(1)}) custom-call(s32[8]{0:T(128)S(1)} %stack.32.flags, f32[256,256]{1,0:T(8,128)S(1)} %get-tuple-element.225.cur.prev, f32[256,256]{1,0:T(8,128)S(1)} %get-tuple-element.218.cur.prev, f32[256,256]{1,0:T(8,128)S(1)} %get-tuple-element.148.k0, ...), custom_call_target="tpu_custom_call" | custom-call | flops 1000 | bytes 5401000 | tf_op jit(solution)/shard_map/adjoint_inner/pallas_call | solution.py:413
  107.4 1.6 %adjoint_inner.12 = (f32[256,256]{1,0:T(8,128)S(1)}, f32[256,256]{1,0:T(8,128)S(1)}) custom-call(s32[8]{0:T(128)S(1)} %stack.32.flags, f32[256,256]{1,0:T(8,128)S(1)} %get-tuple-element.232.cur.prev, f32[256,256]{1,0:T(8,128)S(1)} %get-tuple-element.225.cur.prev, f32[256,256]{1,0:T(8,128)S(1)} %get-tuple-element.148.k0, ...), custom_call_target="tpu_custom_call" | custom-call | flops 1000 | bytes 5401000 | tf_op jit(solution)/shard_map/adjoint_inner/pallas_call | solution.py:413
  112.7 1.6 %adjoint_inner.13 = (f32[256,256]{1,0:T(8,128)S(1)}, f32[256,256]{1,0:T(8,128)S(1)}) custom-call(s32[8]{0:T(128)S(1)} %stack.32.flags, f32[256,256]{1,0:T(8,128)S(1)} %get-tuple-element.249.cur.own, f32[256,256]{1,0:T(8,128)S(1)} %get-tuple-element.232.cur.prev, f32[256,256]{1,0:T(8,128)S(1)} %get-tuple-element.148.k0, ...), custom_call_target="tpu_custom_call" | custom-call | flops 1000 | bytes 5401000 | tf_op jit(solution)/shard_map/adjoint_inner/pallas_call | solution.py:413
  114.3 1.2 collective-permute-start.54
  116.0 3.5 %collective-permute-done.53.ym = f32[32,256]{1,0:T(8,128)S(1)} collective-permute-done((f32[32,256]{1,0:T(8,128)S(1)}, f32[32,256]{1,0:T(8,128)S(1)}, u32[]{:S(2)}, u32[]{:S(2)}) %collective-permute-start.53) | collective-permute-done | bytes 32800 | tf_op jit(solution)/shard_map/ppermute | solution.py:67
  120.6 1.3 collective-permute-start.60
  121.8 1.8 %collective-permute-start.55 = (f32[4,64,128]{2,1,0:T(8,128)S(1)}, f32[4,64,128]{2,1,0:T(8,128)S(1)}, u32[]{:S(2)}, u32[]{:S(2)}) collective-permute-start(f32[4,64,128]{2,1,0:T(8,128)S(1)} %get-tuple-element.251), channel_id=1, source_target_pairs={{0,1},{1,0},{2,3},{3,2},{4,5},{5,4},{6,7},{7,6},{8,9},{9,8},{10,11... | collective-permute-start | bytes 393224 | tf_op jit(solution)/shard_map/ppermute | solution.py:67
  125.2 1.9 %collective-permute-start.56 = (f32[2,64,128]{2,1,0:T(8,128)S(1)}, f32[2,64,128]{2,1,0:T(8,128)S(1)}, u32[]{:S(2)}, u32[]{:S(2)}) collective-permute-start(f32[2,64,128]{2,1,0:T(8,128)S(1)} %get-tuple-element.252), channel_id=1, source_target_pairs={{0,0},{1,2},{2,1},{3,3},{4,4},{5,6},{6,5},{7,7},{8,8},{9,10},{10,9... | collective-permute-start | bytes 196616 | tf_op jit(solution)/shard_map/ppermute | solution.py:67
  127.2 2.2 %collective-permute-start.57 = (f32[2,64,128]{2,1,0:T(8,128)S(1)}, f32[2,64,128]{2,1,0:T(8,128)S(1)}, u32[]{:S(2)}, u32[]{:S(2)}) collective-permute-start(f32[2,64,128]{2,1,0:T(8,128)S(1)} %get-tuple-element.253), channel_id=1, source_target_pairs={{0,4},{1,6},{2,5},{3,7},{4,0},{5,2},{6,1},{7,3},{8,12},{9,14},{10,... | collective-permute-start | bytes 196616 | tf_op jit(solution)/shard_map/ppermute | solution.py:67
  130.2 3.2 %collective-permute-start.59 = (f32[2,64,128]{2,1,0:T(8,128)S(1)}, f32[2,64,128]{2,1,0:T(8,128)S(1)}, u32[]{:S(2)}, u32[]{:S(2)}) collective-permute-start(f32[2,64,128]{2,1,0:T(8,128)S(1)} %get-tuple-element.255), channel_id=1, source_target_pairs={{0,12},{1,14},{2,13},{3,15},{4,8},{5,10},{6,9},{7,11},{8,4},{9,6},... | collective-permute-start | bytes 196616 | tf_op jit(solution)/shard_map/ppermute | solution.py:67
  133.4 1.3 select_previous.1
  134.7 1.3 select_state.1
  136.7 2.0 %filter.1 = f32[32,32,64]{2,1,0:T(8,128)} custom-call(s32[8]{0:T(128)S(1)} %stack.32.flags, f32[2,64,128]{2,1,0:T(8,128)S(1)} %collective-permute-done.56.refs_0_, f32[2,64,128]{2,1,0:T(8,128)S(1)} %collective-permute-done.57.refs_1_, f32[2,64,128]{2,1,0:T(8,128)S(1)} %collective-permute-done.58.refs_2_, f32[2,64,128]{2,1,0:T(8,128)S(1)} %collective-permute-done.59.refs_3_), custom_call_target="tpu_custom_call" | custom-call | flops 1000 | bytes 1000 | tf_op jit(solution)/shard_map/filter/pallas_call | solution.py:413
  (166 shorter events, 57.4 us)
Async XLA Ops:
  0.6 8.5 %collective-permute-start.1 = (f32[256,256]{1,0:T(8,128)}, f32[256,256]{1,0:T(8,128)S(1)}, u32[]{:S(2)}, u32[]{:S(2)}) collective-permute-start(f32[256,256]{1,0:T(8,128)} %bitcast.38), channel_id=1, source_target_pairs={{0,16},{1,2},{2,1},{3,19},{4,20},{5,6},{6,5},{7,23},{8,24},{9,10},... | collective-permute-start | bytes 786440 | tf_op jit(solution)/shard_map/ppermute | solution.py:67
  3.3 7.4 %collective-permute-start = (f32[256,256]{1,0:T(8,128)}, f32[256,256]{1,0:T(8,128)S(1)}, u32[]{:S(2)}, u32[]{:S(2)}) collective-permute-start(f32[256,256]{1,0:T(8,128)} %bitcast.36), channel_id=1, source_target_pairs={{0,16},{1,2},{2,1},{3,19},{4,20},{5,6},{6,5},{7,23},{8,24},{9,10},... | collective-permute-start | bytes 786440 | tf_op jit(solution)/shard_map/ppermute | solution.py:67
  5.3 11.0 %collective-permute-start.2 = (f32[2,256,256]{2,1,0:T(8,128)}, f32[2,256,256]{2,1,0:T(8,128)S(1)}, u32[]{:S(2)}, u32[]{:S(2)}) collective-permute-start(f32[2,256,256]{2,1,0:T(8,128)} %pad_maximum_fusion), channel_id=1, source_target_pairs={{0,16},{1,2},{2,1},{3,19},{4,20},{5,6},{6,5},{7,23},{8,24},{9,10},... | collective-permute-start | bytes 1572872 | tf_op jit(solution)/shard_map/ppermute | solution.py:67
  11.6 8.7 %collective-permute-start.3 = (f32[2,128,256]{2,1,0:T(8,128)S(1)}, f32[2,128,256]{2,1,0:T(8,128)S(1)}, u32[]{:S(2)}, u32[]{:S(2)}) collective-permute-start(f32[2,128,256]{2,1,0:T(8,128)S(1)} %get-tuple-element.134), channel_id=1, source_target_pairs={{0,1},{1,0},{2,3},{3,2},{4,5},{5,4},{6,7},{7,6},{8,9},{9,8},{10,11... | collective-permute-start | bytes 786440 | tf_op jit(solution)/shard_map/ppermute | solution.py:67
  12.1 10.0 %collective-permute-start.4 = (f32[2,128,256]{2,1,0:T(8,128)S(1)}, f32[2,128,256]{2,1,0:T(8,128)S(1)}, u32[]{:S(2)}, u32[]{:S(2)}) collective-permute-start(f32[2,128,256]{2,1,0:T(8,128)S(1)} %get-tuple-element.142), channel_id=1, source_target_pairs={{0,16},{1,4},{2,18},{3,6},{4,1},{5,8},{6,3},{7,10},{8,5},{9,12},{1... | collective-permute-start | bytes 786440 | tf_op jit(solution)/shard_map/ppermute | solution.py:67
  13.9 8.2 %collective-permute-start.6 = (f32[1,9,128]{2,1,0:T(8,128)S(1)}, f32[1,9,128]{2,1,0:T(8,128)S(1)}, u32[]{:S(2)}, u32[]{:S(2)}) collective-permute-start(f32[1,9,128]{2,1,0:T(8,128)S(1)} %maximum_bitcast_fusion.mine), channel_id=1, source_target_pairs={{0,1},{1,0},{2,3},{3,2},{4,5},{5,4},{6,7},{7,6},{8,9},{9,8},{10,11... | collective-permute-start | bytes 13832 | tf_op jit(solution)/shard_map/ppermute | solution.py:67
  14.3 7.8 %collective-permute-start.5 = (f32[2,32,256]{2,1,0:T(8,128)S(1)}, f32[2,32,256]{2,1,0:T(8,128)S(1)}, u32[]{:S(2)}, u32[]{:S(2)}) collective-permute-start(f32[2,32,256]{2,1,0:T(8,128)S(1)} %get-tuple-element.143), channel_id=1, source_target_pairs={{0,2},{1,3},{2,0},{3,1},{4,6},{5,7},{6,4},{7,5},{8,10},{9,11},{10,... | collective-permute-start | bytes 196616 | tf_op jit(solution)/shard_map/ppermute | solution.py:67
  16.3 18.6 %collective-permute-start.14 = (f32[256,256]{1,0:T(8,128)S(1)}, f32[256,256]{1,0:T(8,128)S(1)}, u32[]{:S(2)}, u32[]{:S(2)}) collective-permute-start(f32[256,256]{1,0:T(8,128)S(1)} %bitcast.40), channel_id=1, source_target_pairs={{0,16},{1,2},{2,1},{3,19},{4,20},{5,6},{6,5},{7,23},{8,24},{9,10},... | collective-permute-start | bytes 786440 | tf_op jit(solution)/shard_map/ppermute | solution.py:67
  24.3 5.6 %collective-permute-start.8 = (f32[128,256]{1,0:T(8,128)S(1)}, f32[128,256]{1,0:T(8,128)S(1)}, u32[]{:S(2)}, u32[]{:S(2)}) collective-permute-start(f32[128,256]{1,0:T(8,128)S(1)} %get-tuple-element.154), channel_id=1, source_target_pairs={{0,16},{1,4},{2,18},{3,6},{4,1},{5,8},{6,3},{7,10},{8,5},{9,12},{1... | collective-permute-start | bytes 393224 | tf_op jit(solution)/shard_map/ppermute | solution.py:67
  25.5 11.9 %collective-permute-start.15 = (f32[256,256]{1,0:T(8,128)S(1)}, f32[256,256]{1,0:T(8,128)S(1)}, u32[]{:S(2)}, u32[]{:S(2)}) collective-permute-start(f32[256,256]{1,0:T(8,128)S(1)} %bitcast.42), channel_id=1, source_target_pairs={{0,16},{1,2},{2,1},{3,19},{4,20},{5,6},{6,5},{7,23},{8,24},{9,10},... | collective-permute-start | bytes 786440 | tf_op jit(solution)/shard_map/ppermute | solution.py:67
  25.5 4.4 %collective-permute-start.9 = (f32[32,256]{1,0:T(8,128)S(1)}, f32[32,256]{1,0:T(8,128)S(1)}, u32[]{:S(2)}, u32[]{:S(2)}) collective-permute-start(f32[32,256]{1,0:T(8,128)S(1)} %get-tuple-element.155), channel_id=1, source_target_pairs={{0,2},{1,3},{2,0},{3,1},{4,6},{5,7},{6,4},{7,5},{8,10},{9,11},{10,... | collective-permute-start | bytes 98312 | tf_op jit(solution)/shard_map/ppermute | solution.py:67
  26.2 3.7 %collective-permute-start.10 = (f32[2,9,128]{2,1,0:T(8,128)S(1)}, f32[2,9,128]{2,1,0:T(8,128)S(1)}, u32[]{:S(2)}, u32[]{:S(2)}) collective-permute-start(f32[2,9,128]{2,1,0:T(8,128)S(1)} %get-tuple-element.156.rest_0_), channel_id=1, source_target_pairs={{0,2},{1,3},{2,0},{3,1},{4,6},{5,7},{6,4},{7,5},{8,10},{9,11},{10,... | collective-permute-start | bytes 27656 | tf_op jit(solution)/shard_map/ppermute | solution.py:67
  30.7 7.5 %collective-permute-start.11 = (f32[128,256]{1,0:T(8,128)S(1)}, f32[128,256]{1,0:T(8,128)S(1)}, u32[]{:S(2)}, u32[]{:S(2)}) collective-permute-start(f32[128,256]{1,0:T(8,128)S(1)} %get-tuple-element.158), channel_id=1, source_target_pairs={{0,1},{1,0},{2,3},{3,2},{4,5},{5,4},{6,7},{7,6},{8,9},{9,8},{10,11... | collective-permute-start | bytes 393224 | tf_op jit(solution)/shard_map/ppermute | solution.py:67
  33.6 5.9 %collective-permute-start.12 = (f32[128,256]{1,0:T(8,128)S(1)}, f32[128,256]{1,0:T(8,128)S(1)}, u32[]{:S(2)}, u32[]{:S(2)}) collective-permute-start(f32[128,256]{1,0:T(8,128)S(1)} %get-tuple-element.160), channel_id=1, source_target_pairs={{0,16},{1,4},{2,18},{3,6},{4,1},{5,8},{6,3},{7,10},{8,5},{9,12},{1... | collective-permute-start | bytes 393224 | tf_op jit(solution)/shard_map/ppermute | solution.py:67
  34.9 4.6 %collective-permute-start.13 = (f32[32,256]{1,0:T(8,128)S(1)}, f32[32,256]{1,0:T(8,128)S(1)}, u32[]{:S(2)}, u32[]{:S(2)}) collective-permute-start(f32[32,256]{1,0:T(8,128)S(1)} %get-tuple-element.161), channel_id=1, source_target_pairs={{0,2},{1,3},{2,0},{3,1},{4,6},{5,7},{6,4},{7,5},{8,10},{9,11},{10,... | collective-permute-start | bytes 98312 | tf_op jit(solution)/shard_map/ppermute | solution.py:67
  34.9 4.6 %collective-permute-start.16 = (f32[4,9,128]{2,1,0:T(8,128)S(1)}, f32[4,9,128]{2,1,0:T(8,128)S(1)}, u32[]{:S(2)}, u32[]{:S(2)}) collective-permute-start(f32[4,9,128]{2,1,0:T(8,128)S(1)} %get-tuple-element.165.rest_1_), channel_id=1, source_target_pairs={{0,4},{1,5},{2,6},{3,7},{4,0},{5,1},{6,2},{7,3},{8,12},{9,13},{10,... | collective-permute-start | bytes 55304 | tf_op jit(solution)/shard_map/ppermute | solution.py:67
  40.4 5.2 %collective-permute-start.17 = (f32[2,128,256]{2,1,0:T(8,128)S(1)}, f32[2,128,256]{2,1,0:T(8,128)S(1)}, u32[]{:S(2)}, u32[]{:S(2)}) collective-permute-start(f32[2,128,256]{2,1,0:T(8,128)S(1)} %get-tuple-element.167), channel_id=1, source_target_pairs={{0,1},{1,0},{2,3},{3,2},{4,5},{5,4},{6,7},{7,6},{8,9},{9,8},{10,11... | collective-permute-start | bytes 786440 | tf_op jit(solution)/shard_map/ppermute | solution.py:67
  40.5 8.2 %collective-permute-start.18 = (f32[2,128,256]{2,1,0:T(8,128)S(1)}, f32[2,128,256]{2,1,0:T(8,128)S(1)}, u32[]{:S(2)}, u32[]{:S(2)}) collective-permute-start(f32[2,128,256]{2,1,0:T(8,128)S(1)} %get-tuple-element.169), channel_id=1, source_target_pairs={{0,16},{1,4},{2,18},{3,6},{4,1},{5,8},{6,3},{7,10},{8,5},{9,12},{1... | collective-permute-start | bytes 786440 | tf_op jit(solution)/shard_map/ppermute | solution.py:67
  41.5 7.2 %collective-permute-start.19 = (f32[2,32,256]{2,1,0:T(8,128)S(1)}, f32[2,32,256]{2,1,0:T(8,128)S(1)}, u32[]{:S(2)}, u32[]{:S(2)}) collective-permute-start(f32[2,32,256]{2,1,0:T(8,128)S(1)} %get-tuple-element.170), channel_id=1, source_target_pairs={{0,2},{1,3},{2,0},{3,1},{4,6},{5,7},{6,4},{7,5},{8,10},{9,11},{10,... | collective-permute-start | bytes 196616 | tf_op jit(solution)/shard_map/ppermute | solution.py:67
  43.0 5.7 %collective-permute-start.20 = (f32[8,9,128]{2,1,0:T(8,128)S(1)}, f32[8,9,128]{2,1,0:T(8,128)S(1)}, u32[]{:S(2)}, u32[]{:S(2)}) collective-permute-start(f32[8,9,128]{2,1,0:T(8,128)S(1)} %get-tuple-element.171.rest_0_), channel_id=1, source_target_pairs={{0,8},{1,9},{2,10},{3,11},{4,12},{5,13},{6,14},{7,15},{8,0},{9,1},... | collective-permute-start | bytes 110600 | tf_op jit(solution)/shard_map/ppermute | solution.py:67
  49.5 3.3 %collective-permute-start.21 = (f32[128,256]{1,0:T(8,128)S(1)}, f32[128,256]{1,0:T(8,128)S(1)}, u32[]{:S(2)}, u32[]{:S(2)}) collective-permute-start(f32[128,256]{1,0:T(8,128)S(1)} %get-tuple-element.173), channel_id=1, source_target_pairs={{0,1},{1,0},{2,3},{3,2},{4,5},{5,4},{6,7},{7,6},{8,9},{9,8},{10,11... | collective-permute-start | bytes 393224 | tf_op jit(solution)/shard_map/ppermute | solution.py:67
  51.5 4.7 %collective-permute-start.22 = (f32[128,256]{1,0:T(8,128)S(1)}, f32[128,256]{1,0:T(8,128)S(1)}, u32[]{:S(2)}, u32[]{:S(2)}) collective-permute-start(f32[128,256]{1,0:T(8,128)S(1)} %get-tuple-element.175), channel_id=1, source_target_pairs={{0,16},{1,4},{2,18},{3,6},{4,1},{5,8},{6,3},{7,10},{8,5},{9,12},{1... | collective-permute-start | bytes 393224 | tf_op jit(solution)/shard_map/ppermute | solution.py:67
  52.5 3.2 %collective-permute-start.23 = (f32[32,256]{1,0:T(8,128)S(1)}, f32[32,256]{1,0:T(8,128)S(1)}, u32[]{:S(2)}, u32[]{:S(2)}) collective-permute-start(f32[32,256]{1,0:T(8,128)S(1)} %get-tuple-element.176), channel_id=1, source_target_pairs={{0,2},{1,3},{2,0},{3,1},{4,6},{5,7},{6,4},{7,5},{8,10},{9,11},{10,... | collective-permute-start | bytes 98312 | tf_op jit(solution)/shard_map/ppermute | solution.py:67
  57.4 4.7 %collective-permute-start.25 = (f32[128,256]{1,0:T(8,128)S(1)}, f32[128,256]{1,0:T(8,128)S(1)}, u32[]{:S(2)}, u32[]{:S(2)}) collective-permute-start(f32[128,256]{1,0:T(8,128)S(1)} %get-tuple-element.180), channel_id=1, source_target_pairs={{0,16},{1,4},{2,18},{3,6},{4,1},{5,8},{6,3},{7,10},{8,5},{9,12},{1... | collective-permute-start | bytes 393224 | tf_op jit(solution)/shard_map/ppermute | solution.py:67
  58.2 3.1 %collective-permute-start.26 = (f32[32,256]{1,0:T(8,128)S(1)}, f32[32,256]{1,0:T(8,128)S(1)}, u32[]{:S(2)}, u32[]{:S(2)}) collective-permute-start(f32[32,256]{1,0:T(8,128)S(1)} %get-tuple-element.181), channel_id=1, source_target_pairs={{0,2},{1,3},{2,0},{3,1},{4,6},{5,7},{6,4},{7,5},{8,10},{9,11},{10,... | collective-permute-start | bytes 98312 | tf_op jit(solution)/shard_map/ppermute | solution.py:67
  63.4 4.7 %collective-permute-start.28 = (f32[128,256]{1,0:T(8,128)S(1)}, f32[128,256]{1,0:T(8,128)S(1)}, u32[]{:S(2)}, u32[]{:S(2)}) collective-permute-start(f32[128,256]{1,0:T(8,128)S(1)} %get-tuple-element.185), channel_id=1, source_target_pairs={{0,16},{1,4},{2,18},{3,6},{4,1},{5,8},{6,3},{7,10},{8,5},{9,12},{1... | collective-permute-start | bytes 393224 | tf_op jit(solution)/shard_map/ppermute | solution.py:67
  64.1 3.1 %collective-permute-start.29 = (f32[32,256]{1,0:T(8,128)S(1)}, f32[32,256]{1,0:T(8,128)S(1)}, u32[]{:S(2)}, u32[]{:S(2)}) collective-permute-start(f32[32,256]{1,0:T(8,128)S(1)} %get-tuple-element.186), channel_id=1, source_target_pairs={{0,2},{1,3},{2,0},{3,1},{4,6},{5,7},{6,4},{7,5},{8,10},{9,11},{10,... | collective-permute-start | bytes 98312 | tf_op jit(solution)/shard_map/ppermute | solution.py:67
  68.9 3.5 %collective-permute-start.30 = (f32[128,256]{1,0:T(8,128)S(1)}, f32[128,256]{1,0:T(8,128)S(1)}, u32[]{:S(2)}, u32[]{:S(2)}) collective-permute-start(f32[128,256]{1,0:T(8,128)S(1)} %get-tuple-element.188), channel_id=1, source_target_pairs={{0,1},{1,0},{2,3},{3,2},{4,5},{5,4},{6,7},{7,6},{8,9},{9,8},{10,11... | collective-permute-start | bytes 393224 | tf_op jit(solution)/shard_map/ppermute | solution.py:67
  69.3 4.7 %collective-permute-start.31 = (f32[128,256]{1,0:T(8,128)S(1)}, f32[128,256]{1,0:T(8,128)S(1)}, u32[]{:S(2)}, u32[]{:S(2)}) collective-permute-start(f32[128,256]{1,0:T(8,128)S(1)} %get-tuple-element.190), channel_id=1, source_target_pairs={{0,16},{1,4},{2,18},{3,6},{4,1},{5,8},{6,3},{7,10},{8,5},{9,12},{1... | collective-permute-start | bytes 393224 | tf_op jit(solution)/shard_map/ppermute | solution.py:67
  70.0 3.6 %collective-permute-start.32 = (f32[32,256]{1,0:T(8,128)S(1)}, f32[32,256]{1,0:T(8,128)S(1)}, u32[]{:S(2)}, u32[]{:S(2)}) collective-permute-start(f32[32,256]{1,0:T(8,128)S(1)} %get-tuple-element.191), channel_id=1, source_target_pairs={{0,2},{1,3},{2,0},{3,1},{4,6},{5,7},{6,4},{7,5},{8,10},{9,11},{10,... | collective-permute-start | bytes 98312 | tf_op jit(solution)/shard_map/ppermute | solution.py:67
  76.0 4.7 %collective-permute-start.34 = (f32[128,256]{1,0:T(8,128)S(1)}, f32[128,256]{1,0:T(8,128)S(1)}, u32[]{:S(2)}, u32[]{:S(2)}) collective-permute-start(f32[128,256]{1,0:T(8,128)S(1)} %get-tuple-element.202), channel_id=1, source_target_pairs={{0,16},{1,4},{2,18},{3,6},{4,1},{5,8},{6,3},{7,10},{8,5},{9,12},{1... | collective-permute-start | bytes 393224 | tf_op jit(solution)/shard_map/ppermute | solution.py:67
  76.7 3.1 %collective-permute-start.35 = (f32[32,256]{1,0:T(8,128)S(1)}, f32[32,256]{1,0:T(8,128)S(1)}, u32[]{:S(2)}, u32[]{:S(2)}) collective-permute-start(f32[32,256]{1,0:T(8,128)S(1)} %get-tuple-element.203), channel_id=1, source_target_pairs={{0,2},{1,3},{2,0},{3,1},{4,6},{5,7},{6,4},{7,5},{8,10},{9,11},{10,... | collective-permute-start | bytes 98312 | tf_op jit(solution)/shard_map/ppermute | solution.py:67
  81.9 4.7 %collective-permute-start.37 = (f32[128,256]{1,0:T(8,128)S(1)}, f32[128,256]{1,0:T(8,128)S(1)}, u32[]{:S(2)}, u32[]{:S(2)}) collective-permute-start(f32[128,256]{1,0:T(8,128)S(1)} %get-tuple-element.209), channel_id=1, source_target_pairs={{0,16},{1,4},{2,18},{3,6},{4,1},{5,8},{6,3},{7,10},{8,5},{9,12},{1... | collective-permute-start | bytes 393224 | tf_op jit(solution)/shard_map/ppermute | solution.py:67
  82.6 3.1 %collective-permute-start.38 = (f32[32,256]{1,0:T(8,128)S(1)}, f32[32,256]{1,0:T(8,128)S(1)}, u32[]{:S(2)}, u32[]{:S(2)}) collective-permute-start(f32[32,256]{1,0:T(8,128)S(1)} %get-tuple-element.210), channel_id=1, source_target_pairs={{0,2},{1,3},{2,0},{3,1},{4,6},{5,7},{6,4},{7,5},{8,10},{9,11},{10,... | collective-permute-start | bytes 98312 | tf_op jit(solution)/shard_map/ppermute | solution.py:67
  87.9 4.7 %collective-permute-start.40 = (f32[128,256]{1,0:T(8,128)S(1)}, f32[128,256]{1,0:T(8,128)S(1)}, u32[]{:S(2)}, u32[]{:S(2)}) collective-permute-start(f32[128,256]{1,0:T(8,128)S(1)} %get-tuple-element.216), channel_id=1, source_target_pairs={{0,16},{1,4},{2,18},{3,6},{4,1},{5,8},{6,3},{7,10},{8,5},{9,12},{1... | collective-permute-start | bytes 393224 | tf_op jit(solution)/shard_map/ppermute | solution.py:67
  88.6 3.1 %collective-permute-start.41 = (f32[32,256]{1,0:T(8,128)S(1)}, f32[32,256]{1,0:T(8,128)S(1)}, u32[]{:S(2)}, u32[]{:S(2)}) collective-permute-start(f32[32,256]{1,0:T(8,128)S(1)} %get-tuple-element.217), channel_id=1, source_target_pairs={{0,2},{1,3},{2,0},{3,1},{4,6},{5,7},{6,4},{7,5},{8,10},{9,11},{10,... | collective-permute-start | bytes 98312 | tf_op jit(solution)/shard_map/ppermute | solution.py:67
  93.9 4.7 %collective-permute-start.43 = (f32[128,256]{1,0:T(8,128)S(1)}, f32[128,256]{1,0:T(8,128)S(1)}, u32[]{:S(2)}, u32[]{:S(2)}) collective-permute-start(f32[128,256]{1,0:T(8,128)S(1)} %get-tuple-element.223), channel_id=1, source_target_pairs={{0,16},{1,4},{2,18},{3,6},{4,1},{5,8},{6,3},{7,10},{8,5},{9,12},{1... | collective-permute-start | bytes 393224 | tf_op jit(solution)/shard_map/ppermute | solution.py:67
  94.6 3.1 %collective-permute-start.44 = (f32[32,256]{1,0:T(8,128)S(1)}, f32[32,256]{1,0:T(8,128)S(1)}, u32[]{:S(2)}, u32[]{:S(2)}) collective-permute-start(f32[32,256]{1,0:T(8,128)S(1)} %get-tuple-element.224), channel_id=1, source_target_pairs={{0,2},{1,3},{2,0},{3,1},{4,6},{5,7},{6,4},{7,5},{8,10},{9,11},{10,... | collective-permute-start | bytes 98312 | tf_op jit(solution)/shard_map/ppermute | solution.py:67
  99.8 4.7 %collective-permute-start.46 = (f32[128,256]{1,0:T(8,128)S(1)}, f32[128,256]{1,0:T(8,128)S(1)}, u32[]{:S(2)}, u32[]{:S(2)}) collective-permute-start(f32[128,256]{1,0:T(8,128)S(1)} %get-tuple-element.230), channel_id=1, source_target_pairs={{0,16},{1,4},{2,18},{3,6},{4,1},{5,8},{6,3},{7,10},{8,5},{9,12},{1... | collective-permute-start | bytes 393224 | tf_op jit(solution)/shard_map/ppermute | solution.py:67
  105.8 4.7 %collective-permute-start.49 = (f32[128,256]{1,0:T(8,128)S(1)}, f32[128,256]{1,0:T(8,128)S(1)}, u32[]{:S(2)}, u32[]{:S(2)}) collective-permute-start(f32[128,256]{1,0:T(8,128)S(1)} %get-tuple-element.237), channel_id=1, source_target_pairs={{0,16},{1,4},{2,18},{3,6},{4,1},{5,8},{6,3},{7,10},{8,5},{9,12},{1... | collective-permute-start | bytes 393224 | tf_op jit(solution)/shard_map/ppermute | solution.py:67
  111.8 7.8 %collective-permute-start.52 = (f32[128,256]{1,0:T(8,128)S(1)}, f32[128,256]{1,0:T(8,128)S(1)}, u32[]{:S(2)}, u32[]{:S(2)}) collective-permute-start(f32[128,256]{1,0:T(8,128)S(1)} %get-tuple-element.244), channel_id=1, source_target_pairs={{0,16},{1,4},{2,18},{3,6},{4,1},{5,8},{6,3},{7,10},{8,5},{9,12},{1... | collective-permute-start | bytes 393224 | tf_op jit(solution)/shard_map/ppermute | solution.py:67
  114.3 9.3 %collective-permute-start.54 = (f32[256,256]{1,0:T(8,128)S(1)}, f32[256,256]{1,0:T(8,128)S(1)}, u32[]{:S(2)}, u32[]{:S(2)}) collective-permute-start(f32[256,256]{1,0:T(8,128)S(1)} %get-tuple-element.249.cur.own), channel_id=1, source_target_pairs={{0,16},{1,2},{2,1},{3,19},{4,20},{5,6},{6,5},{7,23},{8,24},{9,10},... | collective-permute-start | bytes 786440 | tf_op jit(solution)/shard_map/ppermute | solution.py:67
  115.5 4.0 %collective-permute-start.53 = (f32[32,256]{1,0:T(8,128)S(1)}, f32[32,256]{1,0:T(8,128)S(1)}, u32[]{:S(2)}, u32[]{:S(2)}) collective-permute-start(f32[32,256]{1,0:T(8,128)S(1)} %get-tuple-element.245), channel_id=1, source_target_pairs={{0,2},{1,3},{2,0},{3,1},{4,6},{5,7},{6,4},{7,5},{8,10},{9,11},{10,... | collective-permute-start | bytes 98312 | tf_op jit(solution)/shard_map/ppermute | solution.py:67
  120.6 14.1 %collective-permute-start.60 = (f32[256,256]{1,0:T(8,128)S(1)}, f32[256,256]{1,0:T(8,128)S(1)}, u32[]{:S(2)}, u32[]{:S(2)}) collective-permute-start(f32[256,256]{1,0:T(8,128)S(1)} %get-tuple-element.256.own), channel_id=1, source_target_pairs={{0,16},{1,2},{2,1},{3,19},{4,20},{5,6},{6,5},{7,23},{8,24},{9,10},... | collective-permute-start | bytes 786440 | tf_op jit(solution)/shard_map/ppermute | solution.py:67
  125.2 10.7 %collective-permute-start.56 = (f32[2,64,128]{2,1,0:T(8,128)S(1)}, f32[2,64,128]{2,1,0:T(8,128)S(1)}, u32[]{:S(2)}, u32[]{:S(2)}) collective-permute-start(f32[2,64,128]{2,1,0:T(8,128)S(1)} %get-tuple-element.252), channel_id=1, source_target_pairs={{0,0},{1,2},{2,1},{3,3},{4,4},{5,6},{6,5},{7,7},{8,8},{9,10},{10,9... | collective-permute-start | bytes 196616 | tf_op jit(solution)/shard_map/ppermute | solution.py:67
  127.2 8.8 %collective-permute-start.57 = (f32[2,64,128]{2,1,0:T(8,128)S(1)}, f32[2,64,128]{2,1,0:T(8,128)S(1)}, u32[]{:S(2)}, u32[]{:S(2)}) collective-permute-start(f32[2,64,128]{2,1,0:T(8,128)S(1)} %get-tuple-element.253), channel_id=1, source_target_pairs={{0,4},{1,6},{2,5},{3,7},{4,0},{5,2},{6,1},{7,3},{8,12},{9,14},{10,... | collective-permute-start | bytes 196616 | tf_op jit(solution)/shard_map/ppermute | solution.py:67
  129.3 6.6 %collective-permute-start.58 = (f32[2,64,128]{2,1,0:T(8,128)S(1)}, f32[2,64,128]{2,1,0:T(8,128)S(1)}, u32[]{:S(2)}, u32[]{:S(2)}) collective-permute-start(f32[2,64,128]{2,1,0:T(8,128)S(1)} %get-tuple-element.254), channel_id=1, source_target_pairs={{0,8},{1,10},{2,9},{3,11},{4,12},{5,14},{6,13},{7,15},{8,0},{9,2},... | collective-permute-start | bytes 196616 | tf_op jit(solution)/shard_map/ppermute | solution.py:67
  130.2 6.5 %collective-permute-start.59 = (f32[2,64,128]{2,1,0:T(8,128)S(1)}, f32[2,64,128]{2,1,0:T(8,128)S(1)}, u32[]{:S(2)}, u32[]{:S(2)}) collective-permute-start(f32[2,64,128]{2,1,0:T(8,128)S(1)} %get-tuple-element.255), channel_id=1, source_target_pairs={{0,12},{1,14},{2,13},{3,15},{4,8},{5,10},{6,9},{7,11},{8,4},{9,6},... | collective-permute-start | bytes 196616 | tf_op jit(solution)/shard_map/ppermute | solution.py:67
  (32 other events, 97.9 us)

commit v7 on v6

--- a/solution.py
+++ b/solution.py
@@ -194,8 +194,8 @@
     choose(flags, [(a, recv.at[0], a_out), (b, recv.at[1], b_out)], sems)
 
 
-def settle_adjoint_kernel(flags, a, b, recv_a, recv_b, a_out, b_out, sems):
-    choose(flags, [(a, recv_a, a_out), (b, recv_b, b_out)], sems)
+def settle_adjoint_kernel(flags, a, recv, out, sems):
+    choose(flags, [(a, recv, out)], sems)
 
 
 def select_kernel(flags, own, recv, out):
@@ -211,9 +211,10 @@
         di_out[here], dx_out[here], dz_out[here] = di, dx, dz
 
 
-def first_outer_kernel(flags, cur, prev, vel, ri, rx, rz, sums, di, dx, dz, inj, zm, ym, side, edge, mine, got, new, zo, co, yo, lists, k0, ki, kx, kz):
+def first_outer_kernel(flags, cur, prev, vel, ri, rx, rz, sums, di, dx, dz, inj, zm, ym, side,
+                       edge, mine, got, new, zo, co, yo, k0, ki, kx, kz, *lists):
     rows = cur.shape[0]
-    merge(0, flags, mine, got, lists)
+    trade(0, flags, mine, got, *lists)
     kz[...] = sums[...]
     ki[...] = di[...]
     here, more, more_i = edge_differences(flags, rows, ym.at[1], edge)
@@ -255,11 +256,20 @@
     new[here] += k0[here] * sums - ki[here] * di
 
 
-def merge(stage, flags, mine, got, out):
-    n = mine.shape[0]
-    bit = flags[4 + stage]
-    out[pl.ds(bit * n, n)] = mine[...]
-    out[pl.ds((1 - bit) * n, n)] = got[...]
+def other_half(stage, flags, count):
+    other = 1 - flags[4 + stage]
+    for n in range(count // 2):
+        high, low = n >> stage, n & ((1 << stage) - 1)
+        yield n, (high << (stage + 1)) + (other << stage) + low
+
+
+def trade(stage, flags, mine, got, out, give=None):
+    out[...] = mine[...]
+    for n, at in other_half(stage, flags, out.shape[0]):
+        out[at] = got[n]
+    if give is not None:
+        for n, at in other_half(stage + 1, flags, out.shape[0]):
+            give[n] = out[at]
 
 
 def source_kernel(step, flags, srow, sz, wave, out):
@@ -283,8 +293,10 @@
     rest = list(rest)
     other = rest.pop(0) if double else None
     if stage is not None:
-        merge(stage, flags, rest.pop(0), rest.pop(0), rest.pop())
-    new, zo, co, yo = rest
+        mine, got, new, zo, co, yo, *lists = rest
+        trade(stage, flags, mine, got, *lists)
+    else:
+        new, zo, co, yo = rest
     outer(flags, part, k0, ki, kx, zm, ym, side, edge, new)
     if double:
         for n, field in enumerate((new, other)):
@@ -296,9 +308,10 @@
 def lists_kernel(flags, lists, spot, pick, at, obs):
     size, n = spot.shape
     depth = at.shape[1]
-    steps = obs.shape[1]
-    sub = flags[2]
-    cell = lists[sub, steps : steps + 1, :]
+    subs, steps = lists.shape[0], obs.shape[1]
+    whole = n // 128
+    cell = jnp.concatenate(
+        [jnp.sum(lists[:, m, :], axis=0, keepdims=True) for m in range(whole)], axis=1)
     along = jnp.floor((cell + 0.5) * (1.0 / depth))
     same = lax.broadcasted_iota(jnp.int32, (n, n), 0) == lax.broadcasted_iota(jnp.int32, (n, n), 1)
 
@@ -311,18 +324,9 @@
     pick[...] = hot.astype(F32).astype(BF16)
     hot = lax.broadcasted_iota(jnp.int32, (n, depth), 1) == column(cell - along * depth)
     at[...] = hot.astype(F32)
-    subs = lists.shape[0]
-    chosen = lax.broadcasted_iota(jnp.int32, (CAP, n), 1) == (
-        sub * CAP + lax.broadcasted_iota(jnp.int32, (CAP, n), 0))
-    chosen = chosen.astype(F32).astype(BF16)
-    traces = lists[:, 0:steps, :].reshape(subs * steps, n)
-    high, mid = split(traces)
-    low = (traces - high.astype(F32) - mid.astype(F32)).astype(BF16)
-    sent = sum(
-        lax.dot_general(chosen, part, (((1,), (1,)), ((), ())), preferred_element_type=F32)
-        for part in (low, mid, high))
-    for s in range(subs):
-        obs[s * CAP : s * CAP + CAP, :] = sent[:, s * steps : s * steps + steps]
+    traces = lists[:, whole, :]
+    for k in range(CAP):
+        obs[k * subs : k * subs + subs, :] = traces[:, k * steps : k * steps + steps]
 
 
 def injection(t, state, spot, pick, at, obs):
@@ -393,13 +397,16 @@
     place = jnp.bitwise_xor(q * (2 * COLS), at - within) + within
     weights = jnp.exp(jnp.abs(y - place).astype(F32) * (-1.0 / SMOOTH))
     weights = split(weights / jnp.sum(weights, axis=0, keepdims=True))
+    ready = []
     for n in range(height // COLS):
         here = slice(n * COLS, n * COLS + COLS)
         lines = jnp.concatenate([piece[b, here, :] for piece in pieces for b in range(2)], axis=0)
         high, low = split(lines.T)
         done = mm(high, weights[0]) + mm(low, weights[0]) + mm(high, weights[1])
-        for g in range(groups):
-            out[:, g * (rows // groups) + n, :] = done[g * chunk : g * chunk + chunk]
+        ready.append(done)
+    for g in range(groups):
+        lines = jnp.stack([done[g * chunk : g * chunk + chunk] for done in ready], axis=0)
+        out[:, g * (rows // groups) : (g + 1) * (rows // groups), :] = jnp.swapaxes(lines, 0, 1)
 
 
 def shaped(*shape):
@@ -471,17 +478,8 @@
     log_density, fwd_now, velocity = flat(log_density), flat(fwd_now), flat(velocity)
     fwd_before, adj_now, adj_before = flat(fwd_before), flat(adj_now), flat(adj_before)
     got = [send(v, swap_perm) for v in (log_density, fwd_now)]
-    got_model = send(jnp.stack([velocity, fwd_before]), swap_perm)
-    density, p_now, *out = call(settle_kernel, "settle",
-                                [field, field] + [shaped(2, *r.shape) for r in rim],
-                                flags, log_density, fwd_now, *got, far=2)
-    zm, cm, ym = halo(*out)
-    got_adjoint = [send(after(v, density), swap_perm) for v in (adj_now, adj_before)]
-    vel, p_before = call(settle_model_kernel, "settle_model", [field, field],
-                         flags, velocity, fwd_before, got_model, weight=0.6, far=2)
-    parts = call(first_inner_kernel, "first_inner", [field] * 7, flags, density, p_now, cm,
-                 near, deep, weight=1.3)
-
+    stacked = jnp.stack([velocity, fwd_before])
+    got_model = send(stacked, swap_perm)
     plane = nx * cols * depth
     src_i = src_cell // plane - y * rows
     src_x = src_cell // depth % (nx * cols) - (2 * q + c) * cols
@@ -490,40 +488,53 @@
     sz = (src_cell % depth)[:, None]
     wave = wavelet.T
 
-    rec_counts, rec_cells, observed = lax.optimization_barrier(
-        (rec_counts, rec_cells, observed, density))[:3]
-    live = jnp.arange(CAP)[None, :] < rec_counts[0][:, None]
-    cells = jnp.where(live.reshape(-1), rec_cells[0], -1)
-    lists = jnp.concatenate([observed, cells[None, :].astype(F32)], axis=0)[None]
-
-    moved = send(lists, stages[0][0])
-
     inj, = call(functools.partial(source_kernel, 0), "source", [field], flags, srow, sz, wave,
                 weight=0.6)
-    grown = shaped(2, *lists.shape[1:])
-    new, zo, co, yo, lists, *model = call(
-        first_outer_kernel, "first_outer", [field] + rim + [grown] + [field] * 4, flags, p_now,
-        p_before, vel, *parts, inj, zm, ym, side, edge, lists, moved)
-    k0, ki, kx, kz = model
+
+    slots = subs * CAP
+    live = jnp.arange(CAP)[None, :] < rec_counts[0][:, None]
+    cells = jnp.where(live, rec_cells[0].reshape(subs, CAP), -1).T.reshape(1, slots).astype(F32)
+    worker = (2 * q + c) * 2 + y
+    cells = jnp.where(jnp.arange(subs)[:, None] == worker, cells, 0.0)
+    traces = observed.reshape(steps, nq, 2, 2, CAP).transpose(1, 3, 2, 4, 0).reshape(subs, CAP * steps)
+    spare = jnp.zeros((subs, 128 - CAP * steps), F32)
+    lists = jnp.concatenate([cells, traces, spare], axis=1).reshape(subs, -1, 128)
+    give = lax.dynamic_index_in_dim(lists.reshape(subs // 2, 2, -1, 128), 1 - c, 1, keepdims=False)
+    give, flags, inj = lax.optimization_barrier((give, flags, inj))
+    got_list = send(give, stages[0][0])
+
+    density, p_now, *out = call(settle_kernel, "settle",
+                                [field, field] + [shaped(2, *r.shape) for r in rim],
+                                flags, log_density, fwd_now, *got, far=2)
+    zm, cm, ym = halo(*out)
+    vel, p_before = call(settle_model_kernel, "settle_model", [field, field],
+                         flags, velocity, fwd_before, got_model, weight=0.6, far=2)
+    parts = call(first_inner_kernel, "first_inner", [field] * 7, flags, density, p_now, cm,
+                 near, deep, weight=1.3)
+
+    entries, half_entries = shaped(*lists.shape), shaped(*give.shape)
+    new, zo, co, yo, k0, ki, kx, kz, lists, give = call(
+        first_outer_kernel, "first_outer", [field] + rim + [field] * 4 + [entries, half_entries],
+        flags, p_now, p_before, vel, *parts, inj, zm, ym, side, edge, lists, got_list)
+    model = (k0, ki, kx, kz)
     states = [p_before, p_now, new]
     changes = []
     zm, cm, ym = halo(zo, co, yo)
-    u_now, u_before = call(settle_adjoint_kernel, "settle_adjoint", [field, field], flags, adj_now,
-                           adj_before, *got_adjoint, weight=0.6, far=2)
-    double = 2
+    double = 3
     for t in range(1, steps):
         cur, prev, before = states[:-4:-1]
         stage = t if t < len(stages) else None
-        extra = [lists, send(lists, stages[t][0])] if stage is not None else []
+        extra = [lists, send(give, stages[t][0])] if stage is not None else []
         part, change = call(
             functools.partial(forward_inner_kernel, t), "forward_inner", [field, field], flags, cur,
             prev, *model, cm, near, deep, srow, sz, wave, before, weight=1.2)
         changes.append(change)
         args = [flags, part, k0, ki, kx, zm, ym, side, edge]
         if t == steps - 1:
+            u_before, = call(settle_adjoint_kernel, "settle_before", [field], flags, adj_before,
+                             got_before, weight=0.6, far=1)
             u_part, = call(adjoint_first_kernel, "adjoint_first", [field], flags, u_now, u_before,
                            *model, u_cm, near, deep, weight=1.1)
-            slots = subs * CAP
             receivers = call(
                 lists_kernel, "lists",
                 [jax.ShapeDtypeStruct((size, slots), BF16),
@@ -534,15 +545,22 @@
                 u_zm, u_ym, *receivers)
             states.append(new)
             break
+        if t == 1:
+            got_now = send(after(adj_now, ym), swap_perm)
+        if t == 4:
+            got_before = send(after(adj_before, ym), swap_perm)
         if t == double:
+            u_now, = call(settle_adjoint_kernel, "settle_adjoint", [field], flags, adj_now, got_now,
+                          weight=0.6, far=1)
             args.append(u_now)
         outs = [field] + ([shaped(2, *r.shape) for r in rim] if t == double else rim)
         if extra:
-            outs = outs + [shaped(2 * lists.shape[0], *lists.shape[1:])]
+            outs = outs + [entries] + ([half_entries] if t + 1 < len(stages) else [])
         new, *out = call(functools.partial(outer_kernel, stage, t == double), "forward_outer", outs,
                          *args, *extra)
         if extra:
-            lists = out.pop()
+            out, (lists, *give) = out[:3], out[3:]
+            give = give[0] if give else None
         states.append(new)
         zm, cm, ym = halo(*out)
         if t == double:
@@ -561,7 +579,7 @@
             u_now, u_before, *model, cm, near, deep, states[t + 2], *receivers, *terms, weight=1.5)
         args = [part, k0, ki, kx, zm, ym, side, edge]
         if j == steps - 1:
-            got_prev = send(after(u_now, part), swap_perm)
+            got_prev = send(after(u_now, ym), swap_perm)
             u_last, mine, other = call(
                 functools.partial(last_kernel, 2.0 / steps), "last", [field, half, half],
                 flags, *args, *image, changes[0], vel)
@@ -574,7 +592,7 @@
     got = send(u_last, swap_perm)
     pieces = call(join_kernel, "join", [shaped(2, *half.shape[1:])] * nq, flags,
                   after(mine, got_prev), send(other, c_perm))
-    pieces = [send(value, plan.spread(s)) for s, value in enumerate(pieces)]
+    pieces = [send(pieces[s], plan.spread(s)) for s in reversed(range(nq))][::-1]
     adj_prev, = call(select_kernel, "select_previous", [field], flags, u_now, got_prev, weight=0.6)
     adj_out, = call(select_kernel, "select_state", [field], flags, u_last, got, weight=0.6)
     gradient, = call(filter_kernel, "filter", [shaped(chunk, rows, nx * cols)], flags, *pieces)

time: 139 us -> 140 us (level)
  other arithmetic: 4.26 us -> 1.79 us
  local copies, waits for them, and re-layouts: 1.45 us -> 3.25 us
  starting transfers between devices: 59.4 us -> 61 us
    ppermute x61, starting transfers between devices: 59.4 us -> 61 us  [send(): return lax.ppermute(value, ALL, pairs)]
    pallas_call x40 -> x41, Pallas kernels: 44.6 us -> 45.5 us  [call(): pl.pallas_call(kernel, name=name, out_shape=outs, in_specs=specs, out_spe...]
  transfers between devices with their start and end apart: 61 -> 61, of which waited for: 27 -> 29; matrix products, arithmetic and copies ran while one was open for 3% -> 1% of each run, Pallas kernels for 23% -> 23%
where the time goes in v7:
time: 140 us
  starting transfers between devices  61 us (44%)
  Pallas kernels  45.5 us (32%)
  waiting for transfers between devices  27 us (19%)
  local copies, waits for them, and re-layouts  3.25 us (2%)
  other arithmetic  1.79 us (1%)
    ppermute x61, starting transfers between devices, send(): return lax.ppermute(value, ALL, pairs)  61 us
    pallas_call x41, Pallas kernels, call(): pl.pallas_call(kernel, name=name, out_shape=outs, in_specs=specs, out_spe...  45.5 us
    ppermute x61, waiting for transfers between devices, send(): return lax.ppermute(value, ALL, pairs)  27 us
  transfers between devices with their start and end apart: 61, of which 29 were waited for; matrix products, arithmetic and copies ran while one was open for 1% of the time, Pallas kernels for 23%

profile of v7, /device:TPU:1, one launch (start us, length us, event | category | flops | bytes accessed | tf_op | source)
XLA Modules:
  0.0 139.8 jit_solution(14325438537571257615)
XLA Ops:
  4.5 2.6 %collective-permute-start.1 = (f32[256,256]{1,0:T(8,128)}, f32[256,256]{1,0:T(8,128)S(1)}, u32[]{:S(2)}, u32[]{:S(2)}) collective-permute-start(f32[256,256]{1,0:T(8,128)} %bitcast.43), channel_id=1, source_target_pairs={{0,16},{1,2},{2,1},{3,19},{4,20},{5,6},{6,5},{7,23},{8,24},{9,10},... | collective-permute-start | bytes 786440 | tf_op jit(solution)/shard_map/ppermute | solution.py:67
  8.1 1.7 %collective-permute-start.2 = (f32[2,256,256]{2,1,0:T(8,128)}, f32[2,256,256]{2,1,0:T(8,128)S(1)}, u32[]{:S(2)}, u32[]{:S(2)}) collective-permute-start(f32[2,256,256]{2,1,0:T(8,128)} %pad_maximum_fusion), channel_id=1, source_target_pairs={{0,16},{1,2},{2,1},{3,19},{4,20},{5,6},{6,5},{7,23},{8,24},{9,10},... | collective-permute-start | bytes 1572872 | tf_op jit(solution)/shard_map/ppermute | solution.py:67
  10.6 1.1 collective-permute-done.1.recv_b
  11.7 2.8 %collective-permute-done.recv_a = f32[256,256]{1,0:T(8,128)S(1)} collective-permute-done((f32[256,256]{1,0:T(8,128)S(1)}, f32[256,256]{1,0:T(8,128)S(1)}, u32[]{:S(2)}, u32[]{:S(2)}) %collective-permute-start) | collective-permute-done | bytes 262176 | tf_op jit(solution)/shard_map/ppermute | solution.py:67
  14.5 1.4 settle.1
  16.3 1.9 %collective-permute-start.4 = (f32[2,128,256]{2,1,0:T(8,128)S(1)}, f32[2,128,256]{2,1,0:T(8,128)S(1)}, u32[]{:S(2)}, u32[]{:S(2)}) collective-permute-start(f32[2,128,256]{2,1,0:T(8,128)S(1)} %get-tuple-element.145), channel_id=1, source_target_pairs={{0,16},{1,4},{2,18},{3,6},{4,1},{5,8},{6,3},{7,10},{8,5},{9,12},{1... | collective-permute-start | bytes 786440 | tf_op jit(solution)/shard_map/ppermute | solution.py:67
  21.2 1.3 first_inner.1
  24.5 1.5 %collective-permute-start.8 = (f32[128,256]{1,0:T(8,128)S(1)}, f32[128,256]{1,0:T(8,128)S(1)}, u32[]{:S(2)}, u32[]{:S(2)}) collective-permute-start(f32[128,256]{1,0:T(8,128)S(1)} %get-tuple-element.155), channel_id=1, source_target_pairs={{0,16},{1,4},{2,18},{3,6},{4,1},{5,8},{6,3},{7,10},{8,5},{9,12},{1... | collective-permute-start | bytes 393224 | tf_op jit(solution)/shard_map/ppermute | solution.py:67
  27.4 1.2 forward_inner.7
  30.0 2.2 %collective-permute-start.11 = (f32[128,256]{1,0:T(8,128)S(1)}, f32[128,256]{1,0:T(8,128)S(1)}, u32[]{:S(2)}, u32[]{:S(2)}) collective-permute-start(f32[128,256]{1,0:T(8,128)S(1)} %get-tuple-element.160), channel_id=1, source_target_pairs={{0,1},{1,0},{2,3},{3,2},{4,5},{5,4},{6,7},{7,6},{8,9},{9,8},{10,11... | collective-permute-start | bytes 393224 | tf_op jit(solution)/shard_map/ppermute | solution.py:67
  33.1 1.2 collective-permute-start.13
  34.3 1.6 %collective-permute-start.14 = (f32[8,2,128]{2,1,0:T(2,128)S(1)}, f32[8,2,128]{2,1,0:T(2,128)S(1)}, u32[]{:S(2)}, u32[]{:S(2)}) collective-permute-start(f32[8,2,128]{2,1,0:T(2,128)S(1)} %get-tuple-element.165), channel_id=1, source_target_pairs={{0,4},{1,5},{2,6},{3,7},{4,0},{5,1},{6,2},{7,3},{8,12},{9,13},{10,... | collective-permute-start | bytes 24584 | tf_op jit(solution)/shard_map/ppermute | solution.py:67
  35.9 1.2 forward_inner.8
  38.1 2.3 %collective-permute-start.15 = (f32[128,256]{1,0:T(8,128)S(1)}, f32[128,256]{1,0:T(8,128)S(1)}, u32[]{:S(2)}, u32[]{:S(2)}) collective-permute-start(f32[128,256]{1,0:T(8,128)S(1)} %get-tuple-element.167), channel_id=1, source_target_pairs={{0,1},{1,0},{2,3},{3,2},{4,5},{5,4},{6,7},{7,6},{8,9},{9,8},{10,11... | collective-permute-start | bytes 393224 | tf_op jit(solution)/shard_map/ppermute | solution.py:67
  40.4 1.2 collective-permute-start.16
  41.8 1.7 %collective-permute-start.19 = (f32[8,2,128]{2,1,0:T(2,128)S(1)}, f32[8,2,128]{2,1,0:T(2,128)S(1)}, u32[]{:S(2)}, u32[]{:S(2)}) collective-permute-start(f32[8,2,128]{2,1,0:T(2,128)S(1)} %get-tuple-element.173), channel_id=1, source_target_pairs={{0,8},{1,9},{2,10},{3,11},{4,12},{5,13},{6,14},{7,15},{8,0},{9,1},... | collective-permute-start | bytes 24584 | tf_op jit(solution)/shard_map/ppermute | solution.py:67
  44.1 1.2 forward_inner.9
  46.2 1.7 %collective-permute-start.20 = (f32[2,128,256]{2,1,0:T(8,128)S(1)}, f32[2,128,256]{2,1,0:T(8,128)S(1)}, u32[]{:S(2)}, u32[]{:S(2)}) collective-permute-start(f32[2,128,256]{2,1,0:T(8,128)S(1)} %get-tuple-element.175), channel_id=1, source_target_pairs={{0,1},{1,0},{2,3},{3,2},{4,5},{5,4},{6,7},{7,6},{8,9},{9,8},{10,11... | collective-permute-start | bytes 786440 | tf_op jit(solution)/shard_map/ppermute | solution.py:67
  49.5 1.2 forward_inner.10
  50.8 1.8 %collective-permute-done.22.ym.u_ym = f32[2,32,256]{2,1,0:T(8,128)S(1)} collective-permute-done((f32[2,32,256]{2,1,0:T(8,128)S(1)}, f32[2,32,256]{2,1,0:T(8,128)S(1)}, u32[]{:S(2)}, u32[]{:S(2)}) %collective-permute-start.22) | collective-permute-done | bytes 65568 | tf_op jit(solution)/shard_map/ppermute | solution.py:67
  52.5 1.4 %collective-permute-done.21.zm.u_zm = f32[2,128,256]{2,1,0:T(8,128)S(1)} collective-permute-done((f32[2,128,256]{2,1,0:T(8,128)S(1)}, f32[2,128,256]{2,1,0:T(8,128)S(1)}, u32[]{:S(2)}, u32[]{:S(2)}) %collective-permute-start.21) | collective-permute-done | bytes 262176 | tf_op jit(solution)/shard_map/ppermute | solution.py:67
  56.6 1.2 forward_inner.11
  61.2 1.3 collective-permute-start.32
  63.7 1.2 forward_inner.12
  64.9 1.6 %collective-permute-done.28.ym = f32[32,256]{1,0:T(8,128)S(1)} collective-permute-done((f32[32,256]{1,0:T(8,128)S(1)}, f32[32,256]{1,0:T(8,128)S(1)}, u32[]{:S(2)}, u32[]{:S(2)}) %collective-permute-start.28) | collective-permute-done | bytes 32800 | tf_op jit(solution)/shard_map/ppermute | solution.py:67
  68.0 2.0 %collective-permute-start.29 = (f32[128,256]{1,0:T(8,128)S(1)}, f32[128,256]{1,0:T(8,128)S(1)}, u32[]{:S(2)}, u32[]{:S(2)}) collective-permute-start(f32[128,256]{1,0:T(8,128)S(1)} %get-tuple-element.190), channel_id=1, source_target_pairs={{0,1},{1,0},{2,3},{3,2},{4,5},{5,4},{6,7},{7,6},{8,9},{9,8},{10,11... | collective-permute-start | bytes 393224 | tf_op jit(solution)/shard_map/ppermute | solution.py:67
  71.8 1.1 adjoint_first.1.u_part
  73.0 1.2 forward_inner.13
  74.7 1.5 %turn.1 = (f32[256,256]{1,0:T(8,128)S(1)}, f32[256,256]{1,0:T(8,128)S(1)}, f32[128,256]{1,0:T(8,128)S(1)}, f32[128,256]{1,0:T(8,128)S(1)}, f32[32,256]{1,0:T(8,128)S(1)}) custom-call(s32[8]{0:T(128)S(1)} %stack.32.flags, f32[256,256]{1,0:T(8,128)S(1)} %get-tuple-element.191.part, f32[256,256]{1,0:T(8,128)S(1)} %get-tuple-element.149.k0, ...), custom_call_target="tpu_custom_call" | custom-call | flops 1000 | bytes 1000 | tf_op jit(solution)/shard_map/turn/pallas_call | solution.py:420
  77.9 1.1 collective-permute-start.35
  79.0 1.7 %adjoint_inner.7 = (f32[256,256]{1,0:T(8,128)S(1)}, f32[256,256]{1,0:T(8,128)S(1)}) custom-call(s32[8]{0:T(128)S(1)} %stack.32.flags, f32[256,256]{1,0:T(8,128)S(1)} %get-tuple-element.200.cur.prev, f32[256,256]{1,0:T(8,128)S(1)} %settle_adjoint.1.rest_0_.cur.prev, f32[256,256]{1,0:T(8,128)S(1)} %get-tuple-element.149.k0, ...), custom_call_target="tpu_custom_call" | custom-call | flops 1000 | bytes 5401000 | tf_op jit(solution)/shard_map/adjoint_inner/pallas_call | solution.py:420
  84.9 1.6 %adjoint_inner.8 = (f32[256,256]{1,0:T(8,128)S(1)}, f32[256,256]{1,0:T(8,128)S(1)}) custom-call(s32[8]{0:T(128)S(1)} %stack.32.flags, f32[256,256]{1,0:T(8,128)S(1)} %get-tuple-element.206.cur.prev, f32[256,256]{1,0:T(8,128)S(1)} %get-tuple-element.200.cur.prev, f32[256,256]{1,0:T(8,128)S(1)} %get-tuple-element.149.k0, ...), custom_call_target="tpu_custom_call" | custom-call | flops 1000 | bytes 5401000 | tf_op jit(solution)/shard_map/adjoint_inner/pallas_call | solution.py:420
  90.8 1.6 %adjoint_inner.9 = (f32[256,256]{1,0:T(8,128)S(1)}, f32[256,256]{1,0:T(8,128)S(1)}) custom-call(s32[8]{0:T(128)S(1)} %stack.32.flags, f32[256,256]{1,0:T(8,128)S(1)} %get-tuple-element.213.cur.prev, f32[256,256]{1,0:T(8,128)S(1)} %get-tuple-element.206.cur.prev, f32[256,256]{1,0:T(8,128)S(1)} %get-tuple-element.149.k0, ...), custom_call_target="tpu_custom_call" | custom-call | flops 1000 | bytes 5401000 | tf_op jit(solution)/shard_map/adjoint_inner/pallas_call | solution.py:420
  95.7 1.1 collective-permute-start.44
  96.8 1.6 %adjoint_inner.10 = (f32[256,256]{1,0:T(8,128)S(1)}, f32[256,256]{1,0:T(8,128)S(1)}) custom-call(s32[8]{0:T(128)S(1)} %stack.32.flags, f32[256,256]{1,0:T(8,128)S(1)} %get-tuple-element.220.cur.prev, f32[256,256]{1,0:T(8,128)S(1)} %get-tuple-element.213.cur.prev, f32[256,256]{1,0:T(8,128)S(1)} %get-tuple-element.149.k0, ...), custom_call_target="tpu_custom_call" | custom-call | flops 1000 | bytes 5401000 | tf_op jit(solution)/shard_map/adjoint_inner/pallas_call | solution.py:420
  102.7 1.6 %adjoint_inner.11 = (f32[256,256]{1,0:T(8,128)S(1)}, f32[256,256]{1,0:T(8,128)S(1)}) custom-call(s32[8]{0:T(128)S(1)} %stack.32.flags, f32[256,256]{1,0:T(8,128)S(1)} %get-tuple-element.227.cur.prev, f32[256,256]{1,0:T(8,128)S(1)} %get-tuple-element.220.cur.prev, f32[256,256]{1,0:T(8,128)S(1)} %get-tuple-element.149.k0, ...), custom_call_target="tpu_custom_call" | custom-call | flops 1000 | bytes 5401000 | tf_op jit(solution)/shard_map/adjoint_inner/pallas_call | solution.py:420
  108.7 1.6 %adjoint_inner.12 = (f32[256,256]{1,0:T(8,128)S(1)}, f32[256,256]{1,0:T(8,128)S(1)}) custom-call(s32[8]{0:T(128)S(1)} %stack.32.flags, f32[256,256]{1,0:T(8,128)S(1)} %get-tuple-element.234.cur.prev, f32[256,256]{1,0:T(8,128)S(1)} %get-tuple-element.227.cur.prev, f32[256,256]{1,0:T(8,128)S(1)} %get-tuple-element.149.k0, ...), custom_call_target="tpu_custom_call" | custom-call | flops 1000 | bytes 5401000 | tf_op jit(solution)/shard_map/adjoint_inner/pallas_call | solution.py:420
  114.7 2.0 %collective-permute-done.53.ym = f32[32,256]{1,0:T(8,128)S(1)} collective-permute-done((f32[32,256]{1,0:T(8,128)S(1)}, f32[32,256]{1,0:T(8,128)S(1)}, u32[]{:S(2)}, u32[]{:S(2)}) %collective-permute-start.53) | collective-permute-done | bytes 32800 | tf_op jit(solution)/shard_map/ppermute | solution.py:67
  116.6 2.3 %collective-permute-start.54 = (f32[256,256]{1,0:T(8,128)S(1)}, f32[256,256]{1,0:T(8,128)S(1)}, u32[]{:S(2)}, u32[]{:S(2)}) collective-permute-start(f32[256,256]{1,0:T(8,128)S(1)} %get-tuple-element.251.cur.own), channel_id=1, source_target_pairs={{0,16},{1,2},{2,1},{3,19},{4,20},{5,6},{6,5},{7,23},{8,24},{9,10},... | collective-permute-start | bytes 786440 | tf_op jit(solution)/shard_map/ppermute | solution.py:67
  118.9 1.6 %adjoint_inner.13 = (f32[256,256]{1,0:T(8,128)S(1)}, f32[256,256]{1,0:T(8,128)S(1)}) custom-call(s32[8]{0:T(128)S(1)} %stack.32.flags, f32[256,256]{1,0:T(8,128)S(1)} %get-tuple-element.251.cur.own, f32[256,256]{1,0:T(8,128)S(1)} %get-tuple-element.234.cur.prev, f32[256,256]{1,0:T(8,128)S(1)} %get-tuple-element.149.k0, ...), custom_call_target="tpu_custom_call" | custom-call | flops 1000 | bytes 5401000 | tf_op jit(solution)/shard_map/adjoint_inner/pallas_call | solution.py:420
  124.2 3.0 %collective-permute-start.56 = (f32[2,64,128]{2,1,0:T(8,128)S(1)}, f32[2,64,128]{2,1,0:T(8,128)S(1)}, u32[]{:S(2)}, u32[]{:S(2)}) collective-permute-start(f32[2,64,128]{2,1,0:T(8,128)S(1)} %get-tuple-element.254), channel_id=1, source_target_pairs={{0,0},{1,2},{2,1},{3,3},{4,4},{5,6},{6,5},{7,7},{8,8},{9,10},{10,9... | collective-permute-start | bytes 196616 | tf_op jit(solution)/shard_map/ppermute | solution.py:67
  127.2 1.2 collective-permute-start.57
  128.4 1.9 %collective-permute-start.58 = (f32[2,64,128]{2,1,0:T(8,128)S(1)}, f32[2,64,128]{2,1,0:T(8,128)S(1)}, u32[]{:S(2)}, u32[]{:S(2)}) collective-permute-start(f32[2,64,128]{2,1,0:T(8,128)S(1)} %get-tuple-element.256), channel_id=1, source_target_pairs={{0,8},{1,10},{2,9},{3,11},{4,12},{5,14},{6,13},{7,15},{8,0},{9,2},... | collective-permute-start | bytes 196616 | tf_op jit(solution)/shard_map/ppermute | solution.py:67
  130.3 2.1 %collective-permute-start.59 = (f32[2,64,128]{2,1,0:T(8,128)S(1)}, f32[2,64,128]{2,1,0:T(8,128)S(1)}, u32[]{:S(2)}, u32[]{:S(2)}) collective-permute-start(f32[2,64,128]{2,1,0:T(8,128)S(1)} %get-tuple-element.257), channel_id=1, source_target_pairs={{0,12},{1,14},{2,13},{3,15},{4,8},{5,10},{6,9},{7,11},{8,4},{9,6},... | collective-permute-start | bytes 196616 | tf_op jit(solution)/shard_map/ppermute | solution.py:67
  132.4 1.3 select_previous.1
  134.6 2.1 %collective-permute-done.59.refs_3_ = f32[2,64,128]{2,1,0:T(8,128)S(1)} collective-permute-done((f32[2,64,128]{2,1,0:T(8,128)S(1)}, f32[2,64,128]{2,1,0:T(8,128)S(1)}, u32[]{:S(2)}, u32[]{:S(2)}) %collective-permute-start.59) | collective-permute-done | bytes 65568 | tf_op jit(solution)/shard_map/ppermute | solution.py:67
  136.7 1.8 %filter.1 = f32[32,32,64]{2,1,0:T(8,128)} custom-call(s32[8]{0:T(128)S(1)} %stack.32.flags, f32[2,64,128]{2,1,0:T(8,128)S(1)} %collective-permute-done.56.refs_0_, f32[2,64,128]{2,1,0:T(8,128)S(1)} %collective-permute-done.57.refs_1_, f32[2,64,128]{2,1,0:T(8,128)S(1)} %collective-permute-done.58.refs_2_, f32[2,64,128]{2,1,0:T(8,128)S(1)} %collective-permute-done.59.refs_3_), custom_call_target="tpu_custom_call" | custom-call | flops 1000 | bytes 1000 | tf_op jit(solution)/shard_map/filter/pallas_call | solution.py:420
  138.5 1.3 select_state.1
  (180 shorter events, 60.7 us)
Async XLA Ops:
  4.4 18.2 %collective-permute-start.6 = (f32[8,2,128]{2,1,0:T(2,128)S(1)}, f32[8,2,128]{2,1,0:T(2,128)S(1)}, u32[]{:S(2)}, u32[]{:S(2)}) collective-permute-start(f32[8,2,128]{2,1,0:T(2,128)S(1)} %dynamic-slice_bitcast_fusion), channel_id=1, source_target_pairs={{0,1},{1,0},{2,3},{3,2},{4,5},{5,4},{6,7},{7,6},{8,9},{9,8},{10,11... | collective-permute-start | bytes 24584 | tf_op jit(solution)/shard_map/ppermute | solution.py:67
  4.5 7.2 %collective-permute-start.1 = (f32[256,256]{1,0:T(8,128)}, f32[256,256]{1,0:T(8,128)S(1)}, u32[]{:S(2)}, u32[]{:S(2)}) collective-permute-start(f32[256,256]{1,0:T(8,128)} %bitcast.43), channel_id=1, source_target_pairs={{0,16},{1,2},{2,1},{3,19},{4,20},{5,6},{6,5},{7,23},{8,24},{9,10},... | collective-permute-start | bytes 786440 | tf_op jit(solution)/shard_map/ppermute | solution.py:67
  7.1 7.4 %collective-permute-start = (f32[256,256]{1,0:T(8,128)S(1)}, f32[256,256]{1,0:T(8,128)S(1)}, u32[]{:S(2)}, u32[]{:S(2)}) collective-permute-start(f32[256,256]{1,0:T(8,128)S(1)} %bitcast.41), channel_id=1, source_target_pairs={{0,16},{1,2},{2,1},{3,19},{4,20},{5,6},{6,5},{7,23},{8,24},{9,10},... | collective-permute-start | bytes 786440 | tf_op jit(solution)/shard_map/ppermute | solution.py:67
  8.1 12.0 %collective-permute-start.2 = (f32[2,256,256]{2,1,0:T(8,128)}, f32[2,256,256]{2,1,0:T(8,128)S(1)}, u32[]{:S(2)}, u32[]{:S(2)}) collective-permute-start(f32[2,256,256]{2,1,0:T(8,128)} %pad_maximum_fusion), channel_id=1, source_target_pairs={{0,16},{1,2},{2,1},{3,19},{4,20},{5,6},{6,5},{7,23},{8,24},{9,10},... | collective-permute-start | bytes 1572872 | tf_op jit(solution)/shard_map/ppermute | solution.py:67
  15.9 4.8 %collective-permute-start.3 = (f32[2,128,256]{2,1,0:T(8,128)}, f32[2,128,256]{2,1,0:T(8,128)S(1)}, u32[]{:S(2)}, u32[]{:S(2)}) collective-permute-start(f32[2,128,256]{2,1,0:T(8,128)} %get-tuple-element.136), channel_id=1, source_target_pairs={{0,1},{1,0},{2,3},{3,2},{4,5},{5,4},{6,7},{7,6},{8,9},{9,8},{10,11... | collective-permute-start | bytes 786440 | tf_op jit(solution)/shard_map/ppermute | solution.py:67
  16.3 6.2 %collective-permute-start.4 = (f32[2,128,256]{2,1,0:T(8,128)S(1)}, f32[2,128,256]{2,1,0:T(8,128)S(1)}, u32[]{:S(2)}, u32[]{:S(2)}) collective-permute-start(f32[2,128,256]{2,1,0:T(8,128)S(1)} %get-tuple-element.145), channel_id=1, source_target_pairs={{0,16},{1,4},{2,18},{3,6},{4,1},{5,8},{6,3},{7,10},{8,5},{9,12},{1... | collective-permute-start | bytes 786440 | tf_op jit(solution)/shard_map/ppermute | solution.py:67
  18.3 4.2 %collective-permute-start.5 = (f32[2,32,256]{2,1,0:T(8,128)S(1)}, f32[2,32,256]{2,1,0:T(8,128)S(1)}, u32[]{:S(2)}, u32[]{:S(2)}) collective-permute-start(f32[2,32,256]{2,1,0:T(8,128)S(1)} %get-tuple-element.146), channel_id=1, source_target_pairs={{0,2},{1,3},{2,0},{3,1},{4,6},{5,7},{6,4},{7,5},{8,10},{9,11},{10,... | collective-permute-start | bytes 196616 | tf_op jit(solution)/shard_map/ppermute | solution.py:67
  23.6 3.8 %collective-permute-start.7 = (f32[128,256]{1,0:T(8,128)S(1)}, f32[128,256]{1,0:T(8,128)S(1)}, u32[]{:S(2)}, u32[]{:S(2)}) collective-permute-start(f32[128,256]{1,0:T(8,128)S(1)} %get-tuple-element.153), channel_id=1, source_target_pairs={{0,1},{1,0},{2,3},{3,2},{4,5},{5,4},{6,7},{7,6},{8,9},{9,8},{10,11... | collective-permute-start | bytes 393224 | tf_op jit(solution)/shard_map/ppermute | solution.py:67
  24.5 4.7 %collective-permute-start.8 = (f32[128,256]{1,0:T(8,128)S(1)}, f32[128,256]{1,0:T(8,128)S(1)}, u32[]{:S(2)}, u32[]{:S(2)}) collective-permute-start(f32[128,256]{1,0:T(8,128)S(1)} %get-tuple-element.155), channel_id=1, source_target_pairs={{0,16},{1,4},{2,18},{3,6},{4,1},{5,8},{6,3},{7,10},{8,5},{9,12},{1... | collective-permute-start | bytes 393224 | tf_op jit(solution)/shard_map/ppermute | solution.py:67
  25.9 3.2 %collective-permute-start.9 = (f32[32,256]{1,0:T(8,128)S(1)}, f32[32,256]{1,0:T(8,128)S(1)}, u32[]{:S(2)}, u32[]{:S(2)}) collective-permute-start(f32[32,256]{1,0:T(8,128)S(1)} %get-tuple-element.156), channel_id=1, source_target_pairs={{0,2},{1,3},{2,0},{3,1},{4,6},{5,7},{6,4},{7,5},{8,10},{9,11},{10,... | collective-permute-start | bytes 98312 | tf_op jit(solution)/shard_map/ppermute | solution.py:67
  30.0 6.0 %collective-permute-start.11 = (f32[128,256]{1,0:T(8,128)S(1)}, f32[128,256]{1,0:T(8,128)S(1)}, u32[]{:S(2)}, u32[]{:S(2)}) collective-permute-start(f32[128,256]{1,0:T(8,128)S(1)} %get-tuple-element.160), channel_id=1, source_target_pairs={{0,1},{1,0},{2,3},{3,2},{4,5},{5,4},{6,7},{7,6},{8,9},{9,8},{10,11... | collective-permute-start | bytes 393224 | tf_op jit(solution)/shard_map/ppermute | solution.py:67
  32.2 5.1 %collective-permute-start.12 = (f32[128,256]{1,0:T(8,128)S(1)}, f32[128,256]{1,0:T(8,128)S(1)}, u32[]{:S(2)}, u32[]{:S(2)}) collective-permute-start(f32[128,256]{1,0:T(8,128)S(1)} %get-tuple-element.162), channel_id=1, source_target_pairs={{0,16},{1,4},{2,18},{3,6},{4,1},{5,8},{6,3},{7,10},{8,5},{9,12},{1... | collective-permute-start | bytes 393224 | tf_op jit(solution)/shard_map/ppermute | solution.py:67
  32.3 11.1 %collective-permute-start.18 = (f32[256,256]{1,0:T(8,128)S(1)}, f32[256,256]{1,0:T(8,128)S(1)}, u32[]{:S(2)}, u32[]{:S(2)}) collective-permute-start(f32[256,256]{1,0:T(8,128)S(1)} %bitcast.45), channel_id=1, source_target_pairs={{0,16},{1,2},{2,1},{3,19},{4,20},{5,6},{6,5},{7,23},{8,24},{9,10},... | collective-permute-start | bytes 786440 | tf_op jit(solution)/shard_map/ppermute | solution.py:67
  33.1 4.1 %collective-permute-start.13 = (f32[32,256]{1,0:T(8,128)S(1)}, f32[32,256]{1,0:T(8,128)S(1)}, u32[]{:S(2)}, u32[]{:S(2)}) collective-permute-start(f32[32,256]{1,0:T(8,128)S(1)} %get-tuple-element.163), channel_id=1, source_target_pairs={{0,2},{1,3},{2,0},{3,1},{4,6},{5,7},{6,4},{7,5},{8,10},{9,11},{10,... | collective-permute-start | bytes 98312 | tf_op jit(solution)/shard_map/ppermute | solution.py:67
  38.1 6.0 %collective-permute-start.15 = (f32[128,256]{1,0:T(8,128)S(1)}, f32[128,256]{1,0:T(8,128)S(1)}, u32[]{:S(2)}, u32[]{:S(2)}) collective-permute-start(f32[128,256]{1,0:T(8,128)S(1)} %get-tuple-element.167), channel_id=1, source_target_pairs={{0,1},{1,0},{2,3},{3,2},{4,5},{5,4},{6,7},{7,6},{8,9},{9,8},{10,11... | collective-permute-start | bytes 393224 | tf_op jit(solution)/shard_map/ppermute | solution.py:67
  40.4 4.9 %collective-permute-start.16 = (f32[128,256]{1,0:T(8,128)S(1)}, f32[128,256]{1,0:T(8,128)S(1)}, u32[]{:S(2)}, u32[]{:S(2)}) collective-permute-start(f32[128,256]{1,0:T(8,128)S(1)} %get-tuple-element.169), channel_id=1, source_target_pairs={{0,16},{1,4},{2,18},{3,6},{4,1},{5,8},{6,3},{7,10},{8,5},{9,12},{1... | collective-permute-start | bytes 393224 | tf_op jit(solution)/shard_map/ppermute | solution.py:67
  41.6 3.7 %collective-permute-start.17 = (f32[32,256]{1,0:T(8,128)S(1)}, f32[32,256]{1,0:T(8,128)S(1)}, u32[]{:S(2)}, u32[]{:S(2)}) collective-permute-start(f32[32,256]{1,0:T(8,128)S(1)} %get-tuple-element.170), channel_id=1, source_target_pairs={{0,2},{1,3},{2,0},{3,1},{4,6},{5,7},{6,4},{7,5},{8,10},{9,11},{10,... | collective-permute-start | bytes 98312 | tf_op jit(solution)/shard_map/ppermute | solution.py:67
  41.8 3.5 %collective-permute-start.19 = (f32[8,2,128]{2,1,0:T(2,128)S(1)}, f32[8,2,128]{2,1,0:T(2,128)S(1)}, u32[]{:S(2)}, u32[]{:S(2)}) collective-permute-start(f32[8,2,128]{2,1,0:T(2,128)S(1)} %get-tuple-element.173), channel_id=1, source_target_pairs={{0,8},{1,9},{2,10},{3,11},{4,12},{5,13},{6,14},{7,15},{8,0},{9,1},... | collective-permute-start | bytes 24584 | tf_op jit(solution)/shard_map/ppermute | solution.py:67
  46.2 3.3 %collective-permute-start.20 = (f32[2,128,256]{2,1,0:T(8,128)S(1)}, f32[2,128,256]{2,1,0:T(8,128)S(1)}, u32[]{:S(2)}, u32[]{:S(2)}) collective-permute-start(f32[2,128,256]{2,1,0:T(8,128)S(1)} %get-tuple-element.175), channel_id=1, source_target_pairs={{0,1},{1,0},{2,3},{3,2},{4,5},{5,4},{6,7},{7,6},{8,9},{9,8},{10,11... | collective-permute-start | bytes 786440 | tf_op jit(solution)/shard_map/ppermute | solution.py:67
  47.9 6.1 %collective-permute-start.21 = (f32[2,128,256]{2,1,0:T(8,128)S(1)}, f32[2,128,256]{2,1,0:T(8,128)S(1)}, u32[]{:S(2)}, u32[]{:S(2)}) collective-permute-start(f32[2,128,256]{2,1,0:T(8,128)S(1)} %get-tuple-element.177), channel_id=1, source_target_pairs={{0,16},{1,4},{2,18},{3,6},{4,1},{5,8},{6,3},{7,10},{8,5},{9,12},{1... | collective-permute-start | bytes 786440 | tf_op jit(solution)/shard_map/ppermute | solution.py:67
  48.8 3.7 %collective-permute-start.22 = (f32[2,32,256]{2,1,0:T(8,128)S(1)}, f32[2,32,256]{2,1,0:T(8,128)S(1)}, u32[]{:S(2)}, u32[]{:S(2)}) collective-permute-start(f32[2,32,256]{2,1,0:T(8,128)S(1)} %get-tuple-element.178), channel_id=1, source_target_pairs={{0,2},{1,3},{2,0},{3,1},{4,6},{5,7},{6,4},{7,5},{8,10},{9,11},{10,... | collective-permute-start | bytes 196616 | tf_op jit(solution)/shard_map/ppermute | solution.py:67
  55.3 4.7 %collective-permute-start.24 = (f32[128,256]{1,0:T(8,128)S(1)}, f32[128,256]{1,0:T(8,128)S(1)}, u32[]{:S(2)}, u32[]{:S(2)}) collective-permute-start(f32[128,256]{1,0:T(8,128)S(1)} %get-tuple-element.182), channel_id=1, source_target_pairs={{0,16},{1,4},{2,18},{3,6},{4,1},{5,8},{6,3},{7,10},{8,5},{9,12},{1... | collective-permute-start | bytes 393224 | tf_op jit(solution)/shard_map/ppermute | solution.py:67
  55.9 3.1 %collective-permute-start.25 = (f32[32,256]{1,0:T(8,128)S(1)}, f32[32,256]{1,0:T(8,128)S(1)}, u32[]{:S(2)}, u32[]{:S(2)}) collective-permute-start(f32[32,256]{1,0:T(8,128)S(1)} %get-tuple-element.183), channel_id=1, source_target_pairs={{0,2},{1,3},{2,0},{3,1},{4,6},{5,7},{6,4},{7,5},{8,10},{9,11},{10,... | collective-permute-start | bytes 98312 | tf_op jit(solution)/shard_map/ppermute | solution.py:67
  61.2 9.2 %collective-permute-start.32 = (f32[256,256]{1,0:T(8,128)S(1)}, f32[256,256]{1,0:T(8,128)S(1)}, u32[]{:S(2)}, u32[]{:S(2)}) collective-permute-start(f32[256,256]{1,0:T(8,128)S(1)} %bitcast.47), channel_id=1, source_target_pairs={{0,16},{1,2},{2,1},{3,19},{4,20},{5,6},{6,5},{7,23},{8,24},{9,10},... | collective-permute-start | bytes 786440 | tf_op jit(solution)/shard_map/ppermute | solution.py:67
  62.5 4.7 %collective-permute-start.27 = (f32[128,256]{1,0:T(8,128)S(1)}, f32[128,256]{1,0:T(8,128)S(1)}, u32[]{:S(2)}, u32[]{:S(2)}) collective-permute-start(f32[128,256]{1,0:T(8,128)S(1)} %get-tuple-element.187), channel_id=1, source_target_pairs={{0,16},{1,4},{2,18},{3,6},{4,1},{5,8},{6,3},{7,10},{8,5},{9,12},{1... | collective-permute-start | bytes 393224 | tf_op jit(solution)/shard_map/ppermute | solution.py:67
  62.7 3.8 %collective-permute-start.28 = (f32[32,256]{1,0:T(8,128)S(1)}, f32[32,256]{1,0:T(8,128)S(1)}, u32[]{:S(2)}, u32[]{:S(2)}) collective-permute-start(f32[32,256]{1,0:T(8,128)S(1)} %get-tuple-element.188), channel_id=1, source_target_pairs={{0,2},{1,3},{2,0},{3,1},{4,6},{5,7},{6,4},{7,5},{8,10},{9,11},{10,... | collective-permute-start | bytes 98312 | tf_op jit(solution)/shard_map/ppermute | solution.py:67
  68.0 4.9 %collective-permute-start.29 = (f32[128,256]{1,0:T(8,128)S(1)}, f32[128,256]{1,0:T(8,128)S(1)}, u32[]{:S(2)}, u32[]{:S(2)}) collective-permute-start(f32[128,256]{1,0:T(8,128)S(1)} %get-tuple-element.190), channel_id=1, source_target_pairs={{0,1},{1,0},{2,3},{3,2},{4,5},{5,4},{6,7},{7,6},{8,9},{9,8},{10,11... | collective-permute-start | bytes 393224 | tf_op jit(solution)/shard_map/ppermute | solution.py:67
  70.0 4.7 %collective-permute-start.30 = (f32[128,256]{1,0:T(8,128)S(1)}, f32[128,256]{1,0:T(8,128)S(1)}, u32[]{:S(2)}, u32[]{:S(2)}) collective-permute-start(f32[128,256]{1,0:T(8,128)S(1)} %get-tuple-element.192), channel_id=1, source_target_pairs={{0,16},{1,4},{2,18},{3,6},{4,1},{5,8},{6,3},{7,10},{8,5},{9,12},{1... | collective-permute-start | bytes 393224 | tf_op jit(solution)/shard_map/ppermute | solution.py:67
  70.0 4.2 %collective-permute-start.31 = (f32[32,256]{1,0:T(8,128)S(1)}, f32[32,256]{1,0:T(8,128)S(1)}, u32[]{:S(2)}, u32[]{:S(2)}) collective-permute-start(f32[32,256]{1,0:T(8,128)S(1)} %get-tuple-element.193), channel_id=1, source_target_pairs={{0,2},{1,3},{2,0},{3,1},{4,6},{5,7},{6,4},{7,5},{8,10},{9,11},{10,... | collective-permute-start | bytes 98312 | tf_op jit(solution)/shard_map/ppermute | solution.py:67
  77.1 4.7 %collective-permute-start.34 = (f32[128,256]{1,0:T(8,128)S(1)}, f32[128,256]{1,0:T(8,128)S(1)}, u32[]{:S(2)}, u32[]{:S(2)}) collective-permute-start(f32[128,256]{1,0:T(8,128)S(1)} %get-tuple-element.204), channel_id=1, source_target_pairs={{0,16},{1,4},{2,18},{3,6},{4,1},{5,8},{6,3},{7,10},{8,5},{9,12},{1... | collective-permute-start | bytes 393224 | tf_op jit(solution)/shard_map/ppermute | solution.py:67
  77.9 3.1 %collective-permute-start.35 = (f32[32,256]{1,0:T(8,128)S(1)}, f32[32,256]{1,0:T(8,128)S(1)}, u32[]{:S(2)}, u32[]{:S(2)}) collective-permute-start(f32[32,256]{1,0:T(8,128)S(1)} %get-tuple-element.205), channel_id=1, source_target_pairs={{0,2},{1,3},{2,0},{3,1},{4,6},{5,7},{6,4},{7,5},{8,10},{9,11},{10,... | collective-permute-start | bytes 98312 | tf_op jit(solution)/shard_map/ppermute | solution.py:67
  83.1 4.7 %collective-permute-start.37 = (f32[128,256]{1,0:T(8,128)S(1)}, f32[128,256]{1,0:T(8,128)S(1)}, u32[]{:S(2)}, u32[]{:S(2)}) collective-permute-start(f32[128,256]{1,0:T(8,128)S(1)} %get-tuple-element.211), channel_id=1, source_target_pairs={{0,16},{1,4},{2,18},{3,6},{4,1},{5,8},{6,3},{7,10},{8,5},{9,12},{1... | collective-permute-start | bytes 393224 | tf_op jit(solution)/shard_map/ppermute | solution.py:67
  83.8 3.1 %collective-permute-start.38 = (f32[32,256]{1,0:T(8,128)S(1)}, f32[32,256]{1,0:T(8,128)S(1)}, u32[]{:S(2)}, u32[]{:S(2)}) collective-permute-start(f32[32,256]{1,0:T(8,128)S(1)} %get-tuple-element.212), channel_id=1, source_target_pairs={{0,2},{1,3},{2,0},{3,1},{4,6},{5,7},{6,4},{7,5},{8,10},{9,11},{10,... | collective-permute-start | bytes 98312 | tf_op jit(solution)/shard_map/ppermute | solution.py:67
  89.0 4.7 %collective-permute-start.40 = (f32[128,256]{1,0:T(8,128)S(1)}, f32[128,256]{1,0:T(8,128)S(1)}, u32[]{:S(2)}, u32[]{:S(2)}) collective-permute-start(f32[128,256]{1,0:T(8,128)S(1)} %get-tuple-element.218), channel_id=1, source_target_pairs={{0,16},{1,4},{2,18},{3,6},{4,1},{5,8},{6,3},{7,10},{8,5},{9,12},{1... | collective-permute-start | bytes 393224 | tf_op jit(solution)/shard_map/ppermute | solution.py:67
  89.7 3.1 %collective-permute-start.41 = (f32[32,256]{1,0:T(8,128)S(1)}, f32[32,256]{1,0:T(8,128)S(1)}, u32[]{:S(2)}, u32[]{:S(2)}) collective-permute-start(f32[32,256]{1,0:T(8,128)S(1)} %get-tuple-element.219), channel_id=1, source_target_pairs={{0,2},{1,3},{2,0},{3,1},{4,6},{5,7},{6,4},{7,5},{8,10},{9,11},{10,... | collective-permute-start | bytes 98312 | tf_op jit(solution)/shard_map/ppermute | solution.py:67
  95.0 4.7 %collective-permute-start.43 = (f32[128,256]{1,0:T(8,128)S(1)}, f32[128,256]{1,0:T(8,128)S(1)}, u32[]{:S(2)}, u32[]{:S(2)}) collective-permute-start(f32[128,256]{1,0:T(8,128)S(1)} %get-tuple-element.225), channel_id=1, source_target_pairs={{0,16},{1,4},{2,18},{3,6},{4,1},{5,8},{6,3},{7,10},{8,5},{9,12},{1... | collective-permute-start | bytes 393224 | tf_op jit(solution)/shard_map/ppermute | solution.py:67
  95.7 3.1 %collective-permute-start.44 = (f32[32,256]{1,0:T(8,128)S(1)}, f32[32,256]{1,0:T(8,128)S(1)}, u32[]{:S(2)}, u32[]{:S(2)}) collective-permute-start(f32[32,256]{1,0:T(8,128)S(1)} %get-tuple-element.226), channel_id=1, source_target_pairs={{0,2},{1,3},{2,0},{3,1},{4,6},{5,7},{6,4},{7,5},{8,10},{9,11},{10,... | collective-permute-start | bytes 98312 | tf_op jit(solution)/shard_map/ppermute | solution.py:67
  100.9 4.7 %collective-permute-start.46 = (f32[128,256]{1,0:T(8,128)S(1)}, f32[128,256]{1,0:T(8,128)S(1)}, u32[]{:S(2)}, u32[]{:S(2)}) collective-permute-start(f32[128,256]{1,0:T(8,128)S(1)} %get-tuple-element.232), channel_id=1, source_target_pairs={{0,16},{1,4},{2,18},{3,6},{4,1},{5,8},{6,3},{7,10},{8,5},{9,12},{1... | collective-permute-start | bytes 393224 | tf_op jit(solution)/shard_map/ppermute | solution.py:67
  101.6 3.1 %collective-permute-start.47 = (f32[32,256]{1,0:T(8,128)S(1)}, f32[32,256]{1,0:T(8,128)S(1)}, u32[]{:S(2)}, u32[]{:S(2)}) collective-permute-start(f32[32,256]{1,0:T(8,128)S(1)} %get-tuple-element.233), channel_id=1, source_target_pairs={{0,2},{1,3},{2,0},{3,1},{4,6},{5,7},{6,4},{7,5},{8,10},{9,11},{10,... | collective-permute-start | bytes 98312 | tf_op jit(solution)/shard_map/ppermute | solution.py:67
  106.9 4.7 %collective-permute-start.49 = (f32[128,256]{1,0:T(8,128)S(1)}, f32[128,256]{1,0:T(8,128)S(1)}, u32[]{:S(2)}, u32[]{:S(2)}) collective-permute-start(f32[128,256]{1,0:T(8,128)S(1)} %get-tuple-element.239), channel_id=1, source_target_pairs={{0,16},{1,4},{2,18},{3,6},{4,1},{5,8},{6,3},{7,10},{8,5},{9,12},{1... | collective-permute-start | bytes 393224 | tf_op jit(solution)/shard_map/ppermute | solution.py:67
  112.4 6.5 %collective-permute-start.51 = (f32[128,256]{1,0:T(8,128)S(1)}, f32[128,256]{1,0:T(8,128)S(1)}, u32[]{:S(2)}, u32[]{:S(2)}) collective-permute-start(f32[128,256]{1,0:T(8,128)S(1)} %get-tuple-element.242), channel_id=1, source_target_pairs={{0,1},{1,0},{2,3},{3,2},{4,5},{5,4},{6,7},{7,6},{8,9},{9,8},{10,11... | collective-permute-start | bytes 393224 | tf_op jit(solution)/shard_map/ppermute | solution.py:67
  112.9 7.6 %collective-permute-start.52 = (f32[128,256]{1,0:T(8,128)S(1)}, f32[128,256]{1,0:T(8,128)S(1)}, u32[]{:S(2)}, u32[]{:S(2)}) collective-permute-start(f32[128,256]{1,0:T(8,128)S(1)} %get-tuple-element.246), channel_id=1, source_target_pairs={{0,16},{1,4},{2,18},{3,6},{4,1},{5,8},{6,3},{7,10},{8,5},{9,12},{1... | collective-permute-start | bytes 393224 | tf_op jit(solution)/shard_map/ppermute | solution.py:67
  116.6 6.6 %collective-permute-start.54 = (f32[256,256]{1,0:T(8,128)S(1)}, f32[256,256]{1,0:T(8,128)S(1)}, u32[]{:S(2)}, u32[]{:S(2)}) collective-permute-start(f32[256,256]{1,0:T(8,128)S(1)} %get-tuple-element.251.cur.own), channel_id=1, source_target_pairs={{0,16},{1,2},{2,1},{3,19},{4,20},{5,6},{6,5},{7,23},{8,24},{9,10},... | collective-permute-start | bytes 786440 | tf_op jit(solution)/shard_map/ppermute | solution.py:67
  121.6 17.0 %collective-permute-start.60 = (f32[256,256]{1,0:T(8,128)S(1)}, f32[256,256]{1,0:T(8,128)S(1)}, u32[]{:S(2)}, u32[]{:S(2)}) collective-permute-start(f32[256,256]{1,0:T(8,128)S(1)} %get-tuple-element.258.own), channel_id=1, source_target_pairs={{0,16},{1,2},{2,1},{3,19},{4,20},{5,6},{6,5},{7,23},{8,24},{9,10},... | collective-permute-start | bytes 786440 | tf_op jit(solution)/shard_map/ppermute | solution.py:67
  124.2 9.4 %collective-permute-start.56 = (f32[2,64,128]{2,1,0:T(8,128)S(1)}, f32[2,64,128]{2,1,0:T(8,128)S(1)}, u32[]{:S(2)}, u32[]{:S(2)}) collective-permute-start(f32[2,64,128]{2,1,0:T(8,128)S(1)} %get-tuple-element.254), channel_id=1, source_target_pairs={{0,0},{1,2},{2,1},{3,3},{4,4},{5,6},{6,5},{7,7},{8,8},{9,10},{10,9... | collective-permute-start | bytes 196616 | tf_op jit(solution)/shard_map/ppermute | solution.py:67
  127.2 6.5 %collective-permute-start.57 = (f32[2,64,128]{2,1,0:T(8,128)S(1)}, f32[2,64,128]{2,1,0:T(8,128)S(1)}, u32[]{:S(2)}, u32[]{:S(2)}) collective-permute-start(f32[2,64,128]{2,1,0:T(8,128)S(1)} %get-tuple-element.255), channel_id=1, source_target_pairs={{0,4},{1,6},{2,5},{3,7},{4,0},{5,2},{6,1},{7,3},{8,12},{9,14},{10,... | collective-permute-start | bytes 196616 | tf_op jit(solution)/shard_map/ppermute | solution.py:67
  128.4 6.2 %collective-permute-start.58 = (f32[2,64,128]{2,1,0:T(8,128)S(1)}, f32[2,64,128]{2,1,0:T(8,128)S(1)}, u32[]{:S(2)}, u32[]{:S(2)}) collective-permute-start(f32[2,64,128]{2,1,0:T(8,128)S(1)} %get-tuple-element.256), channel_id=1, source_target_pairs={{0,8},{1,10},{2,9},{3,11},{4,12},{5,14},{6,13},{7,15},{8,0},{9,2},... | collective-permute-start | bytes 196616 | tf_op jit(solution)/shard_map/ppermute | solution.py:67
  130.3 6.4 %collective-permute-start.59 = (f32[2,64,128]{2,1,0:T(8,128)S(1)}, f32[2,64,128]{2,1,0:T(8,128)S(1)}, u32[]{:S(2)}, u32[]{:S(2)}) collective-permute-start(f32[2,64,128]{2,1,0:T(8,128)S(1)} %get-tuple-element.257), channel_id=1, source_target_pairs={{0,12},{1,14},{2,13},{3,15},{4,8},{5,10},{6,9},{7,11},{8,4},{9,6},... | collective-permute-start | bytes 196616 | tf_op jit(solution)/shard_map/ppermute | solution.py:67
  (32 other events, 92.4 us)

commit v8 on v7

--- a/solution.py
+++ b/solution.py
@@ -190,16 +190,14 @@
         rims(flags, out, zo.at[n], co.at[n], yo.at[n])
 
 
-def settle_model_kernel(flags, a, b, recv, a_out, b_out, sems):
+def settle_pair_kernel(flags, a, b, recv, a_out, b_out, sems):
     choose(flags, [(a, recv.at[0], a_out), (b, recv.at[1], b_out)], sems)
 
 
-def settle_adjoint_kernel(flags, a, recv, out, sems):
-    choose(flags, [(a, recv, out)], sems)
-
-
-def select_kernel(flags, own, recv, out):
-    out[...] = jnp.where(flags[0] == flags[1], own[...], recv[...])
+def select_kernel(flags, own, recv, *outs):
+    keep = flags[0] == flags[1]
+    for n, out in enumerate(outs):
+        out[...] = jnp.where(keep, own[n], recv[n])
 
 
 def first_inner_kernel(flags, lr, cur, cm, near, deep, *outs):
@@ -361,7 +359,9 @@
 
 
 def last_kernel(scale, flags, part, k0, ki, kx, zm, ym, side, edge, image, change, vel,
-                new, mine, other):
+                prev, states, mine, other):
+    new = states.at[1]
+    states[0] = prev[...]
     outer(flags, part, k0, ki, kx, zm, ym, side, edge, new)
     raw = (image[...] + new[...] * change[...]) * scale / vel[...]
     count, height, lanes = mine.shape
@@ -488,10 +488,9 @@
     sz = (src_cell % depth)[:, None]
     wave = wavelet.T
 
-    inj, = call(functools.partial(source_kernel, 0), "source", [field], flags, srow, sz, wave,
-                weight=0.6)
-
     slots = subs * CAP
+    rec_counts, rec_cells, observed = lax.optimization_barrier(
+        (rec_counts, rec_cells, observed, stacked))[:3]
     live = jnp.arange(CAP)[None, :] < rec_counts[0][:, None]
     cells = jnp.where(live, rec_cells[0].reshape(subs, CAP), -1).T.reshape(1, slots).astype(F32)
     worker = (2 * q + c) * 2 + y
@@ -500,6 +499,8 @@
     spare = jnp.zeros((subs, 128 - CAP * steps), F32)
     lists = jnp.concatenate([cells, traces, spare], axis=1).reshape(subs, -1, 128)
     give = lax.dynamic_index_in_dim(lists.reshape(subs // 2, 2, -1, 128), 1 - c, 1, keepdims=False)
+    inj, = call(functools.partial(source_kernel, 0), "source", [field], after(flags, stacked), srow,
+                sz, wave, weight=0.6)
     give, flags, inj = lax.optimization_barrier((give, flags, inj))
     got_list = send(give, stages[0][0])
 
@@ -507,7 +508,8 @@
                                 [field, field] + [shaped(2, *r.shape) for r in rim],
                                 flags, log_density, fwd_now, *got, far=2)
     zm, cm, ym = halo(*out)
-    vel, p_before = call(settle_model_kernel, "settle_model", [field, field],
+    got_adjoint = send(jnp.stack([after(adj_now, density), after(adj_before, density)]), swap_perm)
+    vel, p_before = call(settle_pair_kernel, "settle_model", [field, field],
                          flags, velocity, fwd_before, got_model, weight=0.6, far=2)
     parts = call(first_inner_kernel, "first_inner", [field] * 7, flags, density, p_now, cm,
                  near, deep, weight=1.3)
@@ -520,7 +522,7 @@
     states = [p_before, p_now, new]
     changes = []
     zm, cm, ym = halo(zo, co, yo)
-    double = 3
+    double = 1
     for t in range(1, steps):
         cur, prev, before = states[:-4:-1]
         stage = t if t < len(stages) else None
@@ -531,8 +533,6 @@
         changes.append(change)
         args = [flags, part, k0, ki, kx, zm, ym, side, edge]
         if t == steps - 1:
-            u_before, = call(settle_adjoint_kernel, "settle_before", [field], flags, adj_before,
-                             got_before, weight=0.6, far=1)
             u_part, = call(adjoint_first_kernel, "adjoint_first", [field], flags, u_now, u_before,
                            *model, u_cm, near, deep, weight=1.1)
             receivers = call(
@@ -545,13 +545,9 @@
                 u_zm, u_ym, *receivers)
             states.append(new)
             break
-        if t == 1:
-            got_now = send(after(adj_now, ym), swap_perm)
-        if t == 4:
-            got_before = send(after(adj_before, ym), swap_perm)
         if t == double:
-            u_now, = call(settle_adjoint_kernel, "settle_adjoint", [field], flags, adj_now, got_now,
-                          weight=0.6, far=1)
+            u_now, u_before = call(settle_pair_kernel, "settle_adjoint", [field, field], flags,
+                                   adj_now, adj_before, got_adjoint, weight=0.6, far=2)
             args.append(u_now)
         outs = [field] + ([shaped(2, *r.shape) for r in rim] if t == double else rim)
         if extra:
@@ -579,23 +575,22 @@
             u_now, u_before, *model, cm, near, deep, states[t + 2], *receivers, *terms, weight=1.5)
         args = [part, k0, ki, kx, zm, ym, side, edge]
         if j == steps - 1:
-            got_prev = send(after(u_now, ym), swap_perm)
-            u_last, mine, other = call(
-                functools.partial(last_kernel, 2.0 / steps), "last", [field, half, half],
-                flags, *args, *image, changes[0], vel)
+            final, mine, other = call(
+                functools.partial(last_kernel, 2.0 / steps), "last",
+                [shaped(2, *field.shape), half, half], flags, *args, *image, changes[0], vel, u_now)
             break
         u_before = u_now
         u_now, *out = call(functools.partial(outer_kernel, None, False), "adjoint_outer", [field] + rim,
                            flags, *args)
         zm, cm, ym = halo(*out)
 
-    got = send(u_last, swap_perm)
-    pieces = call(join_kernel, "join", [shaped(2, *half.shape[1:])] * nq, flags,
-                  after(mine, got_prev), send(other, c_perm))
+    got = send(final, swap_perm)
+    pieces = call(join_kernel, "join", [shaped(2, *half.shape[1:])] * nq, flags, mine,
+                  send(other, c_perm))
     pieces = [send(pieces[s], plan.spread(s)) for s in reversed(range(nq))][::-1]
-    adj_prev, = call(select_kernel, "select_previous", [field], flags, u_now, got_prev, weight=0.6)
-    adj_out, = call(select_kernel, "select_state", [field], flags, u_last, got, weight=0.6)
-    gradient, = call(filter_kernel, "filter", [shaped(chunk, rows, nx * cols)], flags, *pieces)
+    adj_prev, adj_out = call(select_kernel, "select", [field, field], flags, final, got, weight=1.2)
+    gradient, = call(filter_kernel, "filter", [shaped(chunk, rows, nx * cols)],
+                     after(flags, adj_out), *pieces)
     block = (rows, cols, depth)
     return gradient, adj_out.reshape(block), adj_prev.reshape(block)
 

time: 140 us -> 136 us (0.971)
  starting transfers between devices: 61 us -> 51.9 us
  other arithmetic: 1.79 us -> 4.4 us
  local copies, waits for them, and re-layouts: 3.25 us -> 5.17 us
    ppermute x61 -> x59, starting transfers between devices: 61 us -> 51.9 us  [send(): return lax.ppermute(value, ALL, pairs)]
    ppermute x61 -> x59, waiting for transfers between devices: 27 us -> 28.1 us  [send(): return lax.ppermute(value, ALL, pairs)]
    pallas_call x41 -> x39, Pallas kernels: 45.5 us -> 44.4 us  [call(): pl.pallas_call(kernel, name=name, out_shape=outs, in_specs=specs, out_spe...]
    unnamed x40 -> x41, local copies, waits for them, and re-layouts: 2.4 us -> 3.15 us
  transfers between devices with their start and end apart: 61 -> 59, of which waited for: 29 -> 31; matrix products, arithmetic and copies ran while one was open for 1% -> 5% of each run, Pallas kernels for 23% -> 22%
where the time goes in v8:
time: 136 us; the launch traced here: 135 us
  starting transfers between devices  51.9 us (38%)
  Pallas kernels  44.4 us (33%)
  waiting for transfers between devices  28.1 us (21%)
  local copies, waits for them, and re-layouts  5.17 us (4%)
  other arithmetic  4.4 us (3%)
    ppermute x59, starting transfers between devices, send(): return lax.ppermute(value, ALL, pairs)  51.9 us
    pallas_call x39, Pallas kernels, call(): pl.pallas_call(kernel, name=name, out_shape=outs, in_specs=specs, out_spe...  44.4 us
    ppermute x59, waiting for transfers between devices, send(): return lax.ppermute(value, ALL, pairs)  28.1 us
    unnamed x41, local copies, waits for them, and re-layouts  3.15 us
  transfers between devices with their start and end apart: 59, of which 31 were waited for; matrix products, arithmetic and copies ran while one was open for 5% of the time, Pallas kernels for 22%

profile of v8, /device:TPU:1, one launch (start us, length us, event | category | flops | bytes accessed | tf_op | source)
XLA Modules:
  0.0 135.3 jit_solution(9558738316100023509)
XLA Ops:
  0.6 2.7 %collective-permute-start.1 = (f32[256,256]{1,0:T(8,128)}, f32[256,256]{1,0:T(8,128)S(1)}, u32[]{:S(2)}, u32[]{:S(2)}) collective-permute-start(f32[256,256]{1,0:T(8,128)} %bitcast.49), channel_id=1, source_target_pairs={{0,16},{1,2},{2,1},{3,19},{4,20},{5,6},{6,5},{7,23},{8,24},{9,10},... | collective-permute-start | bytes 786440 | tf_op jit(solution)/shard_map/ppermute | solution.py:67
  3.4 1.9 %pad_maximum_fusion = f32[2,256,256]{2,1,0:T(8,128)} fusion(f32[1,256,256]{2,1,0:T(8,128)} %bitcast.33, f32[1,256,256]{2,1,0:T(8,128)} %bitcast.31), kind=kLoop, calls=%fused_computation | loop fusion | flops 131072 | bytes 1048576 | tf_op jit(solution)/shard_map/stack | solution.py:481
  5.3 1.7 %collective-permute-start.2 = (f32[2,256,256]{2,1,0:T(8,128)}, f32[2,256,256]{2,1,0:T(8,128)S(1)}, u32[]{:S(2)}, u32[]{:S(2)}) collective-permute-start(f32[2,256,256]{2,1,0:T(8,128)} %pad_maximum_fusion), channel_id=1, source_target_pairs={{0,16},{1,2},{2,1},{3,19},{4,20},{5,6},{6,5},{7,23},{8,24},{9,10},... | collective-permute-start | bytes 1572872 | tf_op jit(solution)/shard_map/ppermute | solution.py:67
  14.8 1.4 %settle.1 = (f32[256,256]{1,0:T(8,128)S(1)}, f32[256,256]{1,0:T(8,128)S(1)}, f32[2,128,256]{2,1,0:T(8,128)}, f32[2,128,256]{2,1,0:T(8,128)}, f32[2,32,256]{2,1,0:T(8,128)S(1)}) custom-call(s32[8]{0:T(128)S(1)} %stack.42.flags, f32[256,256]{1,0:T(8,128)S(1)} %bitcast.48, f32[256,256]{1,0:T(8,128)S(1)} %bitcast.50, ...), custom_call_target="tpu_custom_call" | custom-call | flops 1000 | bytes 1000 | tf_op jit(solution)/shard_map/settle/pallas_call | solution.py:420
  16.4 1.6 %collective-permute-start.4 = (f32[2,128,256]{2,1,0:T(8,128)}, f32[2,128,256]{2,1,0:T(8,128)}, u32[]{:S(2)}, u32[]{:S(2)}) collective-permute-start(f32[2,128,256]{2,1,0:T(8,128)} %get-tuple-element.156), channel_id=1, source_target_pairs={{0,16},{1,4},{2,18},{3,6},{4,1},{5,8},{6,3},{7,10},{8,5},{9,12},{1... | collective-permute-start | bytes 786440 | tf_op jit(solution)/shard_map/ppermute | solution.py:67
  21.0 1.3 first_inner.1
  22.4 4.2 %collective-permute-done.5.ym = f32[2,32,256]{2,1,0:T(8,128)S(1)} collective-permute-done((f32[2,32,256]{2,1,0:T(8,128)S(1)}, f32[2,32,256]{2,1,0:T(8,128)S(1)}, u32[]{:S(2)}, u32[]{:S(2)}) %collective-permute-start.5) | collective-permute-done | bytes 65568 | tf_op jit(solution)/shard_map/ppermute | solution.py:67
  26.6 1.5 %first_outer.1 = (f32[256,256]{1,0:T(8,128)S(1)}, f32[128,256]{1,0:T(8,128)S(1)}, f32[128,256]{1,0:T(8,128)S(1)}, f32[32,256]{1,0:T(8,128)S(1)}, f32[256,256]{1,...) custom-call(s32[8]{0:T(128)S(1)} %stack.42.flags, ...), custom_call_target="tpu_custom_call" | custom-call | flops 1000 | bytes 1000 | tf_op jit(solution)/shard_map/first_outer/pallas_call | solution.py:420
  28.1 2.7 %collective-permute-start.7 = (f32[128,256]{1,0:T(8,128)S(1)}, f32[128,256]{1,0:T(8,128)S(1)}, u32[]{:S(2)}, u32[]{:S(2)}) collective-permute-start(f32[128,256]{1,0:T(8,128)S(1)} %get-tuple-element.164), channel_id=1, source_target_pairs={{0,1},{1,0},{2,3},{3,2},{4,5},{5,4},{6,7},{7,6},{8,9},{9,8},{10,11... | collective-permute-start | bytes 393224 | tf_op jit(solution)/shard_map/ppermute | solution.py:67
  30.8 1.3 collective-permute-start.8
  32.1 1.5 %collective-permute-start.11 = (f32[8,2,128]{2,1,0:T(2,128)S(1)}, f32[8,2,128]{2,1,0:T(2,128)S(1)}, u32[]{:S(2)}, u32[]{:S(2)}) collective-permute-start(f32[8,2,128]{2,1,0:T(2,128)S(1)} %get-tuple-element.172), channel_id=1, source_target_pairs={{0,2},{1,3},{2,0},{3,1},{4,6},{5,7},{6,4},{7,5},{8,10},{9,11},{10,... | collective-permute-start | bytes 24584 | tf_op jit(solution)/shard_map/ppermute | solution.py:67
  33.5 1.2 forward_inner.7
  37.0 1.3 collective-permute-start.13
  39.0 1.3 collective-permute-start.15
  40.3 1.2 forward_inner.8
  45.1 1.0 collective-permute-start.18
  46.1 2.0 %collective-permute-start.19 = (f32[8,2,128]{2,1,0:T(2,128)S(1)}, f32[8,2,128]{2,1,0:T(2,128)S(1)}, u32[]{:S(2)}, u32[]{:S(2)}) collective-permute-start(f32[8,2,128]{2,1,0:T(2,128)S(1)} %get-tuple-element.186), channel_id=1, source_target_pairs={{0,8},{1,9},{2,10},{3,11},{4,12},{5,13},{6,14},{7,15},{8,0},{9,1},... | collective-permute-start | bytes 24584 | tf_op jit(solution)/shard_map/ppermute | solution.py:67
  48.2 1.2 forward_inner.9
  50.4 2.2 %collective-permute-start.20 = (f32[128,256]{1,0:T(8,128)S(1)}, f32[128,256]{1,0:T(8,128)S(1)}, u32[]{:S(2)}, u32[]{:S(2)}) collective-permute-start(f32[128,256]{1,0:T(8,128)S(1)} %get-tuple-element.188), channel_id=1, source_target_pairs={{0,1},{1,0},{2,3},{3,2},{4,5},{5,4},{6,7},{7,6},{8,9},{9,8},{10,11... | collective-permute-start | bytes 393224 | tf_op jit(solution)/shard_map/ppermute | solution.py:67
  53.7 1.2 forward_inner.10
  54.9 1.4 %collective-permute-done.22.ym = f32[32,256]{1,0:T(8,128)S(1)} collective-permute-done((f32[32,256]{1,0:T(8,128)S(1)}, f32[32,256]{1,0:T(8,128)S(1)}, u32[]{:S(2)}, u32[]{:S(2)}) %collective-permute-start.22) | collective-permute-done | bytes 32800 | tf_op jit(solution)/shard_map/ppermute | solution.py:67
  56.3 0.9 collective-permute-done.21.zm
  59.5 1.2 forward_inner.11
  60.8 1.6 %collective-permute-done.25.ym = f32[32,256]{1,0:T(8,128)S(1)} collective-permute-done((f32[32,256]{1,0:T(8,128)S(1)}, f32[32,256]{1,0:T(8,128)S(1)}, u32[]{:S(2)}, u32[]{:S(2)}) %collective-permute-start.25) | collective-permute-done | bytes 32800 | tf_op jit(solution)/shard_map/ppermute | solution.py:67
  65.5 1.2 forward_inner.12
  66.7 1.5 %collective-permute-done.28.ym = f32[32,256]{1,0:T(8,128)S(1)} collective-permute-done((f32[32,256]{1,0:T(8,128)S(1)}, f32[32,256]{1,0:T(8,128)S(1)}, u32[]{:S(2)}, u32[]{:S(2)}) %collective-permute-start.28) | collective-permute-done | bytes 32800 | tf_op jit(solution)/shard_map/ppermute | solution.py:67
  71.3 1.1 adjoint_first.1.u_part
  73.1 1.2 forward_inner.13
  75.1 1.5 %turn.1 = (f32[256,256]{1,0:T(8,128)S(1)}, f32[256,256]{1,0:T(8,128)S(1)}, f32[128,256]{1,0:T(8,128)S(1)}, f32[128,256]{1,0:T(8,128)S(1)}, f32[32,256]{1,0:T(8,128)S(1)}) custom-call(s32[8]{0:T(128)S(1)} %stack.42.flags, f32[256,256]{1,0:T(8,128)S(1)} %get-tuple-element.204.part, f32[256,256]{1,0:T(8,128)S(1)} %get-tuple-element.160.k0, ...), custom_call_target="tpu_custom_call" | custom-call | flops 1000 | bytes 1000 | tf_op jit(solution)/shard_map/turn/pallas_call | solution.py:420
  78.7 1.7 %adjoint_inner.7 = (f32[256,256]{1,0:T(8,128)S(1)}, f32[256,256]{1,0:T(8,128)S(1)}) custom-call(s32[8]{0:T(128)S(1)} %stack.42.flags, f32[256,256]{1,0:T(8,128)S(1)} %get-tuple-element.213.cur.prev, f32[256,256]{1,0:T(8,128)S(1)} %get-tuple-element.170.rest_0_.cur.prev, f32[256,256]{1,0:T(8,128)S(1)} %get-tuple-element.160.k0, ...), custom_call_target="tpu_custom_call" | custom-call | flops 1000 | bytes 5401000 | tf_op jit(solution)/shard_map/adjoint_inner/pallas_call | solution.py:420
  80.8 0.9 collective-permute-done.33.zm
  84.6 1.6 %adjoint_inner.8 = (f32[256,256]{1,0:T(8,128)S(1)}, f32[256,256]{1,0:T(8,128)S(1)}) custom-call(s32[8]{0:T(128)S(1)} %stack.42.flags, f32[256,256]{1,0:T(8,128)S(1)} %get-tuple-element.219.cur.prev, f32[256,256]{1,0:T(8,128)S(1)} %get-tuple-element.213.cur.prev, f32[256,256]{1,0:T(8,128)S(1)} %get-tuple-element.160.k0, ...), custom_call_target="tpu_custom_call" | custom-call | flops 1000 | bytes 5401000 | tf_op jit(solution)/shard_map/adjoint_inner/pallas_call | solution.py:420
  90.5 1.6 %adjoint_inner.9 = (f32[256,256]{1,0:T(8,128)S(1)}, f32[256,256]{1,0:T(8,128)S(1)}) custom-call(s32[8]{0:T(128)S(1)} %stack.42.flags, f32[256,256]{1,0:T(8,128)S(1)} %get-tuple-element.226.cur.prev, f32[256,256]{1,0:T(8,128)S(1)} %get-tuple-element.219.cur.prev, f32[256,256]{1,0:T(8,128)S(1)} %get-tuple-element.160.k0, ...), custom_call_target="tpu_custom_call" | custom-call | flops 1000 | bytes 5401000 | tf_op jit(solution)/shard_map/adjoint_inner/pallas_call | solution.py:420
  96.5 1.6 %adjoint_inner.10 = (f32[256,256]{1,0:T(8,128)S(1)}, f32[256,256]{1,0:T(8,128)S(1)}) custom-call(s32[8]{0:T(128)S(1)} %stack.42.flags, f32[256,256]{1,0:T(8,128)S(1)} %get-tuple-element.233.cur.prev, f32[256,256]{1,0:T(8,128)S(1)} %get-tuple-element.226.cur.prev, f32[256,256]{1,0:T(8,128)S(1)} %get-tuple-element.160.k0, ...), custom_call_target="tpu_custom_call" | custom-call | flops 1000 | bytes 5401000 | tf_op jit(solution)/shard_map/adjoint_inner/pallas_call | solution.py:420
  99.7 1.0 adjoint_outer.9
  102.6 1.6 %adjoint_inner.11 = (f32[256,256]{1,0:T(8,128)S(1)}, f32[256,256]{1,0:T(8,128)S(1)}) custom-call(s32[8]{0:T(128)S(1)} %stack.42.flags, f32[256,256]{1,0:T(8,128)S(1)} %get-tuple-element.240.cur.prev, f32[256,256]{1,0:T(8,128)S(1)} %get-tuple-element.233.cur.prev, f32[256,256]{1,0:T(8,128)S(1)} %get-tuple-element.160.k0, ...), custom_call_target="tpu_custom_call" | custom-call | flops 1000 | bytes 5401000 | tf_op jit(solution)/shard_map/adjoint_inner/pallas_call | solution.py:420
  108.6 1.6 %adjoint_inner.12 = (f32[256,256]{1,0:T(8,128)S(1)}, f32[256,256]{1,0:T(8,128)S(1)}) custom-call(s32[8]{0:T(128)S(1)} %stack.42.flags, f32[256,256]{1,0:T(8,128)S(1)} %get-tuple-element.247.cur.prev, f32[256,256]{1,0:T(8,128)S(1)} %get-tuple-element.240.cur.prev, f32[256,256]{1,0:T(8,128)S(1)} %get-tuple-element.160.k0, ...), custom_call_target="tpu_custom_call" | custom-call | flops 1000 | bytes 5401000 | tf_op jit(solution)/shard_map/adjoint_inner/pallas_call | solution.py:420
  110.9 0.9 collective-permute-done.48.zm
  114.6 1.6 %adjoint_inner.13 = (f32[256,256]{1,0:T(8,128)S(1)}, f32[256,256]{1,0:T(8,128)S(1)}) custom-call(s32[8]{0:T(128)S(1)} %stack.42.flags, f32[256,256]{1,0:T(8,128)S(1)} %get-tuple-element.254.cur.prev, f32[256,256]{1,0:T(8,128)S(1)} %get-tuple-element.247.cur.prev, f32[256,256]{1,0:T(8,128)S(1)} %get-tuple-element.160.k0, ...), custom_call_target="tpu_custom_call" | custom-call | flops 1000 | bytes 5401000 | tf_op jit(solution)/shard_map/adjoint_inner/pallas_call | solution.py:420
  117.8 1.0 last.1
  118.8 1.1 collective-permute-start.53
  120.3 1.0 collective-permute-done.54.got
  121.9 2.6 %collective-permute-start.55 = (f32[2,64,128]{2,1,0:T(8,128)S(1)}, f32[2,64,128]{2,1,0:T(8,128)S(1)}, u32[]{:S(2)}, u32[]{:S(2)}) collective-permute-start(f32[2,64,128]{2,1,0:T(8,128)S(1)} %get-tuple-element.268), channel_id=1, source_target_pairs={{0,0},{1,2},{2,1},{3,3},{4,4},{5,6},{6,5},{7,7},{8,8},{9,10},{10,9... | collective-permute-start | bytes 196616 | tf_op jit(solution)/shard_map/ppermute | solution.py:67
  124.5 1.5 %collective-permute-start.56 = (f32[2,64,128]{2,1,0:T(8,128)S(1)}, f32[2,64,128]{2,1,0:T(8,128)S(1)}, u32[]{:S(2)}, u32[]{:S(2)}) collective-permute-start(f32[2,64,128]{2,1,0:T(8,128)S(1)} %get-tuple-element.269), channel_id=1, source_target_pairs={{0,4},{1,6},{2,5},{3,7},{4,0},{5,2},{6,1},{7,3},{8,12},{9,14},{10,... | collective-permute-start | bytes 196616 | tf_op jit(solution)/shard_map/ppermute | solution.py:67
  126.9 3.1 %collective-permute-start.58 = (f32[2,64,128]{2,1,0:T(8,128)S(1)}, f32[2,64,128]{2,1,0:T(8,128)S(1)}, u32[]{:S(2)}, u32[]{:S(2)}) collective-permute-start(f32[2,64,128]{2,1,0:T(8,128)S(1)} %get-tuple-element.271), channel_id=1, source_target_pairs={{0,12},{1,14},{2,13},{3,15},{4,8},{5,10},{6,9},{7,11},{8,4},{9,6},... | collective-permute-start | bytes 196616 | tf_op jit(solution)/shard_map/ppermute | solution.py:67
  130.0 1.4 %select.19 = (f32[256,256]{1,0:T(8,128)}, f32[256,256]{1,0:T(8,128)}) custom-call(s32[8]{0:T(128)S(1)} %stack.42.flags, f32[2,256,256]{2,1,0:T(8,128)S(1)} %get-tuple-element.263.own, f32[2,256,256]{2,1,0:T(8,128)S(1)} %collective-permute-done.53.recv), custom_call_target="tpu_custom_call" | custom-call | flops 1000 | bytes 4321000 | tf_op jit(solution)/shard_map/select/pallas_call | solution.py:420
  132.2 1.2 collective-permute-done.58.refs_3_
  133.4 1.8 %filter.1 = f32[32,32,64]{2,1,0:T(8,128)} custom-call(s32[8]{0:T(128)S(1)} %stack.42.flags, f32[2,64,128]{2,1,0:T(8,128)S(1)} %collective-permute-done.55.refs_0_, f32[2,64,128]{2,1,0:T(8,128)S(1)} %collective-permute-done.56.refs_1_, f32[2,64,128]{2,1,0:T(8,128)S(1)} %collective-permute-done.57.refs_2_, f32[2,64,128]{2,1,0:T(8,128)S(1)} %collective-permute-done.58.refs_3_), custom_call_target="tpu_custom_call" | custom-call | flops 1000 | bytes 1000 | tf_op jit(solution)/shard_map/filter/pallas_call | solution.py:420
  (177 shorter events, 58.9 us)
Async XLA Ops:
  0.6 14.1 %collective-permute-start.1 = (f32[256,256]{1,0:T(8,128)}, f32[256,256]{1,0:T(8,128)S(1)}, u32[]{:S(2)}, u32[]{:S(2)}) collective-permute-start(f32[256,256]{1,0:T(8,128)} %bitcast.49), channel_id=1, source_target_pairs={{0,16},{1,2},{2,1},{3,19},{4,20},{5,6},{6,5},{7,23},{8,24},{9,10},... | collective-permute-start | bytes 786440 | tf_op jit(solution)/shard_map/ppermute | solution.py:67
  3.3 11.4 %collective-permute-start = (f32[256,256]{1,0:T(8,128)}, f32[256,256]{1,0:T(8,128)S(1)}, u32[]{:S(2)}, u32[]{:S(2)}) collective-permute-start(f32[256,256]{1,0:T(8,128)} %bitcast.47), channel_id=1, source_target_pairs={{0,16},{1,2},{2,1},{3,19},{4,20},{5,6},{6,5},{7,23},{8,24},{9,10},... | collective-permute-start | bytes 786440 | tf_op jit(solution)/shard_map/ppermute | solution.py:67
  5.3 13.8 %collective-permute-start.2 = (f32[2,256,256]{2,1,0:T(8,128)}, f32[2,256,256]{2,1,0:T(8,128)S(1)}, u32[]{:S(2)}, u32[]{:S(2)}) collective-permute-start(f32[2,256,256]{2,1,0:T(8,128)} %pad_maximum_fusion), channel_id=1, source_target_pairs={{0,16},{1,2},{2,1},{3,19},{4,20},{5,6},{6,5},{7,23},{8,24},{9,10},... | collective-permute-start | bytes 1572872 | tf_op jit(solution)/shard_map/ppermute | solution.py:67
  13.4 9.0 %collective-permute-start.6 = (f32[8,2,128]{2,1,0:T(2,128)}, f32[8,2,128]{2,1,0:T(2,128)S(1)}, u32[]{:S(2)}, u32[]{:S(2)}) collective-permute-start(f32[8,2,128]{2,1,0:T(2,128)} %dynamic-slice_bitcast_fusion), channel_id=1, source_target_pairs={{0,1},{1,0},{2,3},{3,2},{4,5},{5,4},{6,7},{7,6},{8,9},{9,8},{10,11... | collective-permute-start | bytes 24584 | tf_op jit(solution)/shard_map/ppermute | solution.py:67
  16.2 4.4 %collective-permute-start.3 = (f32[2,128,256]{2,1,0:T(8,128)}, f32[2,128,256]{2,1,0:T(8,128)S(1)}, u32[]{:S(2)}, u32[]{:S(2)}) collective-permute-start(f32[2,128,256]{2,1,0:T(8,128)} %get-tuple-element.147), channel_id=1, source_target_pairs={{0,1},{1,0},{2,3},{3,2},{4,5},{5,4},{6,7},{7,6},{8,9},{9,8},{10,11... | collective-permute-start | bytes 786440 | tf_op jit(solution)/shard_map/ppermute | solution.py:67
  16.4 10.3 %collective-permute-start.4 = (f32[2,128,256]{2,1,0:T(8,128)}, f32[2,128,256]{2,1,0:T(8,128)}, u32[]{:S(2)}, u32[]{:S(2)}) collective-permute-start(f32[2,128,256]{2,1,0:T(8,128)} %get-tuple-element.156), channel_id=1, source_target_pairs={{0,16},{1,4},{2,18},{3,6},{4,1},{5,8},{6,3},{7,10},{8,5},{9,12},{1... | collective-permute-start | bytes 786440 | tf_op jit(solution)/shard_map/ppermute | solution.py:67
  18.9 15.9 %collective-permute-start.10 = (f32[2,256,256]{2,1,0:T(8,128)}, f32[2,256,256]{2,1,0:T(8,128)S(1)}, u32[]{:S(2)}, u32[]{:S(2)}) collective-permute-start(f32[2,256,256]{2,1,0:T(8,128)} %pad_maximum_fusion.1), channel_id=1, source_target_pairs={{0,16},{1,2},{2,1},{3,19},{4,20},{5,6},{6,5},{7,23},{8,24},{9,10},... | collective-permute-start | bytes 1572872 | tf_op jit(solution)/shard_map/ppermute | solution.py:67
  19.0 7.6 %collective-permute-start.5 = (f32[2,32,256]{2,1,0:T(8,128)S(1)}, f32[2,32,256]{2,1,0:T(8,128)S(1)}, u32[]{:S(2)}, u32[]{:S(2)}) collective-permute-start(f32[2,32,256]{2,1,0:T(8,128)S(1)} %get-tuple-element.157), channel_id=1, source_target_pairs={{0,2},{1,3},{2,0},{3,1},{4,6},{5,7},{6,4},{7,5},{8,10},{9,11},{10,... | collective-permute-start | bytes 196616 | tf_op jit(solution)/shard_map/ppermute | solution.py:67
  28.1 5.4 %collective-permute-start.7 = (f32[128,256]{1,0:T(8,128)S(1)}, f32[128,256]{1,0:T(8,128)S(1)}, u32[]{:S(2)}, u32[]{:S(2)}) collective-permute-start(f32[128,256]{1,0:T(8,128)S(1)} %get-tuple-element.164), channel_id=1, source_target_pairs={{0,1},{1,0},{2,3},{3,2},{4,5},{5,4},{6,7},{7,6},{8,9},{9,8},{10,11... | collective-permute-start | bytes 393224 | tf_op jit(solution)/shard_map/ppermute | solution.py:67
  30.8 4.8 %collective-permute-start.8 = (f32[128,256]{1,0:T(8,128)S(1)}, f32[128,256]{1,0:T(8,128)S(1)}, u32[]{:S(2)}, u32[]{:S(2)}) collective-permute-start(f32[128,256]{1,0:T(8,128)S(1)} %get-tuple-element.166), channel_id=1, source_target_pairs={{0,16},{1,4},{2,18},{3,6},{4,1},{5,8},{6,3},{7,10},{8,5},{9,12},{1... | collective-permute-start | bytes 393224 | tf_op jit(solution)/shard_map/ppermute | solution.py:67
  32.1 3.5 %collective-permute-start.9 = (f32[32,256]{1,0:T(8,128)S(1)}, f32[32,256]{1,0:T(8,128)S(1)}, u32[]{:S(2)}, u32[]{:S(2)}) collective-permute-start(f32[32,256]{1,0:T(8,128)S(1)} %get-tuple-element.167), channel_id=1, source_target_pairs={{0,2},{1,3},{2,0},{3,1},{4,6},{5,7},{6,4},{7,5},{8,10},{9,11},{10,... | collective-permute-start | bytes 98312 | tf_op jit(solution)/shard_map/ppermute | solution.py:67
  32.1 3.5 %collective-permute-start.11 = (f32[8,2,128]{2,1,0:T(2,128)S(1)}, f32[8,2,128]{2,1,0:T(2,128)S(1)}, u32[]{:S(2)}, u32[]{:S(2)}) collective-permute-start(f32[8,2,128]{2,1,0:T(2,128)S(1)} %get-tuple-element.172), channel_id=1, source_target_pairs={{0,2},{1,3},{2,0},{3,1},{4,6},{5,7},{6,4},{7,5},{8,10},{9,11},{10,... | collective-permute-start | bytes 24584 | tf_op jit(solution)/shard_map/ppermute | solution.py:67
  36.5 3.8 %collective-permute-start.12 = (f32[2,128,256]{2,1,0:T(8,128)S(1)}, f32[2,128,256]{2,1,0:T(8,128)S(1)}, u32[]{:S(2)}, u32[]{:S(2)}) collective-permute-start(f32[2,128,256]{2,1,0:T(8,128)S(1)} %get-tuple-element.174), channel_id=1, source_target_pairs={{0,1},{1,0},{2,3},{3,2},{4,5},{5,4},{6,7},{7,6},{8,9},{9,8},{10,11... | collective-permute-start | bytes 786440 | tf_op jit(solution)/shard_map/ppermute | solution.py:67
  37.0 6.1 %collective-permute-start.13 = (f32[2,128,256]{2,1,0:T(8,128)S(1)}, f32[2,128,256]{2,1,0:T(8,128)S(1)}, u32[]{:S(2)}, u32[]{:S(2)}) collective-permute-start(f32[2,128,256]{2,1,0:T(8,128)S(1)} %get-tuple-element.176), channel_id=1, source_target_pairs={{0,16},{1,4},{2,18},{3,6},{4,1},{5,8},{6,3},{7,10},{8,5},{9,12},{1... | collective-permute-start | bytes 786440 | tf_op jit(solution)/shard_map/ppermute | solution.py:67
  38.2 3.9 %collective-permute-start.14 = (f32[2,32,256]{2,1,0:T(8,128)S(1)}, f32[2,32,256]{2,1,0:T(8,128)S(1)}, u32[]{:S(2)}, u32[]{:S(2)}) collective-permute-start(f32[2,32,256]{2,1,0:T(8,128)S(1)} %get-tuple-element.177), channel_id=1, source_target_pairs={{0,2},{1,3},{2,0},{3,1},{4,6},{5,7},{6,4},{7,5},{8,10},{9,11},{10,... | collective-permute-start | bytes 196616 | tf_op jit(solution)/shard_map/ppermute | solution.py:67
  43.9 4.3 %collective-permute-start.16 = (f32[128,256]{1,0:T(8,128)S(1)}, f32[128,256]{1,0:T(8,128)S(1)}, u32[]{:S(2)}, u32[]{:S(2)}) collective-permute-start(f32[128,256]{1,0:T(8,128)S(1)} %get-tuple-element.181), channel_id=1, source_target_pairs={{0,1},{1,0},{2,3},{3,2},{4,5},{5,4},{6,7},{7,6},{8,9},{9,8},{10,11... | collective-permute-start | bytes 393224 | tf_op jit(solution)/shard_map/ppermute | solution.py:67
  44.5 5.0 %collective-permute-start.17 = (f32[128,256]{1,0:T(8,128)S(1)}, f32[128,256]{1,0:T(8,128)S(1)}, u32[]{:S(2)}, u32[]{:S(2)}) collective-permute-start(f32[128,256]{1,0:T(8,128)S(1)} %get-tuple-element.183), channel_id=1, source_target_pairs={{0,16},{1,4},{2,18},{3,6},{4,1},{5,8},{6,3},{7,10},{8,5},{9,12},{1... | collective-permute-start | bytes 393224 | tf_op jit(solution)/shard_map/ppermute | solution.py:67
  45.1 4.4 %collective-permute-start.18 = (f32[32,256]{1,0:T(8,128)S(1)}, f32[32,256]{1,0:T(8,128)S(1)}, u32[]{:S(2)}, u32[]{:S(2)}) collective-permute-start(f32[32,256]{1,0:T(8,128)S(1)} %get-tuple-element.184), channel_id=1, source_target_pairs={{0,2},{1,3},{2,0},{3,1},{4,6},{5,7},{6,4},{7,5},{8,10},{9,11},{10,... | collective-permute-start | bytes 98312 | tf_op jit(solution)/shard_map/ppermute | solution.py:67
  46.1 3.4 %collective-permute-start.19 = (f32[8,2,128]{2,1,0:T(2,128)S(1)}, f32[8,2,128]{2,1,0:T(2,128)S(1)}, u32[]{:S(2)}, u32[]{:S(2)}) collective-permute-start(f32[8,2,128]{2,1,0:T(2,128)S(1)} %get-tuple-element.186), channel_id=1, source_target_pairs={{0,8},{1,9},{2,10},{3,11},{4,12},{5,13},{6,14},{7,15},{8,0},{9,1},... | collective-permute-start | bytes 24584 | tf_op jit(solution)/shard_map/ppermute | solution.py:67
  50.4 3.3 %collective-permute-start.20 = (f32[128,256]{1,0:T(8,128)S(1)}, f32[128,256]{1,0:T(8,128)S(1)}, u32[]{:S(2)}, u32[]{:S(2)}) collective-permute-start(f32[128,256]{1,0:T(8,128)S(1)} %get-tuple-element.188), channel_id=1, source_target_pairs={{0,1},{1,0},{2,3},{3,2},{4,5},{5,4},{6,7},{7,6},{8,9},{9,8},{10,11... | collective-permute-start | bytes 393224 | tf_op jit(solution)/shard_map/ppermute | solution.py:67
  52.6 4.7 %collective-permute-start.21 = (f32[128,256]{1,0:T(8,128)S(1)}, f32[128,256]{1,0:T(8,128)S(1)}, u32[]{:S(2)}, u32[]{:S(2)}) collective-permute-start(f32[128,256]{1,0:T(8,128)S(1)} %get-tuple-element.190), channel_id=1, source_target_pairs={{0,16},{1,4},{2,18},{3,6},{4,1},{5,8},{6,3},{7,10},{8,5},{9,12},{1... | collective-permute-start | bytes 393224 | tf_op jit(solution)/shard_map/ppermute | solution.py:67
  53.2 3.1 %collective-permute-start.22 = (f32[32,256]{1,0:T(8,128)S(1)}, f32[32,256]{1,0:T(8,128)S(1)}, u32[]{:S(2)}, u32[]{:S(2)}) collective-permute-start(f32[32,256]{1,0:T(8,128)S(1)} %get-tuple-element.191), channel_id=1, source_target_pairs={{0,2},{1,3},{2,0},{3,1},{4,6},{5,7},{6,4},{7,5},{8,10},{9,11},{10,... | collective-permute-start | bytes 98312 | tf_op jit(solution)/shard_map/ppermute | solution.py:67
  58.5 4.7 %collective-permute-start.24 = (f32[128,256]{1,0:T(8,128)S(1)}, f32[128,256]{1,0:T(8,128)S(1)}, u32[]{:S(2)}, u32[]{:S(2)}) collective-permute-start(f32[128,256]{1,0:T(8,128)S(1)} %get-tuple-element.195), channel_id=1, source_target_pairs={{0,16},{1,4},{2,18},{3,6},{4,1},{5,8},{6,3},{7,10},{8,5},{9,12},{1... | collective-permute-start | bytes 393224 | tf_op jit(solution)/shard_map/ppermute | solution.py:67
  59.2 3.1 %collective-permute-start.25 = (f32[32,256]{1,0:T(8,128)S(1)}, f32[32,256]{1,0:T(8,128)S(1)}, u32[]{:S(2)}, u32[]{:S(2)}) collective-permute-start(f32[32,256]{1,0:T(8,128)S(1)} %get-tuple-element.196), channel_id=1, source_target_pairs={{0,2},{1,3},{2,0},{3,1},{4,6},{5,7},{6,4},{7,5},{8,10},{9,11},{10,... | collective-permute-start | bytes 98312 | tf_op jit(solution)/shard_map/ppermute | solution.py:67
  64.5 4.7 %collective-permute-start.27 = (f32[128,256]{1,0:T(8,128)S(1)}, f32[128,256]{1,0:T(8,128)S(1)}, u32[]{:S(2)}, u32[]{:S(2)}) collective-permute-start(f32[128,256]{1,0:T(8,128)S(1)} %get-tuple-element.200), channel_id=1, source_target_pairs={{0,16},{1,4},{2,18},{3,6},{4,1},{5,8},{6,3},{7,10},{8,5},{9,12},{1... | collective-permute-start | bytes 393224 | tf_op jit(solution)/shard_map/ppermute | solution.py:67
  65.2 3.1 %collective-permute-start.28 = (f32[32,256]{1,0:T(8,128)S(1)}, f32[32,256]{1,0:T(8,128)S(1)}, u32[]{:S(2)}, u32[]{:S(2)}) collective-permute-start(f32[32,256]{1,0:T(8,128)S(1)} %get-tuple-element.201), channel_id=1, source_target_pairs={{0,2},{1,3},{2,0},{3,1},{4,6},{5,7},{6,4},{7,5},{8,10},{9,11},{10,... | collective-permute-start | bytes 98312 | tf_op jit(solution)/shard_map/ppermute | solution.py:67
  70.0 3.1 %collective-permute-start.29 = (f32[128,256]{1,0:T(8,128)S(1)}, f32[128,256]{1,0:T(8,128)S(1)}, u32[]{:S(2)}, u32[]{:S(2)}) collective-permute-start(f32[128,256]{1,0:T(8,128)S(1)} %get-tuple-element.203), channel_id=1, source_target_pairs={{0,1},{1,0},{2,3},{3,2},{4,5},{5,4},{6,7},{7,6},{8,9},{9,8},{10,11... | collective-permute-start | bytes 393224 | tf_op jit(solution)/shard_map/ppermute | solution.py:67
  70.5 4.7 %collective-permute-start.30 = (f32[128,256]{1,0:T(8,128)S(1)}, f32[128,256]{1,0:T(8,128)S(1)}, u32[]{:S(2)}, u32[]{:S(2)}) collective-permute-start(f32[128,256]{1,0:T(8,128)S(1)} %get-tuple-element.205), channel_id=1, source_target_pairs={{0,16},{1,4},{2,18},{3,6},{4,1},{5,8},{6,3},{7,10},{8,5},{9,12},{1... | collective-permute-start | bytes 393224 | tf_op jit(solution)/shard_map/ppermute | solution.py:67
  71.1 3.2 %collective-permute-start.31 = (f32[32,256]{1,0:T(8,128)S(1)}, f32[32,256]{1,0:T(8,128)S(1)}, u32[]{:S(2)}, u32[]{:S(2)}) collective-permute-start(f32[32,256]{1,0:T(8,128)S(1)} %get-tuple-element.206), channel_id=1, source_target_pairs={{0,2},{1,3},{2,0},{3,1},{4,6},{5,7},{6,4},{7,5},{8,10},{9,11},{10,... | collective-permute-start | bytes 98312 | tf_op jit(solution)/shard_map/ppermute | solution.py:67
  77.1 4.7 %collective-permute-start.33 = (f32[128,256]{1,0:T(8,128)S(1)}, f32[128,256]{1,0:T(8,128)S(1)}, u32[]{:S(2)}, u32[]{:S(2)}) collective-permute-start(f32[128,256]{1,0:T(8,128)S(1)} %get-tuple-element.217), channel_id=1, source_target_pairs={{0,16},{1,4},{2,18},{3,6},{4,1},{5,8},{6,3},{7,10},{8,5},{9,12},{1... | collective-permute-start | bytes 393224 | tf_op jit(solution)/shard_map/ppermute | solution.py:67
  77.8 3.1 %collective-permute-start.34 = (f32[32,256]{1,0:T(8,128)S(1)}, f32[32,256]{1,0:T(8,128)S(1)}, u32[]{:S(2)}, u32[]{:S(2)}) collective-permute-start(f32[32,256]{1,0:T(8,128)S(1)} %get-tuple-element.218), channel_id=1, source_target_pairs={{0,2},{1,3},{2,0},{3,1},{4,6},{5,7},{6,4},{7,5},{8,10},{9,11},{10,... | collective-permute-start | bytes 98312 | tf_op jit(solution)/shard_map/ppermute | solution.py:67
  83.1 4.7 %collective-permute-start.36 = (f32[128,256]{1,0:T(8,128)S(1)}, f32[128,256]{1,0:T(8,128)S(1)}, u32[]{:S(2)}, u32[]{:S(2)}) collective-permute-start(f32[128,256]{1,0:T(8,128)S(1)} %get-tuple-element.224), channel_id=1, source_target_pairs={{0,16},{1,4},{2,18},{3,6},{4,1},{5,8},{6,3},{7,10},{8,5},{9,12},{1... | collective-permute-start | bytes 393224 | tf_op jit(solution)/shard_map/ppermute | solution.py:67
  83.8 3.1 %collective-permute-start.37 = (f32[32,256]{1,0:T(8,128)S(1)}, f32[32,256]{1,0:T(8,128)S(1)}, u32[]{:S(2)}, u32[]{:S(2)}) collective-permute-start(f32[32,256]{1,0:T(8,128)S(1)} %get-tuple-element.225), channel_id=1, source_target_pairs={{0,2},{1,3},{2,0},{3,1},{4,6},{5,7},{6,4},{7,5},{8,10},{9,11},{10,... | collective-permute-start | bytes 98312 | tf_op jit(solution)/shard_map/ppermute | solution.py:67
  89.0 4.7 %collective-permute-start.39 = (f32[128,256]{1,0:T(8,128)S(1)}, f32[128,256]{1,0:T(8,128)S(1)}, u32[]{:S(2)}, u32[]{:S(2)}) collective-permute-start(f32[128,256]{1,0:T(8,128)S(1)} %get-tuple-element.231), channel_id=1, source_target_pairs={{0,16},{1,4},{2,18},{3,6},{4,1},{5,8},{6,3},{7,10},{8,5},{9,12},{1... | collective-permute-start | bytes 393224 | tf_op jit(solution)/shard_map/ppermute | solution.py:67
  89.7 3.1 %collective-permute-start.40 = (f32[32,256]{1,0:T(8,128)S(1)}, f32[32,256]{1,0:T(8,128)S(1)}, u32[]{:S(2)}, u32[]{:S(2)}) collective-permute-start(f32[32,256]{1,0:T(8,128)S(1)} %get-tuple-element.232), channel_id=1, source_target_pairs={{0,2},{1,3},{2,0},{3,1},{4,6},{5,7},{6,4},{7,5},{8,10},{9,11},{10,... | collective-permute-start | bytes 98312 | tf_op jit(solution)/shard_map/ppermute | solution.py:67
  95.0 4.7 %collective-permute-start.42 = (f32[128,256]{1,0:T(8,128)S(1)}, f32[128,256]{1,0:T(8,128)S(1)}, u32[]{:S(2)}, u32[]{:S(2)}) collective-permute-start(f32[128,256]{1,0:T(8,128)S(1)} %get-tuple-element.238), channel_id=1, source_target_pairs={{0,16},{1,4},{2,18},{3,6},{4,1},{5,8},{6,3},{7,10},{8,5},{9,12},{1... | collective-permute-start | bytes 393224 | tf_op jit(solution)/shard_map/ppermute | solution.py:67
  95.7 3.1 %collective-permute-start.43 = (f32[32,256]{1,0:T(8,128)S(1)}, f32[32,256]{1,0:T(8,128)S(1)}, u32[]{:S(2)}, u32[]{:S(2)}) collective-permute-start(f32[32,256]{1,0:T(8,128)S(1)} %get-tuple-element.239), channel_id=1, source_target_pairs={{0,2},{1,3},{2,0},{3,1},{4,6},{5,7},{6,4},{7,5},{8,10},{9,11},{10,... | collective-permute-start | bytes 98312 | tf_op jit(solution)/shard_map/ppermute | solution.py:67
  101.2 4.7 %collective-permute-start.45 = (f32[128,256]{1,0:T(8,128)S(1)}, f32[128,256]{1,0:T(8,128)S(1)}, u32[]{:S(2)}, u32[]{:S(2)}) collective-permute-start(f32[128,256]{1,0:T(8,128)S(1)} %get-tuple-element.245), channel_id=1, source_target_pairs={{0,16},{1,4},{2,18},{3,6},{4,1},{5,8},{6,3},{7,10},{8,5},{9,12},{1... | collective-permute-start | bytes 393224 | tf_op jit(solution)/shard_map/ppermute | solution.py:67
  101.9 3.1 %collective-permute-start.46 = (f32[32,256]{1,0:T(8,128)S(1)}, f32[32,256]{1,0:T(8,128)S(1)}, u32[]{:S(2)}, u32[]{:S(2)}) collective-permute-start(f32[32,256]{1,0:T(8,128)S(1)} %get-tuple-element.246), channel_id=1, source_target_pairs={{0,2},{1,3},{2,0},{3,1},{4,6},{5,7},{6,4},{7,5},{8,10},{9,11},{10,... | collective-permute-start | bytes 98312 | tf_op jit(solution)/shard_map/ppermute | solution.py:67
  107.1 4.7 %collective-permute-start.48 = (f32[128,256]{1,0:T(8,128)S(1)}, f32[128,256]{1,0:T(8,128)S(1)}, u32[]{:S(2)}, u32[]{:S(2)}) collective-permute-start(f32[128,256]{1,0:T(8,128)S(1)} %get-tuple-element.252), channel_id=1, source_target_pairs={{0,16},{1,4},{2,18},{3,6},{4,1},{5,8},{6,3},{7,10},{8,5},{9,12},{1... | collective-permute-start | bytes 393224 | tf_op jit(solution)/shard_map/ppermute | solution.py:67
  107.8 3.1 %collective-permute-start.49 = (f32[32,256]{1,0:T(8,128)S(1)}, f32[32,256]{1,0:T(8,128)S(1)}, u32[]{:S(2)}, u32[]{:S(2)}) collective-permute-start(f32[32,256]{1,0:T(8,128)S(1)} %get-tuple-element.253), channel_id=1, source_target_pairs={{0,2},{1,3},{2,0},{3,1},{4,6},{5,7},{6,4},{7,5},{8,10},{9,11},{10,... | collective-permute-start | bytes 98312 | tf_op jit(solution)/shard_map/ppermute | solution.py:67
  113.1 4.7 %collective-permute-start.51 = (f32[128,256]{1,0:T(8,128)S(1)}, f32[128,256]{1,0:T(8,128)S(1)}, u32[]{:S(2)}, u32[]{:S(2)}) collective-permute-start(f32[128,256]{1,0:T(8,128)S(1)} %get-tuple-element.259), channel_id=1, source_target_pairs={{0,16},{1,4},{2,18},{3,6},{4,1},{5,8},{6,3},{7,10},{8,5},{9,12},{1... | collective-permute-start | bytes 393224 | tf_op jit(solution)/shard_map/ppermute | solution.py:67
  113.8 3.1 %collective-permute-start.52 = (f32[32,256]{1,0:T(8,128)S(1)}, f32[32,256]{1,0:T(8,128)S(1)}, u32[]{:S(2)}, u32[]{:S(2)}) collective-permute-start(f32[32,256]{1,0:T(8,128)S(1)} %get-tuple-element.260), channel_id=1, source_target_pairs={{0,2},{1,3},{2,0},{3,1},{4,6},{5,7},{6,4},{7,5},{8,10},{9,11},{10,... | collective-permute-start | bytes 98312 | tf_op jit(solution)/shard_map/ppermute | solution.py:67
  118.8 11.2 %collective-permute-start.53 = (f32[2,256,256]{2,1,0:T(8,128)S(1)}, f32[2,256,256]{2,1,0:T(8,128)S(1)}, u32[]{:S(2)}, u32[]{:S(2)}) collective-permute-start(f32[2,256,256]{2,1,0:T(8,128)S(1)} %get-tuple-element.263.own), channel_id=1, source_target_pairs={{0,16},{1,2},{2,1},{3,19},{4,20},{5,6},{6,5},{7,23},{8,24},{9,10},... | collective-permute-start | bytes 1572872 | tf_op jit(solution)/shard_map/ppermute | solution.py:67
  121.9 9.6 %collective-permute-start.55 = (f32[2,64,128]{2,1,0:T(8,128)S(1)}, f32[2,64,128]{2,1,0:T(8,128)S(1)}, u32[]{:S(2)}, u32[]{:S(2)}) collective-permute-start(f32[2,64,128]{2,1,0:T(8,128)S(1)} %get-tuple-element.268), channel_id=1, source_target_pairs={{0,0},{1,2},{2,1},{3,3},{4,4},{5,6},{6,5},{7,7},{8,8},{9,10},{10,9... | collective-permute-start | bytes 196616 | tf_op jit(solution)/shard_map/ppermute | solution.py:67
  124.5 7.0 %collective-permute-start.56 = (f32[2,64,128]{2,1,0:T(8,128)S(1)}, f32[2,64,128]{2,1,0:T(8,128)S(1)}, u32[]{:S(2)}, u32[]{:S(2)}) collective-permute-start(f32[2,64,128]{2,1,0:T(8,128)S(1)} %get-tuple-element.269), channel_id=1, source_target_pairs={{0,4},{1,6},{2,5},{3,7},{4,0},{5,2},{6,1},{7,3},{8,12},{9,14},{10,... | collective-permute-start | bytes 196616 | tf_op jit(solution)/shard_map/ppermute | solution.py:67
  126.0 6.2 %collective-permute-start.57 = (f32[2,64,128]{2,1,0:T(8,128)S(1)}, f32[2,64,128]{2,1,0:T(8,128)S(1)}, u32[]{:S(2)}, u32[]{:S(2)}) collective-permute-start(f32[2,64,128]{2,1,0:T(8,128)S(1)} %get-tuple-element.270), channel_id=1, source_target_pairs={{0,8},{1,10},{2,9},{3,11},{4,12},{5,14},{6,13},{7,15},{8,0},{9,2},... | collective-permute-start | bytes 196616 | tf_op jit(solution)/shard_map/ppermute | solution.py:67
  126.9 6.5 %collective-permute-start.58 = (f32[2,64,128]{2,1,0:T(8,128)S(1)}, f32[2,64,128]{2,1,0:T(8,128)S(1)}, u32[]{:S(2)}, u32[]{:S(2)}) collective-permute-start(f32[2,64,128]{2,1,0:T(8,128)S(1)} %get-tuple-element.271), channel_id=1, source_target_pairs={{0,12},{1,14},{2,13},{3,15},{4,8},{5,10},{6,9},{7,11},{8,4},{9,6},... | collective-permute-start | bytes 196616 | tf_op jit(solution)/shard_map/ppermute | solution.py:67
  (31 other events, 52.3 us)

commit v9 on v8

--- a/solution.py
+++ b/solution.py
@@ -210,9 +210,8 @@
 
 
 def first_outer_kernel(flags, cur, prev, vel, ri, rx, rz, sums, di, dx, dz, inj, zm, ym, side,
-                       edge, mine, got, new, zo, co, yo, k0, ki, kx, kz, *lists):
+                       edge, new, zo, co, yo, k0, ki, kx, kz):
     rows = cur.shape[0]
-    trade(0, flags, mine, got, *lists)
     kz[...] = sums[...]
     ki[...] = di[...]
     here, more, more_i = edge_differences(flags, rows, ym.at[1], edge)
@@ -270,19 +269,40 @@
             give[n] = out[at]
 
 
-def source_kernel(step, flags, srow, sz, wave, out):
+def trade_kernel(stage, flags, mine, got, *outs):
+    trade(stage, flags, mine, got, *outs)
+
+
+def source_kernel(step, full, flags, src, wave, out):
     size, depth = out.shape
-    n = srow.shape[1]
-    spot = lax.broadcasted_iota(jnp.int32, (size, n), 0) == srow[...]
+    count = src.shape[0]
+    shift = (depth - 1).bit_length()
+    plane = shift + (full - 1).bit_length()
+    rows = size // COLS
+    lane = lax.broadcasted_iota(jnp.int32, (1, count), 1)
+    sub = lax.broadcasted_iota(jnp.int32, (count, 1), 0)
+    row = jnp.zeros((1, count), jnp.int32)
+    deep = jnp.zeros((count, 1), jnp.int32)
+    size_of = jnp.zeros((count, 1), F32)
+    for n in range(count):
+        cell = src[n]
+        i = jnp.right_shift(cell, plane) - flags[1] * rows
+        x = jnp.bitwise_and(jnp.right_shift(cell, shift), full - 1)
+        x = x - (2 * flags[3] + flags[0]) * COLS
+        ok = (i >= 0) & (i < rows) & (x >= 0) & (x < COLS)
+        row = jnp.where(lane == n, jnp.where(ok, i * COLS + x, -1), row)
+        deep = jnp.where(sub == n, jnp.bitwise_and(cell, depth - 1), deep)
+        size_of = jnp.where(sub == n, wave[step, n], size_of)
+    spot = lax.broadcasted_iota(jnp.int32, (size, count), 0) == row
     spot = spot.astype(F32).astype(BF16)
     high, low = split(jnp.where(
-        lax.broadcasted_iota(jnp.int32, (n, depth), 1) == sz[...], wave[:, step : step + 1], 0.0))
+        lax.broadcasted_iota(jnp.int32, (count, depth), 1) == deep, size_of, 0.0))
     out[...] = mm(spot, high) + mm(spot, low)
 
 
-def forward_inner_kernel(step, flags, cur, prev, k0, ki, kx, kz, cm, near, deep, srow, sz, wave,
+def forward_inner_kernel(step, full, flags, src, wave, cur, prev, k0, ki, kx, kz, cm, near, deep,
                          before, part, change):
-    source_kernel(step, flags, srow, sz, wave, change)
+    source_kernel(step, full, flags, src, wave, change)
     inner(cur, prev, k0, ki, kx, kz, cm, near, deep, change, part)
     change[...] = (cur[...] - prev[...]) - (prev[...] - before[...])
 
@@ -303,13 +323,35 @@
         rims(flags, new, zo, co, yo)
 
 
-def lists_kernel(flags, lists, spot, pick, at, obs):
+def pack_kernel(flags, counts, cells, traces, cells_out, lists, give, counts_v, cells_v, traces_v,
+                sems):
+    pairs = ((counts, counts_v), (cells, cells_v), (traces, traces_v))
+    copies = [pltpu.make_async_copy(a, b, sems.at[n]) for n, (a, b) in enumerate(pairs)]
+    for copy in copies:
+        copy.start()
+    for copy in copies:
+        copy.wait()
+    subs, n = counts.shape[1], cells.shape[1]
+    shape = (subs, n)
+    lane = lax.broadcasted_iota(jnp.int32, shape, 1)
+    mine = lane // CAP == lax.broadcasted_iota(jnp.int32, shape, 0)
+    live = mm(counts_v[...].astype(F32).astype(BF16), mine.astype(F32).astype(BF16))
+    slot = jnp.bitwise_and(lane[0:1], CAP - 1)
+    cells_out[...] = jnp.where(slot.astype(F32) < live, cells_v[...].astype(F32), -1.0)
+    for m in range(subs):
+        q, y, c = m >> 2, (m >> 1) & 1, m & 1
+        start = ((2 * q + c) * 2 + y) * CAP
+        tile = traces_v[:, start // 128 * 128 : start // 128 * 128 + 128]
+        lists[m] = pltpu.roll(tile, (128 - start % 128) % 128, axis=1) if start % 128 else tile
+    for n, at in other_half(0, flags, subs):
+        give[n] = lists[at]
+
+
+def lists_kernel(flags, lists, own, got, spot, pick, at, obs):
     size, n = spot.shape
     depth = at.shape[1]
     subs, steps = lists.shape[0], obs.shape[1]
-    whole = n // 128
-    cell = jnp.concatenate(
-        [jnp.sum(lists[:, m, :], axis=0, keepdims=True) for m in range(whole)], axis=1)
+    cell = jnp.where(flags[0] == flags[1], own[...], got[...])
     along = jnp.floor((cell + 0.5) * (1.0 / depth))
     same = lax.broadcasted_iota(jnp.int32, (n, n), 0) == lax.broadcasted_iota(jnp.int32, (n, n), 1)
 
@@ -322,9 +364,9 @@
     pick[...] = hot.astype(F32).astype(BF16)
     hot = lax.broadcasted_iota(jnp.int32, (n, depth), 1) == column(cell - along * depth)
     at[...] = hot.astype(F32)
-    traces = lists[:, whole, :]
-    for k in range(CAP):
-        obs[k * subs : k * subs + subs, :] = traces[:, k * steps : k * steps + steps]
+    traces = lists[...].reshape(subs * steps, 128).T[0:CAP]
+    for s in range(subs):
+        obs[s * CAP : s * CAP + CAP, :] = traces[:, s * steps : s * steps + steps]
 
 
 def injection(t, state, spot, pick, at, obs):
@@ -413,17 +455,17 @@
     return jax.ShapeDtypeStruct(shape, F32)
 
 
-def call(kernel, name, outs, *args, weight=0, far=0):
-    specs = [pl.BlockSpec(memory_space=pltpu.SMEM)]
+def call(kernel, name, outs, *args, weight=0, far=0, scalars=0, scratch=()):
+    specs = [pl.BlockSpec(memory_space=pltpu.SMEM)] * (1 + scalars)
     specs += [pl.BlockSpec(memory_space=pl.ANY)] * far
-    specs += [pl.BlockSpec(memory_space=pltpu.VMEM)] * (len(args) - 1 - far)
+    specs += [pl.BlockSpec(memory_space=pltpu.VMEM)] * (len(args) - 1 - scalars - far)
     return pl.pallas_call(
         kernel,
         name=name,
         out_shape=outs,
         in_specs=specs,
         out_specs=[pl.BlockSpec(memory_space=pltpu.VMEM)] * len(outs),
-        scratch_shapes=[pltpu.SemaphoreType.DMA((far,))] if far else [],
+        scratch_shapes=list(scratch) + ([pltpu.SemaphoreType.DMA((far,))] if far else []),
         compiler_params=pltpu.CompilerParams(vmem_limit_bytes=VMEM_BYTES),
         cost_estimate=pl.CostEstimate(
             flops=1000, bytes_accessed=1000 + int(weight * 3_600_000), transcendentals=0),
@@ -480,78 +522,73 @@
     got = [send(v, swap_perm) for v in (log_density, fwd_now)]
     stacked = jnp.stack([velocity, fwd_before])
     got_model = send(stacked, swap_perm)
-    plane = nx * cols * depth
-    src_i = src_cell // plane - y * rows
-    src_x = src_cell // depth % (nx * cols) - (2 * q + c) * cols
-    ok = (src_i >= 0) & (src_i < rows) & (src_x >= 0) & (src_x < cols)
-    srow = jnp.where(ok, src_i * cols + src_x, -1)[None, :]
-    sz = (src_cell % depth)[:, None]
-    wave = wavelet.T
-
-    slots = subs * CAP
-    rec_counts, rec_cells, observed = lax.optimization_barrier(
-        (rec_counts, rec_cells, observed, stacked))[:3]
-    live = jnp.arange(CAP)[None, :] < rec_counts[0][:, None]
-    cells = jnp.where(live, rec_cells[0].reshape(subs, CAP), -1).T.reshape(1, slots).astype(F32)
-    worker = (2 * q + c) * 2 + y
-    cells = jnp.where(jnp.arange(subs)[:, None] == worker, cells, 0.0)
-    traces = observed.reshape(steps, nq, 2, 2, CAP).transpose(1, 3, 2, 4, 0).reshape(subs, CAP * steps)
-    spare = jnp.zeros((subs, 128 - CAP * steps), F32)
-    lists = jnp.concatenate([cells, traces, spare], axis=1).reshape(subs, -1, 128)
-    give = lax.dynamic_index_in_dim(lists.reshape(subs // 2, 2, -1, 128), 1 - c, 1, keepdims=False)
-    inj, = call(functools.partial(source_kernel, 0), "source", [field], after(flags, stacked), srow,
-                sz, wave, weight=0.6)
-    give, flags, inj = lax.optimization_barrier((give, flags, inj))
-    got_list = send(give, stages[0][0])
-
+    full = nx * cols
+    inj, = call(functools.partial(source_kernel, 0, full), "source", [field], flags, src_cell, wavelet,
+                weight=0.7, scalars=2)
+    flags_in, inj = lax.optimization_barrier((flags, inj))
     density, p_now, *out = call(settle_kernel, "settle",
                                 [field, field] + [shaped(2, *r.shape) for r in rim],
-                                flags, log_density, fwd_now, *got, far=2)
+                                flags_in, log_density, fwd_now, *got, far=2)
     zm, cm, ym = halo(*out)
-    got_adjoint = send(jnp.stack([after(adj_now, density), after(adj_before, density)]), swap_perm)
+    got_adjoint = send(jnp.stack([after(adj_now, ym), after(adj_before, ym)]), swap_perm)
     vel, p_before = call(settle_pair_kernel, "settle_model", [field, field],
                          flags, velocity, fwd_before, got_model, weight=0.6, far=2)
     parts = call(first_inner_kernel, "first_inner", [field] * 7, flags, density, p_now, cm,
                  near, deep, weight=1.3)
 
-    entries, half_entries = shaped(*lists.shape), shaped(*give.shape)
-    new, zo, co, yo, k0, ki, kx, kz, lists, give = call(
-        first_outer_kernel, "first_outer", [field] + rim + [field] * 4 + [entries, half_entries],
-        flags, p_now, p_before, vel, *parts, inj, zm, ym, side, edge, lists, got_list)
+    new, zo, co, yo, k0, ki, kx, kz = call(
+        first_outer_kernel, "first_outer", [field] + rim + [field] * 4,
+        flags, p_now, p_before, vel, *parts, inj, zm, ym, side, edge)
     model = (k0, ki, kx, kz)
     states = [p_before, p_now, new]
     changes = []
     zm, cm, ym = halo(zo, co, yo)
     double = 1
+
+    slots = subs * CAP
+    entries, half_entries = shaped(subs, steps, 128), shaped(subs // 2, steps, 128)
+    cells, lists, give = call(
+        pack_kernel, "pack", [shaped(1, slots), entries, half_entries], after(flags, k0), rec_counts,
+        rec_cells, observed, weight=0.8, far=3,
+        scratch=[pltpu.VMEM(rec_counts.shape, jnp.int32), pltpu.VMEM(rec_cells.shape, jnp.int32),
+                 pltpu.VMEM(observed.shape, F32)])
     for t in range(1, steps):
         cur, prev, before = states[:-4:-1]
-        stage = t if t < len(stages) else None
-        extra = [lists, send(give, stages[t][0])] if stage is not None else []
+        stage = t - 1 if t <= min(len(stages), steps - 2) else None
+        extra = [lists, send(give, stages[stage][0])] if stage is not None else []
         part, change = call(
-            functools.partial(forward_inner_kernel, t), "forward_inner", [field, field], flags, cur,
-            prev, *model, cm, near, deep, srow, sz, wave, before, weight=1.2)
+            functools.partial(forward_inner_kernel, t, full), "forward_inner", [field, field], flags,
+            src_cell, wavelet, cur, prev, *model, cm, near, deep, before, weight=1.2, scalars=2)
         changes.append(change)
         args = [flags, part, k0, ki, kx, zm, ym, side, edge]
         if t == steps - 1:
             u_part, = call(adjoint_first_kernel, "adjoint_first", [field], flags, u_now, u_before,
                            *model, u_cm, near, deep, weight=1.1)
+            for n in range(steps - 2, len(stages)):
+                lists, *give = call(
+                    functools.partial(trade_kernel, n), "trade",
+                    [entries] + ([half_entries] if n + 1 < len(stages) else []), flags, lists,
+                    send(give, stages[n][0]))
+                give = give[0] if give else None
             receivers = call(
                 lists_kernel, "lists",
                 [jax.ShapeDtypeStruct((size, slots), BF16),
                  jax.ShapeDtypeStruct((slots, size), BF16), shaped(slots, depth),
-                 shaped(slots, steps)], flags, lists, weight=0.8)
+                 shaped(slots, steps)], flags, lists, cells, got_cells, weight=0.8)
             new, u_new, *out = call(
                 functools.partial(turn_kernel, t), "turn", [field, field] + rim, *args, u_part,
                 u_zm, u_ym, *receivers)
             states.append(new)
             break
+        if t == len(stages) - 2:
+            got_cells = send(after(cells, part), swap_perm)
         if t == double:
             u_now, u_before = call(settle_pair_kernel, "settle_adjoint", [field, field], flags,
                                    adj_now, adj_before, got_adjoint, weight=0.6, far=2)
             args.append(u_now)
         outs = [field] + ([shaped(2, *r.shape) for r in rim] if t == double else rim)
         if extra:
-            outs = outs + [entries] + ([half_entries] if t + 1 < len(stages) else [])
+            outs = outs + [entries] + ([half_entries] if t < len(stages) else [])
         new, *out = call(functools.partial(outer_kernel, stage, t == double), "forward_outer", outs,
                          *args, *extra)
         if extra:

time: 136 us -> 132 us (0.971)
  local copies, waits for them, and re-layouts: 5.17 us -> 1.18 us
  other arithmetic: 4.4 us -> 2.17 us
  waiting for transfers between devices: 28.1 us -> 29.5 us
    unnamed x41 -> x38, local copies, waits for them, and re-layouts: 3.15 us -> 1.1 us
    ppermute x59 -> x60, waiting for transfers between devices: 28.1 us -> 29.5 us  [send(): return lax.ppermute(value, ALL, pairs)]
    ppermute x59 -> x60, starting transfers between devices: 51.9 us -> 53.2 us  [send(): return lax.ppermute(value, ALL, pairs)]
    pallas_call x39 -> x40, Pallas kernels: 44.4 us -> 44.9 us  [call(): pl.pallas_call(kernel, name=name, out_shape=outs, in_specs=specs, out_spe...]
  transfers between devices with their start and end apart: 59 -> 60, of which waited for: 31 -> 30; matrix products, arithmetic and copies ran while one was open for 5% -> 2% of each run, Pallas kernels for 22% -> 23%
where the time goes in v9:
time: 132 us
  starting transfers between devices  53.2 us (40%)
  Pallas kernels  44.9 us (34%)
  waiting for transfers between devices  29.5 us (22%)
  other arithmetic  2.17 us (2%)
    ppermute x60, starting transfers between devices, send(): return lax.ppermute(value, ALL, pairs)  53.2 us
    pallas_call x40, Pallas kernels, call(): pl.pallas_call(kernel, name=name, out_shape=outs, in_specs=specs, out_spe...  44.9 us
    ppermute x60, waiting for transfers between devices, send(): return lax.ppermute(value, ALL, pairs)  29.5 us
  transfers between devices with their start and end apart: 60, of which 30 were waited for; matrix products, arithmetic and copies ran while one was open for 2% of the time, Pallas kernels for 23%

profile of v9, /device:TPU:1, one launch (start us, length us, event | category | flops | bytes accessed | tf_op | source)
XLA Modules:
  0.0 132.1 jit_solution(4961208649566102115)
XLA Ops:
  0.6 2.7 %collective-permute-start.1 = (f32[256,256]{1,0:T(8,128)}, f32[256,256]{1,0:T(8,128)S(1)}, u32[]{:S(2)}, u32[]{:S(2)}) collective-permute-start(f32[256,256]{1,0:T(8,128)} %bitcast.28), channel_id=1, source_target_pairs={{0,16},{1,2},{2,1},{3,19},{4,20},{5,6},{6,5},{7,23},{8,24},{9,10},... | collective-permute-start | bytes 786440 | tf_op jit(solution)/shard_map/ppermute | solution.py:67
  3.4 1.9 %pad_maximum_fusion = f32[2,256,256]{2,1,0:T(8,128)} fusion(f32[1,256,256]{2,1,0:T(8,128)} %bitcast.20, f32[1,256,256]{2,1,0:T(8,128)} %bitcast.18), kind=kLoop, calls=%fused_computation | loop fusion | flops 131072 | bytes 1048576 | tf_op jit(solution)/shard_map/stack | solution.py:523
  5.3 1.7 %collective-permute-start.2 = (f32[2,256,256]{2,1,0:T(8,128)}, f32[2,256,256]{2,1,0:T(8,128)S(1)}, u32[]{:S(2)}, u32[]{:S(2)}) collective-permute-start(f32[2,256,256]{2,1,0:T(8,128)} %pad_maximum_fusion), channel_id=1, source_target_pairs={{0,16},{1,2},{2,1},{3,19},{4,20},{5,6},{6,5},{7,23},{8,24},{9,10},... | collective-permute-start | bytes 1572872 | tf_op jit(solution)/shard_map/ppermute | solution.py:67
  8.7 2.0 %collective-permute-done.recv_a = f32[256,256]{1,0:T(8,128)S(1)} collective-permute-done((f32[256,256]{1,0:T(8,128)}, f32[256,256]{1,0:T(8,128)S(1)}, u32[]{:S(2)}, u32[]{:S(2)}) %collective-permute-start) | collective-permute-done | bytes 262176 | tf_op jit(solution)/shard_map/ppermute | solution.py:67
  12.1 1.3 collective-permute-start.3
  13.4 1.3 collective-permute-start.4
  14.7 2.0 %collective-permute-done.5.ym = f32[2,32,256]{2,1,0:T(8,128)S(1)} collective-permute-done((f32[2,32,256]{2,1,0:T(8,128)S(1)}, f32[2,32,256]{2,1,0:T(8,128)S(1)}, u32[]{:S(2)}, u32[]{:S(2)}) %collective-permute-start.5) | collective-permute-done | bytes 65568 | tf_op jit(solution)/shard_map/ppermute | solution.py:67
  16.8 1.3 collective-permute-start.9
  19.4 1.3 %first_inner.1 = (f32[256,256]{1,0:T(8,128)S(1)}, f32[256,256]{1,0:T(8,128)S(1)}, f32[256,256]{1,0:T(8,128)S(1)}, f32[256,256]{1,0:T(8,128)S(1)}, f32[256,256]{1...) custom-call(s32[8]{0:T(128)S(1)} %stack.41.flags, f32[256,256]{1,0:T(8,128)S(1)} %get-tuple-element.142.lr, ...), custom_call_target="tpu_custom_call" | custom-call | flops 1000 | bytes 4681000 | tf_op jit(solution)/shard_map/first_inner/pallas_call | solution.py:462
  20.7 1.1 first_outer.1
  21.8 1.7 %collective-permute-start.6 = (f32[128,256]{1,0:T(8,128)S(1)}, f32[128,256]{1,0:T(8,128)S(1)}, u32[]{:S(2)}, u32[]{:S(2)}) collective-permute-start(f32[128,256]{1,0:T(8,128)S(1)} %get-tuple-element.159), channel_id=1, source_target_pairs={{0,1},{1,0},{2,3},{3,2},{4,5},{5,4},{6,7},{7,6},{8,9},{9,8},{10,11... | collective-permute-start | bytes 393224 | tf_op jit(solution)/shard_map/ppermute | solution.py:67
  23.6 1.3 collective-permute-start.7
  26.7 1.3 %forward_inner.7 = (f32[256,256]{1,0:T(8,128)S(1)}, f32[256,256]{1,0:T(8,128)S(1)}) custom-call(s32[8]{0:T(128)S(1)} %stack.41.flags, s32[16]{0:T(128)S(1)} %copy-done.8, f32[8,16]{1,0:T(8,128)S(1)} %copy-done.5, f32[256,256]{1,0:T(8,128)S(1)} %get-tuple-element.154.cur.prev.before.state, f32[256,256]{1,0:T(8,128)S(1)} %get-tuple-element.139.cur.prev.before, ...), custom_call_target="tpu_custom_call" | custom-call | flops 1000 | bytes 4321000 | tf_op jit(solution)/shard_map/forward_inner/pallas_call | solution.py:462
  30.2 1.3 collective-permute-start.12
  32.9 1.4 %forward_inner.8 = (f32[256,256]{1,0:T(8,128)S(1)}, f32[256,256]{1,0:T(8,128)S(1)}) custom-call(s32[8]{0:T(128)S(1)} %stack.41.flags, s32[16]{0:T(128)S(1)} %copy-done.8, f32[8,16]{1,0:T(8,128)S(1)} %copy-done.5, f32[256,256]{1,0:T(8,128)S(1)} %get-tuple-element.169.cur.prev.before.state, f32[256,256]{1,0:T(8,128)S(1)} %get-tuple-element.154.cur.prev.before.state, ...), custom_call_target="tpu_custom_call" | custom-call | flops 1000 | bytes 4321000 | tf_op jit(solution)/shard_map/forward_inner/pallas_call | solution.py:462
  34.3 1.7 %collective-permute-done.14.rest_1_ = f32[8,8,128]{2,1,0:T(8,128)S(1)} collective-permute-done((f32[8,8,128]{2,1,0:T(8,128)S(1)}, f32[8,8,128]{2,1,0:T(8,128)S(1)}, u32[]{:S(2)}, u32[]{:S(2)}) %collective-permute-start.14) | collective-permute-done | bytes 32800 | tf_op jit(solution)/shard_map/ppermute | solution.py:67
  39.2 1.3 collective-permute-start.18
  40.5 1.3 %forward_inner.9 = (f32[256,256]{1,0:T(8,128)S(1)}, f32[256,256]{1,0:T(8,128)S(1)}) custom-call(s32[8]{0:T(128)S(1)} %stack.41.flags, s32[16]{0:T(128)S(1)} %copy-done.8, f32[8,16]{1,0:T(8,128)S(1)} %copy-done.5, f32[256,256]{1,0:T(8,128)S(1)} %get-tuple-element.176.cur.prev.before.state, f32[256,256]{1,0:T(8,128)S(1)} %get-tuple-element.169.cur.prev.before.state, ...), custom_call_target="tpu_custom_call" | custom-call | flops 1000 | bytes 4321000 | tf_op jit(solution)/shard_map/forward_inner/pallas_call | solution.py:462
  43.1 1.3 collective-permute-start.19
  46.0 2.3 %collective-permute-start.22 = (f32[8,8,128]{2,1,0:T(8,128)S(1)}, f32[8,8,128]{2,1,0:T(8,128)S(1)}, u32[]{:S(2)}, u32[]{:S(2)}) collective-permute-start(f32[8,8,128]{2,1,0:T(8,128)S(1)} %get-tuple-element.189), channel_id=1, source_target_pairs={{0,8},{1,9},{2,10},{3,11},{4,12},{5,13},{6,14},{7,15},{8,0},{9,1},... | collective-permute-start | bytes 98312 | tf_op jit(solution)/shard_map/ppermute | solution.py:67
  48.3 1.3 %forward_inner.10 = (f32[256,256]{1,0:T(8,128)S(1)}, f32[256,256]{1,0:T(8,128)S(1)}) custom-call(s32[8]{0:T(128)S(1)} %stack.41.flags, s32[16]{0:T(128)S(1)} %copy-done.8, f32[8,16]{1,0:T(8,128)S(1)} %copy-done.5, f32[256,256]{1,0:T(8,128)S(1)} %get-tuple-element.183.cur.prev.before.state, f32[256,256]{1,0:T(8,128)S(1)} %get-tuple-element.176.cur.prev.before.state, ...), custom_call_target="tpu_custom_call" | custom-call | flops 1000 | bytes 4321000 | tf_op jit(solution)/shard_map/forward_inner/pallas_call | solution.py:462
  50.6 2.4 %collective-permute-start.23 = (f32[128,256]{1,0:T(8,128)S(1)}, f32[128,256]{1,0:T(8,128)S(1)}, u32[]{:S(2)}, u32[]{:S(2)}) collective-permute-start(f32[128,256]{1,0:T(8,128)S(1)} %get-tuple-element.191), channel_id=1, source_target_pairs={{0,1},{1,0},{2,3},{3,2},{4,5},{5,4},{6,7},{7,6},{8,9},{9,8},{10,11... | collective-permute-start | bytes 393224 | tf_op jit(solution)/shard_map/ppermute | solution.py:67
  53.9 1.3 %forward_inner.11 = (f32[256,256]{1,0:T(8,128)S(1)}, f32[256,256]{1,0:T(8,128)S(1)}) custom-call(s32[8]{0:T(128)S(1)} %stack.41.flags, s32[16]{0:T(128)S(1)} %copy-done.8, f32[8,16]{1,0:T(8,128)S(1)} %copy-done.5, f32[256,256]{1,0:T(8,128)S(1)} %get-tuple-element.190.cur.prev.before.state, f32[256,256]{1,0:T(8,128)S(1)} %get-tuple-element.183.cur.prev.before.state, ...), custom_call_target="tpu_custom_call" | custom-call | flops 1000 | bytes 4321000 | tf_op jit(solution)/shard_map/forward_inner/pallas_call | solution.py:462
  55.8 1.8 %collective-permute-done.24.zm = f32[128,256]{1,0:T(8,128)S(1)} collective-permute-done((f32[128,256]{1,0:T(8,128)S(1)}, f32[128,256]{1,0:T(8,128)S(1)}, u32[]{:S(2)}, u32[]{:S(2)}) %collective-permute-start.24) | collective-permute-done | bytes 131104 | tf_op jit(solution)/shard_map/ppermute | solution.py:67
  60.3 1.3 %forward_inner.12 = (f32[256,256]{1,0:T(8,128)S(1)}, f32[256,256]{1,0:T(8,128)S(1)}) custom-call(s32[8]{0:T(128)S(1)} %stack.41.flags, s32[16]{0:T(128)S(1)} %copy-done.8, f32[8,16]{1,0:T(8,128)S(1)} %copy-done.5, f32[256,256]{1,0:T(8,128)S(1)} %get-tuple-element.195.cur.prev.rest_2_.state, f32[256,256]{1,0:T(8,128)S(1)} %get-tuple-element.190.cur.prev.before.state, ...), custom_call_target="tpu_custom_call" | custom-call | flops 1000 | bytes 4321000 | tf_op jit(solution)/shard_map/forward_inner/pallas_call | solution.py:462
  66.2 1.4 %collective-permute-start.32 = (f32[1,128]{1,0:T(1,128)S(1)}, f32[1,128]{1,0:T(1,128)S(1)}, u32[]{:S(2)}, u32[]{:S(2)}) collective-permute-start(f32[1,128]{1,0:T(1,128)S(1)} %get-tuple-element.208.own), channel_id=1, source_target_pairs={{0,16},{1,2},{2,1},{3,19},{4,20},{5,6},{6,5},{7,23},{8,24},{9,10},... | collective-permute-start | bytes 1544 | tf_op jit(solution)/shard_map/ppermute | solution.py:67
  67.6 1.1 adjoint_first.1.u_part
  70.3 1.3 %forward_inner.13 = (f32[256,256]{1,0:T(8,128)S(1)}, f32[256,256]{1,0:T(8,128)S(1)}) custom-call(s32[8]{0:T(128)S(1)} %stack.41.flags, s32[16]{0:T(128)S(1)} %copy-done.8, f32[8,16]{1,0:T(8,128)S(1)} %copy-done.5, f32[256,256]{1,0:T(8,128)S(1)} %get-tuple-element.200.cur.state.rest_1_, f32[256,256]{1,0:T(8,128)S(1)} %get-tuple-element.195.cur.prev.rest_2_.state, ...), custom_call_target="tpu_custom_call" | custom-call | flops 1000 | bytes 4321000 | tf_op jit(solution)/shard_map/forward_inner/pallas_call | solution.py:462
  71.7 1.5 %turn.1 = (f32[256,256]{1,0:T(8,128)S(1)}, f32[256,256]{1,0:T(8,128)S(1)}, f32[128,256]{1,0:T(8,128)S(1)}, f32[128,256]{1,0:T(8,128)S(1)}, f32[32,256]{1,0:T(8,128)S(1)}) custom-call(s32[8]{0:T(128)S(1)} %stack.41.flags, f32[256,256]{1,0:T(8,128)S(1)} %get-tuple-element.202.part, f32[256,256]{1,0:T(8,128)S(1)} %get-tuple-element.155.k0, ...), custom_call_target="tpu_custom_call" | custom-call | flops 1000 | bytes 1000 | tf_op jit(solution)/shard_map/turn/pallas_call | solution.py:462
  75.2 1.7 %adjoint_inner.7 = (f32[256,256]{1,0:T(8,128)S(1)}, f32[256,256]{1,0:T(8,128)S(1)}) custom-call(s32[8]{0:T(128)S(1)} %stack.41.flags, f32[256,256]{1,0:T(8,128)S(1)} %get-tuple-element.213.cur.prev, f32[256,256]{1,0:T(8,128)S(1)} %get-tuple-element.165.rest_0_.cur.prev, f32[256,256]{1,0:T(8,128)S(1)} %get-tuple-element.155.k0, ...), custom_call_target="tpu_custom_call" | custom-call | flops 1000 | bytes 5401000 | tf_op jit(solution)/shard_map/adjoint_inner/pallas_call | solution.py:462
  76.8 1.1 collective-permute-done.35.ym
  81.1 1.6 %adjoint_inner.8 = (f32[256,256]{1,0:T(8,128)S(1)}, f32[256,256]{1,0:T(8,128)S(1)}) custom-call(s32[8]{0:T(128)S(1)} %stack.41.flags, f32[256,256]{1,0:T(8,128)S(1)} %get-tuple-element.219.cur.prev, f32[256,256]{1,0:T(8,128)S(1)} %get-tuple-element.213.cur.prev, f32[256,256]{1,0:T(8,128)S(1)} %get-tuple-element.155.k0, ...), custom_call_target="tpu_custom_call" | custom-call | flops 1000 | bytes 5401000 | tf_op jit(solution)/shard_map/adjoint_inner/pallas_call | solution.py:462
  82.7 1.2 collective-permute-done.38.ym
  87.1 1.6 %adjoint_inner.9 = (f32[256,256]{1,0:T(8,128)S(1)}, f32[256,256]{1,0:T(8,128)S(1)}) custom-call(s32[8]{0:T(128)S(1)} %stack.41.flags, f32[256,256]{1,0:T(8,128)S(1)} %get-tuple-element.226.cur.prev, f32[256,256]{1,0:T(8,128)S(1)} %get-tuple-element.219.cur.prev, f32[256,256]{1,0:T(8,128)S(1)} %get-tuple-element.155.k0, ...), custom_call_target="tpu_custom_call" | custom-call | flops 1000 | bytes 5401000 | tf_op jit(solution)/shard_map/adjoint_inner/pallas_call | solution.py:462
  88.6 1.2 collective-permute-done.41.ym
  93.0 1.8 %adjoint_inner.10 = (f32[256,256]{1,0:T(8,128)S(1)}, f32[256,256]{1,0:T(8,128)S(1)}) custom-call(s32[8]{0:T(128)S(1)} %stack.41.flags, f32[256,256]{1,0:T(8,128)S(1)} %get-tuple-element.233.cur.prev, f32[256,256]{1,0:T(8,128)S(1)} %get-tuple-element.226.cur.prev, f32[256,256]{1,0:T(8,128)S(1)} %get-tuple-element.155.k0, ...), custom_call_target="tpu_custom_call" | custom-call | flops 1000 | bytes 5401000 | tf_op jit(solution)/shard_map/adjoint_inner/pallas_call | solution.py:462
  99.0 1.6 %adjoint_inner.11 = (f32[256,256]{1,0:T(8,128)S(1)}, f32[256,256]{1,0:T(8,128)S(1)}) custom-call(s32[8]{0:T(128)S(1)} %stack.41.flags, f32[256,256]{1,0:T(8,128)S(1)} %get-tuple-element.240.cur.prev, f32[256,256]{1,0:T(8,128)S(1)} %get-tuple-element.233.cur.prev, f32[256,256]{1,0:T(8,128)S(1)} %get-tuple-element.155.k0, ...), custom_call_target="tpu_custom_call" | custom-call | flops 1000 | bytes 5401000 | tf_op jit(solution)/shard_map/adjoint_inner/pallas_call | solution.py:462
  100.6 1.2 collective-permute-done.47.ym
  104.9 1.6 %adjoint_inner.12 = (f32[256,256]{1,0:T(8,128)S(1)}, f32[256,256]{1,0:T(8,128)S(1)}) custom-call(s32[8]{0:T(128)S(1)} %stack.41.flags, f32[256,256]{1,0:T(8,128)S(1)} %get-tuple-element.247.cur.prev, f32[256,256]{1,0:T(8,128)S(1)} %get-tuple-element.240.cur.prev, f32[256,256]{1,0:T(8,128)S(1)} %get-tuple-element.155.k0, ...), custom_call_target="tpu_custom_call" | custom-call | flops 1000 | bytes 5401000 | tf_op jit(solution)/shard_map/adjoint_inner/pallas_call | solution.py:462
  106.5 1.2 collective-permute-done.50.ym
  110.9 1.6 %adjoint_inner.13 = (f32[256,256]{1,0:T(8,128)S(1)}, f32[256,256]{1,0:T(8,128)S(1)}) custom-call(s32[8]{0:T(128)S(1)} %stack.41.flags, f32[256,256]{1,0:T(8,128)S(1)} %get-tuple-element.254.cur.prev, f32[256,256]{1,0:T(8,128)S(1)} %get-tuple-element.247.cur.prev, f32[256,256]{1,0:T(8,128)S(1)} %get-tuple-element.155.k0, ...), custom_call_target="tpu_custom_call" | custom-call | flops 1000 | bytes 5401000 | tf_op jit(solution)/shard_map/adjoint_inner/pallas_call | solution.py:462
  112.5 1.2 collective-permute-done.53.ym
  118.7 2.6 %collective-permute-start.56 = (f32[2,64,128]{2,1,0:T(8,128)S(1)}, f32[2,64,128]{2,1,0:T(8,128)S(1)}, u32[]{:S(2)}, u32[]{:S(2)}) collective-permute-start(f32[2,64,128]{2,1,0:T(8,128)S(1)} %get-tuple-element.268), channel_id=1, source_target_pairs={{0,0},{1,2},{2,1},{3,3},{4,4},{5,6},{6,5},{7,7},{8,8},{9,10},{10,9... | collective-permute-start | bytes 196616 | tf_op jit(solution)/shard_map/ppermute | solution.py:67
  121.3 1.5 %collective-permute-start.57 = (f32[2,64,128]{2,1,0:T(8,128)S(1)}, f32[2,64,128]{2,1,0:T(8,128)S(1)}, u32[]{:S(2)}, u32[]{:S(2)}) collective-permute-start(f32[2,64,128]{2,1,0:T(8,128)S(1)} %get-tuple-element.269), channel_id=1, source_target_pairs={{0,4},{1,6},{2,5},{3,7},{4,0},{5,2},{6,1},{7,3},{8,12},{9,14},{10,... | collective-permute-start | bytes 196616 | tf_op jit(solution)/shard_map/ppermute | solution.py:67
  123.8 3.1 %collective-permute-start.59 = (f32[2,64,128]{2,1,0:T(8,128)S(1)}, f32[2,64,128]{2,1,0:T(8,128)S(1)}, u32[]{:S(2)}, u32[]{:S(2)}) collective-permute-start(f32[2,64,128]{2,1,0:T(8,128)S(1)} %get-tuple-element.271), channel_id=1, source_target_pairs={{0,12},{1,14},{2,13},{3,15},{4,8},{5,10},{6,9},{7,11},{8,4},{9,6},... | collective-permute-start | bytes 196616 | tf_op jit(solution)/shard_map/ppermute | solution.py:67
  126.9 1.4 %select.7 = (f32[256,256]{1,0:T(8,128)}, f32[256,256]{1,0:T(8,128)}) custom-call(s32[8]{0:T(128)S(1)} %stack.41.flags, f32[2,256,256]{2,1,0:T(8,128)S(1)} %get-tuple-element.263.own, f32[2,256,256]{2,1,0:T(8,128)S(1)} %collective-permute-done.54.recv), custom_call_target="tpu_custom_call" | custom-call | flops 1000 | bytes 4321000 | tf_op jit(solution)/shard_map/select/pallas_call | solution.py:462
  129.1 1.2 collective-permute-done.59.refs_3_
  130.2 1.9 %filter.1 = f32[32,32,64]{2,1,0:T(8,128)} custom-call(s32[8]{0:T(128)S(1)} %stack.41.flags, f32[2,64,128]{2,1,0:T(8,128)S(1)} %collective-permute-done.56.refs_0_, f32[2,64,128]{2,1,0:T(8,128)S(1)} %collective-permute-done.57.refs_1_, f32[2,64,128]{2,1,0:T(8,128)S(1)} %collective-permute-done.58.refs_2_, f32[2,64,128]{2,1,0:T(8,128)S(1)} %collective-permute-done.59.refs_3_), custom_call_target="tpu_custom_call" | custom-call | flops 1000 | bytes 1000 | tf_op jit(solution)/shard_map/filter/pallas_call | solution.py:462
  (158 shorter events, 55.8 us)
Async XLA Ops:
  0.6 8.1 %collective-permute-start.1 = (f32[256,256]{1,0:T(8,128)}, f32[256,256]{1,0:T(8,128)S(1)}, u32[]{:S(2)}, u32[]{:S(2)}) collective-permute-start(f32[256,256]{1,0:T(8,128)} %bitcast.28), channel_id=1, source_target_pairs={{0,16},{1,2},{2,1},{3,19},{4,20},{5,6},{6,5},{7,23},{8,24},{9,10},... | collective-permute-start | bytes 786440 | tf_op jit(solution)/shard_map/ppermute | solution.py:67
  3.3 7.4 %collective-permute-start = (f32[256,256]{1,0:T(8,128)}, f32[256,256]{1,0:T(8,128)S(1)}, u32[]{:S(2)}, u32[]{:S(2)}) collective-permute-start(f32[256,256]{1,0:T(8,128)} %bitcast.26), channel_id=1, source_target_pairs={{0,16},{1,2},{2,1},{3,19},{4,20},{5,6},{6,5},{7,23},{8,24},{9,10},... | collective-permute-start | bytes 786440 | tf_op jit(solution)/shard_map/ppermute | solution.py:67
  5.3 13.0 %collective-permute-start.2 = (f32[2,256,256]{2,1,0:T(8,128)}, f32[2,256,256]{2,1,0:T(8,128)S(1)}, u32[]{:S(2)}, u32[]{:S(2)}) collective-permute-start(f32[2,256,256]{2,1,0:T(8,128)} %pad_maximum_fusion), channel_id=1, source_target_pairs={{0,16},{1,2},{2,1},{3,19},{4,20},{5,6},{6,5},{7,23},{8,24},{9,10},... | collective-permute-start | bytes 1572872 | tf_op jit(solution)/shard_map/ppermute | solution.py:67
  11.4 5.3 %collective-permute-start.5 = (f32[2,32,256]{2,1,0:T(8,128)S(1)}, f32[2,32,256]{2,1,0:T(8,128)S(1)}, u32[]{:S(2)}, u32[]{:S(2)}) collective-permute-start(f32[2,32,256]{2,1,0:T(8,128)S(1)} %get-tuple-element.153), channel_id=1, source_target_pairs={{0,2},{1,3},{2,0},{3,1},{4,6},{5,7},{6,4},{7,5},{8,10},{9,11},{10,... | collective-permute-start | bytes 196616 | tf_op jit(solution)/shard_map/ppermute | solution.py:67
  12.1 6.9 %collective-permute-start.3 = (f32[2,128,256]{2,1,0:T(8,128)S(1)}, f32[2,128,256]{2,1,0:T(8,128)S(1)}, u32[]{:S(2)}, u32[]{:S(2)}) collective-permute-start(f32[2,128,256]{2,1,0:T(8,128)S(1)} %get-tuple-element.143), channel_id=1, source_target_pairs={{0,1},{1,0},{2,3},{3,2},{4,5},{5,4},{6,7},{7,6},{8,9},{9,8},{10,11... | collective-permute-start | bytes 786440 | tf_op jit(solution)/shard_map/ppermute | solution.py:67
  13.4 7.3 %collective-permute-start.4 = (f32[2,128,256]{2,1,0:T(8,128)S(1)}, f32[2,128,256]{2,1,0:T(8,128)S(1)}, u32[]{:S(2)}, u32[]{:S(2)}) collective-permute-start(f32[2,128,256]{2,1,0:T(8,128)S(1)} %get-tuple-element.152), channel_id=1, source_target_pairs={{0,16},{1,4},{2,18},{3,6},{4,1},{5,8},{6,3},{7,10},{8,5},{9,12},{1... | collective-permute-start | bytes 786440 | tf_op jit(solution)/shard_map/ppermute | solution.py:67
  16.8 11.2 %collective-permute-start.9 = (f32[2,256,256]{2,1,0:T(8,128)S(1)}, f32[2,256,256]{2,1,0:T(8,128)S(1)}, u32[]{:S(2)}, u32[]{:S(2)}) collective-permute-start(f32[2,256,256]{2,1,0:T(8,128)S(1)} %pad_maximum_fusion.1), channel_id=1, source_target_pairs={{0,16},{1,2},{2,1},{3,19},{4,20},{5,6},{6,5},{7,23},{8,24},{9,10},... | collective-permute-start | bytes 1572872 | tf_op jit(solution)/shard_map/ppermute | solution.py:67
  21.8 4.8 %collective-permute-start.6 = (f32[128,256]{1,0:T(8,128)S(1)}, f32[128,256]{1,0:T(8,128)S(1)}, u32[]{:S(2)}, u32[]{:S(2)}) collective-permute-start(f32[128,256]{1,0:T(8,128)S(1)} %get-tuple-element.159), channel_id=1, source_target_pairs={{0,1},{1,0},{2,3},{3,2},{4,5},{5,4},{6,7},{7,6},{8,9},{9,8},{10,11... | collective-permute-start | bytes 393224 | tf_op jit(solution)/shard_map/ppermute | solution.py:67
  23.6 5.3 %collective-permute-start.7 = (f32[128,256]{1,0:T(8,128)S(1)}, f32[128,256]{1,0:T(8,128)S(1)}, u32[]{:S(2)}, u32[]{:S(2)}) collective-permute-start(f32[128,256]{1,0:T(8,128)S(1)} %get-tuple-element.161), channel_id=1, source_target_pairs={{0,16},{1,4},{2,18},{3,6},{4,1},{5,8},{6,3},{7,10},{8,5},{9,12},{1... | collective-permute-start | bytes 393224 | tf_op jit(solution)/shard_map/ppermute | solution.py:67
  24.8 4.0 %collective-permute-start.8 = (f32[32,256]{1,0:T(8,128)S(1)}, f32[32,256]{1,0:T(8,128)S(1)}, u32[]{:S(2)}, u32[]{:S(2)}) collective-permute-start(f32[32,256]{1,0:T(8,128)S(1)} %get-tuple-element.162), channel_id=1, source_target_pairs={{0,2},{1,3},{2,0},{3,1},{4,6},{5,7},{6,4},{7,5},{8,10},{9,11},{10,... | collective-permute-start | bytes 98312 | tf_op jit(solution)/shard_map/ppermute | solution.py:67
  29.7 3.2 %collective-permute-start.11 = (f32[2,128,256]{2,1,0:T(8,128)S(1)}, f32[2,128,256]{2,1,0:T(8,128)S(1)}, u32[]{:S(2)}, u32[]{:S(2)}) collective-permute-start(f32[2,128,256]{2,1,0:T(8,128)S(1)} %get-tuple-element.170), channel_id=1, source_target_pairs={{0,1},{1,0},{2,3},{3,2},{4,5},{5,4},{6,7},{7,6},{8,9},{9,8},{10,11... | collective-permute-start | bytes 786440 | tf_op jit(solution)/shard_map/ppermute | solution.py:67
  30.2 6.1 %collective-permute-start.12 = (f32[2,128,256]{2,1,0:T(8,128)S(1)}, f32[2,128,256]{2,1,0:T(8,128)S(1)}, u32[]{:S(2)}, u32[]{:S(2)}) collective-permute-start(f32[2,128,256]{2,1,0:T(8,128)S(1)} %get-tuple-element.172), channel_id=1, source_target_pairs={{0,16},{1,4},{2,18},{3,6},{4,1},{5,8},{6,3},{7,10},{8,5},{9,12},{1... | collective-permute-start | bytes 786440 | tf_op jit(solution)/shard_map/ppermute | solution.py:67
  31.5 4.5 %collective-permute-start.13 = (f32[2,32,256]{2,1,0:T(8,128)S(1)}, f32[2,32,256]{2,1,0:T(8,128)S(1)}, u32[]{:S(2)}, u32[]{:S(2)}) collective-permute-start(f32[2,32,256]{2,1,0:T(8,128)S(1)} %get-tuple-element.173), channel_id=1, source_target_pairs={{0,2},{1,3},{2,0},{3,1},{4,6},{5,7},{6,4},{7,5},{8,10},{9,11},{10,... | collective-permute-start | bytes 196616 | tf_op jit(solution)/shard_map/ppermute | solution.py:67
  32.1 3.9 %collective-permute-start.14 = (f32[8,8,128]{2,1,0:T(8,128)S(1)}, f32[8,8,128]{2,1,0:T(8,128)S(1)}, u32[]{:S(2)}, u32[]{:S(2)}) collective-permute-start(f32[8,8,128]{2,1,0:T(8,128)S(1)} %get-tuple-element.175), channel_id=1, source_target_pairs={{0,2},{1,3},{2,0},{3,1},{4,6},{5,7},{6,4},{7,5},{8,10},{9,11},{10,... | collective-permute-start | bytes 98312 | tf_op jit(solution)/shard_map/ppermute | solution.py:67
  37.1 3.4 %collective-permute-start.15 = (f32[128,256]{1,0:T(8,128)S(1)}, f32[128,256]{1,0:T(8,128)S(1)}, u32[]{:S(2)}, u32[]{:S(2)}) collective-permute-start(f32[128,256]{1,0:T(8,128)S(1)} %get-tuple-element.177), channel_id=1, source_target_pairs={{0,1},{1,0},{2,3},{3,2},{4,5},{5,4},{6,7},{7,6},{8,9},{9,8},{10,11... | collective-permute-start | bytes 393224 | tf_op jit(solution)/shard_map/ppermute | solution.py:67
  37.6 4.7 %collective-permute-start.16 = (f32[128,256]{1,0:T(8,128)S(1)}, f32[128,256]{1,0:T(8,128)S(1)}, u32[]{:S(2)}, u32[]{:S(2)}) collective-permute-start(f32[128,256]{1,0:T(8,128)S(1)} %get-tuple-element.179), channel_id=1, source_target_pairs={{0,16},{1,4},{2,18},{3,6},{4,1},{5,8},{6,3},{7,10},{8,5},{9,12},{1... | collective-permute-start | bytes 393224 | tf_op jit(solution)/shard_map/ppermute | solution.py:67
  38.6 3.3 %collective-permute-start.17 = (f32[32,256]{1,0:T(8,128)S(1)}, f32[32,256]{1,0:T(8,128)S(1)}, u32[]{:S(2)}, u32[]{:S(2)}) collective-permute-start(f32[32,256]{1,0:T(8,128)S(1)} %get-tuple-element.180), channel_id=1, source_target_pairs={{0,2},{1,3},{2,0},{3,1},{4,6},{5,7},{6,4},{7,5},{8,10},{9,11},{10,... | collective-permute-start | bytes 98312 | tf_op jit(solution)/shard_map/ppermute | solution.py:67
  39.2 3.1 %collective-permute-start.18 = (f32[8,8,128]{2,1,0:T(8,128)S(1)}, f32[8,8,128]{2,1,0:T(8,128)S(1)}, u32[]{:S(2)}, u32[]{:S(2)}) collective-permute-start(f32[8,8,128]{2,1,0:T(8,128)S(1)} %get-tuple-element.182), channel_id=1, source_target_pairs={{0,4},{1,5},{2,6},{3,7},{4,0},{5,1},{6,2},{7,3},{8,12},{9,13},{10,... | collective-permute-start | bytes 98312 | tf_op jit(solution)/shard_map/ppermute | solution.py:67
  43.1 5.2 %collective-permute-start.19 = (f32[128,256]{1,0:T(8,128)S(1)}, f32[128,256]{1,0:T(8,128)S(1)}, u32[]{:S(2)}, u32[]{:S(2)}) collective-permute-start(f32[128,256]{1,0:T(8,128)S(1)} %get-tuple-element.184), channel_id=1, source_target_pairs={{0,1},{1,0},{2,3},{3,2},{4,5},{5,4},{6,7},{7,6},{8,9},{9,8},{10,11... | collective-permute-start | bytes 393224 | tf_op jit(solution)/shard_map/ppermute | solution.py:67
  44.4 5.3 %collective-permute-start.20 = (f32[128,256]{1,0:T(8,128)S(1)}, f32[128,256]{1,0:T(8,128)S(1)}, u32[]{:S(2)}, u32[]{:S(2)}) collective-permute-start(f32[128,256]{1,0:T(8,128)S(1)} %get-tuple-element.186), channel_id=1, source_target_pairs={{0,16},{1,4},{2,18},{3,6},{4,1},{5,8},{6,3},{7,10},{8,5},{9,12},{1... | collective-permute-start | bytes 393224 | tf_op jit(solution)/shard_map/ppermute | solution.py:67
  45.2 4.5 %collective-permute-start.21 = (f32[32,256]{1,0:T(8,128)S(1)}, f32[32,256]{1,0:T(8,128)S(1)}, u32[]{:S(2)}, u32[]{:S(2)}) collective-permute-start(f32[32,256]{1,0:T(8,128)S(1)} %get-tuple-element.187), channel_id=1, source_target_pairs={{0,2},{1,3},{2,0},{3,1},{4,6},{5,7},{6,4},{7,5},{8,10},{9,11},{10,... | collective-permute-start | bytes 98312 | tf_op jit(solution)/shard_map/ppermute | solution.py:67
  46.0 3.7 %collective-permute-start.22 = (f32[8,8,128]{2,1,0:T(8,128)S(1)}, f32[8,8,128]{2,1,0:T(8,128)S(1)}, u32[]{:S(2)}, u32[]{:S(2)}) collective-permute-start(f32[8,8,128]{2,1,0:T(8,128)S(1)} %get-tuple-element.189), channel_id=1, source_target_pairs={{0,8},{1,9},{2,10},{3,11},{4,12},{5,13},{6,14},{7,15},{8,0},{9,1},... | collective-permute-start | bytes 98312 | tf_op jit(solution)/shard_map/ppermute | solution.py:67
  50.6 3.3 %collective-permute-start.23 = (f32[128,256]{1,0:T(8,128)S(1)}, f32[128,256]{1,0:T(8,128)S(1)}, u32[]{:S(2)}, u32[]{:S(2)}) collective-permute-start(f32[128,256]{1,0:T(8,128)S(1)} %get-tuple-element.191), channel_id=1, source_target_pairs={{0,1},{1,0},{2,3},{3,2},{4,5},{5,4},{6,7},{7,6},{8,9},{9,8},{10,11... | collective-permute-start | bytes 393224 | tf_op jit(solution)/shard_map/ppermute | solution.py:67
  52.9 4.7 %collective-permute-start.24 = (f32[128,256]{1,0:T(8,128)S(1)}, f32[128,256]{1,0:T(8,128)S(1)}, u32[]{:S(2)}, u32[]{:S(2)}) collective-permute-start(f32[128,256]{1,0:T(8,128)S(1)} %get-tuple-element.193), channel_id=1, source_target_pairs={{0,16},{1,4},{2,18},{3,6},{4,1},{5,8},{6,3},{7,10},{8,5},{9,12},{1... | collective-permute-start | bytes 393224 | tf_op jit(solution)/shard_map/ppermute | solution.py:67
  58.9 4.7 %collective-permute-start.27 = (f32[128,256]{1,0:T(8,128)S(1)}, f32[128,256]{1,0:T(8,128)S(1)}, u32[]{:S(2)}, u32[]{:S(2)}) collective-permute-start(f32[128,256]{1,0:T(8,128)S(1)} %get-tuple-element.198), channel_id=1, source_target_pairs={{0,16},{1,4},{2,18},{3,6},{4,1},{5,8},{6,3},{7,10},{8,5},{9,12},{1... | collective-permute-start | bytes 393224 | tf_op jit(solution)/shard_map/ppermute | solution.py:67
  59.5 3.1 %collective-permute-start.28 = (f32[32,256]{1,0:T(8,128)S(1)}, f32[32,256]{1,0:T(8,128)S(1)}, u32[]{:S(2)}, u32[]{:S(2)}) collective-permute-start(f32[32,256]{1,0:T(8,128)S(1)} %get-tuple-element.199), channel_id=1, source_target_pairs={{0,2},{1,3},{2,0},{3,1},{4,6},{5,7},{6,4},{7,5},{8,10},{9,11},{10,... | collective-permute-start | bytes 98312 | tf_op jit(solution)/shard_map/ppermute | solution.py:67
  64.4 5.9 %collective-permute-start.29 = (f32[128,256]{1,0:T(8,128)S(1)}, f32[128,256]{1,0:T(8,128)S(1)}, u32[]{:S(2)}, u32[]{:S(2)}) collective-permute-start(f32[128,256]{1,0:T(8,128)S(1)} %get-tuple-element.201), channel_id=1, source_target_pairs={{0,1},{1,0},{2,3},{3,2},{4,5},{5,4},{6,7},{7,6},{8,9},{9,8},{10,11... | collective-permute-start | bytes 393224 | tf_op jit(solution)/shard_map/ppermute | solution.py:67
  64.9 6.8 %collective-permute-start.30 = (f32[128,256]{1,0:T(8,128)S(1)}, f32[128,256]{1,0:T(8,128)S(1)}, u32[]{:S(2)}, u32[]{:S(2)}) collective-permute-start(f32[128,256]{1,0:T(8,128)S(1)} %get-tuple-element.203), channel_id=1, source_target_pairs={{0,16},{1,4},{2,18},{3,6},{4,1},{5,8},{6,3},{7,10},{8,5},{9,12},{1... | collective-permute-start | bytes 393224 | tf_op jit(solution)/shard_map/ppermute | solution.py:67
  65.5 6.1 %collective-permute-start.31 = (f32[32,256]{1,0:T(8,128)S(1)}, f32[32,256]{1,0:T(8,128)S(1)}, u32[]{:S(2)}, u32[]{:S(2)}) collective-permute-start(f32[32,256]{1,0:T(8,128)S(1)} %get-tuple-element.204), channel_id=1, source_target_pairs={{0,2},{1,3},{2,0},{3,1},{4,6},{5,7},{6,4},{7,5},{8,10},{9,11},{10,... | collective-permute-start | bytes 98312 | tf_op jit(solution)/shard_map/ppermute | solution.py:67
  66.2 3.3 %collective-permute-start.32 = (f32[1,128]{1,0:T(1,128)S(1)}, f32[1,128]{1,0:T(1,128)S(1)}, u32[]{:S(2)}, u32[]{:S(2)}) collective-permute-start(f32[1,128]{1,0:T(1,128)S(1)} %get-tuple-element.208.own), channel_id=1, source_target_pairs={{0,16},{1,2},{2,1},{3,19},{4,20},{5,6},{6,5},{7,23},{8,24},{9,10},... | collective-permute-start | bytes 1544 | tf_op jit(solution)/shard_map/ppermute | solution.py:67
  74.2 4.7 %collective-permute-start.34 = (f32[128,256]{1,0:T(8,128)S(1)}, f32[128,256]{1,0:T(8,128)S(1)}, u32[]{:S(2)}, u32[]{:S(2)}) collective-permute-start(f32[128,256]{1,0:T(8,128)S(1)} %get-tuple-element.217), channel_id=1, source_target_pairs={{0,16},{1,4},{2,18},{3,6},{4,1},{5,8},{6,3},{7,10},{8,5},{9,12},{1... | collective-permute-start | bytes 393224 | tf_op jit(solution)/shard_map/ppermute | solution.py:67
  74.9 3.1 %collective-permute-start.35 = (f32[32,256]{1,0:T(8,128)S(1)}, f32[32,256]{1,0:T(8,128)S(1)}, u32[]{:S(2)}, u32[]{:S(2)}) collective-permute-start(f32[32,256]{1,0:T(8,128)S(1)} %get-tuple-element.218), channel_id=1, source_target_pairs={{0,2},{1,3},{2,0},{3,1},{4,6},{5,7},{6,4},{7,5},{8,10},{9,11},{10,... | collective-permute-start | bytes 98312 | tf_op jit(solution)/shard_map/ppermute | solution.py:67
  80.1 4.7 %collective-permute-start.37 = (f32[128,256]{1,0:T(8,128)S(1)}, f32[128,256]{1,0:T(8,128)S(1)}, u32[]{:S(2)}, u32[]{:S(2)}) collective-permute-start(f32[128,256]{1,0:T(8,128)S(1)} %get-tuple-element.224), channel_id=1, source_target_pairs={{0,16},{1,4},{2,18},{3,6},{4,1},{5,8},{6,3},{7,10},{8,5},{9,12},{1... | collective-permute-start | bytes 393224 | tf_op jit(solution)/shard_map/ppermute | solution.py:67
  80.8 3.1 %collective-permute-start.38 = (f32[32,256]{1,0:T(8,128)S(1)}, f32[32,256]{1,0:T(8,128)S(1)}, u32[]{:S(2)}, u32[]{:S(2)}) collective-permute-start(f32[32,256]{1,0:T(8,128)S(1)} %get-tuple-element.225), channel_id=1, source_target_pairs={{0,2},{1,3},{2,0},{3,1},{4,6},{5,7},{6,4},{7,5},{8,10},{9,11},{10,... | collective-permute-start | bytes 98312 | tf_op jit(solution)/shard_map/ppermute | solution.py:67
  86.1 4.7 %collective-permute-start.40 = (f32[128,256]{1,0:T(8,128)S(1)}, f32[128,256]{1,0:T(8,128)S(1)}, u32[]{:S(2)}, u32[]{:S(2)}) collective-permute-start(f32[128,256]{1,0:T(8,128)S(1)} %get-tuple-element.231), channel_id=1, source_target_pairs={{0,16},{1,4},{2,18},{3,6},{4,1},{5,8},{6,3},{7,10},{8,5},{9,12},{1... | collective-permute-start | bytes 393224 | tf_op jit(solution)/shard_map/ppermute | solution.py:67
  86.8 3.1 %collective-permute-start.41 = (f32[32,256]{1,0:T(8,128)S(1)}, f32[32,256]{1,0:T(8,128)S(1)}, u32[]{:S(2)}, u32[]{:S(2)}) collective-permute-start(f32[32,256]{1,0:T(8,128)S(1)} %get-tuple-element.232), channel_id=1, source_target_pairs={{0,2},{1,3},{2,0},{3,1},{4,6},{5,7},{6,4},{7,5},{8,10},{9,11},{10,... | collective-permute-start | bytes 98312 | tf_op jit(solution)/shard_map/ppermute | solution.py:67
  92.0 4.7 %collective-permute-start.43 = (f32[128,256]{1,0:T(8,128)S(1)}, f32[128,256]{1,0:T(8,128)S(1)}, u32[]{:S(2)}, u32[]{:S(2)}) collective-permute-start(f32[128,256]{1,0:T(8,128)S(1)} %get-tuple-element.238), channel_id=1, source_target_pairs={{0,16},{1,4},{2,18},{3,6},{4,1},{5,8},{6,3},{7,10},{8,5},{9,12},{1... | collective-permute-start | bytes 393224 | tf_op jit(solution)/shard_map/ppermute | solution.py:67
  92.7 3.1 %collective-permute-start.44 = (f32[32,256]{1,0:T(8,128)S(1)}, f32[32,256]{1,0:T(8,128)S(1)}, u32[]{:S(2)}, u32[]{:S(2)}) collective-permute-start(f32[32,256]{1,0:T(8,128)S(1)} %get-tuple-element.239), channel_id=1, source_target_pairs={{0,2},{1,3},{2,0},{3,1},{4,6},{5,7},{6,4},{7,5},{8,10},{9,11},{10,... | collective-permute-start | bytes 98312 | tf_op jit(solution)/shard_map/ppermute | solution.py:67
  98.0 4.7 %collective-permute-start.46 = (f32[128,256]{1,0:T(8,128)S(1)}, f32[128,256]{1,0:T(8,128)S(1)}, u32[]{:S(2)}, u32[]{:S(2)}) collective-permute-start(f32[128,256]{1,0:T(8,128)S(1)} %get-tuple-element.245), channel_id=1, source_target_pairs={{0,16},{1,4},{2,18},{3,6},{4,1},{5,8},{6,3},{7,10},{8,5},{9,12},{1... | collective-permute-start | bytes 393224 | tf_op jit(solution)/shard_map/ppermute | solution.py:67
  98.7 3.1 %collective-permute-start.47 = (f32[32,256]{1,0:T(8,128)S(1)}, f32[32,256]{1,0:T(8,128)S(1)}, u32[]{:S(2)}, u32[]{:S(2)}) collective-permute-start(f32[32,256]{1,0:T(8,128)S(1)} %get-tuple-element.246), channel_id=1, source_target_pairs={{0,2},{1,3},{2,0},{3,1},{4,6},{5,7},{6,4},{7,5},{8,10},{9,11},{10,... | collective-permute-start | bytes 98312 | tf_op jit(solution)/shard_map/ppermute | solution.py:67
  104.0 4.7 %collective-permute-start.49 = (f32[128,256]{1,0:T(8,128)S(1)}, f32[128,256]{1,0:T(8,128)S(1)}, u32[]{:S(2)}, u32[]{:S(2)}) collective-permute-start(f32[128,256]{1,0:T(8,128)S(1)} %get-tuple-element.252), channel_id=1, source_target_pairs={{0,16},{1,4},{2,18},{3,6},{4,1},{5,8},{6,3},{7,10},{8,5},{9,12},{1... | collective-permute-start | bytes 393224 | tf_op jit(solution)/shard_map/ppermute | solution.py:67
  104.6 3.1 %collective-permute-start.50 = (f32[32,256]{1,0:T(8,128)S(1)}, f32[32,256]{1,0:T(8,128)S(1)}, u32[]{:S(2)}, u32[]{:S(2)}) collective-permute-start(f32[32,256]{1,0:T(8,128)S(1)} %get-tuple-element.253), channel_id=1, source_target_pairs={{0,2},{1,3},{2,0},{3,1},{4,6},{5,7},{6,4},{7,5},{8,10},{9,11},{10,... | collective-permute-start | bytes 98312 | tf_op jit(solution)/shard_map/ppermute | solution.py:67
  109.9 4.7 %collective-permute-start.52 = (f32[128,256]{1,0:T(8,128)S(1)}, f32[128,256]{1,0:T(8,128)S(1)}, u32[]{:S(2)}, u32[]{:S(2)}) collective-permute-start(f32[128,256]{1,0:T(8,128)S(1)} %get-tuple-element.259), channel_id=1, source_target_pairs={{0,16},{1,4},{2,18},{3,6},{4,1},{5,8},{6,3},{7,10},{8,5},{9,12},{1... | collective-permute-start | bytes 393224 | tf_op jit(solution)/shard_map/ppermute | solution.py:67
  115.7 11.2 %collective-permute-start.54 = (f32[2,256,256]{2,1,0:T(8,128)S(1)}, f32[2,256,256]{2,1,0:T(8,128)S(1)}, u32[]{:S(2)}, u32[]{:S(2)}) collective-permute-start(f32[2,256,256]{2,1,0:T(8,128)S(1)} %get-tuple-element.263.own), channel_id=1, source_target_pairs={{0,16},{1,2},{2,1},{3,19},{4,20},{5,6},{6,5},{7,23},{8,24},{9,10},... | collective-permute-start | bytes 1572872 | tf_op jit(solution)/shard_map/ppermute | solution.py:67
  118.7 9.6 %collective-permute-start.56 = (f32[2,64,128]{2,1,0:T(8,128)S(1)}, f32[2,64,128]{2,1,0:T(8,128)S(1)}, u32[]{:S(2)}, u32[]{:S(2)}) collective-permute-start(f32[2,64,128]{2,1,0:T(8,128)S(1)} %get-tuple-element.268), channel_id=1, source_target_pairs={{0,0},{1,2},{2,1},{3,3},{4,4},{5,6},{6,5},{7,7},{8,8},{9,10},{10,9... | collective-permute-start | bytes 196616 | tf_op jit(solution)/shard_map/ppermute | solution.py:67
  121.3 7.0 %collective-permute-start.57 = (f32[2,64,128]{2,1,0:T(8,128)S(1)}, f32[2,64,128]{2,1,0:T(8,128)S(1)}, u32[]{:S(2)}, u32[]{:S(2)}) collective-permute-start(f32[2,64,128]{2,1,0:T(8,128)S(1)} %get-tuple-element.269), channel_id=1, source_target_pairs={{0,4},{1,6},{2,5},{3,7},{4,0},{5,2},{6,1},{7,3},{8,12},{9,14},{10,... | collective-permute-start | bytes 196616 | tf_op jit(solution)/shard_map/ppermute | solution.py:67
  122.9 6.2 %collective-permute-start.58 = (f32[2,64,128]{2,1,0:T(8,128)S(1)}, f32[2,64,128]{2,1,0:T(8,128)S(1)}, u32[]{:S(2)}, u32[]{:S(2)}) collective-permute-start(f32[2,64,128]{2,1,0:T(8,128)S(1)} %get-tuple-element.270), channel_id=1, source_target_pairs={{0,8},{1,10},{2,9},{3,11},{4,12},{5,14},{6,13},{7,15},{8,0},{9,2},... | collective-permute-start | bytes 196616 | tf_op jit(solution)/shard_map/ppermute | solution.py:67
  123.8 6.5 %collective-permute-start.59 = (f32[2,64,128]{2,1,0:T(8,128)S(1)}, f32[2,64,128]{2,1,0:T(8,128)S(1)}, u32[]{:S(2)}, u32[]{:S(2)}) collective-permute-start(f32[2,64,128]{2,1,0:T(8,128)S(1)} %get-tuple-element.271), channel_id=1, source_target_pairs={{0,12},{1,14},{2,13},{3,15},{4,8},{5,10},{6,9},{7,11},{8,4},{9,6},... | collective-permute-start | bytes 196616 | tf_op jit(solution)/shard_map/ppermute | solution.py:67
  (31 other events, 73.6 us)

commit v10 on v9

--- a/solution.py
+++ b/solution.py
@@ -401,9 +401,7 @@
 
 
 def last_kernel(scale, flags, part, k0, ki, kx, zm, ym, side, edge, image, change, vel,
-                prev, states, mine, other):
-    new = states.at[1]
-    states[0] = prev[...]
+                new, mine, other):
     outer(flags, part, k0, ki, kx, zm, ym, side, edge, new)
     raw = (image[...] + new[...] * change[...]) * scale / vel[...]
     count, height, lanes = mine.shape
@@ -416,6 +414,11 @@
             for m in (2 * n, 2 * n + 1))
         mine[n] = jnp.where(flags[0] == 0, even, odd)
         other[n] = jnp.where(flags[0] == 0, odd, even)
+
+
+def both_kernel(flags, a, b, out):
+    out[0] = a[...]
+    out[1] = b[...]
 
 
 def join_kernel(flags, mine, got, *outs):
@@ -529,12 +532,14 @@
     density, p_now, *out = call(settle_kernel, "settle",
                                 [field, field] + [shaped(2, *r.shape) for r in rim],
                                 flags_in, log_density, fwd_now, *got, far=2)
-    zm, cm, ym = halo(*out)
-    got_adjoint = send(jnp.stack([after(adj_now, ym), after(adj_before, ym)]), swap_perm)
+    zm, cm = send(out[0], z_perm), send(out[1], c_perm)
+    ym = send(after(out[2], cm), y_perm)
     vel, p_before = call(settle_pair_kernel, "settle_model", [field, field],
                          flags, velocity, fwd_before, got_model, weight=0.6, far=2)
     parts = call(first_inner_kernel, "first_inner", [field] * 7, flags, density, p_now, cm,
                  near, deep, weight=1.3)
+    got_adjoint = send(
+        jnp.stack([after(adj_now, parts[0]), after(adj_before, parts[0])]), swap_perm)
 
     new, zo, co, yo, k0, ki, kx, kz = call(
         first_outer_kernel, "first_outer", [field] + rim + [field] * 4,
@@ -544,6 +549,7 @@
     changes = []
     zm, cm, ym = halo(zo, co, yo)
     double = 1
+    late = steps - 2 if len(stages) < steps - 2 else steps - 1
 
     slots = subs * CAP
     entries, half_entries = shaped(subs, steps, 128), shaped(subs // 2, steps, 128)
@@ -561,9 +567,11 @@
             src_cell, wavelet, cur, prev, *model, cm, near, deep, before, weight=1.2, scalars=2)
         changes.append(change)
         args = [flags, part, k0, ki, kx, zm, ym, side, edge]
-        if t == steps - 1:
+        if t == steps - 3:
             u_part, = call(adjoint_first_kernel, "adjoint_first", [field], flags, u_now, u_before,
                            *model, u_cm, near, deep, weight=1.1)
+            args[1] = after(part, u_part)
+        if t == late:
             for n in range(steps - 2, len(stages)):
                 lists, *give = call(
                     functools.partial(trade_kernel, n), "trade",
@@ -575,6 +583,8 @@
                 [jax.ShapeDtypeStruct((size, slots), BF16),
                  jax.ShapeDtypeStruct((slots, size), BF16), shaped(slots, depth),
                  shaped(slots, steps)], flags, lists, cells, got_cells, weight=0.8)
+            args[1] = after(part, receivers[0])
+        if t == steps - 1:
             new, u_new, *out = call(
                 functools.partial(turn_kernel, t), "turn", [field, field] + rim, *args, u_part,
                 u_zm, u_ym, *receivers)
@@ -582,6 +592,8 @@
             break
         if t == len(stages) - 2:
             got_cells = send(after(cells, part), swap_perm)
+        if t == len(stages) - 1:
+            args[1] = after(part, got_cells)
         if t == double:
             u_now, u_before = call(settle_pair_kernel, "settle_adjoint", [field, field], flags,
                                    adj_now, adj_before, got_adjoint, weight=0.6, far=2)
@@ -612,15 +624,16 @@
             u_now, u_before, *model, cm, near, deep, states[t + 2], *receivers, *terms, weight=1.5)
         args = [part, k0, ki, kx, zm, ym, side, edge]
         if j == steps - 1:
-            final, mine, other = call(
-                functools.partial(last_kernel, 2.0 / steps), "last",
-                [shaped(2, *field.shape), half, half], flags, *args, *image, changes[0], vel, u_now)
+            u_last, mine, other = call(
+                functools.partial(last_kernel, 2.0 / steps), "last", [field, half, half], flags,
+                *args, *image, changes[0], vel)
             break
         u_before = u_now
         u_now, *out = call(functools.partial(outer_kernel, None, False), "adjoint_outer", [field] + rim,
                            flags, *args)
         zm, cm, ym = halo(*out)
 
+    final, = call(both_kernel, "both", [shaped(2, *field.shape)], flags, u_now, u_last, weight=0.4)
     got = send(final, swap_perm)
     pieces = call(join_kernel, "join", [shaped(2, *half.shape[1:])] * nq, flags, mine,
                   send(other, c_perm))

time: 132 us -> 145 us (1.098)
  local copies, waits for them, and re-layouts: 1.18 us -> 9.64 us
  starting transfers between devices: 53.2 us -> 56.9 us
  waiting for transfers between devices: 29.5 us -> 28 us
    unnamed x38 -> x68, local copies, waits for them, and re-layouts: 1.1 us -> 9.56 us
    ppermute x60, starting transfers between devices: 53.2 us -> 56.9 us  [send(): return lax.ppermute(value, ALL, pairs)]
    ppermute x60, waiting for transfers between devices: 29.5 us -> 28 us  [send(): return lax.ppermute(value, ALL, pairs)]
    pallas_call x40 -> x41, Pallas kernels: 44.9 us -> 45.5 us  [call(): pl.pallas_call(kernel, name=name, out_shape=outs, in_specs=specs, out_spe...]
  transfers between devices with their start and end apart: 60 -> 60, of which waited for: 30 -> 29; matrix products, arithmetic and copies ran while one was open for 2% -> 2% of each run, Pallas kernels for 23% -> 21%
where the time goes in v10:
time: 145 us; the launch traced here: 144 us
  starting transfers between devices  56.9 us (39%)
  Pallas kernels  45.5 us (31%)
  waiting for transfers between devices  28 us (19%)
  local copies, waits for them, and re-layouts  9.64 us (7%)
  other arithmetic  2.96 us (2%)
    ppermute x60, starting transfers between devices, send(): return lax.ppermute(value, ALL, pairs)  56.9 us
    pallas_call x41, Pallas kernels, call(): pl.pallas_call(kernel, name=name, out_shape=outs, in_specs=specs, out_spe...  45.5 us
    ppermute x60, waiting for transfers between devices, send(): return lax.ppermute(value, ALL, pairs)  28 us
    unnamed x68, local copies, waits for them, and re-layouts  9.56 us
  transfers between devices with their start and end apart: 60, of which 29 were waited for; matrix products, arithmetic and copies ran while one was open for 2% of the time, Pallas kernels for 21%

profile of v10, /device:TPU:1, one launch (start us, length us, event | category | flops | bytes accessed | tf_op | source)
XLA Modules:
  0.0 144.2 jit_solution(13767057130409853295)
XLA Ops:
  0.6 2.7 %collective-permute-start.1 = (f32[256,256]{1,0:T(8,128)}, f32[256,256]{1,0:T(8,128)S(1)}, u32[]{:S(2)}, u32[]{:S(2)}) collective-permute-start(f32[256,256]{1,0:T(8,128)} %bitcast.28), channel_id=1, source_target_pairs={{0,16},{1,2},{2,1},{3,19},{4,20},{5,6},{6,5},{7,23},{8,24},{9,10},... | collective-permute-start | bytes 786440 | tf_op jit(solution)/shard_map/ppermute | solution.py:67
  3.4 1.9 %pad_maximum_fusion = f32[2,256,256]{2,1,0:T(8,128)} fusion(f32[1,256,256]{2,1,0:T(8,128)} %bitcast.20, f32[1,256,256]{2,1,0:T(8,128)} %bitcast.18), kind=kLoop, calls=%fused_computation | loop fusion | flops 131072 | bytes 1048576 | tf_op jit(solution)/shard_map/stack | solution.py:526
  5.3 1.7 %collective-permute-start.2 = (f32[2,256,256]{2,1,0:T(8,128)}, f32[2,256,256]{2,1,0:T(8,128)S(1)}, u32[]{:S(2)}, u32[]{:S(2)}) collective-permute-start(f32[2,256,256]{2,1,0:T(8,128)} %pad_maximum_fusion), channel_id=1, source_target_pairs={{0,16},{1,2},{2,1},{3,19},{4,20},{5,6},{6,5},{7,23},{8,24},{9,10},... | collective-permute-start | bytes 1572872 | tf_op jit(solution)/shard_map/ppermute | solution.py:67
  8.7 2.0 %collective-permute-done.recv_a = f32[256,256]{1,0:T(8,128)S(1)} collective-permute-done((f32[256,256]{1,0:T(8,128)}, f32[256,256]{1,0:T(8,128)S(1)}, u32[]{:S(2)}, u32[]{:S(2)}) %collective-permute-start) | collective-permute-done | bytes 262176 | tf_op jit(solution)/shard_map/ppermute | solution.py:67
  13.0 1.3 first_inner.1
  20.2 1.4 %collective-permute-start.9 = (f32[2,256,256]{2,1,0:T(8,128)}, f32[2,256,256]{2,1,0:T(8,128)S(1)}, u32[]{:S(2)}, u32[]{:S(2)}) collective-permute-start(f32[2,256,256]{2,1,0:T(8,128)} %pad_maximum_fusion.1), channel_id=1, source_target_pairs={{0,16},{1,2},{2,1},{3,19},{4,20},{5,6},{6,5},{7,23},{8,24},{9,10},... | collective-permute-start | bytes 1572872 | tf_op jit(solution)/shard_map/ppermute | solution.py:67
  21.6 2.2 %collective-permute-start.4 = (f32[2,128,256]{2,1,0:T(8,128)}, f32[2,128,256]{2,1,0:T(8,128)S(1)}, u32[]{:S(2)}, u32[]{:S(2)}) collective-permute-start(f32[2,128,256]{2,1,0:T(8,128)} %copy-done.26), channel_id=1, source_target_pairs={{0,16},{1,4},{2,18},{3,6},{4,1},{5,8},{6,3},{7,10},{8,5},{9,12},{1... | collective-permute-start | bytes 786440 | tf_op jit(solution)/shard_map/ppermute | solution.py:67
  24.7 3.7 %collective-permute-done.4.zm = f32[2,128,256]{2,1,0:T(8,128)S(1)} collective-permute-done((f32[2,128,256]{2,1,0:T(8,128)}, f32[2,128,256]{2,1,0:T(8,128)S(1)}, u32[]{:S(2)}, u32[]{:S(2)}) %collective-permute-start.4) | collective-permute-done | bytes 262176 | tf_op jit(solution)/shard_map/ppermute | solution.py:67
  32.2 1.1 first_outer.1
  33.3 3.5 %collective-permute-start.6 = (f32[128,256]{1,0:T(8,128)S(1)}, f32[128,256]{1,0:T(8,128)S(1)}, u32[]{:S(2)}, u32[]{:S(2)}) collective-permute-start(f32[128,256]{1,0:T(8,128)S(1)} %get-tuple-element.164), channel_id=1, source_target_pairs={{0,1},{1,0},{2,3},{3,2},{4,5},{5,4},{6,7},{7,6},{8,9},{9,8},{10,11... | collective-permute-start | bytes 393224 | tf_op jit(solution)/shard_map/ppermute | solution.py:67
  38.3 2.1 %collective-permute-start.10 = (f32[8,8,128]{2,1,0:T(8,128)S(1)}, f32[8,8,128]{2,1,0:T(8,128)S(1)}, u32[]{:S(2)}, u32[]{:S(2)}) collective-permute-start(f32[8,8,128]{2,1,0:T(8,128)S(1)} %get-tuple-element.173), channel_id=1, source_target_pairs={{0,1},{1,0},{2,3},{3,2},{4,5},{5,4},{6,7},{7,6},{8,9},{9,8},{10,11... | collective-permute-start | bytes 98312 | tf_op jit(solution)/shard_map/ppermute | solution.py:67
  40.3 1.3 forward_inner.7
  45.2 1.3 forward_inner.8
  46.5 1.2 collective-permute-done.14.rest_1_
  47.7 2.1 %collective-permute-done.12.zm.u_zm = f32[2,128,256]{2,1,0:T(8,128)S(1)} collective-permute-done((f32[2,128,256]{2,1,0:T(8,128)S(1)}, f32[2,128,256]{2,1,0:T(8,128)S(1)}, u32[]{:S(2)}, u32[]{:S(2)}) %collective-permute-start.12) | collective-permute-done | bytes 262176 | tf_op jit(solution)/shard_map/ppermute | solution.py:67
  52.9 2.1 %collective-permute-start.16 = (f32[1,128]{1,0:T(1,128)S(1)}, f32[1,128]{1,0:T(1,128)S(1)}, u32[]{:S(2)}, u32[]{:S(2)}) collective-permute-start(f32[1,128]{1,0:T(1,128)S(1)} %get-tuple-element.185.own), channel_id=1, source_target_pairs={{0,16},{1,2},{2,1},{3,19},{4,20},{5,6},{6,5},{7,23},{8,24},{9,10},... | collective-permute-start | bytes 1544 | tf_op jit(solution)/shard_map/ppermute | solution.py:67
  55.0 1.4 forward_inner.9
  57.3 1.8 %collective-permute-start.20 = (f32[128,256]{1,0:T(8,128)S(1)}, f32[128,256]{1,0:T(8,128)S(1)}, u32[]{:S(2)}, u32[]{:S(2)}) collective-permute-start(f32[128,256]{1,0:T(8,128)S(1)} %get-tuple-element.192), channel_id=1, source_target_pairs={{0,1},{1,0},{2,3},{3,2},{4,5},{5,4},{6,7},{7,6},{8,9},{9,8},{10,11... | collective-permute-start | bytes 393224 | tf_op jit(solution)/shard_map/ppermute | solution.py:67
  60.5 1.4 forward_inner.10
  62.1 1.9 %collective-permute-done.23.rest_1_ = f32[8,8,128]{2,1,0:T(8,128)S(1)} collective-permute-done((f32[8,8,128]{2,1,0:T(8,128)S(1)}, f32[8,8,128]{2,1,0:T(8,128)S(1)}, u32[]{:S(2)}, u32[]{:S(2)}) %collective-permute-start.23) | collective-permute-done | bytes 32800 | tf_op jit(solution)/shard_map/ppermute | solution.py:67
  64.8 1.3 collective-permute-start.24
  66.8 1.7 %collective-permute-start.26 = (f32[32,256]{1,0:T(8,128)S(1)}, f32[32,256]{1,0:T(8,128)S(1)}, u32[]{:S(2)}, u32[]{:S(2)}) collective-permute-start(f32[32,256]{1,0:T(8,128)S(1)} %get-tuple-element.204), channel_id=1, source_target_pairs={{0,2},{1,3},{2,0},{3,1},{4,6},{5,7},{6,4},{7,5},{8,10},{9,11},{10,... | collective-permute-start | bytes 98312 | tf_op jit(solution)/shard_map/ppermute | solution.py:67
  68.4 1.1 adjoint_first.1.u_part
  69.5 1.4 forward_inner.11
  71.7 1.1 collective-permute-start.27
  72.8 1.3 collective-permute-start.29
  74.9 1.4 forward_inner.12
  76.3 1.3 collective-permute-done.28.zm
  79.5 1.1 collective-permute-start.32
  80.5 1.3 forward_inner.13
  83.5 1.5 %turn.1 = (f32[256,256]{1,0:T(8,128)S(1)}, f32[256,256]{1,0:T(8,128)S(1)}, f32[128,256]{1,0:T(8,128)S(1)}, f32[128,256]{1,0:T(8,128)S(1)}, f32[32,256]{1,0:T(8,128)S(1)}) custom-call(s32[8]{0:T(128)S(1)} %stack.41.flags, f32[256,256]{1,0:T(8,128)S(1)} %get-tuple-element.215.part, f32[256,256]{1,0:T(8,128)S(1)} %get-tuple-element.160.k0, ...), custom_call_target="tpu_custom_call" | custom-call | flops 1000 | bytes 1000 | tf_op jit(solution)/shard_map/turn/pallas_call | solution.py:465
  86.1 1.1 collective-permute-start.35
  87.2 1.7 %adjoint_inner.7 = (f32[256,256]{1,0:T(8,128)S(1)}, f32[256,256]{1,0:T(8,128)S(1)}) custom-call(s32[8]{0:T(128)S(1)} %stack.41.flags, f32[256,256]{1,0:T(8,128)S(1)} %get-tuple-element.221.cur.prev, f32[256,256]{1,0:T(8,128)S(1)} %get-tuple-element.170.rest_0_.cur.prev, f32[256,256]{1,0:T(8,128)S(1)} %get-tuple-element.160.k0, ...), custom_call_target="tpu_custom_call" | custom-call | flops 1000 | bytes 5401000 | tf_op jit(solution)/shard_map/adjoint_inner/pallas_call | solution.py:465
  92.1 1.1 collective-permute-start.38
  93.2 1.6 %adjoint_inner.8 = (f32[256,256]{1,0:T(8,128)S(1)}, f32[256,256]{1,0:T(8,128)S(1)}) custom-call(s32[8]{0:T(128)S(1)} %stack.41.flags, f32[256,256]{1,0:T(8,128)S(1)} %get-tuple-element.227.cur.prev, f32[256,256]{1,0:T(8,128)S(1)} %get-tuple-element.221.cur.prev, f32[256,256]{1,0:T(8,128)S(1)} %get-tuple-element.160.k0, ...), custom_call_target="tpu_custom_call" | custom-call | flops 1000 | bytes 5401000 | tf_op jit(solution)/shard_map/adjoint_inner/pallas_call | solution.py:465
  99.1 1.6 %adjoint_inner.9 = (f32[256,256]{1,0:T(8,128)S(1)}, f32[256,256]{1,0:T(8,128)S(1)}) custom-call(s32[8]{0:T(128)S(1)} %stack.41.flags, f32[256,256]{1,0:T(8,128)S(1)} %get-tuple-element.234.cur.prev, f32[256,256]{1,0:T(8,128)S(1)} %get-tuple-element.227.cur.prev, f32[256,256]{1,0:T(8,128)S(1)} %get-tuple-element.160.k0, ...), custom_call_target="tpu_custom_call" | custom-call | flops 1000 | bytes 5401000 | tf_op jit(solution)/shard_map/adjoint_inner/pallas_call | solution.py:465
  105.1 1.8 %adjoint_inner.10 = (f32[256,256]{1,0:T(8,128)S(1)}, f32[256,256]{1,0:T(8,128)S(1)}) custom-call(s32[8]{0:T(128)S(1)} %stack.41.flags, f32[256,256]{1,0:T(8,128)S(1)} %get-tuple-element.241.cur.prev, f32[256,256]{1,0:T(8,128)S(1)} %get-tuple-element.234.cur.prev, f32[256,256]{1,0:T(8,128)S(1)} %get-tuple-element.160.k0, ...), custom_call_target="tpu_custom_call" | custom-call | flops 1000 | bytes 5401000 | tf_op jit(solution)/shard_map/adjoint_inner/pallas_call | solution.py:465
  111.1 1.6 %adjoint_inner.11 = (f32[256,256]{1,0:T(8,128)S(1)}, f32[256,256]{1,0:T(8,128)S(1)}) custom-call(s32[8]{0:T(128)S(1)} %stack.41.flags, f32[256,256]{1,0:T(8,128)S(1)} %get-tuple-element.248.cur.prev, f32[256,256]{1,0:T(8,128)S(1)} %get-tuple-element.241.cur.prev, f32[256,256]{1,0:T(8,128)S(1)} %get-tuple-element.160.k0, ...), custom_call_target="tpu_custom_call" | custom-call | flops 1000 | bytes 5401000 | tf_op jit(solution)/shard_map/adjoint_inner/pallas_call | solution.py:465
  117.0 1.6 %adjoint_inner.12 = (f32[256,256]{1,0:T(8,128)S(1)}, f32[256,256]{1,0:T(8,128)S(1)}) custom-call(s32[8]{0:T(128)S(1)} %stack.41.flags, f32[256,256]{1,0:T(8,128)S(1)} %get-tuple-element.255.cur.prev, f32[256,256]{1,0:T(8,128)S(1)} %get-tuple-element.248.cur.prev, f32[256,256]{1,0:T(8,128)S(1)} %get-tuple-element.160.k0, ...), custom_call_target="tpu_custom_call" | custom-call | flops 1000 | bytes 5401000 | tf_op jit(solution)/shard_map/adjoint_inner/pallas_call | solution.py:465
  123.0 1.6 %adjoint_inner.13 = (f32[256,256]{1,0:T(8,128)S(1)}, f32[256,256]{1,0:T(8,128)S(1)}) custom-call(s32[8]{0:T(128)S(1)} %stack.41.flags, f32[256,256]{1,0:T(8,128)S(1)} %get-tuple-element.262.cur.a, f32[256,256]{1,0:T(8,128)S(1)} %get-tuple-element.255.cur.prev, f32[256,256]{1,0:T(8,128)S(1)} %get-tuple-element.160.k0, f32[256,256]{1,0:T(8,128)S(1)} %get-tuple-element.161.ki, ...), custom_call_target="tpu_custom_call" | custom-call | flops 1000 | bytes 5401000 | tf_op jit(solution)/shard_map/adjoint_inner/pallas_call | solution.py:465
  127.6 1.4 collective-permute-start.54
  129.1 1.2 collective-permute-done.55.got
  130.8 2.4 %collective-permute-start.56 = (f32[2,64,128]{2,1,0:T(8,128)S(1)}, f32[2,64,128]{2,1,0:T(8,128)S(1)}, u32[]{:S(2)}, u32[]{:S(2)}) collective-permute-start(f32[2,64,128]{2,1,0:T(8,128)S(1)} %get-tuple-element.276), channel_id=1, source_target_pairs={{0,0},{1,2},{2,1},{3,3},{4,4},{5,6},{6,5},{7,7},{8,8},{9,10},{10,9... | collective-permute-start | bytes 196616 | tf_op jit(solution)/shard_map/ppermute | solution.py:67
  133.3 1.7 %collective-permute-start.57 = (f32[2,64,128]{2,1,0:T(8,128)S(1)}, f32[2,64,128]{2,1,0:T(8,128)S(1)}, u32[]{:S(2)}, u32[]{:S(2)}) collective-permute-start(f32[2,64,128]{2,1,0:T(8,128)S(1)} %get-tuple-element.277), channel_id=1, source_target_pairs={{0,4},{1,6},{2,5},{3,7},{4,0},{5,2},{6,1},{7,3},{8,12},{9,14},{10,... | collective-permute-start | bytes 196616 | tf_op jit(solution)/shard_map/ppermute | solution.py:67
  135.9 3.1 %collective-permute-start.59 = (f32[2,64,128]{2,1,0:T(8,128)S(1)}, f32[2,64,128]{2,1,0:T(8,128)S(1)}, u32[]{:S(2)}, u32[]{:S(2)}) collective-permute-start(f32[2,64,128]{2,1,0:T(8,128)S(1)} %get-tuple-element.279), channel_id=1, source_target_pairs={{0,12},{1,14},{2,13},{3,15},{4,8},{5,10},{6,9},{7,11},{8,4},{9,6},... | collective-permute-start | bytes 196616 | tf_op jit(solution)/shard_map/ppermute | solution.py:67
  139.0 1.4 select.7
  141.2 1.2 collective-permute-done.59.refs_3_
  142.4 1.8 %filter.1 = f32[32,32,64]{2,1,0:T(8,128)} custom-call(s32[8]{0:T(128)S(1)} %stack.41.flags, f32[2,64,128]{2,1,0:T(8,128)S(1)} %collective-permute-done.56.refs_0_, f32[2,64,128]{2,1,0:T(8,128)S(1)} %collective-permute-done.57.refs_1_, f32[2,64,128]{2,1,0:T(8,128)S(1)} %collective-permute-done.58.refs_2_, f32[2,64,128]{2,1,0:T(8,128)S(1)} %collective-permute-done.59.refs_3_), custom_call_target="tpu_custom_call" | custom-call | flops 1000 | bytes 1000 | tf_op jit(solution)/shard_map/filter/pallas_call | solution.py:465
  (189 shorter events, 63.0 us)
Async XLA Ops:
  0.6 8.0 %collective-permute-start.1 = (f32[256,256]{1,0:T(8,128)}, f32[256,256]{1,0:T(8,128)S(1)}, u32[]{:S(2)}, u32[]{:S(2)}) collective-permute-start(f32[256,256]{1,0:T(8,128)} %bitcast.28), channel_id=1, source_target_pairs={{0,16},{1,2},{2,1},{3,19},{4,20},{5,6},{6,5},{7,23},{8,24},{9,10},... | collective-permute-start | bytes 786440 | tf_op jit(solution)/shard_map/ppermute | solution.py:67
  3.3 7.4 %collective-permute-start = (f32[256,256]{1,0:T(8,128)}, f32[256,256]{1,0:T(8,128)S(1)}, u32[]{:S(2)}, u32[]{:S(2)}) collective-permute-start(f32[256,256]{1,0:T(8,128)} %bitcast.26), channel_id=1, source_target_pairs={{0,16},{1,2},{2,1},{3,19},{4,20},{5,6},{6,5},{7,23},{8,24},{9,10},... | collective-permute-start | bytes 786440 | tf_op jit(solution)/shard_map/ppermute | solution.py:67
  5.3 18.7 %collective-permute-start.2 = (f32[2,256,256]{2,1,0:T(8,128)}, f32[2,256,256]{2,1,0:T(8,128)S(1)}, u32[]{:S(2)}, u32[]{:S(2)}) collective-permute-start(f32[2,256,256]{2,1,0:T(8,128)} %pad_maximum_fusion), channel_id=1, source_target_pairs={{0,16},{1,2},{2,1},{3,19},{4,20},{5,6},{6,5},{7,23},{8,24},{9,10},... | collective-permute-start | bytes 1572872 | tf_op jit(solution)/shard_map/ppermute | solution.py:67
  20.2 21.5 %collective-permute-start.9 = (f32[2,256,256]{2,1,0:T(8,128)}, f32[2,256,256]{2,1,0:T(8,128)S(1)}, u32[]{:S(2)}, u32[]{:S(2)}) collective-permute-start(f32[2,256,256]{2,1,0:T(8,128)} %pad_maximum_fusion.1), channel_id=1, source_target_pairs={{0,16},{1,2},{2,1},{3,19},{4,20},{5,6},{6,5},{7,23},{8,24},{9,10},... | collective-permute-start | bytes 1572872 | tf_op jit(solution)/shard_map/ppermute | solution.py:67
  21.6 6.8 %collective-permute-start.4 = (f32[2,128,256]{2,1,0:T(8,128)}, f32[2,128,256]{2,1,0:T(8,128)S(1)}, u32[]{:S(2)}, u32[]{:S(2)}) collective-permute-start(f32[2,128,256]{2,1,0:T(8,128)} %copy-done.26), channel_id=1, source_target_pairs={{0,16},{1,4},{2,18},{3,6},{4,1},{5,8},{6,3},{7,10},{8,5},{9,12},{1... | collective-permute-start | bytes 786440 | tf_op jit(solution)/shard_map/ppermute | solution.py:67
  23.9 5.5 %collective-permute-start.5 = (f32[2,32,256]{2,1,0:T(8,128)S(1)}, f32[2,32,256]{2,1,0:T(8,128)S(1)}, u32[]{:S(2)}, u32[]{:S(2)}) collective-permute-start(f32[2,32,256]{2,1,0:T(8,128)S(1)} %get-tuple-element.158), channel_id=1, source_target_pairs={{0,2},{1,3},{2,0},{3,1},{4,6},{5,7},{6,4},{7,5},{8,10},{9,11},{10,... | collective-permute-start | bytes 196616 | tf_op jit(solution)/shard_map/ppermute | solution.py:67
  33.3 7.0 %collective-permute-start.6 = (f32[128,256]{1,0:T(8,128)S(1)}, f32[128,256]{1,0:T(8,128)S(1)}, u32[]{:S(2)}, u32[]{:S(2)}) collective-permute-start(f32[128,256]{1,0:T(8,128)S(1)} %get-tuple-element.164), channel_id=1, source_target_pairs={{0,1},{1,0},{2,3},{3,2},{4,5},{5,4},{6,7},{7,6},{8,9},{9,8},{10,11... | collective-permute-start | bytes 393224 | tf_op jit(solution)/shard_map/ppermute | solution.py:67
  36.8 5.7 %collective-permute-start.7 = (f32[128,256]{1,0:T(8,128)S(1)}, f32[128,256]{1,0:T(8,128)S(1)}, u32[]{:S(2)}, u32[]{:S(2)}) collective-permute-start(f32[128,256]{1,0:T(8,128)S(1)} %get-tuple-element.166), channel_id=1, source_target_pairs={{0,16},{1,4},{2,18},{3,6},{4,1},{5,8},{6,3},{7,10},{8,5},{9,12},{1... | collective-permute-start | bytes 393224 | tf_op jit(solution)/shard_map/ppermute | solution.py:67
  36.9 5.6 %collective-permute-start.8 = (f32[32,256]{1,0:T(8,128)S(1)}, f32[32,256]{1,0:T(8,128)S(1)}, u32[]{:S(2)}, u32[]{:S(2)}) collective-permute-start(f32[32,256]{1,0:T(8,128)S(1)} %get-tuple-element.167), channel_id=1, source_target_pairs={{0,2},{1,3},{2,0},{3,1},{4,6},{5,7},{6,4},{7,5},{8,10},{9,11},{10,... | collective-permute-start | bytes 98312 | tf_op jit(solution)/shard_map/ppermute | solution.py:67
  38.3 4.2 %collective-permute-start.10 = (f32[8,8,128]{2,1,0:T(8,128)S(1)}, f32[8,8,128]{2,1,0:T(8,128)S(1)}, u32[]{:S(2)}, u32[]{:S(2)}) collective-permute-start(f32[8,8,128]{2,1,0:T(8,128)S(1)} %get-tuple-element.173), channel_id=1, source_target_pairs={{0,1},{1,0},{2,3},{3,2},{4,5},{5,4},{6,7},{7,6},{8,9},{9,8},{10,11... | collective-permute-start | bytes 98312 | tf_op jit(solution)/shard_map/ppermute | solution.py:67
  43.7 6.1 %collective-permute-start.12 = (f32[2,128,256]{2,1,0:T(8,128)S(1)}, f32[2,128,256]{2,1,0:T(8,128)S(1)}, u32[]{:S(2)}, u32[]{:S(2)}) collective-permute-start(f32[2,128,256]{2,1,0:T(8,128)S(1)} %get-tuple-element.177), channel_id=1, source_target_pairs={{0,16},{1,4},{2,18},{3,6},{4,1},{5,8},{6,3},{7,10},{8,5},{9,12},{1... | collective-permute-start | bytes 786440 | tf_op jit(solution)/shard_map/ppermute | solution.py:67
  43.7 4.0 %collective-permute-start.13 = (f32[2,32,256]{2,1,0:T(8,128)S(1)}, f32[2,32,256]{2,1,0:T(8,128)S(1)}, u32[]{:S(2)}, u32[]{:S(2)}) collective-permute-start(f32[2,32,256]{2,1,0:T(8,128)S(1)} %get-tuple-element.178), channel_id=1, source_target_pairs={{0,2},{1,3},{2,0},{3,1},{4,6},{5,7},{6,4},{7,5},{8,10},{9,11},{10,... | collective-permute-start | bytes 196616 | tf_op jit(solution)/shard_map/ppermute | solution.py:67
  44.7 3.1 %collective-permute-start.14 = (f32[8,8,128]{2,1,0:T(8,128)S(1)}, f32[8,8,128]{2,1,0:T(8,128)S(1)}, u32[]{:S(2)}, u32[]{:S(2)}) collective-permute-start(f32[8,8,128]{2,1,0:T(8,128)S(1)} %get-tuple-element.180), channel_id=1, source_target_pairs={{0,2},{1,3},{2,0},{3,1},{4,6},{5,7},{6,4},{7,5},{8,10},{9,11},{10,... | collective-permute-start | bytes 98312 | tf_op jit(solution)/shard_map/ppermute | solution.py:67
  50.6 4.4 %collective-permute-start.15 = (f32[128,256]{1,0:T(8,128)S(1)}, f32[128,256]{1,0:T(8,128)S(1)}, u32[]{:S(2)}, u32[]{:S(2)}) collective-permute-start(f32[128,256]{1,0:T(8,128)S(1)} %get-tuple-element.182), channel_id=1, source_target_pairs={{0,1},{1,0},{2,3},{3,2},{4,5},{5,4},{6,7},{7,6},{8,9},{9,8},{10,11... | collective-permute-start | bytes 393224 | tf_op jit(solution)/shard_map/ppermute | solution.py:67
  51.2 5.3 %collective-permute-start.17 = (f32[128,256]{1,0:T(8,128)S(1)}, f32[128,256]{1,0:T(8,128)S(1)}, u32[]{:S(2)}, u32[]{:S(2)}) collective-permute-start(f32[128,256]{1,0:T(8,128)S(1)} %get-tuple-element.187), channel_id=1, source_target_pairs={{0,16},{1,4},{2,18},{3,6},{4,1},{5,8},{6,3},{7,10},{8,5},{9,12},{1... | collective-permute-start | bytes 393224 | tf_op jit(solution)/shard_map/ppermute | solution.py:67
  51.5 5.0 %collective-permute-start.18 = (f32[32,256]{1,0:T(8,128)S(1)}, f32[32,256]{1,0:T(8,128)S(1)}, u32[]{:S(2)}, u32[]{:S(2)}) collective-permute-start(f32[32,256]{1,0:T(8,128)S(1)} %get-tuple-element.188), channel_id=1, source_target_pairs={{0,2},{1,3},{2,0},{3,1},{4,6},{5,7},{6,4},{7,5},{8,10},{9,11},{10,... | collective-permute-start | bytes 98312 | tf_op jit(solution)/shard_map/ppermute | solution.py:67
  52.3 4.2 %collective-permute-start.19 = (f32[8,8,128]{2,1,0:T(8,128)S(1)}, f32[8,8,128]{2,1,0:T(8,128)S(1)}, u32[]{:S(2)}, u32[]{:S(2)}) collective-permute-start(f32[8,8,128]{2,1,0:T(8,128)S(1)} %get-tuple-element.190), channel_id=1, source_target_pairs={{0,4},{1,5},{2,6},{3,7},{4,0},{5,1},{6,2},{7,3},{8,12},{9,13},{10,... | collective-permute-start | bytes 98312 | tf_op jit(solution)/shard_map/ppermute | solution.py:67
  52.9 3.6 %collective-permute-start.16 = (f32[1,128]{1,0:T(1,128)S(1)}, f32[1,128]{1,0:T(1,128)S(1)}, u32[]{:S(2)}, u32[]{:S(2)}) collective-permute-start(f32[1,128]{1,0:T(1,128)S(1)} %get-tuple-element.185.own), channel_id=1, source_target_pairs={{0,16},{1,2},{2,1},{3,19},{4,20},{5,6},{6,5},{7,23},{8,24},{9,10},... | collective-permute-start | bytes 1544 | tf_op jit(solution)/shard_map/ppermute | solution.py:67
  57.3 3.1 %collective-permute-start.20 = (f32[128,256]{1,0:T(8,128)S(1)}, f32[128,256]{1,0:T(8,128)S(1)}, u32[]{:S(2)}, u32[]{:S(2)}) collective-permute-start(f32[128,256]{1,0:T(8,128)S(1)} %get-tuple-element.192), channel_id=1, source_target_pairs={{0,1},{1,0},{2,3},{3,2},{4,5},{5,4},{6,7},{7,6},{8,9},{9,8},{10,11... | collective-permute-start | bytes 393224 | tf_op jit(solution)/shard_map/ppermute | solution.py:67
  59.2 4.8 %collective-permute-start.21 = (f32[128,256]{1,0:T(8,128)S(1)}, f32[128,256]{1,0:T(8,128)S(1)}, u32[]{:S(2)}, u32[]{:S(2)}) collective-permute-start(f32[128,256]{1,0:T(8,128)S(1)} %get-tuple-element.194), channel_id=1, source_target_pairs={{0,16},{1,4},{2,18},{3,6},{4,1},{5,8},{6,3},{7,10},{8,5},{9,12},{1... | collective-permute-start | bytes 393224 | tf_op jit(solution)/shard_map/ppermute | solution.py:67
  59.6 4.3 %collective-permute-start.23 = (f32[8,8,128]{2,1,0:T(8,128)S(1)}, f32[8,8,128]{2,1,0:T(8,128)S(1)}, u32[]{:S(2)}, u32[]{:S(2)}) collective-permute-start(f32[8,8,128]{2,1,0:T(8,128)S(1)} %get-tuple-element.197), channel_id=1, source_target_pairs={{0,8},{1,9},{2,10},{3,11},{4,12},{5,13},{6,14},{7,15},{8,0},{9,1},... | collective-permute-start | bytes 98312 | tf_op jit(solution)/shard_map/ppermute | solution.py:67
  64.8 4.8 %collective-permute-start.24 = (f32[128,256]{1,0:T(8,128)S(1)}, f32[128,256]{1,0:T(8,128)S(1)}, u32[]{:S(2)}, u32[]{:S(2)}) collective-permute-start(f32[128,256]{1,0:T(8,128)S(1)} %get-tuple-element.199), channel_id=1, source_target_pairs={{0,1},{1,0},{2,3},{3,2},{4,5},{5,4},{6,7},{7,6},{8,9},{9,8},{10,11... | collective-permute-start | bytes 393224 | tf_op jit(solution)/shard_map/ppermute | solution.py:67
  66.1 4.8 %collective-permute-start.25 = (f32[128,256]{1,0:T(8,128)S(1)}, f32[128,256]{1,0:T(8,128)S(1)}, u32[]{:S(2)}, u32[]{:S(2)}) collective-permute-start(f32[128,256]{1,0:T(8,128)S(1)} %get-tuple-element.203), channel_id=1, source_target_pairs={{0,16},{1,4},{2,18},{3,6},{4,1},{5,8},{6,3},{7,10},{8,5},{9,12},{1... | collective-permute-start | bytes 393224 | tf_op jit(solution)/shard_map/ppermute | solution.py:67
  66.8 4.1 %collective-permute-start.26 = (f32[32,256]{1,0:T(8,128)S(1)}, f32[32,256]{1,0:T(8,128)S(1)}, u32[]{:S(2)}, u32[]{:S(2)}) collective-permute-start(f32[32,256]{1,0:T(8,128)S(1)} %get-tuple-element.204), channel_id=1, source_target_pairs={{0,2},{1,3},{2,0},{3,1},{4,6},{5,7},{6,4},{7,5},{8,10},{9,11},{10,... | collective-permute-start | bytes 98312 | tf_op jit(solution)/shard_map/ppermute | solution.py:67
  71.7 3.1 %collective-permute-start.27 = (f32[128,256]{1,0:T(8,128)S(1)}, f32[128,256]{1,0:T(8,128)S(1)}, u32[]{:S(2)}, u32[]{:S(2)}) collective-permute-start(f32[128,256]{1,0:T(8,128)S(1)} %get-tuple-element.206), channel_id=1, source_target_pairs={{0,1},{1,0},{2,3},{3,2},{4,5},{5,4},{6,7},{7,6},{8,9},{9,8},{10,11... | collective-permute-start | bytes 393224 | tf_op jit(solution)/shard_map/ppermute | solution.py:67
  72.8 4.7 %collective-permute-start.28 = (f32[128,256]{1,0:T(8,128)S(1)}, f32[128,256]{1,0:T(8,128)S(1)}, u32[]{:S(2)}, u32[]{:S(2)}) collective-permute-start(f32[128,256]{1,0:T(8,128)S(1)} %get-tuple-element.211), channel_id=1, source_target_pairs={{0,16},{1,4},{2,18},{3,6},{4,1},{5,8},{6,3},{7,10},{8,5},{9,12},{1... | collective-permute-start | bytes 393224 | tf_op jit(solution)/shard_map/ppermute | solution.py:67
  72.8 3.4 %collective-permute-start.29 = (f32[32,256]{1,0:T(8,128)S(1)}, f32[32,256]{1,0:T(8,128)S(1)}, u32[]{:S(2)}, u32[]{:S(2)}) collective-permute-start(f32[32,256]{1,0:T(8,128)S(1)} %get-tuple-element.212), channel_id=1, source_target_pairs={{0,2},{1,3},{2,0},{3,1},{4,6},{5,7},{6,4},{7,5},{8,10},{9,11},{10,... | collective-permute-start | bytes 98312 | tf_op jit(solution)/shard_map/ppermute | solution.py:67
  78.8 4.7 %collective-permute-start.31 = (f32[128,256]{1,0:T(8,128)S(1)}, f32[128,256]{1,0:T(8,128)S(1)}, u32[]{:S(2)}, u32[]{:S(2)}) collective-permute-start(f32[128,256]{1,0:T(8,128)S(1)} %get-tuple-element.216), channel_id=1, source_target_pairs={{0,16},{1,4},{2,18},{3,6},{4,1},{5,8},{6,3},{7,10},{8,5},{9,12},{1... | collective-permute-start | bytes 393224 | tf_op jit(solution)/shard_map/ppermute | solution.py:67
  79.5 3.1 %collective-permute-start.32 = (f32[32,256]{1,0:T(8,128)S(1)}, f32[32,256]{1,0:T(8,128)S(1)}, u32[]{:S(2)}, u32[]{:S(2)}) collective-permute-start(f32[32,256]{1,0:T(8,128)S(1)} %get-tuple-element.217), channel_id=1, source_target_pairs={{0,2},{1,3},{2,0},{3,1},{4,6},{5,7},{6,4},{7,5},{8,10},{9,11},{10,... | collective-permute-start | bytes 98312 | tf_op jit(solution)/shard_map/ppermute | solution.py:67
  85.5 4.7 %collective-permute-start.34 = (f32[128,256]{1,0:T(8,128)S(1)}, f32[128,256]{1,0:T(8,128)S(1)}, u32[]{:S(2)}, u32[]{:S(2)}) collective-permute-start(f32[128,256]{1,0:T(8,128)S(1)} %get-tuple-element.225), channel_id=1, source_target_pairs={{0,16},{1,4},{2,18},{3,6},{4,1},{5,8},{6,3},{7,10},{8,5},{9,12},{1... | collective-permute-start | bytes 393224 | tf_op jit(solution)/shard_map/ppermute | solution.py:67
  86.1 3.1 %collective-permute-start.35 = (f32[32,256]{1,0:T(8,128)S(1)}, f32[32,256]{1,0:T(8,128)S(1)}, u32[]{:S(2)}, u32[]{:S(2)}) collective-permute-start(f32[32,256]{1,0:T(8,128)S(1)} %get-tuple-element.226), channel_id=1, source_target_pairs={{0,2},{1,3},{2,0},{3,1},{4,6},{5,7},{6,4},{7,5},{8,10},{9,11},{10,... | collective-permute-start | bytes 98312 | tf_op jit(solution)/shard_map/ppermute | solution.py:67
  91.4 4.7 %collective-permute-start.37 = (f32[128,256]{1,0:T(8,128)S(1)}, f32[128,256]{1,0:T(8,128)S(1)}, u32[]{:S(2)}, u32[]{:S(2)}) collective-permute-start(f32[128,256]{1,0:T(8,128)S(1)} %get-tuple-element.232), channel_id=1, source_target_pairs={{0,16},{1,4},{2,18},{3,6},{4,1},{5,8},{6,3},{7,10},{8,5},{9,12},{1... | collective-permute-start | bytes 393224 | tf_op jit(solution)/shard_map/ppermute | solution.py:67
  92.1 3.1 %collective-permute-start.38 = (f32[32,256]{1,0:T(8,128)S(1)}, f32[32,256]{1,0:T(8,128)S(1)}, u32[]{:S(2)}, u32[]{:S(2)}) collective-permute-start(f32[32,256]{1,0:T(8,128)S(1)} %get-tuple-element.233), channel_id=1, source_target_pairs={{0,2},{1,3},{2,0},{3,1},{4,6},{5,7},{6,4},{7,5},{8,10},{9,11},{10,... | collective-permute-start | bytes 98312 | tf_op jit(solution)/shard_map/ppermute | solution.py:67
  97.4 4.7 %collective-permute-start.40 = (f32[128,256]{1,0:T(8,128)S(1)}, f32[128,256]{1,0:T(8,128)S(1)}, u32[]{:S(2)}, u32[]{:S(2)}) collective-permute-start(f32[128,256]{1,0:T(8,128)S(1)} %get-tuple-element.239), channel_id=1, source_target_pairs={{0,16},{1,4},{2,18},{3,6},{4,1},{5,8},{6,3},{7,10},{8,5},{9,12},{1... | collective-permute-start | bytes 393224 | tf_op jit(solution)/shard_map/ppermute | solution.py:67
  98.1 3.1 %collective-permute-start.41 = (f32[32,256]{1,0:T(8,128)S(1)}, f32[32,256]{1,0:T(8,128)S(1)}, u32[]{:S(2)}, u32[]{:S(2)}) collective-permute-start(f32[32,256]{1,0:T(8,128)S(1)} %get-tuple-element.240), channel_id=1, source_target_pairs={{0,2},{1,3},{2,0},{3,1},{4,6},{5,7},{6,4},{7,5},{8,10},{9,11},{10,... | collective-permute-start | bytes 98312 | tf_op jit(solution)/shard_map/ppermute | solution.py:67
  103.4 4.7 %collective-permute-start.43 = (f32[128,256]{1,0:T(8,128)S(1)}, f32[128,256]{1,0:T(8,128)S(1)}, u32[]{:S(2)}, u32[]{:S(2)}) collective-permute-start(f32[128,256]{1,0:T(8,128)S(1)} %get-tuple-element.246), channel_id=1, source_target_pairs={{0,16},{1,4},{2,18},{3,6},{4,1},{5,8},{6,3},{7,10},{8,5},{9,12},{1... | collective-permute-start | bytes 393224 | tf_op jit(solution)/shard_map/ppermute | solution.py:67
  104.1 3.1 %collective-permute-start.44 = (f32[32,256]{1,0:T(8,128)S(1)}, f32[32,256]{1,0:T(8,128)S(1)}, u32[]{:S(2)}, u32[]{:S(2)}) collective-permute-start(f32[32,256]{1,0:T(8,128)S(1)} %get-tuple-element.247), channel_id=1, source_target_pairs={{0,2},{1,3},{2,0},{3,1},{4,6},{5,7},{6,4},{7,5},{8,10},{9,11},{10,... | collective-permute-start | bytes 98312 | tf_op jit(solution)/shard_map/ppermute | solution.py:67
  109.3 4.7 %collective-permute-start.46 = (f32[128,256]{1,0:T(8,128)S(1)}, f32[128,256]{1,0:T(8,128)S(1)}, u32[]{:S(2)}, u32[]{:S(2)}) collective-permute-start(f32[128,256]{1,0:T(8,128)S(1)} %get-tuple-element.253), channel_id=1, source_target_pairs={{0,16},{1,4},{2,18},{3,6},{4,1},{5,8},{6,3},{7,10},{8,5},{9,12},{1... | collective-permute-start | bytes 393224 | tf_op jit(solution)/shard_map/ppermute | solution.py:67
  110.0 3.1 %collective-permute-start.47 = (f32[32,256]{1,0:T(8,128)S(1)}, f32[32,256]{1,0:T(8,128)S(1)}, u32[]{:S(2)}, u32[]{:S(2)}) collective-permute-start(f32[32,256]{1,0:T(8,128)S(1)} %get-tuple-element.254), channel_id=1, source_target_pairs={{0,2},{1,3},{2,0},{3,1},{4,6},{5,7},{6,4},{7,5},{8,10},{9,11},{10,... | collective-permute-start | bytes 98312 | tf_op jit(solution)/shard_map/ppermute | solution.py:67
  115.3 4.7 %collective-permute-start.49 = (f32[128,256]{1,0:T(8,128)S(1)}, f32[128,256]{1,0:T(8,128)S(1)}, u32[]{:S(2)}, u32[]{:S(2)}) collective-permute-start(f32[128,256]{1,0:T(8,128)S(1)} %get-tuple-element.260), channel_id=1, source_target_pairs={{0,16},{1,4},{2,18},{3,6},{4,1},{5,8},{6,3},{7,10},{8,5},{9,12},{1... | collective-permute-start | bytes 393224 | tf_op jit(solution)/shard_map/ppermute | solution.py:67
  116.0 3.1 %collective-permute-start.50 = (f32[32,256]{1,0:T(8,128)S(1)}, f32[32,256]{1,0:T(8,128)S(1)}, u32[]{:S(2)}, u32[]{:S(2)}) collective-permute-start(f32[32,256]{1,0:T(8,128)S(1)} %get-tuple-element.261), channel_id=1, source_target_pairs={{0,2},{1,3},{2,0},{3,1},{4,6},{5,7},{6,4},{7,5},{8,10},{9,11},{10,... | collective-permute-start | bytes 98312 | tf_op jit(solution)/shard_map/ppermute | solution.py:67
  121.2 4.7 %collective-permute-start.52 = (f32[128,256]{1,0:T(8,128)S(1)}, f32[128,256]{1,0:T(8,128)S(1)}, u32[]{:S(2)}, u32[]{:S(2)}) collective-permute-start(f32[128,256]{1,0:T(8,128)S(1)} %get-tuple-element.267), channel_id=1, source_target_pairs={{0,16},{1,4},{2,18},{3,6},{4,1},{5,8},{6,3},{7,10},{8,5},{9,12},{1... | collective-permute-start | bytes 393224 | tf_op jit(solution)/shard_map/ppermute | solution.py:67
  121.9 3.1 %collective-permute-start.53 = (f32[32,256]{1,0:T(8,128)S(1)}, f32[32,256]{1,0:T(8,128)S(1)}, u32[]{:S(2)}, u32[]{:S(2)}) collective-permute-start(f32[32,256]{1,0:T(8,128)S(1)} %get-tuple-element.268), channel_id=1, source_target_pairs={{0,2},{1,3},{2,0},{3,1},{4,6},{5,7},{6,4},{7,5},{8,10},{9,11},{10,... | collective-permute-start | bytes 98312 | tf_op jit(solution)/shard_map/ppermute | solution.py:67
  127.6 11.5 %collective-permute-start.54 = (f32[2,256,256]{2,1,0:T(8,128)S(1)}, f32[2,256,256]{2,1,0:T(8,128)S(1)}, u32[]{:S(2)}, u32[]{:S(2)}) collective-permute-start(f32[2,256,256]{2,1,0:T(8,128)S(1)} %both.1.own), channel_id=1, source_target_pairs={{0,16},{1,2},{2,1},{3,19},{4,20},{5,6},{6,5},{7,23},{8,24},{9,10},... | collective-permute-start | bytes 1572872 | tf_op jit(solution)/shard_map/ppermute | solution.py:67
  130.8 9.6 %collective-permute-start.56 = (f32[2,64,128]{2,1,0:T(8,128)S(1)}, f32[2,64,128]{2,1,0:T(8,128)S(1)}, u32[]{:S(2)}, u32[]{:S(2)}) collective-permute-start(f32[2,64,128]{2,1,0:T(8,128)S(1)} %get-tuple-element.276), channel_id=1, source_target_pairs={{0,0},{1,2},{2,1},{3,3},{4,4},{5,6},{6,5},{7,7},{8,8},{9,10},{10,9... | collective-permute-start | bytes 196616 | tf_op jit(solution)/shard_map/ppermute | solution.py:67
  133.3 7.1 %collective-permute-start.57 = (f32[2,64,128]{2,1,0:T(8,128)S(1)}, f32[2,64,128]{2,1,0:T(8,128)S(1)}, u32[]{:S(2)}, u32[]{:S(2)}) collective-permute-start(f32[2,64,128]{2,1,0:T(8,128)S(1)} %get-tuple-element.277), channel_id=1, source_target_pairs={{0,4},{1,6},{2,5},{3,7},{4,0},{5,2},{6,1},{7,3},{8,12},{9,14},{10,... | collective-permute-start | bytes 196616 | tf_op jit(solution)/shard_map/ppermute | solution.py:67
  135.0 6.2 %collective-permute-start.58 = (f32[2,64,128]{2,1,0:T(8,128)S(1)}, f32[2,64,128]{2,1,0:T(8,128)S(1)}, u32[]{:S(2)}, u32[]{:S(2)}) collective-permute-start(f32[2,64,128]{2,1,0:T(8,128)S(1)} %get-tuple-element.278), channel_id=1, source_target_pairs={{0,8},{1,10},{2,9},{3,11},{4,12},{5,14},{6,13},{7,15},{8,0},{9,2},... | collective-permute-start | bytes 196616 | tf_op jit(solution)/shard_map/ppermute | solution.py:67
  135.9 6.5 %collective-permute-start.59 = (f32[2,64,128]{2,1,0:T(8,128)S(1)}, f32[2,64,128]{2,1,0:T(8,128)S(1)}, u32[]{:S(2)}, u32[]{:S(2)}) collective-permute-start(f32[2,64,128]{2,1,0:T(8,128)S(1)} %get-tuple-element.279), channel_id=1, source_target_pairs={{0,12},{1,14},{2,13},{3,15},{4,8},{5,10},{6,9},{7,11},{8,4},{9,6},... | collective-permute-start | bytes 196616 | tf_op jit(solution)/shard_map/ppermute | solution.py:67
  (46 other events, 123.3 us)

commit v11 on v10

--- a/solution.py
+++ b/solution.py
@@ -190,8 +190,10 @@
         rims(flags, out, zo.at[n], co.at[n], yo.at[n])
 
 
-def settle_pair_kernel(flags, a, b, recv, a_out, b_out, sems):
-    choose(flags, [(a, recv.at[0], a_out), (b, recv.at[1], b_out)], sems)
+def settle_pair_kernel(flags, a, b, *rest):
+    *recv, a_out, b_out, sems = rest
+    recv = recv if len(recv) == 2 else (recv[0].at[0], recv[0].at[1])
+    choose(flags, [(a, recv[0], a_out), (b, recv[1], b_out)], sems)
 
 
 def select_kernel(flags, own, recv, *outs):
@@ -532,14 +534,12 @@
     density, p_now, *out = call(settle_kernel, "settle",
                                 [field, field] + [shaped(2, *r.shape) for r in rim],
                                 flags_in, log_density, fwd_now, *got, far=2)
-    zm, cm = send(out[0], z_perm), send(out[1], c_perm)
-    ym = send(after(out[2], cm), y_perm)
+    zm, cm, ym = halo(*out)
     vel, p_before = call(settle_pair_kernel, "settle_model", [field, field],
                          flags, velocity, fwd_before, got_model, weight=0.6, far=2)
     parts = call(first_inner_kernel, "first_inner", [field] * 7, flags, density, p_now, cm,
                  near, deep, weight=1.3)
-    got_adjoint = send(
-        jnp.stack([after(adj_now, parts[0]), after(adj_before, parts[0])]), swap_perm)
+    got_adjoint = [send(after(v, parts[0]), swap_perm) for v in (adj_now, adj_before)]
 
     new, zo, co, yo, k0, ki, kx, kz = call(
         first_outer_kernel, "first_outer", [field] + rim + [field] * 4,
@@ -596,7 +596,7 @@
             args[1] = after(part, got_cells)
         if t == double:
             u_now, u_before = call(settle_pair_kernel, "settle_adjoint", [field, field], flags,
-                                   adj_now, adj_before, got_adjoint, weight=0.6, far=2)
+                                   adj_now, adj_before, *got_adjoint, weight=0.6, far=2)
             args.append(u_now)
         outs = [field] + ([shaped(2, *r.shape) for r in rim] if t == double else rim)
         if extra:

time: 145 us -> 129 us (0.89)
  local copies, waits for them, and re-layouts: 9.64 us -> 1.59 us
  waiting for transfers between devices: 28 us -> 20.6 us
  other arithmetic: 2.96 us -> 1.32 us
  starting transfers between devices: 56.9 us -> 58.4 us
    unnamed x68 -> x38, local copies, waits for them, and re-layouts: 9.56 us -> 1.5 us
    ppermute x60 -> x61, waiting for transfers between devices: 28 us -> 20.6 us  [send(): return lax.ppermute(value, ALL, pairs)]
    ppermute x60 -> x61, starting transfers between devices: 56.9 us -> 58.4 us  [send(): return lax.ppermute(value, ALL, pairs)]
  transfers between devices with their start and end apart: 60 -> 61, of which waited for: 29 -> 26; matrix products, arithmetic and copies ran while one was open for 2% -> 1% of each run, Pallas kernels for 21% -> 24%
where the time goes in v11:
time: 129 us
  starting transfers between devices  58.4 us (45%)
  Pallas kernels  45.3 us (35%)
  waiting for transfers between devices  20.6 us (16%)
  local copies, waits for them, and re-layouts  1.59 us (1%)
  other arithmetic  1.32 us (1%)
    ppermute x61, starting transfers between devices, send(): return lax.ppermute(value, ALL, pairs)  58.4 us
    pallas_call x41, Pallas kernels, call(): pl.pallas_call(kernel, name=name, out_shape=outs, in_specs=specs, out_spe...  45.3 us
    ppermute x61, waiting for transfers between devices, send(): return lax.ppermute(value, ALL, pairs)  20.6 us
  transfers between devices with their start and end apart: 61, of which 26 were waited for; matrix products, arithmetic and copies ran while one was open for 1% of the time, Pallas kernels for 24%

profile of v11, /device:TPU:1, one launch (start us, length us, event | category | flops | bytes accessed | tf_op | source)
XLA Modules:
  0.0 128.5 jit_solution(3447821170492174607)
XLA Ops:
  0.6 2.7 %collective-permute-start.1 = (f32[256,256]{1,0:T(8,128)}, f32[256,256]{1,0:T(8,128)S(1)}, u32[]{:S(2)}, u32[]{:S(2)}) collective-permute-start(f32[256,256]{1,0:T(8,128)} %bitcast.22), channel_id=1, source_target_pairs={{0,16},{1,2},{2,1},{3,19},{4,20},{5,6},{6,5},{7,23},{8,24},{9,10},... | collective-permute-start | bytes 786440 | tf_op jit(solution)/shard_map/ppermute | solution.py:67
  3.4 1.1 pad_maximum_fusion
  4.5 1.7 %collective-permute-start.2 = (f32[2,256,256]{2,1,0:T(8,128)S(1)}, f32[2,256,256]{2,1,0:T(8,128)S(1)}, u32[]{:S(2)}, u32[]{:S(2)}) collective-permute-start(f32[2,256,256]{2,1,0:T(8,128)S(1)} %pad_maximum_fusion), channel_id=1, source_target_pairs={{0,16},{1,2},{2,1},{3,19},{4,20},{5,6},{6,5},{7,23},{8,24},{9,10},... | collective-permute-start | bytes 1572872 | tf_op jit(solution)/shard_map/ppermute | solution.py:67
  8.7 2.0 %collective-permute-done.recv_a = f32[256,256]{1,0:T(8,128)S(1)} collective-permute-done((f32[256,256]{1,0:T(8,128)}, f32[256,256]{1,0:T(8,128)S(1)}, u32[]{:S(2)}, u32[]{:S(2)}) %collective-permute-start) | collective-permute-done | bytes 262176 | tf_op jit(solution)/shard_map/ppermute | solution.py:67
  11.8 1.8 %collective-permute-start.4 = (f32[2,128,256]{2,1,0:T(8,128)S(1)}, f32[2,128,256]{2,1,0:T(8,128)S(1)}, u32[]{:S(2)}, u32[]{:S(2)}) collective-permute-start(f32[2,128,256]{2,1,0:T(8,128)S(1)} %get-tuple-element.155), channel_id=1, source_target_pairs={{0,16},{1,4},{2,18},{3,6},{4,1},{5,8},{6,3},{7,10},{8,5},{9,12},{1... | collective-permute-start | bytes 786440 | tf_op jit(solution)/shard_map/ppermute | solution.py:67
  14.5 1.3 %first_inner.1 = (f32[256,256]{1,0:T(8,128)S(1)}, f32[256,256]{1,0:T(8,128)S(1)}, f32[256,256]{1,0:T(8,128)S(1)}, f32[256,256]{1,0:T(8,128)S(1)}, f32[256,256]{1...) custom-call(s32[8]{0:T(128)S(1)} %stack.32.flags, f32[256,256]{1,0:T(8,128)S(1)} %get-tuple-element.145.lr, ...), custom_call_target="tpu_custom_call" | custom-call | flops 1000 | bytes 4681000 | tf_op jit(solution)/shard_map/first_inner/pallas_call | solution.py:467
  15.9 1.3 %collective-permute-start.9 = (f32[256,256]{1,0:T(8,128)S(1)}, f32[256,256]{1,0:T(8,128)S(1)}, u32[]{:S(2)}, u32[]{:S(2)}) collective-permute-start(f32[256,256]{1,0:T(8,128)S(1)} %bitcast.24), channel_id=1, source_target_pairs={{0,16},{1,2},{2,1},{3,19},{4,20},{5,6},{6,5},{7,23},{8,24},{9,10},... | collective-permute-start | bytes 786440 | tf_op jit(solution)/shard_map/ppermute | solution.py:67
  19.5 1.1 collective-permute-start.6
  22.7 1.5 %collective-permute-start.11 = (f32[8,8,128]{2,1,0:T(8,128)S(1)}, f32[8,8,128]{2,1,0:T(8,128)S(1)}, u32[]{:S(2)}, u32[]{:S(2)}) collective-permute-start(f32[8,8,128]{2,1,0:T(8,128)S(1)} %get-tuple-element.171), channel_id=1, source_target_pairs={{0,1},{1,0},{2,3},{3,2},{4,5},{5,4},{6,7},{7,6},{8,9},{9,8},{10,11... | collective-permute-start | bytes 98312 | tf_op jit(solution)/shard_map/ppermute | solution.py:67
  24.2 1.3 %forward_inner.7 = (f32[256,256]{1,0:T(8,128)S(1)}, f32[256,256]{1,0:T(8,128)S(1)}) custom-call(s32[8]{0:T(128)S(1)} %stack.32.flags, s32[16]{0:T(128)S(1)} %copy-done.8, f32[8,16]{1,0:T(8,128)S(1)} %copy-done.3, f32[256,256]{1,0:T(8,128)S(1)} %get-tuple-element.157.cur.prev.before.state, f32[256,256]{1,0:T(8,128)S(1)} %get-tuple-element.142.cur.prev.before, ...), custom_call_target="tpu_custom_call" | custom-call | flops 1000 | bytes 4321000 | tf_op jit(solution)/shard_map/forward_inner/pallas_call | solution.py:467
  28.6 1.2 collective-permute-start.15
  29.8 1.3 %forward_inner.8 = (f32[256,256]{1,0:T(8,128)S(1)}, f32[256,256]{1,0:T(8,128)S(1)}) custom-call(s32[8]{0:T(128)S(1)} %stack.32.flags, s32[16]{0:T(128)S(1)} %copy-done.8, f32[8,16]{1,0:T(8,128)S(1)} %copy-done.3, f32[256,256]{1,0:T(8,128)S(1)} %get-tuple-element.172.cur.prev.before.state, f32[256,256]{1,0:T(8,128)S(1)} %get-tuple-element.157.cur.prev.before.state, ...), custom_call_target="tpu_custom_call" | custom-call | flops 1000 | bytes 4321000 | tf_op jit(solution)/shard_map/forward_inner/pallas_call | solution.py:467
  32.1 2.0 %collective-permute-done.13.zm.u_zm = f32[2,128,256]{2,1,0:T(8,128)S(1)} collective-permute-done((f32[2,128,256]{2,1,0:T(8,128)S(1)}, f32[2,128,256]{2,1,0:T(8,128)S(1)}, u32[]{:S(2)}, u32[]{:S(2)}) %collective-permute-start.13) | collective-permute-done | bytes 262176 | tf_op jit(solution)/shard_map/ppermute | solution.py:67
  36.9 1.8 %collective-permute-start.20 = (f32[8,8,128]{2,1,0:T(8,128)S(1)}, f32[8,8,128]{2,1,0:T(8,128)S(1)}, u32[]{:S(2)}, u32[]{:S(2)}) collective-permute-start(f32[8,8,128]{2,1,0:T(8,128)S(1)} %get-tuple-element.188), channel_id=1, source_target_pairs={{0,4},{1,5},{2,6},{3,7},{4,0},{5,1},{6,2},{7,3},{8,12},{9,13},{10,... | collective-permute-start | bytes 98312 | tf_op jit(solution)/shard_map/ppermute | solution.py:67
  39.1 1.3 %forward_inner.9 = (f32[256,256]{1,0:T(8,128)S(1)}, f32[256,256]{1,0:T(8,128)S(1)}) custom-call(s32[8]{0:T(128)S(1)} %stack.32.flags, s32[16]{0:T(128)S(1)} %copy-done.8, f32[8,16]{1,0:T(8,128)S(1)} %copy-done.3, f32[256,256]{1,0:T(8,128)S(1)} %get-tuple-element.179.cur.prev.before.state, f32[256,256]{1,0:T(8,128)S(1)} %get-tuple-element.172.cur.prev.before.state, ...), custom_call_target="tpu_custom_call" | custom-call | flops 1000 | bytes 4321000 | tf_op jit(solution)/shard_map/forward_inner/pallas_call | solution.py:467
  40.5 1.2 collective-permute-done.17.got
  44.2 1.7 %collective-permute-start.24 = (f32[8,8,128]{2,1,0:T(8,128)S(1)}, f32[8,8,128]{2,1,0:T(8,128)S(1)}, u32[]{:S(2)}, u32[]{:S(2)}) collective-permute-start(f32[8,8,128]{2,1,0:T(8,128)S(1)} %get-tuple-element.195), channel_id=1, source_target_pairs={{0,8},{1,9},{2,10},{3,11},{4,12},{5,13},{6,14},{7,15},{8,0},{9,1},... | collective-permute-start | bytes 98312 | tf_op jit(solution)/shard_map/ppermute | solution.py:67
  45.9 1.3 %forward_inner.10 = (f32[256,256]{1,0:T(8,128)S(1)}, f32[256,256]{1,0:T(8,128)S(1)}) custom-call(s32[8]{0:T(128)S(1)} %stack.32.flags, s32[16]{0:T(128)S(1)} %copy-done.8, f32[8,16]{1,0:T(8,128)S(1)} %copy-done.3, f32[256,256]{1,0:T(8,128)S(1)} %get-tuple-element.189.cur.prev.before.state, f32[256,256]{1,0:T(8,128)S(1)} %get-tuple-element.179.cur.prev.before.state, ...), custom_call_target="tpu_custom_call" | custom-call | flops 1000 | bytes 4321000 | tf_op jit(solution)/shard_map/forward_inner/pallas_call | solution.py:467
  48.8 2.0 %collective-permute-start.25 = (f32[128,256]{1,0:T(8,128)S(1)}, f32[128,256]{1,0:T(8,128)S(1)}, u32[]{:S(2)}, u32[]{:S(2)}) collective-permute-start(f32[128,256]{1,0:T(8,128)S(1)} %get-tuple-element.197), channel_id=1, source_target_pairs={{0,1},{1,0},{2,3},{3,2},{4,5},{5,4},{6,7},{7,6},{8,9},{9,8},{10,11... | collective-permute-start | bytes 393224 | tf_op jit(solution)/shard_map/ppermute | solution.py:67
  52.4 1.1 adjoint_first.1.u_part
  53.5 1.3 %forward_inner.11 = (f32[256,256]{1,0:T(8,128)S(1)}, f32[256,256]{1,0:T(8,128)S(1)}) custom-call(s32[8]{0:T(128)S(1)} %stack.32.flags, s32[16]{0:T(128)S(1)} %copy-done.8, f32[8,16]{1,0:T(8,128)S(1)} %copy-done.3, f32[256,256]{1,0:T(8,128)S(1)} %get-tuple-element.196.cur.prev.before.state, f32[256,256]{1,0:T(8,128)S(1)} %get-tuple-element.189.cur.prev.before.state, ...), custom_call_target="tpu_custom_call" | custom-call | flops 1000 | bytes 4321000 | tf_op jit(solution)/shard_map/forward_inner/pallas_call | solution.py:467
  57.8 1.1 collective-permute-start.30
  59.7 1.3 %forward_inner.12 = (f32[256,256]{1,0:T(8,128)S(1)}, f32[256,256]{1,0:T(8,128)S(1)}) custom-call(s32[8]{0:T(128)S(1)} %stack.32.flags, s32[16]{0:T(128)S(1)} %copy-done.8, f32[8,16]{1,0:T(8,128)S(1)} %copy-done.3, f32[256,256]{1,0:T(8,128)S(1)} %get-tuple-element.203.cur.prev.rest_2_.state, f32[256,256]{1,0:T(8,128)S(1)} %get-tuple-element.196.cur.prev.before.state, ...), custom_call_target="tpu_custom_call" | custom-call | flops 1000 | bytes 4321000 | tf_op jit(solution)/shard_map/forward_inner/pallas_call | solution.py:467
  63.5 1.4 %collective-permute-start.33 = (f32[32,256]{1,0:T(8,128)S(1)}, f32[32,256]{1,0:T(8,128)S(1)}, u32[]{:S(2)}, u32[]{:S(2)}) collective-permute-start(f32[32,256]{1,0:T(8,128)S(1)} %get-tuple-element.215), channel_id=1, source_target_pairs={{0,2},{1,3},{2,0},{3,1},{4,6},{5,7},{6,4},{7,5},{8,10},{9,11},{10,... | collective-permute-start | bytes 98312 | tf_op jit(solution)/shard_map/ppermute | solution.py:67
  64.9 1.3 %forward_inner.13 = (f32[256,256]{1,0:T(8,128)S(1)}, f32[256,256]{1,0:T(8,128)S(1)}) custom-call(s32[8]{0:T(128)S(1)} %stack.32.flags, s32[16]{0:T(128)S(1)} %copy-done.8, f32[8,16]{1,0:T(8,128)S(1)} %copy-done.3, f32[256,256]{1,0:T(8,128)S(1)} %get-tuple-element.211.cur.state.rest_1_, f32[256,256]{1,0:T(8,128)S(1)} %get-tuple-element.203.cur.prev.rest_2_.state, ...), custom_call_target="tpu_custom_call" | custom-call | flops 1000 | bytes 4321000 | tf_op jit(solution)/shard_map/forward_inner/pallas_call | solution.py:467
  67.6 1.5 %turn.1 = (f32[256,256]{1,0:T(8,128)S(1)}, f32[256,256]{1,0:T(8,128)S(1)}, f32[128,256]{1,0:T(8,128)S(1)}, f32[128,256]{1,0:T(8,128)S(1)}, f32[32,256]{1,0:T(8,128)S(1)}) custom-call(s32[8]{0:T(128)S(1)} %stack.32.flags, f32[256,256]{1,0:T(8,128)S(1)} %get-tuple-element.213.part, f32[256,256]{1,0:T(8,128)S(1)} %get-tuple-element.158.k0, ...), custom_call_target="tpu_custom_call" | custom-call | flops 1000 | bytes 1000 | tf_op jit(solution)/shard_map/turn/pallas_call | solution.py:467
  70.3 1.3 collective-permute-start.36
  71.5 1.7 %adjoint_inner.7 = (f32[256,256]{1,0:T(8,128)S(1)}, f32[256,256]{1,0:T(8,128)S(1)}) custom-call(s32[8]{0:T(128)S(1)} %stack.32.flags, f32[256,256]{1,0:T(8,128)S(1)} %get-tuple-element.219.cur.prev, f32[256,256]{1,0:T(8,128)S(1)} %get-tuple-element.168.rest_0_.cur.prev, f32[256,256]{1,0:T(8,128)S(1)} %get-tuple-element.158.k0, ...), custom_call_target="tpu_custom_call" | custom-call | flops 1000 | bytes 5401000 | tf_op jit(solution)/shard_map/adjoint_inner/pallas_call | solution.py:467
  76.3 1.2 collective-permute-start.39
  77.5 1.6 %adjoint_inner.8 = (f32[256,256]{1,0:T(8,128)S(1)}, f32[256,256]{1,0:T(8,128)S(1)}) custom-call(s32[8]{0:T(128)S(1)} %stack.32.flags, f32[256,256]{1,0:T(8,128)S(1)} %get-tuple-element.225.cur.prev, f32[256,256]{1,0:T(8,128)S(1)} %get-tuple-element.219.cur.prev, f32[256,256]{1,0:T(8,128)S(1)} %get-tuple-element.158.k0, ...), custom_call_target="tpu_custom_call" | custom-call | flops 1000 | bytes 5401000 | tf_op jit(solution)/shard_map/adjoint_inner/pallas_call | solution.py:467
  82.2 1.2 collective-permute-start.42
  83.4 1.6 %adjoint_inner.9 = (f32[256,256]{1,0:T(8,128)S(1)}, f32[256,256]{1,0:T(8,128)S(1)}) custom-call(s32[8]{0:T(128)S(1)} %stack.32.flags, f32[256,256]{1,0:T(8,128)S(1)} %get-tuple-element.232.cur.prev, f32[256,256]{1,0:T(8,128)S(1)} %get-tuple-element.225.cur.prev, f32[256,256]{1,0:T(8,128)S(1)} %get-tuple-element.158.k0, ...), custom_call_target="tpu_custom_call" | custom-call | flops 1000 | bytes 5401000 | tf_op jit(solution)/shard_map/adjoint_inner/pallas_call | solution.py:467
  88.2 1.2 collective-permute-start.45
  89.4 1.8 %adjoint_inner.10 = (f32[256,256]{1,0:T(8,128)S(1)}, f32[256,256]{1,0:T(8,128)S(1)}) custom-call(s32[8]{0:T(128)S(1)} %stack.32.flags, f32[256,256]{1,0:T(8,128)S(1)} %get-tuple-element.239.cur.prev, f32[256,256]{1,0:T(8,128)S(1)} %get-tuple-element.232.cur.prev, f32[256,256]{1,0:T(8,128)S(1)} %get-tuple-element.158.k0, ...), custom_call_target="tpu_custom_call" | custom-call | flops 1000 | bytes 5401000 | tf_op jit(solution)/shard_map/adjoint_inner/pallas_call | solution.py:467
  94.2 1.2 collective-permute-start.48
  95.4 1.6 %adjoint_inner.11 = (f32[256,256]{1,0:T(8,128)S(1)}, f32[256,256]{1,0:T(8,128)S(1)}) custom-call(s32[8]{0:T(128)S(1)} %stack.32.flags, f32[256,256]{1,0:T(8,128)S(1)} %get-tuple-element.246.cur.prev, f32[256,256]{1,0:T(8,128)S(1)} %get-tuple-element.239.cur.prev, f32[256,256]{1,0:T(8,128)S(1)} %get-tuple-element.158.k0, ...), custom_call_target="tpu_custom_call" | custom-call | flops 1000 | bytes 5401000 | tf_op jit(solution)/shard_map/adjoint_inner/pallas_call | solution.py:467
  100.1 1.2 collective-permute-start.51
  101.3 1.6 %adjoint_inner.12 = (f32[256,256]{1,0:T(8,128)S(1)}, f32[256,256]{1,0:T(8,128)S(1)}) custom-call(s32[8]{0:T(128)S(1)} %stack.32.flags, f32[256,256]{1,0:T(8,128)S(1)} %get-tuple-element.253.cur.prev, f32[256,256]{1,0:T(8,128)S(1)} %get-tuple-element.246.cur.prev, f32[256,256]{1,0:T(8,128)S(1)} %get-tuple-element.158.k0, ...), custom_call_target="tpu_custom_call" | custom-call | flops 1000 | bytes 5401000 | tf_op jit(solution)/shard_map/adjoint_inner/pallas_call | solution.py:467
  106.1 1.2 collective-permute-start.54
  107.3 1.6 %adjoint_inner.13 = (f32[256,256]{1,0:T(8,128)S(1)}, f32[256,256]{1,0:T(8,128)S(1)}) custom-call(s32[8]{0:T(128)S(1)} %stack.32.flags, f32[256,256]{1,0:T(8,128)S(1)} %get-tuple-element.260.cur.a, f32[256,256]{1,0:T(8,128)S(1)} %get-tuple-element.253.cur.prev, f32[256,256]{1,0:T(8,128)S(1)} %get-tuple-element.158.k0, f32[256,256]{1,0:T(8,128)S(1)} %get-tuple-element.159.ki, ...), custom_call_target="tpu_custom_call" | custom-call | flops 1000 | bytes 5401000 | tf_op jit(solution)/shard_map/adjoint_inner/pallas_call | solution.py:467
  111.7 1.5 %collective-permute-start.55 = (f32[2,256,256]{2,1,0:T(8,128)S(1)}, f32[2,256,256]{2,1,0:T(8,128)S(1)}, u32[]{:S(2)}, u32[]{:S(2)}) collective-permute-start(f32[2,256,256]{2,1,0:T(8,128)S(1)} %both.1.own), channel_id=1, source_target_pairs={{0,16},{1,2},{2,1},{3,19},{4,20},{5,6},{6,5},{7,23},{8,24},{9,10},... | collective-permute-start | bytes 1572872 | tf_op jit(solution)/shard_map/ppermute | solution.py:67
  113.2 1.3 %collective-permute-done.56.got = f32[4,64,128]{2,1,0:T(8,128)S(1)} collective-permute-done((f32[4,64,128]{2,1,0:T(8,128)S(1)}, f32[4,64,128]{2,1,0:T(8,128)S(1)}, u32[]{:S(2)}, u32[]{:S(2)}) %collective-permute-start.56) | collective-permute-done | bytes 131104 | tf_op jit(solution)/shard_map/ppermute | solution.py:67
  115.1 2.4 %collective-permute-start.57 = (f32[2,64,128]{2,1,0:T(8,128)S(1)}, f32[2,64,128]{2,1,0:T(8,128)S(1)}, u32[]{:S(2)}, u32[]{:S(2)}) collective-permute-start(f32[2,64,128]{2,1,0:T(8,128)S(1)} %get-tuple-element.274), channel_id=1, source_target_pairs={{0,0},{1,2},{2,1},{3,3},{4,4},{5,6},{6,5},{7,7},{8,8},{9,10},{10,9... | collective-permute-start | bytes 196616 | tf_op jit(solution)/shard_map/ppermute | solution.py:67
  117.5 1.8 %collective-permute-start.58 = (f32[2,64,128]{2,1,0:T(8,128)S(1)}, f32[2,64,128]{2,1,0:T(8,128)S(1)}, u32[]{:S(2)}, u32[]{:S(2)}) collective-permute-start(f32[2,64,128]{2,1,0:T(8,128)S(1)} %get-tuple-element.275), channel_id=1, source_target_pairs={{0,4},{1,6},{2,5},{3,7},{4,0},{5,2},{6,1},{7,3},{8,12},{9,14},{10,... | collective-permute-start | bytes 196616 | tf_op jit(solution)/shard_map/ppermute | solution.py:67
  120.2 3.1 %collective-permute-start.60 = (f32[2,64,128]{2,1,0:T(8,128)S(1)}, f32[2,64,128]{2,1,0:T(8,128)S(1)}, u32[]{:S(2)}, u32[]{:S(2)}) collective-permute-start(f32[2,64,128]{2,1,0:T(8,128)S(1)} %get-tuple-element.277), channel_id=1, source_target_pairs={{0,12},{1,14},{2,13},{3,15},{4,8},{5,10},{6,9},{7,11},{8,4},{9,6},... | collective-permute-start | bytes 196616 | tf_op jit(solution)/shard_map/ppermute | solution.py:67
  123.3 1.4 %select.7 = (f32[256,256]{1,0:T(8,128)}, f32[256,256]{1,0:T(8,128)}) custom-call(s32[8]{0:T(128)S(1)} %stack.32.flags, f32[2,256,256]{2,1,0:T(8,128)S(1)} %both.1.own, f32[2,256,256]{2,1,0:T(8,128)S(1)} %collective-permute-done.55.recv), custom_call_target="tpu_custom_call" | custom-call | flops 1000 | bytes 4321000 | tf_op jit(solution)/shard_map/select/pallas_call | solution.py:467
  125.5 1.2 collective-permute-done.60.refs_3_
  126.7 1.8 %filter.1 = f32[32,32,64]{2,1,0:T(8,128)} custom-call(s32[8]{0:T(128)S(1)} %stack.32.flags, f32[2,64,128]{2,1,0:T(8,128)S(1)} %collective-permute-done.57.refs_0_, f32[2,64,128]{2,1,0:T(8,128)S(1)} %collective-permute-done.58.refs_1_, f32[2,64,128]{2,1,0:T(8,128)S(1)} %collective-permute-done.59.refs_2_, f32[2,64,128]{2,1,0:T(8,128)S(1)} %collective-permute-done.60.refs_3_), custom_call_target="tpu_custom_call" | custom-call | flops 1000 | bytes 1000 | tf_op jit(solution)/shard_map/filter/pallas_call | solution.py:467
  (160 shorter events, 54.0 us)
Async XLA Ops:
  0.6 8.1 %collective-permute-start.1 = (f32[256,256]{1,0:T(8,128)}, f32[256,256]{1,0:T(8,128)S(1)}, u32[]{:S(2)}, u32[]{:S(2)}) collective-permute-start(f32[256,256]{1,0:T(8,128)} %bitcast.22), channel_id=1, source_target_pairs={{0,16},{1,2},{2,1},{3,19},{4,20},{5,6},{6,5},{7,23},{8,24},{9,10},... | collective-permute-start | bytes 786440 | tf_op jit(solution)/shard_map/ppermute | solution.py:67
  3.3 7.4 %collective-permute-start = (f32[256,256]{1,0:T(8,128)}, f32[256,256]{1,0:T(8,128)S(1)}, u32[]{:S(2)}, u32[]{:S(2)}) collective-permute-start(f32[256,256]{1,0:T(8,128)} %bitcast.20), channel_id=1, source_target_pairs={{0,16},{1,2},{2,1},{3,19},{4,20},{5,6},{6,5},{7,23},{8,24},{9,10},... | collective-permute-start | bytes 786440 | tf_op jit(solution)/shard_map/ppermute | solution.py:67
  4.5 13.2 %collective-permute-start.2 = (f32[2,256,256]{2,1,0:T(8,128)S(1)}, f32[2,256,256]{2,1,0:T(8,128)S(1)}, u32[]{:S(2)}, u32[]{:S(2)}) collective-permute-start(f32[2,256,256]{2,1,0:T(8,128)S(1)} %pad_maximum_fusion), channel_id=1, source_target_pairs={{0,16},{1,2},{2,1},{3,19},{4,20},{5,6},{6,5},{7,23},{8,24},{9,10},... | collective-permute-start | bytes 1572872 | tf_op jit(solution)/shard_map/ppermute | solution.py:67
  11.4 3.1 %collective-permute-start.3 = (f32[2,128,256]{2,1,0:T(8,128)S(1)}, f32[2,128,256]{2,1,0:T(8,128)S(1)}, u32[]{:S(2)}, u32[]{:S(2)}) collective-permute-start(f32[2,128,256]{2,1,0:T(8,128)S(1)} %get-tuple-element.146), channel_id=1, source_target_pairs={{0,1},{1,0},{2,3},{3,2},{4,5},{5,4},{6,7},{7,6},{8,9},{9,8},{10,11... | collective-permute-start | bytes 786440 | tf_op jit(solution)/shard_map/ppermute | solution.py:67
  11.8 6.6 %collective-permute-start.4 = (f32[2,128,256]{2,1,0:T(8,128)S(1)}, f32[2,128,256]{2,1,0:T(8,128)S(1)}, u32[]{:S(2)}, u32[]{:S(2)}) collective-permute-start(f32[2,128,256]{2,1,0:T(8,128)S(1)} %get-tuple-element.155), channel_id=1, source_target_pairs={{0,16},{1,4},{2,18},{3,6},{4,1},{5,8},{6,3},{7,10},{8,5},{9,12},{1... | collective-permute-start | bytes 786440 | tf_op jit(solution)/shard_map/ppermute | solution.py:67
  13.7 4.7 %collective-permute-start.5 = (f32[2,32,256]{2,1,0:T(8,128)S(1)}, f32[2,32,256]{2,1,0:T(8,128)S(1)}, u32[]{:S(2)}, u32[]{:S(2)}) collective-permute-start(f32[2,32,256]{2,1,0:T(8,128)S(1)} %get-tuple-element.156), channel_id=1, source_target_pairs={{0,2},{1,3},{2,0},{3,1},{4,6},{5,7},{6,4},{7,5},{8,10},{9,11},{10,... | collective-permute-start | bytes 196616 | tf_op jit(solution)/shard_map/ppermute | solution.py:67
  15.9 9.7 %collective-permute-start.9 = (f32[256,256]{1,0:T(8,128)S(1)}, f32[256,256]{1,0:T(8,128)S(1)}, u32[]{:S(2)}, u32[]{:S(2)}) collective-permute-start(f32[256,256]{1,0:T(8,128)S(1)} %bitcast.24), channel_id=1, source_target_pairs={{0,16},{1,2},{2,1},{3,19},{4,20},{5,6},{6,5},{7,23},{8,24},{9,10},... | collective-permute-start | bytes 786440 | tf_op jit(solution)/shard_map/ppermute | solution.py:67
  17.2 8.3 %collective-permute-start.10 = (f32[256,256]{1,0:T(8,128)S(1)}, f32[256,256]{1,0:T(8,128)S(1)}, u32[]{:S(2)}, u32[]{:S(2)}) collective-permute-start(f32[256,256]{1,0:T(8,128)S(1)} %bitcast.26), channel_id=1, source_target_pairs={{0,16},{1,2},{2,1},{3,19},{4,20},{5,6},{6,5},{7,23},{8,24},{9,10},... | collective-permute-start | bytes 786440 | tf_op jit(solution)/shard_map/ppermute | solution.py:67
  19.5 3.1 %collective-permute-start.6 = (f32[128,256]{1,0:T(8,128)S(1)}, f32[128,256]{1,0:T(8,128)S(1)}, u32[]{:S(2)}, u32[]{:S(2)}) collective-permute-start(f32[128,256]{1,0:T(8,128)S(1)} %get-tuple-element.162), channel_id=1, source_target_pairs={{0,1},{1,0},{2,3},{3,2},{4,5},{5,4},{6,7},{7,6},{8,9},{9,8},{10,11... | collective-permute-start | bytes 393224 | tf_op jit(solution)/shard_map/ppermute | solution.py:67
  20.6 5.7 %collective-permute-start.7 = (f32[128,256]{1,0:T(8,128)S(1)}, f32[128,256]{1,0:T(8,128)S(1)}, u32[]{:S(2)}, u32[]{:S(2)}) collective-permute-start(f32[128,256]{1,0:T(8,128)S(1)} %get-tuple-element.164), channel_id=1, source_target_pairs={{0,16},{1,4},{2,18},{3,6},{4,1},{5,8},{6,3},{7,10},{8,5},{9,12},{1... | collective-permute-start | bytes 393224 | tf_op jit(solution)/shard_map/ppermute | solution.py:67
  21.3 5.1 %collective-permute-start.8 = (f32[32,256]{1,0:T(8,128)S(1)}, f32[32,256]{1,0:T(8,128)S(1)}, u32[]{:S(2)}, u32[]{:S(2)}) collective-permute-start(f32[32,256]{1,0:T(8,128)S(1)} %get-tuple-element.165), channel_id=1, source_target_pairs={{0,2},{1,3},{2,0},{3,1},{4,6},{5,7},{6,4},{7,5},{8,10},{9,11},{10,... | collective-permute-start | bytes 98312 | tf_op jit(solution)/shard_map/ppermute | solution.py:67
  22.7 3.7 %collective-permute-start.11 = (f32[8,8,128]{2,1,0:T(8,128)S(1)}, f32[8,8,128]{2,1,0:T(8,128)S(1)}, u32[]{:S(2)}, u32[]{:S(2)}) collective-permute-start(f32[8,8,128]{2,1,0:T(8,128)S(1)} %get-tuple-element.171), channel_id=1, source_target_pairs={{0,1},{1,0},{2,3},{3,2},{4,5},{5,4},{6,7},{7,6},{8,9},{9,8},{10,11... | collective-permute-start | bytes 98312 | tf_op jit(solution)/shard_map/ppermute | solution.py:67
  28.0 6.1 %collective-permute-start.13 = (f32[2,128,256]{2,1,0:T(8,128)S(1)}, f32[2,128,256]{2,1,0:T(8,128)S(1)}, u32[]{:S(2)}, u32[]{:S(2)}) collective-permute-start(f32[2,128,256]{2,1,0:T(8,128)S(1)} %get-tuple-element.175), channel_id=1, source_target_pairs={{0,16},{1,4},{2,18},{3,6},{4,1},{5,8},{6,3},{7,10},{8,5},{9,12},{1... | collective-permute-start | bytes 786440 | tf_op jit(solution)/shard_map/ppermute | solution.py:67
  28.3 3.8 %collective-permute-start.14 = (f32[2,32,256]{2,1,0:T(8,128)S(1)}, f32[2,32,256]{2,1,0:T(8,128)S(1)}, u32[]{:S(2)}, u32[]{:S(2)}) collective-permute-start(f32[2,32,256]{2,1,0:T(8,128)S(1)} %get-tuple-element.176), channel_id=1, source_target_pairs={{0,2},{1,3},{2,0},{3,1},{4,6},{5,7},{6,4},{7,5},{8,10},{9,11},{10,... | collective-permute-start | bytes 196616 | tf_op jit(solution)/shard_map/ppermute | solution.py:67
  28.6 3.5 %collective-permute-start.15 = (f32[8,8,128]{2,1,0:T(8,128)S(1)}, f32[8,8,128]{2,1,0:T(8,128)S(1)}, u32[]{:S(2)}, u32[]{:S(2)}) collective-permute-start(f32[8,8,128]{2,1,0:T(8,128)S(1)} %get-tuple-element.178), channel_id=1, source_target_pairs={{0,2},{1,3},{2,0},{3,1},{4,6},{5,7},{6,4},{7,5},{8,10},{9,11},{10,... | collective-permute-start | bytes 98312 | tf_op jit(solution)/shard_map/ppermute | solution.py:67
  34.9 4.2 %collective-permute-start.16 = (f32[128,256]{1,0:T(8,128)S(1)}, f32[128,256]{1,0:T(8,128)S(1)}, u32[]{:S(2)}, u32[]{:S(2)}) collective-permute-start(f32[128,256]{1,0:T(8,128)S(1)} %get-tuple-element.180), channel_id=1, source_target_pairs={{0,1},{1,0},{2,3},{3,2},{4,5},{5,4},{6,7},{7,6},{8,9},{9,8},{10,11... | collective-permute-start | bytes 393224 | tf_op jit(solution)/shard_map/ppermute | solution.py:67
  35.4 6.3 %collective-permute-start.18 = (f32[128,256]{1,0:T(8,128)S(1)}, f32[128,256]{1,0:T(8,128)S(1)}, u32[]{:S(2)}, u32[]{:S(2)}) collective-permute-start(f32[128,256]{1,0:T(8,128)S(1)} %get-tuple-element.185), channel_id=1, source_target_pairs={{0,16},{1,4},{2,18},{3,6},{4,1},{5,8},{6,3},{7,10},{8,5},{9,12},{1... | collective-permute-start | bytes 393224 | tf_op jit(solution)/shard_map/ppermute | solution.py:67
  36.1 5.5 %collective-permute-start.19 = (f32[32,256]{1,0:T(8,128)S(1)}, f32[32,256]{1,0:T(8,128)S(1)}, u32[]{:S(2)}, u32[]{:S(2)}) collective-permute-start(f32[32,256]{1,0:T(8,128)S(1)} %get-tuple-element.186), channel_id=1, source_target_pairs={{0,2},{1,3},{2,0},{3,1},{4,6},{5,7},{6,4},{7,5},{8,10},{9,11},{10,... | collective-permute-start | bytes 98312 | tf_op jit(solution)/shard_map/ppermute | solution.py:67
  36.9 4.8 %collective-permute-start.20 = (f32[8,8,128]{2,1,0:T(8,128)S(1)}, f32[8,8,128]{2,1,0:T(8,128)S(1)}, u32[]{:S(2)}, u32[]{:S(2)}) collective-permute-start(f32[8,8,128]{2,1,0:T(8,128)S(1)} %get-tuple-element.188), channel_id=1, source_target_pairs={{0,4},{1,5},{2,6},{3,7},{4,0},{5,1},{6,2},{7,3},{8,12},{9,13},{10,... | collective-permute-start | bytes 98312 | tf_op jit(solution)/shard_map/ppermute | solution.py:67
  42.5 3.5 %collective-permute-start.21 = (f32[128,256]{1,0:T(8,128)S(1)}, f32[128,256]{1,0:T(8,128)S(1)}, u32[]{:S(2)}, u32[]{:S(2)}) collective-permute-start(f32[128,256]{1,0:T(8,128)S(1)} %get-tuple-element.190), channel_id=1, source_target_pairs={{0,1},{1,0},{2,3},{3,2},{4,5},{5,4},{6,7},{7,6},{8,9},{9,8},{10,11... | collective-permute-start | bytes 393224 | tf_op jit(solution)/shard_map/ppermute | solution.py:67
  43.0 4.9 %collective-permute-start.22 = (f32[128,256]{1,0:T(8,128)S(1)}, f32[128,256]{1,0:T(8,128)S(1)}, u32[]{:S(2)}, u32[]{:S(2)}) collective-permute-start(f32[128,256]{1,0:T(8,128)S(1)} %get-tuple-element.192), channel_id=1, source_target_pairs={{0,16},{1,4},{2,18},{3,6},{4,1},{5,8},{6,3},{7,10},{8,5},{9,12},{1... | collective-permute-start | bytes 393224 | tf_op jit(solution)/shard_map/ppermute | solution.py:67
  43.5 3.8 %collective-permute-start.23 = (f32[32,256]{1,0:T(8,128)S(1)}, f32[32,256]{1,0:T(8,128)S(1)}, u32[]{:S(2)}, u32[]{:S(2)}) collective-permute-start(f32[32,256]{1,0:T(8,128)S(1)} %get-tuple-element.193), channel_id=1, source_target_pairs={{0,2},{1,3},{2,0},{3,1},{4,6},{5,7},{6,4},{7,5},{8,10},{9,11},{10,... | collective-permute-start | bytes 98312 | tf_op jit(solution)/shard_map/ppermute | solution.py:67
  44.2 3.7 %collective-permute-start.24 = (f32[8,8,128]{2,1,0:T(8,128)S(1)}, f32[8,8,128]{2,1,0:T(8,128)S(1)}, u32[]{:S(2)}, u32[]{:S(2)}) collective-permute-start(f32[8,8,128]{2,1,0:T(8,128)S(1)} %get-tuple-element.195), channel_id=1, source_target_pairs={{0,8},{1,9},{2,10},{3,11},{4,12},{5,13},{6,14},{7,15},{8,0},{9,1},... | collective-permute-start | bytes 98312 | tf_op jit(solution)/shard_map/ppermute | solution.py:67
  48.8 4.7 %collective-permute-start.25 = (f32[128,256]{1,0:T(8,128)S(1)}, f32[128,256]{1,0:T(8,128)S(1)}, u32[]{:S(2)}, u32[]{:S(2)}) collective-permute-start(f32[128,256]{1,0:T(8,128)S(1)} %get-tuple-element.197), channel_id=1, source_target_pairs={{0,1},{1,0},{2,3},{3,2},{4,5},{5,4},{6,7},{7,6},{8,9},{9,8},{10,11... | collective-permute-start | bytes 393224 | tf_op jit(solution)/shard_map/ppermute | solution.py:67
  50.8 4.7 %collective-permute-start.26 = (f32[128,256]{1,0:T(8,128)S(1)}, f32[128,256]{1,0:T(8,128)S(1)}, u32[]{:S(2)}, u32[]{:S(2)}) collective-permute-start(f32[128,256]{1,0:T(8,128)S(1)} %get-tuple-element.201), channel_id=1, source_target_pairs={{0,16},{1,4},{2,18},{3,6},{4,1},{5,8},{6,3},{7,10},{8,5},{9,12},{1... | collective-permute-start | bytes 393224 | tf_op jit(solution)/shard_map/ppermute | solution.py:67
  51.6 3.3 %collective-permute-start.27 = (f32[32,256]{1,0:T(8,128)S(1)}, f32[32,256]{1,0:T(8,128)S(1)}, u32[]{:S(2)}, u32[]{:S(2)}) collective-permute-start(f32[32,256]{1,0:T(8,128)S(1)} %get-tuple-element.202), channel_id=1, source_target_pairs={{0,2},{1,3},{2,0},{3,1},{4,6},{5,7},{6,4},{7,5},{8,10},{9,11},{10,... | collective-permute-start | bytes 98312 | tf_op jit(solution)/shard_map/ppermute | solution.py:67
  56.3 3.4 %collective-permute-start.28 = (f32[128,256]{1,0:T(8,128)S(1)}, f32[128,256]{1,0:T(8,128)S(1)}, u32[]{:S(2)}, u32[]{:S(2)}) collective-permute-start(f32[128,256]{1,0:T(8,128)S(1)} %get-tuple-element.204), channel_id=1, source_target_pairs={{0,1},{1,0},{2,3},{3,2},{4,5},{5,4},{6,7},{7,6},{8,9},{9,8},{10,11... | collective-permute-start | bytes 393224 | tf_op jit(solution)/shard_map/ppermute | solution.py:67
  56.7 4.7 %collective-permute-start.29 = (f32[128,256]{1,0:T(8,128)S(1)}, f32[128,256]{1,0:T(8,128)S(1)}, u32[]{:S(2)}, u32[]{:S(2)}) collective-permute-start(f32[128,256]{1,0:T(8,128)S(1)} %get-tuple-element.209), channel_id=1, source_target_pairs={{0,16},{1,4},{2,18},{3,6},{4,1},{5,8},{6,3},{7,10},{8,5},{9,12},{1... | collective-permute-start | bytes 393224 | tf_op jit(solution)/shard_map/ppermute | solution.py:67
  57.8 3.3 %collective-permute-start.30 = (f32[32,256]{1,0:T(8,128)S(1)}, f32[32,256]{1,0:T(8,128)S(1)}, u32[]{:S(2)}, u32[]{:S(2)}) collective-permute-start(f32[32,256]{1,0:T(8,128)S(1)} %get-tuple-element.210), channel_id=1, source_target_pairs={{0,2},{1,3},{2,0},{3,1},{4,6},{5,7},{6,4},{7,5},{8,10},{9,11},{10,... | collective-permute-start | bytes 98312 | tf_op jit(solution)/shard_map/ppermute | solution.py:67
  62.9 4.7 %collective-permute-start.32 = (f32[128,256]{1,0:T(8,128)S(1)}, f32[128,256]{1,0:T(8,128)S(1)}, u32[]{:S(2)}, u32[]{:S(2)}) collective-permute-start(f32[128,256]{1,0:T(8,128)S(1)} %get-tuple-element.214), channel_id=1, source_target_pairs={{0,16},{1,4},{2,18},{3,6},{4,1},{5,8},{6,3},{7,10},{8,5},{9,12},{1... | collective-permute-start | bytes 393224 | tf_op jit(solution)/shard_map/ppermute | solution.py:67
  63.5 3.1 %collective-permute-start.33 = (f32[32,256]{1,0:T(8,128)S(1)}, f32[32,256]{1,0:T(8,128)S(1)}, u32[]{:S(2)}, u32[]{:S(2)}) collective-permute-start(f32[32,256]{1,0:T(8,128)S(1)} %get-tuple-element.215), channel_id=1, source_target_pairs={{0,2},{1,3},{2,0},{3,1},{4,6},{5,7},{6,4},{7,5},{8,10},{9,11},{10,... | collective-permute-start | bytes 98312 | tf_op jit(solution)/shard_map/ppermute | solution.py:67
  69.6 4.7 %collective-permute-start.35 = (f32[128,256]{1,0:T(8,128)S(1)}, f32[128,256]{1,0:T(8,128)S(1)}, u32[]{:S(2)}, u32[]{:S(2)}) collective-permute-start(f32[128,256]{1,0:T(8,128)S(1)} %get-tuple-element.223), channel_id=1, source_target_pairs={{0,16},{1,4},{2,18},{3,6},{4,1},{5,8},{6,3},{7,10},{8,5},{9,12},{1... | collective-permute-start | bytes 393224 | tf_op jit(solution)/shard_map/ppermute | solution.py:67
  70.3 3.1 %collective-permute-start.36 = (f32[32,256]{1,0:T(8,128)S(1)}, f32[32,256]{1,0:T(8,128)S(1)}, u32[]{:S(2)}, u32[]{:S(2)}) collective-permute-start(f32[32,256]{1,0:T(8,128)S(1)} %get-tuple-element.224), channel_id=1, source_target_pairs={{0,2},{1,3},{2,0},{3,1},{4,6},{5,7},{6,4},{7,5},{8,10},{9,11},{10,... | collective-permute-start | bytes 98312 | tf_op jit(solution)/shard_map/ppermute | solution.py:67
  75.6 4.7 %collective-permute-start.38 = (f32[128,256]{1,0:T(8,128)S(1)}, f32[128,256]{1,0:T(8,128)S(1)}, u32[]{:S(2)}, u32[]{:S(2)}) collective-permute-start(f32[128,256]{1,0:T(8,128)S(1)} %get-tuple-element.230), channel_id=1, source_target_pairs={{0,16},{1,4},{2,18},{3,6},{4,1},{5,8},{6,3},{7,10},{8,5},{9,12},{1... | collective-permute-start | bytes 393224 | tf_op jit(solution)/shard_map/ppermute | solution.py:67
  76.3 3.1 %collective-permute-start.39 = (f32[32,256]{1,0:T(8,128)S(1)}, f32[32,256]{1,0:T(8,128)S(1)}, u32[]{:S(2)}, u32[]{:S(2)}) collective-permute-start(f32[32,256]{1,0:T(8,128)S(1)} %get-tuple-element.231), channel_id=1, source_target_pairs={{0,2},{1,3},{2,0},{3,1},{4,6},{5,7},{6,4},{7,5},{8,10},{9,11},{10,... | collective-permute-start | bytes 98312 | tf_op jit(solution)/shard_map/ppermute | solution.py:67
  81.5 4.7 %collective-permute-start.41 = (f32[128,256]{1,0:T(8,128)S(1)}, f32[128,256]{1,0:T(8,128)S(1)}, u32[]{:S(2)}, u32[]{:S(2)}) collective-permute-start(f32[128,256]{1,0:T(8,128)S(1)} %get-tuple-element.237), channel_id=1, source_target_pairs={{0,16},{1,4},{2,18},{3,6},{4,1},{5,8},{6,3},{7,10},{8,5},{9,12},{1... | collective-permute-start | bytes 393224 | tf_op jit(solution)/shard_map/ppermute | solution.py:67
  82.2 3.1 %collective-permute-start.42 = (f32[32,256]{1,0:T(8,128)S(1)}, f32[32,256]{1,0:T(8,128)S(1)}, u32[]{:S(2)}, u32[]{:S(2)}) collective-permute-start(f32[32,256]{1,0:T(8,128)S(1)} %get-tuple-element.238), channel_id=1, source_target_pairs={{0,2},{1,3},{2,0},{3,1},{4,6},{5,7},{6,4},{7,5},{8,10},{9,11},{10,... | collective-permute-start | bytes 98312 | tf_op jit(solution)/shard_map/ppermute | solution.py:67
  87.5 4.7 %collective-permute-start.44 = (f32[128,256]{1,0:T(8,128)S(1)}, f32[128,256]{1,0:T(8,128)S(1)}, u32[]{:S(2)}, u32[]{:S(2)}) collective-permute-start(f32[128,256]{1,0:T(8,128)S(1)} %get-tuple-element.244), channel_id=1, source_target_pairs={{0,16},{1,4},{2,18},{3,6},{4,1},{5,8},{6,3},{7,10},{8,5},{9,12},{1... | collective-permute-start | bytes 393224 | tf_op jit(solution)/shard_map/ppermute | solution.py:67
  88.2 3.1 %collective-permute-start.45 = (f32[32,256]{1,0:T(8,128)S(1)}, f32[32,256]{1,0:T(8,128)S(1)}, u32[]{:S(2)}, u32[]{:S(2)}) collective-permute-start(f32[32,256]{1,0:T(8,128)S(1)} %get-tuple-element.245), channel_id=1, source_target_pairs={{0,2},{1,3},{2,0},{3,1},{4,6},{5,7},{6,4},{7,5},{8,10},{9,11},{10,... | collective-permute-start | bytes 98312 | tf_op jit(solution)/shard_map/ppermute | solution.py:67
  93.5 4.7 %collective-permute-start.47 = (f32[128,256]{1,0:T(8,128)S(1)}, f32[128,256]{1,0:T(8,128)S(1)}, u32[]{:S(2)}, u32[]{:S(2)}) collective-permute-start(f32[128,256]{1,0:T(8,128)S(1)} %get-tuple-element.251), channel_id=1, source_target_pairs={{0,16},{1,4},{2,18},{3,6},{4,1},{5,8},{6,3},{7,10},{8,5},{9,12},{1... | collective-permute-start | bytes 393224 | tf_op jit(solution)/shard_map/ppermute | solution.py:67
  94.2 3.1 %collective-permute-start.48 = (f32[32,256]{1,0:T(8,128)S(1)}, f32[32,256]{1,0:T(8,128)S(1)}, u32[]{:S(2)}, u32[]{:S(2)}) collective-permute-start(f32[32,256]{1,0:T(8,128)S(1)} %get-tuple-element.252), channel_id=1, source_target_pairs={{0,2},{1,3},{2,0},{3,1},{4,6},{5,7},{6,4},{7,5},{8,10},{9,11},{10,... | collective-permute-start | bytes 98312 | tf_op jit(solution)/shard_map/ppermute | solution.py:67
  99.4 4.7 %collective-permute-start.50 = (f32[128,256]{1,0:T(8,128)S(1)}, f32[128,256]{1,0:T(8,128)S(1)}, u32[]{:S(2)}, u32[]{:S(2)}) collective-permute-start(f32[128,256]{1,0:T(8,128)S(1)} %get-tuple-element.258), channel_id=1, source_target_pairs={{0,16},{1,4},{2,18},{3,6},{4,1},{5,8},{6,3},{7,10},{8,5},{9,12},{1... | collective-permute-start | bytes 393224 | tf_op jit(solution)/shard_map/ppermute | solution.py:67
  105.4 4.7 %collective-permute-start.53 = (f32[128,256]{1,0:T(8,128)S(1)}, f32[128,256]{1,0:T(8,128)S(1)}, u32[]{:S(2)}, u32[]{:S(2)}) collective-permute-start(f32[128,256]{1,0:T(8,128)S(1)} %get-tuple-element.265), channel_id=1, source_target_pairs={{0,16},{1,4},{2,18},{3,6},{4,1},{5,8},{6,3},{7,10},{8,5},{9,12},{1... | collective-permute-start | bytes 393224 | tf_op jit(solution)/shard_map/ppermute | solution.py:67
  111.7 11.6 %collective-permute-start.55 = (f32[2,256,256]{2,1,0:T(8,128)S(1)}, f32[2,256,256]{2,1,0:T(8,128)S(1)}, u32[]{:S(2)}, u32[]{:S(2)}) collective-permute-start(f32[2,256,256]{2,1,0:T(8,128)S(1)} %both.1.own), channel_id=1, source_target_pairs={{0,16},{1,2},{2,1},{3,19},{4,20},{5,6},{6,5},{7,23},{8,24},{9,10},... | collective-permute-start | bytes 1572872 | tf_op jit(solution)/shard_map/ppermute | solution.py:67
  115.1 9.6 %collective-permute-start.57 = (f32[2,64,128]{2,1,0:T(8,128)S(1)}, f32[2,64,128]{2,1,0:T(8,128)S(1)}, u32[]{:S(2)}, u32[]{:S(2)}) collective-permute-start(f32[2,64,128]{2,1,0:T(8,128)S(1)} %get-tuple-element.274), channel_id=1, source_target_pairs={{0,0},{1,2},{2,1},{3,3},{4,4},{5,6},{6,5},{7,7},{8,8},{9,10},{10,9... | collective-permute-start | bytes 196616 | tf_op jit(solution)/shard_map/ppermute | solution.py:67
  117.5 7.2 %collective-permute-start.58 = (f32[2,64,128]{2,1,0:T(8,128)S(1)}, f32[2,64,128]{2,1,0:T(8,128)S(1)}, u32[]{:S(2)}, u32[]{:S(2)}) collective-permute-start(f32[2,64,128]{2,1,0:T(8,128)S(1)} %get-tuple-element.275), channel_id=1, source_target_pairs={{0,4},{1,6},{2,5},{3,7},{4,0},{5,2},{6,1},{7,3},{8,12},{9,14},{10,... | collective-permute-start | bytes 196616 | tf_op jit(solution)/shard_map/ppermute | solution.py:67
  119.3 6.2 %collective-permute-start.59 = (f32[2,64,128]{2,1,0:T(8,128)S(1)}, f32[2,64,128]{2,1,0:T(8,128)S(1)}, u32[]{:S(2)}, u32[]{:S(2)}) collective-permute-start(f32[2,64,128]{2,1,0:T(8,128)S(1)} %get-tuple-element.276), channel_id=1, source_target_pairs={{0,8},{1,10},{2,9},{3,11},{4,12},{5,14},{6,13},{7,15},{8,0},{9,2},... | collective-permute-start | bytes 196616 | tf_op jit(solution)/shard_map/ppermute | solution.py:67
  120.2 6.5 %collective-permute-start.60 = (f32[2,64,128]{2,1,0:T(8,128)S(1)}, f32[2,64,128]{2,1,0:T(8,128)S(1)}, u32[]{:S(2)}, u32[]{:S(2)}) collective-permute-start(f32[2,64,128]{2,1,0:T(8,128)S(1)} %get-tuple-element.277), channel_id=1, source_target_pairs={{0,12},{1,14},{2,13},{3,15},{4,8},{5,10},{6,9},{7,11},{8,4},{9,6},... | collective-permute-start | bytes 196616 | tf_op jit(solution)/shard_map/ppermute | solution.py:67
  (32 other events, 84.8 us)

commit v12 on v11

--- a/solution.py
+++ b/solution.py
@@ -102,6 +102,46 @@
     return m.reshape(3 * rows * cols, own + rows * 8)
 
 
+def halved(rows, cols, c):
+    at = np.arange(rows)[:, None] * cols
+    z_side = (at + 4 * c + np.arange(4)).reshape(-1)
+    return np.concatenate([z_side, (at + 4 * (1 - c) + np.arange(4)).reshape(-1)])
+
+
+def near_matrix(rows, cols, c):
+    m = stencil_matrix(rows, cols)
+    own = (rows + 8) * cols
+    place = halved(rows, cols, c)
+    out = np.concatenate([place + k * rows * cols for k in range(3)])
+    side = own + (1 - c) * rows * 4 + np.arange(rows * 4)
+    return m[out][:, np.concatenate([halved(rows + 8, cols, c), side])]
+
+
+def side_matrix(rows, c):
+    m = np.zeros((2, rows, 4, rows, 4), np.float32)
+    for x in range(4):
+        for k in range(4):
+            d = x + 4 - k if c == 0 else k + 4 - x
+            if d <= 4:
+                for i in range(rows):
+                    m[0, i, x, i, k] = round(SECOND[d] * 5040)
+                    m[1, i, x, i, k] = round(FIRST[d - 1] * 840) * (-1 if c == 0 else 1)
+    return m.reshape(2 * rows * 4, rows * 4)
+
+
+def edge_matrix(y):
+    m = np.zeros((2, 2, 4, 4, 2, 4, 4), np.float32)
+    for i in range(4):
+        for k in range(4):
+            d = i + 4 - k if y == 1 else k + 4 - i
+            if d <= 4:
+                for part in range(2):
+                    for x in range(4):
+                        m[0, part, i, x, part, k, x] = round(SECOND[d] * 5040)
+                        m[1, part, i, x, part, k, x] = round(FIRST[d - 1] * 840) * (-1 if y == 1 else 1)
+    return m.reshape(64, 32)
+
+
 def split(value):
     high = value.astype(BF16)
     return high, (value - high.astype(F32)).astype(BF16)
@@ -112,58 +152,77 @@
 
 
 def inner_differences(cur, cm, near, deep):
-    depth = cur.shape[1]
-    size = GROUP * COLS
+    size, depth = cur.shape
+    half = size // 2
     cm = cm.at[0] if len(cm.shape) == 3 else cm
     own = split(cur[...])
     along = mm(jnp.concatenate(own, axis=1), deep[...])
-    blank = jnp.zeros((4 * COLS, depth), BF16)
-    ext = [jnp.concatenate([blank, part, blank], axis=0) for part in own]
+    blank = jnp.zeros((16, depth), BF16)
+    ext = [[jnp.concatenate([blank, part[h * half : h * half + half], blank], axis=0)
+            for h in range(2)] for part in own]
     from_c = split(cm[...])
-    for n in range(cur.shape[0] // size):
-        here = slice(n * size, n * size + size)
-        sides = slice(n * GROUP * 4, n * GROUP * 4 + GROUP * 4)
-        rhs = [part[n * size : n * size + size + 8 * COLS] for part in ext]
-        rhs += [part[sides] for part in from_c]
+    step = GROUP * 4
+    for n in range(half // step):
+        rhs = [part[h][n * step : n * step + step + 32] for part in ext for h in range(2)]
+        rhs += [part[n * step : n * step + step] for part in from_c]
         out = mm(near[...], jnp.concatenate(rhs, axis=0))
-        yield (here, out[0:size], along[here, 0:depth], out[size : 2 * size], out[2 * size :],
-               along[here, depth:])
-
-
-def side_differences(rows, zm, side):
-    size = GROUP * COLS
+        for h in range(2):
+            here = slice(h * half + n * step, h * half + n * step + step)
+            sums, di, dx = (out[(2 * k + h) * step : (2 * k + h + 1) * step] for k in range(3))
+            yield here, sums, along[here, 0:depth], di, dx, along[here, depth:]
+
+
+def side_differences(zm, side):
     zm = zm.at[0] if len(zm.shape) == 3 else zm
-    from_z = split(zm[...])
-    for n in range(rows // size):
-        sides = slice(n * GROUP * 4, n * GROUP * 4 + GROUP * 4)
-        out = mm(side[...], jnp.concatenate([part[sides] for part in from_z], axis=0))
-        yield slice(n * size, n * size + size), out[0:size], out[size:]
-
-
-def edge_differences(flags, rows, ym, edge):
-    size = GROUP * COLS
+    out = mm(side[...], jnp.concatenate(split(zm[...]), axis=0))
+    half = out.shape[0] // 2
+    return out[0:half], out[half:]
+
+
+def edge_differences(flags, size, ym, edge):
     ym = ym.at[0] if len(ym.shape) == 3 else ym
     out = mm(edge[...], jnp.concatenate(split(ym[...]), axis=0))
-    start = jnp.where(flags[1] == 1, 0, rows - size)
-    return pl.ds(pl.multiple_of(start, size), size), out[0:size], out[size:]
-
-
-def halves(value):
+    start = jnp.where(flags[1] == 1, 0, size // 2 - 16)
+    for h in range(2):
+        at = pl.ds(pl.multiple_of(start + h * (size // 2), 16), 16)
+        yield at, out[h * 16 : h * 16 + 16], out[32 + h * 16 : 48 + h * 16]
+
+
+def to_halves(flags, value):
     rows, depth = value.shape
     pairs = value.reshape(rows // (2 * COLS), 2, COLS, depth)
     a, b = pairs[:, 0], pairs[:, 1]
     low = lax.broadcasted_iota(jnp.int32, a.shape, 1) < 4
-    first = jnp.where(low, a, pltpu.roll(b, 4, axis=1))
-    last = jnp.where(low, pltpu.roll(a, 4, axis=1), b)
-    return first.reshape(rows // 2, depth), last.reshape(rows // 2, depth)
+    first = jnp.where(low, a, pltpu.roll(b, 4, axis=1)).reshape(rows // 2, depth)
+    last = jnp.where(low, pltpu.roll(a, 4, axis=1), b).reshape(rows // 2, depth)
+    return jnp.where(flags[0] == 0, first, last), jnp.where(flags[0] == 0, last, first)
+
+
+def from_halves(flags, value):
+    rows, depth = value.shape
+    z_side, c_side = value[0 : rows // 2], value[rows // 2 :]
+    shape = (rows // (2 * COLS), COLS, depth)
+    first = jnp.where(flags[0] == 0, z_side, c_side).reshape(shape)
+    last = jnp.where(flags[0] == 0, c_side, z_side).reshape(shape)
+    low = lax.broadcasted_iota(jnp.int32, shape, 1) < 4
+    a = jnp.where(low, first, pltpu.roll(last, 4, axis=1))
+    b = jnp.where(low, pltpu.roll(first, 4, axis=1), last)
+    return jnp.stack([a, b], axis=1).reshape(rows, depth)
+
+
+def place_of(flags, size, i, x):
+    near = x - 4 * flags[0]
+    return i * 4 + jnp.where((near >= 0) & (near < 4), near, size // 2 + x - 4 * (1 - flags[0]))
 
 
 def rims(flags, new, zo, co, yo):
-    first, last = halves(new[...])
-    zo[...] = jnp.where(flags[0] == 0, first, last)
-    co[...] = jnp.where(flags[0] == 0, last, first)
     size = new.shape[0]
-    yo[...] = jnp.where(flags[1] == 0, new[size - 4 * COLS :], new[0 : 4 * COLS])
+    half = size // 2
+    zo[...] = new[0:half]
+    co[...] = new[half:]
+    last = jnp.concatenate([new[half - 16 : half], new[size - 16 :]], axis=0)
+    first = jnp.concatenate([new[0:16], new[half : half + 16]], axis=0)
+    yo[...] = jnp.where(flags[1] == 0, last, first)
 
 
 def choose(flags, pairs, sems):
@@ -183,6 +242,12 @@
         for own, recv, out in pairs:
             out[...] = recv[...]
 
+    for own, recv, out in pairs:
+        half = out.shape[0] // 2
+        z_side, c_side = to_halves(flags, out[...])
+        out[0:half] = z_side
+        out[half:] = c_side
+
 
 def settle_kernel(flags, a, b, recv_a, recv_b, a_out, b_out, zo, co, yo, sems):
     choose(flags, [(a, recv_a, a_out), (b, recv_b, b_out)], sems)
@@ -213,24 +278,28 @@
 
 def first_outer_kernel(flags, cur, prev, vel, ri, rx, rz, sums, di, dx, dz, inj, zm, ym, side,
                        edge, new, zo, co, yo, k0, ki, kx, kz):
-    rows = cur.shape[0]
-    kz[...] = sums[...]
-    ki[...] = di[...]
-    here, more, more_i = edge_differences(flags, rows, ym.at[1], edge)
-    kz[here] += more
-    ki[here] += more_i
-    lr_here, spare, lr_more_i = edge_differences(flags, rows, ym.at[0], edge)
-    k0[...] = ri[...]
-    k0[lr_here] += lr_more_i
-    first = side_differences(rows, zm.at[0], side)
-    second = side_differences(rows, zm.at[1], side)
-    for (here, spare, more_r), (spare_here, more, more_x) in zip(first, second):
+    size = cur.shape[0]
+    half = size // 2
+    kz[...], ki[...], kx[...] = sums[...], di[...], dx[...]
+    k0[...], new[...] = ri[...], rx[...]
+    more, more_x = side_differences(zm.at[1], side)
+    kz[0:half] += more
+    kx[0:half] += more_x
+    spare, more_x = side_differences(zm.at[0], side)
+    new[0:half] += more_x
+    for here, more, more_i in edge_differences(flags, size, ym.at[1], edge):
+        kz[here] += more
+        ki[here] += more_i
+    for here, spare, more_i in edge_differences(flags, size, ym.at[0], edge):
+        k0[here] += more_i
+    for n in range(4):
+        here = slice(n * (size // 4), (n + 1) * (size // 4))
         square = vel[here] * vel[here]
         scaled = square * (1.0 / (840 * 840))
         factor = square * (1.0 / 5040)
-        along_i, along_x, along_z = scaled * k0[here], scaled * (rx[here] + more_r), scaled * rz[here]
-        change = factor * (kz[here] + more) - (
-            along_i * ki[here] + along_x * (dx[here] + more_x) + along_z * dz[here])
+        along_i, along_x, along_z = scaled * k0[here], scaled * new[here], scaled * rz[here]
+        change = factor * kz[here] - (
+            along_i * ki[here] + along_x * kx[here] + along_z * dz[here])
         k0[here], ki[here], kx[here], kz[here] = factor, along_i, along_x, along_z
         center = cur[here]
         new[here] = (center - prev[here]) + (center + (change + inj[here]))
@@ -248,11 +317,13 @@
 
 
 def outer(flags, part, k0, ki, kx, zm, ym, side, edge, new):
-    rows = part.shape[0]
-    for here, sums, dx in side_differences(rows, zm, side):
-        new[here] = part[here] + (k0[here] * sums - kx[here] * dx)
-    here, sums, di = edge_differences(flags, rows, ym, edge)
-    new[here] += k0[here] * sums - ki[here] * di
+    size = part.shape[0]
+    half = size // 2
+    sums, dx = side_differences(zm, side)
+    new[0:half] = part[0:half] + (k0[0:half] * sums - kx[0:half] * dx)
+    new[half:] = part[half:]
+    for here, sums, di in edge_differences(flags, size, ym, edge):
+        new[here] += k0[here] * sums - ki[here] * di
 
 
 def other_half(stage, flags, count):
@@ -292,7 +363,7 @@
         x = jnp.bitwise_and(jnp.right_shift(cell, shift), full - 1)
         x = x - (2 * flags[3] + flags[0]) * COLS
         ok = (i >= 0) & (i < rows) & (x >= 0) & (x < COLS)
-        row = jnp.where(lane == n, jnp.where(ok, i * COLS + x, -1), row)
+        row = jnp.where(lane == n, jnp.where(ok, place_of(flags, size, i, x), -1), row)
         deep = jnp.where(sub == n, jnp.bitwise_and(cell, depth - 1), deep)
         size_of = jnp.where(sub == n, wave[step, n], size_of)
     spot = lax.broadcasted_iota(jnp.int32, (size, count), 0) == row
@@ -355,14 +426,17 @@
     subs, steps = lists.shape[0], obs.shape[1]
     cell = jnp.where(flags[0] == flags[1], own[...], got[...])
     along = jnp.floor((cell + 0.5) * (1.0 / depth))
+    place = along.astype(jnp.int32)
+    place = jnp.where(place < 0, -1, place_of(
+        flags, size, jnp.right_shift(place, 3), jnp.bitwise_and(place, COLS - 1)))
     same = lax.broadcasted_iota(jnp.int32, (n, n), 0) == lax.broadcasted_iota(jnp.int32, (n, n), 1)
 
     def column(row):
         return jnp.sum(jnp.where(same, row, 0.0), axis=1, keepdims=True).astype(jnp.int32)
 
-    hot = lax.broadcasted_iota(jnp.int32, (size, n), 0) == along.astype(jnp.int32)
+    hot = lax.broadcasted_iota(jnp.int32, (size, n), 0) == place
     spot[...] = hot.astype(F32).astype(BF16)
-    hot = lax.broadcasted_iota(jnp.int32, (n, size), 1) == column(along)
+    hot = lax.broadcasted_iota(jnp.int32, (n, size), 1) == column(place.astype(F32))
     pick[...] = hot.astype(F32).astype(BF16)
     hot = lax.broadcasted_iota(jnp.int32, (n, depth), 1) == column(cell - along * depth)
     at[...] = hot.astype(F32)
@@ -405,7 +479,7 @@
 def last_kernel(scale, flags, part, k0, ki, kx, zm, ym, side, edge, image, change, vel,
                 new, mine, other):
     outer(flags, part, k0, ki, kx, zm, ym, side, edge, new)
-    raw = (image[...] + new[...] * change[...]) * scale / vel[...]
+    raw = from_halves(flags, (image[...] + new[...] * change[...]) * scale / vel[...])
     count, height, lanes = mine.shape
     chunk = raw.shape[1] // (2 * count)
     for n in range(count):
@@ -419,8 +493,8 @@
 
 
 def both_kernel(flags, a, b, out):
-    out[0] = a[...]
-    out[1] = b[...]
+    out[0] = from_halves(flags, a[...])
+    out[1] = from_halves(flags, b[...])
 
 
 def join_kernel(flags, mine, got, *outs):
@@ -493,25 +567,22 @@
     sub = (2 * q + c) * 2 + y
     flags = jnp.stack([c, y, sub, q] + [bit for pairs, bit in stages]).astype(jnp.int32)
     field = shaped(size, depth)
-    side, edge = (size // 2, depth), (4 * cols, depth)
-    rim = [shaped(*side), shaped(*side), shaped(*edge)]
+    rim = [shaped(size // 2, depth), shaped(size // 2, depth), shaped(4 * cols, depth)]
 
     deep = depth_matrix(depth)
     deep = jnp.asarray(np.concatenate([deep, deep]), BF16)
-    near = stencil_matrix(GROUP, cols)
-    group, own, half = GROUP * cols, near.shape[1] - GROUP * 8, GROUP * 4
-    both = [near[:, own : own + half], near[:, own + half :]]
-    from_z = [np.concatenate([part[:group], part[2 * group :]]) for part in both]
     inside = jnp.where(c == 0, q > 0, q < nq - 1)
-    side = jnp.where(c == 0, jnp.asarray(from_z[0], F32), jnp.asarray(from_z[1], F32))
-    side = jnp.where(inside, side, 0.0).astype(BF16)
+    near = [near_matrix(GROUP, cols, k) for k in range(2)]
+    wide = (GROUP + 8) * cols
+    near = [np.concatenate([m[:, :wide], m[:, :wide], m[:, wide:], m[:, wide:]], axis=1) for m in near]
+    near = jnp.where(c == 0, jnp.asarray(near[0], F32), jnp.asarray(near[1], F32)).astype(BF16)
+    side = [side_matrix(rows, k) for k in range(2)]
+    side = jnp.where(c == 0, jnp.asarray(side[0], BF16), jnp.asarray(side[1], BF16))
+    side = jnp.where(inside, side, jnp.zeros_like(side))
     side = jnp.concatenate([side, side], axis=1)
-    core = jnp.where(c == 0, jnp.asarray(both[1], F32), jnp.asarray(both[0], F32)).astype(BF16)
-    edge = jnp.where(y == 1, jnp.asarray(near[: 2 * group, : 4 * cols], F32),
-                     jnp.asarray(near[: 2 * group, own - 4 * cols : own], F32)).astype(BF16)
+    edge = [edge_matrix(k) for k in range(2)]
+    edge = jnp.where(y == 0, jnp.asarray(edge[0], F32), jnp.asarray(edge[1], F32)).astype(BF16)
     edge = jnp.concatenate([edge, edge], axis=1)
-    near = jnp.asarray(np.concatenate([near[:, :own], near[:, :own]], axis=1), BF16)
-    near = jnp.concatenate([near, core, core], axis=1)
 
     def halo(zo, co, yo):
         return send(zo, z_perm), send(co, c_perm), send(yo, y_perm)

time: 129 us -> 128 us (level)
  transfers between devices with their start and end apart: 61 -> 61, of which waited for: 26 -> 25; matrix products, arithmetic and copies ran while one was open for 1% -> 1% of each run, Pallas kernels for 24% -> 24%
where the time goes in v12:
time: 128 us
  starting transfers between devices  58.5 us (46%)
  Pallas kernels  45.2 us (35%)
  waiting for transfers between devices  20.5 us (16%)
  local copies, waits for them, and re-layouts  1.54 us (1%)
  between operations  1.3 us (1%)
    ppermute x61, starting transfers between devices, send(): return lax.ppermute(value, ALL, pairs)  58.5 us
    pallas_call x41, Pallas kernels, call(): pl.pallas_call(kernel, name=name, out_shape=outs, in_specs=specs, out_spe...  45.2 us
    ppermute x61, waiting for transfers between devices, send(): return lax.ppermute(value, ALL, pairs)  20.5 us
  transfers between devices with their start and end apart: 61, of which 25 were waited for; matrix products, arithmetic and copies ran while one was open for 1% of the time, Pallas kernels for 24%

profile of v12, /device:TPU:1, one launch (start us, length us, event | category | flops | bytes accessed | tf_op | source)
XLA Modules:
  0.0 128.2 jit_solution(16538792405548654689)
XLA Ops:
  0.6 2.7 %collective-permute-start.1 = (f32[256,256]{1,0:T(8,128)}, f32[256,256]{1,0:T(8,128)S(1)}, u32[]{:S(2)}, u32[]{:S(2)}) collective-permute-start(f32[256,256]{1,0:T(8,128)} %bitcast.22), channel_id=1, source_target_pairs={{0,16},{1,2},{2,1},{3,19},{4,20},{5,6},{6,5},{7,23},{8,24},{9,10},... | collective-permute-start | bytes 786440 | tf_op jit(solution)/shard_map/ppermute | solution.py:67
  3.4 1.1 pad_maximum_fusion
  4.5 1.7 %collective-permute-start.2 = (f32[2,256,256]{2,1,0:T(8,128)S(1)}, f32[2,256,256]{2,1,0:T(8,128)S(1)}, u32[]{:S(2)}, u32[]{:S(2)}) collective-permute-start(f32[2,256,256]{2,1,0:T(8,128)S(1)} %pad_maximum_fusion), channel_id=1, source_target_pairs={{0,16},{1,2},{2,1},{3,19},{4,20},{5,6},{6,5},{7,23},{8,24},{9,10},... | collective-permute-start | bytes 1572872 | tf_op jit(solution)/shard_map/ppermute | solution.py:67
  8.9 1.8 %collective-permute-done.recv_a = f32[256,256]{1,0:T(8,128)S(1)} collective-permute-done((f32[256,256]{1,0:T(8,128)}, f32[256,256]{1,0:T(8,128)S(1)}, u32[]{:S(2)}, u32[]{:S(2)}) %collective-permute-start) | collective-permute-done | bytes 262176 | tf_op jit(solution)/shard_map/ppermute | solution.py:67
  11.9 1.8 %collective-permute-start.4 = (f32[2,128,256]{2,1,0:T(8,128)S(1)}, f32[2,128,256]{2,1,0:T(8,128)S(1)}, u32[]{:S(2)}, u32[]{:S(2)}) collective-permute-start(f32[2,128,256]{2,1,0:T(8,128)S(1)} %get-tuple-element.155), channel_id=1, source_target_pairs={{0,16},{1,4},{2,18},{3,6},{4,1},{5,8},{6,3},{7,10},{8,5},{9,12},{1... | collective-permute-start | bytes 786440 | tf_op jit(solution)/shard_map/ppermute | solution.py:67
  14.5 1.3 %first_inner.1 = (f32[256,256]{1,0:T(8,128)S(1)}, f32[256,256]{1,0:T(8,128)S(1)}, f32[256,256]{1,0:T(8,128)S(1)}, f32[256,256]{1,0:T(8,128)S(1)}, f32[256,256]{1...) custom-call(s32[8]{0:T(128)S(1)} %stack.32.flags, f32[256,256]{1,0:T(8,128)S(1)} %get-tuple-element.145.lr, ...), custom_call_target="tpu_custom_call" | custom-call | flops 1000 | bytes 4681000 | tf_op jit(solution)/shard_map/first_inner/pallas_call | solution.py:541
  15.8 1.3 %collective-permute-start.9 = (f32[256,256]{1,0:T(8,128)S(1)}, f32[256,256]{1,0:T(8,128)S(1)}, u32[]{:S(2)}, u32[]{:S(2)}) collective-permute-start(f32[256,256]{1,0:T(8,128)S(1)} %bitcast.24), channel_id=1, source_target_pairs={{0,16},{1,2},{2,1},{3,19},{4,20},{5,6},{6,5},{7,23},{8,24},{9,10},... | collective-permute-start | bytes 786440 | tf_op jit(solution)/shard_map/ppermute | solution.py:67
  19.5 1.1 collective-permute-start.6
  22.7 1.5 %collective-permute-start.11 = (f32[8,8,128]{2,1,0:T(8,128)S(1)}, f32[8,8,128]{2,1,0:T(8,128)S(1)}, u32[]{:S(2)}, u32[]{:S(2)}) collective-permute-start(f32[8,8,128]{2,1,0:T(8,128)S(1)} %get-tuple-element.171), channel_id=1, source_target_pairs={{0,1},{1,0},{2,3},{3,2},{4,5},{5,4},{6,7},{7,6},{8,9},{9,8},{10,11... | collective-permute-start | bytes 98312 | tf_op jit(solution)/shard_map/ppermute | solution.py:67
  24.2 1.4 %forward_inner.7 = (f32[256,256]{1,0:T(8,128)S(1)}, f32[256,256]{1,0:T(8,128)S(1)}) custom-call(s32[8]{0:T(128)S(1)} %stack.32.flags, s32[16]{0:T(128)S(1)} %copy-done.8, f32[8,16]{1,0:T(8,128)S(1)} %copy-done.3, f32[256,256]{1,0:T(8,128)S(1)} %get-tuple-element.157.cur.prev.before.state, f32[256,256]{1,0:T(8,128)S(1)} %get-tuple-element.142.cur.prev.before, ...), custom_call_target="tpu_custom_call" | custom-call | flops 1000 | bytes 4321000 | tf_op jit(solution)/shard_map/forward_inner/pallas_call | solution.py:541
  28.6 1.1 collective-permute-start.15
  29.7 1.4 %forward_inner.8 = (f32[256,256]{1,0:T(8,128)S(1)}, f32[256,256]{1,0:T(8,128)S(1)}) custom-call(s32[8]{0:T(128)S(1)} %stack.32.flags, s32[16]{0:T(128)S(1)} %copy-done.8, f32[8,16]{1,0:T(8,128)S(1)} %copy-done.3, f32[256,256]{1,0:T(8,128)S(1)} %get-tuple-element.172.cur.prev.before.state, f32[256,256]{1,0:T(8,128)S(1)} %get-tuple-element.157.cur.prev.before.state, ...), custom_call_target="tpu_custom_call" | custom-call | flops 1000 | bytes 4321000 | tf_op jit(solution)/shard_map/forward_inner/pallas_call | solution.py:541
  32.0 1.9 %collective-permute-done.13.zm.u_zm = f32[2,128,256]{2,1,0:T(8,128)S(1)} collective-permute-done((f32[2,128,256]{2,1,0:T(8,128)S(1)}, f32[2,128,256]{2,1,0:T(8,128)S(1)}, u32[]{:S(2)}, u32[]{:S(2)}) %collective-permute-start.13) | collective-permute-done | bytes 262176 | tf_op jit(solution)/shard_map/ppermute | solution.py:67
  35.2 1.2 collective-permute-start.18
  37.1 1.8 %collective-permute-start.20 = (f32[8,8,128]{2,1,0:T(8,128)S(1)}, f32[8,8,128]{2,1,0:T(8,128)S(1)}, u32[]{:S(2)}, u32[]{:S(2)}) collective-permute-start(f32[8,8,128]{2,1,0:T(8,128)S(1)} %get-tuple-element.188), channel_id=1, source_target_pairs={{0,4},{1,5},{2,6},{3,7},{4,0},{5,1},{6,2},{7,3},{8,12},{9,13},{10,... | collective-permute-start | bytes 98312 | tf_op jit(solution)/shard_map/ppermute | solution.py:67
  39.0 1.4 %forward_inner.9 = (f32[256,256]{1,0:T(8,128)S(1)}, f32[256,256]{1,0:T(8,128)S(1)}) custom-call(s32[8]{0:T(128)S(1)} %stack.32.flags, s32[16]{0:T(128)S(1)} %copy-done.8, f32[8,16]{1,0:T(8,128)S(1)} %copy-done.3, f32[256,256]{1,0:T(8,128)S(1)} %get-tuple-element.179.cur.prev.before.state, f32[256,256]{1,0:T(8,128)S(1)} %get-tuple-element.172.cur.prev.before.state, ...), custom_call_target="tpu_custom_call" | custom-call | flops 1000 | bytes 4321000 | tf_op jit(solution)/shard_map/forward_inner/pallas_call | solution.py:541
  40.3 1.5 %collective-permute-done.17.got = f32[1,128]{1,0:T(1,128)S(1)} collective-permute-done((f32[1,128]{1,0:T(1,128)S(1)}, f32[1,128]{1,0:T(1,128)S(1)}, u32[]{:S(2)}, u32[]{:S(2)}) %collective-permute-start.17) | collective-permute-done | bytes 544 | tf_op jit(solution)/shard_map/ppermute | solution.py:67
  44.1 1.8 %collective-permute-start.24 = (f32[8,8,128]{2,1,0:T(8,128)S(1)}, f32[8,8,128]{2,1,0:T(8,128)S(1)}, u32[]{:S(2)}, u32[]{:S(2)}) collective-permute-start(f32[8,8,128]{2,1,0:T(8,128)S(1)} %get-tuple-element.195), channel_id=1, source_target_pairs={{0,8},{1,9},{2,10},{3,11},{4,12},{5,13},{6,14},{7,15},{8,0},{9,1},... | collective-permute-start | bytes 98312 | tf_op jit(solution)/shard_map/ppermute | solution.py:67
  45.9 1.4 %forward_inner.10 = (f32[256,256]{1,0:T(8,128)S(1)}, f32[256,256]{1,0:T(8,128)S(1)}) custom-call(s32[8]{0:T(128)S(1)} %stack.32.flags, s32[16]{0:T(128)S(1)} %copy-done.8, f32[8,16]{1,0:T(8,128)S(1)} %copy-done.3, f32[256,256]{1,0:T(8,128)S(1)} %get-tuple-element.189.cur.prev.before.state, f32[256,256]{1,0:T(8,128)S(1)} %get-tuple-element.179.cur.prev.before.state, ...), custom_call_target="tpu_custom_call" | custom-call | flops 1000 | bytes 4321000 | tf_op jit(solution)/shard_map/forward_inner/pallas_call | solution.py:541
  48.8 2.1 %collective-permute-start.25 = (f32[128,256]{1,0:T(8,128)S(1)}, f32[128,256]{1,0:T(8,128)S(1)}, u32[]{:S(2)}, u32[]{:S(2)}) collective-permute-start(f32[128,256]{1,0:T(8,128)S(1)} %get-tuple-element.197), channel_id=1, source_target_pairs={{0,1},{1,0},{2,3},{3,2},{4,5},{5,4},{6,7},{7,6},{8,9},{9,8},{10,11... | collective-permute-start | bytes 393224 | tf_op jit(solution)/shard_map/ppermute | solution.py:67
  53.6 1.4 %forward_inner.11 = (f32[256,256]{1,0:T(8,128)S(1)}, f32[256,256]{1,0:T(8,128)S(1)}) custom-call(s32[8]{0:T(128)S(1)} %stack.32.flags, s32[16]{0:T(128)S(1)} %copy-done.8, f32[8,16]{1,0:T(8,128)S(1)} %copy-done.3, f32[256,256]{1,0:T(8,128)S(1)} %get-tuple-element.196.cur.prev.before.state, f32[256,256]{1,0:T(8,128)S(1)} %get-tuple-element.189.cur.prev.before.state, ...), custom_call_target="tpu_custom_call" | custom-call | flops 1000 | bytes 4321000 | tf_op jit(solution)/shard_map/forward_inner/pallas_call | solution.py:541
  56.8 1.2 collective-permute-start.29
  59.8 1.4 %forward_inner.12 = (f32[256,256]{1,0:T(8,128)S(1)}, f32[256,256]{1,0:T(8,128)S(1)}) custom-call(s32[8]{0:T(128)S(1)} %stack.32.flags, s32[16]{0:T(128)S(1)} %copy-done.8, f32[8,16]{1,0:T(8,128)S(1)} %copy-done.3, f32[256,256]{1,0:T(8,128)S(1)} %get-tuple-element.203.cur.prev.rest_2_.state, f32[256,256]{1,0:T(8,128)S(1)} %get-tuple-element.196.cur.prev.before.state, ...), custom_call_target="tpu_custom_call" | custom-call | flops 1000 | bytes 4321000 | tf_op jit(solution)/shard_map/forward_inner/pallas_call | solution.py:541
  63.6 1.4 %collective-permute-start.33 = (f32[32,256]{1,0:T(8,128)S(1)}, f32[32,256]{1,0:T(8,128)S(1)}, u32[]{:S(2)}, u32[]{:S(2)}) collective-permute-start(f32[32,256]{1,0:T(8,128)S(1)} %get-tuple-element.215), channel_id=1, source_target_pairs={{0,2},{1,3},{2,0},{3,1},{4,6},{5,7},{6,4},{7,5},{8,10},{9,11},{10,... | collective-permute-start | bytes 98312 | tf_op jit(solution)/shard_map/ppermute | solution.py:67
  65.0 1.4 %forward_inner.13 = (f32[256,256]{1,0:T(8,128)S(1)}, f32[256,256]{1,0:T(8,128)S(1)}) custom-call(s32[8]{0:T(128)S(1)} %stack.32.flags, s32[16]{0:T(128)S(1)} %copy-done.8, f32[8,16]{1,0:T(8,128)S(1)} %copy-done.3, f32[256,256]{1,0:T(8,128)S(1)} %get-tuple-element.211.cur.state.rest_1_, f32[256,256]{1,0:T(8,128)S(1)} %get-tuple-element.203.cur.prev.rest_2_.state, ...), custom_call_target="tpu_custom_call" | custom-call | flops 1000 | bytes 4321000 | tf_op jit(solution)/shard_map/forward_inner/pallas_call | solution.py:541
  67.7 1.4 %turn.1 = (f32[256,256]{1,0:T(8,128)S(1)}, f32[256,256]{1,0:T(8,128)S(1)}, f32[128,256]{1,0:T(8,128)S(1)}, f32[128,256]{1,0:T(8,128)S(1)}, f32[32,256]{1,0:T(8,128)S(1)}) custom-call(s32[8]{0:T(128)S(1)} %stack.32.flags, f32[256,256]{1,0:T(8,128)S(1)} %get-tuple-element.213.part, f32[256,256]{1,0:T(8,128)S(1)} %get-tuple-element.158.k0, ...), custom_call_target="tpu_custom_call" | custom-call | flops 1000 | bytes 1000 | tf_op jit(solution)/shard_map/turn/pallas_call | solution.py:541
  70.3 1.2 collective-permute-start.36
  71.5 1.7 %adjoint_inner.7 = (f32[256,256]{1,0:T(8,128)S(1)}, f32[256,256]{1,0:T(8,128)S(1)}) custom-call(s32[8]{0:T(128)S(1)} %stack.32.flags, f32[256,256]{1,0:T(8,128)S(1)} %get-tuple-element.219.cur.prev, f32[256,256]{1,0:T(8,128)S(1)} %get-tuple-element.168.rest_0_.cur.prev, f32[256,256]{1,0:T(8,128)S(1)} %get-tuple-element.158.k0, ...), custom_call_target="tpu_custom_call" | custom-call | flops 1000 | bytes 5401000 | tf_op jit(solution)/shard_map/adjoint_inner/pallas_call | solution.py:541
  76.2 1.2 collective-permute-start.39
  77.4 1.6 %adjoint_inner.8 = (f32[256,256]{1,0:T(8,128)S(1)}, f32[256,256]{1,0:T(8,128)S(1)}) custom-call(s32[8]{0:T(128)S(1)} %stack.32.flags, f32[256,256]{1,0:T(8,128)S(1)} %get-tuple-element.225.cur.prev, f32[256,256]{1,0:T(8,128)S(1)} %get-tuple-element.219.cur.prev, f32[256,256]{1,0:T(8,128)S(1)} %get-tuple-element.158.k0, ...), custom_call_target="tpu_custom_call" | custom-call | flops 1000 | bytes 5401000 | tf_op jit(solution)/shard_map/adjoint_inner/pallas_call | solution.py:541
  82.1 1.2 collective-permute-start.42
  83.3 1.6 %adjoint_inner.9 = (f32[256,256]{1,0:T(8,128)S(1)}, f32[256,256]{1,0:T(8,128)S(1)}) custom-call(s32[8]{0:T(128)S(1)} %stack.32.flags, f32[256,256]{1,0:T(8,128)S(1)} %get-tuple-element.232.cur.prev, f32[256,256]{1,0:T(8,128)S(1)} %get-tuple-element.225.cur.prev, f32[256,256]{1,0:T(8,128)S(1)} %get-tuple-element.158.k0, ...), custom_call_target="tpu_custom_call" | custom-call | flops 1000 | bytes 5401000 | tf_op jit(solution)/shard_map/adjoint_inner/pallas_call | solution.py:541
  88.0 1.2 collective-permute-start.45
  89.3 1.8 %adjoint_inner.10 = (f32[256,256]{1,0:T(8,128)S(1)}, f32[256,256]{1,0:T(8,128)S(1)}) custom-call(s32[8]{0:T(128)S(1)} %stack.32.flags, f32[256,256]{1,0:T(8,128)S(1)} %get-tuple-element.239.cur.prev, f32[256,256]{1,0:T(8,128)S(1)} %get-tuple-element.232.cur.prev, f32[256,256]{1,0:T(8,128)S(1)} %get-tuple-element.158.k0, ...), custom_call_target="tpu_custom_call" | custom-call | flops 1000 | bytes 5401000 | tf_op jit(solution)/shard_map/adjoint_inner/pallas_call | solution.py:541
  94.0 1.2 collective-permute-start.48
  95.2 1.6 %adjoint_inner.11 = (f32[256,256]{1,0:T(8,128)S(1)}, f32[256,256]{1,0:T(8,128)S(1)}) custom-call(s32[8]{0:T(128)S(1)} %stack.32.flags, f32[256,256]{1,0:T(8,128)S(1)} %get-tuple-element.246.cur.prev, f32[256,256]{1,0:T(8,128)S(1)} %get-tuple-element.239.cur.prev, f32[256,256]{1,0:T(8,128)S(1)} %get-tuple-element.158.k0, ...), custom_call_target="tpu_custom_call" | custom-call | flops 1000 | bytes 5401000 | tf_op jit(solution)/shard_map/adjoint_inner/pallas_call | solution.py:541
  99.9 1.2 collective-permute-start.51
  101.1 1.6 %adjoint_inner.12 = (f32[256,256]{1,0:T(8,128)S(1)}, f32[256,256]{1,0:T(8,128)S(1)}) custom-call(s32[8]{0:T(128)S(1)} %stack.32.flags, f32[256,256]{1,0:T(8,128)S(1)} %get-tuple-element.253.cur.prev, f32[256,256]{1,0:T(8,128)S(1)} %get-tuple-element.246.cur.prev, f32[256,256]{1,0:T(8,128)S(1)} %get-tuple-element.158.k0, ...), custom_call_target="tpu_custom_call" | custom-call | flops 1000 | bytes 5401000 | tf_op jit(solution)/shard_map/adjoint_inner/pallas_call | solution.py:541
  105.8 1.2 collective-permute-start.54
  107.0 1.6 %adjoint_inner.13 = (f32[256,256]{1,0:T(8,128)S(1)}, f32[256,256]{1,0:T(8,128)S(1)}) custom-call(s32[8]{0:T(128)S(1)} %stack.32.flags, f32[256,256]{1,0:T(8,128)S(1)} %get-tuple-element.260.cur.a, f32[256,256]{1,0:T(8,128)S(1)} %get-tuple-element.253.cur.prev, f32[256,256]{1,0:T(8,128)S(1)} %get-tuple-element.158.k0, f32[256,256]{1,0:T(8,128)S(1)} %get-tuple-element.159.ki, ...), custom_call_target="tpu_custom_call" | custom-call | flops 1000 | bytes 5401000 | tf_op jit(solution)/shard_map/adjoint_inner/pallas_call | solution.py:541
  111.4 1.6 %collective-permute-start.55 = (f32[2,256,256]{2,1,0:T(8,128)S(1)}, f32[2,256,256]{2,1,0:T(8,128)S(1)}, u32[]{:S(2)}, u32[]{:S(2)}) collective-permute-start(f32[2,256,256]{2,1,0:T(8,128)S(1)} %both.1.own), channel_id=1, source_target_pairs={{0,16},{1,2},{2,1},{3,19},{4,20},{5,6},{6,5},{7,23},{8,24},{9,10},... | collective-permute-start | bytes 1572872 | tf_op jit(solution)/shard_map/ppermute | solution.py:67
  113.0 1.3 %collective-permute-done.56.got = f32[4,64,128]{2,1,0:T(8,128)S(1)} collective-permute-done((f32[4,64,128]{2,1,0:T(8,128)S(1)}, f32[4,64,128]{2,1,0:T(8,128)S(1)}, u32[]{:S(2)}, u32[]{:S(2)}) %collective-permute-start.56) | collective-permute-done | bytes 131104 | tf_op jit(solution)/shard_map/ppermute | solution.py:67
  114.9 2.4 %collective-permute-start.57 = (f32[2,64,128]{2,1,0:T(8,128)S(1)}, f32[2,64,128]{2,1,0:T(8,128)S(1)}, u32[]{:S(2)}, u32[]{:S(2)}) collective-permute-start(f32[2,64,128]{2,1,0:T(8,128)S(1)} %get-tuple-element.274), channel_id=1, source_target_pairs={{0,0},{1,2},{2,1},{3,3},{4,4},{5,6},{6,5},{7,7},{8,8},{9,10},{10,9... | collective-permute-start | bytes 196616 | tf_op jit(solution)/shard_map/ppermute | solution.py:67
  117.2 1.8 %collective-permute-start.58 = (f32[2,64,128]{2,1,0:T(8,128)S(1)}, f32[2,64,128]{2,1,0:T(8,128)S(1)}, u32[]{:S(2)}, u32[]{:S(2)}) collective-permute-start(f32[2,64,128]{2,1,0:T(8,128)S(1)} %get-tuple-element.275), channel_id=1, source_target_pairs={{0,4},{1,6},{2,5},{3,7},{4,0},{5,2},{6,1},{7,3},{8,12},{9,14},{10,... | collective-permute-start | bytes 196616 | tf_op jit(solution)/shard_map/ppermute | solution.py:67
  119.9 3.1 %collective-permute-start.60 = (f32[2,64,128]{2,1,0:T(8,128)S(1)}, f32[2,64,128]{2,1,0:T(8,128)S(1)}, u32[]{:S(2)}, u32[]{:S(2)}) collective-permute-start(f32[2,64,128]{2,1,0:T(8,128)S(1)} %get-tuple-element.277), channel_id=1, source_target_pairs={{0,12},{1,14},{2,13},{3,15},{4,8},{5,10},{6,9},{7,11},{8,4},{9,6},... | collective-permute-start | bytes 196616 | tf_op jit(solution)/shard_map/ppermute | solution.py:67
  123.0 1.4 %select.7 = (f32[256,256]{1,0:T(8,128)}, f32[256,256]{1,0:T(8,128)}) custom-call(s32[8]{0:T(128)S(1)} %stack.32.flags, f32[2,256,256]{2,1,0:T(8,128)S(1)} %both.1.own, f32[2,256,256]{2,1,0:T(8,128)S(1)} %collective-permute-done.55.recv), custom_call_target="tpu_custom_call" | custom-call | flops 1000 | bytes 4321000 | tf_op jit(solution)/shard_map/select/pallas_call | solution.py:541
  125.2 1.2 collective-permute-done.60.refs_3_
  126.4 1.8 %filter.1 = f32[32,32,64]{2,1,0:T(8,128)} custom-call(s32[8]{0:T(128)S(1)} %stack.32.flags, f32[2,64,128]{2,1,0:T(8,128)S(1)} %collective-permute-done.57.refs_0_, f32[2,64,128]{2,1,0:T(8,128)S(1)} %collective-permute-done.58.refs_1_, f32[2,64,128]{2,1,0:T(8,128)S(1)} %collective-permute-done.59.refs_2_, f32[2,64,128]{2,1,0:T(8,128)S(1)} %collective-permute-done.60.refs_3_), custom_call_target="tpu_custom_call" | custom-call | flops 1000 | bytes 1000 | tf_op jit(solution)/shard_map/filter/pallas_call | solution.py:541
  (158 shorter events, 53.0 us)
Async XLA Ops:
  0.6 8.2 %collective-permute-start.1 = (f32[256,256]{1,0:T(8,128)}, f32[256,256]{1,0:T(8,128)S(1)}, u32[]{:S(2)}, u32[]{:S(2)}) collective-permute-start(f32[256,256]{1,0:T(8,128)} %bitcast.22), channel_id=1, source_target_pairs={{0,16},{1,2},{2,1},{3,19},{4,20},{5,6},{6,5},{7,23},{8,24},{9,10},... | collective-permute-start | bytes 786440 | tf_op jit(solution)/shard_map/ppermute | solution.py:67
  3.3 7.4 %collective-permute-start = (f32[256,256]{1,0:T(8,128)}, f32[256,256]{1,0:T(8,128)S(1)}, u32[]{:S(2)}, u32[]{:S(2)}) collective-permute-start(f32[256,256]{1,0:T(8,128)} %bitcast.20), channel_id=1, source_target_pairs={{0,16},{1,2},{2,1},{3,19},{4,20},{5,6},{6,5},{7,23},{8,24},{9,10},... | collective-permute-start | bytes 786440 | tf_op jit(solution)/shard_map/ppermute | solution.py:67
  4.5 13.2 %collective-permute-start.2 = (f32[2,256,256]{2,1,0:T(8,128)S(1)}, f32[2,256,256]{2,1,0:T(8,128)S(1)}, u32[]{:S(2)}, u32[]{:S(2)}) collective-permute-start(f32[2,256,256]{2,1,0:T(8,128)S(1)} %pad_maximum_fusion), channel_id=1, source_target_pairs={{0,16},{1,2},{2,1},{3,19},{4,20},{5,6},{6,5},{7,23},{8,24},{9,10},... | collective-permute-start | bytes 1572872 | tf_op jit(solution)/shard_map/ppermute | solution.py:67
  11.9 6.5 %collective-permute-start.4 = (f32[2,128,256]{2,1,0:T(8,128)S(1)}, f32[2,128,256]{2,1,0:T(8,128)S(1)}, u32[]{:S(2)}, u32[]{:S(2)}) collective-permute-start(f32[2,128,256]{2,1,0:T(8,128)S(1)} %get-tuple-element.155), channel_id=1, source_target_pairs={{0,16},{1,4},{2,18},{3,6},{4,1},{5,8},{6,3},{7,10},{8,5},{9,12},{1... | collective-permute-start | bytes 786440 | tf_op jit(solution)/shard_map/ppermute | solution.py:67
  13.7 4.7 %collective-permute-start.5 = (f32[2,32,256]{2,1,0:T(8,128)S(1)}, f32[2,32,256]{2,1,0:T(8,128)S(1)}, u32[]{:S(2)}, u32[]{:S(2)}) collective-permute-start(f32[2,32,256]{2,1,0:T(8,128)S(1)} %get-tuple-element.156), channel_id=1, source_target_pairs={{0,2},{1,3},{2,0},{3,1},{4,6},{5,7},{6,4},{7,5},{8,10},{9,11},{10,... | collective-permute-start | bytes 196616 | tf_op jit(solution)/shard_map/ppermute | solution.py:67
  15.8 9.8 %collective-permute-start.9 = (f32[256,256]{1,0:T(8,128)S(1)}, f32[256,256]{1,0:T(8,128)S(1)}, u32[]{:S(2)}, u32[]{:S(2)}) collective-permute-start(f32[256,256]{1,0:T(8,128)S(1)} %bitcast.24), channel_id=1, source_target_pairs={{0,16},{1,2},{2,1},{3,19},{4,20},{5,6},{6,5},{7,23},{8,24},{9,10},... | collective-permute-start | bytes 786440 | tf_op jit(solution)/shard_map/ppermute | solution.py:67
  17.2 8.4 %collective-permute-start.10 = (f32[256,256]{1,0:T(8,128)S(1)}, f32[256,256]{1,0:T(8,128)S(1)}, u32[]{:S(2)}, u32[]{:S(2)}) collective-permute-start(f32[256,256]{1,0:T(8,128)S(1)} %bitcast.26), channel_id=1, source_target_pairs={{0,16},{1,2},{2,1},{3,19},{4,20},{5,6},{6,5},{7,23},{8,24},{9,10},... | collective-permute-start | bytes 786440 | tf_op jit(solution)/shard_map/ppermute | solution.py:67
  19.5 3.2 %collective-permute-start.6 = (f32[128,256]{1,0:T(8,128)S(1)}, f32[128,256]{1,0:T(8,128)S(1)}, u32[]{:S(2)}, u32[]{:S(2)}) collective-permute-start(f32[128,256]{1,0:T(8,128)S(1)} %get-tuple-element.162), channel_id=1, source_target_pairs={{0,1},{1,0},{2,3},{3,2},{4,5},{5,4},{6,7},{7,6},{8,9},{9,8},{10,11... | collective-permute-start | bytes 393224 | tf_op jit(solution)/shard_map/ppermute | solution.py:67
  20.6 5.8 %collective-permute-start.7 = (f32[128,256]{1,0:T(8,128)S(1)}, f32[128,256]{1,0:T(8,128)S(1)}, u32[]{:S(2)}, u32[]{:S(2)}) collective-permute-start(f32[128,256]{1,0:T(8,128)S(1)} %get-tuple-element.164), channel_id=1, source_target_pairs={{0,16},{1,4},{2,18},{3,6},{4,1},{5,8},{6,3},{7,10},{8,5},{9,12},{1... | collective-permute-start | bytes 393224 | tf_op jit(solution)/shard_map/ppermute | solution.py:67
  21.3 5.2 %collective-permute-start.8 = (f32[32,256]{1,0:T(8,128)S(1)}, f32[32,256]{1,0:T(8,128)S(1)}, u32[]{:S(2)}, u32[]{:S(2)}) collective-permute-start(f32[32,256]{1,0:T(8,128)S(1)} %get-tuple-element.165), channel_id=1, source_target_pairs={{0,2},{1,3},{2,0},{3,1},{4,6},{5,7},{6,4},{7,5},{8,10},{9,11},{10,... | collective-permute-start | bytes 98312 | tf_op jit(solution)/shard_map/ppermute | solution.py:67
  22.7 3.7 %collective-permute-start.11 = (f32[8,8,128]{2,1,0:T(8,128)S(1)}, f32[8,8,128]{2,1,0:T(8,128)S(1)}, u32[]{:S(2)}, u32[]{:S(2)}) collective-permute-start(f32[8,8,128]{2,1,0:T(8,128)S(1)} %get-tuple-element.171), channel_id=1, source_target_pairs={{0,1},{1,0},{2,3},{3,2},{4,5},{5,4},{6,7},{7,6},{8,9},{9,8},{10,11... | collective-permute-start | bytes 98312 | tf_op jit(solution)/shard_map/ppermute | solution.py:67
  27.9 6.1 %collective-permute-start.13 = (f32[2,128,256]{2,1,0:T(8,128)S(1)}, f32[2,128,256]{2,1,0:T(8,128)S(1)}, u32[]{:S(2)}, u32[]{:S(2)}) collective-permute-start(f32[2,128,256]{2,1,0:T(8,128)S(1)} %get-tuple-element.175), channel_id=1, source_target_pairs={{0,16},{1,4},{2,18},{3,6},{4,1},{5,8},{6,3},{7,10},{8,5},{9,12},{1... | collective-permute-start | bytes 786440 | tf_op jit(solution)/shard_map/ppermute | solution.py:67
  28.3 3.8 %collective-permute-start.14 = (f32[2,32,256]{2,1,0:T(8,128)S(1)}, f32[2,32,256]{2,1,0:T(8,128)S(1)}, u32[]{:S(2)}, u32[]{:S(2)}) collective-permute-start(f32[2,32,256]{2,1,0:T(8,128)S(1)} %get-tuple-element.176), channel_id=1, source_target_pairs={{0,2},{1,3},{2,0},{3,1},{4,6},{5,7},{6,4},{7,5},{8,10},{9,11},{10,... | collective-permute-start | bytes 196616 | tf_op jit(solution)/shard_map/ppermute | solution.py:67
  28.6 3.4 %collective-permute-start.15 = (f32[8,8,128]{2,1,0:T(8,128)S(1)}, f32[8,8,128]{2,1,0:T(8,128)S(1)}, u32[]{:S(2)}, u32[]{:S(2)}) collective-permute-start(f32[8,8,128]{2,1,0:T(8,128)S(1)} %get-tuple-element.178), channel_id=1, source_target_pairs={{0,2},{1,3},{2,0},{3,1},{4,6},{5,7},{6,4},{7,5},{8,10},{9,11},{10,... | collective-permute-start | bytes 98312 | tf_op jit(solution)/shard_map/ppermute | solution.py:67
  34.7 4.2 %collective-permute-start.16 = (f32[128,256]{1,0:T(8,128)S(1)}, f32[128,256]{1,0:T(8,128)S(1)}, u32[]{:S(2)}, u32[]{:S(2)}) collective-permute-start(f32[128,256]{1,0:T(8,128)S(1)} %get-tuple-element.180), channel_id=1, source_target_pairs={{0,1},{1,0},{2,3},{3,2},{4,5},{5,4},{6,7},{7,6},{8,9},{9,8},{10,11... | collective-permute-start | bytes 393224 | tf_op jit(solution)/shard_map/ppermute | solution.py:67
  35.2 6.7 %collective-permute-start.18 = (f32[128,256]{1,0:T(8,128)S(1)}, f32[128,256]{1,0:T(8,128)S(1)}, u32[]{:S(2)}, u32[]{:S(2)}) collective-permute-start(f32[128,256]{1,0:T(8,128)S(1)} %get-tuple-element.185), channel_id=1, source_target_pairs={{0,16},{1,4},{2,18},{3,6},{4,1},{5,8},{6,3},{7,10},{8,5},{9,12},{1... | collective-permute-start | bytes 393224 | tf_op jit(solution)/shard_map/ppermute | solution.py:67
  36.3 5.6 %collective-permute-start.19 = (f32[32,256]{1,0:T(8,128)S(1)}, f32[32,256]{1,0:T(8,128)S(1)}, u32[]{:S(2)}, u32[]{:S(2)}) collective-permute-start(f32[32,256]{1,0:T(8,128)S(1)} %get-tuple-element.186), channel_id=1, source_target_pairs={{0,2},{1,3},{2,0},{3,1},{4,6},{5,7},{6,4},{7,5},{8,10},{9,11},{10,... | collective-permute-start | bytes 98312 | tf_op jit(solution)/shard_map/ppermute | solution.py:67
  37.1 4.7 %collective-permute-start.20 = (f32[8,8,128]{2,1,0:T(8,128)S(1)}, f32[8,8,128]{2,1,0:T(8,128)S(1)}, u32[]{:S(2)}, u32[]{:S(2)}) collective-permute-start(f32[8,8,128]{2,1,0:T(8,128)S(1)} %get-tuple-element.188), channel_id=1, source_target_pairs={{0,4},{1,5},{2,6},{3,7},{4,0},{5,1},{6,2},{7,3},{8,12},{9,13},{10,... | collective-permute-start | bytes 98312 | tf_op jit(solution)/shard_map/ppermute | solution.py:67
  42.7 3.2 %collective-permute-start.21 = (f32[128,256]{1,0:T(8,128)S(1)}, f32[128,256]{1,0:T(8,128)S(1)}, u32[]{:S(2)}, u32[]{:S(2)}) collective-permute-start(f32[128,256]{1,0:T(8,128)S(1)} %get-tuple-element.190), channel_id=1, source_target_pairs={{0,1},{1,0},{2,3},{3,2},{4,5},{5,4},{6,7},{7,6},{8,9},{9,8},{10,11... | collective-permute-start | bytes 393224 | tf_op jit(solution)/shard_map/ppermute | solution.py:67
  43.0 5.1 %collective-permute-start.22 = (f32[128,256]{1,0:T(8,128)S(1)}, f32[128,256]{1,0:T(8,128)S(1)}, u32[]{:S(2)}, u32[]{:S(2)}) collective-permute-start(f32[128,256]{1,0:T(8,128)S(1)} %get-tuple-element.192), channel_id=1, source_target_pairs={{0,16},{1,4},{2,18},{3,6},{4,1},{5,8},{6,3},{7,10},{8,5},{9,12},{1... | collective-permute-start | bytes 393224 | tf_op jit(solution)/shard_map/ppermute | solution.py:67
  43.3 3.9 %collective-permute-start.23 = (f32[32,256]{1,0:T(8,128)S(1)}, f32[32,256]{1,0:T(8,128)S(1)}, u32[]{:S(2)}, u32[]{:S(2)}) collective-permute-start(f32[32,256]{1,0:T(8,128)S(1)} %get-tuple-element.193), channel_id=1, source_target_pairs={{0,2},{1,3},{2,0},{3,1},{4,6},{5,7},{6,4},{7,5},{8,10},{9,11},{10,... | collective-permute-start | bytes 98312 | tf_op jit(solution)/shard_map/ppermute | solution.py:67
  44.1 4.0 %collective-permute-start.24 = (f32[8,8,128]{2,1,0:T(8,128)S(1)}, f32[8,8,128]{2,1,0:T(8,128)S(1)}, u32[]{:S(2)}, u32[]{:S(2)}) collective-permute-start(f32[8,8,128]{2,1,0:T(8,128)S(1)} %get-tuple-element.195), channel_id=1, source_target_pairs={{0,8},{1,9},{2,10},{3,11},{4,12},{5,13},{6,14},{7,15},{8,0},{9,1},... | collective-permute-start | bytes 98312 | tf_op jit(solution)/shard_map/ppermute | solution.py:67
  48.8 4.7 %collective-permute-start.25 = (f32[128,256]{1,0:T(8,128)S(1)}, f32[128,256]{1,0:T(8,128)S(1)}, u32[]{:S(2)}, u32[]{:S(2)}) collective-permute-start(f32[128,256]{1,0:T(8,128)S(1)} %get-tuple-element.197), channel_id=1, source_target_pairs={{0,1},{1,0},{2,3},{3,2},{4,5},{5,4},{6,7},{7,6},{8,9},{9,8},{10,11... | collective-permute-start | bytes 393224 | tf_op jit(solution)/shard_map/ppermute | solution.py:67
  50.9 4.7 %collective-permute-start.26 = (f32[128,256]{1,0:T(8,128)S(1)}, f32[128,256]{1,0:T(8,128)S(1)}, u32[]{:S(2)}, u32[]{:S(2)}) collective-permute-start(f32[128,256]{1,0:T(8,128)S(1)} %get-tuple-element.201), channel_id=1, source_target_pairs={{0,16},{1,4},{2,18},{3,6},{4,1},{5,8},{6,3},{7,10},{8,5},{9,12},{1... | collective-permute-start | bytes 393224 | tf_op jit(solution)/shard_map/ppermute | solution.py:67
  51.7 3.3 %collective-permute-start.27 = (f32[32,256]{1,0:T(8,128)S(1)}, f32[32,256]{1,0:T(8,128)S(1)}, u32[]{:S(2)}, u32[]{:S(2)}) collective-permute-start(f32[32,256]{1,0:T(8,128)S(1)} %get-tuple-element.202), channel_id=1, source_target_pairs={{0,2},{1,3},{2,0},{3,1},{4,6},{5,7},{6,4},{7,5},{8,10},{9,11},{10,... | collective-permute-start | bytes 98312 | tf_op jit(solution)/shard_map/ppermute | solution.py:67
  56.3 3.5 %collective-permute-start.28 = (f32[128,256]{1,0:T(8,128)S(1)}, f32[128,256]{1,0:T(8,128)S(1)}, u32[]{:S(2)}, u32[]{:S(2)}) collective-permute-start(f32[128,256]{1,0:T(8,128)S(1)} %get-tuple-element.204), channel_id=1, source_target_pairs={{0,1},{1,0},{2,3},{3,2},{4,5},{5,4},{6,7},{7,6},{8,9},{9,8},{10,11... | collective-permute-start | bytes 393224 | tf_op jit(solution)/shard_map/ppermute | solution.py:67
  56.8 4.7 %collective-permute-start.29 = (f32[128,256]{1,0:T(8,128)S(1)}, f32[128,256]{1,0:T(8,128)S(1)}, u32[]{:S(2)}, u32[]{:S(2)}) collective-permute-start(f32[128,256]{1,0:T(8,128)S(1)} %get-tuple-element.209), channel_id=1, source_target_pairs={{0,16},{1,4},{2,18},{3,6},{4,1},{5,8},{6,3},{7,10},{8,5},{9,12},{1... | collective-permute-start | bytes 393224 | tf_op jit(solution)/shard_map/ppermute | solution.py:67
  57.9 3.3 %collective-permute-start.30 = (f32[32,256]{1,0:T(8,128)S(1)}, f32[32,256]{1,0:T(8,128)S(1)}, u32[]{:S(2)}, u32[]{:S(2)}) collective-permute-start(f32[32,256]{1,0:T(8,128)S(1)} %get-tuple-element.210), channel_id=1, source_target_pairs={{0,2},{1,3},{2,0},{3,1},{4,6},{5,7},{6,4},{7,5},{8,10},{9,11},{10,... | collective-permute-start | bytes 98312 | tf_op jit(solution)/shard_map/ppermute | solution.py:67
  63.1 4.7 %collective-permute-start.32 = (f32[128,256]{1,0:T(8,128)S(1)}, f32[128,256]{1,0:T(8,128)S(1)}, u32[]{:S(2)}, u32[]{:S(2)}) collective-permute-start(f32[128,256]{1,0:T(8,128)S(1)} %get-tuple-element.214), channel_id=1, source_target_pairs={{0,16},{1,4},{2,18},{3,6},{4,1},{5,8},{6,3},{7,10},{8,5},{9,12},{1... | collective-permute-start | bytes 393224 | tf_op jit(solution)/shard_map/ppermute | solution.py:67
  63.6 3.1 %collective-permute-start.33 = (f32[32,256]{1,0:T(8,128)S(1)}, f32[32,256]{1,0:T(8,128)S(1)}, u32[]{:S(2)}, u32[]{:S(2)}) collective-permute-start(f32[32,256]{1,0:T(8,128)S(1)} %get-tuple-element.215), channel_id=1, source_target_pairs={{0,2},{1,3},{2,0},{3,1},{4,6},{5,7},{6,4},{7,5},{8,10},{9,11},{10,... | collective-permute-start | bytes 98312 | tf_op jit(solution)/shard_map/ppermute | solution.py:67
  69.6 4.7 %collective-permute-start.35 = (f32[128,256]{1,0:T(8,128)S(1)}, f32[128,256]{1,0:T(8,128)S(1)}, u32[]{:S(2)}, u32[]{:S(2)}) collective-permute-start(f32[128,256]{1,0:T(8,128)S(1)} %get-tuple-element.223), channel_id=1, source_target_pairs={{0,16},{1,4},{2,18},{3,6},{4,1},{5,8},{6,3},{7,10},{8,5},{9,12},{1... | collective-permute-start | bytes 393224 | tf_op jit(solution)/shard_map/ppermute | solution.py:67
  70.3 3.1 %collective-permute-start.36 = (f32[32,256]{1,0:T(8,128)S(1)}, f32[32,256]{1,0:T(8,128)S(1)}, u32[]{:S(2)}, u32[]{:S(2)}) collective-permute-start(f32[32,256]{1,0:T(8,128)S(1)} %get-tuple-element.224), channel_id=1, source_target_pairs={{0,2},{1,3},{2,0},{3,1},{4,6},{5,7},{6,4},{7,5},{8,10},{9,11},{10,... | collective-permute-start | bytes 98312 | tf_op jit(solution)/shard_map/ppermute | solution.py:67
  75.5 4.7 %collective-permute-start.38 = (f32[128,256]{1,0:T(8,128)S(1)}, f32[128,256]{1,0:T(8,128)S(1)}, u32[]{:S(2)}, u32[]{:S(2)}) collective-permute-start(f32[128,256]{1,0:T(8,128)S(1)} %get-tuple-element.230), channel_id=1, source_target_pairs={{0,16},{1,4},{2,18},{3,6},{4,1},{5,8},{6,3},{7,10},{8,5},{9,12},{1... | collective-permute-start | bytes 393224 | tf_op jit(solution)/shard_map/ppermute | solution.py:67
  76.2 3.1 %collective-permute-start.39 = (f32[32,256]{1,0:T(8,128)S(1)}, f32[32,256]{1,0:T(8,128)S(1)}, u32[]{:S(2)}, u32[]{:S(2)}) collective-permute-start(f32[32,256]{1,0:T(8,128)S(1)} %get-tuple-element.231), channel_id=1, source_target_pairs={{0,2},{1,3},{2,0},{3,1},{4,6},{5,7},{6,4},{7,5},{8,10},{9,11},{10,... | collective-permute-start | bytes 98312 | tf_op jit(solution)/shard_map/ppermute | solution.py:67
  81.4 4.7 %collective-permute-start.41 = (f32[128,256]{1,0:T(8,128)S(1)}, f32[128,256]{1,0:T(8,128)S(1)}, u32[]{:S(2)}, u32[]{:S(2)}) collective-permute-start(f32[128,256]{1,0:T(8,128)S(1)} %get-tuple-element.237), channel_id=1, source_target_pairs={{0,16},{1,4},{2,18},{3,6},{4,1},{5,8},{6,3},{7,10},{8,5},{9,12},{1... | collective-permute-start | bytes 393224 | tf_op jit(solution)/shard_map/ppermute | solution.py:67
  82.1 3.1 %collective-permute-start.42 = (f32[32,256]{1,0:T(8,128)S(1)}, f32[32,256]{1,0:T(8,128)S(1)}, u32[]{:S(2)}, u32[]{:S(2)}) collective-permute-start(f32[32,256]{1,0:T(8,128)S(1)} %get-tuple-element.238), channel_id=1, source_target_pairs={{0,2},{1,3},{2,0},{3,1},{4,6},{5,7},{6,4},{7,5},{8,10},{9,11},{10,... | collective-permute-start | bytes 98312 | tf_op jit(solution)/shard_map/ppermute | solution.py:67
  87.3 4.7 %collective-permute-start.44 = (f32[128,256]{1,0:T(8,128)S(1)}, f32[128,256]{1,0:T(8,128)S(1)}, u32[]{:S(2)}, u32[]{:S(2)}) collective-permute-start(f32[128,256]{1,0:T(8,128)S(1)} %get-tuple-element.244), channel_id=1, source_target_pairs={{0,16},{1,4},{2,18},{3,6},{4,1},{5,8},{6,3},{7,10},{8,5},{9,12},{1... | collective-permute-start | bytes 393224 | tf_op jit(solution)/shard_map/ppermute | solution.py:67
  88.0 3.1 %collective-permute-start.45 = (f32[32,256]{1,0:T(8,128)S(1)}, f32[32,256]{1,0:T(8,128)S(1)}, u32[]{:S(2)}, u32[]{:S(2)}) collective-permute-start(f32[32,256]{1,0:T(8,128)S(1)} %get-tuple-element.245), channel_id=1, source_target_pairs={{0,2},{1,3},{2,0},{3,1},{4,6},{5,7},{6,4},{7,5},{8,10},{9,11},{10,... | collective-permute-start | bytes 98312 | tf_op jit(solution)/shard_map/ppermute | solution.py:67
  93.3 4.7 %collective-permute-start.47 = (f32[128,256]{1,0:T(8,128)S(1)}, f32[128,256]{1,0:T(8,128)S(1)}, u32[]{:S(2)}, u32[]{:S(2)}) collective-permute-start(f32[128,256]{1,0:T(8,128)S(1)} %get-tuple-element.251), channel_id=1, source_target_pairs={{0,16},{1,4},{2,18},{3,6},{4,1},{5,8},{6,3},{7,10},{8,5},{9,12},{1... | collective-permute-start | bytes 393224 | tf_op jit(solution)/shard_map/ppermute | solution.py:67
  94.0 3.1 %collective-permute-start.48 = (f32[32,256]{1,0:T(8,128)S(1)}, f32[32,256]{1,0:T(8,128)S(1)}, u32[]{:S(2)}, u32[]{:S(2)}) collective-permute-start(f32[32,256]{1,0:T(8,128)S(1)} %get-tuple-element.252), channel_id=1, source_target_pairs={{0,2},{1,3},{2,0},{3,1},{4,6},{5,7},{6,4},{7,5},{8,10},{9,11},{10,... | collective-permute-start | bytes 98312 | tf_op jit(solution)/shard_map/ppermute | solution.py:67
  99.2 4.7 %collective-permute-start.50 = (f32[128,256]{1,0:T(8,128)S(1)}, f32[128,256]{1,0:T(8,128)S(1)}, u32[]{:S(2)}, u32[]{:S(2)}) collective-permute-start(f32[128,256]{1,0:T(8,128)S(1)} %get-tuple-element.258), channel_id=1, source_target_pairs={{0,16},{1,4},{2,18},{3,6},{4,1},{5,8},{6,3},{7,10},{8,5},{9,12},{1... | collective-permute-start | bytes 393224 | tf_op jit(solution)/shard_map/ppermute | solution.py:67
  99.9 3.1 %collective-permute-start.51 = (f32[32,256]{1,0:T(8,128)S(1)}, f32[32,256]{1,0:T(8,128)S(1)}, u32[]{:S(2)}, u32[]{:S(2)}) collective-permute-start(f32[32,256]{1,0:T(8,128)S(1)} %get-tuple-element.259), channel_id=1, source_target_pairs={{0,2},{1,3},{2,0},{3,1},{4,6},{5,7},{6,4},{7,5},{8,10},{9,11},{10,... | collective-permute-start | bytes 98312 | tf_op jit(solution)/shard_map/ppermute | solution.py:67
  105.1 4.7 %collective-permute-start.53 = (f32[128,256]{1,0:T(8,128)S(1)}, f32[128,256]{1,0:T(8,128)S(1)}, u32[]{:S(2)}, u32[]{:S(2)}) collective-permute-start(f32[128,256]{1,0:T(8,128)S(1)} %get-tuple-element.265), channel_id=1, source_target_pairs={{0,16},{1,4},{2,18},{3,6},{4,1},{5,8},{6,3},{7,10},{8,5},{9,12},{1... | collective-permute-start | bytes 393224 | tf_op jit(solution)/shard_map/ppermute | solution.py:67
  111.4 11.7 %collective-permute-start.55 = (f32[2,256,256]{2,1,0:T(8,128)S(1)}, f32[2,256,256]{2,1,0:T(8,128)S(1)}, u32[]{:S(2)}, u32[]{:S(2)}) collective-permute-start(f32[2,256,256]{2,1,0:T(8,128)S(1)} %both.1.own), channel_id=1, source_target_pairs={{0,16},{1,2},{2,1},{3,19},{4,20},{5,6},{6,5},{7,23},{8,24},{9,10},... | collective-permute-start | bytes 1572872 | tf_op jit(solution)/shard_map/ppermute | solution.py:67
  114.9 9.6 %collective-permute-start.57 = (f32[2,64,128]{2,1,0:T(8,128)S(1)}, f32[2,64,128]{2,1,0:T(8,128)S(1)}, u32[]{:S(2)}, u32[]{:S(2)}) collective-permute-start(f32[2,64,128]{2,1,0:T(8,128)S(1)} %get-tuple-element.274), channel_id=1, source_target_pairs={{0,0},{1,2},{2,1},{3,3},{4,4},{5,6},{6,5},{7,7},{8,8},{9,10},{10,9... | collective-permute-start | bytes 196616 | tf_op jit(solution)/shard_map/ppermute | solution.py:67
  117.2 7.2 %collective-permute-start.58 = (f32[2,64,128]{2,1,0:T(8,128)S(1)}, f32[2,64,128]{2,1,0:T(8,128)S(1)}, u32[]{:S(2)}, u32[]{:S(2)}) collective-permute-start(f32[2,64,128]{2,1,0:T(8,128)S(1)} %get-tuple-element.275), channel_id=1, source_target_pairs={{0,4},{1,6},{2,5},{3,7},{4,0},{5,2},{6,1},{7,3},{8,12},{9,14},{10,... | collective-permute-start | bytes 196616 | tf_op jit(solution)/shard_map/ppermute | solution.py:67
  119.0 6.2 %collective-permute-start.59 = (f32[2,64,128]{2,1,0:T(8,128)S(1)}, f32[2,64,128]{2,1,0:T(8,128)S(1)}, u32[]{:S(2)}, u32[]{:S(2)}) collective-permute-start(f32[2,64,128]{2,1,0:T(8,128)S(1)} %get-tuple-element.276), channel_id=1, source_target_pairs={{0,8},{1,10},{2,9},{3,11},{4,12},{5,14},{6,13},{7,15},{8,0},{9,2},... | collective-permute-start | bytes 196616 | tf_op jit(solution)/shard_map/ppermute | solution.py:67
  119.9 6.5 %collective-permute-start.60 = (f32[2,64,128]{2,1,0:T(8,128)S(1)}, f32[2,64,128]{2,1,0:T(8,128)S(1)}, u32[]{:S(2)}, u32[]{:S(2)}) collective-permute-start(f32[2,64,128]{2,1,0:T(8,128)S(1)} %get-tuple-element.277), channel_id=1, source_target_pairs={{0,12},{1,14},{2,13},{3,15},{4,8},{5,10},{6,9},{7,11},{8,4},{9,6},... | collective-permute-start | bytes 196616 | tf_op jit(solution)/shard_map/ppermute | solution.py:67
  (31 other events, 79.7 us)

commit v13 on v12

--- a/solution.py
+++ b/solution.py
@@ -477,9 +477,12 @@
 
 
 def last_kernel(scale, flags, part, k0, ki, kx, zm, ym, side, edge, image, change, vel,
-                new, mine, other):
+                prev, states, mine, other):
+    new = states.at[1]
     outer(flags, part, k0, ki, kx, zm, ym, side, edge, new)
     raw = from_halves(flags, (image[...] + new[...] * change[...]) * scale / vel[...])
+    new[...] = from_halves(flags, new[...])
+    states[0] = from_halves(flags, prev[...])
     count, height, lanes = mine.shape
     chunk = raw.shape[1] // (2 * count)
     for n in range(count):
@@ -490,11 +493,6 @@
             for m in (2 * n, 2 * n + 1))
         mine[n] = jnp.where(flags[0] == 0, even, odd)
         other[n] = jnp.where(flags[0] == 0, odd, even)
-
-
-def both_kernel(flags, a, b, out):
-    out[0] = from_halves(flags, a[...])
-    out[1] = from_halves(flags, b[...])
 
 
 def join_kernel(flags, mine, got, *outs):
@@ -534,12 +532,25 @@
     return jax.ShapeDtypeStruct(shape, F32)
 
 
+class Flags:
+    def __getitem__(self, n):
+        if n == 0:
+            return lax.axis_index("inline")
+        xline = lax.axis_index("xline")
+        if n == 1:
+            return jnp.bitwise_and(xline, 1)
+        if n == 3:
+            return jnp.right_shift(xline, 1)
+        place = 2 * xline + lax.axis_index("inline")
+        return jnp.bitwise_and(jnp.right_shift(place, n - 4), 1)
+
+
 def call(kernel, name, outs, *args, weight=0, far=0, scalars=0, scratch=()):
-    specs = [pl.BlockSpec(memory_space=pltpu.SMEM)] * (1 + scalars)
+    specs = [pl.BlockSpec(memory_space=pltpu.SMEM)] * scalars
     specs += [pl.BlockSpec(memory_space=pl.ANY)] * far
-    specs += [pl.BlockSpec(memory_space=pltpu.VMEM)] * (len(args) - 1 - scalars - far)
+    specs += [pl.BlockSpec(memory_space=pltpu.VMEM)] * (len(args) - scalars - far)
     return pl.pallas_call(
-        kernel,
+        functools.partial(kernel, Flags()),
         name=name,
         out_shape=outs,
         in_specs=specs,
@@ -564,8 +575,6 @@
     z_perm, c_perm, y_perm, swap_perm = plan.z(), plan.core(), plan.y(), plan.swap()
     stages = [(c_perm, c), (y_perm, y)]
     stages += [(plan.flip(1 << b), (q >> b) & 1) for b in range((nq - 1).bit_length())]
-    sub = (2 * q + c) * 2 + y
-    flags = jnp.stack([c, y, sub, q] + [bit for pairs, bit in stages]).astype(jnp.int32)
     field = shaped(size, depth)
     rim = [shaped(size // 2, depth), shaped(size // 2, depth), shaped(4 * cols, depth)]
 
@@ -599,22 +608,22 @@
     stacked = jnp.stack([velocity, fwd_before])
     got_model = send(stacked, swap_perm)
     full = nx * cols
-    inj, = call(functools.partial(source_kernel, 0, full), "source", [field], flags, src_cell, wavelet,
+    inj, = call(functools.partial(source_kernel, 0, full), "source", [field], src_cell, wavelet,
                 weight=0.7, scalars=2)
-    flags_in, inj = lax.optimization_barrier((flags, inj))
+    got[0], inj = lax.optimization_barrier((got[0], inj))
     density, p_now, *out = call(settle_kernel, "settle",
                                 [field, field] + [shaped(2, *r.shape) for r in rim],
-                                flags_in, log_density, fwd_now, *got, far=2)
+                                log_density, fwd_now, *got, far=2)
     zm, cm, ym = halo(*out)
     vel, p_before = call(settle_pair_kernel, "settle_model", [field, field],
-                         flags, velocity, fwd_before, got_model, weight=0.6, far=2)
-    parts = call(first_inner_kernel, "first_inner", [field] * 7, flags, density, p_now, cm,
+                         velocity, fwd_before, got_model, weight=0.6, far=2)
+    parts = call(first_inner_kernel, "first_inner", [field] * 7, density, p_now, cm,
                  near, deep, weight=1.3)
     got_adjoint = [send(after(v, parts[0]), swap_perm) for v in (adj_now, adj_before)]
 
     new, zo, co, yo, k0, ki, kx, kz = call(
         first_outer_kernel, "first_outer", [field] + rim + [field] * 4,
-        flags, p_now, p_before, vel, *parts, inj, zm, ym, side, edge)
+        p_now, p_before, vel, *parts, inj, zm, ym, side, edge)
     model = (k0, ki, kx, kz)
     states = [p_before, p_now, new]
     changes = []
@@ -625,7 +634,7 @@
     slots = subs * CAP
     entries, half_entries = shaped(subs, steps, 128), shaped(subs // 2, steps, 128)
     cells, lists, give = call(
-        pack_kernel, "pack", [shaped(1, slots), entries, half_entries], after(flags, k0), rec_counts,
+        pack_kernel, "pack", [shaped(1, slots), entries, half_entries], after(rec_counts, k0),
         rec_cells, observed, weight=0.8, far=3,
         scratch=[pltpu.VMEM(rec_counts.shape, jnp.int32), pltpu.VMEM(rec_cells.shape, jnp.int32),
                  pltpu.VMEM(observed.shape, F32)])
@@ -634,27 +643,26 @@
         stage = t - 1 if t <= min(len(stages), steps - 2) else None
         extra = [lists, send(give, stages[stage][0])] if stage is not None else []
         part, change = call(
-            functools.partial(forward_inner_kernel, t, full), "forward_inner", [field, field], flags,
-            src_cell, wavelet, cur, prev, *model, cm, near, deep, before, weight=1.2, scalars=2)
+            functools.partial(forward_inner_kernel, t, full), "forward_inner", [field, field], src_cell, wavelet, cur, prev, *model, cm, near, deep, before, weight=1.2, scalars=2)
         changes.append(change)
-        args = [flags, part, k0, ki, kx, zm, ym, side, edge]
+        args = [part, k0, ki, kx, zm, ym, side, edge]
         if t == steps - 3:
-            u_part, = call(adjoint_first_kernel, "adjoint_first", [field], flags, u_now, u_before,
+            u_part, = call(adjoint_first_kernel, "adjoint_first", [field], u_now, u_before,
                            *model, u_cm, near, deep, weight=1.1)
-            args[1] = after(part, u_part)
+            args[0] = after(part, u_part)
         if t == late:
             for n in range(steps - 2, len(stages)):
                 lists, *give = call(
                     functools.partial(trade_kernel, n), "trade",
-                    [entries] + ([half_entries] if n + 1 < len(stages) else []), flags, lists,
+                    [entries] + ([half_entries] if n + 1 < len(stages) else []), lists,
                     send(give, stages[n][0]))
                 give = give[0] if give else None
             receivers = call(
                 lists_kernel, "lists",
                 [jax.ShapeDtypeStruct((size, slots), BF16),
                  jax.ShapeDtypeStruct((slots, size), BF16), shaped(slots, depth),
-                 shaped(slots, steps)], flags, lists, cells, got_cells, weight=0.8)
-            args[1] = after(part, receivers[0])
+                 shaped(slots, steps)], lists, cells, got_cells, weight=0.8)
+            args[0] = after(part, receivers[0])
         if t == steps - 1:
             new, u_new, *out = call(
                 functools.partial(turn_kernel, t), "turn", [field, field] + rim, *args, u_part,
@@ -664,10 +672,9 @@
         if t == len(stages) - 2:
             got_cells = send(after(cells, part), swap_perm)
         if t == len(stages) - 1:
-            args[1] = after(part, got_cells)
+            args[0] = after(part, got_cells)
         if t == double:
-            u_now, u_before = call(settle_pair_kernel, "settle_adjoint", [field, field], flags,
-                                   adj_now, adj_before, *got_adjoint, weight=0.6, far=2)
+            u_now, u_before = call(settle_pair_kernel, "settle_adjoint", [field, field], adj_now, adj_before, *got_adjoint, weight=0.6, far=2)
             args.append(u_now)
         outs = [field] + ([shaped(2, *r.shape) for r in rim] if t == double else rim)
         if extra:
@@ -691,27 +698,25 @@
         t = steps - 1 - j
         terms = [changes[t + 1], *image] if image else states[:-4:-1]
         part, *image = call(
-            functools.partial(adjoint_inner_kernel, t), "adjoint_inner", [field, field], flags,
-            u_now, u_before, *model, cm, near, deep, states[t + 2], *receivers, *terms, weight=1.5)
+            functools.partial(adjoint_inner_kernel, t), "adjoint_inner", [field, field], u_now, u_before, *model, cm, near, deep, states[t + 2], *receivers, *terms, weight=1.5)
         args = [part, k0, ki, kx, zm, ym, side, edge]
         if j == steps - 1:
-            u_last, mine, other = call(
-                functools.partial(last_kernel, 2.0 / steps), "last", [field, half, half], flags,
-                *args, *image, changes[0], vel)
+            final, mine, other = call(
+                functools.partial(last_kernel, 2.0 / steps), "last",
+                [shaped(2, *field.shape), half, half], *args, *image, changes[0], vel, u_now)
             break
         u_before = u_now
         u_now, *out = call(functools.partial(outer_kernel, None, False), "adjoint_outer", [field] + rim,
-                           flags, *args)
+                           *args)
         zm, cm, ym = halo(*out)
 
-    final, = call(both_kernel, "both", [shaped(2, *field.shape)], flags, u_now, u_last, weight=0.4)
     got = send(final, swap_perm)
-    pieces = call(join_kernel, "join", [shaped(2, *half.shape[1:])] * nq, flags, mine,
+    pieces = call(join_kernel, "join", [shaped(2, *half.shape[1:])] * nq, mine,
                   send(other, c_perm))
     pieces = [send(pieces[s], plan.spread(s)) for s in reversed(range(nq))][::-1]
-    adj_prev, adj_out = call(select_kernel, "select", [field, field], flags, final, got, weight=1.2)
+    adj_prev, adj_out = call(select_kernel, "select", [field, field], final, got, weight=1.2)
     gradient, = call(filter_kernel, "filter", [shaped(chunk, rows, nx * cols)],
-                     after(flags, adj_out), *pieces)
+                     after(pieces[0], adj_out), *pieces[1:])
     block = (rows, cols, depth)
     return gradient, adj_out.reshape(block), adj_prev.reshape(block)
 

time: 128 us -> 118 us (0.922)
  Pallas kernels: 45.2 us -> 26.1 us
  waiting for transfers between devices: 20.5 us -> 31.8 us
  starting transfers between devices: 58.5 us -> 56.1 us
    pallas_call x41 -> x40, Pallas kernels: 45.2 us -> 26.1 us  [call(): pl.pallas_call(functools.partial(kernel, Flags()), name=name, out_shape=o...]
    ppermute x61, waiting for transfers between devices: 20.5 us -> 31.8 us  [send(): return lax.ppermute(value, ALL, pairs)]
    ppermute x61, starting transfers between devices: 58.5 us -> 56.1 us  [send(): return lax.ppermute(value, ALL, pairs)]
  transfers between devices with their start and end apart: 61 -> 61, of which waited for: 25 -> 30; matrix products, arithmetic and copies ran while one was open for 1% -> 1% of each run, Pallas kernels for 24% -> 18%
where the time goes in v13:
time: 118 us
  starting transfers between devices  56.1 us (48%)
  waiting for transfers between devices  31.8 us (27%)
  Pallas kernels  26.1 us (22%)
  local copies, waits for them, and re-layouts  1.66 us (1%)
  other arithmetic  1.24 us (1%)
  between operations  1.21 us (1%)
    ppermute x61, starting transfers between devices, send(): return lax.ppermute(value, ALL, pairs)  56.1 us
    ppermute x61, waiting for transfers between devices, send(): return lax.ppermute(value, ALL, pairs)  31.8 us
    pallas_call x40, Pallas kernels, call(): pl.pallas_call(functools.partial(kernel, Flags()), name=name, out_shape=o...  26.1 us
  transfers between devices with their start and end apart: 61, of which 30 were waited for; matrix products, arithmetic and copies ran while one was open for 1% of the time, Pallas kernels for 18%

profile of v13, /device:TPU:1, one launch (start us, length us, event | category | flops | bytes accessed | tf_op | source)
XLA Modules:
  0.0 118.2 jit_solution(7797314132317649105)
XLA Ops:
  0.6 2.7 %collective-permute-start.1 = (f32[256,256]{1,0:T(8,128)}, f32[256,256]{1,0:T(8,128)S(1)}, u32[]{:S(2)}, u32[]{:S(2)}) collective-permute-start(f32[256,256]{1,0:T(8,128)} %bitcast.16), channel_id=1, source_target_pairs={{0,16},{1,2},{2,1},{3,19},{4,20},{5,6},{6,5},{7,23},{8,24},{9,10},... | collective-permute-start | bytes 786440 | tf_op jit(solution)/shard_map/ppermute | solution.py:67
  3.4 1.1 pad_maximum_fusion
  4.5 1.7 %collective-permute-start.2 = (f32[2,256,256]{2,1,0:T(8,128)S(1)}, f32[2,256,256]{2,1,0:T(8,128)S(1)}, u32[]{:S(2)}, u32[]{:S(2)}) collective-permute-start(f32[2,256,256]{2,1,0:T(8,128)S(1)} %pad_maximum_fusion), channel_id=1, source_target_pairs={{0,16},{1,2},{2,1},{3,19},{4,20},{5,6},{6,5},{7,23},{8,24},{9,10},... | collective-permute-start | bytes 1572872 | tf_op jit(solution)/shard_map/ppermute | solution.py:67
  8.8 1.9 %collective-permute-done.recv_a = f32[256,256]{1,0:T(8,128)S(1)} collective-permute-done((f32[256,256]{1,0:T(8,128)}, f32[256,256]{1,0:T(8,128)S(1)}, u32[]{:S(2)}, u32[]{:S(2)}) %collective-permute-start) | collective-permute-done | bytes 262176 | tf_op jit(solution)/shard_map/ppermute | solution.py:67
  11.3 1.8 %collective-permute-start.4 = (f32[2,128,256]{2,1,0:T(8,128)S(1)}, f32[2,128,256]{2,1,0:T(8,128)S(1)}, u32[]{:S(2)}, u32[]{:S(2)}) collective-permute-start(f32[2,128,256]{2,1,0:T(8,128)S(1)} %get-tuple-element.155), channel_id=1, source_target_pairs={{0,16},{1,4},{2,18},{3,6},{4,1},{5,8},{6,3},{7,10},{8,5},{9,12},{1... | collective-permute-start | bytes 786440 | tf_op jit(solution)/shard_map/ppermute | solution.py:67
  14.8 1.3 %collective-permute-start.9 = (f32[256,256]{1,0:T(8,128)S(1)}, f32[256,256]{1,0:T(8,128)S(1)}, u32[]{:S(2)}, u32[]{:S(2)}) collective-permute-start(f32[256,256]{1,0:T(8,128)S(1)} %bitcast.18), channel_id=1, source_target_pairs={{0,16},{1,2},{2,1},{3,19},{4,20},{5,6},{6,5},{7,23},{8,24},{9,10},... | collective-permute-start | bytes 786440 | tf_op jit(solution)/shard_map/ppermute | solution.py:67
  18.0 2.1 %collective-permute-start.6 = (f32[128,256]{1,0:T(8,128)S(1)}, f32[128,256]{1,0:T(8,128)S(1)}, u32[]{:S(2)}, u32[]{:S(2)}) collective-permute-start(f32[128,256]{1,0:T(8,128)S(1)} %get-tuple-element.162), channel_id=1, source_target_pairs={{0,1},{1,0},{2,3},{3,2},{4,5},{5,4},{6,7},{7,6},{8,9},{9,8},{10,11... | collective-permute-start | bytes 393224 | tf_op jit(solution)/shard_map/ppermute | solution.py:67
  20.2 1.8 %collective-permute-start.8 = (f32[32,256]{1,0:T(8,128)S(1)}, f32[32,256]{1,0:T(8,128)S(1)}, u32[]{:S(2)}, u32[]{:S(2)}) collective-permute-start(f32[32,256]{1,0:T(8,128)S(1)} %get-tuple-element.165), channel_id=1, source_target_pairs={{0,2},{1,3},{2,0},{3,1},{4,6},{5,7},{6,4},{7,5},{8,10},{9,11},{10,... | collective-permute-start | bytes 98312 | tf_op jit(solution)/shard_map/ppermute | solution.py:67
  22.1 1.9 %collective-permute-start.11 = (f32[8,8,128]{2,1,0:T(8,128)S(1)}, f32[8,8,128]{2,1,0:T(8,128)S(1)}, u32[]{:S(2)}, u32[]{:S(2)}) collective-permute-start(f32[8,8,128]{2,1,0:T(8,128)S(1)} %get-tuple-element.171), channel_id=1, source_target_pairs={{0,1},{1,0},{2,3},{3,2},{4,5},{5,4},{6,7},{7,6},{8,9},{9,8},{10,11... | collective-permute-start | bytes 98312 | tf_op jit(solution)/shard_map/ppermute | solution.py:67
  24.1 1.3 %forward_inner.7 = (f32[256,256]{1,0:T(8,128)S(1)}, f32[256,256]{1,0:T(8,128)S(1)}) custom-call(s32[16]{0:T(128)S(1)} %copy-done.8, f32[8,16]{1,0:T(8,128)S(1)} %copy-done.3, f32[256,256]{1,0:T(8,128)S(1)} %get-tuple-element.157.cur.prev.before.state, f32[256,256]{1,0:T(8,128)S(1)} %get-tuple-element.142.cur.prev.before, ...), custom_call_target="tpu_custom_call" | custom-call | flops 1000 | bytes 4321000 | tf_op jit(solution)/shard_map/forward_inner/pallas_call | solution.py:552
  26.8 1.2 %collective-permute-start.14 = (f32[2,32,256]{2,1,0:T(8,128)S(1)}, f32[2,32,256]{2,1,0:T(8,128)S(1)}, u32[]{:S(2)}, u32[]{:S(2)}) collective-permute-start(f32[2,32,256]{2,1,0:T(8,128)S(1)} %get-tuple-element.176), channel_id=1, source_target_pairs={{0,2},{1,3},{2,0},{3,1},{4,6},{5,7},{6,4},{7,5},{8,10},{9,11},{10,... | collective-permute-start | bytes 196616 | tf_op jit(solution)/shard_map/ppermute | solution.py:67
  28.3 1.3 %forward_inner.8 = (f32[256,256]{1,0:T(8,128)S(1)}, f32[256,256]{1,0:T(8,128)S(1)}) custom-call(s32[16]{0:T(128)S(1)} %copy-done.8, f32[8,16]{1,0:T(8,128)S(1)} %copy-done.3, f32[256,256]{1,0:T(8,128)S(1)} %get-tuple-element.172.cur.prev.before.state, f32[256,256]{1,0:T(8,128)S(1)} %get-tuple-element.157.cur.prev.before.state, ...), custom_call_target="tpu_custom_call" | custom-call | flops 1000 | bytes 4321000 | tf_op jit(solution)/shard_map/forward_inner/pallas_call | solution.py:552
  29.6 1.5 %collective-permute-done.15.rest_1_ = f32[8,8,128]{2,1,0:T(8,128)S(1)} collective-permute-done((f32[8,8,128]{2,1,0:T(8,128)S(1)}, f32[8,8,128]{2,1,0:T(8,128)S(1)}, u32[]{:S(2)}, u32[]{:S(2)}) %collective-permute-start.15) | collective-permute-done | bytes 32800 | tf_op jit(solution)/shard_map/ppermute | solution.py:67
  31.1 1.8 %collective-permute-done.13.zm.u_zm = f32[2,128,256]{2,1,0:T(8,128)S(1)} collective-permute-done((f32[2,128,256]{2,1,0:T(8,128)S(1)}, f32[2,128,256]{2,1,0:T(8,128)S(1)}, u32[]{:S(2)}, u32[]{:S(2)}) %collective-permute-start.13) | collective-permute-done | bytes 262176 | tf_op jit(solution)/shard_map/ppermute | solution.py:67
  34.9 1.6 %collective-permute-start.20 = (f32[8,8,128]{2,1,0:T(8,128)S(1)}, f32[8,8,128]{2,1,0:T(8,128)S(1)}, u32[]{:S(2)}, u32[]{:S(2)}) collective-permute-start(f32[8,8,128]{2,1,0:T(8,128)S(1)} %get-tuple-element.188), channel_id=1, source_target_pairs={{0,4},{1,5},{2,6},{3,7},{4,0},{5,1},{6,2},{7,3},{8,12},{9,13},{10,... | collective-permute-start | bytes 98312 | tf_op jit(solution)/shard_map/ppermute | solution.py:67
  36.5 1.1 collective-permute-start.17
  37.6 1.3 %forward_inner.9 = (f32[256,256]{1,0:T(8,128)S(1)}, f32[256,256]{1,0:T(8,128)S(1)}) custom-call(s32[16]{0:T(128)S(1)} %copy-done.8, f32[8,16]{1,0:T(8,128)S(1)} %copy-done.3, f32[256,256]{1,0:T(8,128)S(1)} %get-tuple-element.179.cur.prev.before.state, f32[256,256]{1,0:T(8,128)S(1)} %get-tuple-element.172.cur.prev.before.state, ...), custom_call_target="tpu_custom_call" | custom-call | flops 1000 | bytes 4321000 | tf_op jit(solution)/shard_map/forward_inner/pallas_call | solution.py:552
  39.8 1.3 %collective-permute-start.21 = (f32[128,256]{1,0:T(8,128)S(1)}, f32[128,256]{1,0:T(8,128)S(1)}, u32[]{:S(2)}, u32[]{:S(2)}) collective-permute-start(f32[128,256]{1,0:T(8,128)S(1)} %get-tuple-element.190), channel_id=1, source_target_pairs={{0,1},{1,0},{2,3},{3,2},{4,5},{5,4},{6,7},{7,6},{8,9},{9,8},{10,11... | collective-permute-start | bytes 393224 | tf_op jit(solution)/shard_map/ppermute | solution.py:67
  42.4 1.2 %collective-permute-start.24 = (f32[8,8,128]{2,1,0:T(8,128)S(1)}, f32[8,8,128]{2,1,0:T(8,128)S(1)}, u32[]{:S(2)}, u32[]{:S(2)}) collective-permute-start(f32[8,8,128]{2,1,0:T(8,128)S(1)} %get-tuple-element.195), channel_id=1, source_target_pairs={{0,8},{1,9},{2,10},{3,11},{4,12},{5,13},{6,14},{7,15},{8,0},{9,1},... | collective-permute-start | bytes 98312 | tf_op jit(solution)/shard_map/ppermute | solution.py:67
  43.7 1.3 %forward_inner.10 = (f32[256,256]{1,0:T(8,128)S(1)}, f32[256,256]{1,0:T(8,128)S(1)}) custom-call(s32[16]{0:T(128)S(1)} %copy-done.8, f32[8,16]{1,0:T(8,128)S(1)} %copy-done.3, f32[256,256]{1,0:T(8,128)S(1)} %get-tuple-element.189.cur.prev.before.state, f32[256,256]{1,0:T(8,128)S(1)} %get-tuple-element.179.cur.prev.before.state, ...), custom_call_target="tpu_custom_call" | custom-call | flops 1000 | bytes 4321000 | tf_op jit(solution)/shard_map/forward_inner/pallas_call | solution.py:552
  45.0 1.1 collective-permute-done.24.rest_1_
  46.4 1.9 %collective-permute-start.25 = (f32[128,256]{1,0:T(8,128)S(1)}, f32[128,256]{1,0:T(8,128)S(1)}, u32[]{:S(2)}, u32[]{:S(2)}) collective-permute-start(f32[128,256]{1,0:T(8,128)S(1)} %get-tuple-element.197), channel_id=1, source_target_pairs={{0,1},{1,0},{2,3},{3,2},{4,5},{5,4},{6,7},{7,6},{8,9},{9,8},{10,11... | collective-permute-start | bytes 393224 | tf_op jit(solution)/shard_map/ppermute | solution.py:67
  48.9 1.0 collective-permute-start.27
  50.4 1.3 %forward_inner.11 = (f32[256,256]{1,0:T(8,128)S(1)}, f32[256,256]{1,0:T(8,128)S(1)}) custom-call(s32[16]{0:T(128)S(1)} %copy-done.8, f32[8,16]{1,0:T(8,128)S(1)} %copy-done.3, f32[256,256]{1,0:T(8,128)S(1)} %get-tuple-element.196.cur.prev.before.state, f32[256,256]{1,0:T(8,128)S(1)} %get-tuple-element.189.cur.prev.before.state, ...), custom_call_target="tpu_custom_call" | custom-call | flops 1000 | bytes 4321000 | tf_op jit(solution)/shard_map/forward_inner/pallas_call | solution.py:552
  53.1 1.0 collective-permute-start.28
  55.2 1.4 %forward_inner.12 = (f32[256,256]{1,0:T(8,128)S(1)}, f32[256,256]{1,0:T(8,128)S(1)}) custom-call(s32[16]{0:T(128)S(1)} %copy-done.8, f32[8,16]{1,0:T(8,128)S(1)} %copy-done.3, f32[256,256]{1,0:T(8,128)S(1)} %get-tuple-element.203.cur.prev.rest_2_.state, f32[256,256]{1,0:T(8,128)S(1)} %get-tuple-element.196.cur.prev.before.state, ...), custom_call_target="tpu_custom_call" | custom-call | flops 1000 | bytes 4321000 | tf_op jit(solution)/shard_map/forward_inner/pallas_call | solution.py:552
  57.3 1.4 %collective-permute-done.29.zm = f32[128,256]{1,0:T(8,128)S(1)} collective-permute-done((f32[128,256]{1,0:T(8,128)S(1)}, f32[128,256]{1,0:T(8,128)S(1)}, u32[]{:S(2)}, u32[]{:S(2)}) %collective-permute-start.29) | collective-permute-done | bytes 131104 | tf_op jit(solution)/shard_map/ppermute | solution.py:67
  60.9 1.3 %forward_inner.13 = (f32[256,256]{1,0:T(8,128)S(1)}, f32[256,256]{1,0:T(8,128)S(1)}) custom-call(s32[16]{0:T(128)S(1)} %copy-done.8, f32[8,16]{1,0:T(8,128)S(1)} %copy-done.3, f32[256,256]{1,0:T(8,128)S(1)} %get-tuple-element.211.cur.state.rest_1_, f32[256,256]{1,0:T(8,128)S(1)} %get-tuple-element.203.cur.prev.rest_2_.state, ...), custom_call_target="tpu_custom_call" | custom-call | flops 1000 | bytes 4321000 | tf_op jit(solution)/shard_map/forward_inner/pallas_call | solution.py:552
  66.9 1.0 adjoint_inner.7
  67.9 1.3 %collective-permute-done.36.ym = f32[32,256]{1,0:T(8,128)S(1)} collective-permute-done((f32[32,256]{1,0:T(8,128)S(1)}, f32[32,256]{1,0:T(8,128)S(1)}, u32[]{:S(2)}, u32[]{:S(2)}) %collective-permute-start.36) | collective-permute-done | bytes 32800 | tf_op jit(solution)/shard_map/ppermute | solution.py:67
  72.3 1.0 adjoint_inner.8
  73.3 1.3 %collective-permute-done.39.ym = f32[32,256]{1,0:T(8,128)S(1)} collective-permute-done((f32[32,256]{1,0:T(8,128)S(1)}, f32[32,256]{1,0:T(8,128)S(1)}, u32[]{:S(2)}, u32[]{:S(2)}) %collective-permute-start.39) | collective-permute-done | bytes 32800 | tf_op jit(solution)/shard_map/ppermute | solution.py:67
  77.7 1.0 adjoint_inner.9
  78.6 1.3 %collective-permute-done.42.ym = f32[32,256]{1,0:T(8,128)S(1)} collective-permute-done((f32[32,256]{1,0:T(8,128)S(1)}, f32[32,256]{1,0:T(8,128)S(1)}, u32[]{:S(2)}, u32[]{:S(2)}) %collective-permute-start.42) | collective-permute-done | bytes 32800 | tf_op jit(solution)/shard_map/ppermute | solution.py:67
  83.0 1.2 %adjoint_inner.10 = (f32[256,256]{1,0:T(8,128)S(1)}, f32[256,256]{1,0:T(8,128)S(1)}) custom-call(f32[256,256]{1,0:T(8,128)S(1)} %get-tuple-element.239.cur.prev, f32[256,256]{1,0:T(8,128)S(1)} %get-tuple-element.232.cur.prev, f32[256,256]{1,0:T(8,128)S(1)} %get-tuple-element.158.k0, f32[256,256]{1,0:T(8,128)S(1)} %get-tuple-element.159.ki, ...), custom_call_target="tpu_custom_call" | custom-call | flops 1000 | bytes 5401000 | tf_op jit(solution)/shard_map/adjoint_inner/pallas_call | solution.py:552
  84.2 1.1 collective-permute-done.45.ym
  89.4 1.3 %collective-permute-done.48.ym = f32[32,256]{1,0:T(8,128)S(1)} collective-permute-done((f32[32,256]{1,0:T(8,128)S(1)}, f32[32,256]{1,0:T(8,128)S(1)}, u32[]{:S(2)}, u32[]{:S(2)}) %collective-permute-start.48) | collective-permute-done | bytes 32800 | tf_op jit(solution)/shard_map/ppermute | solution.py:67
  93.8 1.0 adjoint_inner.12
  94.7 1.3 %collective-permute-done.51.ym = f32[32,256]{1,0:T(8,128)S(1)} collective-permute-done((f32[32,256]{1,0:T(8,128)S(1)}, f32[32,256]{1,0:T(8,128)S(1)}, u32[]{:S(2)}, u32[]{:S(2)}) %collective-permute-start.51) | collective-permute-done | bytes 32800 | tf_op jit(solution)/shard_map/ppermute | solution.py:67
  100.1 1.3 %collective-permute-done.54.ym = f32[32,256]{1,0:T(8,128)S(1)} collective-permute-done((f32[32,256]{1,0:T(8,128)S(1)}, f32[32,256]{1,0:T(8,128)S(1)}, u32[]{:S(2)}, u32[]{:S(2)}) %collective-permute-start.54) | collective-permute-done | bytes 32800 | tf_op jit(solution)/shard_map/ppermute | solution.py:67
  102.9 1.1 collective-permute-start.57
  104.4 1.0 collective-permute-done.55.got
  105.4 2.6 %collective-permute-start.56 = (f32[2,64,128]{2,1,0:T(8,128)S(1)}, f32[2,64,128]{2,1,0:T(8,128)S(1)}, u32[]{:S(2)}, u32[]{:S(2)}) collective-permute-start(f32[2,64,128]{2,1,0:T(8,128)S(1)} %get-tuple-element.271), channel_id=1, source_target_pairs={{0,0},{1,2},{2,1},{3,3},{4,4},{5,6},{6,5},{7,7},{8,8},{9,10},{10,9... | collective-permute-start | bytes 196616 | tf_op jit(solution)/shard_map/ppermute | solution.py:67
  108.0 1.6 %collective-permute-start.58 = (f32[2,64,128]{2,1,0:T(8,128)S(1)}, f32[2,64,128]{2,1,0:T(8,128)S(1)}, u32[]{:S(2)}, u32[]{:S(2)}) collective-permute-start(f32[2,64,128]{2,1,0:T(8,128)S(1)} %get-tuple-element.275), channel_id=1, source_target_pairs={{0,4},{1,6},{2,5},{3,7},{4,0},{5,2},{6,1},{7,3},{8,12},{9,14},{10,... | collective-permute-start | bytes 196616 | tf_op jit(solution)/shard_map/ppermute | solution.py:67
  110.4 3.1 %collective-permute-start.60 = (f32[2,64,128]{2,1,0:T(8,128)S(1)}, f32[2,64,128]{2,1,0:T(8,128)S(1)}, u32[]{:S(2)}, u32[]{:S(2)}) collective-permute-start(f32[2,64,128]{2,1,0:T(8,128)S(1)} %get-tuple-element.277), channel_id=1, source_target_pairs={{0,12},{1,14},{2,13},{3,15},{4,8},{5,10},{6,9},{7,11},{8,4},{9,6},... | collective-permute-start | bytes 196616 | tf_op jit(solution)/shard_map/ppermute | solution.py:67
  114.4 1.3 %collective-permute-done.59.refs_2_ = f32[2,64,128]{2,1,0:T(8,128)S(1)} collective-permute-done((f32[2,64,128]{2,1,0:T(8,128)S(1)}, f32[2,64,128]{2,1,0:T(8,128)S(1)}, u32[]{:S(2)}, u32[]{:S(2)}) %collective-permute-start.59) | collective-permute-done | bytes 65568 | tf_op jit(solution)/shard_map/ppermute | solution.py:67
  115.7 1.2 %collective-permute-done.60.refs_3_ = f32[2,64,128]{2,1,0:T(8,128)S(1)} collective-permute-done((f32[2,64,128]{2,1,0:T(8,128)S(1)}, f32[2,64,128]{2,1,0:T(8,128)S(1)}, u32[]{:S(2)}, u32[]{:S(2)}) %collective-permute-start.60) | collective-permute-done | bytes 65568 | tf_op jit(solution)/shard_map/ppermute | solution.py:67
  116.9 1.3 %filter.1 = f32[32,32,64]{2,1,0:T(8,128)} custom-call(f32[2,64,128]{2,1,0:T(8,128)S(1)} %collective-permute-done.56.refs_0_, f32[2,64,128]{2,1,0:T(8,128)S(1)} %collective-permute-done.58.refs_1_, f32[2,64,128]{2,1,0:T(8,128)S(1)} %collective-permute-done.59.refs_2_, f32[2,64,128]{2,1,0:T(8,128)S(1)} %collective-permute-done.60.refs_3_), custom_call_target="tpu_custom_call" | custom-call | flops 1000 | bytes 1000 | tf_op jit(solution)/shard_map/filter/pallas_call | solution.py:552
  (156 shorter events, 48.2 us)
Async XLA Ops:
  0.6 10.1 %collective-permute-start.1 = (f32[256,256]{1,0:T(8,128)}, f32[256,256]{1,0:T(8,128)S(1)}, u32[]{:S(2)}, u32[]{:S(2)}) collective-permute-start(f32[256,256]{1,0:T(8,128)} %bitcast.16), channel_id=1, source_target_pairs={{0,16},{1,2},{2,1},{3,19},{4,20},{5,6},{6,5},{7,23},{8,24},{9,10},... | collective-permute-start | bytes 786440 | tf_op jit(solution)/shard_map/ppermute | solution.py:67
  3.3 7.4 %collective-permute-start = (f32[256,256]{1,0:T(8,128)}, f32[256,256]{1,0:T(8,128)S(1)}, u32[]{:S(2)}, u32[]{:S(2)}) collective-permute-start(f32[256,256]{1,0:T(8,128)} %bitcast.14), channel_id=1, source_target_pairs={{0,16},{1,2},{2,1},{3,19},{4,20},{5,6},{6,5},{7,23},{8,24},{9,10},... | collective-permute-start | bytes 786440 | tf_op jit(solution)/shard_map/ppermute | solution.py:67
  4.5 12.2 %collective-permute-start.2 = (f32[2,256,256]{2,1,0:T(8,128)S(1)}, f32[2,256,256]{2,1,0:T(8,128)S(1)}, u32[]{:S(2)}, u32[]{:S(2)}) collective-permute-start(f32[2,256,256]{2,1,0:T(8,128)S(1)} %pad_maximum_fusion), channel_id=1, source_target_pairs={{0,16},{1,2},{2,1},{3,19},{4,20},{5,6},{6,5},{7,23},{8,24},{9,10},... | collective-permute-start | bytes 1572872 | tf_op jit(solution)/shard_map/ppermute | solution.py:67
  11.3 6.1 %collective-permute-start.4 = (f32[2,128,256]{2,1,0:T(8,128)S(1)}, f32[2,128,256]{2,1,0:T(8,128)S(1)}, u32[]{:S(2)}, u32[]{:S(2)}) collective-permute-start(f32[2,128,256]{2,1,0:T(8,128)S(1)} %get-tuple-element.155), channel_id=1, source_target_pairs={{0,16},{1,4},{2,18},{3,6},{4,1},{5,8},{6,3},{7,10},{8,5},{9,12},{1... | collective-permute-start | bytes 786440 | tf_op jit(solution)/shard_map/ppermute | solution.py:67
  13.2 4.2 %collective-permute-start.5 = (f32[2,32,256]{2,1,0:T(8,128)S(1)}, f32[2,32,256]{2,1,0:T(8,128)S(1)}, u32[]{:S(2)}, u32[]{:S(2)}) collective-permute-start(f32[2,32,256]{2,1,0:T(8,128)S(1)} %get-tuple-element.156), channel_id=1, source_target_pairs={{0,2},{1,3},{2,0},{3,1},{4,6},{5,7},{6,4},{7,5},{8,10},{9,11},{10,... | collective-permute-start | bytes 196616 | tf_op jit(solution)/shard_map/ppermute | solution.py:67
  14.8 10.5 %collective-permute-start.9 = (f32[256,256]{1,0:T(8,128)S(1)}, f32[256,256]{1,0:T(8,128)S(1)}, u32[]{:S(2)}, u32[]{:S(2)}) collective-permute-start(f32[256,256]{1,0:T(8,128)S(1)} %bitcast.18), channel_id=1, source_target_pairs={{0,16},{1,2},{2,1},{3,19},{4,20},{5,6},{6,5},{7,23},{8,24},{9,10},... | collective-permute-start | bytes 786440 | tf_op jit(solution)/shard_map/ppermute | solution.py:67
  16.1 9.3 %collective-permute-start.10 = (f32[256,256]{1,0:T(8,128)S(1)}, f32[256,256]{1,0:T(8,128)S(1)}, u32[]{:S(2)}, u32[]{:S(2)}) collective-permute-start(f32[256,256]{1,0:T(8,128)S(1)} %bitcast.20), channel_id=1, source_target_pairs={{0,16},{1,2},{2,1},{3,19},{4,20},{5,6},{6,5},{7,23},{8,24},{9,10},... | collective-permute-start | bytes 786440 | tf_op jit(solution)/shard_map/ppermute | solution.py:67
  18.0 4.2 %collective-permute-start.6 = (f32[128,256]{1,0:T(8,128)S(1)}, f32[128,256]{1,0:T(8,128)S(1)}, u32[]{:S(2)}, u32[]{:S(2)}) collective-permute-start(f32[128,256]{1,0:T(8,128)S(1)} %get-tuple-element.162), channel_id=1, source_target_pairs={{0,1},{1,0},{2,3},{3,2},{4,5},{5,4},{6,7},{7,6},{8,9},{9,8},{10,11... | collective-permute-start | bytes 393224 | tf_op jit(solution)/shard_map/ppermute | solution.py:67
  20.0 5.7 %collective-permute-start.7 = (f32[128,256]{1,0:T(8,128)S(1)}, f32[128,256]{1,0:T(8,128)S(1)}, u32[]{:S(2)}, u32[]{:S(2)}) collective-permute-start(f32[128,256]{1,0:T(8,128)S(1)} %get-tuple-element.164), channel_id=1, source_target_pairs={{0,16},{1,4},{2,18},{3,6},{4,1},{5,8},{6,3},{7,10},{8,5},{9,12},{1... | collective-permute-start | bytes 393224 | tf_op jit(solution)/shard_map/ppermute | solution.py:67
  20.2 5.5 %collective-permute-start.8 = (f32[32,256]{1,0:T(8,128)S(1)}, f32[32,256]{1,0:T(8,128)S(1)}, u32[]{:S(2)}, u32[]{:S(2)}) collective-permute-start(f32[32,256]{1,0:T(8,128)S(1)} %get-tuple-element.165), channel_id=1, source_target_pairs={{0,2},{1,3},{2,0},{3,1},{4,6},{5,7},{6,4},{7,5},{8,10},{9,11},{10,... | collective-permute-start | bytes 98312 | tf_op jit(solution)/shard_map/ppermute | solution.py:67
  22.1 3.6 %collective-permute-start.11 = (f32[8,8,128]{2,1,0:T(8,128)S(1)}, f32[8,8,128]{2,1,0:T(8,128)S(1)}, u32[]{:S(2)}, u32[]{:S(2)}) collective-permute-start(f32[8,8,128]{2,1,0:T(8,128)S(1)} %get-tuple-element.171), channel_id=1, source_target_pairs={{0,1},{1,0},{2,3},{3,2},{4,5},{5,4},{6,7},{7,6},{8,9},{9,8},{10,11... | collective-permute-start | bytes 98312 | tf_op jit(solution)/shard_map/ppermute | solution.py:67
  26.8 6.1 %collective-permute-start.13 = (f32[2,128,256]{2,1,0:T(8,128)S(1)}, f32[2,128,256]{2,1,0:T(8,128)S(1)}, u32[]{:S(2)}, u32[]{:S(2)}) collective-permute-start(f32[2,128,256]{2,1,0:T(8,128)S(1)} %get-tuple-element.175), channel_id=1, source_target_pairs={{0,16},{1,4},{2,18},{3,6},{4,1},{5,8},{6,3},{7,10},{8,5},{9,12},{1... | collective-permute-start | bytes 786440 | tf_op jit(solution)/shard_map/ppermute | solution.py:67
  26.8 4.3 %collective-permute-start.14 = (f32[2,32,256]{2,1,0:T(8,128)S(1)}, f32[2,32,256]{2,1,0:T(8,128)S(1)}, u32[]{:S(2)}, u32[]{:S(2)}) collective-permute-start(f32[2,32,256]{2,1,0:T(8,128)S(1)} %get-tuple-element.176), channel_id=1, source_target_pairs={{0,2},{1,3},{2,0},{3,1},{4,6},{5,7},{6,4},{7,5},{8,10},{9,11},{10,... | collective-permute-start | bytes 196616 | tf_op jit(solution)/shard_map/ppermute | solution.py:67
  28.0 3.1 %collective-permute-start.15 = (f32[8,8,128]{2,1,0:T(8,128)S(1)}, f32[8,8,128]{2,1,0:T(8,128)S(1)}, u32[]{:S(2)}, u32[]{:S(2)}) collective-permute-start(f32[8,8,128]{2,1,0:T(8,128)S(1)} %get-tuple-element.178), channel_id=1, source_target_pairs={{0,2},{1,3},{2,0},{3,1},{4,6},{5,7},{6,4},{7,5},{8,10},{9,11},{10,... | collective-permute-start | bytes 98312 | tf_op jit(solution)/shard_map/ppermute | solution.py:67
  33.1 4.5 %collective-permute-start.16 = (f32[128,256]{1,0:T(8,128)S(1)}, f32[128,256]{1,0:T(8,128)S(1)}, u32[]{:S(2)}, u32[]{:S(2)}) collective-permute-start(f32[128,256]{1,0:T(8,128)S(1)} %get-tuple-element.180), channel_id=1, source_target_pairs={{0,1},{1,0},{2,3},{3,2},{4,5},{5,4},{6,7},{7,6},{8,9},{9,8},{10,11... | collective-permute-start | bytes 393224 | tf_op jit(solution)/shard_map/ppermute | solution.py:67
  33.8 5.8 %collective-permute-start.18 = (f32[128,256]{1,0:T(8,128)S(1)}, f32[128,256]{1,0:T(8,128)S(1)}, u32[]{:S(2)}, u32[]{:S(2)}) collective-permute-start(f32[128,256]{1,0:T(8,128)S(1)} %get-tuple-element.185), channel_id=1, source_target_pairs={{0,16},{1,4},{2,18},{3,6},{4,1},{5,8},{6,3},{7,10},{8,5},{9,12},{1... | collective-permute-start | bytes 393224 | tf_op jit(solution)/shard_map/ppermute | solution.py:67
  34.1 5.5 %collective-permute-start.19 = (f32[32,256]{1,0:T(8,128)S(1)}, f32[32,256]{1,0:T(8,128)S(1)}, u32[]{:S(2)}, u32[]{:S(2)}) collective-permute-start(f32[32,256]{1,0:T(8,128)S(1)} %get-tuple-element.186), channel_id=1, source_target_pairs={{0,2},{1,3},{2,0},{3,1},{4,6},{5,7},{6,4},{7,5},{8,10},{9,11},{10,... | collective-permute-start | bytes 98312 | tf_op jit(solution)/shard_map/ppermute | solution.py:67
  34.9 4.7 %collective-permute-start.20 = (f32[8,8,128]{2,1,0:T(8,128)S(1)}, f32[8,8,128]{2,1,0:T(8,128)S(1)}, u32[]{:S(2)}, u32[]{:S(2)}) collective-permute-start(f32[8,8,128]{2,1,0:T(8,128)S(1)} %get-tuple-element.188), channel_id=1, source_target_pairs={{0,4},{1,5},{2,6},{3,7},{4,0},{5,1},{6,2},{7,3},{8,12},{9,13},{10,... | collective-permute-start | bytes 98312 | tf_op jit(solution)/shard_map/ppermute | solution.py:67
  36.5 3.1 %collective-permute-start.17 = (f32[1,128]{1,0:T(1,128)S(1)}, f32[1,128]{1,0:T(1,128)S(1)}, u32[]{:S(2)}, u32[]{:S(2)}) collective-permute-start(f32[1,128]{1,0:T(1,128)S(1)} %get-tuple-element.183.own), channel_id=1, source_target_pairs={{0,16},{1,2},{2,1},{3,19},{4,20},{5,6},{6,5},{7,23},{8,24},{9,10},... | collective-permute-start | bytes 1544 | tf_op jit(solution)/shard_map/ppermute | solution.py:67
  39.8 3.8 %collective-permute-start.21 = (f32[128,256]{1,0:T(8,128)S(1)}, f32[128,256]{1,0:T(8,128)S(1)}, u32[]{:S(2)}, u32[]{:S(2)}) collective-permute-start(f32[128,256]{1,0:T(8,128)S(1)} %get-tuple-element.190), channel_id=1, source_target_pairs={{0,1},{1,0},{2,3},{3,2},{4,5},{5,4},{6,7},{7,6},{8,9},{9,8},{10,11... | collective-permute-start | bytes 393224 | tf_op jit(solution)/shard_map/ppermute | solution.py:67
  41.1 5.0 %collective-permute-start.22 = (f32[128,256]{1,0:T(8,128)S(1)}, f32[128,256]{1,0:T(8,128)S(1)}, u32[]{:S(2)}, u32[]{:S(2)}) collective-permute-start(f32[128,256]{1,0:T(8,128)S(1)} %get-tuple-element.192), channel_id=1, source_target_pairs={{0,16},{1,4},{2,18},{3,6},{4,1},{5,8},{6,3},{7,10},{8,5},{9,12},{1... | collective-permute-start | bytes 393224 | tf_op jit(solution)/shard_map/ppermute | solution.py:67
  41.6 3.4 %collective-permute-start.23 = (f32[32,256]{1,0:T(8,128)S(1)}, f32[32,256]{1,0:T(8,128)S(1)}, u32[]{:S(2)}, u32[]{:S(2)}) collective-permute-start(f32[32,256]{1,0:T(8,128)S(1)} %get-tuple-element.193), channel_id=1, source_target_pairs={{0,2},{1,3},{2,0},{3,1},{4,6},{5,7},{6,4},{7,5},{8,10},{9,11},{10,... | collective-permute-start | bytes 98312 | tf_op jit(solution)/shard_map/ppermute | solution.py:67
  42.4 3.7 %collective-permute-start.24 = (f32[8,8,128]{2,1,0:T(8,128)S(1)}, f32[8,8,128]{2,1,0:T(8,128)S(1)}, u32[]{:S(2)}, u32[]{:S(2)}) collective-permute-start(f32[8,8,128]{2,1,0:T(8,128)S(1)} %get-tuple-element.195), channel_id=1, source_target_pairs={{0,8},{1,9},{2,10},{3,11},{4,12},{5,13},{6,14},{7,15},{8,0},{9,1},... | collective-permute-start | bytes 98312 | tf_op jit(solution)/shard_map/ppermute | solution.py:67
  46.4 4.0 %collective-permute-start.25 = (f32[128,256]{1,0:T(8,128)S(1)}, f32[128,256]{1,0:T(8,128)S(1)}, u32[]{:S(2)}, u32[]{:S(2)}) collective-permute-start(f32[128,256]{1,0:T(8,128)S(1)} %get-tuple-element.197), channel_id=1, source_target_pairs={{0,1},{1,0},{2,3},{3,2},{4,5},{5,4},{6,7},{7,6},{8,9},{9,8},{10,11... | collective-permute-start | bytes 393224 | tf_op jit(solution)/shard_map/ppermute | solution.py:67
  48.2 4.7 %collective-permute-start.26 = (f32[128,256]{1,0:T(8,128)S(1)}, f32[128,256]{1,0:T(8,128)S(1)}, u32[]{:S(2)}, u32[]{:S(2)}) collective-permute-start(f32[128,256]{1,0:T(8,128)S(1)} %get-tuple-element.201), channel_id=1, source_target_pairs={{0,16},{1,4},{2,18},{3,6},{4,1},{5,8},{6,3},{7,10},{8,5},{9,12},{1... | collective-permute-start | bytes 393224 | tf_op jit(solution)/shard_map/ppermute | solution.py:67
  48.9 3.1 %collective-permute-start.27 = (f32[32,256]{1,0:T(8,128)S(1)}, f32[32,256]{1,0:T(8,128)S(1)}, u32[]{:S(2)}, u32[]{:S(2)}) collective-permute-start(f32[32,256]{1,0:T(8,128)S(1)} %get-tuple-element.202), channel_id=1, source_target_pairs={{0,2},{1,3},{2,0},{3,1},{4,6},{5,7},{6,4},{7,5},{8,10},{9,11},{10,... | collective-permute-start | bytes 98312 | tf_op jit(solution)/shard_map/ppermute | solution.py:67
  54.1 4.7 %collective-permute-start.29 = (f32[128,256]{1,0:T(8,128)S(1)}, f32[128,256]{1,0:T(8,128)S(1)}, u32[]{:S(2)}, u32[]{:S(2)}) collective-permute-start(f32[128,256]{1,0:T(8,128)S(1)} %get-tuple-element.209), channel_id=1, source_target_pairs={{0,16},{1,4},{2,18},{3,6},{4,1},{5,8},{6,3},{7,10},{8,5},{9,12},{1... | collective-permute-start | bytes 393224 | tf_op jit(solution)/shard_map/ppermute | solution.py:67
  54.3 3.1 %collective-permute-start.30 = (f32[32,256]{1,0:T(8,128)S(1)}, f32[32,256]{1,0:T(8,128)S(1)}, u32[]{:S(2)}, u32[]{:S(2)}) collective-permute-start(f32[32,256]{1,0:T(8,128)S(1)} %get-tuple-element.210), channel_id=1, source_target_pairs={{0,2},{1,3},{2,0},{3,1},{4,6},{5,7},{6,4},{7,5},{8,10},{9,11},{10,... | collective-permute-start | bytes 98312 | tf_op jit(solution)/shard_map/ppermute | solution.py:67
  59.4 4.7 %collective-permute-start.32 = (f32[128,256]{1,0:T(8,128)S(1)}, f32[128,256]{1,0:T(8,128)S(1)}, u32[]{:S(2)}, u32[]{:S(2)}) collective-permute-start(f32[128,256]{1,0:T(8,128)S(1)} %get-tuple-element.214), channel_id=1, source_target_pairs={{0,16},{1,4},{2,18},{3,6},{4,1},{5,8},{6,3},{7,10},{8,5},{9,12},{1... | collective-permute-start | bytes 393224 | tf_op jit(solution)/shard_map/ppermute | solution.py:67
  60.1 3.1 %collective-permute-start.33 = (f32[32,256]{1,0:T(8,128)S(1)}, f32[32,256]{1,0:T(8,128)S(1)}, u32[]{:S(2)}, u32[]{:S(2)}) collective-permute-start(f32[32,256]{1,0:T(8,128)S(1)} %get-tuple-element.215), channel_id=1, source_target_pairs={{0,2},{1,3},{2,0},{3,1},{4,6},{5,7},{6,4},{7,5},{8,10},{9,11},{10,... | collective-permute-start | bytes 98312 | tf_op jit(solution)/shard_map/ppermute | solution.py:67
  65.4 4.7 %collective-permute-start.35 = (f32[128,256]{1,0:T(8,128)S(1)}, f32[128,256]{1,0:T(8,128)S(1)}, u32[]{:S(2)}, u32[]{:S(2)}) collective-permute-start(f32[128,256]{1,0:T(8,128)S(1)} %get-tuple-element.223), channel_id=1, source_target_pairs={{0,16},{1,4},{2,18},{3,6},{4,1},{5,8},{6,3},{7,10},{8,5},{9,12},{1... | collective-permute-start | bytes 393224 | tf_op jit(solution)/shard_map/ppermute | solution.py:67
  66.1 3.1 %collective-permute-start.36 = (f32[32,256]{1,0:T(8,128)S(1)}, f32[32,256]{1,0:T(8,128)S(1)}, u32[]{:S(2)}, u32[]{:S(2)}) collective-permute-start(f32[32,256]{1,0:T(8,128)S(1)} %get-tuple-element.224), channel_id=1, source_target_pairs={{0,2},{1,3},{2,0},{3,1},{4,6},{5,7},{6,4},{7,5},{8,10},{9,11},{10,... | collective-permute-start | bytes 98312 | tf_op jit(solution)/shard_map/ppermute | solution.py:67
  70.8 4.7 %collective-permute-start.38 = (f32[128,256]{1,0:T(8,128)S(1)}, f32[128,256]{1,0:T(8,128)S(1)}, u32[]{:S(2)}, u32[]{:S(2)}) collective-permute-start(f32[128,256]{1,0:T(8,128)S(1)} %get-tuple-element.230), channel_id=1, source_target_pairs={{0,16},{1,4},{2,18},{3,6},{4,1},{5,8},{6,3},{7,10},{8,5},{9,12},{1... | collective-permute-start | bytes 393224 | tf_op jit(solution)/shard_map/ppermute | solution.py:67
  71.5 3.1 %collective-permute-start.39 = (f32[32,256]{1,0:T(8,128)S(1)}, f32[32,256]{1,0:T(8,128)S(1)}, u32[]{:S(2)}, u32[]{:S(2)}) collective-permute-start(f32[32,256]{1,0:T(8,128)S(1)} %get-tuple-element.231), channel_id=1, source_target_pairs={{0,2},{1,3},{2,0},{3,1},{4,6},{5,7},{6,4},{7,5},{8,10},{9,11},{10,... | collective-permute-start | bytes 98312 | tf_op jit(solution)/shard_map/ppermute | solution.py:67
  76.2 4.7 %collective-permute-start.41 = (f32[128,256]{1,0:T(8,128)S(1)}, f32[128,256]{1,0:T(8,128)S(1)}, u32[]{:S(2)}, u32[]{:S(2)}) collective-permute-start(f32[128,256]{1,0:T(8,128)S(1)} %get-tuple-element.237), channel_id=1, source_target_pairs={{0,16},{1,4},{2,18},{3,6},{4,1},{5,8},{6,3},{7,10},{8,5},{9,12},{1... | collective-permute-start | bytes 393224 | tf_op jit(solution)/shard_map/ppermute | solution.py:67
  76.9 3.1 %collective-permute-start.42 = (f32[32,256]{1,0:T(8,128)S(1)}, f32[32,256]{1,0:T(8,128)S(1)}, u32[]{:S(2)}, u32[]{:S(2)}) collective-permute-start(f32[32,256]{1,0:T(8,128)S(1)} %get-tuple-element.238), channel_id=1, source_target_pairs={{0,2},{1,3},{2,0},{3,1},{4,6},{5,7},{6,4},{7,5},{8,10},{9,11},{10,... | collective-permute-start | bytes 98312 | tf_op jit(solution)/shard_map/ppermute | solution.py:67
  81.6 4.7 %collective-permute-start.44 = (f32[128,256]{1,0:T(8,128)S(1)}, f32[128,256]{1,0:T(8,128)S(1)}, u32[]{:S(2)}, u32[]{:S(2)}) collective-permute-start(f32[128,256]{1,0:T(8,128)S(1)} %get-tuple-element.244), channel_id=1, source_target_pairs={{0,16},{1,4},{2,18},{3,6},{4,1},{5,8},{6,3},{7,10},{8,5},{9,12},{1... | collective-permute-start | bytes 393224 | tf_op jit(solution)/shard_map/ppermute | solution.py:67
  82.3 3.1 %collective-permute-start.45 = (f32[32,256]{1,0:T(8,128)S(1)}, f32[32,256]{1,0:T(8,128)S(1)}, u32[]{:S(2)}, u32[]{:S(2)}) collective-permute-start(f32[32,256]{1,0:T(8,128)S(1)} %get-tuple-element.245), channel_id=1, source_target_pairs={{0,2},{1,3},{2,0},{3,1},{4,6},{5,7},{6,4},{7,5},{8,10},{9,11},{10,... | collective-permute-start | bytes 98312 | tf_op jit(solution)/shard_map/ppermute | solution.py:67
  86.9 4.7 %collective-permute-start.47 = (f32[128,256]{1,0:T(8,128)S(1)}, f32[128,256]{1,0:T(8,128)S(1)}, u32[]{:S(2)}, u32[]{:S(2)}) collective-permute-start(f32[128,256]{1,0:T(8,128)S(1)} %get-tuple-element.251), channel_id=1, source_target_pairs={{0,16},{1,4},{2,18},{3,6},{4,1},{5,8},{6,3},{7,10},{8,5},{9,12},{1... | collective-permute-start | bytes 393224 | tf_op jit(solution)/shard_map/ppermute | solution.py:67
  87.6 3.1 %collective-permute-start.48 = (f32[32,256]{1,0:T(8,128)S(1)}, f32[32,256]{1,0:T(8,128)S(1)}, u32[]{:S(2)}, u32[]{:S(2)}) collective-permute-start(f32[32,256]{1,0:T(8,128)S(1)} %get-tuple-element.252), channel_id=1, source_target_pairs={{0,2},{1,3},{2,0},{3,1},{4,6},{5,7},{6,4},{7,5},{8,10},{9,11},{10,... | collective-permute-start | bytes 98312 | tf_op jit(solution)/shard_map/ppermute | solution.py:67
  92.3 4.7 %collective-permute-start.50 = (f32[128,256]{1,0:T(8,128)S(1)}, f32[128,256]{1,0:T(8,128)S(1)}, u32[]{:S(2)}, u32[]{:S(2)}) collective-permute-start(f32[128,256]{1,0:T(8,128)S(1)} %get-tuple-element.258), channel_id=1, source_target_pairs={{0,16},{1,4},{2,18},{3,6},{4,1},{5,8},{6,3},{7,10},{8,5},{9,12},{1... | collective-permute-start | bytes 393224 | tf_op jit(solution)/shard_map/ppermute | solution.py:67
  93.0 3.1 %collective-permute-start.51 = (f32[32,256]{1,0:T(8,128)S(1)}, f32[32,256]{1,0:T(8,128)S(1)}, u32[]{:S(2)}, u32[]{:S(2)}) collective-permute-start(f32[32,256]{1,0:T(8,128)S(1)} %get-tuple-element.259), channel_id=1, source_target_pairs={{0,2},{1,3},{2,0},{3,1},{4,6},{5,7},{6,4},{7,5},{8,10},{9,11},{10,... | collective-permute-start | bytes 98312 | tf_op jit(solution)/shard_map/ppermute | solution.py:67
  97.7 4.7 %collective-permute-start.53 = (f32[128,256]{1,0:T(8,128)S(1)}, f32[128,256]{1,0:T(8,128)S(1)}, u32[]{:S(2)}, u32[]{:S(2)}) collective-permute-start(f32[128,256]{1,0:T(8,128)S(1)} %get-tuple-element.265), channel_id=1, source_target_pairs={{0,16},{1,4},{2,18},{3,6},{4,1},{5,8},{6,3},{7,10},{8,5},{9,12},{1... | collective-permute-start | bytes 393224 | tf_op jit(solution)/shard_map/ppermute | solution.py:67
  102.9 10.7 %collective-permute-start.57 = (f32[2,256,256]{2,1,0:T(8,128)S(1)}, f32[2,256,256]{2,1,0:T(8,128)S(1)}, u32[]{:S(2)}, u32[]{:S(2)}) collective-permute-start(f32[2,256,256]{2,1,0:T(8,128)S(1)} %get-tuple-element.272.own), channel_id=1, source_target_pairs={{0,16},{1,2},{2,1},{3,19},{4,20},{5,6},{6,5},{7,23},{8,24},{9,10},... | collective-permute-start | bytes 1572872 | tf_op jit(solution)/shard_map/ppermute | solution.py:67
  105.4 9.0 %collective-permute-start.56 = (f32[2,64,128]{2,1,0:T(8,128)S(1)}, f32[2,64,128]{2,1,0:T(8,128)S(1)}, u32[]{:S(2)}, u32[]{:S(2)}) collective-permute-start(f32[2,64,128]{2,1,0:T(8,128)S(1)} %get-tuple-element.271), channel_id=1, source_target_pairs={{0,0},{1,2},{2,1},{3,3},{4,4},{5,6},{6,5},{7,7},{8,8},{9,10},{10,9... | collective-permute-start | bytes 196616 | tf_op jit(solution)/shard_map/ppermute | solution.py:67
  108.0 6.4 %collective-permute-start.58 = (f32[2,64,128]{2,1,0:T(8,128)S(1)}, f32[2,64,128]{2,1,0:T(8,128)S(1)}, u32[]{:S(2)}, u32[]{:S(2)}) collective-permute-start(f32[2,64,128]{2,1,0:T(8,128)S(1)} %get-tuple-element.275), channel_id=1, source_target_pairs={{0,4},{1,6},{2,5},{3,7},{4,0},{5,2},{6,1},{7,3},{8,12},{9,14},{10,... | collective-permute-start | bytes 196616 | tf_op jit(solution)/shard_map/ppermute | solution.py:67
  109.5 6.2 %collective-permute-start.59 = (f32[2,64,128]{2,1,0:T(8,128)S(1)}, f32[2,64,128]{2,1,0:T(8,128)S(1)}, u32[]{:S(2)}, u32[]{:S(2)}) collective-permute-start(f32[2,64,128]{2,1,0:T(8,128)S(1)} %get-tuple-element.276), channel_id=1, source_target_pairs={{0,8},{1,10},{2,9},{3,11},{4,12},{5,14},{6,13},{7,15},{8,0},{9,2},... | collective-permute-start | bytes 196616 | tf_op jit(solution)/shard_map/ppermute | solution.py:67
  110.4 6.5 %collective-permute-start.60 = (f32[2,64,128]{2,1,0:T(8,128)S(1)}, f32[2,64,128]{2,1,0:T(8,128)S(1)}, u32[]{:S(2)}, u32[]{:S(2)}) collective-permute-start(f32[2,64,128]{2,1,0:T(8,128)S(1)} %get-tuple-element.277), channel_id=1, source_target_pairs={{0,12},{1,14},{2,13},{3,15},{4,8},{5,10},{6,9},{7,11},{8,4},{9,6},... | collective-permute-start | bytes 196616 | tf_op jit(solution)/shard_map/ppermute | solution.py:67
  (31 other events, 75.0 us)

commit v14 on v13

--- a/solution.py
+++ b/solution.py
@@ -160,7 +160,7 @@
     blank = jnp.zeros((16, depth), BF16)
     ext = [[jnp.concatenate([blank, part[h * half : h * half + half], blank], axis=0)
             for h in range(2)] for part in own]
-    from_c = split(cm[...])
+    from_c = split(cm[0:half])
     step = GROUP * 4
     for n in range(half // step):
         rhs = [part[h][n * step : n * step + step + 32] for part in ext for h in range(2)]
@@ -181,7 +181,7 @@
 
 def edge_differences(flags, size, ym, edge):
     ym = ym.at[0] if len(ym.shape) == 3 else ym
-    out = mm(edge[...], jnp.concatenate(split(ym[...]), axis=0))
+    out = mm(edge[...], jnp.concatenate(split(ym[0:32]), axis=0))
     start = jnp.where(flags[1] == 1, 0, size // 2 - 16)
     for h in range(2):
         at = pl.ds(pl.multiple_of(start + h * (size // 2), 16), 16)
@@ -277,7 +277,7 @@
 
 
 def first_outer_kernel(flags, cur, prev, vel, ri, rx, rz, sums, di, dx, dz, inj, zm, ym, side,
-                       edge, new, zo, co, yo, k0, ki, kx, kz):
+                       edge, give, cells, new, zo, co, yo, k0, ki, kx, kz):
     size = cur.shape[0]
     half = size // 2
     kz[...], ki[...], kx[...] = sums[...], di[...], dx[...]
@@ -303,7 +303,8 @@
         k0[here], ki[here], kx[here], kz[here] = factor, along_i, along_x, along_z
         center = cur[here]
         new[here] = (center - prev[here]) + (center + (change + inj[here]))
-    rims(flags, new, zo, co, yo)
+    rims(flags, new, zo, co.at[pl.ds(0, half)], yo)
+    load(co, half, lambda n: give[n], give.shape[0], [cells[...]])
 
 
 def inner(cur, prev, k0, ki, kx, kz, cm, near, deep, inj, out):
@@ -336,10 +337,40 @@
 def trade(stage, flags, mine, got, out, give=None):
     out[...] = mine[...]
     for n, at in other_half(stage, flags, out.shape[0]):
-        out[at] = got[n]
+        out[at] = got(n) if callable(got) else got[n]
     if give is not None:
         for n, at in other_half(stage + 1, flags, out.shape[0]):
             give[n] = out[at]
+
+
+def load(message, rim, entry, count, cells):
+    for n in range(count):
+        message[rim + n // 2 * 8 : rim + n // 2 * 8 + 8, n % 2 * 128 : n % 2 * 128 + 128] = entry(n)
+    at = rim + count // 2 * 8
+    wide = message.shape[1]
+    for k, row in enumerate(cells):
+        for m in range(row.shape[1] // 128):
+            lane = k * row.shape[1] + m * 128
+            message[at + lane // wide : at + lane // wide + 1, lane % wide : lane % wide + 128] = (
+                row[:, m * 128 : m * 128 + 128])
+
+
+def unload(message, rim, count, rows, slots):
+    wide = message.shape[1]
+    at = rim + count // 2 * 8
+
+    def entry(n):
+        return message[rim + n // 2 * 8 : rim + n // 2 * 8 + 8, n % 2 * 128 : n % 2 * 128 + 128]
+
+    cells = []
+    for k in range(rows):
+        tiles = []
+        for m in range(slots // 128):
+            lane = k * slots + m * 128
+            tiles.append(message[at + lane // wide : at + lane // wide + 1,
+                                 lane % wide : lane % wide + 128])
+        cells.append(jnp.concatenate(tiles, axis=1) if len(tiles) > 1 else tiles[0])
+    return entry, cells
 
 
 def trade_kernel(stage, flags, mine, got, *outs):
@@ -380,20 +411,14 @@
     change[...] = (cur[...] - prev[...]) - (prev[...] - before[...])
 
 
-def outer_kernel(stage, double, flags, part, k0, ki, kx, zm, ym, side, edge, *rest):
-    rest = list(rest)
-    other = rest.pop(0) if double else None
+def outer_kernel(stage, flags, part, k0, ki, kx, zm, ym, side, edge, *rest):
     if stage is not None:
         mine, got, new, zo, co, yo, *lists = rest
         trade(stage, flags, mine, got, *lists)
     else:
         new, zo, co, yo = rest
     outer(flags, part, k0, ki, kx, zm, ym, side, edge, new)
-    if double:
-        for n, field in enumerate((new, other)):
-            rims(flags, field, zo.at[n], co.at[n], yo.at[n])
-    else:
-        rims(flags, new, zo, co, yo)
+    rims(flags, new, zo, co, yo)
 
 
 def pack_kernel(flags, counts, cells, traces, cells_out, lists, give, counts_v, cells_v, traces_v,
@@ -420,11 +445,38 @@
         give[n] = lists[at]
 
 
-def lists_kernel(flags, lists, own, got, spot, pick, at, obs):
+def core_stage_kernel(flags, part, k0, ki, kx, zm, ym, side, edge, lists, cells, cm, new, zo, co, yo,
+                      lists_out, pair):
+    outer(flags, part, k0, ki, kx, zm, ym, side, edge, new)
+    count, half = lists.shape[0] // 2, new.shape[0] // 2
+    entry, (theirs,) = unload(cm, half, count, 1, cells.shape[1])
+    trade(0, flags, lists, entry, lists_out)
+    mine = cells[...]
+    pair[0:1] = jnp.where(flags[0] == 0, mine, theirs)
+    pair[1:2] = jnp.where(flags[0] == 0, theirs, mine)
+    rims(flags, new, zo, co, yo.at[pl.ds(0, 32)])
+    at = [k for n, k in other_half(1, flags, lists.shape[0])]
+    load(yo, 32, lambda n: lists_out[at[n]], count, [pair[0:1], pair[1:2]])
+
+
+def y_stage_kernel(flags, part, k0, ki, kx, zm, ym, side, edge, lists, pair, other, new, zo, co, yo,
+                   lists_out, give, cells):
+    outer(flags, part, k0, ki, kx, zm, ym, side, edge, new)
+    for n, field in enumerate((new, other)):
+        rims(flags, field, zo.at[n], co.at[n], yo.at[n])
+    entry, theirs = unload(ym, 32, lists.shape[0] // 2, 2, pair.shape[1])
+    trade(1, flags, lists, entry, lists_out, give)
+    away = flags[0] != flags[1]
+    low = jnp.where(away, theirs[0], pair[0:1])
+    high = jnp.where(away, theirs[1], pair[1:2])
+    cells[...] = jnp.where(flags[1] == 0, low, high)
+
+
+def lists_kernel(flags, lists, cells, spot, pick, at, obs):
     size, n = spot.shape
     depth = at.shape[1]
     subs, steps = lists.shape[0], obs.shape[1]
-    cell = jnp.where(flags[0] == flags[1], own[...], got[...])
+    cell = cells[...]
     along = jnp.floor((cell + 0.5) * (1.0 / depth))
     place = along.astype(jnp.int32)
     place = jnp.where(place < 0, -1, place_of(
@@ -621,26 +673,28 @@
                  near, deep, weight=1.3)
     got_adjoint = [send(after(v, parts[0]), swap_perm) for v in (adj_now, adj_before)]
 
+    slots = subs * CAP
+    entries, half_entries = shaped(subs, steps, 128), shaped(subs // 2, steps, 128)
+    cells, lists, give = call(
+        pack_kernel, "pack", [shaped(1, slots), entries, half_entries], after(rec_counts, density),
+        rec_cells, observed, weight=0.2, far=3,
+        scratch=[pltpu.VMEM(rec_counts.shape, jnp.int32), pltpu.VMEM(rec_cells.shape, jnp.int32),
+                 pltpu.VMEM(observed.shape, F32)])
+    riders = subs // 4 * 8 + 8
+    core_rim = shaped(size // 2 + riders, depth)
+    y_rim = shaped(4 * cols + riders, depth)
+
     new, zo, co, yo, k0, ki, kx, kz = call(
-        first_outer_kernel, "first_outer", [field] + rim + [field] * 4,
-        p_now, p_before, vel, *parts, inj, zm, ym, side, edge)
+        first_outer_kernel, "first_outer", [field, rim[0], core_rim, rim[2]] + [field] * 4,
+        p_now, p_before, vel, *parts, inj, zm, ym, side, edge, give, cells)
     model = (k0, ki, kx, kz)
     states = [p_before, p_now, new]
     changes = []
     zm, cm, ym = halo(zo, co, yo)
-    double = 1
-    late = steps - 2 if len(stages) < steps - 2 else steps - 1
-
-    slots = subs * CAP
-    entries, half_entries = shaped(subs, steps, 128), shaped(subs // 2, steps, 128)
-    cells, lists, give = call(
-        pack_kernel, "pack", [shaped(1, slots), entries, half_entries], after(rec_counts, k0),
-        rec_cells, observed, weight=0.8, far=3,
-        scratch=[pltpu.VMEM(rec_counts.shape, jnp.int32), pltpu.VMEM(rec_cells.shape, jnp.int32),
-                 pltpu.VMEM(observed.shape, F32)])
+    late = steps - 2 if len(stages) < steps - 1 else steps - 1
     for t in range(1, steps):
         cur, prev, before = states[:-4:-1]
-        stage = t - 1 if t <= min(len(stages), steps - 2) else None
+        stage = t - 1 if 2 < t <= min(len(stages), steps - 2) else None
         extra = [lists, send(give, stages[stage][0])] if stage is not None else []
         part, change = call(
             functools.partial(forward_inner_kernel, t, full), "forward_inner", [field, field], src_cell, wavelet, cur, prev, *model, cm, near, deep, before, weight=1.2, scalars=2)
@@ -661,7 +715,7 @@
                 lists_kernel, "lists",
                 [jax.ShapeDtypeStruct((size, slots), BF16),
                  jax.ShapeDtypeStruct((slots, size), BF16), shaped(slots, depth),
-                 shaped(slots, steps)], lists, cells, got_cells, weight=0.8)
+                 shaped(slots, steps)], lists, cells, weight=0.3)
             args[0] = after(part, receivers[0])
         if t == steps - 1:
             new, u_new, *out = call(
@@ -669,25 +723,35 @@
                 u_zm, u_ym, *receivers)
             states.append(new)
             break
-        if t == len(stages) - 2:
-            got_cells = send(after(cells, part), swap_perm)
-        if t == len(stages) - 1:
-            args[0] = after(part, got_cells)
-        if t == double:
-            u_now, u_before = call(settle_pair_kernel, "settle_adjoint", [field, field], adj_now, adj_before, *got_adjoint, weight=0.6, far=2)
-            args.append(u_now)
-        outs = [field] + ([shaped(2, *r.shape) for r in rim] if t == double else rim)
+        if t == 1:
+            new, *out, lists, pair = call(
+                core_stage_kernel, "forward_outer",
+                [field, rim[0], rim[1], y_rim, entries, shaped(2, slots)], *args, lists, cells, cm)
+            states.append(new)
+            zm, cm, ym = halo(*out)
+            continue
+        if t == 2:
+            u_now, u_before = call(settle_pair_kernel, "settle_adjoint", [field, field], adj_now,
+                                   adj_before, *got_adjoint, weight=0.3, far=2)
+            new, *out, lists, give, cells = call(
+                y_stage_kernel, "forward_outer",
+                [field] + [shaped(2, *r.shape) for r in rim] + [entries, half_entries,
+                                                                shaped(1, slots)],
+                *args, lists, pair, u_now)
+            states.append(new)
+            zm, cm, ym = halo(*out)
+            u_zm, u_cm, u_ym = zm, cm, ym
+            continue
+        outs = [field] + rim
         if extra:
             outs = outs + [entries] + ([half_entries] if t < len(stages) else [])
-        new, *out = call(functools.partial(outer_kernel, stage, t == double), "forward_outer", outs,
+        new, *out = call(functools.partial(outer_kernel, stage), "forward_outer", outs,
                          *args, *extra)
         if extra:
             out, (lists, *give) = out[:3], out[3:]
             give = give[0] if give else None
         states.append(new)
         zm, cm, ym = halo(*out)
-        if t == double:
-            u_zm, u_cm, u_ym = zm, cm, ym
 
     zm, cm, ym = halo(*out)
     u_before, u_now = u_now, u_new
@@ -706,7 +770,7 @@
                 [shaped(2, *field.shape), half, half], *args, *image, changes[0], vel, u_now)
             break
         u_before = u_now
-        u_now, *out = call(functools.partial(outer_kernel, None, False), "adjoint_outer", [field] + rim,
+        u_now, *out = call(functools.partial(outer_kernel, None), "adjoint_outer", [field] + rim,
                            *args)
         zm, cm, ym = halo(*out)
 

time: 118 us -> 124 us (1.051)
  starting transfers between devices: 56.1 us -> 62 us
  waiting for transfers between devices: 31.8 us -> 29.3 us
  local copies, waits for them, and re-layouts: 1.66 us -> 3.08 us
    ppermute x61 -> x58, starting transfers between devices: 56.1 us -> 62 us  [send(): return lax.ppermute(value, ALL, pairs)]
    ppermute x61 -> x58, waiting for transfers between devices: 31.8 us -> 29.3 us  [send(): return lax.ppermute(value, ALL, pairs)]
    unnamed x36, local copies, waits for them, and re-layouts: 1.66 us -> 3.08 us
  transfers between devices with their start and end apart: 61 -> 58, of which waited for: 30 -> 29; matrix products, arithmetic and copies ran while one was open for 1% -> 1% of each run, Pallas kernels for 18% -> 17%
where the time goes in v14:
time: 124 us; the launch traced here: 123 us
  starting transfers between devices  62 us (50%)
  waiting for transfers between devices  29.3 us (24%)
  Pallas kernels  26.6 us (21%)
  local copies, waits for them, and re-layouts  3.08 us (2%)
  other arithmetic  1.24 us (1%)
    ppermute x58, starting transfers between devices, send(): return lax.ppermute(value, ALL, pairs)  62 us
    ppermute x58, waiting for transfers between devices, send(): return lax.ppermute(value, ALL, pairs)  29.3 us
    pallas_call x40, Pallas kernels, call(): pl.pallas_call(functools.partial(kernel, Flags()), name=name, out_shape=o...  26.6 us
    unnamed x36, local copies, waits for them, and re-layouts  3.08 us
  transfers between devices with their start and end apart: 58, of which 29 were waited for; matrix products, arithmetic and copies ran while one was open for 1% of the time, Pallas kernels for 17%

profile of v14, /device:TPU:1, one launch (start us, length us, event | category | flops | bytes accessed | tf_op | source)
XLA Modules:
  0.0 123.4 jit_solution(9444043861201920258)
XLA Ops:
  0.6 2.7 %collective-permute-start.1 = (f32[256,256]{1,0:T(8,128)}, f32[256,256]{1,0:T(8,128)S(1)}, u32[]{:S(2)}, u32[]{:S(2)}) collective-permute-start(f32[256,256]{1,0:T(8,128)} %bitcast.16), channel_id=1, source_target_pairs={{0,16},{1,2},{2,1},{3,19},{4,20},{5,6},{6,5},{7,23},{8,24},{9,10},... | collective-permute-start | bytes 786440 | tf_op jit(solution)/shard_map/ppermute | solution.py:67
  3.4 1.1 pad_maximum_fusion
  4.5 1.7 %collective-permute-start.2 = (f32[2,256,256]{2,1,0:T(8,128)S(1)}, f32[2,256,256]{2,1,0:T(8,128)S(1)}, u32[]{:S(2)}, u32[]{:S(2)}) collective-permute-start(f32[2,256,256]{2,1,0:T(8,128)S(1)} %pad_maximum_fusion), channel_id=1, source_target_pairs={{0,16},{1,2},{2,1},{3,19},{4,20},{5,6},{6,5},{7,23},{8,24},{9,10},... | collective-permute-start | bytes 1572872 | tf_op jit(solution)/shard_map/ppermute | solution.py:67
  8.8 1.9 %collective-permute-done.recv_a = f32[256,256]{1,0:T(8,128)S(1)} collective-permute-done((f32[256,256]{1,0:T(8,128)}, f32[256,256]{1,0:T(8,128)S(1)}, u32[]{:S(2)}, u32[]{:S(2)}) %collective-permute-start) | collective-permute-done | bytes 262176 | tf_op jit(solution)/shard_map/ppermute | solution.py:67
  11.4 1.8 %collective-permute-start.4 = (f32[2,128,256]{2,1,0:T(8,128)S(1)}, f32[2,128,256]{2,1,0:T(8,128)S(1)}, u32[]{:S(2)}, u32[]{:S(2)}) collective-permute-start(f32[2,128,256]{2,1,0:T(8,128)S(1)} %get-tuple-element.154), channel_id=1, source_target_pairs={{0,16},{1,4},{2,18},{3,6},{4,1},{5,8},{6,3},{7,10},{8,5},{9,12},{1... | collective-permute-start | bytes 786440 | tf_op jit(solution)/shard_map/ppermute | solution.py:67
  14.8 1.7 %collective-permute-done.2.rest_0_ = f32[2,256,256]{2,1,0:T(8,128)S(1)} collective-permute-done((f32[2,256,256]{2,1,0:T(8,128)S(1)}, f32[2,256,256]{2,1,0:T(8,128)S(1)}, u32[]{:S(2)}, u32[]{:S(2)}) %collective-permute-start.2) | collective-permute-done | bytes 524320 | tf_op jit(solution)/shard_map/ppermute | solution.py:67
  19.0 1.1 collective-permute-start.6
  20.9 1.6 %collective-permute-start.12 = (f32[256,256]{1,0:T(8,128)S(1)}, f32[256,256]{1,0:T(8,128)S(1)}, u32[]{:S(2)}, u32[]{:S(2)}) collective-permute-start(f32[256,256]{1,0:T(8,128)S(1)} %bitcast.18), channel_id=1, source_target_pairs={{0,16},{1,2},{2,1},{3,19},{4,20},{5,6},{6,5},{7,23},{8,24},{9,10},... | collective-permute-start | bytes 786440 | tf_op jit(solution)/shard_map/ppermute | solution.py:67
  22.7 1.1 collective-permute-start.8
  23.8 1.4 %forward_inner.7 = (f32[256,256]{1,0:T(8,128)S(1)}, f32[256,256]{1,0:T(8,128)S(1)}) custom-call(s32[16]{0:T(128)S(1)} %copy-done.8, f32[8,16]{1,0:T(8,128)S(1)} %copy-done.3, f32[256,256]{1,0:T(8,128)S(1)} %get-tuple-element.159.cur.prev.before.state, f32[256,256]{1,0:T(8,128)S(1)} %get-tuple-element.141.cur.prev.before, ...), custom_call_target="tpu_custom_call" | custom-call | flops 1000 | bytes 4321000 | tf_op jit(solution)/shard_map/forward_inner/pallas_call | solution.py:604
  25.2 4.2 %collective-permute-done.8.ym = f32[32,256]{1,0:T(8,128)S(1)} collective-permute-done((f32[32,256]{1,0:T(8,128)S(1)}, f32[32,256]{1,0:T(8,128)S(1)}, u32[]{:S(2)}, u32[]{:S(2)}) %collective-permute-start.8) | collective-permute-done | bytes 32800 | tf_op jit(solution)/shard_map/ppermute | solution.py:67
  29.6 1.7 %collective-permute-start.9 = (f32[128,256]{1,0:T(8,128)S(1)}, f32[128,256]{1,0:T(8,128)S(1)}, u32[]{:S(2)}, u32[]{:S(2)}) collective-permute-start(f32[128,256]{1,0:T(8,128)S(1)} %get-tuple-element.170), channel_id=1, source_target_pairs={{0,1},{1,0},{2,3},{3,2},{4,5},{5,4},{6,7},{7,6},{8,9},{9,8},{10,11... | collective-permute-start | bytes 393224 | tf_op jit(solution)/shard_map/ppermute | solution.py:67
  31.2 1.3 %collective-permute-start.10 = (f32[128,256]{1,0:T(8,128)S(1)}, f32[128,256]{1,0:T(8,128)S(1)}, u32[]{:S(2)}, u32[]{:S(2)}) collective-permute-start(f32[128,256]{1,0:T(8,128)S(1)} %get-tuple-element.172), channel_id=1, source_target_pairs={{0,16},{1,4},{2,18},{3,6},{4,1},{5,8},{6,3},{7,10},{8,5},{9,12},{1... | collective-permute-start | bytes 393224 | tf_op jit(solution)/shard_map/ppermute | solution.py:67
  32.8 1.4 %forward_inner.8 = (f32[256,256]{1,0:T(8,128)S(1)}, f32[256,256]{1,0:T(8,128)S(1)}) custom-call(s32[16]{0:T(128)S(1)} %copy-done.8, f32[8,16]{1,0:T(8,128)S(1)} %copy-done.3, f32[256,256]{1,0:T(8,128)S(1)} %get-tuple-element.169.cur.prev.before.state, f32[256,256]{1,0:T(8,128)S(1)} %get-tuple-element.159.cur.prev.before.state, ...), custom_call_target="tpu_custom_call" | custom-call | flops 1000 | bytes 4321000 | tf_op jit(solution)/shard_map/forward_inner/pallas_call | solution.py:604
  34.2 1.8 %collective-permute-done.11.ym = f32[72,256]{1,0:T(8,128)S(1)} collective-permute-done((f32[72,256]{1,0:T(8,128)S(1)}, f32[72,256]{1,0:T(8,128)S(1)}, u32[]{:S(2)}, u32[]{:S(2)}) %collective-permute-start.11) | collective-permute-done | bytes 73760 | tf_op jit(solution)/shard_map/ppermute | solution.py:67
  36.3 1.2 collective-permute-start.14
  37.5 2.4 %collective-permute-start.15 = (f32[2,128,256]{2,1,0:T(8,128)S(1)}, f32[2,128,256]{2,1,0:T(8,128)S(1)}, u32[]{:S(2)}, u32[]{:S(2)}) collective-permute-start(f32[2,128,256]{2,1,0:T(8,128)S(1)} %get-tuple-element.182), channel_id=1, source_target_pairs={{0,16},{1,4},{2,18},{3,6},{4,1},{5,8},{6,3},{7,10},{8,5},{9,12},{1... | collective-permute-start | bytes 786440 | tf_op jit(solution)/shard_map/ppermute | solution.py:67
  39.8 1.4 %collective-permute-start.17 = (f32[8,8,128]{2,1,0:T(8,128)S(1)}, f32[8,8,128]{2,1,0:T(8,128)S(1)}, u32[]{:S(2)}, u32[]{:S(2)}) collective-permute-start(f32[8,8,128]{2,1,0:T(8,128)S(1)} %get-tuple-element.185), channel_id=1, source_target_pairs={{0,4},{1,5},{2,6},{3,7},{4,0},{5,1},{6,2},{7,3},{8,12},{9,13},{10,... | collective-permute-start | bytes 98312 | tf_op jit(solution)/shard_map/ppermute | solution.py:67
  41.3 1.4 %forward_inner.9 = (f32[256,256]{1,0:T(8,128)S(1)}, f32[256,256]{1,0:T(8,128)S(1)}) custom-call(s32[16]{0:T(128)S(1)} %copy-done.8, f32[8,16]{1,0:T(8,128)S(1)} %copy-done.3, f32[256,256]{1,0:T(8,128)S(1)} %get-tuple-element.179.cur.prev.before.state, f32[256,256]{1,0:T(8,128)S(1)} %get-tuple-element.169.cur.prev.before.state, ...), custom_call_target="tpu_custom_call" | custom-call | flops 1000 | bytes 4321000 | tf_op jit(solution)/shard_map/forward_inner/pallas_call | solution.py:604
  42.7 1.2 collective-permute-done.17.rest_1_
  44.5 1.1 collective-permute-start.18
  46.5 2.5 %collective-permute-start.21 = (f32[8,8,128]{2,1,0:T(8,128)S(1)}, f32[8,8,128]{2,1,0:T(8,128)S(1)}, u32[]{:S(2)}, u32[]{:S(2)}) collective-permute-start(f32[8,8,128]{2,1,0:T(8,128)S(1)} %get-tuple-element.192), channel_id=1, source_target_pairs={{0,8},{1,9},{2,10},{3,11},{4,12},{5,13},{6,14},{7,15},{8,0},{9,1},... | collective-permute-start | bytes 98312 | tf_op jit(solution)/shard_map/ppermute | solution.py:67
  49.0 1.4 %forward_inner.10 = (f32[256,256]{1,0:T(8,128)S(1)}, f32[256,256]{1,0:T(8,128)S(1)}) custom-call(s32[16]{0:T(128)S(1)} %copy-done.8, f32[8,16]{1,0:T(8,128)S(1)} %copy-done.3, f32[256,256]{1,0:T(8,128)S(1)} %get-tuple-element.186.cur.prev.before.state, f32[256,256]{1,0:T(8,128)S(1)} %get-tuple-element.179.cur.prev.before.state, ...), custom_call_target="tpu_custom_call" | custom-call | flops 1000 | bytes 4321000 | tf_op jit(solution)/shard_map/forward_inner/pallas_call | solution.py:604
  50.8 1.7 %collective-permute-start.22 = (f32[128,256]{1,0:T(8,128)S(1)}, f32[128,256]{1,0:T(8,128)S(1)}, u32[]{:S(2)}, u32[]{:S(2)}) collective-permute-start(f32[128,256]{1,0:T(8,128)S(1)} %get-tuple-element.194), channel_id=1, source_target_pairs={{0,1},{1,0},{2,3},{3,2},{4,5},{5,4},{6,7},{7,6},{8,9},{9,8},{10,11... | collective-permute-start | bytes 393224 | tf_op jit(solution)/shard_map/ppermute | solution.py:67
  52.6 1.7 %collective-permute-start.23 = (f32[128,256]{1,0:T(8,128)S(1)}, f32[128,256]{1,0:T(8,128)S(1)}, u32[]{:S(2)}, u32[]{:S(2)}) collective-permute-start(f32[128,256]{1,0:T(8,128)S(1)} %get-tuple-element.198), channel_id=1, source_target_pairs={{0,16},{1,4},{2,18},{3,6},{4,1},{5,8},{6,3},{7,10},{8,5},{9,12},{1... | collective-permute-start | bytes 393224 | tf_op jit(solution)/shard_map/ppermute | solution.py:67
  55.3 1.4 %forward_inner.11 = (f32[256,256]{1,0:T(8,128)S(1)}, f32[256,256]{1,0:T(8,128)S(1)}) custom-call(s32[16]{0:T(128)S(1)} %copy-done.8, f32[8,16]{1,0:T(8,128)S(1)} %copy-done.3, f32[256,256]{1,0:T(8,128)S(1)} %get-tuple-element.193.cur.prev.before.state, f32[256,256]{1,0:T(8,128)S(1)} %get-tuple-element.186.cur.prev.before.state, ...), custom_call_target="tpu_custom_call" | custom-call | flops 1000 | bytes 4321000 | tf_op jit(solution)/shard_map/forward_inner/pallas_call | solution.py:604
  57.4 1.1 collective-permute-start.25
  59.4 1.3 %collective-permute-start.27 = (f32[32,256]{1,0:T(8,128)S(1)}, f32[32,256]{1,0:T(8,128)S(1)}, u32[]{:S(2)}, u32[]{:S(2)}) collective-permute-start(f32[32,256]{1,0:T(8,128)S(1)} %get-tuple-element.208), channel_id=1, source_target_pairs={{0,2},{1,3},{2,0},{3,1},{4,6},{5,7},{6,4},{7,5},{8,10},{9,11},{10,... | collective-permute-start | bytes 98312 | tf_op jit(solution)/shard_map/ppermute | solution.py:67
  61.0 1.4 %forward_inner.12 = (f32[256,256]{1,0:T(8,128)S(1)}, f32[256,256]{1,0:T(8,128)S(1)}) custom-call(s32[16]{0:T(128)S(1)} %copy-done.8, f32[8,16]{1,0:T(8,128)S(1)} %copy-done.3, f32[256,256]{1,0:T(8,128)S(1)} %get-tuple-element.200.cur.prev.rest_2_.state, f32[256,256]{1,0:T(8,128)S(1)} %get-tuple-element.193.cur.prev.before.state, ...), custom_call_target="tpu_custom_call" | custom-call | flops 1000 | bytes 4321000 | tf_op jit(solution)/shard_map/forward_inner/pallas_call | solution.py:604
  64.5 1.6 %collective-permute-start.30 = (f32[32,256]{1,0:T(8,128)S(1)}, f32[32,256]{1,0:T(8,128)S(1)}, u32[]{:S(2)}, u32[]{:S(2)}) collective-permute-start(f32[32,256]{1,0:T(8,128)S(1)} %get-tuple-element.213), channel_id=1, source_target_pairs={{0,2},{1,3},{2,0},{3,1},{4,6},{5,7},{6,4},{7,5},{8,10},{9,11},{10,... | collective-permute-start | bytes 98312 | tf_op jit(solution)/shard_map/ppermute | solution.py:67
  66.1 1.4 %forward_inner.13 = (f32[256,256]{1,0:T(8,128)S(1)}, f32[256,256]{1,0:T(8,128)S(1)}) custom-call(s32[16]{0:T(128)S(1)} %copy-done.8, f32[8,16]{1,0:T(8,128)S(1)} %copy-done.3, f32[256,256]{1,0:T(8,128)S(1)} %get-tuple-element.209.cur.state.rest_1_, f32[256,256]{1,0:T(8,128)S(1)} %get-tuple-element.200.cur.prev.rest_2_.state, ...), custom_call_target="tpu_custom_call" | custom-call | flops 1000 | bytes 4321000 | tf_op jit(solution)/shard_map/forward_inner/pallas_call | solution.py:604
  70.6 1.5 %collective-permute-start.33 = (f32[32,256]{1,0:T(8,128)S(1)}, f32[32,256]{1,0:T(8,128)S(1)}, u32[]{:S(2)}, u32[]{:S(2)}) collective-permute-start(f32[32,256]{1,0:T(8,128)S(1)} %get-tuple-element.222), channel_id=1, source_target_pairs={{0,2},{1,3},{2,0},{3,1},{4,6},{5,7},{6,4},{7,5},{8,10},{9,11},{10,... | collective-permute-start | bytes 98312 | tf_op jit(solution)/shard_map/ppermute | solution.py:67
  72.1 1.0 adjoint_inner.7
  73.7 1.1 collective-permute-done.32.zm
  76.2 1.3 %collective-permute-start.36 = (f32[32,256]{1,0:T(8,128)S(1)}, f32[32,256]{1,0:T(8,128)S(1)}, u32[]{:S(2)}, u32[]{:S(2)}) collective-permute-start(f32[32,256]{1,0:T(8,128)S(1)} %get-tuple-element.229), channel_id=1, source_target_pairs={{0,2},{1,3},{2,0},{3,1},{4,6},{5,7},{6,4},{7,5},{8,10},{9,11},{10,... | collective-permute-start | bytes 98312 | tf_op jit(solution)/shard_map/ppermute | solution.py:67
  81.6 1.3 %collective-permute-start.39 = (f32[32,256]{1,0:T(8,128)S(1)}, f32[32,256]{1,0:T(8,128)S(1)}, u32[]{:S(2)}, u32[]{:S(2)}) collective-permute-start(f32[32,256]{1,0:T(8,128)S(1)} %get-tuple-element.236), channel_id=1, source_target_pairs={{0,2},{1,3},{2,0},{3,1},{4,6},{5,7},{6,4},{7,5},{8,10},{9,11},{10,... | collective-permute-start | bytes 98312 | tf_op jit(solution)/shard_map/ppermute | solution.py:67
  86.9 1.3 %collective-permute-start.42 = (f32[32,256]{1,0:T(8,128)S(1)}, f32[32,256]{1,0:T(8,128)S(1)}, u32[]{:S(2)}, u32[]{:S(2)}) collective-permute-start(f32[32,256]{1,0:T(8,128)S(1)} %get-tuple-element.243), channel_id=1, source_target_pairs={{0,2},{1,3},{2,0},{3,1},{4,6},{5,7},{6,4},{7,5},{8,10},{9,11},{10,... | collective-permute-start | bytes 98312 | tf_op jit(solution)/shard_map/ppermute | solution.py:67
  92.5 1.3 %collective-permute-start.45 = (f32[32,256]{1,0:T(8,128)S(1)}, f32[32,256]{1,0:T(8,128)S(1)}, u32[]{:S(2)}, u32[]{:S(2)}) collective-permute-start(f32[32,256]{1,0:T(8,128)S(1)} %get-tuple-element.250), channel_id=1, source_target_pairs={{0,2},{1,3},{2,0},{3,1},{4,6},{5,7},{6,4},{7,5},{8,10},{9,11},{10,... | collective-permute-start | bytes 98312 | tf_op jit(solution)/shard_map/ppermute | solution.py:67
  97.7 1.3 %collective-permute-start.48 = (f32[32,256]{1,0:T(8,128)S(1)}, f32[32,256]{1,0:T(8,128)S(1)}, u32[]{:S(2)}, u32[]{:S(2)}) collective-permute-start(f32[32,256]{1,0:T(8,128)S(1)} %get-tuple-element.257), channel_id=1, source_target_pairs={{0,2},{1,3},{2,0},{3,1},{4,6},{5,7},{6,4},{7,5},{8,10},{9,11},{10,... | collective-permute-start | bytes 98312 | tf_op jit(solution)/shard_map/ppermute | solution.py:67
  100.8 1.1 collective-permute-done.47.zm
  103.2 1.3 %collective-permute-start.51 = (f32[32,256]{1,0:T(8,128)S(1)}, f32[32,256]{1,0:T(8,128)S(1)}, u32[]{:S(2)}, u32[]{:S(2)}) collective-permute-start(f32[32,256]{1,0:T(8,128)S(1)} %get-tuple-element.264), channel_id=1, source_target_pairs={{0,2},{1,3},{2,0},{3,1},{4,6},{5,7},{6,4},{7,5},{8,10},{9,11},{10,... | collective-permute-start | bytes 98312 | tf_op jit(solution)/shard_map/ppermute | solution.py:67
  107.7 1.6 %collective-permute-start.54 = (f32[2,256,256]{2,1,0:T(8,128)S(1)}, f32[2,256,256]{2,1,0:T(8,128)S(1)}, u32[]{:S(2)}, u32[]{:S(2)}) collective-permute-start(f32[2,256,256]{2,1,0:T(8,128)S(1)} %get-tuple-element.270.own), channel_id=1, source_target_pairs={{0,16},{1,2},{2,1},{3,19},{4,20},{5,6},{6,5},{7,23},{8,24},{9,10},... | collective-permute-start | bytes 1572872 | tf_op jit(solution)/shard_map/ppermute | solution.py:67
  109.4 1.3 %collective-permute-done.52.got = f32[4,64,128]{2,1,0:T(8,128)S(1)} collective-permute-done((f32[4,64,128]{2,1,0:T(8,128)S(1)}, f32[4,64,128]{2,1,0:T(8,128)S(1)}, u32[]{:S(2)}, u32[]{:S(2)}) %collective-permute-start.52) | collective-permute-done | bytes 131104 | tf_op jit(solution)/shard_map/ppermute | solution.py:67
  110.7 2.4 %collective-permute-start.53 = (f32[2,64,128]{2,1,0:T(8,128)S(1)}, f32[2,64,128]{2,1,0:T(8,128)S(1)}, u32[]{:S(2)}, u32[]{:S(2)}) collective-permute-start(f32[2,64,128]{2,1,0:T(8,128)S(1)} %get-tuple-element.269), channel_id=1, source_target_pairs={{0,0},{1,2},{2,1},{3,3},{4,4},{5,6},{6,5},{7,7},{8,8},{9,10},{10,9... | collective-permute-start | bytes 196616 | tf_op jit(solution)/shard_map/ppermute | solution.py:67
  113.1 1.8 %collective-permute-start.55 = (f32[2,64,128]{2,1,0:T(8,128)S(1)}, f32[2,64,128]{2,1,0:T(8,128)S(1)}, u32[]{:S(2)}, u32[]{:S(2)}) collective-permute-start(f32[2,64,128]{2,1,0:T(8,128)S(1)} %get-tuple-element.273), channel_id=1, source_target_pairs={{0,4},{1,6},{2,5},{3,7},{4,0},{5,2},{6,1},{7,3},{8,12},{9,14},{10,... | collective-permute-start | bytes 196616 | tf_op jit(solution)/shard_map/ppermute | solution.py:67
  115.6 3.3 %collective-permute-start.57 = (f32[2,64,128]{2,1,0:T(8,128)S(1)}, f32[2,64,128]{2,1,0:T(8,128)S(1)}, u32[]{:S(2)}, u32[]{:S(2)}) collective-permute-start(f32[2,64,128]{2,1,0:T(8,128)S(1)} %get-tuple-element.275), channel_id=1, source_target_pairs={{0,12},{1,14},{2,13},{3,15},{4,8},{5,10},{6,9},{7,11},{8,4},{9,6},... | collective-permute-start | bytes 196616 | tf_op jit(solution)/shard_map/ppermute | solution.py:67
  119.8 1.3 %collective-permute-done.56.refs_2_ = f32[2,64,128]{2,1,0:T(8,128)S(1)} collective-permute-done((f32[2,64,128]{2,1,0:T(8,128)S(1)}, f32[2,64,128]{2,1,0:T(8,128)S(1)}, u32[]{:S(2)}, u32[]{:S(2)}) %collective-permute-start.56) | collective-permute-done | bytes 65568 | tf_op jit(solution)/shard_map/ppermute | solution.py:67
  122.0 1.3 %filter.1 = f32[32,32,64]{2,1,0:T(8,128)} custom-call(f32[2,64,128]{2,1,0:T(8,128)S(1)} %collective-permute-done.53.refs_0_, f32[2,64,128]{2,1,0:T(8,128)S(1)} %collective-permute-done.55.refs_1_, f32[2,64,128]{2,1,0:T(8,128)S(1)} %collective-permute-done.56.refs_2_, f32[2,64,128]{2,1,0:T(8,128)S(1)} %collective-permute-done.57.refs_3_), custom_call_target="tpu_custom_call" | custom-call | flops 1000 | bytes 1000 | tf_op jit(solution)/shard_map/filter/pallas_call | solution.py:604
  (150 shorter events, 46.1 us)
Async XLA Ops:
  0.6 10.1 %collective-permute-start.1 = (f32[256,256]{1,0:T(8,128)}, f32[256,256]{1,0:T(8,128)S(1)}, u32[]{:S(2)}, u32[]{:S(2)}) collective-permute-start(f32[256,256]{1,0:T(8,128)} %bitcast.16), channel_id=1, source_target_pairs={{0,16},{1,2},{2,1},{3,19},{4,20},{5,6},{6,5},{7,23},{8,24},{9,10},... | collective-permute-start | bytes 786440 | tf_op jit(solution)/shard_map/ppermute | solution.py:67
  3.3 7.4 %collective-permute-start = (f32[256,256]{1,0:T(8,128)}, f32[256,256]{1,0:T(8,128)S(1)}, u32[]{:S(2)}, u32[]{:S(2)}) collective-permute-start(f32[256,256]{1,0:T(8,128)} %bitcast.14), channel_id=1, source_target_pairs={{0,16},{1,2},{2,1},{3,19},{4,20},{5,6},{6,5},{7,23},{8,24},{9,10},... | collective-permute-start | bytes 786440 | tf_op jit(solution)/shard_map/ppermute | solution.py:67
  4.5 12.1 %collective-permute-start.2 = (f32[2,256,256]{2,1,0:T(8,128)S(1)}, f32[2,256,256]{2,1,0:T(8,128)S(1)}, u32[]{:S(2)}, u32[]{:S(2)}) collective-permute-start(f32[2,256,256]{2,1,0:T(8,128)S(1)} %pad_maximum_fusion), channel_id=1, source_target_pairs={{0,16},{1,2},{2,1},{3,19},{4,20},{5,6},{6,5},{7,23},{8,24},{9,10},... | collective-permute-start | bytes 1572872 | tf_op jit(solution)/shard_map/ppermute | solution.py:67
  10.9 5.8 %collective-permute-start.3 = (f32[2,128,256]{2,1,0:T(8,128)S(1)}, f32[2,128,256]{2,1,0:T(8,128)S(1)}, u32[]{:S(2)}, u32[]{:S(2)}) collective-permute-start(f32[2,128,256]{2,1,0:T(8,128)S(1)} %get-tuple-element.145), channel_id=1, source_target_pairs={{0,1},{1,0},{2,3},{3,2},{4,5},{5,4},{6,7},{7,6},{8,9},{9,8},{10,11... | collective-permute-start | bytes 786440 | tf_op jit(solution)/shard_map/ppermute | solution.py:67
  11.4 7.1 %collective-permute-start.4 = (f32[2,128,256]{2,1,0:T(8,128)S(1)}, f32[2,128,256]{2,1,0:T(8,128)S(1)}, u32[]{:S(2)}, u32[]{:S(2)}) collective-permute-start(f32[2,128,256]{2,1,0:T(8,128)S(1)} %get-tuple-element.154), channel_id=1, source_target_pairs={{0,16},{1,4},{2,18},{3,6},{4,1},{5,8},{6,3},{7,10},{8,5},{9,12},{1... | collective-permute-start | bytes 786440 | tf_op jit(solution)/shard_map/ppermute | solution.py:67
  13.2 5.2 %collective-permute-start.5 = (f32[2,32,256]{2,1,0:T(8,128)S(1)}, f32[2,32,256]{2,1,0:T(8,128)S(1)}, u32[]{:S(2)}, u32[]{:S(2)}) collective-permute-start(f32[2,32,256]{2,1,0:T(8,128)S(1)} %get-tuple-element.155), channel_id=1, source_target_pairs={{0,2},{1,3},{2,0},{3,1},{4,6},{5,7},{6,4},{7,5},{8,10},{9,11},{10,... | collective-permute-start | bytes 196616 | tf_op jit(solution)/shard_map/ppermute | solution.py:67
  19.0 4.8 %collective-permute-start.6 = (f32[168,256]{1,0:T(8,128)S(1)}, f32[168,256]{1,0:T(8,128)S(1)}, u32[]{:S(2)}, u32[]{:S(2)}) collective-permute-start(f32[168,256]{1,0:T(8,128)S(1)} %get-tuple-element.164), channel_id=1, source_target_pairs={{0,1},{1,0},{2,3},{3,2},{4,5},{5,4},{6,7},{7,6},{8,9},{9,8},{10,11... | collective-permute-start | bytes 516104 | tf_op jit(solution)/shard_map/ppermute | solution.py:67
  20.0 9.3 %collective-permute-start.7 = (f32[128,256]{1,0:T(8,128)S(1)}, f32[128,256]{1,0:T(8,128)S(1)}, u32[]{:S(2)}, u32[]{:S(2)}) collective-permute-start(f32[128,256]{1,0:T(8,128)S(1)} %get-tuple-element.166), channel_id=1, source_target_pairs={{0,16},{1,4},{2,18},{3,6},{4,1},{5,8},{6,3},{7,10},{8,5},{9,12},{1... | collective-permute-start | bytes 393224 | tf_op jit(solution)/shard_map/ppermute | solution.py:67
  20.9 11.6 %collective-permute-start.12 = (f32[256,256]{1,0:T(8,128)S(1)}, f32[256,256]{1,0:T(8,128)S(1)}, u32[]{:S(2)}, u32[]{:S(2)}) collective-permute-start(f32[256,256]{1,0:T(8,128)S(1)} %bitcast.18), channel_id=1, source_target_pairs={{0,16},{1,2},{2,1},{3,19},{4,20},{5,6},{6,5},{7,23},{8,24},{9,10},... | collective-permute-start | bytes 786440 | tf_op jit(solution)/shard_map/ppermute | solution.py:67
  22.5 10.0 %collective-permute-start.13 = (f32[256,256]{1,0:T(8,128)S(1)}, f32[256,256]{1,0:T(8,128)S(1)}, u32[]{:S(2)}, u32[]{:S(2)}) collective-permute-start(f32[256,256]{1,0:T(8,128)S(1)} %bitcast.20), channel_id=1, source_target_pairs={{0,16},{1,2},{2,1},{3,19},{4,20},{5,6},{6,5},{7,23},{8,24},{9,10},... | collective-permute-start | bytes 786440 | tf_op jit(solution)/shard_map/ppermute | solution.py:67
  22.7 6.6 %collective-permute-start.8 = (f32[32,256]{1,0:T(8,128)S(1)}, f32[32,256]{1,0:T(8,128)S(1)}, u32[]{:S(2)}, u32[]{:S(2)}) collective-permute-start(f32[32,256]{1,0:T(8,128)S(1)} %get-tuple-element.167), channel_id=1, source_target_pairs={{0,2},{1,3},{2,0},{3,1},{4,6},{5,7},{6,4},{7,5},{8,10},{9,11},{10,... | collective-permute-start | bytes 98312 | tf_op jit(solution)/shard_map/ppermute | solution.py:67
  29.6 3.3 %collective-permute-start.9 = (f32[128,256]{1,0:T(8,128)S(1)}, f32[128,256]{1,0:T(8,128)S(1)}, u32[]{:S(2)}, u32[]{:S(2)}) collective-permute-start(f32[128,256]{1,0:T(8,128)S(1)} %get-tuple-element.170), channel_id=1, source_target_pairs={{0,1},{1,0},{2,3},{3,2},{4,5},{5,4},{6,7},{7,6},{8,9},{9,8},{10,11... | collective-permute-start | bytes 393224 | tf_op jit(solution)/shard_map/ppermute | solution.py:67
  31.2 4.8 %collective-permute-start.10 = (f32[128,256]{1,0:T(8,128)S(1)}, f32[128,256]{1,0:T(8,128)S(1)}, u32[]{:S(2)}, u32[]{:S(2)}) collective-permute-start(f32[128,256]{1,0:T(8,128)S(1)} %get-tuple-element.172), channel_id=1, source_target_pairs={{0,16},{1,4},{2,18},{3,6},{4,1},{5,8},{6,3},{7,10},{8,5},{9,12},{1... | collective-permute-start | bytes 393224 | tf_op jit(solution)/shard_map/ppermute | solution.py:67
  32.5 3.6 %collective-permute-start.11 = (f32[72,256]{1,0:T(8,128)S(1)}, f32[72,256]{1,0:T(8,128)S(1)}, u32[]{:S(2)}, u32[]{:S(2)}) collective-permute-start(f32[72,256]{1,0:T(8,128)S(1)} %get-tuple-element.173), channel_id=1, source_target_pairs={{0,2},{1,3},{2,0},{3,1},{4,6},{5,7},{6,4},{7,5},{8,10},{9,11},{10,... | collective-permute-start | bytes 221192 | tf_op jit(solution)/shard_map/ppermute | solution.py:67
  36.3 5.0 %collective-permute-start.14 = (f32[2,128,256]{2,1,0:T(8,128)S(1)}, f32[2,128,256]{2,1,0:T(8,128)S(1)}, u32[]{:S(2)}, u32[]{:S(2)}) collective-permute-start(f32[2,128,256]{2,1,0:T(8,128)S(1)} %get-tuple-element.180), channel_id=1, source_target_pairs={{0,1},{1,0},{2,3},{3,2},{4,5},{5,4},{6,7},{7,6},{8,9},{9,8},{10,11... | collective-permute-start | bytes 786440 | tf_op jit(solution)/shard_map/ppermute | solution.py:67
  37.5 6.8 %collective-permute-start.15 = (f32[2,128,256]{2,1,0:T(8,128)S(1)}, f32[2,128,256]{2,1,0:T(8,128)S(1)}, u32[]{:S(2)}, u32[]{:S(2)}) collective-permute-start(f32[2,128,256]{2,1,0:T(8,128)S(1)} %get-tuple-element.182), channel_id=1, source_target_pairs={{0,16},{1,4},{2,18},{3,6},{4,1},{5,8},{6,3},{7,10},{8,5},{9,12},{1... | collective-permute-start | bytes 786440 | tf_op jit(solution)/shard_map/ppermute | solution.py:67
  39.8 4.0 %collective-permute-start.16 = (f32[2,32,256]{2,1,0:T(8,128)S(1)}, f32[2,32,256]{2,1,0:T(8,128)S(1)}, u32[]{:S(2)}, u32[]{:S(2)}) collective-permute-start(f32[2,32,256]{2,1,0:T(8,128)S(1)} %get-tuple-element.183), channel_id=1, source_target_pairs={{0,2},{1,3},{2,0},{3,1},{4,6},{5,7},{6,4},{7,5},{8,10},{9,11},{10,... | collective-permute-start | bytes 196616 | tf_op jit(solution)/shard_map/ppermute | solution.py:67
  39.8 4.0 %collective-permute-start.17 = (f32[8,8,128]{2,1,0:T(8,128)S(1)}, f32[8,8,128]{2,1,0:T(8,128)S(1)}, u32[]{:S(2)}, u32[]{:S(2)}) collective-permute-start(f32[8,8,128]{2,1,0:T(8,128)S(1)} %get-tuple-element.185), channel_id=1, source_target_pairs={{0,4},{1,5},{2,6},{3,7},{4,0},{5,1},{6,2},{7,3},{8,12},{9,13},{10,... | collective-permute-start | bytes 98312 | tf_op jit(solution)/shard_map/ppermute | solution.py:67
  44.5 4.5 %collective-permute-start.18 = (f32[128,256]{1,0:T(8,128)S(1)}, f32[128,256]{1,0:T(8,128)S(1)}, u32[]{:S(2)}, u32[]{:S(2)}) collective-permute-start(f32[128,256]{1,0:T(8,128)S(1)} %get-tuple-element.187), channel_id=1, source_target_pairs={{0,1},{1,0},{2,3},{3,2},{4,5},{5,4},{6,7},{7,6},{8,9},{9,8},{10,11... | collective-permute-start | bytes 393224 | tf_op jit(solution)/shard_map/ppermute | solution.py:67
  45.6 5.0 %collective-permute-start.19 = (f32[128,256]{1,0:T(8,128)S(1)}, f32[128,256]{1,0:T(8,128)S(1)}, u32[]{:S(2)}, u32[]{:S(2)}) collective-permute-start(f32[128,256]{1,0:T(8,128)S(1)} %get-tuple-element.189), channel_id=1, source_target_pairs={{0,16},{1,4},{2,18},{3,6},{4,1},{5,8},{6,3},{7,10},{8,5},{9,12},{1... | collective-permute-start | bytes 393224 | tf_op jit(solution)/shard_map/ppermute | solution.py:67
  46.5 3.9 %collective-permute-start.20 = (f32[32,256]{1,0:T(8,128)S(1)}, f32[32,256]{1,0:T(8,128)S(1)}, u32[]{:S(2)}, u32[]{:S(2)}) collective-permute-start(f32[32,256]{1,0:T(8,128)S(1)} %get-tuple-element.190), channel_id=1, source_target_pairs={{0,2},{1,3},{2,0},{3,1},{4,6},{5,7},{6,4},{7,5},{8,10},{9,11},{10,... | collective-permute-start | bytes 98312 | tf_op jit(solution)/shard_map/ppermute | solution.py:67
  46.5 4.1 %collective-permute-start.21 = (f32[8,8,128]{2,1,0:T(8,128)S(1)}, f32[8,8,128]{2,1,0:T(8,128)S(1)}, u32[]{:S(2)}, u32[]{:S(2)}) collective-permute-start(f32[8,8,128]{2,1,0:T(8,128)S(1)} %get-tuple-element.192), channel_id=1, source_target_pairs={{0,8},{1,9},{2,10},{3,11},{4,12},{5,13},{6,14},{7,15},{8,0},{9,1},... | collective-permute-start | bytes 98312 | tf_op jit(solution)/shard_map/ppermute | solution.py:67
  50.8 4.5 %collective-permute-start.22 = (f32[128,256]{1,0:T(8,128)S(1)}, f32[128,256]{1,0:T(8,128)S(1)}, u32[]{:S(2)}, u32[]{:S(2)}) collective-permute-start(f32[128,256]{1,0:T(8,128)S(1)} %get-tuple-element.194), channel_id=1, source_target_pairs={{0,1},{1,0},{2,3},{3,2},{4,5},{5,4},{6,7},{7,6},{8,9},{9,8},{10,11... | collective-permute-start | bytes 393224 | tf_op jit(solution)/shard_map/ppermute | solution.py:67
  52.6 4.7 %collective-permute-start.23 = (f32[128,256]{1,0:T(8,128)S(1)}, f32[128,256]{1,0:T(8,128)S(1)}, u32[]{:S(2)}, u32[]{:S(2)}) collective-permute-start(f32[128,256]{1,0:T(8,128)S(1)} %get-tuple-element.198), channel_id=1, source_target_pairs={{0,16},{1,4},{2,18},{3,6},{4,1},{5,8},{6,3},{7,10},{8,5},{9,12},{1... | collective-permute-start | bytes 393224 | tf_op jit(solution)/shard_map/ppermute | solution.py:67
  57.4 3.5 %collective-permute-start.25 = (f32[128,256]{1,0:T(8,128)S(1)}, f32[128,256]{1,0:T(8,128)S(1)}, u32[]{:S(2)}, u32[]{:S(2)}) collective-permute-start(f32[128,256]{1,0:T(8,128)S(1)} %get-tuple-element.201), channel_id=1, source_target_pairs={{0,1},{1,0},{2,3},{3,2},{4,5},{5,4},{6,7},{7,6},{8,9},{9,8},{10,11... | collective-permute-start | bytes 393224 | tf_op jit(solution)/shard_map/ppermute | solution.py:67
  58.5 4.7 %collective-permute-start.26 = (f32[128,256]{1,0:T(8,128)S(1)}, f32[128,256]{1,0:T(8,128)S(1)}, u32[]{:S(2)}, u32[]{:S(2)}) collective-permute-start(f32[128,256]{1,0:T(8,128)S(1)} %get-tuple-element.207), channel_id=1, source_target_pairs={{0,16},{1,4},{2,18},{3,6},{4,1},{5,8},{6,3},{7,10},{8,5},{9,12},{1... | collective-permute-start | bytes 393224 | tf_op jit(solution)/shard_map/ppermute | solution.py:67
  59.4 3.1 %collective-permute-start.27 = (f32[32,256]{1,0:T(8,128)S(1)}, f32[32,256]{1,0:T(8,128)S(1)}, u32[]{:S(2)}, u32[]{:S(2)}) collective-permute-start(f32[32,256]{1,0:T(8,128)S(1)} %get-tuple-element.208), channel_id=1, source_target_pairs={{0,2},{1,3},{2,0},{3,1},{4,6},{5,7},{6,4},{7,5},{8,10},{9,11},{10,... | collective-permute-start | bytes 98312 | tf_op jit(solution)/shard_map/ppermute | solution.py:67
  63.9 4.7 %collective-permute-start.29 = (f32[128,256]{1,0:T(8,128)S(1)}, f32[128,256]{1,0:T(8,128)S(1)}, u32[]{:S(2)}, u32[]{:S(2)}) collective-permute-start(f32[128,256]{1,0:T(8,128)S(1)} %get-tuple-element.212), channel_id=1, source_target_pairs={{0,16},{1,4},{2,18},{3,6},{4,1},{5,8},{6,3},{7,10},{8,5},{9,12},{1... | collective-permute-start | bytes 393224 | tf_op jit(solution)/shard_map/ppermute | solution.py:67
  64.5 3.2 %collective-permute-start.30 = (f32[32,256]{1,0:T(8,128)S(1)}, f32[32,256]{1,0:T(8,128)S(1)}, u32[]{:S(2)}, u32[]{:S(2)}) collective-permute-start(f32[32,256]{1,0:T(8,128)S(1)} %get-tuple-element.213), channel_id=1, source_target_pairs={{0,2},{1,3},{2,0},{3,1},{4,6},{5,7},{6,4},{7,5},{8,10},{9,11},{10,... | collective-permute-start | bytes 98312 | tf_op jit(solution)/shard_map/ppermute | solution.py:67
  70.1 4.7 %collective-permute-start.32 = (f32[128,256]{1,0:T(8,128)S(1)}, f32[128,256]{1,0:T(8,128)S(1)}, u32[]{:S(2)}, u32[]{:S(2)}) collective-permute-start(f32[128,256]{1,0:T(8,128)S(1)} %get-tuple-element.221), channel_id=1, source_target_pairs={{0,16},{1,4},{2,18},{3,6},{4,1},{5,8},{6,3},{7,10},{8,5},{9,12},{1... | collective-permute-start | bytes 393224 | tf_op jit(solution)/shard_map/ppermute | solution.py:67
  70.6 3.1 %collective-permute-start.33 = (f32[32,256]{1,0:T(8,128)S(1)}, f32[32,256]{1,0:T(8,128)S(1)}, u32[]{:S(2)}, u32[]{:S(2)}) collective-permute-start(f32[32,256]{1,0:T(8,128)S(1)} %get-tuple-element.222), channel_id=1, source_target_pairs={{0,2},{1,3},{2,0},{3,1},{4,6},{5,7},{6,4},{7,5},{8,10},{9,11},{10,... | collective-permute-start | bytes 98312 | tf_op jit(solution)/shard_map/ppermute | solution.py:67
  75.5 4.7 %collective-permute-start.35 = (f32[128,256]{1,0:T(8,128)S(1)}, f32[128,256]{1,0:T(8,128)S(1)}, u32[]{:S(2)}, u32[]{:S(2)}) collective-permute-start(f32[128,256]{1,0:T(8,128)S(1)} %get-tuple-element.228), channel_id=1, source_target_pairs={{0,16},{1,4},{2,18},{3,6},{4,1},{5,8},{6,3},{7,10},{8,5},{9,12},{1... | collective-permute-start | bytes 393224 | tf_op jit(solution)/shard_map/ppermute | solution.py:67
  76.2 3.1 %collective-permute-start.36 = (f32[32,256]{1,0:T(8,128)S(1)}, f32[32,256]{1,0:T(8,128)S(1)}, u32[]{:S(2)}, u32[]{:S(2)}) collective-permute-start(f32[32,256]{1,0:T(8,128)S(1)} %get-tuple-element.229), channel_id=1, source_target_pairs={{0,2},{1,3},{2,0},{3,1},{4,6},{5,7},{6,4},{7,5},{8,10},{9,11},{10,... | collective-permute-start | bytes 98312 | tf_op jit(solution)/shard_map/ppermute | solution.py:67
  80.9 4.7 %collective-permute-start.38 = (f32[128,256]{1,0:T(8,128)S(1)}, f32[128,256]{1,0:T(8,128)S(1)}, u32[]{:S(2)}, u32[]{:S(2)}) collective-permute-start(f32[128,256]{1,0:T(8,128)S(1)} %get-tuple-element.235), channel_id=1, source_target_pairs={{0,16},{1,4},{2,18},{3,6},{4,1},{5,8},{6,3},{7,10},{8,5},{9,12},{1... | collective-permute-start | bytes 393224 | tf_op jit(solution)/shard_map/ppermute | solution.py:67
  81.6 3.1 %collective-permute-start.39 = (f32[32,256]{1,0:T(8,128)S(1)}, f32[32,256]{1,0:T(8,128)S(1)}, u32[]{:S(2)}, u32[]{:S(2)}) collective-permute-start(f32[32,256]{1,0:T(8,128)S(1)} %get-tuple-element.236), channel_id=1, source_target_pairs={{0,2},{1,3},{2,0},{3,1},{4,6},{5,7},{6,4},{7,5},{8,10},{9,11},{10,... | collective-permute-start | bytes 98312 | tf_op jit(solution)/shard_map/ppermute | solution.py:67
  86.3 4.7 %collective-permute-start.41 = (f32[128,256]{1,0:T(8,128)S(1)}, f32[128,256]{1,0:T(8,128)S(1)}, u32[]{:S(2)}, u32[]{:S(2)}) collective-permute-start(f32[128,256]{1,0:T(8,128)S(1)} %get-tuple-element.242), channel_id=1, source_target_pairs={{0,16},{1,4},{2,18},{3,6},{4,1},{5,8},{6,3},{7,10},{8,5},{9,12},{1... | collective-permute-start | bytes 393224 | tf_op jit(solution)/shard_map/ppermute | solution.py:67
  86.9 3.1 %collective-permute-start.42 = (f32[32,256]{1,0:T(8,128)S(1)}, f32[32,256]{1,0:T(8,128)S(1)}, u32[]{:S(2)}, u32[]{:S(2)}) collective-permute-start(f32[32,256]{1,0:T(8,128)S(1)} %get-tuple-element.243), channel_id=1, source_target_pairs={{0,2},{1,3},{2,0},{3,1},{4,6},{5,7},{6,4},{7,5},{8,10},{9,11},{10,... | collective-permute-start | bytes 98312 | tf_op jit(solution)/shard_map/ppermute | solution.py:67
  91.6 4.7 %collective-permute-start.44 = (f32[128,256]{1,0:T(8,128)S(1)}, f32[128,256]{1,0:T(8,128)S(1)}, u32[]{:S(2)}, u32[]{:S(2)}) collective-permute-start(f32[128,256]{1,0:T(8,128)S(1)} %get-tuple-element.249), channel_id=1, source_target_pairs={{0,16},{1,4},{2,18},{3,6},{4,1},{5,8},{6,3},{7,10},{8,5},{9,12},{1... | collective-permute-start | bytes 393224 | tf_op jit(solution)/shard_map/ppermute | solution.py:67
  92.5 3.1 %collective-permute-start.45 = (f32[32,256]{1,0:T(8,128)S(1)}, f32[32,256]{1,0:T(8,128)S(1)}, u32[]{:S(2)}, u32[]{:S(2)}) collective-permute-start(f32[32,256]{1,0:T(8,128)S(1)} %get-tuple-element.250), channel_id=1, source_target_pairs={{0,2},{1,3},{2,0},{3,1},{4,6},{5,7},{6,4},{7,5},{8,10},{9,11},{10,... | collective-permute-start | bytes 98312 | tf_op jit(solution)/shard_map/ppermute | solution.py:67
  97.2 4.7 %collective-permute-start.47 = (f32[128,256]{1,0:T(8,128)S(1)}, f32[128,256]{1,0:T(8,128)S(1)}, u32[]{:S(2)}, u32[]{:S(2)}) collective-permute-start(f32[128,256]{1,0:T(8,128)S(1)} %get-tuple-element.256), channel_id=1, source_target_pairs={{0,16},{1,4},{2,18},{3,6},{4,1},{5,8},{6,3},{7,10},{8,5},{9,12},{1... | collective-permute-start | bytes 393224 | tf_op jit(solution)/shard_map/ppermute | solution.py:67
  97.7 3.1 %collective-permute-start.48 = (f32[32,256]{1,0:T(8,128)S(1)}, f32[32,256]{1,0:T(8,128)S(1)}, u32[]{:S(2)}, u32[]{:S(2)}) collective-permute-start(f32[32,256]{1,0:T(8,128)S(1)} %get-tuple-element.257), channel_id=1, source_target_pairs={{0,2},{1,3},{2,0},{3,1},{4,6},{5,7},{6,4},{7,5},{8,10},{9,11},{10,... | collective-permute-start | bytes 98312 | tf_op jit(solution)/shard_map/ppermute | solution.py:67
  102.5 4.7 %collective-permute-start.50 = (f32[128,256]{1,0:T(8,128)S(1)}, f32[128,256]{1,0:T(8,128)S(1)}, u32[]{:S(2)}, u32[]{:S(2)}) collective-permute-start(f32[128,256]{1,0:T(8,128)S(1)} %get-tuple-element.263), channel_id=1, source_target_pairs={{0,16},{1,4},{2,18},{3,6},{4,1},{5,8},{6,3},{7,10},{8,5},{9,12},{1... | collective-permute-start | bytes 393224 | tf_op jit(solution)/shard_map/ppermute | solution.py:67
  103.2 3.1 %collective-permute-start.51 = (f32[32,256]{1,0:T(8,128)S(1)}, f32[32,256]{1,0:T(8,128)S(1)}, u32[]{:S(2)}, u32[]{:S(2)}) collective-permute-start(f32[32,256]{1,0:T(8,128)S(1)} %get-tuple-element.264), channel_id=1, source_target_pairs={{0,2},{1,3},{2,0},{3,1},{4,6},{5,7},{6,4},{7,5},{8,10},{9,11},{10,... | collective-permute-start | bytes 98312 | tf_op jit(solution)/shard_map/ppermute | solution.py:67
  107.7 11.2 %collective-permute-start.54 = (f32[2,256,256]{2,1,0:T(8,128)S(1)}, f32[2,256,256]{2,1,0:T(8,128)S(1)}, u32[]{:S(2)}, u32[]{:S(2)}) collective-permute-start(f32[2,256,256]{2,1,0:T(8,128)S(1)} %get-tuple-element.270.own), channel_id=1, source_target_pairs={{0,16},{1,2},{2,1},{3,19},{4,20},{5,6},{6,5},{7,23},{8,24},{9,10},... | collective-permute-start | bytes 1572872 | tf_op jit(solution)/shard_map/ppermute | solution.py:67
  110.7 9.0 %collective-permute-start.53 = (f32[2,64,128]{2,1,0:T(8,128)S(1)}, f32[2,64,128]{2,1,0:T(8,128)S(1)}, u32[]{:S(2)}, u32[]{:S(2)}) collective-permute-start(f32[2,64,128]{2,1,0:T(8,128)S(1)} %get-tuple-element.269), channel_id=1, source_target_pairs={{0,0},{1,2},{2,1},{3,3},{4,4},{5,6},{6,5},{7,7},{8,8},{9,10},{10,9... | collective-permute-start | bytes 196616 | tf_op jit(solution)/shard_map/ppermute | solution.py:67
  113.1 6.7 %collective-permute-start.55 = (f32[2,64,128]{2,1,0:T(8,128)S(1)}, f32[2,64,128]{2,1,0:T(8,128)S(1)}, u32[]{:S(2)}, u32[]{:S(2)}) collective-permute-start(f32[2,64,128]{2,1,0:T(8,128)S(1)} %get-tuple-element.273), channel_id=1, source_target_pairs={{0,4},{1,6},{2,5},{3,7},{4,0},{5,2},{6,1},{7,3},{8,12},{9,14},{10,... | collective-permute-start | bytes 196616 | tf_op jit(solution)/shard_map/ppermute | solution.py:67
  114.9 6.2 %collective-permute-start.56 = (f32[2,64,128]{2,1,0:T(8,128)S(1)}, f32[2,64,128]{2,1,0:T(8,128)S(1)}, u32[]{:S(2)}, u32[]{:S(2)}) collective-permute-start(f32[2,64,128]{2,1,0:T(8,128)S(1)} %get-tuple-element.274), channel_id=1, source_target_pairs={{0,8},{1,10},{2,9},{3,11},{4,12},{5,14},{6,13},{7,15},{8,0},{9,2},... | collective-permute-start | bytes 196616 | tf_op jit(solution)/shard_map/ppermute | solution.py:67
  115.6 6.4 %collective-permute-start.57 = (f32[2,64,128]{2,1,0:T(8,128)S(1)}, f32[2,64,128]{2,1,0:T(8,128)S(1)}, u32[]{:S(2)}, u32[]{:S(2)}) collective-permute-start(f32[2,64,128]{2,1,0:T(8,128)S(1)} %get-tuple-element.275), channel_id=1, source_target_pairs={{0,12},{1,14},{2,13},{3,15},{4,8},{5,10},{6,9},{7,11},{8,4},{9,6},... | collective-permute-start | bytes 196616 | tf_op jit(solution)/shard_map/ppermute | solution.py:67
  (28 other events, 72.2 us)

commit v15 on v14

--- a/solution.py
+++ b/solution.py
@@ -724,6 +724,9 @@
             states.append(new)
             break
         if t == 1:
+            u_now, u_before = call(settle_pair_kernel, "settle_adjoint", [field, field], adj_now,
+                                   adj_before, *got_adjoint, weight=0.6, far=2)
+            args[0] = after(part, u_now)
             new, *out, lists, pair = call(
                 core_stage_kernel, "forward_outer",
                 [field, rim[0], rim[1], y_rim, entries, shaped(2, slots)], *args, lists, cells, cm)
@@ -731,8 +734,6 @@
             zm, cm, ym = halo(*out)
             continue
         if t == 2:
-            u_now, u_before = call(settle_pair_kernel, "settle_adjoint", [field, field], adj_now,
-                                   adj_before, *got_adjoint, weight=0.3, far=2)
             new, *out, lists, give, cells = call(
                 y_stage_kernel, "forward_outer",
                 [field] + [shaped(2, *r.shape) for r in rim] + [entries, half_entries,

time: 124 us -> 118 us (0.952)
  waiting for transfers between devices: 29.3 us -> 25.1 us
  local copies, waits for them, and re-layouts: 3.08 us -> 1.64 us
    ppermute x58, waiting for transfers between devices: 29.3 us -> 25.1 us  [send(): return lax.ppermute(value, ALL, pairs)]
    unnamed x36, local copies, waits for them, and re-layouts: 3.08 us -> 1.64 us
  transfers between devices with their start and end apart: 58 -> 58, of which waited for: 29 -> 33; matrix products, arithmetic and copies ran while one was open for 1% -> 1% of each run, Pallas kernels for 17% -> 18%
where the time goes in v15:
time: 118 us
  starting transfers between devices  62.3 us (53%)
  Pallas kernels  26.8 us (23%)
  waiting for transfers between devices  25.1 us (21%)
  local copies, waits for them, and re-layouts  1.64 us (1%)
  other arithmetic  1.24 us (1%)
    ppermute x58, starting transfers between devices, send(): return lax.ppermute(value, ALL, pairs)  62.3 us
    pallas_call x40, Pallas kernels, call(): pl.pallas_call(functools.partial(kernel, Flags()), name=name, out_shape=o...  26.8 us
    ppermute x58, waiting for transfers between devices, send(): return lax.ppermute(value, ALL, pairs)  25.1 us
  transfers between devices with their start and end apart: 58, of which 33 were waited for; matrix products, arithmetic and copies ran while one was open for 1% of the time, Pallas kernels for 18%

profile of v15, /device:TPU:1, one launch (start us, length us, event | category | flops | bytes accessed | tf_op | source)
XLA Modules:
  0.0 118.3 jit_solution(5148828097202712913)
XLA Ops:
  0.6 2.7 %collective-permute-start.1 = (f32[256,256]{1,0:T(8,128)}, f32[256,256]{1,0:T(8,128)S(1)}, u32[]{:S(2)}, u32[]{:S(2)}) collective-permute-start(f32[256,256]{1,0:T(8,128)} %bitcast.16), channel_id=1, source_target_pairs={{0,16},{1,2},{2,1},{3,19},{4,20},{5,6},{6,5},{7,23},{8,24},{9,10},... | collective-permute-start | bytes 786440 | tf_op jit(solution)/shard_map/ppermute | solution.py:67
  3.4 1.1 pad_maximum_fusion
  4.5 1.7 %collective-permute-start.2 = (f32[2,256,256]{2,1,0:T(8,128)S(1)}, f32[2,256,256]{2,1,0:T(8,128)S(1)}, u32[]{:S(2)}, u32[]{:S(2)}) collective-permute-start(f32[2,256,256]{2,1,0:T(8,128)S(1)} %pad_maximum_fusion), channel_id=1, source_target_pairs={{0,16},{1,2},{2,1},{3,19},{4,20},{5,6},{6,5},{7,23},{8,24},{9,10},... | collective-permute-start | bytes 1572872 | tf_op jit(solution)/shard_map/ppermute | solution.py:67
  8.8 1.9 %collective-permute-done.recv_a = f32[256,256]{1,0:T(8,128)S(1)} collective-permute-done((f32[256,256]{1,0:T(8,128)}, f32[256,256]{1,0:T(8,128)S(1)}, u32[]{:S(2)}, u32[]{:S(2)}) %collective-permute-start) | collective-permute-done | bytes 262176 | tf_op jit(solution)/shard_map/ppermute | solution.py:67
  11.3 1.8 %collective-permute-start.4 = (f32[2,128,256]{2,1,0:T(8,128)S(1)}, f32[2,128,256]{2,1,0:T(8,128)S(1)}, u32[]{:S(2)}, u32[]{:S(2)}) collective-permute-start(f32[2,128,256]{2,1,0:T(8,128)S(1)} %get-tuple-element.155), channel_id=1, source_target_pairs={{0,16},{1,4},{2,18},{3,6},{4,1},{5,8},{6,3},{7,10},{8,5},{9,12},{1... | collective-permute-start | bytes 786440 | tf_op jit(solution)/shard_map/ppermute | solution.py:67
  14.9 1.3 %collective-permute-start.7 = (f32[256,256]{1,0:T(8,128)S(1)}, f32[256,256]{1,0:T(8,128)S(1)}, u32[]{:S(2)}, u32[]{:S(2)}) collective-permute-start(f32[256,256]{1,0:T(8,128)S(1)} %bitcast.18), channel_id=1, source_target_pairs={{0,16},{1,2},{2,1},{3,19},{4,20},{5,6},{6,5},{7,23},{8,24},{9,10},... | collective-permute-start | bytes 786440 | tf_op jit(solution)/shard_map/ppermute | solution.py:67
  18.0 2.1 %collective-permute-start.6 = (f32[168,256]{1,0:T(8,128)S(1)}, f32[168,256]{1,0:T(8,128)S(1)}, u32[]{:S(2)}, u32[]{:S(2)}) collective-permute-start(f32[168,256]{1,0:T(8,128)S(1)} %get-tuple-element.165), channel_id=1, source_target_pairs={{0,1},{1,0},{2,3},{3,2},{4,5},{5,4},{6,7},{7,6},{8,9},{9,8},{10,11... | collective-permute-start | bytes 516104 | tf_op jit(solution)/shard_map/ppermute | solution.py:67
  20.2 1.7 %collective-permute-start.10 = (f32[32,256]{1,0:T(8,128)S(1)}, f32[32,256]{1,0:T(8,128)S(1)}, u32[]{:S(2)}, u32[]{:S(2)}) collective-permute-start(f32[32,256]{1,0:T(8,128)S(1)} %get-tuple-element.172), channel_id=1, source_target_pairs={{0,2},{1,3},{2,0},{3,1},{4,6},{5,7},{6,4},{7,5},{8,10},{9,11},{10,... | collective-permute-start | bytes 98312 | tf_op jit(solution)/shard_map/ppermute | solution.py:67
  22.0 1.4 %forward_inner.7 = (f32[256,256]{1,0:T(8,128)S(1)}, f32[256,256]{1,0:T(8,128)S(1)}) custom-call(s32[16]{0:T(128)S(1)} %copy-done.8, f32[8,16]{1,0:T(8,128)S(1)} %copy-done.3, f32[256,256]{1,0:T(8,128)S(1)} %get-tuple-element.160.cur.prev.before.state, f32[256,256]{1,0:T(8,128)S(1)} %get-tuple-element.142.cur.prev.before, ...), custom_call_target="tpu_custom_call" | custom-call | flops 1000 | bytes 4321000 | tf_op jit(solution)/shard_map/forward_inner/pallas_call | solution.py:604
  25.0 1.8 %collective-permute-start.11 = (f32[128,256]{1,0:T(8,128)S(1)}, f32[128,256]{1,0:T(8,128)S(1)}, u32[]{:S(2)}, u32[]{:S(2)}) collective-permute-start(f32[128,256]{1,0:T(8,128)S(1)} %get-tuple-element.175), channel_id=1, source_target_pairs={{0,1},{1,0},{2,3},{3,2},{4,5},{5,4},{6,7},{7,6},{8,9},{9,8},{10,11... | collective-permute-start | bytes 393224 | tf_op jit(solution)/shard_map/ppermute | solution.py:67
  26.8 1.2 %collective-permute-start.13 = (f32[72,256]{1,0:T(8,128)S(1)}, f32[72,256]{1,0:T(8,128)S(1)}, u32[]{:S(2)}, u32[]{:S(2)}) collective-permute-start(f32[72,256]{1,0:T(8,128)S(1)} %get-tuple-element.178), channel_id=1, source_target_pairs={{0,2},{1,3},{2,0},{3,1},{4,6},{5,7},{6,4},{7,5},{8,10},{9,11},{10,... | collective-permute-start | bytes 221192 | tf_op jit(solution)/shard_map/ppermute | solution.py:67
  28.0 1.4 %forward_inner.8 = (f32[256,256]{1,0:T(8,128)S(1)}, f32[256,256]{1,0:T(8,128)S(1)}) custom-call(s32[16]{0:T(128)S(1)} %copy-done.8, f32[8,16]{1,0:T(8,128)S(1)} %copy-done.3, f32[256,256]{1,0:T(8,128)S(1)} %get-tuple-element.174.cur.prev.before.state, f32[256,256]{1,0:T(8,128)S(1)} %get-tuple-element.160.cur.prev.before.state, ...), custom_call_target="tpu_custom_call" | custom-call | flops 1000 | bytes 4321000 | tf_op jit(solution)/shard_map/forward_inner/pallas_call | solution.py:604
  30.3 1.1 collective-permute-done.12.zm
  31.7 1.9 %collective-permute-start.14 = (f32[2,128,256]{2,1,0:T(8,128)S(1)}, f32[2,128,256]{2,1,0:T(8,128)S(1)}, u32[]{:S(2)}, u32[]{:S(2)}) collective-permute-start(f32[2,128,256]{2,1,0:T(8,128)S(1)} %get-tuple-element.182), channel_id=1, source_target_pairs={{0,1},{1,0},{2,3},{3,2},{4,5},{5,4},{6,7},{7,6},{8,9},{9,8},{10,11... | collective-permute-start | bytes 786440 | tf_op jit(solution)/shard_map/ppermute | solution.py:67
  34.2 1.2 %collective-permute-start.17 = (f32[8,8,128]{2,1,0:T(8,128)S(1)}, f32[8,8,128]{2,1,0:T(8,128)S(1)}, u32[]{:S(2)}, u32[]{:S(2)}) collective-permute-start(f32[8,8,128]{2,1,0:T(8,128)S(1)} %get-tuple-element.187), channel_id=1, source_target_pairs={{0,4},{1,5},{2,6},{3,7},{4,0},{5,1},{6,2},{7,3},{8,12},{9,13},{10,... | collective-permute-start | bytes 98312 | tf_op jit(solution)/shard_map/ppermute | solution.py:67
  35.5 1.4 %forward_inner.9 = (f32[256,256]{1,0:T(8,128)S(1)}, f32[256,256]{1,0:T(8,128)S(1)}) custom-call(s32[16]{0:T(128)S(1)} %copy-done.8, f32[8,16]{1,0:T(8,128)S(1)} %copy-done.3, f32[256,256]{1,0:T(8,128)S(1)} %get-tuple-element.181.cur.prev.before.state, f32[256,256]{1,0:T(8,128)S(1)} %get-tuple-element.174.cur.prev.before.state, ...), custom_call_target="tpu_custom_call" | custom-call | flops 1000 | bytes 4321000 | tf_op jit(solution)/shard_map/forward_inner/pallas_call | solution.py:604
  37.6 2.1 %collective-permute-done.15.zm.u_zm = f32[2,128,256]{2,1,0:T(8,128)S(1)} collective-permute-done((f32[2,128,256]{2,1,0:T(8,128)S(1)}, f32[2,128,256]{2,1,0:T(8,128)S(1)}, u32[]{:S(2)}, u32[]{:S(2)}) %collective-permute-start.15) | collective-permute-done | bytes 262176 | tf_op jit(solution)/shard_map/ppermute | solution.py:67
  39.9 1.1 collective-permute-start.18
  41.4 1.9 %collective-permute-start.21 = (f32[8,8,128]{2,1,0:T(8,128)S(1)}, f32[8,8,128]{2,1,0:T(8,128)S(1)}, u32[]{:S(2)}, u32[]{:S(2)}) collective-permute-start(f32[8,8,128]{2,1,0:T(8,128)S(1)} %get-tuple-element.194), channel_id=1, source_target_pairs={{0,8},{1,9},{2,10},{3,11},{4,12},{5,13},{6,14},{7,15},{8,0},{9,1},... | collective-permute-start | bytes 98312 | tf_op jit(solution)/shard_map/ppermute | solution.py:67
  43.2 1.4 %forward_inner.10 = (f32[256,256]{1,0:T(8,128)S(1)}, f32[256,256]{1,0:T(8,128)S(1)}) custom-call(s32[16]{0:T(128)S(1)} %copy-done.8, f32[8,16]{1,0:T(8,128)S(1)} %copy-done.3, f32[256,256]{1,0:T(8,128)S(1)} %get-tuple-element.188.cur.prev.before.state, f32[256,256]{1,0:T(8,128)S(1)} %get-tuple-element.181.cur.prev.before.state, ...), custom_call_target="tpu_custom_call" | custom-call | flops 1000 | bytes 4321000 | tf_op jit(solution)/shard_map/forward_inner/pallas_call | solution.py:604
  46.0 1.5 %collective-permute-start.22 = (f32[128,256]{1,0:T(8,128)S(1)}, f32[128,256]{1,0:T(8,128)S(1)}, u32[]{:S(2)}, u32[]{:S(2)}) collective-permute-start(f32[128,256]{1,0:T(8,128)S(1)} %get-tuple-element.196), channel_id=1, source_target_pairs={{0,1},{1,0},{2,3},{3,2},{4,5},{5,4},{6,7},{7,6},{8,9},{9,8},{10,11... | collective-permute-start | bytes 393224 | tf_op jit(solution)/shard_map/ppermute | solution.py:67
  48.4 1.4 %collective-permute-start.24 = (f32[32,256]{1,0:T(8,128)S(1)}, f32[32,256]{1,0:T(8,128)S(1)}, u32[]{:S(2)}, u32[]{:S(2)}) collective-permute-start(f32[32,256]{1,0:T(8,128)S(1)} %get-tuple-element.201), channel_id=1, source_target_pairs={{0,2},{1,3},{2,0},{3,1},{4,6},{5,7},{6,4},{7,5},{8,10},{9,11},{10,... | collective-permute-start | bytes 98312 | tf_op jit(solution)/shard_map/ppermute | solution.py:67
  50.3 1.4 %forward_inner.11 = (f32[256,256]{1,0:T(8,128)S(1)}, f32[256,256]{1,0:T(8,128)S(1)}) custom-call(s32[16]{0:T(128)S(1)} %copy-done.8, f32[8,16]{1,0:T(8,128)S(1)} %copy-done.3, f32[256,256]{1,0:T(8,128)S(1)} %get-tuple-element.195.cur.prev.before.state, f32[256,256]{1,0:T(8,128)S(1)} %get-tuple-element.188.cur.prev.before.state, ...), custom_call_target="tpu_custom_call" | custom-call | flops 1000 | bytes 4321000 | tf_op jit(solution)/shard_map/forward_inner/pallas_call | solution.py:604
  53.6 1.3 %collective-permute-start.27 = (f32[32,256]{1,0:T(8,128)S(1)}, f32[32,256]{1,0:T(8,128)S(1)}, u32[]{:S(2)}, u32[]{:S(2)}) collective-permute-start(f32[32,256]{1,0:T(8,128)S(1)} %get-tuple-element.210), channel_id=1, source_target_pairs={{0,2},{1,3},{2,0},{3,1},{4,6},{5,7},{6,4},{7,5},{8,10},{9,11},{10,... | collective-permute-start | bytes 98312 | tf_op jit(solution)/shard_map/ppermute | solution.py:67
  55.1 1.4 %forward_inner.12 = (f32[256,256]{1,0:T(8,128)S(1)}, f32[256,256]{1,0:T(8,128)S(1)}) custom-call(s32[16]{0:T(128)S(1)} %copy-done.8, f32[8,16]{1,0:T(8,128)S(1)} %copy-done.3, f32[256,256]{1,0:T(8,128)S(1)} %get-tuple-element.202.cur.prev.rest_2_.state, f32[256,256]{1,0:T(8,128)S(1)} %get-tuple-element.195.cur.prev.before.state, ...), custom_call_target="tpu_custom_call" | custom-call | flops 1000 | bytes 4321000 | tf_op jit(solution)/shard_map/forward_inner/pallas_call | solution.py:604
  56.7 1.2 %collective-permute-done.26.zm = f32[128,256]{1,0:T(8,128)S(1)} collective-permute-done((f32[128,256]{1,0:T(8,128)S(1)}, f32[128,256]{1,0:T(8,128)S(1)}, u32[]{:S(2)}, u32[]{:S(2)}) %collective-permute-start.26) | collective-permute-done | bytes 131104 | tf_op jit(solution)/shard_map/ppermute | solution.py:67
  59.3 1.7 %collective-permute-start.30 = (f32[32,256]{1,0:T(8,128)S(1)}, f32[32,256]{1,0:T(8,128)S(1)}, u32[]{:S(2)}, u32[]{:S(2)}) collective-permute-start(f32[32,256]{1,0:T(8,128)S(1)} %get-tuple-element.215), channel_id=1, source_target_pairs={{0,2},{1,3},{2,0},{3,1},{4,6},{5,7},{6,4},{7,5},{8,10},{9,11},{10,... | collective-permute-start | bytes 98312 | tf_op jit(solution)/shard_map/ppermute | solution.py:67
  60.9 1.4 %forward_inner.13 = (f32[256,256]{1,0:T(8,128)S(1)}, f32[256,256]{1,0:T(8,128)S(1)}) custom-call(s32[16]{0:T(128)S(1)} %copy-done.8, f32[8,16]{1,0:T(8,128)S(1)} %copy-done.3, f32[256,256]{1,0:T(8,128)S(1)} %get-tuple-element.211.cur.state.rest_1_, f32[256,256]{1,0:T(8,128)S(1)} %get-tuple-element.202.cur.prev.rest_2_.state, ...), custom_call_target="tpu_custom_call" | custom-call | flops 1000 | bytes 4321000 | tf_op jit(solution)/shard_map/forward_inner/pallas_call | solution.py:604
  65.3 1.7 %collective-permute-start.33 = (f32[32,256]{1,0:T(8,128)S(1)}, f32[32,256]{1,0:T(8,128)S(1)}, u32[]{:S(2)}, u32[]{:S(2)}) collective-permute-start(f32[32,256]{1,0:T(8,128)S(1)} %get-tuple-element.224), channel_id=1, source_target_pairs={{0,2},{1,3},{2,0},{3,1},{4,6},{5,7},{6,4},{7,5},{8,10},{9,11},{10,... | collective-permute-start | bytes 98312 | tf_op jit(solution)/shard_map/ppermute | solution.py:67
  67.0 1.0 adjoint_inner.7
  70.6 1.7 %collective-permute-start.36 = (f32[32,256]{1,0:T(8,128)S(1)}, f32[32,256]{1,0:T(8,128)S(1)}, u32[]{:S(2)}, u32[]{:S(2)}) collective-permute-start(f32[32,256]{1,0:T(8,128)S(1)} %get-tuple-element.231), channel_id=1, source_target_pairs={{0,2},{1,3},{2,0},{3,1},{4,6},{5,7},{6,4},{7,5},{8,10},{9,11},{10,... | collective-permute-start | bytes 98312 | tf_op jit(solution)/shard_map/ppermute | solution.py:67
  72.3 1.0 adjoint_inner.8
  76.0 1.7 %collective-permute-start.39 = (f32[32,256]{1,0:T(8,128)S(1)}, f32[32,256]{1,0:T(8,128)S(1)}, u32[]{:S(2)}, u32[]{:S(2)}) collective-permute-start(f32[32,256]{1,0:T(8,128)S(1)} %get-tuple-element.238), channel_id=1, source_target_pairs={{0,2},{1,3},{2,0},{3,1},{4,6},{5,7},{6,4},{7,5},{8,10},{9,11},{10,... | collective-permute-start | bytes 98312 | tf_op jit(solution)/shard_map/ppermute | solution.py:67
  77.7 1.0 adjoint_inner.9
  81.4 1.7 %collective-permute-start.42 = (f32[32,256]{1,0:T(8,128)S(1)}, f32[32,256]{1,0:T(8,128)S(1)}, u32[]{:S(2)}, u32[]{:S(2)}) collective-permute-start(f32[32,256]{1,0:T(8,128)S(1)} %get-tuple-element.245), channel_id=1, source_target_pairs={{0,2},{1,3},{2,0},{3,1},{4,6},{5,7},{6,4},{7,5},{8,10},{9,11},{10,... | collective-permute-start | bytes 98312 | tf_op jit(solution)/shard_map/ppermute | solution.py:67
  83.1 1.2 %adjoint_inner.10 = (f32[256,256]{1,0:T(8,128)S(1)}, f32[256,256]{1,0:T(8,128)S(1)}) custom-call(f32[256,256]{1,0:T(8,128)S(1)} %get-tuple-element.239.cur.prev, f32[256,256]{1,0:T(8,128)S(1)} %get-tuple-element.232.cur.prev, f32[256,256]{1,0:T(8,128)S(1)} %get-tuple-element.161.k0, f32[256,256]{1,0:T(8,128)S(1)} %get-tuple-element.162.ki, ...), custom_call_target="tpu_custom_call" | custom-call | flops 1000 | bytes 5401000 | tf_op jit(solution)/shard_map/adjoint_inner/pallas_call | solution.py:604
  86.8 1.7 %collective-permute-start.45 = (f32[32,256]{1,0:T(8,128)S(1)}, f32[32,256]{1,0:T(8,128)S(1)}, u32[]{:S(2)}, u32[]{:S(2)}) collective-permute-start(f32[32,256]{1,0:T(8,128)S(1)} %get-tuple-element.252), channel_id=1, source_target_pairs={{0,2},{1,3},{2,0},{3,1},{4,6},{5,7},{6,4},{7,5},{8,10},{9,11},{10,... | collective-permute-start | bytes 98312 | tf_op jit(solution)/shard_map/ppermute | solution.py:67
  88.5 1.0 adjoint_inner.11
  92.1 1.7 %collective-permute-start.48 = (f32[32,256]{1,0:T(8,128)S(1)}, f32[32,256]{1,0:T(8,128)S(1)}, u32[]{:S(2)}, u32[]{:S(2)}) collective-permute-start(f32[32,256]{1,0:T(8,128)S(1)} %get-tuple-element.259), channel_id=1, source_target_pairs={{0,2},{1,3},{2,0},{3,1},{4,6},{5,7},{6,4},{7,5},{8,10},{9,11},{10,... | collective-permute-start | bytes 98312 | tf_op jit(solution)/shard_map/ppermute | solution.py:67
  97.5 1.7 %collective-permute-start.51 = (f32[32,256]{1,0:T(8,128)S(1)}, f32[32,256]{1,0:T(8,128)S(1)}, u32[]{:S(2)}, u32[]{:S(2)}) collective-permute-start(f32[32,256]{1,0:T(8,128)S(1)} %get-tuple-element.266), channel_id=1, source_target_pairs={{0,2},{1,3},{2,0},{3,1},{4,6},{5,7},{6,4},{7,5},{8,10},{9,11},{10,... | collective-permute-start | bytes 98312 | tf_op jit(solution)/shard_map/ppermute | solution.py:67
  102.0 2.0 %collective-permute-start.54 = (f32[2,256,256]{2,1,0:T(8,128)S(1)}, f32[2,256,256]{2,1,0:T(8,128)S(1)}, u32[]{:S(2)}, u32[]{:S(2)}) collective-permute-start(f32[2,256,256]{2,1,0:T(8,128)S(1)} %get-tuple-element.272.own), channel_id=1, source_target_pairs={{0,16},{1,2},{2,1},{3,19},{4,20},{5,6},{6,5},{7,23},{8,24},{9,10},... | collective-permute-start | bytes 1572872 | tf_op jit(solution)/shard_map/ppermute | solution.py:67
  104.1 1.3 %collective-permute-done.52.got = f32[4,64,128]{2,1,0:T(8,128)S(1)} collective-permute-done((f32[4,64,128]{2,1,0:T(8,128)S(1)}, f32[4,64,128]{2,1,0:T(8,128)S(1)}, u32[]{:S(2)}, u32[]{:S(2)}) %collective-permute-start.52) | collective-permute-done | bytes 131104 | tf_op jit(solution)/shard_map/ppermute | solution.py:67
  105.4 2.4 %collective-permute-start.53 = (f32[2,64,128]{2,1,0:T(8,128)S(1)}, f32[2,64,128]{2,1,0:T(8,128)S(1)}, u32[]{:S(2)}, u32[]{:S(2)}) collective-permute-start(f32[2,64,128]{2,1,0:T(8,128)S(1)} %get-tuple-element.271), channel_id=1, source_target_pairs={{0,0},{1,2},{2,1},{3,3},{4,4},{5,6},{6,5},{7,7},{8,8},{9,10},{10,9... | collective-permute-start | bytes 196616 | tf_op jit(solution)/shard_map/ppermute | solution.py:67
  107.9 1.7 %collective-permute-start.55 = (f32[2,64,128]{2,1,0:T(8,128)S(1)}, f32[2,64,128]{2,1,0:T(8,128)S(1)}, u32[]{:S(2)}, u32[]{:S(2)}) collective-permute-start(f32[2,64,128]{2,1,0:T(8,128)S(1)} %get-tuple-element.275), channel_id=1, source_target_pairs={{0,4},{1,6},{2,5},{3,7},{4,0},{5,2},{6,1},{7,3},{8,12},{9,14},{10,... | collective-permute-start | bytes 196616 | tf_op jit(solution)/shard_map/ppermute | solution.py:67
  110.5 3.1 %collective-permute-start.57 = (f32[2,64,128]{2,1,0:T(8,128)S(1)}, f32[2,64,128]{2,1,0:T(8,128)S(1)}, u32[]{:S(2)}, u32[]{:S(2)}) collective-permute-start(f32[2,64,128]{2,1,0:T(8,128)S(1)} %get-tuple-element.277), channel_id=1, source_target_pairs={{0,12},{1,14},{2,13},{3,15},{4,8},{5,10},{6,9},{7,11},{8,4},{9,6},... | collective-permute-start | bytes 196616 | tf_op jit(solution)/shard_map/ppermute | solution.py:67
  114.5 1.3 %collective-permute-done.56.refs_2_ = f32[2,64,128]{2,1,0:T(8,128)S(1)} collective-permute-done((f32[2,64,128]{2,1,0:T(8,128)S(1)}, f32[2,64,128]{2,1,0:T(8,128)S(1)}, u32[]{:S(2)}, u32[]{:S(2)}) %collective-permute-start.56) | collective-permute-done | bytes 65568 | tf_op jit(solution)/shard_map/ppermute | solution.py:67
  115.8 1.2 %collective-permute-done.57.refs_3_ = f32[2,64,128]{2,1,0:T(8,128)S(1)} collective-permute-done((f32[2,64,128]{2,1,0:T(8,128)S(1)}, f32[2,64,128]{2,1,0:T(8,128)S(1)}, u32[]{:S(2)}, u32[]{:S(2)}) %collective-permute-start.57) | collective-permute-done | bytes 65568 | tf_op jit(solution)/shard_map/ppermute | solution.py:67
  117.0 1.3 %filter.1 = f32[32,32,64]{2,1,0:T(8,128)} custom-call(f32[2,64,128]{2,1,0:T(8,128)S(1)} %collective-permute-done.53.refs_0_, f32[2,64,128]{2,1,0:T(8,128)S(1)} %collective-permute-done.55.refs_1_, f32[2,64,128]{2,1,0:T(8,128)S(1)} %collective-permute-done.56.refs_2_, f32[2,64,128]{2,1,0:T(8,128)S(1)} %collective-permute-done.57.refs_3_), custom_call_target="tpu_custom_call" | custom-call | flops 1000 | bytes 1000 | tf_op jit(solution)/shard_map/filter/pallas_call | solution.py:604
  (150 shorter events, 42.4 us)
Async XLA Ops:
  0.6 10.1 %collective-permute-start.1 = (f32[256,256]{1,0:T(8,128)}, f32[256,256]{1,0:T(8,128)S(1)}, u32[]{:S(2)}, u32[]{:S(2)}) collective-permute-start(f32[256,256]{1,0:T(8,128)} %bitcast.16), channel_id=1, source_target_pairs={{0,16},{1,2},{2,1},{3,19},{4,20},{5,6},{6,5},{7,23},{8,24},{9,10},... | collective-permute-start | bytes 786440 | tf_op jit(solution)/shard_map/ppermute | solution.py:67
  3.3 7.4 %collective-permute-start = (f32[256,256]{1,0:T(8,128)}, f32[256,256]{1,0:T(8,128)S(1)}, u32[]{:S(2)}, u32[]{:S(2)}) collective-permute-start(f32[256,256]{1,0:T(8,128)} %bitcast.14), channel_id=1, source_target_pairs={{0,16},{1,2},{2,1},{3,19},{4,20},{5,6},{6,5},{7,23},{8,24},{9,10},... | collective-permute-start | bytes 786440 | tf_op jit(solution)/shard_map/ppermute | solution.py:67
  4.5 12.4 %collective-permute-start.2 = (f32[2,256,256]{2,1,0:T(8,128)S(1)}, f32[2,256,256]{2,1,0:T(8,128)S(1)}, u32[]{:S(2)}, u32[]{:S(2)}) collective-permute-start(f32[2,256,256]{2,1,0:T(8,128)S(1)} %pad_maximum_fusion), channel_id=1, source_target_pairs={{0,16},{1,2},{2,1},{3,19},{4,20},{5,6},{6,5},{7,23},{8,24},{9,10},... | collective-permute-start | bytes 1572872 | tf_op jit(solution)/shard_map/ppermute | solution.py:67
  10.9 3.0 %collective-permute-start.3 = (f32[2,128,256]{2,1,0:T(8,128)S(1)}, f32[2,128,256]{2,1,0:T(8,128)S(1)}, u32[]{:S(2)}, u32[]{:S(2)}) collective-permute-start(f32[2,128,256]{2,1,0:T(8,128)S(1)} %get-tuple-element.146), channel_id=1, source_target_pairs={{0,1},{1,0},{2,3},{3,2},{4,5},{5,4},{6,7},{7,6},{8,9},{9,8},{10,11... | collective-permute-start | bytes 786440 | tf_op jit(solution)/shard_map/ppermute | solution.py:67
  11.3 6.1 %collective-permute-start.4 = (f32[2,128,256]{2,1,0:T(8,128)S(1)}, f32[2,128,256]{2,1,0:T(8,128)S(1)}, u32[]{:S(2)}, u32[]{:S(2)}) collective-permute-start(f32[2,128,256]{2,1,0:T(8,128)S(1)} %get-tuple-element.155), channel_id=1, source_target_pairs={{0,16},{1,4},{2,18},{3,6},{4,1},{5,8},{6,3},{7,10},{8,5},{9,12},{1... | collective-permute-start | bytes 786440 | tf_op jit(solution)/shard_map/ppermute | solution.py:67
  13.2 4.2 %collective-permute-start.5 = (f32[2,32,256]{2,1,0:T(8,128)S(1)}, f32[2,32,256]{2,1,0:T(8,128)S(1)}, u32[]{:S(2)}, u32[]{:S(2)}) collective-permute-start(f32[2,32,256]{2,1,0:T(8,128)S(1)} %get-tuple-element.156), channel_id=1, source_target_pairs={{0,2},{1,3},{2,0},{3,1},{4,6},{5,7},{6,4},{7,5},{8,10},{9,11},{10,... | collective-permute-start | bytes 196616 | tf_op jit(solution)/shard_map/ppermute | solution.py:67
  14.9 8.5 %collective-permute-start.7 = (f32[256,256]{1,0:T(8,128)S(1)}, f32[256,256]{1,0:T(8,128)S(1)}, u32[]{:S(2)}, u32[]{:S(2)}) collective-permute-start(f32[256,256]{1,0:T(8,128)S(1)} %bitcast.18), channel_id=1, source_target_pairs={{0,16},{1,2},{2,1},{3,19},{4,20},{5,6},{6,5},{7,23},{8,24},{9,10},... | collective-permute-start | bytes 786440 | tf_op jit(solution)/shard_map/ppermute | solution.py:67
  16.1 8.0 %collective-permute-start.8 = (f32[256,256]{1,0:T(8,128)S(1)}, f32[256,256]{1,0:T(8,128)S(1)}, u32[]{:S(2)}, u32[]{:S(2)}) collective-permute-start(f32[256,256]{1,0:T(8,128)S(1)} %bitcast.20), channel_id=1, source_target_pairs={{0,16},{1,2},{2,1},{3,19},{4,20},{5,6},{6,5},{7,23},{8,24},{9,10},... | collective-permute-start | bytes 786440 | tf_op jit(solution)/shard_map/ppermute | solution.py:67
  18.0 4.0 %collective-permute-start.6 = (f32[168,256]{1,0:T(8,128)S(1)}, f32[168,256]{1,0:T(8,128)S(1)}, u32[]{:S(2)}, u32[]{:S(2)}) collective-permute-start(f32[168,256]{1,0:T(8,128)S(1)} %get-tuple-element.165), channel_id=1, source_target_pairs={{0,1},{1,0},{2,3},{3,2},{4,5},{5,4},{6,7},{7,6},{8,9},{9,8},{10,11... | collective-permute-start | bytes 516104 | tf_op jit(solution)/shard_map/ppermute | solution.py:67
  20.1 4.7 %collective-permute-start.9 = (f32[128,256]{1,0:T(8,128)S(1)}, f32[128,256]{1,0:T(8,128)S(1)}, u32[]{:S(2)}, u32[]{:S(2)}) collective-permute-start(f32[128,256]{1,0:T(8,128)S(1)} %get-tuple-element.171), channel_id=1, source_target_pairs={{0,16},{1,4},{2,18},{3,6},{4,1},{5,8},{6,3},{7,10},{8,5},{9,12},{1... | collective-permute-start | bytes 393224 | tf_op jit(solution)/shard_map/ppermute | solution.py:67
  20.2 4.2 %collective-permute-start.10 = (f32[32,256]{1,0:T(8,128)S(1)}, f32[32,256]{1,0:T(8,128)S(1)}, u32[]{:S(2)}, u32[]{:S(2)}) collective-permute-start(f32[32,256]{1,0:T(8,128)S(1)} %get-tuple-element.172), channel_id=1, source_target_pairs={{0,2},{1,3},{2,0},{3,1},{4,6},{5,7},{6,4},{7,5},{8,10},{9,11},{10,... | collective-permute-start | bytes 98312 | tf_op jit(solution)/shard_map/ppermute | solution.py:67
  25.0 3.0 %collective-permute-start.11 = (f32[128,256]{1,0:T(8,128)S(1)}, f32[128,256]{1,0:T(8,128)S(1)}, u32[]{:S(2)}, u32[]{:S(2)}) collective-permute-start(f32[128,256]{1,0:T(8,128)S(1)} %get-tuple-element.175), channel_id=1, source_target_pairs={{0,1},{1,0},{2,3},{3,2},{4,5},{5,4},{6,7},{7,6},{8,9},{9,8},{10,11... | collective-permute-start | bytes 393224 | tf_op jit(solution)/shard_map/ppermute | solution.py:67
  26.8 4.7 %collective-permute-start.12 = (f32[128,256]{1,0:T(8,128)S(1)}, f32[128,256]{1,0:T(8,128)S(1)}, u32[]{:S(2)}, u32[]{:S(2)}) collective-permute-start(f32[128,256]{1,0:T(8,128)S(1)} %get-tuple-element.177), channel_id=1, source_target_pairs={{0,16},{1,4},{2,18},{3,6},{4,1},{5,8},{6,3},{7,10},{8,5},{9,12},{1... | collective-permute-start | bytes 393224 | tf_op jit(solution)/shard_map/ppermute | solution.py:67
  26.8 3.5 %collective-permute-start.13 = (f32[72,256]{1,0:T(8,128)S(1)}, f32[72,256]{1,0:T(8,128)S(1)}, u32[]{:S(2)}, u32[]{:S(2)}) collective-permute-start(f32[72,256]{1,0:T(8,128)S(1)} %get-tuple-element.178), channel_id=1, source_target_pairs={{0,2},{1,3},{2,0},{3,1},{4,6},{5,7},{6,4},{7,5},{8,10},{9,11},{10,... | collective-permute-start | bytes 221192 | tf_op jit(solution)/shard_map/ppermute | solution.py:67
  31.7 3.8 %collective-permute-start.14 = (f32[2,128,256]{2,1,0:T(8,128)S(1)}, f32[2,128,256]{2,1,0:T(8,128)S(1)}, u32[]{:S(2)}, u32[]{:S(2)}) collective-permute-start(f32[2,128,256]{2,1,0:T(8,128)S(1)} %get-tuple-element.182), channel_id=1, source_target_pairs={{0,1},{1,0},{2,3},{3,2},{4,5},{5,4},{6,7},{7,6},{8,9},{9,8},{10,11... | collective-permute-start | bytes 786440 | tf_op jit(solution)/shard_map/ppermute | solution.py:67
  33.6 6.1 %collective-permute-start.15 = (f32[2,128,256]{2,1,0:T(8,128)S(1)}, f32[2,128,256]{2,1,0:T(8,128)S(1)}, u32[]{:S(2)}, u32[]{:S(2)}) collective-permute-start(f32[2,128,256]{2,1,0:T(8,128)S(1)} %get-tuple-element.184), channel_id=1, source_target_pairs={{0,16},{1,4},{2,18},{3,6},{4,1},{5,8},{6,3},{7,10},{8,5},{9,12},{1... | collective-permute-start | bytes 786440 | tf_op jit(solution)/shard_map/ppermute | solution.py:67
  33.6 4.1 %collective-permute-start.16 = (f32[2,32,256]{2,1,0:T(8,128)S(1)}, f32[2,32,256]{2,1,0:T(8,128)S(1)}, u32[]{:S(2)}, u32[]{:S(2)}) collective-permute-start(f32[2,32,256]{2,1,0:T(8,128)S(1)} %get-tuple-element.185), channel_id=1, source_target_pairs={{0,2},{1,3},{2,0},{3,1},{4,6},{5,7},{6,4},{7,5},{8,10},{9,11},{10,... | collective-permute-start | bytes 196616 | tf_op jit(solution)/shard_map/ppermute | solution.py:67
  34.2 3.4 %collective-permute-start.17 = (f32[8,8,128]{2,1,0:T(8,128)S(1)}, f32[8,8,128]{2,1,0:T(8,128)S(1)}, u32[]{:S(2)}, u32[]{:S(2)}) collective-permute-start(f32[8,8,128]{2,1,0:T(8,128)S(1)} %get-tuple-element.187), channel_id=1, source_target_pairs={{0,4},{1,5},{2,6},{3,7},{4,0},{5,1},{6,2},{7,3},{8,12},{9,13},{10,... | collective-permute-start | bytes 98312 | tf_op jit(solution)/shard_map/ppermute | solution.py:67
  39.9 3.3 %collective-permute-start.18 = (f32[128,256]{1,0:T(8,128)S(1)}, f32[128,256]{1,0:T(8,128)S(1)}, u32[]{:S(2)}, u32[]{:S(2)}) collective-permute-start(f32[128,256]{1,0:T(8,128)S(1)} %get-tuple-element.189), channel_id=1, source_target_pairs={{0,1},{1,0},{2,3},{3,2},{4,5},{5,4},{6,7},{7,6},{8,9},{9,8},{10,11... | collective-permute-start | bytes 393224 | tf_op jit(solution)/shard_map/ppermute | solution.py:67
  41.1 4.7 %collective-permute-start.19 = (f32[128,256]{1,0:T(8,128)S(1)}, f32[128,256]{1,0:T(8,128)S(1)}, u32[]{:S(2)}, u32[]{:S(2)}) collective-permute-start(f32[128,256]{1,0:T(8,128)S(1)} %get-tuple-element.191), channel_id=1, source_target_pairs={{0,16},{1,4},{2,18},{3,6},{4,1},{5,8},{6,3},{7,10},{8,5},{9,12},{1... | collective-permute-start | bytes 393224 | tf_op jit(solution)/shard_map/ppermute | solution.py:67
  41.1 3.5 %collective-permute-start.20 = (f32[32,256]{1,0:T(8,128)S(1)}, f32[32,256]{1,0:T(8,128)S(1)}, u32[]{:S(2)}, u32[]{:S(2)}) collective-permute-start(f32[32,256]{1,0:T(8,128)S(1)} %get-tuple-element.192), channel_id=1, source_target_pairs={{0,2},{1,3},{2,0},{3,1},{4,6},{5,7},{6,4},{7,5},{8,10},{9,11},{10,... | collective-permute-start | bytes 98312 | tf_op jit(solution)/shard_map/ppermute | solution.py:67
  41.4 4.1 %collective-permute-start.21 = (f32[8,8,128]{2,1,0:T(8,128)S(1)}, f32[8,8,128]{2,1,0:T(8,128)S(1)}, u32[]{:S(2)}, u32[]{:S(2)}) collective-permute-start(f32[8,8,128]{2,1,0:T(8,128)S(1)} %get-tuple-element.194), channel_id=1, source_target_pairs={{0,8},{1,9},{2,10},{3,11},{4,12},{5,13},{6,14},{7,15},{8,0},{9,1},... | collective-permute-start | bytes 98312 | tf_op jit(solution)/shard_map/ppermute | solution.py:67
  46.0 4.3 %collective-permute-start.22 = (f32[128,256]{1,0:T(8,128)S(1)}, f32[128,256]{1,0:T(8,128)S(1)}, u32[]{:S(2)}, u32[]{:S(2)}) collective-permute-start(f32[128,256]{1,0:T(8,128)S(1)} %get-tuple-element.196), channel_id=1, source_target_pairs={{0,1},{1,0},{2,3},{3,2},{4,5},{5,4},{6,7},{7,6},{8,9},{9,8},{10,11... | collective-permute-start | bytes 393224 | tf_op jit(solution)/shard_map/ppermute | solution.py:67
  47.5 4.7 %collective-permute-start.23 = (f32[128,256]{1,0:T(8,128)S(1)}, f32[128,256]{1,0:T(8,128)S(1)}, u32[]{:S(2)}, u32[]{:S(2)}) collective-permute-start(f32[128,256]{1,0:T(8,128)S(1)} %get-tuple-element.200), channel_id=1, source_target_pairs={{0,16},{1,4},{2,18},{3,6},{4,1},{5,8},{6,3},{7,10},{8,5},{9,12},{1... | collective-permute-start | bytes 393224 | tf_op jit(solution)/shard_map/ppermute | solution.py:67
  48.4 3.3 %collective-permute-start.24 = (f32[32,256]{1,0:T(8,128)S(1)}, f32[32,256]{1,0:T(8,128)S(1)}, u32[]{:S(2)}, u32[]{:S(2)}) collective-permute-start(f32[32,256]{1,0:T(8,128)S(1)} %get-tuple-element.201), channel_id=1, source_target_pairs={{0,2},{1,3},{2,0},{3,1},{4,6},{5,7},{6,4},{7,5},{8,10},{9,11},{10,... | collective-permute-start | bytes 98312 | tf_op jit(solution)/shard_map/ppermute | solution.py:67
  53.2 4.7 %collective-permute-start.26 = (f32[128,256]{1,0:T(8,128)S(1)}, f32[128,256]{1,0:T(8,128)S(1)}, u32[]{:S(2)}, u32[]{:S(2)}) collective-permute-start(f32[128,256]{1,0:T(8,128)S(1)} %get-tuple-element.209), channel_id=1, source_target_pairs={{0,16},{1,4},{2,18},{3,6},{4,1},{5,8},{6,3},{7,10},{8,5},{9,12},{1... | collective-permute-start | bytes 393224 | tf_op jit(solution)/shard_map/ppermute | solution.py:67
  53.6 3.1 %collective-permute-start.27 = (f32[32,256]{1,0:T(8,128)S(1)}, f32[32,256]{1,0:T(8,128)S(1)}, u32[]{:S(2)}, u32[]{:S(2)}) collective-permute-start(f32[32,256]{1,0:T(8,128)S(1)} %get-tuple-element.210), channel_id=1, source_target_pairs={{0,2},{1,3},{2,0},{3,1},{4,6},{5,7},{6,4},{7,5},{8,10},{9,11},{10,... | collective-permute-start | bytes 98312 | tf_op jit(solution)/shard_map/ppermute | solution.py:67
  58.6 4.7 %collective-permute-start.29 = (f32[128,256]{1,0:T(8,128)S(1)}, f32[128,256]{1,0:T(8,128)S(1)}, u32[]{:S(2)}, u32[]{:S(2)}) collective-permute-start(f32[128,256]{1,0:T(8,128)S(1)} %get-tuple-element.214), channel_id=1, source_target_pairs={{0,16},{1,4},{2,18},{3,6},{4,1},{5,8},{6,3},{7,10},{8,5},{9,12},{1... | collective-permute-start | bytes 393224 | tf_op jit(solution)/shard_map/ppermute | solution.py:67
  59.3 3.3 %collective-permute-start.30 = (f32[32,256]{1,0:T(8,128)S(1)}, f32[32,256]{1,0:T(8,128)S(1)}, u32[]{:S(2)}, u32[]{:S(2)}) collective-permute-start(f32[32,256]{1,0:T(8,128)S(1)} %get-tuple-element.215), channel_id=1, source_target_pairs={{0,2},{1,3},{2,0},{3,1},{4,6},{5,7},{6,4},{7,5},{8,10},{9,11},{10,... | collective-permute-start | bytes 98312 | tf_op jit(solution)/shard_map/ppermute | solution.py:67
  64.6 4.7 %collective-permute-start.32 = (f32[128,256]{1,0:T(8,128)S(1)}, f32[128,256]{1,0:T(8,128)S(1)}, u32[]{:S(2)}, u32[]{:S(2)}) collective-permute-start(f32[128,256]{1,0:T(8,128)S(1)} %get-tuple-element.223), channel_id=1, source_target_pairs={{0,16},{1,4},{2,18},{3,6},{4,1},{5,8},{6,3},{7,10},{8,5},{9,12},{1... | collective-permute-start | bytes 393224 | tf_op jit(solution)/shard_map/ppermute | solution.py:67
  65.3 3.3 %collective-permute-start.33 = (f32[32,256]{1,0:T(8,128)S(1)}, f32[32,256]{1,0:T(8,128)S(1)}, u32[]{:S(2)}, u32[]{:S(2)}) collective-permute-start(f32[32,256]{1,0:T(8,128)S(1)} %get-tuple-element.224), channel_id=1, source_target_pairs={{0,2},{1,3},{2,0},{3,1},{4,6},{5,7},{6,4},{7,5},{8,10},{9,11},{10,... | collective-permute-start | bytes 98312 | tf_op jit(solution)/shard_map/ppermute | solution.py:67
  69.9 4.7 %collective-permute-start.35 = (f32[128,256]{1,0:T(8,128)S(1)}, f32[128,256]{1,0:T(8,128)S(1)}, u32[]{:S(2)}, u32[]{:S(2)}) collective-permute-start(f32[128,256]{1,0:T(8,128)S(1)} %get-tuple-element.230), channel_id=1, source_target_pairs={{0,16},{1,4},{2,18},{3,6},{4,1},{5,8},{6,3},{7,10},{8,5},{9,12},{1... | collective-permute-start | bytes 393224 | tf_op jit(solution)/shard_map/ppermute | solution.py:67
  70.6 3.3 %collective-permute-start.36 = (f32[32,256]{1,0:T(8,128)S(1)}, f32[32,256]{1,0:T(8,128)S(1)}, u32[]{:S(2)}, u32[]{:S(2)}) collective-permute-start(f32[32,256]{1,0:T(8,128)S(1)} %get-tuple-element.231), channel_id=1, source_target_pairs={{0,2},{1,3},{2,0},{3,1},{4,6},{5,7},{6,4},{7,5},{8,10},{9,11},{10,... | collective-permute-start | bytes 98312 | tf_op jit(solution)/shard_map/ppermute | solution.py:67
  75.3 4.7 %collective-permute-start.38 = (f32[128,256]{1,0:T(8,128)S(1)}, f32[128,256]{1,0:T(8,128)S(1)}, u32[]{:S(2)}, u32[]{:S(2)}) collective-permute-start(f32[128,256]{1,0:T(8,128)S(1)} %get-tuple-element.237), channel_id=1, source_target_pairs={{0,16},{1,4},{2,18},{3,6},{4,1},{5,8},{6,3},{7,10},{8,5},{9,12},{1... | collective-permute-start | bytes 393224 | tf_op jit(solution)/shard_map/ppermute | solution.py:67
  76.0 3.3 %collective-permute-start.39 = (f32[32,256]{1,0:T(8,128)S(1)}, f32[32,256]{1,0:T(8,128)S(1)}, u32[]{:S(2)}, u32[]{:S(2)}) collective-permute-start(f32[32,256]{1,0:T(8,128)S(1)} %get-tuple-element.238), channel_id=1, source_target_pairs={{0,2},{1,3},{2,0},{3,1},{4,6},{5,7},{6,4},{7,5},{8,10},{9,11},{10,... | collective-permute-start | bytes 98312 | tf_op jit(solution)/shard_map/ppermute | solution.py:67
  80.7 4.7 %collective-permute-start.41 = (f32[128,256]{1,0:T(8,128)S(1)}, f32[128,256]{1,0:T(8,128)S(1)}, u32[]{:S(2)}, u32[]{:S(2)}) collective-permute-start(f32[128,256]{1,0:T(8,128)S(1)} %get-tuple-element.244), channel_id=1, source_target_pairs={{0,16},{1,4},{2,18},{3,6},{4,1},{5,8},{6,3},{7,10},{8,5},{9,12},{1... | collective-permute-start | bytes 393224 | tf_op jit(solution)/shard_map/ppermute | solution.py:67
  81.4 3.3 %collective-permute-start.42 = (f32[32,256]{1,0:T(8,128)S(1)}, f32[32,256]{1,0:T(8,128)S(1)}, u32[]{:S(2)}, u32[]{:S(2)}) collective-permute-start(f32[32,256]{1,0:T(8,128)S(1)} %get-tuple-element.245), channel_id=1, source_target_pairs={{0,2},{1,3},{2,0},{3,1},{4,6},{5,7},{6,4},{7,5},{8,10},{9,11},{10,... | collective-permute-start | bytes 98312 | tf_op jit(solution)/shard_map/ppermute | solution.py:67
  86.1 4.7 %collective-permute-start.44 = (f32[128,256]{1,0:T(8,128)S(1)}, f32[128,256]{1,0:T(8,128)S(1)}, u32[]{:S(2)}, u32[]{:S(2)}) collective-permute-start(f32[128,256]{1,0:T(8,128)S(1)} %get-tuple-element.251), channel_id=1, source_target_pairs={{0,16},{1,4},{2,18},{3,6},{4,1},{5,8},{6,3},{7,10},{8,5},{9,12},{1... | collective-permute-start | bytes 393224 | tf_op jit(solution)/shard_map/ppermute | solution.py:67
  86.8 3.3 %collective-permute-start.45 = (f32[32,256]{1,0:T(8,128)S(1)}, f32[32,256]{1,0:T(8,128)S(1)}, u32[]{:S(2)}, u32[]{:S(2)}) collective-permute-start(f32[32,256]{1,0:T(8,128)S(1)} %get-tuple-element.252), channel_id=1, source_target_pairs={{0,2},{1,3},{2,0},{3,1},{4,6},{5,7},{6,4},{7,5},{8,10},{9,11},{10,... | collective-permute-start | bytes 98312 | tf_op jit(solution)/shard_map/ppermute | solution.py:67
  91.4 4.7 %collective-permute-start.47 = (f32[128,256]{1,0:T(8,128)S(1)}, f32[128,256]{1,0:T(8,128)S(1)}, u32[]{:S(2)}, u32[]{:S(2)}) collective-permute-start(f32[128,256]{1,0:T(8,128)S(1)} %get-tuple-element.258), channel_id=1, source_target_pairs={{0,16},{1,4},{2,18},{3,6},{4,1},{5,8},{6,3},{7,10},{8,5},{9,12},{1... | collective-permute-start | bytes 393224 | tf_op jit(solution)/shard_map/ppermute | solution.py:67
  92.1 3.3 %collective-permute-start.48 = (f32[32,256]{1,0:T(8,128)S(1)}, f32[32,256]{1,0:T(8,128)S(1)}, u32[]{:S(2)}, u32[]{:S(2)}) collective-permute-start(f32[32,256]{1,0:T(8,128)S(1)} %get-tuple-element.259), channel_id=1, source_target_pairs={{0,2},{1,3},{2,0},{3,1},{4,6},{5,7},{6,4},{7,5},{8,10},{9,11},{10,... | collective-permute-start | bytes 98312 | tf_op jit(solution)/shard_map/ppermute | solution.py:67
  96.8 4.7 %collective-permute-start.50 = (f32[128,256]{1,0:T(8,128)S(1)}, f32[128,256]{1,0:T(8,128)S(1)}, u32[]{:S(2)}, u32[]{:S(2)}) collective-permute-start(f32[128,256]{1,0:T(8,128)S(1)} %get-tuple-element.265), channel_id=1, source_target_pairs={{0,16},{1,4},{2,18},{3,6},{4,1},{5,8},{6,3},{7,10},{8,5},{9,12},{1... | collective-permute-start | bytes 393224 | tf_op jit(solution)/shard_map/ppermute | solution.py:67
  97.5 3.3 %collective-permute-start.51 = (f32[32,256]{1,0:T(8,128)S(1)}, f32[32,256]{1,0:T(8,128)S(1)}, u32[]{:S(2)}, u32[]{:S(2)}) collective-permute-start(f32[32,256]{1,0:T(8,128)S(1)} %get-tuple-element.266), channel_id=1, source_target_pairs={{0,2},{1,3},{2,0},{3,1},{4,6},{5,7},{6,4},{7,5},{8,10},{9,11},{10,... | collective-permute-start | bytes 98312 | tf_op jit(solution)/shard_map/ppermute | solution.py:67
  102.0 11.6 %collective-permute-start.54 = (f32[2,256,256]{2,1,0:T(8,128)S(1)}, f32[2,256,256]{2,1,0:T(8,128)S(1)}, u32[]{:S(2)}, u32[]{:S(2)}) collective-permute-start(f32[2,256,256]{2,1,0:T(8,128)S(1)} %get-tuple-element.272.own), channel_id=1, source_target_pairs={{0,16},{1,2},{2,1},{3,19},{4,20},{5,6},{6,5},{7,23},{8,24},{9,10},... | collective-permute-start | bytes 1572872 | tf_op jit(solution)/shard_map/ppermute | solution.py:67
  105.4 9.0 %collective-permute-start.53 = (f32[2,64,128]{2,1,0:T(8,128)S(1)}, f32[2,64,128]{2,1,0:T(8,128)S(1)}, u32[]{:S(2)}, u32[]{:S(2)}) collective-permute-start(f32[2,64,128]{2,1,0:T(8,128)S(1)} %get-tuple-element.271), channel_id=1, source_target_pairs={{0,0},{1,2},{2,1},{3,3},{4,4},{5,6},{6,5},{7,7},{8,8},{9,10},{10,9... | collective-permute-start | bytes 196616 | tf_op jit(solution)/shard_map/ppermute | solution.py:67
  107.9 6.6 %collective-permute-start.55 = (f32[2,64,128]{2,1,0:T(8,128)S(1)}, f32[2,64,128]{2,1,0:T(8,128)S(1)}, u32[]{:S(2)}, u32[]{:S(2)}) collective-permute-start(f32[2,64,128]{2,1,0:T(8,128)S(1)} %get-tuple-element.275), channel_id=1, source_target_pairs={{0,4},{1,6},{2,5},{3,7},{4,0},{5,2},{6,1},{7,3},{8,12},{9,14},{10,... | collective-permute-start | bytes 196616 | tf_op jit(solution)/shard_map/ppermute | solution.py:67
  109.6 6.2 %collective-permute-start.56 = (f32[2,64,128]{2,1,0:T(8,128)S(1)}, f32[2,64,128]{2,1,0:T(8,128)S(1)}, u32[]{:S(2)}, u32[]{:S(2)}) collective-permute-start(f32[2,64,128]{2,1,0:T(8,128)S(1)} %get-tuple-element.276), channel_id=1, source_target_pairs={{0,8},{1,10},{2,9},{3,11},{4,12},{5,14},{6,13},{7,15},{8,0},{9,2},... | collective-permute-start | bytes 196616 | tf_op jit(solution)/shard_map/ppermute | solution.py:67
  110.5 6.5 %collective-permute-start.57 = (f32[2,64,128]{2,1,0:T(8,128)S(1)}, f32[2,64,128]{2,1,0:T(8,128)S(1)}, u32[]{:S(2)}, u32[]{:S(2)}) collective-permute-start(f32[2,64,128]{2,1,0:T(8,128)S(1)} %get-tuple-element.277), channel_id=1, source_target_pairs={{0,12},{1,14},{2,13},{3,15},{4,8},{5,10},{6,9},{7,11},{8,4},{9,6},... | collective-permute-start | bytes 196616 | tf_op jit(solution)/shard_map/ppermute | solution.py:67
  (28 other events, 72.9 us)

commit v16 on v15

--- a/solution.py
+++ b/solution.py
@@ -249,10 +249,9 @@
         out[half:] = c_side
 
 
-def settle_kernel(flags, a, b, recv_a, recv_b, a_out, b_out, zo, co, yo, sems):
-    choose(flags, [(a, recv_a, a_out), (b, recv_b, b_out)], sems)
-    for n, out in enumerate((a_out, b_out)):
-        rims(flags, out, zo.at[n], co.at[n], yo.at[n])
+def settle_kernel(flags, a, recv, out, zo, co, yo, sems):
+    choose(flags, [(a, recv, out)], sems)
+    rims(flags, out, zo, co, yo)
 
 
 def settle_pair_kernel(flags, a, b, *rest):
@@ -267,30 +266,30 @@
         out[...] = jnp.where(keep, own[n], recv[n])
 
 
-def first_inner_kernel(flags, lr, cur, cm, near, deep, *outs):
+def first_inner_kernel(flags, lr, cur, lr_cm, cm, near, deep, *outs):
     ri, rx, rz, sums_out, di_out, dx_out, dz_out = outs
-    for here, spare, spare_z, di, dx, dz in inner_differences(lr, cm.at[0], near, deep):
+    for here, spare, spare_z, di, dx, dz in inner_differences(lr, lr_cm, near, deep):
         ri[here], rx[here], rz[here] = di, dx, dz
-    for here, sums, sums_z, di, dx, dz in inner_differences(cur, cm.at[1], near, deep):
+    for here, sums, sums_z, di, dx, dz in inner_differences(cur, cm, near, deep):
         sums_out[here] = sums + sums_z + (3.0 * SECOND[0] * 5040) * cur[here]
         di_out[here], dx_out[here], dz_out[here] = di, dx, dz
 
 
-def first_outer_kernel(flags, cur, prev, vel, ri, rx, rz, sums, di, dx, dz, inj, zm, ym, side,
-                       edge, give, cells, new, zo, co, yo, k0, ki, kx, kz):
+def first_outer_kernel(flags, cur, prev, vel, ri, rx, rz, sums, di, dx, dz, inj, lr_zm, lr_ym, zm, ym,
+                       side, edge, give, cells, new, zo, co, yo, k0, ki, kx, kz):
     size = cur.shape[0]
     half = size // 2
     kz[...], ki[...], kx[...] = sums[...], di[...], dx[...]
     k0[...], new[...] = ri[...], rx[...]
-    more, more_x = side_differences(zm.at[1], side)
+    more, more_x = side_differences(zm, side)
     kz[0:half] += more
     kx[0:half] += more_x
-    spare, more_x = side_differences(zm.at[0], side)
+    spare, more_x = side_differences(lr_zm, side)
     new[0:half] += more_x
-    for here, more, more_i in edge_differences(flags, size, ym.at[1], edge):
+    for here, more, more_i in edge_differences(flags, size, ym, edge):
         kz[here] += more
         ki[here] += more_i
-    for here, spare, more_i in edge_differences(flags, size, ym.at[0], edge):
+    for here, spare, more_i in edge_differences(flags, size, lr_ym, edge):
         k0[here] += more_i
     for n in range(4):
         here = slice(n * (size // 4), (n + 1) * (size // 4))
@@ -557,6 +556,7 @@
 
 def filter_kernel(flags, *refs):
     *pieces, out = refs
+    pieces = pieces[::-1]
     height, lanes = pieces[0].shape[1:]
     chunk, rows, full = out.shape
     groups = lanes // chunk
@@ -656,21 +656,23 @@
 
     log_density, fwd_now, velocity = flat(log_density), flat(fwd_now), flat(velocity)
     fwd_before, adj_now, adj_before = flat(fwd_before), flat(adj_now), flat(adj_before)
-    got = [send(v, swap_perm) for v in (log_density, fwd_now)]
+    got_density = send(log_density, swap_perm)
     stacked = jnp.stack([velocity, fwd_before])
+    got_now = send(after(fwd_now, stacked), swap_perm)
     got_model = send(stacked, swap_perm)
     full = nx * cols
     inj, = call(functools.partial(source_kernel, 0, full), "source", [field], src_cell, wavelet,
                 weight=0.7, scalars=2)
-    got[0], inj = lax.optimization_barrier((got[0], inj))
-    density, p_now, *out = call(settle_kernel, "settle",
-                                [field, field] + [shaped(2, *r.shape) for r in rim],
-                                log_density, fwd_now, *got, far=2)
+    got_density, inj = lax.optimization_barrier((got_density, inj))
+    density, *out = call(settle_kernel, "settle_density", [field] + rim, log_density, got_density,
+                         weight=0.2, far=1)
+    lr_zm, lr_cm, lr_ym = halo(*out)
+    p_now, *out = call(settle_kernel, "settle", [field] + rim, fwd_now, got_now, weight=0.2, far=1)
     zm, cm, ym = halo(*out)
     vel, p_before = call(settle_pair_kernel, "settle_model", [field, field],
                          velocity, fwd_before, got_model, weight=0.6, far=2)
-    parts = call(first_inner_kernel, "first_inner", [field] * 7, density, p_now, cm,
-                 near, deep, weight=1.3)
+    parts = call(first_inner_kernel, "first_inner", [field] * 7, density, p_now, lr_cm, cm, near,
+                 deep, weight=0.8)
     got_adjoint = [send(after(v, parts[0]), swap_perm) for v in (adj_now, adj_before)]
 
     slots = subs * CAP
@@ -686,7 +688,7 @@
 
     new, zo, co, yo, k0, ki, kx, kz = call(
         first_outer_kernel, "first_outer", [field, rim[0], core_rim, rim[2]] + [field] * 4,
-        p_now, p_before, vel, *parts, inj, zm, ym, side, edge, give, cells)
+        p_now, p_before, vel, *parts, inj, lr_zm, lr_ym, zm, ym, side, edge, give, cells)
     model = (k0, ki, kx, kz)
     states = [p_before, p_now, new]
     changes = []
@@ -781,7 +783,7 @@
     pieces = [send(pieces[s], plan.spread(s)) for s in reversed(range(nq))][::-1]
     adj_prev, adj_out = call(select_kernel, "select", [field, field], final, got, weight=1.2)
     gradient, = call(filter_kernel, "filter", [shaped(chunk, rows, nx * cols)],
-                     after(pieces[0], adj_out), *pieces[1:])
+                     after(pieces[-1], adj_out), *pieces[-2::-1])
     block = (rows, cols, depth)
     return gradient, adj_out.reshape(block), adj_prev.reshape(block)
 

time: 118 us -> 124 us (1.051)
  waiting for transfers between devices: 25.1 us -> 41.9 us
  starting transfers between devices: 62.3 us -> 52 us
    ppermute x58 -> x61, waiting for transfers between devices: 25.1 us -> 41.9 us  [send(): return lax.ppermute(value, ALL, pairs)]
    ppermute x58 -> x61, starting transfers between devices: 62.3 us -> 52 us  [send(): return lax.ppermute(value, ALL, pairs)]
    pallas_call x40 -> x41, Pallas kernels: 26.8 us -> 26.5 us  [call(): pl.pallas_call(functools.partial(kernel, Flags()), name=name, out_shape=o...]
  transfers between devices with their start and end apart: 58 -> 61, of which waited for: 33 -> 31; matrix products, arithmetic and copies ran while one was open for 1% -> 1% of each run, Pallas kernels for 18% -> 17%
where the time goes in v16:
time: 124 us
  starting transfers between devices  52 us (42%)
  waiting for transfers between devices  41.9 us (34%)
  Pallas kernels  26.5 us (21%)
  between operations  1.26 us (1%)
  other arithmetic  1.25 us (1%)
    ppermute x61, starting transfers between devices, send(): return lax.ppermute(value, ALL, pairs)  52 us
    ppermute x61, waiting for transfers between devices, send(): return lax.ppermute(value, ALL, pairs)  41.9 us
    pallas_call x41, Pallas kernels, call(): pl.pallas_call(functools.partial(kernel, Flags()), name=name, out_shape=o...  26.5 us
  transfers between devices with their start and end apart: 61, of which 31 were waited for; matrix products, arithmetic and copies ran while one was open for 1% of the time, Pallas kernels for 17%

profile of v16, /device:TPU:1, one launch (start us, length us, event | category | flops | bytes accessed | tf_op | source)
XLA Modules:
  0.0 123.7 jit_solution(14947066973715883690)
XLA Ops:
  0.6 2.7 %collective-permute-start.2 = (f32[256,256]{1,0:T(8,128)}, f32[256,256]{1,0:T(8,128)S(1)}, u32[]{:S(2)}, u32[]{:S(2)}) collective-permute-start(f32[256,256]{1,0:T(8,128)} %bitcast.14), channel_id=1, source_target_pairs={{0,16},{1,2},{2,1},{3,19},{4,20},{5,6},{6,5},{7,23},{8,24},{9,10},... | collective-permute-start | bytes 786440 | tf_op jit(solution)/shard_map/ppermute | solution.py:67
  3.3 1.1 pad_maximum_fusion
  4.6 1.7 %collective-permute-start = (f32[256,256]{1,0:T(8,128)S(1)}, f32[256,256]{1,0:T(8,128)S(1)}, u32[]{:S(2)}, u32[]{:S(2)}) collective-permute-start(f32[256,256]{1,0:T(8,128)S(1)} %bitcast.16), channel_id=1, source_target_pairs={{0,16},{1,2},{2,1},{3,19},{4,20},{5,6},{6,5},{7,23},{8,24},{9,10},... | collective-permute-start | bytes 786440 | tf_op jit(solution)/shard_map/ppermute | solution.py:67
  8.9 7.4 %collective-permute-done.recv = f32[256,256]{1,0:T(8,128)S(1)} collective-permute-done((f32[256,256]{1,0:T(8,128)S(1)}, f32[256,256]{1,0:T(8,128)S(1)}, u32[]{:S(2)}, u32[]{:S(2)}) %collective-permute-start) | collective-permute-done | bytes 262176 | tf_op jit(solution)/shard_map/ppermute | solution.py:67
  17.1 1.1 collective-permute-start.6
  18.1 1.5 %collective-permute-start.5 = (f32[128,256]{1,0:T(8,128)S(1)}, f32[128,256]{1,0:T(8,128)S(1)}, u32[]{:S(2)}, u32[]{:S(2)}) collective-permute-start(f32[128,256]{1,0:T(8,128)S(1)} %get-tuple-element.161), channel_id=1, source_target_pairs={{0,16},{1,4},{2,18},{3,6},{4,1},{5,8},{6,3},{7,10},{8,5},{9,12},{1... | collective-permute-start | bytes 393224 | tf_op jit(solution)/shard_map/ppermute | solution.py:67
  21.5 1.6 %collective-permute-start.10 = (f32[256,256]{1,0:T(8,128)S(1)}, f32[256,256]{1,0:T(8,128)S(1)}, u32[]{:S(2)}, u32[]{:S(2)}) collective-permute-start(f32[256,256]{1,0:T(8,128)S(1)} %bitcast.18), channel_id=1, source_target_pairs={{0,16},{1,2},{2,1},{3,19},{4,20},{5,6},{6,5},{7,23},{8,24},{9,10},... | collective-permute-start | bytes 786440 | tf_op jit(solution)/shard_map/ppermute | solution.py:67
  25.5 1.2 collective-permute-start.12
  27.6 3.2 %collective-permute-done.11.rest_1_ = f32[256,256]{1,0:T(8,128)S(1)} collective-permute-done((f32[256,256]{1,0:T(8,128)S(1)}, f32[256,256]{1,0:T(8,128)S(1)}, u32[]{:S(2)}, u32[]{:S(2)}) %collective-permute-start.11) | collective-permute-done | bytes 262176 | tf_op jit(solution)/shard_map/ppermute | solution.py:67
  31.0 1.4 %forward_inner.7 = (f32[256,256]{1,0:T(8,128)S(1)}, f32[256,256]{1,0:T(8,128)S(1)}) custom-call(s32[16]{0:T(128)S(1)} %copy-done.8, f32[8,16]{1,0:T(8,128)S(1)} %copy-done.3, f32[256,256]{1,0:T(8,128)S(1)} %get-tuple-element.168.cur.prev.before.state, f32[256,256]{1,0:T(8,128)S(1)} %get-tuple-element.146.cur.prev.before, ...), custom_call_target="tpu_custom_call" | custom-call | flops 1000 | bytes 4321000 | tf_op jit(solution)/shard_map/forward_inner/pallas_call | solution.py:604
  33.5 1.3 %collective-permute-start.15 = (f32[128,256]{1,0:T(8,128)S(1)}, f32[128,256]{1,0:T(8,128)S(1)}, u32[]{:S(2)}, u32[]{:S(2)}) collective-permute-start(f32[128,256]{1,0:T(8,128)S(1)} %get-tuple-element.185), channel_id=1, source_target_pairs={{0,16},{1,4},{2,18},{3,6},{4,1},{5,8},{6,3},{7,10},{8,5},{9,12},{1... | collective-permute-start | bytes 393224 | tf_op jit(solution)/shard_map/ppermute | solution.py:67
  35.2 1.4 %forward_inner.8 = (f32[256,256]{1,0:T(8,128)S(1)}, f32[256,256]{1,0:T(8,128)S(1)}) custom-call(s32[16]{0:T(128)S(1)} %copy-done.8, f32[8,16]{1,0:T(8,128)S(1)} %copy-done.3, f32[256,256]{1,0:T(8,128)S(1)} %get-tuple-element.182.cur.prev.before.state, f32[256,256]{1,0:T(8,128)S(1)} %get-tuple-element.168.cur.prev.before.state, ...), custom_call_target="tpu_custom_call" | custom-call | flops 1000 | bytes 4321000 | tf_op jit(solution)/shard_map/forward_inner/pallas_call | solution.py:604
  36.6 1.5 %collective-permute-done.16.ym = f32[72,256]{1,0:T(8,128)S(1)} collective-permute-done((f32[72,256]{1,0:T(8,128)S(1)}, f32[72,256]{1,0:T(8,128)S(1)}, u32[]{:S(2)}, u32[]{:S(2)}) %collective-permute-start.16) | collective-permute-done | bytes 73760 | tf_op jit(solution)/shard_map/ppermute | solution.py:67
  38.4 1.7 %collective-permute-start.17 = (f32[2,128,256]{2,1,0:T(8,128)S(1)}, f32[2,128,256]{2,1,0:T(8,128)S(1)}, u32[]{:S(2)}, u32[]{:S(2)}) collective-permute-start(f32[2,128,256]{2,1,0:T(8,128)S(1)} %get-tuple-element.190), channel_id=1, source_target_pairs={{0,1},{1,0},{2,3},{3,2},{4,5},{5,4},{6,7},{7,6},{8,9},{9,8},{10,11... | collective-permute-start | bytes 786440 | tf_op jit(solution)/shard_map/ppermute | solution.py:67
  40.5 1.0 collective-permute-start.19
  41.5 1.2 collective-permute-start.20
  42.7 1.4 %forward_inner.9 = (f32[256,256]{1,0:T(8,128)S(1)}, f32[256,256]{1,0:T(8,128)S(1)}) custom-call(s32[16]{0:T(128)S(1)} %copy-done.8, f32[8,16]{1,0:T(8,128)S(1)} %copy-done.3, f32[256,256]{1,0:T(8,128)S(1)} %get-tuple-element.189.cur.prev.before.state, f32[256,256]{1,0:T(8,128)S(1)} %get-tuple-element.182.cur.prev.before.state, ...), custom_call_target="tpu_custom_call" | custom-call | flops 1000 | bytes 4321000 | tf_op jit(solution)/shard_map/forward_inner/pallas_call | solution.py:604
  44.8 1.3 %collective-permute-done.18.zm.u_zm = f32[2,128,256]{2,1,0:T(8,128)S(1)} collective-permute-done((f32[2,128,256]{2,1,0:T(8,128)S(1)}, f32[2,128,256]{2,1,0:T(8,128)S(1)}, u32[]{:S(2)}, u32[]{:S(2)}) %collective-permute-start.18) | collective-permute-done | bytes 262176 | tf_op jit(solution)/shard_map/ppermute | solution.py:67
  46.4 1.1 collective-permute-start.21
  48.3 2.2 %collective-permute-start.24 = (f32[8,8,128]{2,1,0:T(8,128)S(1)}, f32[8,8,128]{2,1,0:T(8,128)S(1)}, u32[]{:S(2)}, u32[]{:S(2)}) collective-permute-start(f32[8,8,128]{2,1,0:T(8,128)S(1)} %get-tuple-element.202), channel_id=1, source_target_pairs={{0,8},{1,9},{2,10},{3,11},{4,12},{5,13},{6,14},{7,15},{8,0},{9,1},... | collective-permute-start | bytes 98312 | tf_op jit(solution)/shard_map/ppermute | solution.py:67
  50.5 1.4 %forward_inner.10 = (f32[256,256]{1,0:T(8,128)S(1)}, f32[256,256]{1,0:T(8,128)S(1)}) custom-call(s32[16]{0:T(128)S(1)} %copy-done.8, f32[8,16]{1,0:T(8,128)S(1)} %copy-done.3, f32[256,256]{1,0:T(8,128)S(1)} %get-tuple-element.196.cur.prev.before.state, f32[256,256]{1,0:T(8,128)S(1)} %get-tuple-element.189.cur.prev.before.state, ...), custom_call_target="tpu_custom_call" | custom-call | flops 1000 | bytes 4321000 | tf_op jit(solution)/shard_map/forward_inner/pallas_call | solution.py:604
  52.5 2.2 %collective-permute-start.25 = (f32[128,256]{1,0:T(8,128)S(1)}, f32[128,256]{1,0:T(8,128)S(1)}, u32[]{:S(2)}, u32[]{:S(2)}) collective-permute-start(f32[128,256]{1,0:T(8,128)S(1)} %get-tuple-element.204), channel_id=1, source_target_pairs={{0,1},{1,0},{2,3},{3,2},{4,5},{5,4},{6,7},{7,6},{8,9},{9,8},{10,11... | collective-permute-start | bytes 393224 | tf_op jit(solution)/shard_map/ppermute | solution.py:67
  56.8 1.4 %forward_inner.11 = (f32[256,256]{1,0:T(8,128)S(1)}, f32[256,256]{1,0:T(8,128)S(1)}) custom-call(s32[16]{0:T(128)S(1)} %copy-done.8, f32[8,16]{1,0:T(8,128)S(1)} %copy-done.3, f32[256,256]{1,0:T(8,128)S(1)} %get-tuple-element.203.cur.prev.before.state, f32[256,256]{1,0:T(8,128)S(1)} %get-tuple-element.196.cur.prev.before.state, ...), custom_call_target="tpu_custom_call" | custom-call | flops 1000 | bytes 4321000 | tf_op jit(solution)/shard_map/forward_inner/pallas_call | solution.py:604
  61.6 1.4 %forward_inner.12 = (f32[256,256]{1,0:T(8,128)S(1)}, f32[256,256]{1,0:T(8,128)S(1)}) custom-call(s32[16]{0:T(128)S(1)} %copy-done.8, f32[8,16]{1,0:T(8,128)S(1)} %copy-done.3, f32[256,256]{1,0:T(8,128)S(1)} %get-tuple-element.210.cur.prev.rest_2_.state, f32[256,256]{1,0:T(8,128)S(1)} %get-tuple-element.203.cur.prev.before.state, ...), custom_call_target="tpu_custom_call" | custom-call | flops 1000 | bytes 4321000 | tf_op jit(solution)/shard_map/forward_inner/pallas_call | solution.py:604
  63.9 1.1 collective-permute-done.29.zm
  66.8 1.4 %forward_inner.13 = (f32[256,256]{1,0:T(8,128)S(1)}, f32[256,256]{1,0:T(8,128)S(1)}) custom-call(s32[16]{0:T(128)S(1)} %copy-done.8, f32[8,16]{1,0:T(8,128)S(1)} %copy-done.3, f32[256,256]{1,0:T(8,128)S(1)} %get-tuple-element.219.cur.state.rest_1_, f32[256,256]{1,0:T(8,128)S(1)} %get-tuple-element.210.cur.prev.rest_2_.state, ...), custom_call_target="tpu_custom_call" | custom-call | flops 1000 | bytes 4321000 | tf_op jit(solution)/shard_map/forward_inner/pallas_call | solution.py:604
  68.2 1.2 %collective-permute-done.33.ym = f32[32,256]{1,0:T(8,128)S(1)} collective-permute-done((f32[32,256]{1,0:T(8,128)S(1)}, f32[32,256]{1,0:T(8,128)S(1)}, u32[]{:S(2)}, u32[]{:S(2)}) %collective-permute-start.33) | collective-permute-done | bytes 32800 | tf_op jit(solution)/shard_map/ppermute | solution.py:67
  72.9 1.0 adjoint_inner.7
  73.9 1.6 %collective-permute-done.36.ym = f32[32,256]{1,0:T(8,128)S(1)} collective-permute-done((f32[32,256]{1,0:T(8,128)S(1)}, f32[32,256]{1,0:T(8,128)S(1)}, u32[]{:S(2)}, u32[]{:S(2)}) %collective-permute-start.36) | collective-permute-done | bytes 32800 | tf_op jit(solution)/shard_map/ppermute | solution.py:67
  78.2 1.0 adjoint_inner.8
  79.2 1.6 %collective-permute-done.39.ym = f32[32,256]{1,0:T(8,128)S(1)} collective-permute-done((f32[32,256]{1,0:T(8,128)S(1)}, f32[32,256]{1,0:T(8,128)S(1)}, u32[]{:S(2)}, u32[]{:S(2)}) %collective-permute-start.39) | collective-permute-done | bytes 32800 | tf_op jit(solution)/shard_map/ppermute | solution.py:67
  83.6 1.0 adjoint_inner.9
  84.6 1.6 %collective-permute-done.42.ym = f32[32,256]{1,0:T(8,128)S(1)} collective-permute-done((f32[32,256]{1,0:T(8,128)S(1)}, f32[32,256]{1,0:T(8,128)S(1)}, u32[]{:S(2)}, u32[]{:S(2)}) %collective-permute-start.42) | collective-permute-done | bytes 32800 | tf_op jit(solution)/shard_map/ppermute | solution.py:67
  89.0 1.0 adjoint_inner.10
  90.0 1.6 %collective-permute-done.45.ym = f32[32,256]{1,0:T(8,128)S(1)} collective-permute-done((f32[32,256]{1,0:T(8,128)S(1)}, f32[32,256]{1,0:T(8,128)S(1)}, u32[]{:S(2)}, u32[]{:S(2)}) %collective-permute-start.45) | collective-permute-done | bytes 32800 | tf_op jit(solution)/shard_map/ppermute | solution.py:67
  94.3 1.0 adjoint_inner.11
  95.3 1.6 %collective-permute-done.48.ym = f32[32,256]{1,0:T(8,128)S(1)} collective-permute-done((f32[32,256]{1,0:T(8,128)S(1)}, f32[32,256]{1,0:T(8,128)S(1)}, u32[]{:S(2)}, u32[]{:S(2)}) %collective-permute-start.48) | collective-permute-done | bytes 32800 | tf_op jit(solution)/shard_map/ppermute | solution.py:67
  99.7 1.0 adjoint_inner.12
  100.7 1.6 %collective-permute-done.51.ym = f32[32,256]{1,0:T(8,128)S(1)} collective-permute-done((f32[32,256]{1,0:T(8,128)S(1)}, f32[32,256]{1,0:T(8,128)S(1)}, u32[]{:S(2)}, u32[]{:S(2)}) %collective-permute-start.51) | collective-permute-done | bytes 32800 | tf_op jit(solution)/shard_map/ppermute | solution.py:67
  105.1 1.0 adjoint_inner.13
  106.1 1.6 %collective-permute-done.54.ym = f32[32,256]{1,0:T(8,128)S(1)} collective-permute-done((f32[32,256]{1,0:T(8,128)S(1)}, f32[32,256]{1,0:T(8,128)S(1)}, u32[]{:S(2)}, u32[]{:S(2)}) %collective-permute-start.54) | collective-permute-done | bytes 32800 | tf_op jit(solution)/shard_map/ppermute | solution.py:67
  110.7 1.0 collective-permute-done.55.got
  111.7 1.4 %collective-permute-start.56 = (f32[2,64,128]{2,1,0:T(8,128)S(1)}, f32[2,64,128]{2,1,0:T(8,128)S(1)}, u32[]{:S(2)}, u32[]{:S(2)}) collective-permute-start(f32[2,64,128]{2,1,0:T(8,128)S(1)} %get-tuple-element.279), channel_id=1, source_target_pairs={{0,12},{1,14},{2,13},{3,15},{4,8},{5,10},{6,9},{7,11},{8,4},{9,6},... | collective-permute-start | bytes 196616 | tf_op jit(solution)/shard_map/ppermute | solution.py:67
  113.1 1.8 %collective-permute-start.58 = (f32[2,64,128]{2,1,0:T(8,128)S(1)}, f32[2,64,128]{2,1,0:T(8,128)S(1)}, u32[]{:S(2)}, u32[]{:S(2)}) collective-permute-start(f32[2,64,128]{2,1,0:T(8,128)S(1)} %get-tuple-element.283), channel_id=1, source_target_pairs={{0,8},{1,10},{2,9},{3,11},{4,12},{5,14},{6,13},{7,15},{8,0},{9,2},... | collective-permute-start | bytes 196616 | tf_op jit(solution)/shard_map/ppermute | solution.py:67
  114.8 2.1 %collective-permute-start.59 = (f32[2,64,128]{2,1,0:T(8,128)S(1)}, f32[2,64,128]{2,1,0:T(8,128)S(1)}, u32[]{:S(2)}, u32[]{:S(2)}) collective-permute-start(f32[2,64,128]{2,1,0:T(8,128)S(1)} %get-tuple-element.284), channel_id=1, source_target_pairs={{0,4},{1,6},{2,5},{3,7},{4,0},{5,2},{6,1},{7,3},{8,12},{9,14},{10,... | collective-permute-start | bytes 196616 | tf_op jit(solution)/shard_map/ppermute | solution.py:67
  116.9 3.0 %collective-permute-start.60 = (f32[2,64,128]{2,1,0:T(8,128)S(1)}, f32[2,64,128]{2,1,0:T(8,128)S(1)}, u32[]{:S(2)}, u32[]{:S(2)}) collective-permute-start(f32[2,64,128]{2,1,0:T(8,128)S(1)} %get-tuple-element.285), channel_id=1, source_target_pairs={{0,0},{1,2},{2,1},{3,3},{4,4},{5,6},{6,5},{7,7},{8,8},{9,10},{10,9... | collective-permute-start | bytes 196616 | tf_op jit(solution)/shard_map/ppermute | solution.py:67
  121.0 1.5 %collective-permute-done.60.refs_3_ = f32[2,64,128]{2,1,0:T(8,128)S(1)} collective-permute-done((f32[2,64,128]{2,1,0:T(8,128)S(1)}, f32[2,64,128]{2,1,0:T(8,128)S(1)}, u32[]{:S(2)}, u32[]{:S(2)}) %collective-permute-start.60) | collective-permute-done | bytes 65568 | tf_op jit(solution)/shard_map/ppermute | solution.py:67
  122.4 1.3 %filter.1 = f32[32,32,64]{2,1,0:T(8,128)} custom-call(f32[2,64,128]{2,1,0:T(8,128)S(1)} %collective-permute-done.56.refs_0_, f32[2,64,128]{2,1,0:T(8,128)S(1)} %collective-permute-done.58.refs_1_, f32[2,64,128]{2,1,0:T(8,128)S(1)} %collective-permute-done.59.refs_2_, f32[2,64,128]{2,1,0:T(8,128)S(1)} %collective-permute-done.60.refs_3_), custom_call_target="tpu_custom_call" | custom-call | flops 1000 | bytes 1000 | tf_op jit(solution)/shard_map/filter/pallas_call | solution.py:604
  (157 shorter events, 45.2 us)
Async XLA Ops:
  0.6 7.4 %collective-permute-start.2 = (f32[256,256]{1,0:T(8,128)}, f32[256,256]{1,0:T(8,128)S(1)}, u32[]{:S(2)}, u32[]{:S(2)}) collective-permute-start(f32[256,256]{1,0:T(8,128)} %bitcast.14), channel_id=1, source_target_pairs={{0,16},{1,2},{2,1},{3,19},{4,20},{5,6},{6,5},{7,23},{8,24},{9,10},... | collective-permute-start | bytes 786440 | tf_op jit(solution)/shard_map/ppermute | solution.py:67
  4.5 18.7 %collective-permute-start.1 = (f32[2,256,256]{2,1,0:T(8,128)S(1)}, f32[2,256,256]{2,1,0:T(8,128)S(1)}, u32[]{:S(2)}, u32[]{:S(2)}) collective-permute-start(f32[2,256,256]{2,1,0:T(8,128)S(1)} %pad_maximum_fusion), channel_id=1, source_target_pairs={{0,16},{1,2},{2,1},{3,19},{4,20},{5,6},{6,5},{7,23},{8,24},{9,10},... | collective-permute-start | bytes 1572872 | tf_op jit(solution)/shard_map/ppermute | solution.py:67
  4.6 11.7 %collective-permute-start = (f32[256,256]{1,0:T(8,128)S(1)}, f32[256,256]{1,0:T(8,128)S(1)}, u32[]{:S(2)}, u32[]{:S(2)}) collective-permute-start(f32[256,256]{1,0:T(8,128)S(1)} %bitcast.16), channel_id=1, source_target_pairs={{0,16},{1,2},{2,1},{3,19},{4,20},{5,6},{6,5},{7,23},{8,24},{9,10},... | collective-permute-start | bytes 786440 | tf_op jit(solution)/shard_map/ppermute | solution.py:67
  8.2 11.4 %collective-permute-start.3 = (f32[128,256]{1,0:T(8,128)S(1)}, f32[128,256]{1,0:T(8,128)S(1)}, u32[]{:S(2)}, u32[]{:S(2)}) collective-permute-start(f32[128,256]{1,0:T(8,128)S(1)} %get-tuple-element.151), channel_id=1, source_target_pairs={{0,1},{1,0},{2,3},{3,2},{4,5},{5,4},{6,7},{7,6},{8,9},{9,8},{10,11... | collective-permute-start | bytes 393224 | tf_op jit(solution)/shard_map/ppermute | solution.py:67
  16.4 3.5 %collective-permute-start.4 = (f32[128,256]{1,0:T(8,128)S(1)}, f32[128,256]{1,0:T(8,128)S(1)}, u32[]{:S(2)}, u32[]{:S(2)}) collective-permute-start(f32[128,256]{1,0:T(8,128)S(1)} %get-tuple-element.152), channel_id=1, source_target_pairs={{0,1},{1,0},{2,3},{3,2},{4,5},{5,4},{6,7},{7,6},{8,9},{9,8},{10,11... | collective-permute-start | bytes 393224 | tf_op jit(solution)/shard_map/ppermute | solution.py:67
  17.1 4.3 %collective-permute-start.6 = (f32[32,256]{1,0:T(8,128)S(1)}, f32[32,256]{1,0:T(8,128)S(1)}, u32[]{:S(2)}, u32[]{:S(2)}) collective-permute-start(f32[32,256]{1,0:T(8,128)S(1)} %get-tuple-element.162), channel_id=1, source_target_pairs={{0,2},{1,3},{2,0},{3,1},{4,6},{5,7},{6,4},{7,5},{8,10},{9,11},{10,... | collective-permute-start | bytes 98312 | tf_op jit(solution)/shard_map/ppermute | solution.py:67
  18.1 5.6 %collective-permute-start.5 = (f32[128,256]{1,0:T(8,128)S(1)}, f32[128,256]{1,0:T(8,128)S(1)}, u32[]{:S(2)}, u32[]{:S(2)}) collective-permute-start(f32[128,256]{1,0:T(8,128)S(1)} %get-tuple-element.161), channel_id=1, source_target_pairs={{0,16},{1,4},{2,18},{3,6},{4,1},{5,8},{6,3},{7,10},{8,5},{9,12},{1... | collective-permute-start | bytes 393224 | tf_op jit(solution)/shard_map/ppermute | solution.py:67
  19.6 4.7 %collective-permute-start.7 = (f32[128,256]{1,0:T(8,128)S(1)}, f32[128,256]{1,0:T(8,128)S(1)}, u32[]{:S(2)}, u32[]{:S(2)}) collective-permute-start(f32[128,256]{1,0:T(8,128)S(1)} %get-tuple-element.163), channel_id=1, source_target_pairs={{0,16},{1,4},{2,18},{3,6},{4,1},{5,8},{6,3},{7,10},{8,5},{9,12},{1... | collective-permute-start | bytes 393224 | tf_op jit(solution)/shard_map/ppermute | solution.py:67
  19.9 3.8 %collective-permute-start.8 = (f32[32,256]{1,0:T(8,128)S(1)}, f32[32,256]{1,0:T(8,128)S(1)}, u32[]{:S(2)}, u32[]{:S(2)}) collective-permute-start(f32[32,256]{1,0:T(8,128)S(1)} %get-tuple-element.164), channel_id=1, source_target_pairs={{0,2},{1,3},{2,0},{3,1},{4,6},{5,7},{6,4},{7,5},{8,10},{9,11},{10,... | collective-permute-start | bytes 98312 | tf_op jit(solution)/shard_map/ppermute | solution.py:67
  21.5 6.1 %collective-permute-start.10 = (f32[256,256]{1,0:T(8,128)S(1)}, f32[256,256]{1,0:T(8,128)S(1)}, u32[]{:S(2)}, u32[]{:S(2)}) collective-permute-start(f32[256,256]{1,0:T(8,128)S(1)} %bitcast.18), channel_id=1, source_target_pairs={{0,16},{1,2},{2,1},{3,19},{4,20},{5,6},{6,5},{7,23},{8,24},{9,10},... | collective-permute-start | bytes 786440 | tf_op jit(solution)/shard_map/ppermute | solution.py:67
  23.1 7.6 %collective-permute-start.11 = (f32[256,256]{1,0:T(8,128)S(1)}, f32[256,256]{1,0:T(8,128)S(1)}, u32[]{:S(2)}, u32[]{:S(2)}) collective-permute-start(f32[256,256]{1,0:T(8,128)S(1)} %bitcast.20), channel_id=1, source_target_pairs={{0,16},{1,2},{2,1},{3,19},{4,20},{5,6},{6,5},{7,23},{8,24},{9,10},... | collective-permute-start | bytes 786440 | tf_op jit(solution)/shard_map/ppermute | solution.py:67
  24.8 6.2 %collective-permute-start.9 = (f32[168,256]{1,0:T(8,128)S(1)}, f32[168,256]{1,0:T(8,128)S(1)}, u32[]{:S(2)}, u32[]{:S(2)}) collective-permute-start(f32[168,256]{1,0:T(8,128)S(1)} %get-tuple-element.173), channel_id=1, source_target_pairs={{0,1},{1,0},{2,3},{3,2},{4,5},{5,4},{6,7},{7,6},{8,9},{9,8},{10,11... | collective-permute-start | bytes 516104 | tf_op jit(solution)/shard_map/ppermute | solution.py:67
  25.5 7.0 %collective-permute-start.12 = (f32[128,256]{1,0:T(8,128)S(1)}, f32[128,256]{1,0:T(8,128)S(1)}, u32[]{:S(2)}, u32[]{:S(2)}) collective-permute-start(f32[128,256]{1,0:T(8,128)S(1)} %get-tuple-element.179), channel_id=1, source_target_pairs={{0,16},{1,4},{2,18},{3,6},{4,1},{5,8},{6,3},{7,10},{8,5},{9,12},{1... | collective-permute-start | bytes 393224 | tf_op jit(solution)/shard_map/ppermute | solution.py:67
  26.6 5.8 %collective-permute-start.13 = (f32[32,256]{1,0:T(8,128)S(1)}, f32[32,256]{1,0:T(8,128)S(1)}, u32[]{:S(2)}, u32[]{:S(2)}) collective-permute-start(f32[32,256]{1,0:T(8,128)S(1)} %get-tuple-element.180), channel_id=1, source_target_pairs={{0,2},{1,3},{2,0},{3,1},{4,6},{5,7},{6,4},{7,5},{8,10},{9,11},{10,... | collective-permute-start | bytes 98312 | tf_op jit(solution)/shard_map/ppermute | solution.py:67
  33.5 4.7 %collective-permute-start.15 = (f32[128,256]{1,0:T(8,128)S(1)}, f32[128,256]{1,0:T(8,128)S(1)}, u32[]{:S(2)}, u32[]{:S(2)}) collective-permute-start(f32[128,256]{1,0:T(8,128)S(1)} %get-tuple-element.185), channel_id=1, source_target_pairs={{0,16},{1,4},{2,18},{3,6},{4,1},{5,8},{6,3},{7,10},{8,5},{9,12},{1... | collective-permute-start | bytes 393224 | tf_op jit(solution)/shard_map/ppermute | solution.py:67
  34.8 3.3 %collective-permute-start.16 = (f32[72,256]{1,0:T(8,128)S(1)}, f32[72,256]{1,0:T(8,128)S(1)}, u32[]{:S(2)}, u32[]{:S(2)}) collective-permute-start(f32[72,256]{1,0:T(8,128)S(1)} %get-tuple-element.186), channel_id=1, source_target_pairs={{0,2},{1,3},{2,0},{3,1},{4,6},{5,7},{6,4},{7,5},{8,10},{9,11},{10,... | collective-permute-start | bytes 221192 | tf_op jit(solution)/shard_map/ppermute | solution.py:67
  38.4 4.3 %collective-permute-start.17 = (f32[2,128,256]{2,1,0:T(8,128)S(1)}, f32[2,128,256]{2,1,0:T(8,128)S(1)}, u32[]{:S(2)}, u32[]{:S(2)}) collective-permute-start(f32[2,128,256]{2,1,0:T(8,128)S(1)} %get-tuple-element.190), channel_id=1, source_target_pairs={{0,1},{1,0},{2,3},{3,2},{4,5},{5,4},{6,7},{7,6},{8,9},{9,8},{10,11... | collective-permute-start | bytes 786440 | tf_op jit(solution)/shard_map/ppermute | solution.py:67
  40.0 6.1 %collective-permute-start.18 = (f32[2,128,256]{2,1,0:T(8,128)S(1)}, f32[2,128,256]{2,1,0:T(8,128)S(1)}, u32[]{:S(2)}, u32[]{:S(2)}) collective-permute-start(f32[2,128,256]{2,1,0:T(8,128)S(1)} %get-tuple-element.192), channel_id=1, source_target_pairs={{0,16},{1,4},{2,18},{3,6},{4,1},{5,8},{6,3},{7,10},{8,5},{9,12},{1... | collective-permute-start | bytes 786440 | tf_op jit(solution)/shard_map/ppermute | solution.py:67
  40.5 4.4 %collective-permute-start.19 = (f32[2,32,256]{2,1,0:T(8,128)S(1)}, f32[2,32,256]{2,1,0:T(8,128)S(1)}, u32[]{:S(2)}, u32[]{:S(2)}) collective-permute-start(f32[2,32,256]{2,1,0:T(8,128)S(1)} %get-tuple-element.193), channel_id=1, source_target_pairs={{0,2},{1,3},{2,0},{3,1},{4,6},{5,7},{6,4},{7,5},{8,10},{9,11},{10,... | collective-permute-start | bytes 196616 | tf_op jit(solution)/shard_map/ppermute | solution.py:67
  41.5 3.4 %collective-permute-start.20 = (f32[8,8,128]{2,1,0:T(8,128)S(1)}, f32[8,8,128]{2,1,0:T(8,128)S(1)}, u32[]{:S(2)}, u32[]{:S(2)}) collective-permute-start(f32[8,8,128]{2,1,0:T(8,128)S(1)} %get-tuple-element.195), channel_id=1, source_target_pairs={{0,4},{1,5},{2,6},{3,7},{4,0},{5,1},{6,2},{7,3},{8,12},{9,13},{10,... | collective-permute-start | bytes 98312 | tf_op jit(solution)/shard_map/ppermute | solution.py:67
  46.4 4.1 %collective-permute-start.21 = (f32[128,256]{1,0:T(8,128)S(1)}, f32[128,256]{1,0:T(8,128)S(1)}, u32[]{:S(2)}, u32[]{:S(2)}) collective-permute-start(f32[128,256]{1,0:T(8,128)S(1)} %get-tuple-element.197), channel_id=1, source_target_pairs={{0,1},{1,0},{2,3},{3,2},{4,5},{5,4},{6,7},{7,6},{8,9},{9,8},{10,11... | collective-permute-start | bytes 393224 | tf_op jit(solution)/shard_map/ppermute | solution.py:67
  47.5 4.8 %collective-permute-start.22 = (f32[128,256]{1,0:T(8,128)S(1)}, f32[128,256]{1,0:T(8,128)S(1)}, u32[]{:S(2)}, u32[]{:S(2)}) collective-permute-start(f32[128,256]{1,0:T(8,128)S(1)} %get-tuple-element.199), channel_id=1, source_target_pairs={{0,16},{1,4},{2,18},{3,6},{4,1},{5,8},{6,3},{7,10},{8,5},{9,12},{1... | collective-permute-start | bytes 393224 | tf_op jit(solution)/shard_map/ppermute | solution.py:67
  47.5 4.3 %collective-permute-start.23 = (f32[32,256]{1,0:T(8,128)S(1)}, f32[32,256]{1,0:T(8,128)S(1)}, u32[]{:S(2)}, u32[]{:S(2)}) collective-permute-start(f32[32,256]{1,0:T(8,128)S(1)} %get-tuple-element.200), channel_id=1, source_target_pairs={{0,2},{1,3},{2,0},{3,1},{4,6},{5,7},{6,4},{7,5},{8,10},{9,11},{10,... | collective-permute-start | bytes 98312 | tf_op jit(solution)/shard_map/ppermute | solution.py:67
  48.3 4.0 %collective-permute-start.24 = (f32[8,8,128]{2,1,0:T(8,128)S(1)}, f32[8,8,128]{2,1,0:T(8,128)S(1)}, u32[]{:S(2)}, u32[]{:S(2)}) collective-permute-start(f32[8,8,128]{2,1,0:T(8,128)S(1)} %get-tuple-element.202), channel_id=1, source_target_pairs={{0,8},{1,9},{2,10},{3,11},{4,12},{5,13},{6,14},{7,15},{8,0},{9,1},... | collective-permute-start | bytes 98312 | tf_op jit(solution)/shard_map/ppermute | solution.py:67
  52.5 4.3 %collective-permute-start.25 = (f32[128,256]{1,0:T(8,128)S(1)}, f32[128,256]{1,0:T(8,128)S(1)}, u32[]{:S(2)}, u32[]{:S(2)}) collective-permute-start(f32[128,256]{1,0:T(8,128)S(1)} %get-tuple-element.204), channel_id=1, source_target_pairs={{0,1},{1,0},{2,3},{3,2},{4,5},{5,4},{6,7},{7,6},{8,9},{9,8},{10,11... | collective-permute-start | bytes 393224 | tf_op jit(solution)/shard_map/ppermute | solution.py:67
  54.7 4.7 %collective-permute-start.26 = (f32[128,256]{1,0:T(8,128)S(1)}, f32[128,256]{1,0:T(8,128)S(1)}, u32[]{:S(2)}, u32[]{:S(2)}) collective-permute-start(f32[128,256]{1,0:T(8,128)S(1)} %get-tuple-element.208), channel_id=1, source_target_pairs={{0,16},{1,4},{2,18},{3,6},{4,1},{5,8},{6,3},{7,10},{8,5},{9,12},{1... | collective-permute-start | bytes 393224 | tf_op jit(solution)/shard_map/ppermute | solution.py:67
  55.6 3.1 %collective-permute-start.27 = (f32[32,256]{1,0:T(8,128)S(1)}, f32[32,256]{1,0:T(8,128)S(1)}, u32[]{:S(2)}, u32[]{:S(2)}) collective-permute-start(f32[32,256]{1,0:T(8,128)S(1)} %get-tuple-element.209), channel_id=1, source_target_pairs={{0,2},{1,3},{2,0},{3,1},{4,6},{5,7},{6,4},{7,5},{8,10},{9,11},{10,... | collective-permute-start | bytes 98312 | tf_op jit(solution)/shard_map/ppermute | solution.py:67
  60.3 4.7 %collective-permute-start.29 = (f32[128,256]{1,0:T(8,128)S(1)}, f32[128,256]{1,0:T(8,128)S(1)}, u32[]{:S(2)}, u32[]{:S(2)}) collective-permute-start(f32[128,256]{1,0:T(8,128)S(1)} %get-tuple-element.217), channel_id=1, source_target_pairs={{0,16},{1,4},{2,18},{3,6},{4,1},{5,8},{6,3},{7,10},{8,5},{9,12},{1... | collective-permute-start | bytes 393224 | tf_op jit(solution)/shard_map/ppermute | solution.py:67
  60.8 3.1 %collective-permute-start.30 = (f32[32,256]{1,0:T(8,128)S(1)}, f32[32,256]{1,0:T(8,128)S(1)}, u32[]{:S(2)}, u32[]{:S(2)}) collective-permute-start(f32[32,256]{1,0:T(8,128)S(1)} %get-tuple-element.218), channel_id=1, source_target_pairs={{0,2},{1,3},{2,0},{3,1},{4,6},{5,7},{6,4},{7,5},{8,10},{9,11},{10,... | collective-permute-start | bytes 98312 | tf_op jit(solution)/shard_map/ppermute | solution.py:67
  65.7 4.7 %collective-permute-start.32 = (f32[128,256]{1,0:T(8,128)S(1)}, f32[128,256]{1,0:T(8,128)S(1)}, u32[]{:S(2)}, u32[]{:S(2)}) collective-permute-start(f32[128,256]{1,0:T(8,128)S(1)} %get-tuple-element.222), channel_id=1, source_target_pairs={{0,16},{1,4},{2,18},{3,6},{4,1},{5,8},{6,3},{7,10},{8,5},{9,12},{1... | collective-permute-start | bytes 393224 | tf_op jit(solution)/shard_map/ppermute | solution.py:67
  66.4 3.1 %collective-permute-start.33 = (f32[32,256]{1,0:T(8,128)S(1)}, f32[32,256]{1,0:T(8,128)S(1)}, u32[]{:S(2)}, u32[]{:S(2)}) collective-permute-start(f32[32,256]{1,0:T(8,128)S(1)} %get-tuple-element.223), channel_id=1, source_target_pairs={{0,2},{1,3},{2,0},{3,1},{4,6},{5,7},{6,4},{7,5},{8,10},{9,11},{10,... | collective-permute-start | bytes 98312 | tf_op jit(solution)/shard_map/ppermute | solution.py:67
  71.7 4.7 %collective-permute-start.35 = (f32[128,256]{1,0:T(8,128)S(1)}, f32[128,256]{1,0:T(8,128)S(1)}, u32[]{:S(2)}, u32[]{:S(2)}) collective-permute-start(f32[128,256]{1,0:T(8,128)S(1)} %get-tuple-element.231), channel_id=1, source_target_pairs={{0,16},{1,4},{2,18},{3,6},{4,1},{5,8},{6,3},{7,10},{8,5},{9,12},{1... | collective-permute-start | bytes 393224 | tf_op jit(solution)/shard_map/ppermute | solution.py:67
  72.4 3.1 %collective-permute-start.36 = (f32[32,256]{1,0:T(8,128)S(1)}, f32[32,256]{1,0:T(8,128)S(1)}, u32[]{:S(2)}, u32[]{:S(2)}) collective-permute-start(f32[32,256]{1,0:T(8,128)S(1)} %get-tuple-element.232), channel_id=1, source_target_pairs={{0,2},{1,3},{2,0},{3,1},{4,6},{5,7},{6,4},{7,5},{8,10},{9,11},{10,... | collective-permute-start | bytes 98312 | tf_op jit(solution)/shard_map/ppermute | solution.py:67
  77.1 4.7 %collective-permute-start.38 = (f32[128,256]{1,0:T(8,128)S(1)}, f32[128,256]{1,0:T(8,128)S(1)}, u32[]{:S(2)}, u32[]{:S(2)}) collective-permute-start(f32[128,256]{1,0:T(8,128)S(1)} %get-tuple-element.238), channel_id=1, source_target_pairs={{0,16},{1,4},{2,18},{3,6},{4,1},{5,8},{6,3},{7,10},{8,5},{9,12},{1... | collective-permute-start | bytes 393224 | tf_op jit(solution)/shard_map/ppermute | solution.py:67
  77.8 3.1 %collective-permute-start.39 = (f32[32,256]{1,0:T(8,128)S(1)}, f32[32,256]{1,0:T(8,128)S(1)}, u32[]{:S(2)}, u32[]{:S(2)}) collective-permute-start(f32[32,256]{1,0:T(8,128)S(1)} %get-tuple-element.239), channel_id=1, source_target_pairs={{0,2},{1,3},{2,0},{3,1},{4,6},{5,7},{6,4},{7,5},{8,10},{9,11},{10,... | collective-permute-start | bytes 98312 | tf_op jit(solution)/shard_map/ppermute | solution.py:67
  82.5 4.7 %collective-permute-start.41 = (f32[128,256]{1,0:T(8,128)S(1)}, f32[128,256]{1,0:T(8,128)S(1)}, u32[]{:S(2)}, u32[]{:S(2)}) collective-permute-start(f32[128,256]{1,0:T(8,128)S(1)} %get-tuple-element.245), channel_id=1, source_target_pairs={{0,16},{1,4},{2,18},{3,6},{4,1},{5,8},{6,3},{7,10},{8,5},{9,12},{1... | collective-permute-start | bytes 393224 | tf_op jit(solution)/shard_map/ppermute | solution.py:67
  83.2 3.1 %collective-permute-start.42 = (f32[32,256]{1,0:T(8,128)S(1)}, f32[32,256]{1,0:T(8,128)S(1)}, u32[]{:S(2)}, u32[]{:S(2)}) collective-permute-start(f32[32,256]{1,0:T(8,128)S(1)} %get-tuple-element.246), channel_id=1, source_target_pairs={{0,2},{1,3},{2,0},{3,1},{4,6},{5,7},{6,4},{7,5},{8,10},{9,11},{10,... | collective-permute-start | bytes 98312 | tf_op jit(solution)/shard_map/ppermute | solution.py:67
  87.8 4.7 %collective-permute-start.44 = (f32[128,256]{1,0:T(8,128)S(1)}, f32[128,256]{1,0:T(8,128)S(1)}, u32[]{:S(2)}, u32[]{:S(2)}) collective-permute-start(f32[128,256]{1,0:T(8,128)S(1)} %get-tuple-element.252), channel_id=1, source_target_pairs={{0,16},{1,4},{2,18},{3,6},{4,1},{5,8},{6,3},{7,10},{8,5},{9,12},{1... | collective-permute-start | bytes 393224 | tf_op jit(solution)/shard_map/ppermute | solution.py:67
  88.5 3.1 %collective-permute-start.45 = (f32[32,256]{1,0:T(8,128)S(1)}, f32[32,256]{1,0:T(8,128)S(1)}, u32[]{:S(2)}, u32[]{:S(2)}) collective-permute-start(f32[32,256]{1,0:T(8,128)S(1)} %get-tuple-element.253), channel_id=1, source_target_pairs={{0,2},{1,3},{2,0},{3,1},{4,6},{5,7},{6,4},{7,5},{8,10},{9,11},{10,... | collective-permute-start | bytes 98312 | tf_op jit(solution)/shard_map/ppermute | solution.py:67
  93.2 4.7 %collective-permute-start.47 = (f32[128,256]{1,0:T(8,128)S(1)}, f32[128,256]{1,0:T(8,128)S(1)}, u32[]{:S(2)}, u32[]{:S(2)}) collective-permute-start(f32[128,256]{1,0:T(8,128)S(1)} %get-tuple-element.259), channel_id=1, source_target_pairs={{0,16},{1,4},{2,18},{3,6},{4,1},{5,8},{6,3},{7,10},{8,5},{9,12},{1... | collective-permute-start | bytes 393224 | tf_op jit(solution)/shard_map/ppermute | solution.py:67
  93.9 3.1 %collective-permute-start.48 = (f32[32,256]{1,0:T(8,128)S(1)}, f32[32,256]{1,0:T(8,128)S(1)}, u32[]{:S(2)}, u32[]{:S(2)}) collective-permute-start(f32[32,256]{1,0:T(8,128)S(1)} %get-tuple-element.260), channel_id=1, source_target_pairs={{0,2},{1,3},{2,0},{3,1},{4,6},{5,7},{6,4},{7,5},{8,10},{9,11},{10,... | collective-permute-start | bytes 98312 | tf_op jit(solution)/shard_map/ppermute | solution.py:67
  98.6 4.7 %collective-permute-start.50 = (f32[128,256]{1,0:T(8,128)S(1)}, f32[128,256]{1,0:T(8,128)S(1)}, u32[]{:S(2)}, u32[]{:S(2)}) collective-permute-start(f32[128,256]{1,0:T(8,128)S(1)} %get-tuple-element.266), channel_id=1, source_target_pairs={{0,16},{1,4},{2,18},{3,6},{4,1},{5,8},{6,3},{7,10},{8,5},{9,12},{1... | collective-permute-start | bytes 393224 | tf_op jit(solution)/shard_map/ppermute | solution.py:67
  104.0 4.7 %collective-permute-start.53 = (f32[128,256]{1,0:T(8,128)S(1)}, f32[128,256]{1,0:T(8,128)S(1)}, u32[]{:S(2)}, u32[]{:S(2)}) collective-permute-start(f32[128,256]{1,0:T(8,128)S(1)} %get-tuple-element.273), channel_id=1, source_target_pairs={{0,16},{1,4},{2,18},{3,6},{4,1},{5,8},{6,3},{7,10},{8,5},{9,12},{1... | collective-permute-start | bytes 393224 | tf_op jit(solution)/shard_map/ppermute | solution.py:67
  109.2 10.7 %collective-permute-start.57 = (f32[2,256,256]{2,1,0:T(8,128)S(1)}, f32[2,256,256]{2,1,0:T(8,128)S(1)}, u32[]{:S(2)}, u32[]{:S(2)}) collective-permute-start(f32[2,256,256]{2,1,0:T(8,128)S(1)} %get-tuple-element.280.own), channel_id=1, source_target_pairs={{0,16},{1,2},{2,1},{3,19},{4,20},{5,6},{6,5},{7,23},{8,24},{9,10},... | collective-permute-start | bytes 1572872 | tf_op jit(solution)/shard_map/ppermute | solution.py:67
  111.7 9.0 %collective-permute-start.56 = (f32[2,64,128]{2,1,0:T(8,128)S(1)}, f32[2,64,128]{2,1,0:T(8,128)S(1)}, u32[]{:S(2)}, u32[]{:S(2)}) collective-permute-start(f32[2,64,128]{2,1,0:T(8,128)S(1)} %get-tuple-element.279), channel_id=1, source_target_pairs={{0,12},{1,14},{2,13},{3,15},{4,8},{5,10},{6,9},{7,11},{8,4},{9,6},... | collective-permute-start | bytes 196616 | tf_op jit(solution)/shard_map/ppermute | solution.py:67
  113.1 7.9 %collective-permute-start.58 = (f32[2,64,128]{2,1,0:T(8,128)S(1)}, f32[2,64,128]{2,1,0:T(8,128)S(1)}, u32[]{:S(2)}, u32[]{:S(2)}) collective-permute-start(f32[2,64,128]{2,1,0:T(8,128)S(1)} %get-tuple-element.283), channel_id=1, source_target_pairs={{0,8},{1,10},{2,9},{3,11},{4,12},{5,14},{6,13},{7,15},{8,0},{9,2},... | collective-permute-start | bytes 196616 | tf_op jit(solution)/shard_map/ppermute | solution.py:67
  114.8 6.2 %collective-permute-start.59 = (f32[2,64,128]{2,1,0:T(8,128)S(1)}, f32[2,64,128]{2,1,0:T(8,128)S(1)}, u32[]{:S(2)}, u32[]{:S(2)}) collective-permute-start(f32[2,64,128]{2,1,0:T(8,128)S(1)} %get-tuple-element.284), channel_id=1, source_target_pairs={{0,4},{1,6},{2,5},{3,7},{4,0},{5,2},{6,1},{7,3},{8,12},{9,14},{10,... | collective-permute-start | bytes 196616 | tf_op jit(solution)/shard_map/ppermute | solution.py:67
  116.9 5.6 %collective-permute-start.60 = (f32[2,64,128]{2,1,0:T(8,128)S(1)}, f32[2,64,128]{2,1,0:T(8,128)S(1)}, u32[]{:S(2)}, u32[]{:S(2)}) collective-permute-start(f32[2,64,128]{2,1,0:T(8,128)S(1)} %get-tuple-element.285), channel_id=1, source_target_pairs={{0,0},{1,2},{2,1},{3,3},{4,4},{5,6},{6,5},{7,7},{8,8},{9,10},{10,9... | collective-permute-start | bytes 196616 | tf_op jit(solution)/shard_map/ppermute | solution.py:67
  (31 other events, 83.6 us)

commit v17 on v15

--- a/solution.py
+++ b/solution.py
@@ -334,12 +334,12 @@
         yield n, (high << (stage + 1)) + (other << stage) + low
 
 
-def trade(stage, flags, mine, got, out, give=None):
+def trade(stage, then, flags, mine, got, out, give=None):
     out[...] = mine[...]
     for n, at in other_half(stage, flags, out.shape[0]):
         out[at] = got(n) if callable(got) else got[n]
     if give is not None:
-        for n, at in other_half(stage + 1, flags, out.shape[0]):
+        for n, at in other_half(then, flags, out.shape[0]):
             give[n] = out[at]
 
 
@@ -373,8 +373,8 @@
     return entry, cells
 
 
-def trade_kernel(stage, flags, mine, got, *outs):
-    trade(stage, flags, mine, got, *outs)
+def trade_kernel(stage, then, flags, mine, got, out, give):
+    trade(stage, then, flags, mine, got, out, give)
 
 
 def source_kernel(step, full, flags, src, wave, out):
@@ -411,17 +411,12 @@
     change[...] = (cur[...] - prev[...]) - (prev[...] - before[...])
 
 
-def outer_kernel(stage, flags, part, k0, ki, kx, zm, ym, side, edge, *rest):
-    if stage is not None:
-        mine, got, new, zo, co, yo, *lists = rest
-        trade(stage, flags, mine, got, *lists)
-    else:
-        new, zo, co, yo = rest
+def outer_kernel(flags, part, k0, ki, kx, zm, ym, side, edge, new, zo, co, yo):
     outer(flags, part, k0, ki, kx, zm, ym, side, edge, new)
     rims(flags, new, zo, co, yo)
 
 
-def pack_kernel(flags, counts, cells, traces, cells_out, lists, give, counts_v, cells_v, traces_v,
+def pack_kernel(stage, flags, counts, cells, traces, cells_out, lists, give, counts_v, cells_v, traces_v,
                 sems):
     pairs = ((counts, counts_v), (cells, cells_v), (traces, traces_v))
     copies = [pltpu.make_async_copy(a, b, sems.at[n]) for n, (a, b) in enumerate(pairs)]
@@ -441,7 +436,7 @@
         start = ((2 * q + c) * 2 + y) * CAP
         tile = traces_v[:, start // 128 * 128 : start // 128 * 128 + 128]
         lists[m] = pltpu.roll(tile, (128 - start % 128) % 128, axis=1) if start % 128 else tile
-    for n, at in other_half(0, flags, subs):
+    for n, at in other_half(stage, flags, subs):
         give[n] = lists[at]
 
 
@@ -450,7 +445,7 @@
     outer(flags, part, k0, ki, kx, zm, ym, side, edge, new)
     count, half = lists.shape[0] // 2, new.shape[0] // 2
     entry, (theirs,) = unload(cm, half, count, 1, cells.shape[1])
-    trade(0, flags, lists, entry, lists_out)
+    trade(0, None, flags, lists, entry, lists_out)
     mine = cells[...]
     pair[0:1] = jnp.where(flags[0] == 0, mine, theirs)
     pair[1:2] = jnp.where(flags[0] == 0, theirs, mine)
@@ -460,12 +455,12 @@
 
 
 def y_stage_kernel(flags, part, k0, ki, kx, zm, ym, side, edge, lists, pair, other, new, zo, co, yo,
-                   lists_out, give, cells):
+                   lists_out, cells):
     outer(flags, part, k0, ki, kx, zm, ym, side, edge, new)
     for n, field in enumerate((new, other)):
         rims(flags, field, zo.at[n], co.at[n], yo.at[n])
     entry, theirs = unload(ym, 32, lists.shape[0] // 2, 2, pair.shape[1])
-    trade(1, flags, lists, entry, lists_out, give)
+    trade(1, None, flags, lists, entry, lists_out)
     away = flags[0] != flags[1]
     low = jnp.where(away, theirs[0], pair[0:1])
     high = jnp.where(away, theirs[1], pair[1:2])
@@ -557,6 +552,7 @@
 
 def filter_kernel(flags, *refs):
     *pieces, out = refs
+    pieces = pieces[::-1]
     height, lanes = pieces[0].shape[1:]
     chunk, rows, full = out.shape
     groups = lanes // chunk
@@ -663,6 +659,21 @@
     inj, = call(functools.partial(source_kernel, 0, full), "source", [field], src_cell, wavelet,
                 weight=0.7, scalars=2)
     got[0], inj = lax.optimization_barrier((got[0], inj))
+    slots = subs * CAP
+    entries, half_entries = shaped(subs, steps, 128), shaped(subs // 2, steps, 128)
+    order = [*range(2, len(stages)), 0]
+    cells, lists, give = call(
+        functools.partial(pack_kernel, order[0]), "pack", [shaped(1, slots), entries, half_entries], after(rec_counts, stacked),
+        rec_cells, observed, weight=0.2, far=3,
+        scratch=[pltpu.VMEM(rec_counts.shape, jnp.int32), pltpu.VMEM(rec_cells.shape, jnp.int32),
+                 pltpu.VMEM(observed.shape, F32)])
+    for n, bit in enumerate(order[:-1]):
+        lists, give = call(
+            functools.partial(trade_kernel, bit, order[n + 1]), "trade", [entries, half_entries],
+            lists, send(give, stages[bit][0]), weight=0.1)
+        if n == 0:
+            got[0], give = lax.optimization_barrier((got[0], give))
+
     density, p_now, *out = call(settle_kernel, "settle",
                                 [field, field] + [shaped(2, *r.shape) for r in rim],
                                 log_density, fwd_now, *got, far=2)
@@ -673,13 +684,6 @@
                  near, deep, weight=1.3)
     got_adjoint = [send(after(v, parts[0]), swap_perm) for v in (adj_now, adj_before)]
 
-    slots = subs * CAP
-    entries, half_entries = shaped(subs, steps, 128), shaped(subs // 2, steps, 128)
-    cells, lists, give = call(
-        pack_kernel, "pack", [shaped(1, slots), entries, half_entries], after(rec_counts, density),
-        rec_cells, observed, weight=0.2, far=3,
-        scratch=[pltpu.VMEM(rec_counts.shape, jnp.int32), pltpu.VMEM(rec_cells.shape, jnp.int32),
-                 pltpu.VMEM(observed.shape, F32)])
     riders = subs // 4 * 8 + 8
     core_rim = shaped(size // 2 + riders, depth)
     y_rim = shaped(4 * cols + riders, depth)
@@ -691,11 +695,8 @@
     states = [p_before, p_now, new]
     changes = []
     zm, cm, ym = halo(zo, co, yo)
-    late = steps - 2 if len(stages) < steps - 1 else steps - 1
     for t in range(1, steps):
         cur, prev, before = states[:-4:-1]
-        stage = t - 1 if 2 < t <= min(len(stages), steps - 2) else None
-        extra = [lists, send(give, stages[stage][0])] if stage is not None else []
         part, change = call(
             functools.partial(forward_inner_kernel, t, full), "forward_inner", [field, field], src_cell, wavelet, cur, prev, *model, cm, near, deep, before, weight=1.2, scalars=2)
         changes.append(change)
@@ -704,13 +705,7 @@
             u_part, = call(adjoint_first_kernel, "adjoint_first", [field], u_now, u_before,
                            *model, u_cm, near, deep, weight=1.1)
             args[0] = after(part, u_part)
-        if t == late:
-            for n in range(steps - 2, len(stages)):
-                lists, *give = call(
-                    functools.partial(trade_kernel, n), "trade",
-                    [entries] + ([half_entries] if n + 1 < len(stages) else []), lists,
-                    send(give, stages[n][0]))
-                give = give[0] if give else None
+        if t == steps - 2:
             receivers = call(
                 lists_kernel, "lists",
                 [jax.ShapeDtypeStruct((size, slots), BF16),
@@ -734,23 +729,15 @@
             zm, cm, ym = halo(*out)
             continue
         if t == 2:
-            new, *out, lists, give, cells = call(
+            new, *out, lists, cells = call(
                 y_stage_kernel, "forward_outer",
-                [field] + [shaped(2, *r.shape) for r in rim] + [entries, half_entries,
-                                                                shaped(1, slots)],
+                [field] + [shaped(2, *r.shape) for r in rim] + [entries, shaped(1, slots)],
                 *args, lists, pair, u_now)
             states.append(new)
             zm, cm, ym = halo(*out)
             u_zm, u_cm, u_ym = zm, cm, ym
             continue
-        outs = [field] + rim
-        if extra:
-            outs = outs + [entries] + ([half_entries] if t < len(stages) else [])
-        new, *out = call(functools.partial(outer_kernel, stage), "forward_outer", outs,
-                         *args, *extra)
-        if extra:
-            out, (lists, *give) = out[:3], out[3:]
-            give = give[0] if give else None
+        new, *out = call(outer_kernel, "forward_outer", [field] + rim, *args)
         states.append(new)
         zm, cm, ym = halo(*out)
 
@@ -771,7 +758,7 @@
                 [shaped(2, *field.shape), half, half], *args, *image, changes[0], vel, u_now)
             break
         u_before = u_now
-        u_now, *out = call(functools.partial(outer_kernel, None), "adjoint_outer", [field] + rim,
+        u_now, *out = call(outer_kernel, "adjoint_outer", [field] + rim,
                            *args)
         zm, cm, ym = halo(*out)
 
@@ -781,7 +768,7 @@
     pieces = [send(pieces[s], plan.spread(s)) for s in reversed(range(nq))][::-1]
     adj_prev, adj_out = call(select_kernel, "select", [field, field], final, got, weight=1.2)
     gradient, = call(filter_kernel, "filter", [shaped(chunk, rows, nx * cols)],
-                     after(pieces[0], adj_out), *pieces[1:])
+                     after(pieces[-1], adj_out), *pieces[-2::-1])
     block = (rows, cols, depth)
     return gradient, adj_out.reshape(block), adj_prev.reshape(block)
 

time: 118 us -> 116 us (0.983)
  starting transfers between devices: 62.3 us -> 41.2 us
  waiting for transfers between devices: 25.1 us -> 43.8 us
    ppermute x58, starting transfers between devices: 62.3 us -> 41.2 us  [send(): return lax.ppermute(value, ALL, pairs)]
    ppermute x58, waiting for transfers between devices: 25.1 us -> 43.8 us  [send(): return lax.ppermute(value, ALL, pairs)]
    pallas_call x40 -> x42, Pallas kernels: 26.8 us -> 26.8 us  [call(): pl.pallas_call(functools.partial(kernel, Flags()), name=name, out_shape=o...]
  transfers between devices with their start and end apart: 58 -> 58, of which waited for: 33 -> 46; matrix products, arithmetic and copies ran while one was open for 1% -> 1% of each run, Pallas kernels for 18% -> 18%
where the time goes in v17:
time: 116 us
  waiting for transfers between devices  43.8 us (38%)
  starting transfers between devices  41.2 us (36%)
  Pallas kernels  26.8 us (23%)
  local copies, waits for them, and re-layouts  1.64 us (1%)
  other arithmetic  1.27 us (1%)
  between operations  1.18 us (1%)
    ppermute x58, waiting for transfers between devices, send(): return lax.ppermute(value, ALL, pairs)  43.8 us
    ppermute x58, starting transfers between devices, send(): return lax.ppermute(value, ALL, pairs)  41.2 us
    pallas_call x42, Pallas kernels, call(): pl.pallas_call(functools.partial(kernel, Flags()), name=name, out_shape=o...  26.8 us
  transfers between devices with their start and end apart: 58, of which 46 were waited for; matrix products, arithmetic and copies ran while one was open for 1% of the time, Pallas kernels for 18%

profile of v17, /device:TPU:1, one launch (start us, length us, event | category | flops | bytes accessed | tf_op | source)
XLA Modules:
  0.0 115.9 jit_solution(149241973546080766)
XLA Ops:
  0.6 2.7 %collective-permute-start.2 = (f32[256,256]{1,0:T(8,128)}, f32[256,256]{1,0:T(8,128)S(1)}, u32[]{:S(2)}, u32[]{:S(2)}) collective-permute-start(f32[256,256]{1,0:T(8,128)} %bitcast.16), channel_id=1, source_target_pairs={{0,16},{1,2},{2,1},{3,19},{4,20},{5,6},{6,5},{7,23},{8,24},{9,10},... | collective-permute-start | bytes 786440 | tf_op jit(solution)/shard_map/ppermute | solution.py:67
  3.4 1.1 pad_maximum_fusion
  4.6 1.7 %collective-permute-start.3 = (f32[2,256,256]{2,1,0:T(8,128)S(1)}, f32[2,256,256]{2,1,0:T(8,128)S(1)}, u32[]{:S(2)}, u32[]{:S(2)}) collective-permute-start(f32[2,256,256]{2,1,0:T(8,128)S(1)} %pad_maximum_fusion), channel_id=1, source_target_pairs={{0,16},{1,2},{2,1},{3,19},{4,20},{5,6},{6,5},{7,23},{8,24},{9,10},... | collective-permute-start | bytes 1572872 | tf_op jit(solution)/shard_map/ppermute | solution.py:67
  6.5 1.4 %collective-permute-start.1 = (f32[8,8,128]{2,1,0:T(8,128)S(1)}, f32[8,8,128]{2,1,0:T(8,128)S(1)}, u32[]{:S(2)}, u32[]{:S(2)}) collective-permute-start(f32[8,8,128]{2,1,0:T(8,128)S(1)} %get-tuple-element.146), channel_id=1, source_target_pairs={{0,4},{1,5},{2,6},{3,7},{4,0},{5,1},{6,2},{7,3},{8,12},{9,13},{10,... | collective-permute-start | bytes 98312 | tf_op jit(solution)/shard_map/ppermute | solution.py:67
  9.4 1.0 source.1.inj
  11.7 1.5 %collective-permute-start.5 = (f32[2,128,256]{2,1,0:T(8,128)S(1)}, f32[2,128,256]{2,1,0:T(8,128)S(1)}, u32[]{:S(2)}, u32[]{:S(2)}) collective-permute-start(f32[2,128,256]{2,1,0:T(8,128)S(1)} %get-tuple-element.162), channel_id=1, source_target_pairs={{0,16},{1,4},{2,18},{3,6},{4,1},{5,8},{6,3},{7,10},{8,5},{9,12},{1... | collective-permute-start | bytes 786440 | tf_op jit(solution)/shard_map/ppermute | solution.py:67
  13.2 2.4 %collective-permute-start.7 = (f32[8,8,128]{2,1,0:T(8,128)S(1)}, f32[8,8,128]{2,1,0:T(8,128)S(1)}, u32[]{:S(2)}, u32[]{:S(2)}) collective-permute-start(f32[8,8,128]{2,1,0:T(8,128)S(1)} %get-tuple-element.165), channel_id=1, source_target_pairs={{0,8},{1,9},{2,10},{3,11},{4,12},{5,13},{6,14},{7,15},{8,0},{9,1},... | collective-permute-start | bytes 98312 | tf_op jit(solution)/shard_map/ppermute | solution.py:67
  17.8 3.2 %collective-permute-start.10 = (f32[256,256]{1,0:T(8,128)S(1)}, f32[256,256]{1,0:T(8,128)S(1)}, u32[]{:S(2)}, u32[]{:S(2)}) collective-permute-start(f32[256,256]{1,0:T(8,128)S(1)} %bitcast.20), channel_id=1, source_target_pairs={{0,16},{1,2},{2,1},{3,19},{4,20},{5,6},{6,5},{7,23},{8,24},{9,10},... | collective-permute-start | bytes 786440 | tf_op jit(solution)/shard_map/ppermute | solution.py:67
  21.8 1.0 collective-permute-start.8
  23.9 1.4 %forward_inner.7 = (f32[256,256]{1,0:T(8,128)S(1)}, f32[256,256]{1,0:T(8,128)S(1)}) custom-call(s32[16]{0:T(128)S(1)} %copy-done.8, f32[8,16]{1,0:T(8,128)S(1)} %copy-done.3, f32[256,256]{1,0:T(8,128)S(1)} %get-tuple-element.168.cur.prev.before.state, f32[256,256]{1,0:T(8,128)S(1)} %get-tuple-element.149.cur.prev.before, ...), custom_call_target="tpu_custom_call" | custom-call | flops 1000 | bytes 4321000 | tf_op jit(solution)/shard_map/forward_inner/pallas_call | solution.py:600
  29.5 1.4 %forward_inner.8 = (f32[256,256]{1,0:T(8,128)S(1)}, f32[256,256]{1,0:T(8,128)S(1)}) custom-call(s32[16]{0:T(128)S(1)} %copy-done.8, f32[8,16]{1,0:T(8,128)S(1)} %copy-done.3, f32[256,256]{1,0:T(8,128)S(1)} %get-tuple-element.182.cur.prev.before.state, f32[256,256]{1,0:T(8,128)S(1)} %get-tuple-element.168.cur.prev.before.state, ...), custom_call_target="tpu_custom_call" | custom-call | flops 1000 | bytes 4321000 | tf_op jit(solution)/shard_map/forward_inner/pallas_call | solution.py:600
  30.9 1.5 %collective-permute-done.15.ym = f32[72,256]{1,0:T(8,128)S(1)} collective-permute-done((f32[72,256]{1,0:T(8,128)S(1)}, f32[72,256]{1,0:T(8,128)S(1)}, u32[]{:S(2)}, u32[]{:S(2)}) %collective-permute-start.15) | collective-permute-done | bytes 73760 | tf_op jit(solution)/shard_map/ppermute | solution.py:67
  33.4 1.3 %collective-permute-start.16 = (f32[2,128,256]{2,1,0:T(8,128)S(1)}, f32[2,128,256]{2,1,0:T(8,128)S(1)}, u32[]{:S(2)}, u32[]{:S(2)}) collective-permute-start(f32[2,128,256]{2,1,0:T(8,128)S(1)} %get-tuple-element.190), channel_id=1, source_target_pairs={{0,1},{1,0},{2,3},{3,2},{4,5},{5,4},{6,7},{7,6},{8,9},{9,8},{10,11... | collective-permute-start | bytes 786440 | tf_op jit(solution)/shard_map/ppermute | solution.py:67
  35.9 1.4 %forward_inner.9 = (f32[256,256]{1,0:T(8,128)S(1)}, f32[256,256]{1,0:T(8,128)S(1)}) custom-call(s32[16]{0:T(128)S(1)} %copy-done.8, f32[8,16]{1,0:T(8,128)S(1)} %copy-done.3, f32[256,256]{1,0:T(8,128)S(1)} %get-tuple-element.189.cur.prev.before.state, f32[256,256]{1,0:T(8,128)S(1)} %get-tuple-element.182.cur.prev.before.state, ...), custom_call_target="tpu_custom_call" | custom-call | flops 1000 | bytes 4321000 | tf_op jit(solution)/shard_map/forward_inner/pallas_call | solution.py:600
  37.3 1.1 collective-permute-done.18.ym.u_ym
  38.4 2.4 %collective-permute-done.17.zm.u_zm = f32[2,128,256]{2,1,0:T(8,128)S(1)} collective-permute-done((f32[2,128,256]{2,1,0:T(8,128)S(1)}, f32[2,128,256]{2,1,0:T(8,128)S(1)}, u32[]{:S(2)}, u32[]{:S(2)}) %collective-permute-start.17) | collective-permute-done | bytes 262176 | tf_op jit(solution)/shard_map/ppermute | solution.py:67
  41.5 1.0 collective-permute-done.19.cm
  42.5 1.4 %forward_inner.10 = (f32[256,256]{1,0:T(8,128)S(1)}, f32[256,256]{1,0:T(8,128)S(1)}) custom-call(s32[16]{0:T(128)S(1)} %copy-done.8, f32[8,16]{1,0:T(8,128)S(1)} %copy-done.3, f32[256,256]{1,0:T(8,128)S(1)} %get-tuple-element.194.cur.prev.before.state, f32[256,256]{1,0:T(8,128)S(1)} %get-tuple-element.189.cur.prev.before.state, ...), custom_call_target="tpu_custom_call" | custom-call | flops 1000 | bytes 4321000 | tf_op jit(solution)/shard_map/forward_inner/pallas_call | solution.py:600
  44.3 1.9 %collective-permute-done.20.zm = f32[128,256]{1,0:T(8,128)S(1)} collective-permute-done((f32[128,256]{1,0:T(8,128)S(1)}, f32[128,256]{1,0:T(8,128)S(1)}, u32[]{:S(2)}, u32[]{:S(2)}) %collective-permute-start.20) | collective-permute-done | bytes 131104 | tf_op jit(solution)/shard_map/ppermute | solution.py:67
  48.1 1.4 %forward_inner.11 = (f32[256,256]{1,0:T(8,128)S(1)}, f32[256,256]{1,0:T(8,128)S(1)}) custom-call(s32[16]{0:T(128)S(1)} %copy-done.8, f32[8,16]{1,0:T(8,128)S(1)} %copy-done.3, f32[256,256]{1,0:T(8,128)S(1)} %get-tuple-element.199.cur.prev.before.state, f32[256,256]{1,0:T(8,128)S(1)} %get-tuple-element.194.cur.prev.before.state, ...), custom_call_target="tpu_custom_call" | custom-call | flops 1000 | bytes 4321000 | tf_op jit(solution)/shard_map/forward_inner/pallas_call | solution.py:600
  49.5 1.1 collective-permute-done.24.ym
  50.6 1.0 collective-permute-done.23.zm
  53.3 1.4 %forward_inner.12 = (f32[256,256]{1,0:T(8,128)S(1)}, f32[256,256]{1,0:T(8,128)S(1)}) custom-call(s32[16]{0:T(128)S(1)} %copy-done.8, f32[8,16]{1,0:T(8,128)S(1)} %copy-done.3, f32[256,256]{1,0:T(8,128)S(1)} %get-tuple-element.206.cur.prev.rest_2_.state, f32[256,256]{1,0:T(8,128)S(1)} %get-tuple-element.199.cur.prev.before.state, ...), custom_call_target="tpu_custom_call" | custom-call | flops 1000 | bytes 4321000 | tf_op jit(solution)/shard_map/forward_inner/pallas_call | solution.py:600
  54.6 1.4 %collective-permute-done.27.ym = f32[32,256]{1,0:T(8,128)S(1)} collective-permute-done((f32[32,256]{1,0:T(8,128)S(1)}, f32[32,256]{1,0:T(8,128)S(1)}, u32[]{:S(2)}, u32[]{:S(2)}) %collective-permute-start.27) | collective-permute-done | bytes 32800 | tf_op jit(solution)/shard_map/ppermute | solution.py:67
  58.6 1.4 %forward_inner.13 = (f32[256,256]{1,0:T(8,128)S(1)}, f32[256,256]{1,0:T(8,128)S(1)}) custom-call(s32[16]{0:T(128)S(1)} %copy-done.8, f32[8,16]{1,0:T(8,128)S(1)} %copy-done.3, f32[256,256]{1,0:T(8,128)S(1)} %get-tuple-element.215.cur.state.rest_1_, f32[256,256]{1,0:T(8,128)S(1)} %get-tuple-element.206.cur.prev.rest_2_.state, ...), custom_call_target="tpu_custom_call" | custom-call | flops 1000 | bytes 4321000 | tf_op jit(solution)/shard_map/forward_inner/pallas_call | solution.py:600
  60.0 1.4 %collective-permute-done.30.ym = f32[32,256]{1,0:T(8,128)S(1)} collective-permute-done((f32[32,256]{1,0:T(8,128)S(1)}, f32[32,256]{1,0:T(8,128)S(1)}, u32[]{:S(2)}, u32[]{:S(2)}) %collective-permute-start.30) | collective-permute-done | bytes 32800 | tf_op jit(solution)/shard_map/ppermute | solution.py:67
  64.6 1.0 adjoint_inner.7
  65.7 1.7 %collective-permute-done.33.ym = f32[32,256]{1,0:T(8,128)S(1)} collective-permute-done((f32[32,256]{1,0:T(8,128)S(1)}, f32[32,256]{1,0:T(8,128)S(1)}, u32[]{:S(2)}, u32[]{:S(2)}) %collective-permute-start.33) | collective-permute-done | bytes 32800 | tf_op jit(solution)/shard_map/ppermute | solution.py:67
  70.0 1.0 adjoint_inner.8
  71.0 1.8 %collective-permute-done.36.ym = f32[32,256]{1,0:T(8,128)S(1)} collective-permute-done((f32[32,256]{1,0:T(8,128)S(1)}, f32[32,256]{1,0:T(8,128)S(1)}, u32[]{:S(2)}, u32[]{:S(2)}) %collective-permute-start.36) | collective-permute-done | bytes 32800 | tf_op jit(solution)/shard_map/ppermute | solution.py:67
  75.4 1.0 adjoint_inner.9
  76.4 1.8 %collective-permute-done.39.ym = f32[32,256]{1,0:T(8,128)S(1)} collective-permute-done((f32[32,256]{1,0:T(8,128)S(1)}, f32[32,256]{1,0:T(8,128)S(1)}, u32[]{:S(2)}, u32[]{:S(2)}) %collective-permute-start.39) | collective-permute-done | bytes 32800 | tf_op jit(solution)/shard_map/ppermute | solution.py:67
  80.8 1.0 adjoint_inner.10
  81.8 1.8 %collective-permute-done.42.ym = f32[32,256]{1,0:T(8,128)S(1)} collective-permute-done((f32[32,256]{1,0:T(8,128)S(1)}, f32[32,256]{1,0:T(8,128)S(1)}, u32[]{:S(2)}, u32[]{:S(2)}) %collective-permute-start.42) | collective-permute-done | bytes 32800 | tf_op jit(solution)/shard_map/ppermute | solution.py:67
  86.3 1.0 adjoint_inner.11
  87.3 1.8 %collective-permute-done.45.ym = f32[32,256]{1,0:T(8,128)S(1)} collective-permute-done((f32[32,256]{1,0:T(8,128)S(1)}, f32[32,256]{1,0:T(8,128)S(1)}, u32[]{:S(2)}, u32[]{:S(2)}) %collective-permute-start.45) | collective-permute-done | bytes 32800 | tf_op jit(solution)/shard_map/ppermute | solution.py:67
  91.7 1.0 adjoint_inner.12
  92.7 1.8 %collective-permute-done.48.ym = f32[32,256]{1,0:T(8,128)S(1)} collective-permute-done((f32[32,256]{1,0:T(8,128)S(1)}, f32[32,256]{1,0:T(8,128)S(1)}, u32[]{:S(2)}, u32[]{:S(2)}) %collective-permute-start.48) | collective-permute-done | bytes 32800 | tf_op jit(solution)/shard_map/ppermute | solution.py:67
  97.1 1.0 adjoint_inner.13
  98.1 1.8 %collective-permute-done.51.ym = f32[32,256]{1,0:T(8,128)S(1)} collective-permute-done((f32[32,256]{1,0:T(8,128)S(1)}, f32[32,256]{1,0:T(8,128)S(1)}, u32[]{:S(2)}, u32[]{:S(2)}) %collective-permute-start.51) | collective-permute-done | bytes 32800 | tf_op jit(solution)/shard_map/ppermute | solution.py:67
  101.6 1.1 collective-permute-start.52
  102.7 1.0 collective-permute-done.52.got
  103.8 1.4 %collective-permute-start.53 = (f32[2,64,128]{2,1,0:T(8,128)S(1)}, f32[2,64,128]{2,1,0:T(8,128)S(1)}, u32[]{:S(2)}, u32[]{:S(2)}) collective-permute-start(f32[2,64,128]{2,1,0:T(8,128)S(1)} %get-tuple-element.275), channel_id=1, source_target_pairs={{0,12},{1,14},{2,13},{3,15},{4,8},{5,10},{6,9},{7,11},{8,4},{9,6},... | collective-permute-start | bytes 196616 | tf_op jit(solution)/shard_map/ppermute | solution.py:67
  105.2 1.7 %collective-permute-start.55 = (f32[2,64,128]{2,1,0:T(8,128)S(1)}, f32[2,64,128]{2,1,0:T(8,128)S(1)}, u32[]{:S(2)}, u32[]{:S(2)}) collective-permute-start(f32[2,64,128]{2,1,0:T(8,128)S(1)} %get-tuple-element.279), channel_id=1, source_target_pairs={{0,8},{1,10},{2,9},{3,11},{4,12},{5,14},{6,13},{7,15},{8,0},{9,2},... | collective-permute-start | bytes 196616 | tf_op jit(solution)/shard_map/ppermute | solution.py:67
  106.9 2.1 %collective-permute-start.56 = (f32[2,64,128]{2,1,0:T(8,128)S(1)}, f32[2,64,128]{2,1,0:T(8,128)S(1)}, u32[]{:S(2)}, u32[]{:S(2)}) collective-permute-start(f32[2,64,128]{2,1,0:T(8,128)S(1)} %get-tuple-element.280), channel_id=1, source_target_pairs={{0,4},{1,6},{2,5},{3,7},{4,0},{5,2},{6,1},{7,3},{8,12},{9,14},{10,... | collective-permute-start | bytes 196616 | tf_op jit(solution)/shard_map/ppermute | solution.py:67
  109.0 2.9 %collective-permute-start.57 = (f32[2,64,128]{2,1,0:T(8,128)S(1)}, f32[2,64,128]{2,1,0:T(8,128)S(1)}, u32[]{:S(2)}, u32[]{:S(2)}) collective-permute-start(f32[2,64,128]{2,1,0:T(8,128)S(1)} %get-tuple-element.281), channel_id=1, source_target_pairs={{0,0},{1,2},{2,1},{3,3},{4,4},{5,6},{6,5},{7,7},{8,8},{9,10},{10,9... | collective-permute-start | bytes 196616 | tf_op jit(solution)/shard_map/ppermute | solution.py:67
  113.0 1.5 %collective-permute-done.57.refs_3_ = f32[2,64,128]{2,1,0:T(8,128)S(1)} collective-permute-done((f32[2,64,128]{2,1,0:T(8,128)S(1)}, f32[2,64,128]{2,1,0:T(8,128)S(1)}, u32[]{:S(2)}, u32[]{:S(2)}) %collective-permute-start.57) | collective-permute-done | bytes 65568 | tf_op jit(solution)/shard_map/ppermute | solution.py:67
  114.6 1.3 %filter.1 = f32[32,32,64]{2,1,0:T(8,128)} custom-call(f32[2,64,128]{2,1,0:T(8,128)S(1)} %collective-permute-done.53.refs_0_, f32[2,64,128]{2,1,0:T(8,128)S(1)} %collective-permute-done.55.refs_1_, f32[2,64,128]{2,1,0:T(8,128)S(1)} %collective-permute-done.56.refs_2_, f32[2,64,128]{2,1,0:T(8,128)S(1)} %collective-permute-done.57.refs_3_), custom_call_target="tpu_custom_call" | custom-call | flops 1000 | bytes 1000 | tf_op jit(solution)/shard_map/filter/pallas_call | solution.py:600
  (152 shorter events, 42.7 us)
Async XLA Ops:
  0.6 10.1 %collective-permute-start.2 = (f32[256,256]{1,0:T(8,128)}, f32[256,256]{1,0:T(8,128)S(1)}, u32[]{:S(2)}, u32[]{:S(2)}) collective-permute-start(f32[256,256]{1,0:T(8,128)} %bitcast.16), channel_id=1, source_target_pairs={{0,16},{1,2},{2,1},{3,19},{4,20},{5,6},{6,5},{7,23},{8,24},{9,10},... | collective-permute-start | bytes 786440 | tf_op jit(solution)/shard_map/ppermute | solution.py:67
  3.3 7.4 %collective-permute-start = (f32[256,256]{1,0:T(8,128)}, f32[256,256]{1,0:T(8,128)S(1)}, u32[]{:S(2)}, u32[]{:S(2)}) collective-permute-start(f32[256,256]{1,0:T(8,128)} %bitcast.14), channel_id=1, source_target_pairs={{0,16},{1,2},{2,1},{3,19},{4,20},{5,6},{6,5},{7,23},{8,24},{9,10},... | collective-permute-start | bytes 786440 | tf_op jit(solution)/shard_map/ppermute | solution.py:67
  4.6 16.5 %collective-permute-start.3 = (f32[2,256,256]{2,1,0:T(8,128)S(1)}, f32[2,256,256]{2,1,0:T(8,128)S(1)}, u32[]{:S(2)}, u32[]{:S(2)}) collective-permute-start(f32[2,256,256]{2,1,0:T(8,128)S(1)} %pad_maximum_fusion), channel_id=1, source_target_pairs={{0,16},{1,2},{2,1},{3,19},{4,20},{5,6},{6,5},{7,23},{8,24},{9,10},... | collective-permute-start | bytes 1572872 | tf_op jit(solution)/shard_map/ppermute | solution.py:67
  6.5 3.9 %collective-permute-start.1 = (f32[8,8,128]{2,1,0:T(8,128)S(1)}, f32[8,8,128]{2,1,0:T(8,128)S(1)}, u32[]{:S(2)}, u32[]{:S(2)}) collective-permute-start(f32[8,8,128]{2,1,0:T(8,128)S(1)} %get-tuple-element.146), channel_id=1, source_target_pairs={{0,4},{1,5},{2,6},{3,7},{4,0},{5,1},{6,2},{7,3},{8,12},{9,13},{10,... | collective-permute-start | bytes 98312 | tf_op jit(solution)/shard_map/ppermute | solution.py:67
  10.9 5.4 %collective-permute-start.4 = (f32[2,128,256]{2,1,0:T(8,128)S(1)}, f32[2,128,256]{2,1,0:T(8,128)S(1)}, u32[]{:S(2)}, u32[]{:S(2)}) collective-permute-start(f32[2,128,256]{2,1,0:T(8,128)S(1)} %get-tuple-element.153), channel_id=1, source_target_pairs={{0,1},{1,0},{2,3},{3,2},{4,5},{5,4},{6,7},{7,6},{8,9},{9,8},{10,11... | collective-permute-start | bytes 786440 | tf_op jit(solution)/shard_map/ppermute | solution.py:67
  11.7 9.6 %collective-permute-start.5 = (f32[2,128,256]{2,1,0:T(8,128)S(1)}, f32[2,128,256]{2,1,0:T(8,128)S(1)}, u32[]{:S(2)}, u32[]{:S(2)}) collective-permute-start(f32[2,128,256]{2,1,0:T(8,128)S(1)} %get-tuple-element.162), channel_id=1, source_target_pairs={{0,16},{1,4},{2,18},{3,6},{4,1},{5,8},{6,3},{7,10},{8,5},{9,12},{1... | collective-permute-start | bytes 786440 | tf_op jit(solution)/shard_map/ppermute | solution.py:67
  13.2 4.6 %collective-permute-start.7 = (f32[8,8,128]{2,1,0:T(8,128)S(1)}, f32[8,8,128]{2,1,0:T(8,128)S(1)}, u32[]{:S(2)}, u32[]{:S(2)}) collective-permute-start(f32[8,8,128]{2,1,0:T(8,128)S(1)} %get-tuple-element.165), channel_id=1, source_target_pairs={{0,8},{1,9},{2,10},{3,11},{4,12},{5,13},{6,14},{7,15},{8,0},{9,1},... | collective-permute-start | bytes 98312 | tf_op jit(solution)/shard_map/ppermute | solution.py:67
  15.6 5.7 %collective-permute-start.6 = (f32[2,32,256]{2,1,0:T(8,128)S(1)}, f32[2,32,256]{2,1,0:T(8,128)S(1)}, u32[]{:S(2)}, u32[]{:S(2)}) collective-permute-start(f32[2,32,256]{2,1,0:T(8,128)S(1)} %get-tuple-element.163), channel_id=1, source_target_pairs={{0,2},{1,3},{2,0},{3,1},{4,6},{5,7},{6,4},{7,5},{8,10},{9,11},{10,... | collective-permute-start | bytes 196616 | tf_op jit(solution)/shard_map/ppermute | solution.py:67
  17.2 8.0 %collective-permute-start.9 = (f32[256,256]{1,0:T(8,128)S(1)}, f32[256,256]{1,0:T(8,128)S(1)}, u32[]{:S(2)}, u32[]{:S(2)}) collective-permute-start(f32[256,256]{1,0:T(8,128)S(1)} %bitcast.18), channel_id=1, source_target_pairs={{0,16},{1,2},{2,1},{3,19},{4,20},{5,6},{6,5},{7,23},{8,24},{9,10},... | collective-permute-start | bytes 786440 | tf_op jit(solution)/shard_map/ppermute | solution.py:67
  17.8 8.3 %collective-permute-start.10 = (f32[256,256]{1,0:T(8,128)S(1)}, f32[256,256]{1,0:T(8,128)S(1)}, u32[]{:S(2)}, u32[]{:S(2)}) collective-permute-start(f32[256,256]{1,0:T(8,128)S(1)} %bitcast.20), channel_id=1, source_target_pairs={{0,16},{1,2},{2,1},{3,19},{4,20},{5,6},{6,5},{7,23},{8,24},{9,10},... | collective-permute-start | bytes 786440 | tf_op jit(solution)/shard_map/ppermute | solution.py:67
  21.8 2.1 %collective-permute-start.8 = (f32[168,256]{1,0:T(8,128)S(1)}, f32[168,256]{1,0:T(8,128)S(1)}, u32[]{:S(2)}, u32[]{:S(2)}) collective-permute-start(f32[168,256]{1,0:T(8,128)S(1)} %get-tuple-element.173), channel_id=1, source_target_pairs={{0,1},{1,0},{2,3},{3,2},{4,5},{5,4},{6,7},{7,6},{8,9},{9,8},{10,11... | collective-permute-start | bytes 516104 | tf_op jit(solution)/shard_map/ppermute | solution.py:67
  22.8 4.7 %collective-permute-start.11 = (f32[128,256]{1,0:T(8,128)S(1)}, f32[128,256]{1,0:T(8,128)S(1)}, u32[]{:S(2)}, u32[]{:S(2)}) collective-permute-start(f32[128,256]{1,0:T(8,128)S(1)} %get-tuple-element.179), channel_id=1, source_target_pairs={{0,16},{1,4},{2,18},{3,6},{4,1},{5,8},{6,3},{7,10},{8,5},{9,12},{1... | collective-permute-start | bytes 393224 | tf_op jit(solution)/shard_map/ppermute | solution.py:67
  23.7 3.1 %collective-permute-start.12 = (f32[32,256]{1,0:T(8,128)S(1)}, f32[32,256]{1,0:T(8,128)S(1)}, u32[]{:S(2)}, u32[]{:S(2)}) collective-permute-start(f32[32,256]{1,0:T(8,128)S(1)} %get-tuple-element.180), channel_id=1, source_target_pairs={{0,2},{1,3},{2,0},{3,1},{4,6},{5,7},{6,4},{7,5},{8,10},{9,11},{10,... | collective-permute-start | bytes 98312 | tf_op jit(solution)/shard_map/ppermute | solution.py:67
  27.8 1.8 %collective-permute-start.13 = (f32[128,256]{1,0:T(8,128)S(1)}, f32[128,256]{1,0:T(8,128)S(1)}, u32[]{:S(2)}, u32[]{:S(2)}) collective-permute-start(f32[128,256]{1,0:T(8,128)S(1)} %get-tuple-element.183), channel_id=1, source_target_pairs={{0,1},{1,0},{2,3},{3,2},{4,5},{5,4},{6,7},{7,6},{8,9},{9,8},{10,11... | collective-permute-start | bytes 393224 | tf_op jit(solution)/shard_map/ppermute | solution.py:67
  28.5 4.7 %collective-permute-start.14 = (f32[128,256]{1,0:T(8,128)S(1)}, f32[128,256]{1,0:T(8,128)S(1)}, u32[]{:S(2)}, u32[]{:S(2)}) collective-permute-start(f32[128,256]{1,0:T(8,128)S(1)} %get-tuple-element.185), channel_id=1, source_target_pairs={{0,16},{1,4},{2,18},{3,6},{4,1},{5,8},{6,3},{7,10},{8,5},{9,12},{1... | collective-permute-start | bytes 393224 | tf_op jit(solution)/shard_map/ppermute | solution.py:67
  28.9 3.5 %collective-permute-start.15 = (f32[72,256]{1,0:T(8,128)S(1)}, f32[72,256]{1,0:T(8,128)S(1)}, u32[]{:S(2)}, u32[]{:S(2)}) collective-permute-start(f32[72,256]{1,0:T(8,128)S(1)} %get-tuple-element.186), channel_id=1, source_target_pairs={{0,2},{1,3},{2,0},{3,1},{4,6},{5,7},{6,4},{7,5},{8,10},{9,11},{10,... | collective-permute-start | bytes 221192 | tf_op jit(solution)/shard_map/ppermute | solution.py:67
  33.4 2.5 %collective-permute-start.16 = (f32[2,128,256]{2,1,0:T(8,128)S(1)}, f32[2,128,256]{2,1,0:T(8,128)S(1)}, u32[]{:S(2)}, u32[]{:S(2)}) collective-permute-start(f32[2,128,256]{2,1,0:T(8,128)S(1)} %get-tuple-element.190), channel_id=1, source_target_pairs={{0,1},{1,0},{2,3},{3,2},{4,5},{5,4},{6,7},{7,6},{8,9},{9,8},{10,11... | collective-permute-start | bytes 786440 | tf_op jit(solution)/shard_map/ppermute | solution.py:67
  34.8 6.1 %collective-permute-start.17 = (f32[2,128,256]{2,1,0:T(8,128)S(1)}, f32[2,128,256]{2,1,0:T(8,128)S(1)}, u32[]{:S(2)}, u32[]{:S(2)}) collective-permute-start(f32[2,128,256]{2,1,0:T(8,128)S(1)} %get-tuple-element.192), channel_id=1, source_target_pairs={{0,16},{1,4},{2,18},{3,6},{4,1},{5,8},{6,3},{7,10},{8,5},{9,12},{1... | collective-permute-start | bytes 786440 | tf_op jit(solution)/shard_map/ppermute | solution.py:67
  35.0 3.4 %collective-permute-start.18 = (f32[2,32,256]{2,1,0:T(8,128)S(1)}, f32[2,32,256]{2,1,0:T(8,128)S(1)}, u32[]{:S(2)}, u32[]{:S(2)}) collective-permute-start(f32[2,32,256]{2,1,0:T(8,128)S(1)} %get-tuple-element.193), channel_id=1, source_target_pairs={{0,2},{1,3},{2,0},{3,1},{4,6},{5,7},{6,4},{7,5},{8,10},{9,11},{10,... | collective-permute-start | bytes 196616 | tf_op jit(solution)/shard_map/ppermute | solution.py:67
  41.5 4.7 %collective-permute-start.20 = (f32[128,256]{1,0:T(8,128)S(1)}, f32[128,256]{1,0:T(8,128)S(1)}, u32[]{:S(2)}, u32[]{:S(2)}) collective-permute-start(f32[128,256]{1,0:T(8,128)S(1)} %get-tuple-element.197), channel_id=1, source_target_pairs={{0,16},{1,4},{2,18},{3,6},{4,1},{5,8},{6,3},{7,10},{8,5},{9,12},{1... | collective-permute-start | bytes 393224 | tf_op jit(solution)/shard_map/ppermute | solution.py:67
  41.5 2.8 %collective-permute-start.21 = (f32[32,256]{1,0:T(8,128)S(1)}, f32[32,256]{1,0:T(8,128)S(1)}, u32[]{:S(2)}, u32[]{:S(2)}) collective-permute-start(f32[32,256]{1,0:T(8,128)S(1)} %get-tuple-element.198), channel_id=1, source_target_pairs={{0,2},{1,3},{2,0},{3,1},{4,6},{5,7},{6,4},{7,5},{8,10},{9,11},{10,... | collective-permute-start | bytes 98312 | tf_op jit(solution)/shard_map/ppermute | solution.py:67
  46.4 1.7 %collective-permute-start.22 = (f32[128,256]{1,0:T(8,128)S(1)}, f32[128,256]{1,0:T(8,128)S(1)}, u32[]{:S(2)}, u32[]{:S(2)}) collective-permute-start(f32[128,256]{1,0:T(8,128)S(1)} %get-tuple-element.200), channel_id=1, source_target_pairs={{0,1},{1,0},{2,3},{3,2},{4,5},{5,4},{6,7},{7,6},{8,9},{9,8},{10,11... | collective-permute-start | bytes 393224 | tf_op jit(solution)/shard_map/ppermute | solution.py:67
  46.9 4.7 %collective-permute-start.23 = (f32[128,256]{1,0:T(8,128)S(1)}, f32[128,256]{1,0:T(8,128)S(1)}, u32[]{:S(2)}, u32[]{:S(2)}) collective-permute-start(f32[128,256]{1,0:T(8,128)S(1)} %get-tuple-element.204), channel_id=1, source_target_pairs={{0,16},{1,4},{2,18},{3,6},{4,1},{5,8},{6,3},{7,10},{8,5},{9,12},{1... | collective-permute-start | bytes 393224 | tf_op jit(solution)/shard_map/ppermute | solution.py:67
  47.5 3.1 %collective-permute-start.24 = (f32[32,256]{1,0:T(8,128)S(1)}, f32[32,256]{1,0:T(8,128)S(1)}, u32[]{:S(2)}, u32[]{:S(2)}) collective-permute-start(f32[32,256]{1,0:T(8,128)S(1)} %get-tuple-element.205), channel_id=1, source_target_pairs={{0,2},{1,3},{2,0},{3,1},{4,6},{5,7},{6,4},{7,5},{8,10},{9,11},{10,... | collective-permute-start | bytes 98312 | tf_op jit(solution)/shard_map/ppermute | solution.py:67
  52.3 4.7 %collective-permute-start.26 = (f32[128,256]{1,0:T(8,128)S(1)}, f32[128,256]{1,0:T(8,128)S(1)}, u32[]{:S(2)}, u32[]{:S(2)}) collective-permute-start(f32[128,256]{1,0:T(8,128)S(1)} %get-tuple-element.213), channel_id=1, source_target_pairs={{0,16},{1,4},{2,18},{3,6},{4,1},{5,8},{6,3},{7,10},{8,5},{9,12},{1... | collective-permute-start | bytes 393224 | tf_op jit(solution)/shard_map/ppermute | solution.py:67
  53.0 3.1 %collective-permute-start.27 = (f32[32,256]{1,0:T(8,128)S(1)}, f32[32,256]{1,0:T(8,128)S(1)}, u32[]{:S(2)}, u32[]{:S(2)}) collective-permute-start(f32[32,256]{1,0:T(8,128)S(1)} %get-tuple-element.214), channel_id=1, source_target_pairs={{0,2},{1,3},{2,0},{3,1},{4,6},{5,7},{6,4},{7,5},{8,10},{9,11},{10,... | collective-permute-start | bytes 98312 | tf_op jit(solution)/shard_map/ppermute | solution.py:67
  57.6 4.7 %collective-permute-start.29 = (f32[128,256]{1,0:T(8,128)S(1)}, f32[128,256]{1,0:T(8,128)S(1)}, u32[]{:S(2)}, u32[]{:S(2)}) collective-permute-start(f32[128,256]{1,0:T(8,128)S(1)} %get-tuple-element.218), channel_id=1, source_target_pairs={{0,16},{1,4},{2,18},{3,6},{4,1},{5,8},{6,3},{7,10},{8,5},{9,12},{1... | collective-permute-start | bytes 393224 | tf_op jit(solution)/shard_map/ppermute | solution.py:67
  58.3 3.1 %collective-permute-start.30 = (f32[32,256]{1,0:T(8,128)S(1)}, f32[32,256]{1,0:T(8,128)S(1)}, u32[]{:S(2)}, u32[]{:S(2)}) collective-permute-start(f32[32,256]{1,0:T(8,128)S(1)} %get-tuple-element.219), channel_id=1, source_target_pairs={{0,2},{1,3},{2,0},{3,1},{4,6},{5,7},{6,4},{7,5},{8,10},{9,11},{10,... | collective-permute-start | bytes 98312 | tf_op jit(solution)/shard_map/ppermute | solution.py:67
  63.6 4.7 %collective-permute-start.32 = (f32[128,256]{1,0:T(8,128)S(1)}, f32[128,256]{1,0:T(8,128)S(1)}, u32[]{:S(2)}, u32[]{:S(2)}) collective-permute-start(f32[128,256]{1,0:T(8,128)S(1)} %get-tuple-element.227), channel_id=1, source_target_pairs={{0,16},{1,4},{2,18},{3,6},{4,1},{5,8},{6,3},{7,10},{8,5},{9,12},{1... | collective-permute-start | bytes 393224 | tf_op jit(solution)/shard_map/ppermute | solution.py:67
  64.3 3.1 %collective-permute-start.33 = (f32[32,256]{1,0:T(8,128)S(1)}, f32[32,256]{1,0:T(8,128)S(1)}, u32[]{:S(2)}, u32[]{:S(2)}) collective-permute-start(f32[32,256]{1,0:T(8,128)S(1)} %get-tuple-element.228), channel_id=1, source_target_pairs={{0,2},{1,3},{2,0},{3,1},{4,6},{5,7},{6,4},{7,5},{8,10},{9,11},{10,... | collective-permute-start | bytes 98312 | tf_op jit(solution)/shard_map/ppermute | solution.py:67
  69.0 4.7 %collective-permute-start.35 = (f32[128,256]{1,0:T(8,128)S(1)}, f32[128,256]{1,0:T(8,128)S(1)}, u32[]{:S(2)}, u32[]{:S(2)}) collective-permute-start(f32[128,256]{1,0:T(8,128)S(1)} %get-tuple-element.234), channel_id=1, source_target_pairs={{0,16},{1,4},{2,18},{3,6},{4,1},{5,8},{6,3},{7,10},{8,5},{9,12},{1... | collective-permute-start | bytes 393224 | tf_op jit(solution)/shard_map/ppermute | solution.py:67
  69.7 3.1 %collective-permute-start.36 = (f32[32,256]{1,0:T(8,128)S(1)}, f32[32,256]{1,0:T(8,128)S(1)}, u32[]{:S(2)}, u32[]{:S(2)}) collective-permute-start(f32[32,256]{1,0:T(8,128)S(1)} %get-tuple-element.235), channel_id=1, source_target_pairs={{0,2},{1,3},{2,0},{3,1},{4,6},{5,7},{6,4},{7,5},{8,10},{9,11},{10,... | collective-permute-start | bytes 98312 | tf_op jit(solution)/shard_map/ppermute | solution.py:67
  74.4 4.7 %collective-permute-start.38 = (f32[128,256]{1,0:T(8,128)S(1)}, f32[128,256]{1,0:T(8,128)S(1)}, u32[]{:S(2)}, u32[]{:S(2)}) collective-permute-start(f32[128,256]{1,0:T(8,128)S(1)} %get-tuple-element.241), channel_id=1, source_target_pairs={{0,16},{1,4},{2,18},{3,6},{4,1},{5,8},{6,3},{7,10},{8,5},{9,12},{1... | collective-permute-start | bytes 393224 | tf_op jit(solution)/shard_map/ppermute | solution.py:67
  75.1 3.1 %collective-permute-start.39 = (f32[32,256]{1,0:T(8,128)S(1)}, f32[32,256]{1,0:T(8,128)S(1)}, u32[]{:S(2)}, u32[]{:S(2)}) collective-permute-start(f32[32,256]{1,0:T(8,128)S(1)} %get-tuple-element.242), channel_id=1, source_target_pairs={{0,2},{1,3},{2,0},{3,1},{4,6},{5,7},{6,4},{7,5},{8,10},{9,11},{10,... | collective-permute-start | bytes 98312 | tf_op jit(solution)/shard_map/ppermute | solution.py:67
  79.8 4.7 %collective-permute-start.41 = (f32[128,256]{1,0:T(8,128)S(1)}, f32[128,256]{1,0:T(8,128)S(1)}, u32[]{:S(2)}, u32[]{:S(2)}) collective-permute-start(f32[128,256]{1,0:T(8,128)S(1)} %get-tuple-element.248), channel_id=1, source_target_pairs={{0,16},{1,4},{2,18},{3,6},{4,1},{5,8},{6,3},{7,10},{8,5},{9,12},{1... | collective-permute-start | bytes 393224 | tf_op jit(solution)/shard_map/ppermute | solution.py:67
  80.5 3.1 %collective-permute-start.42 = (f32[32,256]{1,0:T(8,128)S(1)}, f32[32,256]{1,0:T(8,128)S(1)}, u32[]{:S(2)}, u32[]{:S(2)}) collective-permute-start(f32[32,256]{1,0:T(8,128)S(1)} %get-tuple-element.249), channel_id=1, source_target_pairs={{0,2},{1,3},{2,0},{3,1},{4,6},{5,7},{6,4},{7,5},{8,10},{9,11},{10,... | collective-permute-start | bytes 98312 | tf_op jit(solution)/shard_map/ppermute | solution.py:67
  85.4 4.7 %collective-permute-start.44 = (f32[128,256]{1,0:T(8,128)S(1)}, f32[128,256]{1,0:T(8,128)S(1)}, u32[]{:S(2)}, u32[]{:S(2)}) collective-permute-start(f32[128,256]{1,0:T(8,128)S(1)} %get-tuple-element.255), channel_id=1, source_target_pairs={{0,16},{1,4},{2,18},{3,6},{4,1},{5,8},{6,3},{7,10},{8,5},{9,12},{1... | collective-permute-start | bytes 393224 | tf_op jit(solution)/shard_map/ppermute | solution.py:67
  86.0 3.1 %collective-permute-start.45 = (f32[32,256]{1,0:T(8,128)S(1)}, f32[32,256]{1,0:T(8,128)S(1)}, u32[]{:S(2)}, u32[]{:S(2)}) collective-permute-start(f32[32,256]{1,0:T(8,128)S(1)} %get-tuple-element.256), channel_id=1, source_target_pairs={{0,2},{1,3},{2,0},{3,1},{4,6},{5,7},{6,4},{7,5},{8,10},{9,11},{10,... | collective-permute-start | bytes 98312 | tf_op jit(solution)/shard_map/ppermute | solution.py:67
  90.7 4.7 %collective-permute-start.47 = (f32[128,256]{1,0:T(8,128)S(1)}, f32[128,256]{1,0:T(8,128)S(1)}, u32[]{:S(2)}, u32[]{:S(2)}) collective-permute-start(f32[128,256]{1,0:T(8,128)S(1)} %get-tuple-element.262), channel_id=1, source_target_pairs={{0,16},{1,4},{2,18},{3,6},{4,1},{5,8},{6,3},{7,10},{8,5},{9,12},{1... | collective-permute-start | bytes 393224 | tf_op jit(solution)/shard_map/ppermute | solution.py:67
  91.4 3.1 %collective-permute-start.48 = (f32[32,256]{1,0:T(8,128)S(1)}, f32[32,256]{1,0:T(8,128)S(1)}, u32[]{:S(2)}, u32[]{:S(2)}) collective-permute-start(f32[32,256]{1,0:T(8,128)S(1)} %get-tuple-element.263), channel_id=1, source_target_pairs={{0,2},{1,3},{2,0},{3,1},{4,6},{5,7},{6,4},{7,5},{8,10},{9,11},{10,... | collective-permute-start | bytes 98312 | tf_op jit(solution)/shard_map/ppermute | solution.py:67
  96.1 4.7 %collective-permute-start.50 = (f32[128,256]{1,0:T(8,128)S(1)}, f32[128,256]{1,0:T(8,128)S(1)}, u32[]{:S(2)}, u32[]{:S(2)}) collective-permute-start(f32[128,256]{1,0:T(8,128)S(1)} %get-tuple-element.269), channel_id=1, source_target_pairs={{0,16},{1,4},{2,18},{3,6},{4,1},{5,8},{6,3},{7,10},{8,5},{9,12},{1... | collective-permute-start | bytes 393224 | tf_op jit(solution)/shard_map/ppermute | solution.py:67
  96.8 3.1 %collective-permute-start.51 = (f32[32,256]{1,0:T(8,128)S(1)}, f32[32,256]{1,0:T(8,128)S(1)}, u32[]{:S(2)}, u32[]{:S(2)}) collective-permute-start(f32[32,256]{1,0:T(8,128)S(1)} %get-tuple-element.270), channel_id=1, source_target_pairs={{0,2},{1,3},{2,0},{3,1},{4,6},{5,7},{6,4},{7,5},{8,10},{9,11},{10,... | collective-permute-start | bytes 98312 | tf_op jit(solution)/shard_map/ppermute | solution.py:67
  101.3 10.6 %collective-permute-start.54 = (f32[2,256,256]{2,1,0:T(8,128)S(1)}, f32[2,256,256]{2,1,0:T(8,128)S(1)}, u32[]{:S(2)}, u32[]{:S(2)}) collective-permute-start(f32[2,256,256]{2,1,0:T(8,128)S(1)} %get-tuple-element.276.own), channel_id=1, source_target_pairs={{0,16},{1,2},{2,1},{3,19},{4,20},{5,6},{6,5},{7,23},{8,24},{9,10},... | collective-permute-start | bytes 1572872 | tf_op jit(solution)/shard_map/ppermute | solution.py:67
  101.6 2.1 %collective-permute-start.52 = (f32[4,64,128]{2,1,0:T(8,128)S(1)}, f32[4,64,128]{2,1,0:T(8,128)S(1)}, u32[]{:S(2)}, u32[]{:S(2)}) collective-permute-start(f32[4,64,128]{2,1,0:T(8,128)S(1)} %get-tuple-element.274), channel_id=1, source_target_pairs={{0,1},{1,0},{2,3},{3,2},{4,5},{5,4},{6,7},{7,6},{8,9},{9,8},{10,11... | collective-permute-start | bytes 393224 | tf_op jit(solution)/shard_map/ppermute | solution.py:67
  103.8 9.0 %collective-permute-start.53 = (f32[2,64,128]{2,1,0:T(8,128)S(1)}, f32[2,64,128]{2,1,0:T(8,128)S(1)}, u32[]{:S(2)}, u32[]{:S(2)}) collective-permute-start(f32[2,64,128]{2,1,0:T(8,128)S(1)} %get-tuple-element.275), channel_id=1, source_target_pairs={{0,12},{1,14},{2,13},{3,15},{4,8},{5,10},{6,9},{7,11},{8,4},{9,6},... | collective-permute-start | bytes 196616 | tf_op jit(solution)/shard_map/ppermute | solution.py:67
  105.2 7.9 %collective-permute-start.55 = (f32[2,64,128]{2,1,0:T(8,128)S(1)}, f32[2,64,128]{2,1,0:T(8,128)S(1)}, u32[]{:S(2)}, u32[]{:S(2)}) collective-permute-start(f32[2,64,128]{2,1,0:T(8,128)S(1)} %get-tuple-element.279), channel_id=1, source_target_pairs={{0,8},{1,10},{2,9},{3,11},{4,12},{5,14},{6,13},{7,15},{8,0},{9,2},... | collective-permute-start | bytes 196616 | tf_op jit(solution)/shard_map/ppermute | solution.py:67
  106.9 6.2 %collective-permute-start.56 = (f32[2,64,128]{2,1,0:T(8,128)S(1)}, f32[2,64,128]{2,1,0:T(8,128)S(1)}, u32[]{:S(2)}, u32[]{:S(2)}) collective-permute-start(f32[2,64,128]{2,1,0:T(8,128)S(1)} %get-tuple-element.280), channel_id=1, source_target_pairs={{0,4},{1,6},{2,5},{3,7},{4,0},{5,2},{6,1},{7,3},{8,12},{9,14},{10,... | collective-permute-start | bytes 196616 | tf_op jit(solution)/shard_map/ppermute | solution.py:67
  109.0 5.6 %collective-permute-start.57 = (f32[2,64,128]{2,1,0:T(8,128)S(1)}, f32[2,64,128]{2,1,0:T(8,128)S(1)}, u32[]{:S(2)}, u32[]{:S(2)}) collective-permute-start(f32[2,64,128]{2,1,0:T(8,128)S(1)} %get-tuple-element.281), channel_id=1, source_target_pairs={{0,0},{1,2},{2,1},{3,3},{4,4},{5,6},{6,5},{7,7},{8,8},{9,10},{10,9... | collective-permute-start | bytes 196616 | tf_op jit(solution)/shard_map/ppermute | solution.py:67
  (28 other events, 61.9 us)

commit v18 on v17

--- a/solution.py
+++ b/solution.py
@@ -259,6 +259,14 @@
     *recv, a_out, b_out, sems = rest
     recv = recv if len(recv) == 2 else (recv[0].at[0], recv[0].at[1])
     choose(flags, [(a, recv[0], a_out), (b, recv[1], b_out)], sems)
+
+
+def gather_kernel(flags, a, b, out, sems):
+    copies = [pltpu.make_async_copy(part, out.at[n], sems.at[n]) for n, part in enumerate((a, b))]
+    for copy in copies:
+        copy.start()
+    for copy in copies:
+        copy.wait()
 
 
 def select_kernel(flags, own, recv, *outs):
@@ -658,7 +666,9 @@
     full = nx * cols
     inj, = call(functools.partial(source_kernel, 0, full), "source", [field], src_cell, wavelet,
                 weight=0.7, scalars=2)
-    got[0], inj = lax.optimization_barrier((got[0], inj))
+    adjoint, = call(gather_kernel, "gather", [shaped(2, *field.shape)], after(adj_now, stacked),
+                    adj_before, weight=0.3, far=2)
+    got[0], inj, adjoint = lax.optimization_barrier((got[0], inj, adjoint))
     slots = subs * CAP
     entries, half_entries = shaped(subs, steps, 128), shaped(subs // 2, steps, 128)
     order = [*range(2, len(stages)), 0]
@@ -682,7 +692,7 @@
                          velocity, fwd_before, got_model, weight=0.6, far=2)
     parts = call(first_inner_kernel, "first_inner", [field] * 7, density, p_now, cm,
                  near, deep, weight=1.3)
-    got_adjoint = [send(after(v, parts[0]), swap_perm) for v in (adj_now, adj_before)]
+    got_adjoint = send(after(adjoint, parts[0]), swap_perm)
 
     riders = subs // 4 * 8 + 8
     core_rim = shaped(size // 2 + riders, depth)
@@ -720,7 +730,7 @@
             break
         if t == 1:
             u_now, u_before = call(settle_pair_kernel, "settle_adjoint", [field, field], adj_now,
-                                   adj_before, *got_adjoint, weight=0.6, far=2)
+                                   adj_before, got_adjoint, weight=0.6, far=2)
             args[0] = after(part, u_now)
             new, *out, lists, pair = call(
                 core_stage_kernel, "forward_outer",

time: 116 us -> 122 us (1.052)
  waiting for transfers between devices: 43.8 us -> 46.2 us
  other arithmetic: 1.27 us -> 2.9 us
    ppermute x58 -> x57, waiting for transfers between devices: 43.8 us -> 46.2 us  [send(): return lax.ppermute(value, ALL, pairs)]
    ppermute x58 -> x57, starting transfers between devices: 41.2 us -> 42.2 us  [send(): return lax.ppermute(value, ALL, pairs)]
    pallas_call x42 -> x43, Pallas kernels: 26.8 us -> 27.2 us  [call(): pl.pallas_call(functools.partial(kernel, Flags()), name=name, out_shape=o...]
  transfers between devices with their start and end apart: 58 -> 57, of which waited for: 46 -> 46; matrix products, arithmetic and copies ran while one was open for 1% -> 2% of each run, Pallas kernels for 18% -> 18%
where the time goes in v18:
time: 122 us
  waiting for transfers between devices  46.2 us (38%)
  starting transfers between devices  42.2 us (35%)
  Pallas kernels  27.2 us (22%)
  other arithmetic  2.9 us (2%)
  local copies, waits for them, and re-layouts  2.42 us (2%)
    ppermute x57, waiting for transfers between devices, send(): return lax.ppermute(value, ALL, pairs)  46.2 us
    ppermute x57, starting transfers between devices, send(): return lax.ppermute(value, ALL, pairs)  42.2 us
    pallas_call x43, Pallas kernels, call(): pl.pallas_call(functools.partial(kernel, Flags()), name=name, out_shape=o...  27.2 us
  transfers between devices with their start and end apart: 57, of which 46 were waited for; matrix products, arithmetic and copies ran while one was open for 2% of the time, Pallas kernels for 18%

profile of v18, /device:TPU:1, one launch (start us, length us, event | category | flops | bytes accessed | tf_op | source)
XLA Modules:
  0.0 122.2 jit_solution(6451727647610618120)
XLA Ops:
  0.6 2.7 %collective-permute-start = (f32[256,256]{1,0:T(8,128)}, f32[256,256]{1,0:T(8,128)S(1)}, u32[]{:S(2)}, u32[]{:S(2)}) collective-permute-start(f32[256,256]{1,0:T(8,128)} %bitcast.18), channel_id=1, source_target_pairs={{0,16},{1,2},{2,1},{3,19},{4,20},{5,6},{6,5},{7,23},{8,24},{9,10},... | collective-permute-start | bytes 786440 | tf_op jit(solution)/shard_map/ppermute | solution.py:67
  3.4 1.9 %pad_maximum_fusion = f32[2,256,256]{2,1,0:T(8,128)} fusion(f32[1,256,256]{2,1,0:T(8,128)} %bitcast.12, f32[1,256,256]{2,1,0:T(8,128)} %bitcast.10), kind=kLoop, calls=%fused_computation | loop fusion | flops 131072 | bytes 1048576 | tf_op jit(solution)/shard_map/stack | solution.py:664
  5.6 1.4 %collective-permute-start.1 = (f32[8,8,128]{2,1,0:T(8,128)S(1)}, f32[8,8,128]{2,1,0:T(8,128)S(1)}, u32[]{:S(2)}, u32[]{:S(2)}) collective-permute-start(f32[8,8,128]{2,1,0:T(8,128)S(1)} %get-tuple-element.148), channel_id=1, source_target_pairs={{0,4},{1,5},{2,6},{3,7},{4,0},{5,1},{6,2},{7,3},{8,12},{9,13},{10,... | collective-permute-start | bytes 98312 | tf_op jit(solution)/shard_map/ppermute | solution.py:67
  6.9 1.9 %collective-permute-start.3 = (f32[2,256,256]{2,1,0:T(8,128)}, f32[2,256,256]{2,1,0:T(8,128)S(1)}, u32[]{:S(2)}, u32[]{:S(2)}) collective-permute-start(f32[2,256,256]{2,1,0:T(8,128)} %pad_maximum_fusion), channel_id=1, source_target_pairs={{0,16},{1,2},{2,1},{3,19},{4,20},{5,6},{6,5},{7,23},{8,24},{9,10},... | collective-permute-start | bytes 1572872 | tf_op jit(solution)/shard_map/ppermute | solution.py:67
  15.3 1.8 %collective-permute-start.5 = (f32[2,128,256]{2,1,0:T(8,128)}, f32[2,128,256]{2,1,0:T(8,128)S(1)}, u32[]{:S(2)}, u32[]{:S(2)}) collective-permute-start(f32[2,128,256]{2,1,0:T(8,128)} %copy-done.14), channel_id=1, source_target_pairs={{0,16},{1,4},{2,18},{3,6},{4,1},{5,8},{6,3},{7,10},{8,5},{9,12},{1... | collective-permute-start | bytes 786440 | tf_op jit(solution)/shard_map/ppermute | solution.py:67
  18.9 1.6 %collective-permute-start.7 = (f32[8,8,128]{2,1,0:T(8,128)S(1)}, f32[8,8,128]{2,1,0:T(8,128)S(1)}, u32[]{:S(2)}, u32[]{:S(2)}) collective-permute-start(f32[8,8,128]{2,1,0:T(8,128)S(1)} %get-tuple-element.167), channel_id=1, source_target_pairs={{0,8},{1,9},{2,10},{3,11},{4,12},{5,13},{6,14},{7,15},{8,0},{9,1},... | collective-permute-start | bytes 98312 | tf_op jit(solution)/shard_map/ppermute | solution.py:67
  20.5 1.8 %collective-permute-start.6 = (f32[2,32,256]{2,1,0:T(8,128)S(1)}, f32[2,32,256]{2,1,0:T(8,128)S(1)}, u32[]{:S(2)}, u32[]{:S(2)}) collective-permute-start(f32[2,32,256]{2,1,0:T(8,128)S(1)} %get-tuple-element.165), channel_id=1, source_target_pairs={{0,2},{1,3},{2,0},{3,1},{4,6},{5,7},{6,4},{7,5},{8,10},{9,11},{10,... | collective-permute-start | bytes 196616 | tf_op jit(solution)/shard_map/ppermute | solution.py:67
  22.4 1.0 collective-permute-done.7.got
  23.6 2.8 %collective-permute-done.6.ym = f32[2,32,256]{2,1,0:T(8,128)S(1)} collective-permute-done((f32[2,32,256]{2,1,0:T(8,128)S(1)}, f32[2,32,256]{2,1,0:T(8,128)S(1)}, u32[]{:S(2)}, u32[]{:S(2)}) %collective-permute-start.6) | collective-permute-done | bytes 65568 | tf_op jit(solution)/shard_map/ppermute | solution.py:67
  26.9 2.4 %collective-permute-start.8 = (f32[168,256]{1,0:T(8,128)S(1)}, f32[168,256]{1,0:T(8,128)S(1)}, u32[]{:S(2)}, u32[]{:S(2)}) collective-permute-start(f32[168,256]{1,0:T(8,128)S(1)} %get-tuple-element.175), channel_id=1, source_target_pairs={{0,1},{1,0},{2,3},{3,2},{4,5},{5,4},{6,7},{7,6},{8,9},{9,8},{10,11... | collective-permute-start | bytes 516104 | tf_op jit(solution)/shard_map/ppermute | solution.py:67
  29.3 1.3 %collective-permute-start.10 = (f32[128,256]{1,0:T(8,128)S(1)}, f32[128,256]{1,0:T(8,128)S(1)}, u32[]{:S(2)}, u32[]{:S(2)}) collective-permute-start(f32[128,256]{1,0:T(8,128)S(1)} %get-tuple-element.181), channel_id=1, source_target_pairs={{0,16},{1,4},{2,18},{3,6},{4,1},{5,8},{6,3},{7,10},{8,5},{9,12},{1... | collective-permute-start | bytes 393224 | tf_op jit(solution)/shard_map/ppermute | solution.py:67
  30.5 1.3 %forward_inner.7 = (f32[256,256]{1,0:T(8,128)S(1)}, f32[256,256]{1,0:T(8,128)S(1)}) custom-call(s32[16]{0:T(128)S(1)} %copy-done.10, f32[8,16]{1,0:T(8,128)S(1)} %copy-done.5, f32[256,256]{1,0:T(8,128)S(1)} %get-tuple-element.170.cur.prev.before.state, f32[256,256]{1,0:T(8,128)S(1)} %get-tuple-element.151.cur.prev.before, ...), custom_call_target="tpu_custom_call" | custom-call | flops 1000 | bytes 4321000 | tf_op jit(solution)/shard_map/forward_inner/pallas_call | solution.py:608
  32.2 1.4 %collective-permute-done.11.ym = f32[32,256]{1,0:T(8,128)S(1)} collective-permute-done((f32[32,256]{1,0:T(8,128)S(1)}, f32[32,256]{1,0:T(8,128)S(1)}, u32[]{:S(2)}, u32[]{:S(2)}) %collective-permute-start.11) | collective-permute-done | bytes 32800 | tf_op jit(solution)/shard_map/ppermute | solution.py:67
  36.0 1.3 %forward_inner.8 = (f32[256,256]{1,0:T(8,128)S(1)}, f32[256,256]{1,0:T(8,128)S(1)}) custom-call(s32[16]{0:T(128)S(1)} %copy-done.10, f32[8,16]{1,0:T(8,128)S(1)} %copy-done.5, f32[256,256]{1,0:T(8,128)S(1)} %get-tuple-element.184.cur.prev.before.state, f32[256,256]{1,0:T(8,128)S(1)} %get-tuple-element.170.cur.prev.before.state, ...), custom_call_target="tpu_custom_call" | custom-call | flops 1000 | bytes 4321000 | tf_op jit(solution)/shard_map/forward_inner/pallas_call | solution.py:608
  37.4 1.8 %collective-permute-done.14.ym = f32[72,256]{1,0:T(8,128)S(1)} collective-permute-done((f32[72,256]{1,0:T(8,128)S(1)}, f32[72,256]{1,0:T(8,128)S(1)}, u32[]{:S(2)}, u32[]{:S(2)}) %collective-permute-start.14) | collective-permute-done | bytes 73760 | tf_op jit(solution)/shard_map/ppermute | solution.py:67
  40.9 1.0 collective-permute-start.16
  42.0 1.3 %forward_inner.9 = (f32[256,256]{1,0:T(8,128)S(1)}, f32[256,256]{1,0:T(8,128)S(1)}) custom-call(s32[16]{0:T(128)S(1)} %copy-done.10, f32[8,16]{1,0:T(8,128)S(1)} %copy-done.5, f32[256,256]{1,0:T(8,128)S(1)} %get-tuple-element.191.cur.prev.before.state, f32[256,256]{1,0:T(8,128)S(1)} %get-tuple-element.184.cur.prev.before.state, ...), custom_call_target="tpu_custom_call" | custom-call | flops 1000 | bytes 4321000 | tf_op jit(solution)/shard_map/forward_inner/pallas_call | solution.py:608
  43.4 1.9 %collective-permute-done.17.ym.u_ym = f32[2,32,256]{2,1,0:T(8,128)S(1)} collective-permute-done((f32[2,32,256]{2,1,0:T(8,128)S(1)}, f32[2,32,256]{2,1,0:T(8,128)S(1)}, u32[]{:S(2)}, u32[]{:S(2)}) %collective-permute-start.17) | collective-permute-done | bytes 65568 | tf_op jit(solution)/shard_map/ppermute | solution.py:67
  45.3 1.6 %collective-permute-done.16.zm.u_zm = f32[2,128,256]{2,1,0:T(8,128)S(1)} collective-permute-done((f32[2,128,256]{2,1,0:T(8,128)S(1)}, f32[2,128,256]{2,1,0:T(8,128)S(1)}, u32[]{:S(2)}, u32[]{:S(2)}) %collective-permute-start.16) | collective-permute-done | bytes 262176 | tf_op jit(solution)/shard_map/ppermute | solution.py:67
  48.6 1.4 %forward_inner.10 = (f32[256,256]{1,0:T(8,128)S(1)}, f32[256,256]{1,0:T(8,128)S(1)}) custom-call(s32[16]{0:T(128)S(1)} %copy-done.10, f32[8,16]{1,0:T(8,128)S(1)} %copy-done.5, f32[256,256]{1,0:T(8,128)S(1)} %get-tuple-element.196.cur.prev.before.state, f32[256,256]{1,0:T(8,128)S(1)} %get-tuple-element.191.cur.prev.before.state, ...), custom_call_target="tpu_custom_call" | custom-call | flops 1000 | bytes 4321000 | tf_op jit(solution)/shard_map/forward_inner/pallas_call | solution.py:608
  50.0 1.5 %collective-permute-done.20.ym = f32[32,256]{1,0:T(8,128)S(1)} collective-permute-done((f32[32,256]{1,0:T(8,128)S(1)}, f32[32,256]{1,0:T(8,128)S(1)}, u32[]{:S(2)}, u32[]{:S(2)}) %collective-permute-start.20) | collective-permute-done | bytes 32800 | tf_op jit(solution)/shard_map/ppermute | solution.py:67
  54.2 1.4 %forward_inner.11 = (f32[256,256]{1,0:T(8,128)S(1)}, f32[256,256]{1,0:T(8,128)S(1)}) custom-call(s32[16]{0:T(128)S(1)} %copy-done.10, f32[8,16]{1,0:T(8,128)S(1)} %copy-done.5, f32[256,256]{1,0:T(8,128)S(1)} %get-tuple-element.201.cur.prev.before.state, f32[256,256]{1,0:T(8,128)S(1)} %get-tuple-element.196.cur.prev.before.state, ...), custom_call_target="tpu_custom_call" | custom-call | flops 1000 | bytes 4321000 | tf_op jit(solution)/shard_map/forward_inner/pallas_call | solution.py:608
  55.6 1.1 collective-permute-done.23.ym
  56.7 1.2 collective-permute-done.22.zm
  59.6 1.4 %forward_inner.12 = (f32[256,256]{1,0:T(8,128)S(1)}, f32[256,256]{1,0:T(8,128)S(1)}) custom-call(s32[16]{0:T(128)S(1)} %copy-done.10, f32[8,16]{1,0:T(8,128)S(1)} %copy-done.5, f32[256,256]{1,0:T(8,128)S(1)} %get-tuple-element.208.cur.prev.rest_2_.state, f32[256,256]{1,0:T(8,128)S(1)} %get-tuple-element.201.cur.prev.before.state, ...), custom_call_target="tpu_custom_call" | custom-call | flops 1000 | bytes 4321000 | tf_op jit(solution)/shard_map/forward_inner/pallas_call | solution.py:608
  60.9 1.4 %collective-permute-done.26.ym = f32[32,256]{1,0:T(8,128)S(1)} collective-permute-done((f32[32,256]{1,0:T(8,128)S(1)}, f32[32,256]{1,0:T(8,128)S(1)}, u32[]{:S(2)}, u32[]{:S(2)}) %collective-permute-start.26) | collective-permute-done | bytes 32800 | tf_op jit(solution)/shard_map/ppermute | solution.py:67
  64.9 1.4 %forward_inner.13 = (f32[256,256]{1,0:T(8,128)S(1)}, f32[256,256]{1,0:T(8,128)S(1)}) custom-call(s32[16]{0:T(128)S(1)} %copy-done.10, f32[8,16]{1,0:T(8,128)S(1)} %copy-done.5, f32[256,256]{1,0:T(8,128)S(1)} %get-tuple-element.217.cur.state.rest_1_, f32[256,256]{1,0:T(8,128)S(1)} %get-tuple-element.208.cur.prev.rest_2_.state, ...), custom_call_target="tpu_custom_call" | custom-call | flops 1000 | bytes 4321000 | tf_op jit(solution)/shard_map/forward_inner/pallas_call | solution.py:608
  66.3 1.4 %collective-permute-done.29.ym = f32[32,256]{1,0:T(8,128)S(1)} collective-permute-done((f32[32,256]{1,0:T(8,128)S(1)}, f32[32,256]{1,0:T(8,128)S(1)}, u32[]{:S(2)}, u32[]{:S(2)}) %collective-permute-start.29) | collective-permute-done | bytes 32800 | tf_op jit(solution)/shard_map/ppermute | solution.py:67
  70.9 1.0 adjoint_inner.7
  71.9 1.8 %collective-permute-done.32.ym = f32[32,256]{1,0:T(8,128)S(1)} collective-permute-done((f32[32,256]{1,0:T(8,128)S(1)}, f32[32,256]{1,0:T(8,128)S(1)}, u32[]{:S(2)}, u32[]{:S(2)}) %collective-permute-start.32) | collective-permute-done | bytes 32800 | tf_op jit(solution)/shard_map/ppermute | solution.py:67
  76.3 1.0 adjoint_inner.8
  77.3 1.8 %collective-permute-done.35.ym = f32[32,256]{1,0:T(8,128)S(1)} collective-permute-done((f32[32,256]{1,0:T(8,128)S(1)}, f32[32,256]{1,0:T(8,128)S(1)}, u32[]{:S(2)}, u32[]{:S(2)}) %collective-permute-start.35) | collective-permute-done | bytes 32800 | tf_op jit(solution)/shard_map/ppermute | solution.py:67
  82.7 1.8 %collective-permute-done.38.ym = f32[32,256]{1,0:T(8,128)S(1)} collective-permute-done((f32[32,256]{1,0:T(8,128)S(1)}, f32[32,256]{1,0:T(8,128)S(1)}, u32[]{:S(2)}, u32[]{:S(2)}) %collective-permute-start.38) | collective-permute-done | bytes 32800 | tf_op jit(solution)/shard_map/ppermute | solution.py:67
  87.1 1.0 adjoint_inner.10
  88.0 1.8 %collective-permute-done.41.ym = f32[32,256]{1,0:T(8,128)S(1)} collective-permute-done((f32[32,256]{1,0:T(8,128)S(1)}, f32[32,256]{1,0:T(8,128)S(1)}, u32[]{:S(2)}, u32[]{:S(2)}) %collective-permute-start.41) | collective-permute-done | bytes 32800 | tf_op jit(solution)/shard_map/ppermute | solution.py:67
  93.6 1.8 %collective-permute-done.44.ym = f32[32,256]{1,0:T(8,128)S(1)} collective-permute-done((f32[32,256]{1,0:T(8,128)S(1)}, f32[32,256]{1,0:T(8,128)S(1)}, u32[]{:S(2)}, u32[]{:S(2)}) %collective-permute-start.44) | collective-permute-done | bytes 32800 | tf_op jit(solution)/shard_map/ppermute | solution.py:67
  98.0 1.0 adjoint_inner.12
  99.0 1.8 %collective-permute-done.47.ym = f32[32,256]{1,0:T(8,128)S(1)} collective-permute-done((f32[32,256]{1,0:T(8,128)S(1)}, f32[32,256]{1,0:T(8,128)S(1)}, u32[]{:S(2)}, u32[]{:S(2)}) %collective-permute-start.47) | collective-permute-done | bytes 32800 | tf_op jit(solution)/shard_map/ppermute | solution.py:67
  103.4 1.0 adjoint_inner.13
  104.4 1.8 %collective-permute-done.50.ym = f32[32,256]{1,0:T(8,128)S(1)} collective-permute-done((f32[32,256]{1,0:T(8,128)S(1)}, f32[32,256]{1,0:T(8,128)S(1)}, u32[]{:S(2)}, u32[]{:S(2)}) %collective-permute-start.50) | collective-permute-done | bytes 32800 | tf_op jit(solution)/shard_map/ppermute | solution.py:67
  108.0 1.2 collective-permute-start.51
  109.1 1.0 collective-permute-done.51.got
  110.1 1.4 %collective-permute-start.52 = (f32[2,64,128]{2,1,0:T(8,128)S(1)}, f32[2,64,128]{2,1,0:T(8,128)S(1)}, u32[]{:S(2)}, u32[]{:S(2)}) collective-permute-start(f32[2,64,128]{2,1,0:T(8,128)S(1)} %get-tuple-element.277), channel_id=1, source_target_pairs={{0,12},{1,14},{2,13},{3,15},{4,8},{5,10},{6,9},{7,11},{8,4},{9,6},... | collective-permute-start | bytes 196616 | tf_op jit(solution)/shard_map/ppermute | solution.py:67
  111.5 1.8 %collective-permute-start.54 = (f32[2,64,128]{2,1,0:T(8,128)S(1)}, f32[2,64,128]{2,1,0:T(8,128)S(1)}, u32[]{:S(2)}, u32[]{:S(2)}) collective-permute-start(f32[2,64,128]{2,1,0:T(8,128)S(1)} %get-tuple-element.281), channel_id=1, source_target_pairs={{0,8},{1,10},{2,9},{3,11},{4,12},{5,14},{6,13},{7,15},{8,0},{9,2},... | collective-permute-start | bytes 196616 | tf_op jit(solution)/shard_map/ppermute | solution.py:67
  113.2 2.0 %collective-permute-start.55 = (f32[2,64,128]{2,1,0:T(8,128)S(1)}, f32[2,64,128]{2,1,0:T(8,128)S(1)}, u32[]{:S(2)}, u32[]{:S(2)}) collective-permute-start(f32[2,64,128]{2,1,0:T(8,128)S(1)} %get-tuple-element.282), channel_id=1, source_target_pairs={{0,4},{1,6},{2,5},{3,7},{4,0},{5,2},{6,1},{7,3},{8,12},{9,14},{10,... | collective-permute-start | bytes 196616 | tf_op jit(solution)/shard_map/ppermute | solution.py:67
  115.3 3.0 %collective-permute-start.56 = (f32[2,64,128]{2,1,0:T(8,128)S(1)}, f32[2,64,128]{2,1,0:T(8,128)S(1)}, u32[]{:S(2)}, u32[]{:S(2)}) collective-permute-start(f32[2,64,128]{2,1,0:T(8,128)S(1)} %get-tuple-element.283), channel_id=1, source_target_pairs={{0,0},{1,2},{2,1},{3,3},{4,4},{5,6},{6,5},{7,7},{8,8},{9,10},{10,9... | collective-permute-start | bytes 196616 | tf_op jit(solution)/shard_map/ppermute | solution.py:67
  119.4 1.5 %collective-permute-done.56.refs_3_ = f32[2,64,128]{2,1,0:T(8,128)S(1)} collective-permute-done((f32[2,64,128]{2,1,0:T(8,128)S(1)}, f32[2,64,128]{2,1,0:T(8,128)S(1)}, u32[]{:S(2)}, u32[]{:S(2)}) %collective-permute-start.56) | collective-permute-done | bytes 65568 | tf_op jit(solution)/shard_map/ppermute | solution.py:67
  120.9 1.3 %filter.1 = f32[32,32,64]{2,1,0:T(8,128)} custom-call(f32[2,64,128]{2,1,0:T(8,128)S(1)} %collective-permute-done.52.refs_0_, f32[2,64,128]{2,1,0:T(8,128)S(1)} %collective-permute-done.54.refs_1_, f32[2,64,128]{2,1,0:T(8,128)S(1)} %collective-permute-done.55.refs_2_, f32[2,64,128]{2,1,0:T(8,128)S(1)} %collective-permute-done.56.refs_3_), custom_call_target="tpu_custom_call" | custom-call | flops 1000 | bytes 1000 | tf_op jit(solution)/shard_map/filter/pallas_call | solution.py:608
  (153 shorter events, 46.2 us)
Async XLA Ops:
  0.6 9.4 %collective-permute-start = (f32[256,256]{1,0:T(8,128)}, f32[256,256]{1,0:T(8,128)S(1)}, u32[]{:S(2)}, u32[]{:S(2)}) collective-permute-start(f32[256,256]{1,0:T(8,128)} %bitcast.18), channel_id=1, source_target_pairs={{0,16},{1,2},{2,1},{3,19},{4,20},{5,6},{6,5},{7,23},{8,24},{9,10},... | collective-permute-start | bytes 786440 | tf_op jit(solution)/shard_map/ppermute | solution.py:67
  3.3 7.3 %collective-permute-start.2 = (f32[256,256]{1,0:T(8,128)}, f32[256,256]{1,0:T(8,128)S(1)}, u32[]{:S(2)}, u32[]{:S(2)}) collective-permute-start(f32[256,256]{1,0:T(8,128)} %bitcast.20), channel_id=1, source_target_pairs={{0,16},{1,2},{2,1},{3,19},{4,20},{5,6},{6,5},{7,23},{8,24},{9,10},... | collective-permute-start | bytes 786440 | tf_op jit(solution)/shard_map/ppermute | solution.py:67
  5.6 4.4 %collective-permute-start.1 = (f32[8,8,128]{2,1,0:T(8,128)S(1)}, f32[8,8,128]{2,1,0:T(8,128)S(1)}, u32[]{:S(2)}, u32[]{:S(2)}) collective-permute-start(f32[8,8,128]{2,1,0:T(8,128)S(1)} %get-tuple-element.148), channel_id=1, source_target_pairs={{0,4},{1,5},{2,6},{3,7},{4,0},{5,1},{6,2},{7,3},{8,12},{9,13},{10,... | collective-permute-start | bytes 98312 | tf_op jit(solution)/shard_map/ppermute | solution.py:67
  6.9 16.5 %collective-permute-start.3 = (f32[2,256,256]{2,1,0:T(8,128)}, f32[2,256,256]{2,1,0:T(8,128)S(1)}, u32[]{:S(2)}, u32[]{:S(2)}) collective-permute-start(f32[2,256,256]{2,1,0:T(8,128)} %pad_maximum_fusion), channel_id=1, source_target_pairs={{0,16},{1,2},{2,1},{3,19},{4,20},{5,6},{6,5},{7,23},{8,24},{9,10},... | collective-permute-start | bytes 1572872 | tf_op jit(solution)/shard_map/ppermute | solution.py:67
  13.9 3.2 %collective-permute-start.4 = (f32[2,128,256]{2,1,0:T(8,128)}, f32[2,128,256]{2,1,0:T(8,128)S(1)}, u32[]{:S(2)}, u32[]{:S(2)}) collective-permute-start(f32[2,128,256]{2,1,0:T(8,128)} %get-tuple-element.155), channel_id=1, source_target_pairs={{0,1},{1,0},{2,3},{3,2},{4,5},{5,4},{6,7},{7,6},{8,9},{9,8},{10,11... | collective-permute-start | bytes 786440 | tf_op jit(solution)/shard_map/ppermute | solution.py:67
  15.3 11.1 %collective-permute-start.5 = (f32[2,128,256]{2,1,0:T(8,128)}, f32[2,128,256]{2,1,0:T(8,128)S(1)}, u32[]{:S(2)}, u32[]{:S(2)}) collective-permute-start(f32[2,128,256]{2,1,0:T(8,128)} %copy-done.14), channel_id=1, source_target_pairs={{0,16},{1,4},{2,18},{3,6},{4,1},{5,8},{6,3},{7,10},{8,5},{9,12},{1... | collective-permute-start | bytes 786440 | tf_op jit(solution)/shard_map/ppermute | solution.py:67
  17.9 14.0 %collective-permute-start.9 = (f32[2,256,256]{2,1,0:T(8,128)S(1)}, f32[2,256,256]{2,1,0:T(8,128)S(1)}, u32[]{:S(2)}, u32[]{:S(2)}) collective-permute-start(f32[2,256,256]{2,1,0:T(8,128)S(1)} %gather.1), channel_id=1, source_target_pairs={{0,16},{1,2},{2,1},{3,19},{4,20},{5,6},{6,5},{7,23},{8,24},{9,10},... | collective-permute-start | bytes 1572872 | tf_op jit(solution)/shard_map/ppermute | solution.py:67
  18.9 4.5 %collective-permute-start.7 = (f32[8,8,128]{2,1,0:T(8,128)S(1)}, f32[8,8,128]{2,1,0:T(8,128)S(1)}, u32[]{:S(2)}, u32[]{:S(2)}) collective-permute-start(f32[8,8,128]{2,1,0:T(8,128)S(1)} %get-tuple-element.167), channel_id=1, source_target_pairs={{0,8},{1,9},{2,10},{3,11},{4,12},{5,13},{6,14},{7,15},{8,0},{9,1},... | collective-permute-start | bytes 98312 | tf_op jit(solution)/shard_map/ppermute | solution.py:67
  20.5 5.9 %collective-permute-start.6 = (f32[2,32,256]{2,1,0:T(8,128)S(1)}, f32[2,32,256]{2,1,0:T(8,128)S(1)}, u32[]{:S(2)}, u32[]{:S(2)}) collective-permute-start(f32[2,32,256]{2,1,0:T(8,128)S(1)} %get-tuple-element.165), channel_id=1, source_target_pairs={{0,2},{1,3},{2,0},{3,1},{4,6},{5,7},{6,4},{7,5},{8,10},{9,11},{10,... | collective-permute-start | bytes 196616 | tf_op jit(solution)/shard_map/ppermute | solution.py:67
  26.9 3.6 %collective-permute-start.8 = (f32[168,256]{1,0:T(8,128)S(1)}, f32[168,256]{1,0:T(8,128)S(1)}, u32[]{:S(2)}, u32[]{:S(2)}) collective-permute-start(f32[168,256]{1,0:T(8,128)S(1)} %get-tuple-element.175), channel_id=1, source_target_pairs={{0,1},{1,0},{2,3},{3,2},{4,5},{5,4},{6,7},{7,6},{8,9},{9,8},{10,11... | collective-permute-start | bytes 516104 | tf_op jit(solution)/shard_map/ppermute | solution.py:67
  29.3 4.7 %collective-permute-start.10 = (f32[128,256]{1,0:T(8,128)S(1)}, f32[128,256]{1,0:T(8,128)S(1)}, u32[]{:S(2)}, u32[]{:S(2)}) collective-permute-start(f32[128,256]{1,0:T(8,128)S(1)} %get-tuple-element.181), channel_id=1, source_target_pairs={{0,16},{1,4},{2,18},{3,6},{4,1},{5,8},{6,3},{7,10},{8,5},{9,12},{1... | collective-permute-start | bytes 393224 | tf_op jit(solution)/shard_map/ppermute | solution.py:67
  30.5 3.1 %collective-permute-start.11 = (f32[32,256]{1,0:T(8,128)S(1)}, f32[32,256]{1,0:T(8,128)S(1)}, u32[]{:S(2)}, u32[]{:S(2)}) collective-permute-start(f32[32,256]{1,0:T(8,128)S(1)} %get-tuple-element.182), channel_id=1, source_target_pairs={{0,2},{1,3},{2,0},{3,1},{4,6},{5,7},{6,4},{7,5},{8,10},{9,11},{10,... | collective-permute-start | bytes 98312 | tf_op jit(solution)/shard_map/ppermute | solution.py:67
  34.2 1.9 %collective-permute-start.12 = (f32[128,256]{1,0:T(8,128)S(1)}, f32[128,256]{1,0:T(8,128)S(1)}, u32[]{:S(2)}, u32[]{:S(2)}) collective-permute-start(f32[128,256]{1,0:T(8,128)S(1)} %get-tuple-element.185), channel_id=1, source_target_pairs={{0,1},{1,0},{2,3},{3,2},{4,5},{5,4},{6,7},{7,6},{8,9},{9,8},{10,11... | collective-permute-start | bytes 393224 | tf_op jit(solution)/shard_map/ppermute | solution.py:67
  35.1 4.7 %collective-permute-start.13 = (f32[128,256]{1,0:T(8,128)S(1)}, f32[128,256]{1,0:T(8,128)S(1)}, u32[]{:S(2)}, u32[]{:S(2)}) collective-permute-start(f32[128,256]{1,0:T(8,128)S(1)} %get-tuple-element.187), channel_id=1, source_target_pairs={{0,16},{1,4},{2,18},{3,6},{4,1},{5,8},{6,3},{7,10},{8,5},{9,12},{1... | collective-permute-start | bytes 393224 | tf_op jit(solution)/shard_map/ppermute | solution.py:67
  35.7 3.5 %collective-permute-start.14 = (f32[72,256]{1,0:T(8,128)S(1)}, f32[72,256]{1,0:T(8,128)S(1)}, u32[]{:S(2)}, u32[]{:S(2)}) collective-permute-start(f32[72,256]{1,0:T(8,128)S(1)} %get-tuple-element.188), channel_id=1, source_target_pairs={{0,2},{1,3},{2,0},{3,1},{4,6},{5,7},{6,4},{7,5},{8,10},{9,11},{10,... | collective-permute-start | bytes 221192 | tf_op jit(solution)/shard_map/ppermute | solution.py:67
  40.0 2.1 %collective-permute-start.15 = (f32[2,128,256]{2,1,0:T(8,128)S(1)}, f32[2,128,256]{2,1,0:T(8,128)S(1)}, u32[]{:S(2)}, u32[]{:S(2)}) collective-permute-start(f32[2,128,256]{2,1,0:T(8,128)S(1)} %get-tuple-element.192), channel_id=1, source_target_pairs={{0,1},{1,0},{2,3},{3,2},{4,5},{5,4},{6,7},{7,6},{8,9},{9,8},{10,11... | collective-permute-start | bytes 786440 | tf_op jit(solution)/shard_map/ppermute | solution.py:67
  40.9 6.1 %collective-permute-start.16 = (f32[2,128,256]{2,1,0:T(8,128)S(1)}, f32[2,128,256]{2,1,0:T(8,128)S(1)}, u32[]{:S(2)}, u32[]{:S(2)}) collective-permute-start(f32[2,128,256]{2,1,0:T(8,128)S(1)} %get-tuple-element.194), channel_id=1, source_target_pairs={{0,16},{1,4},{2,18},{3,6},{4,1},{5,8},{6,3},{7,10},{8,5},{9,12},{1... | collective-permute-start | bytes 786440 | tf_op jit(solution)/shard_map/ppermute | solution.py:67
  41.9 3.4 %collective-permute-start.17 = (f32[2,32,256]{2,1,0:T(8,128)S(1)}, f32[2,32,256]{2,1,0:T(8,128)S(1)}, u32[]{:S(2)}, u32[]{:S(2)}) collective-permute-start(f32[2,32,256]{2,1,0:T(8,128)S(1)} %get-tuple-element.195), channel_id=1, source_target_pairs={{0,2},{1,3},{2,0},{3,1},{4,6},{5,7},{6,4},{7,5},{8,10},{9,11},{10,... | collective-permute-start | bytes 196616 | tf_op jit(solution)/shard_map/ppermute | solution.py:67
  47.6 4.7 %collective-permute-start.19 = (f32[128,256]{1,0:T(8,128)S(1)}, f32[128,256]{1,0:T(8,128)S(1)}, u32[]{:S(2)}, u32[]{:S(2)}) collective-permute-start(f32[128,256]{1,0:T(8,128)S(1)} %get-tuple-element.199), channel_id=1, source_target_pairs={{0,16},{1,4},{2,18},{3,6},{4,1},{5,8},{6,3},{7,10},{8,5},{9,12},{1... | collective-permute-start | bytes 393224 | tf_op jit(solution)/shard_map/ppermute | solution.py:67
  48.4 3.1 %collective-permute-start.20 = (f32[32,256]{1,0:T(8,128)S(1)}, f32[32,256]{1,0:T(8,128)S(1)}, u32[]{:S(2)}, u32[]{:S(2)}) collective-permute-start(f32[32,256]{1,0:T(8,128)S(1)} %get-tuple-element.200), channel_id=1, source_target_pairs={{0,2},{1,3},{2,0},{3,1},{4,6},{5,7},{6,4},{7,5},{8,10},{9,11},{10,... | collective-permute-start | bytes 98312 | tf_op jit(solution)/shard_map/ppermute | solution.py:67
  52.5 1.7 %collective-permute-start.21 = (f32[128,256]{1,0:T(8,128)S(1)}, f32[128,256]{1,0:T(8,128)S(1)}, u32[]{:S(2)}, u32[]{:S(2)}) collective-permute-start(f32[128,256]{1,0:T(8,128)S(1)} %get-tuple-element.202), channel_id=1, source_target_pairs={{0,1},{1,0},{2,3},{3,2},{4,5},{5,4},{6,7},{7,6},{8,9},{9,8},{10,11... | collective-permute-start | bytes 393224 | tf_op jit(solution)/shard_map/ppermute | solution.py:67
  53.2 4.7 %collective-permute-start.22 = (f32[128,256]{1,0:T(8,128)S(1)}, f32[128,256]{1,0:T(8,128)S(1)}, u32[]{:S(2)}, u32[]{:S(2)}) collective-permute-start(f32[128,256]{1,0:T(8,128)S(1)} %get-tuple-element.206), channel_id=1, source_target_pairs={{0,16},{1,4},{2,18},{3,6},{4,1},{5,8},{6,3},{7,10},{8,5},{9,12},{1... | collective-permute-start | bytes 393224 | tf_op jit(solution)/shard_map/ppermute | solution.py:67
  53.7 3.1 %collective-permute-start.23 = (f32[32,256]{1,0:T(8,128)S(1)}, f32[32,256]{1,0:T(8,128)S(1)}, u32[]{:S(2)}, u32[]{:S(2)}) collective-permute-start(f32[32,256]{1,0:T(8,128)S(1)} %get-tuple-element.207), channel_id=1, source_target_pairs={{0,2},{1,3},{2,0},{3,1},{4,6},{5,7},{6,4},{7,5},{8,10},{9,11},{10,... | collective-permute-start | bytes 98312 | tf_op jit(solution)/shard_map/ppermute | solution.py:67
  58.6 4.7 %collective-permute-start.25 = (f32[128,256]{1,0:T(8,128)S(1)}, f32[128,256]{1,0:T(8,128)S(1)}, u32[]{:S(2)}, u32[]{:S(2)}) collective-permute-start(f32[128,256]{1,0:T(8,128)S(1)} %get-tuple-element.215), channel_id=1, source_target_pairs={{0,16},{1,4},{2,18},{3,6},{4,1},{5,8},{6,3},{7,10},{8,5},{9,12},{1... | collective-permute-start | bytes 393224 | tf_op jit(solution)/shard_map/ppermute | solution.py:67
  59.2 3.1 %collective-permute-start.26 = (f32[32,256]{1,0:T(8,128)S(1)}, f32[32,256]{1,0:T(8,128)S(1)}, u32[]{:S(2)}, u32[]{:S(2)}) collective-permute-start(f32[32,256]{1,0:T(8,128)S(1)} %get-tuple-element.216), channel_id=1, source_target_pairs={{0,2},{1,3},{2,0},{3,1},{4,6},{5,7},{6,4},{7,5},{8,10},{9,11},{10,... | collective-permute-start | bytes 98312 | tf_op jit(solution)/shard_map/ppermute | solution.py:67
  63.9 4.7 %collective-permute-start.28 = (f32[128,256]{1,0:T(8,128)S(1)}, f32[128,256]{1,0:T(8,128)S(1)}, u32[]{:S(2)}, u32[]{:S(2)}) collective-permute-start(f32[128,256]{1,0:T(8,128)S(1)} %get-tuple-element.220), channel_id=1, source_target_pairs={{0,16},{1,4},{2,18},{3,6},{4,1},{5,8},{6,3},{7,10},{8,5},{9,12},{1... | collective-permute-start | bytes 393224 | tf_op jit(solution)/shard_map/ppermute | solution.py:67
  64.6 3.1 %collective-permute-start.29 = (f32[32,256]{1,0:T(8,128)S(1)}, f32[32,256]{1,0:T(8,128)S(1)}, u32[]{:S(2)}, u32[]{:S(2)}) collective-permute-start(f32[32,256]{1,0:T(8,128)S(1)} %get-tuple-element.221), channel_id=1, source_target_pairs={{0,2},{1,3},{2,0},{3,1},{4,6},{5,7},{6,4},{7,5},{8,10},{9,11},{10,... | collective-permute-start | bytes 98312 | tf_op jit(solution)/shard_map/ppermute | solution.py:67
  70.0 4.7 %collective-permute-start.31 = (f32[128,256]{1,0:T(8,128)S(1)}, f32[128,256]{1,0:T(8,128)S(1)}, u32[]{:S(2)}, u32[]{:S(2)}) collective-permute-start(f32[128,256]{1,0:T(8,128)S(1)} %get-tuple-element.229), channel_id=1, source_target_pairs={{0,16},{1,4},{2,18},{3,6},{4,1},{5,8},{6,3},{7,10},{8,5},{9,12},{1... | collective-permute-start | bytes 393224 | tf_op jit(solution)/shard_map/ppermute | solution.py:67
  70.6 3.1 %collective-permute-start.32 = (f32[32,256]{1,0:T(8,128)S(1)}, f32[32,256]{1,0:T(8,128)S(1)}, u32[]{:S(2)}, u32[]{:S(2)}) collective-permute-start(f32[32,256]{1,0:T(8,128)S(1)} %get-tuple-element.230), channel_id=1, source_target_pairs={{0,2},{1,3},{2,0},{3,1},{4,6},{5,7},{6,4},{7,5},{8,10},{9,11},{10,... | collective-permute-start | bytes 98312 | tf_op jit(solution)/shard_map/ppermute | solution.py:67
  75.3 4.7 %collective-permute-start.34 = (f32[128,256]{1,0:T(8,128)S(1)}, f32[128,256]{1,0:T(8,128)S(1)}, u32[]{:S(2)}, u32[]{:S(2)}) collective-permute-start(f32[128,256]{1,0:T(8,128)S(1)} %get-tuple-element.236), channel_id=1, source_target_pairs={{0,16},{1,4},{2,18},{3,6},{4,1},{5,8},{6,3},{7,10},{8,5},{9,12},{1... | collective-permute-start | bytes 393224 | tf_op jit(solution)/shard_map/ppermute | solution.py:67
  76.0 3.1 %collective-permute-start.35 = (f32[32,256]{1,0:T(8,128)S(1)}, f32[32,256]{1,0:T(8,128)S(1)}, u32[]{:S(2)}, u32[]{:S(2)}) collective-permute-start(f32[32,256]{1,0:T(8,128)S(1)} %get-tuple-element.237), channel_id=1, source_target_pairs={{0,2},{1,3},{2,0},{3,1},{4,6},{5,7},{6,4},{7,5},{8,10},{9,11},{10,... | collective-permute-start | bytes 98312 | tf_op jit(solution)/shard_map/ppermute | solution.py:67
  80.7 4.7 %collective-permute-start.37 = (f32[128,256]{1,0:T(8,128)S(1)}, f32[128,256]{1,0:T(8,128)S(1)}, u32[]{:S(2)}, u32[]{:S(2)}) collective-permute-start(f32[128,256]{1,0:T(8,128)S(1)} %get-tuple-element.243), channel_id=1, source_target_pairs={{0,16},{1,4},{2,18},{3,6},{4,1},{5,8},{6,3},{7,10},{8,5},{9,12},{1... | collective-permute-start | bytes 393224 | tf_op jit(solution)/shard_map/ppermute | solution.py:67
  81.4 3.1 %collective-permute-start.38 = (f32[32,256]{1,0:T(8,128)S(1)}, f32[32,256]{1,0:T(8,128)S(1)}, u32[]{:S(2)}, u32[]{:S(2)}) collective-permute-start(f32[32,256]{1,0:T(8,128)S(1)} %get-tuple-element.244), channel_id=1, source_target_pairs={{0,2},{1,3},{2,0},{3,1},{4,6},{5,7},{6,4},{7,5},{8,10},{9,11},{10,... | collective-permute-start | bytes 98312 | tf_op jit(solution)/shard_map/ppermute | solution.py:67
  85.6 1.5 %collective-permute-start.39 = (f32[128,256]{1,0:T(8,128)S(1)}, f32[128,256]{1,0:T(8,128)S(1)}, u32[]{:S(2)}, u32[]{:S(2)}) collective-permute-start(f32[128,256]{1,0:T(8,128)S(1)} %get-tuple-element.246), channel_id=1, source_target_pairs={{0,1},{1,0},{2,3},{3,2},{4,5},{5,4},{6,7},{7,6},{8,9},{9,8},{10,11... | collective-permute-start | bytes 393224 | tf_op jit(solution)/shard_map/ppermute | solution.py:67
  86.1 4.7 %collective-permute-start.40 = (f32[128,256]{1,0:T(8,128)S(1)}, f32[128,256]{1,0:T(8,128)S(1)}, u32[]{:S(2)}, u32[]{:S(2)}) collective-permute-start(f32[128,256]{1,0:T(8,128)S(1)} %get-tuple-element.250), channel_id=1, source_target_pairs={{0,16},{1,4},{2,18},{3,6},{4,1},{5,8},{6,3},{7,10},{8,5},{9,12},{1... | collective-permute-start | bytes 393224 | tf_op jit(solution)/shard_map/ppermute | solution.py:67
  86.8 3.1 %collective-permute-start.41 = (f32[32,256]{1,0:T(8,128)S(1)}, f32[32,256]{1,0:T(8,128)S(1)}, u32[]{:S(2)}, u32[]{:S(2)}) collective-permute-start(f32[32,256]{1,0:T(8,128)S(1)} %get-tuple-element.251), channel_id=1, source_target_pairs={{0,2},{1,3},{2,0},{3,1},{4,6},{5,7},{6,4},{7,5},{8,10},{9,11},{10,... | collective-permute-start | bytes 98312 | tf_op jit(solution)/shard_map/ppermute | solution.py:67
  91.7 4.7 %collective-permute-start.43 = (f32[128,256]{1,0:T(8,128)S(1)}, f32[128,256]{1,0:T(8,128)S(1)}, u32[]{:S(2)}, u32[]{:S(2)}) collective-permute-start(f32[128,256]{1,0:T(8,128)S(1)} %get-tuple-element.257), channel_id=1, source_target_pairs={{0,16},{1,4},{2,18},{3,6},{4,1},{5,8},{6,3},{7,10},{8,5},{9,12},{1... | collective-permute-start | bytes 393224 | tf_op jit(solution)/shard_map/ppermute | solution.py:67
  92.3 3.1 %collective-permute-start.44 = (f32[32,256]{1,0:T(8,128)S(1)}, f32[32,256]{1,0:T(8,128)S(1)}, u32[]{:S(2)}, u32[]{:S(2)}) collective-permute-start(f32[32,256]{1,0:T(8,128)S(1)} %get-tuple-element.258), channel_id=1, source_target_pairs={{0,2},{1,3},{2,0},{3,1},{4,6},{5,7},{6,4},{7,5},{8,10},{9,11},{10,... | collective-permute-start | bytes 98312 | tf_op jit(solution)/shard_map/ppermute | solution.py:67
  97.0 4.7 %collective-permute-start.46 = (f32[128,256]{1,0:T(8,128)S(1)}, f32[128,256]{1,0:T(8,128)S(1)}, u32[]{:S(2)}, u32[]{:S(2)}) collective-permute-start(f32[128,256]{1,0:T(8,128)S(1)} %get-tuple-element.264), channel_id=1, source_target_pairs={{0,16},{1,4},{2,18},{3,6},{4,1},{5,8},{6,3},{7,10},{8,5},{9,12},{1... | collective-permute-start | bytes 393224 | tf_op jit(solution)/shard_map/ppermute | solution.py:67
  97.7 3.1 %collective-permute-start.47 = (f32[32,256]{1,0:T(8,128)S(1)}, f32[32,256]{1,0:T(8,128)S(1)}, u32[]{:S(2)}, u32[]{:S(2)}) collective-permute-start(f32[32,256]{1,0:T(8,128)S(1)} %get-tuple-element.265), channel_id=1, source_target_pairs={{0,2},{1,3},{2,0},{3,1},{4,6},{5,7},{6,4},{7,5},{8,10},{9,11},{10,... | collective-permute-start | bytes 98312 | tf_op jit(solution)/shard_map/ppermute | solution.py:67
  102.4 4.7 %collective-permute-start.49 = (f32[128,256]{1,0:T(8,128)S(1)}, f32[128,256]{1,0:T(8,128)S(1)}, u32[]{:S(2)}, u32[]{:S(2)}) collective-permute-start(f32[128,256]{1,0:T(8,128)S(1)} %get-tuple-element.271), channel_id=1, source_target_pairs={{0,16},{1,4},{2,18},{3,6},{4,1},{5,8},{6,3},{7,10},{8,5},{9,12},{1... | collective-permute-start | bytes 393224 | tf_op jit(solution)/shard_map/ppermute | solution.py:67
  103.1 3.1 %collective-permute-start.50 = (f32[32,256]{1,0:T(8,128)S(1)}, f32[32,256]{1,0:T(8,128)S(1)}, u32[]{:S(2)}, u32[]{:S(2)}) collective-permute-start(f32[32,256]{1,0:T(8,128)S(1)} %get-tuple-element.272), channel_id=1, source_target_pairs={{0,2},{1,3},{2,0},{3,1},{4,6},{5,7},{6,4},{7,5},{8,10},{9,11},{10,... | collective-permute-start | bytes 98312 | tf_op jit(solution)/shard_map/ppermute | solution.py:67
  107.6 10.7 %collective-permute-start.53 = (f32[2,256,256]{2,1,0:T(8,128)S(1)}, f32[2,256,256]{2,1,0:T(8,128)S(1)}, u32[]{:S(2)}, u32[]{:S(2)}) collective-permute-start(f32[2,256,256]{2,1,0:T(8,128)S(1)} %get-tuple-element.278.own), channel_id=1, source_target_pairs={{0,16},{1,2},{2,1},{3,19},{4,20},{5,6},{6,5},{7,23},{8,24},{9,10},... | collective-permute-start | bytes 1572872 | tf_op jit(solution)/shard_map/ppermute | solution.py:67
  108.0 2.1 %collective-permute-start.51 = (f32[4,64,128]{2,1,0:T(8,128)S(1)}, f32[4,64,128]{2,1,0:T(8,128)S(1)}, u32[]{:S(2)}, u32[]{:S(2)}) collective-permute-start(f32[4,64,128]{2,1,0:T(8,128)S(1)} %get-tuple-element.276), channel_id=1, source_target_pairs={{0,1},{1,0},{2,3},{3,2},{4,5},{5,4},{6,7},{7,6},{8,9},{9,8},{10,11... | collective-permute-start | bytes 393224 | tf_op jit(solution)/shard_map/ppermute | solution.py:67
  110.1 9.0 %collective-permute-start.52 = (f32[2,64,128]{2,1,0:T(8,128)S(1)}, f32[2,64,128]{2,1,0:T(8,128)S(1)}, u32[]{:S(2)}, u32[]{:S(2)}) collective-permute-start(f32[2,64,128]{2,1,0:T(8,128)S(1)} %get-tuple-element.277), channel_id=1, source_target_pairs={{0,12},{1,14},{2,13},{3,15},{4,8},{5,10},{6,9},{7,11},{8,4},{9,6},... | collective-permute-start | bytes 196616 | tf_op jit(solution)/shard_map/ppermute | solution.py:67
  111.5 7.9 %collective-permute-start.54 = (f32[2,64,128]{2,1,0:T(8,128)S(1)}, f32[2,64,128]{2,1,0:T(8,128)S(1)}, u32[]{:S(2)}, u32[]{:S(2)}) collective-permute-start(f32[2,64,128]{2,1,0:T(8,128)S(1)} %get-tuple-element.281), channel_id=1, source_target_pairs={{0,8},{1,10},{2,9},{3,11},{4,12},{5,14},{6,13},{7,15},{8,0},{9,2},... | collective-permute-start | bytes 196616 | tf_op jit(solution)/shard_map/ppermute | solution.py:67
  113.2 6.2 %collective-permute-start.55 = (f32[2,64,128]{2,1,0:T(8,128)S(1)}, f32[2,64,128]{2,1,0:T(8,128)S(1)}, u32[]{:S(2)}, u32[]{:S(2)}) collective-permute-start(f32[2,64,128]{2,1,0:T(8,128)S(1)} %get-tuple-element.282), channel_id=1, source_target_pairs={{0,4},{1,6},{2,5},{3,7},{4,0},{5,2},{6,1},{7,3},{8,12},{9,14},{10,... | collective-permute-start | bytes 196616 | tf_op jit(solution)/shard_map/ppermute | solution.py:67
  115.3 5.6 %collective-permute-start.56 = (f32[2,64,128]{2,1,0:T(8,128)S(1)}, f32[2,64,128]{2,1,0:T(8,128)S(1)}, u32[]{:S(2)}, u32[]{:S(2)}) collective-permute-start(f32[2,64,128]{2,1,0:T(8,128)S(1)} %get-tuple-element.283), channel_id=1, source_target_pairs={{0,0},{1,2},{2,1},{3,3},{4,4},{5,6},{6,5},{7,7},{8,8},{9,10},{10,9... | collective-permute-start | bytes 196616 | tf_op jit(solution)/shard_map/ppermute | solution.py:67
  (28 other events, 68.6 us)

commit v19 on v17

--- a/solution.py
+++ b/solution.py
@@ -663,7 +663,7 @@
     entries, half_entries = shaped(subs, steps, 128), shaped(subs // 2, steps, 128)
     order = [*range(2, len(stages)), 0]
     cells, lists, give = call(
-        functools.partial(pack_kernel, order[0]), "pack", [shaped(1, slots), entries, half_entries], after(rec_counts, stacked),
+        functools.partial(pack_kernel, order[0]), "pack", [shaped(1, slots), entries, half_entries], rec_counts,
         rec_cells, observed, weight=0.2, far=3,
         scratch=[pltpu.VMEM(rec_counts.shape, jnp.int32), pltpu.VMEM(rec_cells.shape, jnp.int32),
                  pltpu.VMEM(observed.shape, F32)])
@@ -671,7 +671,7 @@
         lists, give = call(
             functools.partial(trade_kernel, bit, order[n + 1]), "trade", [entries, half_entries],
             lists, send(give, stages[bit][0]), weight=0.1)
-        if n == 0:
+        if n == len(order) - 2:
             got[0], give = lax.optimization_barrier((got[0], give))
 
     density, p_now, *out = call(settle_kernel, "settle",

time: 116 us -> 119 us (1.026)
  starting transfers between devices: 41.2 us -> 47.4 us
  waiting for transfers between devices: 43.8 us -> 39.7 us
    ppermute x58, starting transfers between devices: 41.2 us -> 47.4 us  [send(): return lax.ppermute(value, ALL, pairs)]
    ppermute x58, waiting for transfers between devices: 43.8 us -> 39.7 us  [send(): return lax.ppermute(value, ALL, pairs)]
  transfers between devices with their start and end apart: 58 -> 58, of which waited for: 46 -> 38; matrix products, arithmetic and copies ran while one was open for 1% -> 1% of each run, Pallas kernels for 18% -> 18%
where the time goes in v19:
time: 119 us; the launch traced here: 118 us
  starting transfers between devices  47.4 us (40%)
  waiting for transfers between devices  39.7 us (33%)
  Pallas kernels  26.8 us (23%)
  local copies, waits for them, and re-layouts  2.19 us (2%)
  other arithmetic  1.24 us (1%)
  between operations  1.2 us (1%)
    ppermute x58, starting transfers between devices, send(): return lax.ppermute(value, ALL, pairs)  47.4 us
    ppermute x58, waiting for transfers between devices, send(): return lax.ppermute(value, ALL, pairs)  39.7 us
    pallas_call x42, Pallas kernels, call(): pl.pallas_call(functools.partial(kernel, Flags()), name=name, out_shape=o...  26.8 us
  transfers between devices with their start and end apart: 58, of which 38 were waited for; matrix products, arithmetic and copies ran while one was open for 1% of the time, Pallas kernels for 18%

profile of v19, /device:TPU:1, one launch (start us, length us, event | category | flops | bytes accessed | tf_op | source)
XLA Modules:
  0.0 118.4 jit_solution(14576428903264102448)
XLA Ops:
  2.8 2.2 %collective-permute-start.1 = (f32[8,8,128]{2,1,0:T(8,128)S(1)}, f32[8,8,128]{2,1,0:T(8,128)S(1)}, u32[]{:S(2)}, u32[]{:S(2)}) collective-permute-start(f32[8,8,128]{2,1,0:T(8,128)S(1)} %get-tuple-element.144), channel_id=1, source_target_pairs={{0,4},{1,5},{2,6},{3,7},{4,0},{5,1},{6,2},{7,3},{8,12},{9,13},{10,... | collective-permute-start | bytes 98312 | tf_op jit(solution)/shard_map/ppermute | solution.py:67
  5.0 2.1 %collective-permute-start.3 = (f32[256,256]{1,0:T(8,128)}, f32[256,256]{1,0:T(8,128)S(1)}, u32[]{:S(2)}, u32[]{:S(2)}) collective-permute-start(f32[256,256]{1,0:T(8,128)} %bitcast.16), channel_id=1, source_target_pairs={{0,16},{1,2},{2,1},{3,19},{4,20},{5,6},{6,5},{7,23},{8,24},{9,10},... | collective-permute-start | bytes 786440 | tf_op jit(solution)/shard_map/ppermute | solution.py:67
  7.1 1.1 pad_maximum_fusion
  8.2 1.8 %collective-permute-start.4 = (f32[2,256,256]{2,1,0:T(8,128)S(1)}, f32[2,256,256]{2,1,0:T(8,128)S(1)}, u32[]{:S(2)}, u32[]{:S(2)}) collective-permute-start(f32[2,256,256]{2,1,0:T(8,128)S(1)} %pad_maximum_fusion), channel_id=1, source_target_pairs={{0,16},{1,2},{2,1},{3,19},{4,20},{5,6},{6,5},{7,23},{8,24},{9,10},... | collective-permute-start | bytes 1572872 | tf_op jit(solution)/shard_map/ppermute | solution.py:67
  10.2 2.4 %collective-permute-start.2 = (f32[8,8,128]{2,1,0:T(8,128)S(1)}, f32[8,8,128]{2,1,0:T(8,128)S(1)}, u32[]{:S(2)}, u32[]{:S(2)}) collective-permute-start(f32[8,8,128]{2,1,0:T(8,128)S(1)} %get-tuple-element.146), channel_id=1, source_target_pairs={{0,8},{1,9},{2,10},{3,11},{4,12},{5,13},{6,14},{7,15},{8,0},{9,1},... | collective-permute-start | bytes 98312 | tf_op jit(solution)/shard_map/ppermute | solution.py:67
  14.7 1.6 %collective-permute-start.5 = (f32[2,128,256]{2,1,0:T(8,128)S(1)}, f32[2,128,256]{2,1,0:T(8,128)S(1)}, u32[]{:S(2)}, u32[]{:S(2)}) collective-permute-start(f32[2,128,256]{2,1,0:T(8,128)S(1)} %get-tuple-element.153), channel_id=1, source_target_pairs={{0,1},{1,0},{2,3},{3,2},{4,5},{5,4},{6,7},{7,6},{8,9},{9,8},{10,11... | collective-permute-start | bytes 786440 | tf_op jit(solution)/shard_map/ppermute | solution.py:67
  18.4 1.6 %collective-permute-start.9 = (f32[256,256]{1,0:T(8,128)S(1)}, f32[256,256]{1,0:T(8,128)S(1)}, u32[]{:S(2)}, u32[]{:S(2)}) collective-permute-start(f32[256,256]{1,0:T(8,128)S(1)} %bitcast.18), channel_id=1, source_target_pairs={{0,16},{1,2},{2,1},{3,19},{4,20},{5,6},{6,5},{7,23},{8,24},{9,10},... | collective-permute-start | bytes 786440 | tf_op jit(solution)/shard_map/ppermute | solution.py:67
  20.9 1.5 %collective-permute-done.6.zm = f32[2,128,256]{2,1,0:T(8,128)S(1)} collective-permute-done((f32[2,128,256]{2,1,0:T(8,128)S(1)}, f32[2,128,256]{2,1,0:T(8,128)S(1)}, u32[]{:S(2)}, u32[]{:S(2)}) %collective-permute-start.6) | collective-permute-done | bytes 262176 | tf_op jit(solution)/shard_map/ppermute | solution.py:67
  22.9 1.4 %collective-permute-start.8 = (f32[168,256]{1,0:T(8,128)S(1)}, f32[168,256]{1,0:T(8,128)S(1)}, u32[]{:S(2)}, u32[]{:S(2)}) collective-permute-start(f32[168,256]{1,0:T(8,128)S(1)} %get-tuple-element.171), channel_id=1, source_target_pairs={{0,1},{1,0},{2,3},{3,2},{4,5},{5,4},{6,7},{7,6},{8,9},{9,8},{10,11... | collective-permute-start | bytes 516104 | tf_op jit(solution)/shard_map/ppermute | solution.py:67
  24.3 1.4 %collective-permute-start.12 = (f32[32,256]{1,0:T(8,128)S(1)}, f32[32,256]{1,0:T(8,128)S(1)}, u32[]{:S(2)}, u32[]{:S(2)}) collective-permute-start(f32[32,256]{1,0:T(8,128)S(1)} %get-tuple-element.178), channel_id=1, source_target_pairs={{0,2},{1,3},{2,0},{3,1},{4,6},{5,7},{6,4},{7,5},{8,10},{9,11},{10,... | collective-permute-start | bytes 98312 | tf_op jit(solution)/shard_map/ppermute | solution.py:67
  25.8 1.4 %forward_inner.7 = (f32[256,256]{1,0:T(8,128)S(1)}, f32[256,256]{1,0:T(8,128)S(1)}) custom-call(s32[16]{0:T(128)S(1)} %copy-done.8, f32[8,16]{1,0:T(8,128)S(1)} %copy-done.3, f32[256,256]{1,0:T(8,128)S(1)} %get-tuple-element.166.cur.prev.before.state, f32[256,256]{1,0:T(8,128)S(1)} %get-tuple-element.149.cur.prev.before, ...), custom_call_target="tpu_custom_call" | custom-call | flops 1000 | bytes 4321000 | tf_op jit(solution)/shard_map/forward_inner/pallas_call | solution.py:600
  27.8 1.2 %collective-permute-done.11.zm = f32[128,256]{1,0:T(8,128)S(1)} collective-permute-done((f32[128,256]{1,0:T(8,128)S(1)}, f32[128,256]{1,0:T(8,128)S(1)}, u32[]{:S(2)}, u32[]{:S(2)}) %collective-permute-start.11) | collective-permute-done | bytes 131104 | tf_op jit(solution)/shard_map/ppermute | solution.py:67
  29.2 1.8 %collective-permute-start.13 = (f32[128,256]{1,0:T(8,128)S(1)}, f32[128,256]{1,0:T(8,128)S(1)}, u32[]{:S(2)}, u32[]{:S(2)}) collective-permute-start(f32[128,256]{1,0:T(8,128)S(1)} %get-tuple-element.181), channel_id=1, source_target_pairs={{0,1},{1,0},{2,3},{3,2},{4,5},{5,4},{6,7},{7,6},{8,9},{9,8},{10,11... | collective-permute-start | bytes 393224 | tf_op jit(solution)/shard_map/ppermute | solution.py:67
  32.1 1.4 %forward_inner.8 = (f32[256,256]{1,0:T(8,128)S(1)}, f32[256,256]{1,0:T(8,128)S(1)}) custom-call(s32[16]{0:T(128)S(1)} %copy-done.8, f32[8,16]{1,0:T(8,128)S(1)} %copy-done.3, f32[256,256]{1,0:T(8,128)S(1)} %get-tuple-element.180.cur.prev.before.state, f32[256,256]{1,0:T(8,128)S(1)} %get-tuple-element.166.cur.prev.before.state, ...), custom_call_target="tpu_custom_call" | custom-call | flops 1000 | bytes 4321000 | tf_op jit(solution)/shard_map/forward_inner/pallas_call | solution.py:600
  33.4 1.1 collective-permute-done.15.ym
  34.6 1.1 collective-permute-done.14.zm
  36.0 1.3 %collective-permute-start.16 = (f32[2,128,256]{2,1,0:T(8,128)S(1)}, f32[2,128,256]{2,1,0:T(8,128)S(1)}, u32[]{:S(2)}, u32[]{:S(2)}) collective-permute-start(f32[2,128,256]{2,1,0:T(8,128)S(1)} %get-tuple-element.188), channel_id=1, source_target_pairs={{0,1},{1,0},{2,3},{3,2},{4,5},{5,4},{6,7},{7,6},{8,9},{9,8},{10,11... | collective-permute-start | bytes 786440 | tf_op jit(solution)/shard_map/ppermute | solution.py:67
  38.5 1.4 %forward_inner.9 = (f32[256,256]{1,0:T(8,128)S(1)}, f32[256,256]{1,0:T(8,128)S(1)}) custom-call(s32[16]{0:T(128)S(1)} %copy-done.8, f32[8,16]{1,0:T(8,128)S(1)} %copy-done.3, f32[256,256]{1,0:T(8,128)S(1)} %get-tuple-element.187.cur.prev.before.state, f32[256,256]{1,0:T(8,128)S(1)} %get-tuple-element.180.cur.prev.before.state, ...), custom_call_target="tpu_custom_call" | custom-call | flops 1000 | bytes 4321000 | tf_op jit(solution)/shard_map/forward_inner/pallas_call | solution.py:600
  39.8 1.1 collective-permute-done.18.ym.u_ym
  41.0 2.4 %collective-permute-done.17.zm.u_zm = f32[2,128,256]{2,1,0:T(8,128)S(1)} collective-permute-done((f32[2,128,256]{2,1,0:T(8,128)S(1)}, f32[2,128,256]{2,1,0:T(8,128)S(1)}, u32[]{:S(2)}, u32[]{:S(2)}) %collective-permute-start.17) | collective-permute-done | bytes 262176 | tf_op jit(solution)/shard_map/ppermute | solution.py:67
  45.0 1.4 %forward_inner.10 = (f32[256,256]{1,0:T(8,128)S(1)}, f32[256,256]{1,0:T(8,128)S(1)}) custom-call(s32[16]{0:T(128)S(1)} %copy-done.8, f32[8,16]{1,0:T(8,128)S(1)} %copy-done.3, f32[256,256]{1,0:T(8,128)S(1)} %get-tuple-element.192.cur.prev.before.state, f32[256,256]{1,0:T(8,128)S(1)} %get-tuple-element.187.cur.prev.before.state, ...), custom_call_target="tpu_custom_call" | custom-call | flops 1000 | bytes 4321000 | tf_op jit(solution)/shard_map/forward_inner/pallas_call | solution.py:600
  46.9 1.9 %collective-permute-done.20.zm = f32[128,256]{1,0:T(8,128)S(1)} collective-permute-done((f32[128,256]{1,0:T(8,128)S(1)}, f32[128,256]{1,0:T(8,128)S(1)}, u32[]{:S(2)}, u32[]{:S(2)}) %collective-permute-start.20) | collective-permute-done | bytes 131104 | tf_op jit(solution)/shard_map/ppermute | solution.py:67
  51.1 1.4 %forward_inner.11 = (f32[256,256]{1,0:T(8,128)S(1)}, f32[256,256]{1,0:T(8,128)S(1)}) custom-call(s32[16]{0:T(128)S(1)} %copy-done.8, f32[8,16]{1,0:T(8,128)S(1)} %copy-done.3, f32[256,256]{1,0:T(8,128)S(1)} %get-tuple-element.197.cur.prev.before.state, f32[256,256]{1,0:T(8,128)S(1)} %get-tuple-element.192.cur.prev.before.state, ...), custom_call_target="tpu_custom_call" | custom-call | flops 1000 | bytes 4321000 | tf_op jit(solution)/shard_map/forward_inner/pallas_call | solution.py:600
  53.2 1.0 collective-permute-done.23.zm
  56.2 1.4 %forward_inner.12 = (f32[256,256]{1,0:T(8,128)S(1)}, f32[256,256]{1,0:T(8,128)S(1)}) custom-call(s32[16]{0:T(128)S(1)} %copy-done.8, f32[8,16]{1,0:T(8,128)S(1)} %copy-done.3, f32[256,256]{1,0:T(8,128)S(1)} %get-tuple-element.204.cur.prev.rest_2_.state, f32[256,256]{1,0:T(8,128)S(1)} %get-tuple-element.197.cur.prev.before.state, ...), custom_call_target="tpu_custom_call" | custom-call | flops 1000 | bytes 4321000 | tf_op jit(solution)/shard_map/forward_inner/pallas_call | solution.py:600
  61.4 1.4 %forward_inner.13 = (f32[256,256]{1,0:T(8,128)S(1)}, f32[256,256]{1,0:T(8,128)S(1)}) custom-call(s32[16]{0:T(128)S(1)} %copy-done.8, f32[8,16]{1,0:T(8,128)S(1)} %copy-done.3, f32[256,256]{1,0:T(8,128)S(1)} %get-tuple-element.213.cur.state.rest_1_, f32[256,256]{1,0:T(8,128)S(1)} %get-tuple-element.204.cur.prev.rest_2_.state, ...), custom_call_target="tpu_custom_call" | custom-call | flops 1000 | bytes 4321000 | tf_op jit(solution)/shard_map/forward_inner/pallas_call | solution.py:600
  62.8 1.2 %collective-permute-done.30.ym = f32[32,256]{1,0:T(8,128)S(1)} collective-permute-done((f32[32,256]{1,0:T(8,128)S(1)}, f32[32,256]{1,0:T(8,128)S(1)}, u32[]{:S(2)}, u32[]{:S(2)}) %collective-permute-start.30) | collective-permute-done | bytes 32800 | tf_op jit(solution)/shard_map/ppermute | solution.py:67
  67.4 1.0 adjoint_inner.7
  68.4 1.6 %collective-permute-done.33.ym = f32[32,256]{1,0:T(8,128)S(1)} collective-permute-done((f32[32,256]{1,0:T(8,128)S(1)}, f32[32,256]{1,0:T(8,128)S(1)}, u32[]{:S(2)}, u32[]{:S(2)}) %collective-permute-start.33) | collective-permute-done | bytes 32800 | tf_op jit(solution)/shard_map/ppermute | solution.py:67
  72.8 1.0 adjoint_inner.8
  73.7 1.6 %collective-permute-done.36.ym = f32[32,256]{1,0:T(8,128)S(1)} collective-permute-done((f32[32,256]{1,0:T(8,128)S(1)}, f32[32,256]{1,0:T(8,128)S(1)}, u32[]{:S(2)}, u32[]{:S(2)}) %collective-permute-start.36) | collective-permute-done | bytes 32800 | tf_op jit(solution)/shard_map/ppermute | solution.py:67
  78.1 1.0 adjoint_inner.9
  79.1 1.6 %collective-permute-done.39.ym = f32[32,256]{1,0:T(8,128)S(1)} collective-permute-done((f32[32,256]{1,0:T(8,128)S(1)}, f32[32,256]{1,0:T(8,128)S(1)}, u32[]{:S(2)}, u32[]{:S(2)}) %collective-permute-start.39) | collective-permute-done | bytes 32800 | tf_op jit(solution)/shard_map/ppermute | solution.py:67
  83.5 1.0 adjoint_inner.10
  84.5 1.6 %collective-permute-done.42.ym = f32[32,256]{1,0:T(8,128)S(1)} collective-permute-done((f32[32,256]{1,0:T(8,128)S(1)}, f32[32,256]{1,0:T(8,128)S(1)}, u32[]{:S(2)}, u32[]{:S(2)}) %collective-permute-start.42) | collective-permute-done | bytes 32800 | tf_op jit(solution)/shard_map/ppermute | solution.py:67
  89.1 1.0 adjoint_inner.11
  90.1 1.6 %collective-permute-done.45.ym = f32[32,256]{1,0:T(8,128)S(1)} collective-permute-done((f32[32,256]{1,0:T(8,128)S(1)}, f32[32,256]{1,0:T(8,128)S(1)}, u32[]{:S(2)}, u32[]{:S(2)}) %collective-permute-start.45) | collective-permute-done | bytes 32800 | tf_op jit(solution)/shard_map/ppermute | solution.py:67
  94.5 1.0 adjoint_inner.12
  95.4 1.6 %collective-permute-done.48.ym = f32[32,256]{1,0:T(8,128)S(1)} collective-permute-done((f32[32,256]{1,0:T(8,128)S(1)}, f32[32,256]{1,0:T(8,128)S(1)}, u32[]{:S(2)}, u32[]{:S(2)}) %collective-permute-start.48) | collective-permute-done | bytes 32800 | tf_op jit(solution)/shard_map/ppermute | solution.py:67
  99.8 1.0 adjoint_inner.13
  100.8 1.6 %collective-permute-done.51.ym = f32[32,256]{1,0:T(8,128)S(1)} collective-permute-done((f32[32,256]{1,0:T(8,128)S(1)}, f32[32,256]{1,0:T(8,128)S(1)}, u32[]{:S(2)}, u32[]{:S(2)}) %collective-permute-start.51) | collective-permute-done | bytes 32800 | tf_op jit(solution)/shard_map/ppermute | solution.py:67
  105.3 1.0 collective-permute-done.52.got
  106.3 1.4 %collective-permute-start.53 = (f32[2,64,128]{2,1,0:T(8,128)S(1)}, f32[2,64,128]{2,1,0:T(8,128)S(1)}, u32[]{:S(2)}, u32[]{:S(2)}) collective-permute-start(f32[2,64,128]{2,1,0:T(8,128)S(1)} %get-tuple-element.273), channel_id=1, source_target_pairs={{0,12},{1,14},{2,13},{3,15},{4,8},{5,10},{6,9},{7,11},{8,4},{9,6},... | collective-permute-start | bytes 196616 | tf_op jit(solution)/shard_map/ppermute | solution.py:67
  107.7 1.7 %collective-permute-start.55 = (f32[2,64,128]{2,1,0:T(8,128)S(1)}, f32[2,64,128]{2,1,0:T(8,128)S(1)}, u32[]{:S(2)}, u32[]{:S(2)}) collective-permute-start(f32[2,64,128]{2,1,0:T(8,128)S(1)} %get-tuple-element.277), channel_id=1, source_target_pairs={{0,8},{1,10},{2,9},{3,11},{4,12},{5,14},{6,13},{7,15},{8,0},{9,2},... | collective-permute-start | bytes 196616 | tf_op jit(solution)/shard_map/ppermute | solution.py:67
  109.4 2.1 %collective-permute-start.56 = (f32[2,64,128]{2,1,0:T(8,128)S(1)}, f32[2,64,128]{2,1,0:T(8,128)S(1)}, u32[]{:S(2)}, u32[]{:S(2)}) collective-permute-start(f32[2,64,128]{2,1,0:T(8,128)S(1)} %get-tuple-element.278), channel_id=1, source_target_pairs={{0,4},{1,6},{2,5},{3,7},{4,0},{5,2},{6,1},{7,3},{8,12},{9,14},{10,... | collective-permute-start | bytes 196616 | tf_op jit(solution)/shard_map/ppermute | solution.py:67
  111.6 2.9 %collective-permute-start.57 = (f32[2,64,128]{2,1,0:T(8,128)S(1)}, f32[2,64,128]{2,1,0:T(8,128)S(1)}, u32[]{:S(2)}, u32[]{:S(2)}) collective-permute-start(f32[2,64,128]{2,1,0:T(8,128)S(1)} %get-tuple-element.279), channel_id=1, source_target_pairs={{0,0},{1,2},{2,1},{3,3},{4,4},{5,6},{6,5},{7,7},{8,8},{9,10},{10,9... | collective-permute-start | bytes 196616 | tf_op jit(solution)/shard_map/ppermute | solution.py:67
  115.6 1.5 %collective-permute-done.57.refs_3_ = f32[2,64,128]{2,1,0:T(8,128)S(1)} collective-permute-done((f32[2,64,128]{2,1,0:T(8,128)S(1)}, f32[2,64,128]{2,1,0:T(8,128)S(1)}, u32[]{:S(2)}, u32[]{:S(2)}) %collective-permute-start.57) | collective-permute-done | bytes 65568 | tf_op jit(solution)/shard_map/ppermute | solution.py:67
  117.1 1.3 %filter.1 = f32[32,32,64]{2,1,0:T(8,128)} custom-call(f32[2,64,128]{2,1,0:T(8,128)S(1)} %collective-permute-done.53.refs_0_, f32[2,64,128]{2,1,0:T(8,128)S(1)} %collective-permute-done.55.refs_1_, f32[2,64,128]{2,1,0:T(8,128)S(1)} %collective-permute-done.56.refs_2_, f32[2,64,128]{2,1,0:T(8,128)S(1)} %collective-permute-done.57.refs_3_), custom_call_target="tpu_custom_call" | custom-call | flops 1000 | bytes 1000 | tf_op jit(solution)/shard_map/filter/pallas_call | solution.py:600
  (152 shorter events, 46.3 us)
Async XLA Ops:
  2.8 7.3 %collective-permute-start.1 = (f32[8,8,128]{2,1,0:T(8,128)S(1)}, f32[8,8,128]{2,1,0:T(8,128)S(1)}, u32[]{:S(2)}, u32[]{:S(2)}) collective-permute-start(f32[8,8,128]{2,1,0:T(8,128)S(1)} %get-tuple-element.144), channel_id=1, source_target_pairs={{0,4},{1,5},{2,6},{3,7},{4,0},{5,1},{6,2},{7,3},{8,12},{9,13},{10,... | collective-permute-start | bytes 98312 | tf_op jit(solution)/shard_map/ppermute | solution.py:67
  5.0 9.5 %collective-permute-start.3 = (f32[256,256]{1,0:T(8,128)}, f32[256,256]{1,0:T(8,128)S(1)}, u32[]{:S(2)}, u32[]{:S(2)}) collective-permute-start(f32[256,256]{1,0:T(8,128)} %bitcast.16), channel_id=1, source_target_pairs={{0,16},{1,2},{2,1},{3,19},{4,20},{5,6},{6,5},{7,23},{8,24},{9,10},... | collective-permute-start | bytes 786440 | tf_op jit(solution)/shard_map/ppermute | solution.py:67
  7.1 7.4 %collective-permute-start = (f32[256,256]{1,0:T(8,128)}, f32[256,256]{1,0:T(8,128)S(1)}, u32[]{:S(2)}, u32[]{:S(2)}) collective-permute-start(f32[256,256]{1,0:T(8,128)} %bitcast.14), channel_id=1, source_target_pairs={{0,16},{1,2},{2,1},{3,19},{4,20},{5,6},{6,5},{7,23},{8,24},{9,10},... | collective-permute-start | bytes 786440 | tf_op jit(solution)/shard_map/ppermute | solution.py:67
  8.2 12.5 %collective-permute-start.4 = (f32[2,256,256]{2,1,0:T(8,128)S(1)}, f32[2,256,256]{2,1,0:T(8,128)S(1)}, u32[]{:S(2)}, u32[]{:S(2)}) collective-permute-start(f32[2,256,256]{2,1,0:T(8,128)S(1)} %pad_maximum_fusion), channel_id=1, source_target_pairs={{0,16},{1,2},{2,1},{3,19},{4,20},{5,6},{6,5},{7,23},{8,24},{9,10},... | collective-permute-start | bytes 1572872 | tf_op jit(solution)/shard_map/ppermute | solution.py:67
  10.2 4.0 %collective-permute-start.2 = (f32[8,8,128]{2,1,0:T(8,128)S(1)}, f32[8,8,128]{2,1,0:T(8,128)S(1)}, u32[]{:S(2)}, u32[]{:S(2)}) collective-permute-start(f32[8,8,128]{2,1,0:T(8,128)S(1)} %get-tuple-element.146), channel_id=1, source_target_pairs={{0,8},{1,9},{2,10},{3,11},{4,12},{5,13},{6,14},{7,15},{8,0},{9,1},... | collective-permute-start | bytes 98312 | tf_op jit(solution)/shard_map/ppermute | solution.py:67
  14.7 2.8 %collective-permute-start.5 = (f32[2,128,256]{2,1,0:T(8,128)S(1)}, f32[2,128,256]{2,1,0:T(8,128)S(1)}, u32[]{:S(2)}, u32[]{:S(2)}) collective-permute-start(f32[2,128,256]{2,1,0:T(8,128)S(1)} %get-tuple-element.153), channel_id=1, source_target_pairs={{0,1},{1,0},{2,3},{3,2},{4,5},{5,4},{6,7},{7,6},{8,9},{9,8},{10,11... | collective-permute-start | bytes 786440 | tf_op jit(solution)/shard_map/ppermute | solution.py:67
  16.3 6.1 %collective-permute-start.6 = (f32[2,128,256]{2,1,0:T(8,128)S(1)}, f32[2,128,256]{2,1,0:T(8,128)S(1)}, u32[]{:S(2)}, u32[]{:S(2)}) collective-permute-start(f32[2,128,256]{2,1,0:T(8,128)S(1)} %get-tuple-element.162), channel_id=1, source_target_pairs={{0,16},{1,4},{2,18},{3,6},{4,1},{5,8},{6,3},{7,10},{8,5},{9,12},{1... | collective-permute-start | bytes 786440 | tf_op jit(solution)/shard_map/ppermute | solution.py:67
  16.3 4.5 %collective-permute-start.7 = (f32[2,32,256]{2,1,0:T(8,128)S(1)}, f32[2,32,256]{2,1,0:T(8,128)S(1)}, u32[]{:S(2)}, u32[]{:S(2)}) collective-permute-start(f32[2,32,256]{2,1,0:T(8,128)S(1)} %get-tuple-element.163), channel_id=1, source_target_pairs={{0,2},{1,3},{2,0},{3,1},{4,6},{5,7},{6,4},{7,5},{8,10},{9,11},{10,... | collective-permute-start | bytes 196616 | tf_op jit(solution)/shard_map/ppermute | solution.py:67
  18.4 8.7 %collective-permute-start.9 = (f32[256,256]{1,0:T(8,128)S(1)}, f32[256,256]{1,0:T(8,128)S(1)}, u32[]{:S(2)}, u32[]{:S(2)}) collective-permute-start(f32[256,256]{1,0:T(8,128)S(1)} %bitcast.18), channel_id=1, source_target_pairs={{0,16},{1,2},{2,1},{3,19},{4,20},{5,6},{6,5},{7,23},{8,24},{9,10},... | collective-permute-start | bytes 786440 | tf_op jit(solution)/shard_map/ppermute | solution.py:67
  20.0 7.5 %collective-permute-start.10 = (f32[256,256]{1,0:T(8,128)S(1)}, f32[256,256]{1,0:T(8,128)S(1)}, u32[]{:S(2)}, u32[]{:S(2)}) collective-permute-start(f32[256,256]{1,0:T(8,128)S(1)} %bitcast.20), channel_id=1, source_target_pairs={{0,16},{1,2},{2,1},{3,19},{4,20},{5,6},{6,5},{7,23},{8,24},{9,10},... | collective-permute-start | bytes 786440 | tf_op jit(solution)/shard_map/ppermute | solution.py:67
  22.9 2.9 %collective-permute-start.8 = (f32[168,256]{1,0:T(8,128)S(1)}, f32[168,256]{1,0:T(8,128)S(1)}, u32[]{:S(2)}, u32[]{:S(2)}) collective-permute-start(f32[168,256]{1,0:T(8,128)S(1)} %get-tuple-element.171), channel_id=1, source_target_pairs={{0,1},{1,0},{2,3},{3,2},{4,5},{5,4},{6,7},{7,6},{8,9},{9,8},{10,11... | collective-permute-start | bytes 516104 | tf_op jit(solution)/shard_map/ppermute | solution.py:67
  24.3 4.7 %collective-permute-start.11 = (f32[128,256]{1,0:T(8,128)S(1)}, f32[128,256]{1,0:T(8,128)S(1)}, u32[]{:S(2)}, u32[]{:S(2)}) collective-permute-start(f32[128,256]{1,0:T(8,128)S(1)} %get-tuple-element.177), channel_id=1, source_target_pairs={{0,16},{1,4},{2,18},{3,6},{4,1},{5,8},{6,3},{7,10},{8,5},{9,12},{1... | collective-permute-start | bytes 393224 | tf_op jit(solution)/shard_map/ppermute | solution.py:67
  24.3 3.5 %collective-permute-start.12 = (f32[32,256]{1,0:T(8,128)S(1)}, f32[32,256]{1,0:T(8,128)S(1)}, u32[]{:S(2)}, u32[]{:S(2)}) collective-permute-start(f32[32,256]{1,0:T(8,128)S(1)} %get-tuple-element.178), channel_id=1, source_target_pairs={{0,2},{1,3},{2,0},{3,1},{4,6},{5,7},{6,4},{7,5},{8,10},{9,11},{10,... | collective-permute-start | bytes 98312 | tf_op jit(solution)/shard_map/ppermute | solution.py:67
  29.2 2.8 %collective-permute-start.13 = (f32[128,256]{1,0:T(8,128)S(1)}, f32[128,256]{1,0:T(8,128)S(1)}, u32[]{:S(2)}, u32[]{:S(2)}) collective-permute-start(f32[128,256]{1,0:T(8,128)S(1)} %get-tuple-element.181), channel_id=1, source_target_pairs={{0,1},{1,0},{2,3},{3,2},{4,5},{5,4},{6,7},{7,6},{8,9},{9,8},{10,11... | collective-permute-start | bytes 393224 | tf_op jit(solution)/shard_map/ppermute | solution.py:67
  31.1 4.7 %collective-permute-start.14 = (f32[128,256]{1,0:T(8,128)S(1)}, f32[128,256]{1,0:T(8,128)S(1)}, u32[]{:S(2)}, u32[]{:S(2)}) collective-permute-start(f32[128,256]{1,0:T(8,128)S(1)} %get-tuple-element.183), channel_id=1, source_target_pairs={{0,16},{1,4},{2,18},{3,6},{4,1},{5,8},{6,3},{7,10},{8,5},{9,12},{1... | collective-permute-start | bytes 393224 | tf_op jit(solution)/shard_map/ppermute | solution.py:67
  31.1 3.5 %collective-permute-start.15 = (f32[72,256]{1,0:T(8,128)S(1)}, f32[72,256]{1,0:T(8,128)S(1)}, u32[]{:S(2)}, u32[]{:S(2)}) collective-permute-start(f32[72,256]{1,0:T(8,128)S(1)} %get-tuple-element.184), channel_id=1, source_target_pairs={{0,2},{1,3},{2,0},{3,1},{4,6},{5,7},{6,4},{7,5},{8,10},{9,11},{10,... | collective-permute-start | bytes 221192 | tf_op jit(solution)/shard_map/ppermute | solution.py:67
  36.0 2.5 %collective-permute-start.16 = (f32[2,128,256]{2,1,0:T(8,128)S(1)}, f32[2,128,256]{2,1,0:T(8,128)S(1)}, u32[]{:S(2)}, u32[]{:S(2)}) collective-permute-start(f32[2,128,256]{2,1,0:T(8,128)S(1)} %get-tuple-element.188), channel_id=1, source_target_pairs={{0,1},{1,0},{2,3},{3,2},{4,5},{5,4},{6,7},{7,6},{8,9},{9,8},{10,11... | collective-permute-start | bytes 786440 | tf_op jit(solution)/shard_map/ppermute | solution.py:67
  37.3 6.1 %collective-permute-start.17 = (f32[2,128,256]{2,1,0:T(8,128)S(1)}, f32[2,128,256]{2,1,0:T(8,128)S(1)}, u32[]{:S(2)}, u32[]{:S(2)}) collective-permute-start(f32[2,128,256]{2,1,0:T(8,128)S(1)} %get-tuple-element.190), channel_id=1, source_target_pairs={{0,16},{1,4},{2,18},{3,6},{4,1},{5,8},{6,3},{7,10},{8,5},{9,12},{1... | collective-permute-start | bytes 786440 | tf_op jit(solution)/shard_map/ppermute | solution.py:67
  37.6 3.4 %collective-permute-start.18 = (f32[2,32,256]{2,1,0:T(8,128)S(1)}, f32[2,32,256]{2,1,0:T(8,128)S(1)}, u32[]{:S(2)}, u32[]{:S(2)}) collective-permute-start(f32[2,32,256]{2,1,0:T(8,128)S(1)} %get-tuple-element.191), channel_id=1, source_target_pairs={{0,2},{1,3},{2,0},{3,1},{4,6},{5,7},{6,4},{7,5},{8,10},{9,11},{10,... | collective-permute-start | bytes 196616 | tf_op jit(solution)/shard_map/ppermute | solution.py:67
  44.1 4.7 %collective-permute-start.20 = (f32[128,256]{1,0:T(8,128)S(1)}, f32[128,256]{1,0:T(8,128)S(1)}, u32[]{:S(2)}, u32[]{:S(2)}) collective-permute-start(f32[128,256]{1,0:T(8,128)S(1)} %get-tuple-element.195), channel_id=1, source_target_pairs={{0,16},{1,4},{2,18},{3,6},{4,1},{5,8},{6,3},{7,10},{8,5},{9,12},{1... | collective-permute-start | bytes 393224 | tf_op jit(solution)/shard_map/ppermute | solution.py:67
  44.1 2.8 %collective-permute-start.21 = (f32[32,256]{1,0:T(8,128)S(1)}, f32[32,256]{1,0:T(8,128)S(1)}, u32[]{:S(2)}, u32[]{:S(2)}) collective-permute-start(f32[32,256]{1,0:T(8,128)S(1)} %get-tuple-element.196), channel_id=1, source_target_pairs={{0,2},{1,3},{2,0},{3,1},{4,6},{5,7},{6,4},{7,5},{8,10},{9,11},{10,... | collective-permute-start | bytes 98312 | tf_op jit(solution)/shard_map/ppermute | solution.py:67
  49.0 2.2 %collective-permute-start.22 = (f32[128,256]{1,0:T(8,128)S(1)}, f32[128,256]{1,0:T(8,128)S(1)}, u32[]{:S(2)}, u32[]{:S(2)}) collective-permute-start(f32[128,256]{1,0:T(8,128)S(1)} %get-tuple-element.198), channel_id=1, source_target_pairs={{0,1},{1,0},{2,3},{3,2},{4,5},{5,4},{6,7},{7,6},{8,9},{9,8},{10,11... | collective-permute-start | bytes 393224 | tf_op jit(solution)/shard_map/ppermute | solution.py:67
  49.4 4.7 %collective-permute-start.23 = (f32[128,256]{1,0:T(8,128)S(1)}, f32[128,256]{1,0:T(8,128)S(1)}, u32[]{:S(2)}, u32[]{:S(2)}) collective-permute-start(f32[128,256]{1,0:T(8,128)S(1)} %get-tuple-element.202), channel_id=1, source_target_pairs={{0,16},{1,4},{2,18},{3,6},{4,1},{5,8},{6,3},{7,10},{8,5},{9,12},{1... | collective-permute-start | bytes 393224 | tf_op jit(solution)/shard_map/ppermute | solution.py:67
  50.1 3.1 %collective-permute-start.24 = (f32[32,256]{1,0:T(8,128)S(1)}, f32[32,256]{1,0:T(8,128)S(1)}, u32[]{:S(2)}, u32[]{:S(2)}) collective-permute-start(f32[32,256]{1,0:T(8,128)S(1)} %get-tuple-element.203), channel_id=1, source_target_pairs={{0,2},{1,3},{2,0},{3,1},{4,6},{5,7},{6,4},{7,5},{8,10},{9,11},{10,... | collective-permute-start | bytes 98312 | tf_op jit(solution)/shard_map/ppermute | solution.py:67
  54.3 1.9 %collective-permute-start.25 = (f32[128,256]{1,0:T(8,128)S(1)}, f32[128,256]{1,0:T(8,128)S(1)}, u32[]{:S(2)}, u32[]{:S(2)}) collective-permute-start(f32[128,256]{1,0:T(8,128)S(1)} %get-tuple-element.205), channel_id=1, source_target_pairs={{0,1},{1,0},{2,3},{3,2},{4,5},{5,4},{6,7},{7,6},{8,9},{9,8},{10,11... | collective-permute-start | bytes 393224 | tf_op jit(solution)/shard_map/ppermute | solution.py:67
  54.8 4.7 %collective-permute-start.26 = (f32[128,256]{1,0:T(8,128)S(1)}, f32[128,256]{1,0:T(8,128)S(1)}, u32[]{:S(2)}, u32[]{:S(2)}) collective-permute-start(f32[128,256]{1,0:T(8,128)S(1)} %get-tuple-element.211), channel_id=1, source_target_pairs={{0,16},{1,4},{2,18},{3,6},{4,1},{5,8},{6,3},{7,10},{8,5},{9,12},{1... | collective-permute-start | bytes 393224 | tf_op jit(solution)/shard_map/ppermute | solution.py:67
  55.5 3.1 %collective-permute-start.27 = (f32[32,256]{1,0:T(8,128)S(1)}, f32[32,256]{1,0:T(8,128)S(1)}, u32[]{:S(2)}, u32[]{:S(2)}) collective-permute-start(f32[32,256]{1,0:T(8,128)S(1)} %get-tuple-element.212), channel_id=1, source_target_pairs={{0,2},{1,3},{2,0},{3,1},{4,6},{5,7},{6,4},{7,5},{8,10},{9,11},{10,... | collective-permute-start | bytes 98312 | tf_op jit(solution)/shard_map/ppermute | solution.py:67
  60.2 4.7 %collective-permute-start.29 = (f32[128,256]{1,0:T(8,128)S(1)}, f32[128,256]{1,0:T(8,128)S(1)}, u32[]{:S(2)}, u32[]{:S(2)}) collective-permute-start(f32[128,256]{1,0:T(8,128)S(1)} %get-tuple-element.216), channel_id=1, source_target_pairs={{0,16},{1,4},{2,18},{3,6},{4,1},{5,8},{6,3},{7,10},{8,5},{9,12},{1... | collective-permute-start | bytes 393224 | tf_op jit(solution)/shard_map/ppermute | solution.py:67
  60.9 3.1 %collective-permute-start.30 = (f32[32,256]{1,0:T(8,128)S(1)}, f32[32,256]{1,0:T(8,128)S(1)}, u32[]{:S(2)}, u32[]{:S(2)}) collective-permute-start(f32[32,256]{1,0:T(8,128)S(1)} %get-tuple-element.217), channel_id=1, source_target_pairs={{0,2},{1,3},{2,0},{3,1},{4,6},{5,7},{6,4},{7,5},{8,10},{9,11},{10,... | collective-permute-start | bytes 98312 | tf_op jit(solution)/shard_map/ppermute | solution.py:67
  66.2 4.7 %collective-permute-start.32 = (f32[128,256]{1,0:T(8,128)S(1)}, f32[128,256]{1,0:T(8,128)S(1)}, u32[]{:S(2)}, u32[]{:S(2)}) collective-permute-start(f32[128,256]{1,0:T(8,128)S(1)} %get-tuple-element.225), channel_id=1, source_target_pairs={{0,16},{1,4},{2,18},{3,6},{4,1},{5,8},{6,3},{7,10},{8,5},{9,12},{1... | collective-permute-start | bytes 393224 | tf_op jit(solution)/shard_map/ppermute | solution.py:67
  66.9 3.1 %collective-permute-start.33 = (f32[32,256]{1,0:T(8,128)S(1)}, f32[32,256]{1,0:T(8,128)S(1)}, u32[]{:S(2)}, u32[]{:S(2)}) collective-permute-start(f32[32,256]{1,0:T(8,128)S(1)} %get-tuple-element.226), channel_id=1, source_target_pairs={{0,2},{1,3},{2,0},{3,1},{4,6},{5,7},{6,4},{7,5},{8,10},{9,11},{10,... | collective-permute-start | bytes 98312 | tf_op jit(solution)/shard_map/ppermute | solution.py:67
  71.6 4.7 %collective-permute-start.35 = (f32[128,256]{1,0:T(8,128)S(1)}, f32[128,256]{1,0:T(8,128)S(1)}, u32[]{:S(2)}, u32[]{:S(2)}) collective-permute-start(f32[128,256]{1,0:T(8,128)S(1)} %get-tuple-element.232), channel_id=1, source_target_pairs={{0,16},{1,4},{2,18},{3,6},{4,1},{5,8},{6,3},{7,10},{8,5},{9,12},{1... | collective-permute-start | bytes 393224 | tf_op jit(solution)/shard_map/ppermute | solution.py:67
  72.3 3.1 %collective-permute-start.36 = (f32[32,256]{1,0:T(8,128)S(1)}, f32[32,256]{1,0:T(8,128)S(1)}, u32[]{:S(2)}, u32[]{:S(2)}) collective-permute-start(f32[32,256]{1,0:T(8,128)S(1)} %get-tuple-element.233), channel_id=1, source_target_pairs={{0,2},{1,3},{2,0},{3,1},{4,6},{5,7},{6,4},{7,5},{8,10},{9,11},{10,... | collective-permute-start | bytes 98312 | tf_op jit(solution)/shard_map/ppermute | solution.py:67
  77.0 4.7 %collective-permute-start.38 = (f32[128,256]{1,0:T(8,128)S(1)}, f32[128,256]{1,0:T(8,128)S(1)}, u32[]{:S(2)}, u32[]{:S(2)}) collective-permute-start(f32[128,256]{1,0:T(8,128)S(1)} %get-tuple-element.239), channel_id=1, source_target_pairs={{0,16},{1,4},{2,18},{3,6},{4,1},{5,8},{6,3},{7,10},{8,5},{9,12},{1... | collective-permute-start | bytes 393224 | tf_op jit(solution)/shard_map/ppermute | solution.py:67
  77.6 3.1 %collective-permute-start.39 = (f32[32,256]{1,0:T(8,128)S(1)}, f32[32,256]{1,0:T(8,128)S(1)}, u32[]{:S(2)}, u32[]{:S(2)}) collective-permute-start(f32[32,256]{1,0:T(8,128)S(1)} %get-tuple-element.240), channel_id=1, source_target_pairs={{0,2},{1,3},{2,0},{3,1},{4,6},{5,7},{6,4},{7,5},{8,10},{9,11},{10,... | collective-permute-start | bytes 98312 | tf_op jit(solution)/shard_map/ppermute | solution.py:67
  82.3 4.7 %collective-permute-start.41 = (f32[128,256]{1,0:T(8,128)S(1)}, f32[128,256]{1,0:T(8,128)S(1)}, u32[]{:S(2)}, u32[]{:S(2)}) collective-permute-start(f32[128,256]{1,0:T(8,128)S(1)} %get-tuple-element.246), channel_id=1, source_target_pairs={{0,16},{1,4},{2,18},{3,6},{4,1},{5,8},{6,3},{7,10},{8,5},{9,12},{1... | collective-permute-start | bytes 393224 | tf_op jit(solution)/shard_map/ppermute | solution.py:67
  83.0 3.1 %collective-permute-start.42 = (f32[32,256]{1,0:T(8,128)S(1)}, f32[32,256]{1,0:T(8,128)S(1)}, u32[]{:S(2)}, u32[]{:S(2)}) collective-permute-start(f32[32,256]{1,0:T(8,128)S(1)} %get-tuple-element.247), channel_id=1, source_target_pairs={{0,2},{1,3},{2,0},{3,1},{4,6},{5,7},{6,4},{7,5},{8,10},{9,11},{10,... | collective-permute-start | bytes 98312 | tf_op jit(solution)/shard_map/ppermute | solution.py:67
  87.9 4.7 %collective-permute-start.44 = (f32[128,256]{1,0:T(8,128)S(1)}, f32[128,256]{1,0:T(8,128)S(1)}, u32[]{:S(2)}, u32[]{:S(2)}) collective-permute-start(f32[128,256]{1,0:T(8,128)S(1)} %get-tuple-element.253), channel_id=1, source_target_pairs={{0,16},{1,4},{2,18},{3,6},{4,1},{5,8},{6,3},{7,10},{8,5},{9,12},{1... | collective-permute-start | bytes 393224 | tf_op jit(solution)/shard_map/ppermute | solution.py:67
  88.6 3.1 %collective-permute-start.45 = (f32[32,256]{1,0:T(8,128)S(1)}, f32[32,256]{1,0:T(8,128)S(1)}, u32[]{:S(2)}, u32[]{:S(2)}) collective-permute-start(f32[32,256]{1,0:T(8,128)S(1)} %get-tuple-element.254), channel_id=1, source_target_pairs={{0,2},{1,3},{2,0},{3,1},{4,6},{5,7},{6,4},{7,5},{8,10},{9,11},{10,... | collective-permute-start | bytes 98312 | tf_op jit(solution)/shard_map/ppermute | solution.py:67
  93.3 4.7 %collective-permute-start.47 = (f32[128,256]{1,0:T(8,128)S(1)}, f32[128,256]{1,0:T(8,128)S(1)}, u32[]{:S(2)}, u32[]{:S(2)}) collective-permute-start(f32[128,256]{1,0:T(8,128)S(1)} %get-tuple-element.260), channel_id=1, source_target_pairs={{0,16},{1,4},{2,18},{3,6},{4,1},{5,8},{6,3},{7,10},{8,5},{9,12},{1... | collective-permute-start | bytes 393224 | tf_op jit(solution)/shard_map/ppermute | solution.py:67
  94.0 3.1 %collective-permute-start.48 = (f32[32,256]{1,0:T(8,128)S(1)}, f32[32,256]{1,0:T(8,128)S(1)}, u32[]{:S(2)}, u32[]{:S(2)}) collective-permute-start(f32[32,256]{1,0:T(8,128)S(1)} %get-tuple-element.261), channel_id=1, source_target_pairs={{0,2},{1,3},{2,0},{3,1},{4,6},{5,7},{6,4},{7,5},{8,10},{9,11},{10,... | collective-permute-start | bytes 98312 | tf_op jit(solution)/shard_map/ppermute | solution.py:67
  98.7 4.7 %collective-permute-start.50 = (f32[128,256]{1,0:T(8,128)S(1)}, f32[128,256]{1,0:T(8,128)S(1)}, u32[]{:S(2)}, u32[]{:S(2)}) collective-permute-start(f32[128,256]{1,0:T(8,128)S(1)} %get-tuple-element.267), channel_id=1, source_target_pairs={{0,16},{1,4},{2,18},{3,6},{4,1},{5,8},{6,3},{7,10},{8,5},{9,12},{1... | collective-permute-start | bytes 393224 | tf_op jit(solution)/shard_map/ppermute | solution.py:67
  99.3 3.1 %collective-permute-start.51 = (f32[32,256]{1,0:T(8,128)S(1)}, f32[32,256]{1,0:T(8,128)S(1)}, u32[]{:S(2)}, u32[]{:S(2)}) collective-permute-start(f32[32,256]{1,0:T(8,128)S(1)} %get-tuple-element.268), channel_id=1, source_target_pairs={{0,2},{1,3},{2,0},{3,1},{4,6},{5,7},{6,4},{7,5},{8,10},{9,11},{10,... | collective-permute-start | bytes 98312 | tf_op jit(solution)/shard_map/ppermute | solution.py:67
  103.9 10.6 %collective-permute-start.54 = (f32[2,256,256]{2,1,0:T(8,128)S(1)}, f32[2,256,256]{2,1,0:T(8,128)S(1)}, u32[]{:S(2)}, u32[]{:S(2)}) collective-permute-start(f32[2,256,256]{2,1,0:T(8,128)S(1)} %get-tuple-element.274.own), channel_id=1, source_target_pairs={{0,16},{1,2},{2,1},{3,19},{4,20},{5,6},{6,5},{7,23},{8,24},{9,10},... | collective-permute-start | bytes 1572872 | tf_op jit(solution)/shard_map/ppermute | solution.py:67
  106.3 9.0 %collective-permute-start.53 = (f32[2,64,128]{2,1,0:T(8,128)S(1)}, f32[2,64,128]{2,1,0:T(8,128)S(1)}, u32[]{:S(2)}, u32[]{:S(2)}) collective-permute-start(f32[2,64,128]{2,1,0:T(8,128)S(1)} %get-tuple-element.273), channel_id=1, source_target_pairs={{0,12},{1,14},{2,13},{3,15},{4,8},{5,10},{6,9},{7,11},{8,4},{9,6},... | collective-permute-start | bytes 196616 | tf_op jit(solution)/shard_map/ppermute | solution.py:67
  107.7 7.9 %collective-permute-start.55 = (f32[2,64,128]{2,1,0:T(8,128)S(1)}, f32[2,64,128]{2,1,0:T(8,128)S(1)}, u32[]{:S(2)}, u32[]{:S(2)}) collective-permute-start(f32[2,64,128]{2,1,0:T(8,128)S(1)} %get-tuple-element.277), channel_id=1, source_target_pairs={{0,8},{1,10},{2,9},{3,11},{4,12},{5,14},{6,13},{7,15},{8,0},{9,2},... | collective-permute-start | bytes 196616 | tf_op jit(solution)/shard_map/ppermute | solution.py:67
  109.4 6.2 %collective-permute-start.56 = (f32[2,64,128]{2,1,0:T(8,128)S(1)}, f32[2,64,128]{2,1,0:T(8,128)S(1)}, u32[]{:S(2)}, u32[]{:S(2)}) collective-permute-start(f32[2,64,128]{2,1,0:T(8,128)S(1)} %get-tuple-element.278), channel_id=1, source_target_pairs={{0,4},{1,6},{2,5},{3,7},{4,0},{5,2},{6,1},{7,3},{8,12},{9,14},{10,... | collective-permute-start | bytes 196616 | tf_op jit(solution)/shard_map/ppermute | solution.py:67
  111.6 5.6 %collective-permute-start.57 = (f32[2,64,128]{2,1,0:T(8,128)S(1)}, f32[2,64,128]{2,1,0:T(8,128)S(1)}, u32[]{:S(2)}, u32[]{:S(2)}) collective-permute-start(f32[2,64,128]{2,1,0:T(8,128)S(1)} %get-tuple-element.279), channel_id=1, source_target_pairs={{0,0},{1,2},{2,1},{3,3},{4,4},{5,6},{6,5},{7,7},{8,8},{9,10},{10,9... | collective-permute-start | bytes 196616 | tf_op jit(solution)/shard_map/ppermute | solution.py:67
  (28 other events, 59.3 us)

commit v20 on v17

--- a/solution.py
+++ b/solution.py
@@ -667,10 +667,13 @@
         rec_cells, observed, weight=0.2, far=3,
         scratch=[pltpu.VMEM(rec_counts.shape, jnp.int32), pltpu.VMEM(rec_cells.shape, jnp.int32),
                  pltpu.VMEM(observed.shape, F32)])
+    vel, p_before = call(settle_pair_kernel, "settle_model", [field, field],
+                         velocity, fwd_before, got_model, weight=0.6, far=2)
     for n, bit in enumerate(order[:-1]):
         lists, give = call(
             functools.partial(trade_kernel, bit, order[n + 1]), "trade", [entries, half_entries],
-            lists, send(give, stages[bit][0]), weight=0.1)
+            after(lists, vel) if n == len(order) - 2 else lists, send(give, stages[bit][0]),
+            weight=0.1)
         if n == 0:
             got[0], give = lax.optimization_barrier((got[0], give))
 
@@ -678,8 +681,6 @@
                                 [field, field] + [shaped(2, *r.shape) for r in rim],
                                 log_density, fwd_now, *got, far=2)
     zm, cm, ym = halo(*out)
-    vel, p_before = call(settle_pair_kernel, "settle_model", [field, field],
-                         velocity, fwd_before, got_model, weight=0.6, far=2)
     parts = call(first_inner_kernel, "first_inner", [field] * 7, density, p_now, cm,
                  near, deep, weight=1.3)
     got_adjoint = [send(after(v, parts[0]), swap_perm) for v in (adj_now, adj_before)]

time: 116 us -> 115 us (level)
  waiting for transfers between devices: 43.8 us -> 36 us
  starting transfers between devices: 41.2 us -> 48.4 us
    ppermute x58, waiting for transfers between devices: 43.8 us -> 36 us  [send(): return lax.ppermute(value, ALL, pairs)]
    ppermute x58, starting transfers between devices: 41.2 us -> 48.4 us  [send(): return lax.ppermute(value, ALL, pairs)]
  transfers between devices with their start and end apart: 58 -> 58, of which waited for: 46 -> 35; matrix products, arithmetic and copies ran while one was open for 1% -> 1% of each run, Pallas kernels for 18% -> 18%
where the time goes in v20:
time: 115 us
  starting transfers between devices  48.4 us (42%)
  waiting for transfers between devices  36 us (31%)
  Pallas kernels  26.8 us (23%)
  local copies, waits for them, and re-layouts  1.64 us (1%)
  other arithmetic  1.27 us (1%)
  between operations  1.18 us (1%)
    ppermute x58, starting transfers between devices, send(): return lax.ppermute(value, ALL, pairs)  48.4 us
    ppermute x58, waiting for transfers between devices, send(): return lax.ppermute(value, ALL, pairs)  36 us
    pallas_call x42, Pallas kernels, call(): pl.pallas_call(functools.partial(kernel, Flags()), name=name, out_shape=o...  26.8 us
  transfers between devices with their start and end apart: 58, of which 35 were waited for; matrix products, arithmetic and copies ran while one was open for 1% of the time, Pallas kernels for 18%

profile of v20, /device:TPU:1, one launch (start us, length us, event | category | flops | bytes accessed | tf_op | source)
XLA Modules:
  0.0 115.3 jit_solution(12709592298428609885)
XLA Ops:
  0.6 2.7 %collective-permute-start.2 = (f32[256,256]{1,0:T(8,128)}, f32[256,256]{1,0:T(8,128)S(1)}, u32[]{:S(2)}, u32[]{:S(2)}) collective-permute-start(f32[256,256]{1,0:T(8,128)} %bitcast.16), channel_id=1, source_target_pairs={{0,16},{1,2},{2,1},{3,19},{4,20},{5,6},{6,5},{7,23},{8,24},{9,10},... | collective-permute-start | bytes 786440 | tf_op jit(solution)/shard_map/ppermute | solution.py:67
  3.4 1.1 pad_maximum_fusion
  4.6 1.7 %collective-permute-start.3 = (f32[2,256,256]{2,1,0:T(8,128)S(1)}, f32[2,256,256]{2,1,0:T(8,128)S(1)}, u32[]{:S(2)}, u32[]{:S(2)}) collective-permute-start(f32[2,256,256]{2,1,0:T(8,128)S(1)} %pad_maximum_fusion), channel_id=1, source_target_pairs={{0,16},{1,2},{2,1},{3,19},{4,20},{5,6},{6,5},{7,23},{8,24},{9,10},... | collective-permute-start | bytes 1572872 | tf_op jit(solution)/shard_map/ppermute | solution.py:67
  6.5 1.4 %collective-permute-start.1 = (f32[8,8,128]{2,1,0:T(8,128)S(1)}, f32[8,8,128]{2,1,0:T(8,128)S(1)}, u32[]{:S(2)}, u32[]{:S(2)}) collective-permute-start(f32[8,8,128]{2,1,0:T(8,128)S(1)} %get-tuple-element.147), channel_id=1, source_target_pairs={{0,4},{1,5},{2,6},{3,7},{4,0},{5,1},{6,2},{7,3},{8,12},{9,13},{10,... | collective-permute-start | bytes 98312 | tf_op jit(solution)/shard_map/ppermute | solution.py:67
  9.4 1.0 source.1.inj
  11.7 1.5 %collective-permute-start.5 = (f32[2,128,256]{2,1,0:T(8,128)S(1)}, f32[2,128,256]{2,1,0:T(8,128)S(1)}, u32[]{:S(2)}, u32[]{:S(2)}) collective-permute-start(f32[2,128,256]{2,1,0:T(8,128)S(1)} %get-tuple-element.163), channel_id=1, source_target_pairs={{0,16},{1,4},{2,18},{3,6},{4,1},{5,8},{6,3},{7,10},{8,5},{9,12},{1... | collective-permute-start | bytes 786440 | tf_op jit(solution)/shard_map/ppermute | solution.py:67
  13.2 2.4 %collective-permute-start.7 = (f32[8,8,128]{2,1,0:T(8,128)S(1)}, f32[8,8,128]{2,1,0:T(8,128)S(1)}, u32[]{:S(2)}, u32[]{:S(2)}) collective-permute-start(f32[8,8,128]{2,1,0:T(8,128)S(1)} %get-tuple-element.167), channel_id=1, source_target_pairs={{0,8},{1,9},{2,10},{3,11},{4,12},{5,13},{6,14},{7,15},{8,0},{9,1},... | collective-permute-start | bytes 98312 | tf_op jit(solution)/shard_map/ppermute | solution.py:67
  17.7 1.2 %collective-permute-start.10 = (f32[256,256]{1,0:T(8,128)S(1)}, f32[256,256]{1,0:T(8,128)S(1)}, u32[]{:S(2)}, u32[]{:S(2)}) collective-permute-start(f32[256,256]{1,0:T(8,128)S(1)} %bitcast.20), channel_id=1, source_target_pairs={{0,16},{1,2},{2,1},{3,19},{4,20},{5,6},{6,5},{7,23},{8,24},{9,10},... | collective-permute-start | bytes 786440 | tf_op jit(solution)/shard_map/ppermute | solution.py:67
  22.6 1.4 %forward_inner.7 = (f32[256,256]{1,0:T(8,128)S(1)}, f32[256,256]{1,0:T(8,128)S(1)}) custom-call(s32[16]{0:T(128)S(1)} %copy-done.8, f32[8,16]{1,0:T(8,128)S(1)} %copy-done.3, f32[256,256]{1,0:T(8,128)S(1)} %get-tuple-element.170.cur.prev.before.state, f32[256,256]{1,0:T(8,128)S(1)} %get-tuple-element.150.cur.prev.before, ...), custom_call_target="tpu_custom_call" | custom-call | flops 1000 | bytes 4321000 | tf_op jit(solution)/shard_map/forward_inner/pallas_call | solution.py:600
  24.0 2.4 %collective-permute-done.10.rest_1_ = f32[256,256]{1,0:T(8,128)S(1)} collective-permute-done((f32[256,256]{1,0:T(8,128)S(1)}, f32[256,256]{1,0:T(8,128)S(1)}, u32[]{:S(2)}, u32[]{:S(2)}) %collective-permute-start.10) | collective-permute-done | bytes 262176 | tf_op jit(solution)/shard_map/ppermute | solution.py:67
  27.0 0.9 collective-permute-start.13
  28.9 1.4 %forward_inner.8 = (f32[256,256]{1,0:T(8,128)S(1)}, f32[256,256]{1,0:T(8,128)S(1)}) custom-call(s32[16]{0:T(128)S(1)} %copy-done.8, f32[8,16]{1,0:T(8,128)S(1)} %copy-done.3, f32[256,256]{1,0:T(8,128)S(1)} %get-tuple-element.184.cur.prev.before.state, f32[256,256]{1,0:T(8,128)S(1)} %get-tuple-element.170.cur.prev.before.state, ...), custom_call_target="tpu_custom_call" | custom-call | flops 1000 | bytes 4321000 | tf_op jit(solution)/shard_map/forward_inner/pallas_call | solution.py:600
  30.3 1.9 %collective-permute-done.15.ym = f32[72,256]{1,0:T(8,128)S(1)} collective-permute-done((f32[72,256]{1,0:T(8,128)S(1)}, f32[72,256]{1,0:T(8,128)S(1)}, u32[]{:S(2)}, u32[]{:S(2)}) %collective-permute-start.15) | collective-permute-done | bytes 73760 | tf_op jit(solution)/shard_map/ppermute | solution.py:67
  32.8 1.3 %collective-permute-start.16 = (f32[2,128,256]{2,1,0:T(8,128)S(1)}, f32[2,128,256]{2,1,0:T(8,128)S(1)}, u32[]{:S(2)}, u32[]{:S(2)}) collective-permute-start(f32[2,128,256]{2,1,0:T(8,128)S(1)} %get-tuple-element.192), channel_id=1, source_target_pairs={{0,1},{1,0},{2,3},{3,2},{4,5},{5,4},{6,7},{7,6},{8,9},{9,8},{10,11... | collective-permute-start | bytes 786440 | tf_op jit(solution)/shard_map/ppermute | solution.py:67
  35.3 1.4 %forward_inner.9 = (f32[256,256]{1,0:T(8,128)S(1)}, f32[256,256]{1,0:T(8,128)S(1)}) custom-call(s32[16]{0:T(128)S(1)} %copy-done.8, f32[8,16]{1,0:T(8,128)S(1)} %copy-done.3, f32[256,256]{1,0:T(8,128)S(1)} %get-tuple-element.191.cur.prev.before.state, f32[256,256]{1,0:T(8,128)S(1)} %get-tuple-element.184.cur.prev.before.state, ...), custom_call_target="tpu_custom_call" | custom-call | flops 1000 | bytes 4321000 | tf_op jit(solution)/shard_map/forward_inner/pallas_call | solution.py:600
  36.7 1.1 collective-permute-done.18.ym.u_ym
  37.8 2.4 %collective-permute-done.17.zm.u_zm = f32[2,128,256]{2,1,0:T(8,128)S(1)} collective-permute-done((f32[2,128,256]{2,1,0:T(8,128)S(1)}, f32[2,128,256]{2,1,0:T(8,128)S(1)}, u32[]{:S(2)}, u32[]{:S(2)}) %collective-permute-start.17) | collective-permute-done | bytes 262176 | tf_op jit(solution)/shard_map/ppermute | solution.py:67
  41.9 1.4 %forward_inner.10 = (f32[256,256]{1,0:T(8,128)S(1)}, f32[256,256]{1,0:T(8,128)S(1)}) custom-call(s32[16]{0:T(128)S(1)} %copy-done.8, f32[8,16]{1,0:T(8,128)S(1)} %copy-done.3, f32[256,256]{1,0:T(8,128)S(1)} %get-tuple-element.196.cur.prev.before.state, f32[256,256]{1,0:T(8,128)S(1)} %get-tuple-element.191.cur.prev.before.state, ...), custom_call_target="tpu_custom_call" | custom-call | flops 1000 | bytes 4321000 | tf_op jit(solution)/shard_map/forward_inner/pallas_call | solution.py:600
  43.7 1.9 %collective-permute-done.20.zm = f32[128,256]{1,0:T(8,128)S(1)} collective-permute-done((f32[128,256]{1,0:T(8,128)S(1)}, f32[128,256]{1,0:T(8,128)S(1)}, u32[]{:S(2)}, u32[]{:S(2)}) %collective-permute-start.20) | collective-permute-done | bytes 131104 | tf_op jit(solution)/shard_map/ppermute | solution.py:67
  48.2 1.4 %forward_inner.11 = (f32[256,256]{1,0:T(8,128)S(1)}, f32[256,256]{1,0:T(8,128)S(1)}) custom-call(s32[16]{0:T(128)S(1)} %copy-done.8, f32[8,16]{1,0:T(8,128)S(1)} %copy-done.3, f32[256,256]{1,0:T(8,128)S(1)} %get-tuple-element.201.cur.prev.before.state, f32[256,256]{1,0:T(8,128)S(1)} %get-tuple-element.196.cur.prev.before.state, ...), custom_call_target="tpu_custom_call" | custom-call | flops 1000 | bytes 4321000 | tf_op jit(solution)/shard_map/forward_inner/pallas_call | solution.py:600
  50.0 1.0 collective-permute-done.23.zm
  53.3 1.4 %forward_inner.12 = (f32[256,256]{1,0:T(8,128)S(1)}, f32[256,256]{1,0:T(8,128)S(1)}) custom-call(s32[16]{0:T(128)S(1)} %copy-done.8, f32[8,16]{1,0:T(8,128)S(1)} %copy-done.3, f32[256,256]{1,0:T(8,128)S(1)} %get-tuple-element.208.cur.prev.rest_2_.state, f32[256,256]{1,0:T(8,128)S(1)} %get-tuple-element.201.cur.prev.before.state, ...), custom_call_target="tpu_custom_call" | custom-call | flops 1000 | bytes 4321000 | tf_op jit(solution)/shard_map/forward_inner/pallas_call | solution.py:600
  58.4 1.4 %forward_inner.13 = (f32[256,256]{1,0:T(8,128)S(1)}, f32[256,256]{1,0:T(8,128)S(1)}) custom-call(s32[16]{0:T(128)S(1)} %copy-done.8, f32[8,16]{1,0:T(8,128)S(1)} %copy-done.3, f32[256,256]{1,0:T(8,128)S(1)} %get-tuple-element.217.cur.state.rest_1_, f32[256,256]{1,0:T(8,128)S(1)} %get-tuple-element.208.cur.prev.rest_2_.state, ...), custom_call_target="tpu_custom_call" | custom-call | flops 1000 | bytes 4321000 | tf_op jit(solution)/shard_map/forward_inner/pallas_call | solution.py:600
  59.8 1.0 collective-permute-done.30.ym
  60.8 0.9 collective-permute-done.29.zm
  64.4 1.0 adjoint_inner.7
  65.5 1.3 %collective-permute-done.33.ym = f32[32,256]{1,0:T(8,128)S(1)} collective-permute-done((f32[32,256]{1,0:T(8,128)S(1)}, f32[32,256]{1,0:T(8,128)S(1)}, u32[]{:S(2)}, u32[]{:S(2)}) %collective-permute-start.33) | collective-permute-done | bytes 32800 | tf_op jit(solution)/shard_map/ppermute | solution.py:67
  69.8 1.0 adjoint_inner.8
  70.8 1.4 %collective-permute-done.36.ym = f32[32,256]{1,0:T(8,128)S(1)} collective-permute-done((f32[32,256]{1,0:T(8,128)S(1)}, f32[32,256]{1,0:T(8,128)S(1)}, u32[]{:S(2)}, u32[]{:S(2)}) %collective-permute-start.36) | collective-permute-done | bytes 32800 | tf_op jit(solution)/shard_map/ppermute | solution.py:67
  72.2 0.9 collective-permute-done.35.zm
  75.2 1.0 adjoint_inner.9
  76.2 1.4 %collective-permute-done.39.ym = f32[32,256]{1,0:T(8,128)S(1)} collective-permute-done((f32[32,256]{1,0:T(8,128)S(1)}, f32[32,256]{1,0:T(8,128)S(1)}, u32[]{:S(2)}, u32[]{:S(2)}) %collective-permute-start.39) | collective-permute-done | bytes 32800 | tf_op jit(solution)/shard_map/ppermute | solution.py:67
  80.6 1.0 adjoint_inner.10
  81.6 1.4 %collective-permute-done.42.ym = f32[32,256]{1,0:T(8,128)S(1)} collective-permute-done((f32[32,256]{1,0:T(8,128)S(1)}, f32[32,256]{1,0:T(8,128)S(1)}, u32[]{:S(2)}, u32[]{:S(2)}) %collective-permute-start.42) | collective-permute-done | bytes 32800 | tf_op jit(solution)/shard_map/ppermute | solution.py:67
  86.1 1.0 adjoint_inner.11
  87.1 1.4 %collective-permute-done.45.ym = f32[32,256]{1,0:T(8,128)S(1)} collective-permute-done((f32[32,256]{1,0:T(8,128)S(1)}, f32[32,256]{1,0:T(8,128)S(1)}, u32[]{:S(2)}, u32[]{:S(2)}) %collective-permute-start.45) | collective-permute-done | bytes 32800 | tf_op jit(solution)/shard_map/ppermute | solution.py:67
  91.5 1.0 adjoint_inner.12
  92.5 1.4 %collective-permute-done.48.ym = f32[32,256]{1,0:T(8,128)S(1)} collective-permute-done((f32[32,256]{1,0:T(8,128)S(1)}, f32[32,256]{1,0:T(8,128)S(1)}, u32[]{:S(2)}, u32[]{:S(2)}) %collective-permute-start.48) | collective-permute-done | bytes 32800 | tf_op jit(solution)/shard_map/ppermute | solution.py:67
  96.9 1.0 adjoint_inner.13
  97.9 1.4 %collective-permute-done.51.ym = f32[32,256]{1,0:T(8,128)S(1)} collective-permute-done((f32[32,256]{1,0:T(8,128)S(1)}, f32[32,256]{1,0:T(8,128)S(1)}, u32[]{:S(2)}, u32[]{:S(2)}) %collective-permute-start.51) | collective-permute-done | bytes 32800 | tf_op jit(solution)/shard_map/ppermute | solution.py:67
  100.7 1.0 collective-permute-start.54
  102.2 1.0 collective-permute-done.52.got
  103.2 1.4 %collective-permute-start.53 = (f32[2,64,128]{2,1,0:T(8,128)S(1)}, f32[2,64,128]{2,1,0:T(8,128)S(1)}, u32[]{:S(2)}, u32[]{:S(2)}) collective-permute-start(f32[2,64,128]{2,1,0:T(8,128)S(1)} %get-tuple-element.277), channel_id=1, source_target_pairs={{0,12},{1,14},{2,13},{3,15},{4,8},{5,10},{6,9},{7,11},{8,4},{9,6},... | collective-permute-start | bytes 196616 | tf_op jit(solution)/shard_map/ppermute | solution.py:67
  104.6 1.7 %collective-permute-start.55 = (f32[2,64,128]{2,1,0:T(8,128)S(1)}, f32[2,64,128]{2,1,0:T(8,128)S(1)}, u32[]{:S(2)}, u32[]{:S(2)}) collective-permute-start(f32[2,64,128]{2,1,0:T(8,128)S(1)} %get-tuple-element.281), channel_id=1, source_target_pairs={{0,8},{1,10},{2,9},{3,11},{4,12},{5,14},{6,13},{7,15},{8,0},{9,2},... | collective-permute-start | bytes 196616 | tf_op jit(solution)/shard_map/ppermute | solution.py:67
  106.3 2.1 %collective-permute-start.56 = (f32[2,64,128]{2,1,0:T(8,128)S(1)}, f32[2,64,128]{2,1,0:T(8,128)S(1)}, u32[]{:S(2)}, u32[]{:S(2)}) collective-permute-start(f32[2,64,128]{2,1,0:T(8,128)S(1)} %get-tuple-element.282), channel_id=1, source_target_pairs={{0,4},{1,6},{2,5},{3,7},{4,0},{5,2},{6,1},{7,3},{8,12},{9,14},{10,... | collective-permute-start | bytes 196616 | tf_op jit(solution)/shard_map/ppermute | solution.py:67
  108.4 2.9 %collective-permute-start.57 = (f32[2,64,128]{2,1,0:T(8,128)S(1)}, f32[2,64,128]{2,1,0:T(8,128)S(1)}, u32[]{:S(2)}, u32[]{:S(2)}) collective-permute-start(f32[2,64,128]{2,1,0:T(8,128)S(1)} %get-tuple-element.283), channel_id=1, source_target_pairs={{0,0},{1,2},{2,1},{3,3},{4,4},{5,6},{6,5},{7,7},{8,8},{9,10},{10,9... | collective-permute-start | bytes 196616 | tf_op jit(solution)/shard_map/ppermute | solution.py:67
  112.4 1.5 %collective-permute-done.57.refs_3_ = f32[2,64,128]{2,1,0:T(8,128)S(1)} collective-permute-done((f32[2,64,128]{2,1,0:T(8,128)S(1)}, f32[2,64,128]{2,1,0:T(8,128)S(1)}, u32[]{:S(2)}, u32[]{:S(2)}) %collective-permute-start.57) | collective-permute-done | bytes 65568 | tf_op jit(solution)/shard_map/ppermute | solution.py:67
  114.0 1.3 %filter.1 = f32[32,32,64]{2,1,0:T(8,128)} custom-call(f32[2,64,128]{2,1,0:T(8,128)S(1)} %collective-permute-done.53.refs_0_, f32[2,64,128]{2,1,0:T(8,128)S(1)} %collective-permute-done.55.refs_1_, f32[2,64,128]{2,1,0:T(8,128)S(1)} %collective-permute-done.56.refs_2_, f32[2,64,128]{2,1,0:T(8,128)S(1)} %collective-permute-done.57.refs_3_), custom_call_target="tpu_custom_call" | custom-call | flops 1000 | bytes 1000 | tf_op jit(solution)/shard_map/filter/pallas_call | solution.py:600
  (152 shorter events, 46.3 us)
Async XLA Ops:
  0.6 10.1 %collective-permute-start.2 = (f32[256,256]{1,0:T(8,128)}, f32[256,256]{1,0:T(8,128)S(1)}, u32[]{:S(2)}, u32[]{:S(2)}) collective-permute-start(f32[256,256]{1,0:T(8,128)} %bitcast.16), channel_id=1, source_target_pairs={{0,16},{1,2},{2,1},{3,19},{4,20},{5,6},{6,5},{7,23},{8,24},{9,10},... | collective-permute-start | bytes 786440 | tf_op jit(solution)/shard_map/ppermute | solution.py:67
  3.3 7.4 %collective-permute-start = (f32[256,256]{1,0:T(8,128)}, f32[256,256]{1,0:T(8,128)S(1)}, u32[]{:S(2)}, u32[]{:S(2)}) collective-permute-start(f32[256,256]{1,0:T(8,128)} %bitcast.14), channel_id=1, source_target_pairs={{0,16},{1,2},{2,1},{3,19},{4,20},{5,6},{6,5},{7,23},{8,24},{9,10},... | collective-permute-start | bytes 786440 | tf_op jit(solution)/shard_map/ppermute | solution.py:67
  4.6 13.2 %collective-permute-start.3 = (f32[2,256,256]{2,1,0:T(8,128)S(1)}, f32[2,256,256]{2,1,0:T(8,128)S(1)}, u32[]{:S(2)}, u32[]{:S(2)}) collective-permute-start(f32[2,256,256]{2,1,0:T(8,128)S(1)} %pad_maximum_fusion), channel_id=1, source_target_pairs={{0,16},{1,2},{2,1},{3,19},{4,20},{5,6},{6,5},{7,23},{8,24},{9,10},... | collective-permute-start | bytes 1572872 | tf_op jit(solution)/shard_map/ppermute | solution.py:67
  6.5 3.9 %collective-permute-start.1 = (f32[8,8,128]{2,1,0:T(8,128)S(1)}, f32[8,8,128]{2,1,0:T(8,128)S(1)}, u32[]{:S(2)}, u32[]{:S(2)}) collective-permute-start(f32[8,8,128]{2,1,0:T(8,128)S(1)} %get-tuple-element.147), channel_id=1, source_target_pairs={{0,4},{1,5},{2,6},{3,7},{4,0},{5,1},{6,2},{7,3},{8,12},{9,13},{10,... | collective-permute-start | bytes 98312 | tf_op jit(solution)/shard_map/ppermute | solution.py:67
  10.9 5.3 %collective-permute-start.4 = (f32[2,128,256]{2,1,0:T(8,128)S(1)}, f32[2,128,256]{2,1,0:T(8,128)S(1)}, u32[]{:S(2)}, u32[]{:S(2)}) collective-permute-start(f32[2,128,256]{2,1,0:T(8,128)S(1)} %get-tuple-element.154), channel_id=1, source_target_pairs={{0,1},{1,0},{2,3},{3,2},{4,5},{5,4},{6,7},{7,6},{8,9},{9,8},{10,11... | collective-permute-start | bytes 786440 | tf_op jit(solution)/shard_map/ppermute | solution.py:67
  11.7 7.9 %collective-permute-start.5 = (f32[2,128,256]{2,1,0:T(8,128)S(1)}, f32[2,128,256]{2,1,0:T(8,128)S(1)}, u32[]{:S(2)}, u32[]{:S(2)}) collective-permute-start(f32[2,128,256]{2,1,0:T(8,128)S(1)} %get-tuple-element.163), channel_id=1, source_target_pairs={{0,16},{1,4},{2,18},{3,6},{4,1},{5,8},{6,3},{7,10},{8,5},{9,12},{1... | collective-permute-start | bytes 786440 | tf_op jit(solution)/shard_map/ppermute | solution.py:67
  13.2 6.0 %collective-permute-start.7 = (f32[8,8,128]{2,1,0:T(8,128)S(1)}, f32[8,8,128]{2,1,0:T(8,128)S(1)}, u32[]{:S(2)}, u32[]{:S(2)}) collective-permute-start(f32[8,8,128]{2,1,0:T(8,128)S(1)} %get-tuple-element.167), channel_id=1, source_target_pairs={{0,8},{1,9},{2,10},{3,11},{4,12},{5,13},{6,14},{7,15},{8,0},{9,1},... | collective-permute-start | bytes 98312 | tf_op jit(solution)/shard_map/ppermute | solution.py:67
  15.6 4.1 %collective-permute-start.6 = (f32[2,32,256]{2,1,0:T(8,128)S(1)}, f32[2,32,256]{2,1,0:T(8,128)S(1)}, u32[]{:S(2)}, u32[]{:S(2)}) collective-permute-start(f32[2,32,256]{2,1,0:T(8,128)S(1)} %get-tuple-element.164), channel_id=1, source_target_pairs={{0,2},{1,3},{2,0},{3,1},{4,6},{5,7},{6,4},{7,5},{8,10},{9,11},{10,... | collective-permute-start | bytes 196616 | tf_op jit(solution)/shard_map/ppermute | solution.py:67
  17.2 6.9 %collective-permute-start.9 = (f32[256,256]{1,0:T(8,128)S(1)}, f32[256,256]{1,0:T(8,128)S(1)}, u32[]{:S(2)}, u32[]{:S(2)}) collective-permute-start(f32[256,256]{1,0:T(8,128)S(1)} %bitcast.18), channel_id=1, source_target_pairs={{0,16},{1,2},{2,1},{3,19},{4,20},{5,6},{6,5},{7,23},{8,24},{9,10},... | collective-permute-start | bytes 786440 | tf_op jit(solution)/shard_map/ppermute | solution.py:67
  17.7 8.7 %collective-permute-start.10 = (f32[256,256]{1,0:T(8,128)S(1)}, f32[256,256]{1,0:T(8,128)S(1)}, u32[]{:S(2)}, u32[]{:S(2)}) collective-permute-start(f32[256,256]{1,0:T(8,128)S(1)} %bitcast.20), channel_id=1, source_target_pairs={{0,16},{1,2},{2,1},{3,19},{4,20},{5,6},{6,5},{7,23},{8,24},{9,10},... | collective-permute-start | bytes 786440 | tf_op jit(solution)/shard_map/ppermute | solution.py:67
  20.1 2.5 %collective-permute-start.8 = (f32[168,256]{1,0:T(8,128)S(1)}, f32[168,256]{1,0:T(8,128)S(1)}, u32[]{:S(2)}, u32[]{:S(2)}) collective-permute-start(f32[168,256]{1,0:T(8,128)S(1)} %get-tuple-element.175), channel_id=1, source_target_pairs={{0,1},{1,0},{2,3},{3,2},{4,5},{5,4},{6,7},{7,6},{8,9},{9,8},{10,11... | collective-permute-start | bytes 516104 | tf_op jit(solution)/shard_map/ppermute | solution.py:67
  21.1 5.7 %collective-permute-start.11 = (f32[128,256]{1,0:T(8,128)S(1)}, f32[128,256]{1,0:T(8,128)S(1)}, u32[]{:S(2)}, u32[]{:S(2)}) collective-permute-start(f32[128,256]{1,0:T(8,128)S(1)} %get-tuple-element.181), channel_id=1, source_target_pairs={{0,16},{1,4},{2,18},{3,6},{4,1},{5,8},{6,3},{7,10},{8,5},{9,12},{1... | collective-permute-start | bytes 393224 | tf_op jit(solution)/shard_map/ppermute | solution.py:67
  22.0 4.8 %collective-permute-start.12 = (f32[32,256]{1,0:T(8,128)S(1)}, f32[32,256]{1,0:T(8,128)S(1)}, u32[]{:S(2)}, u32[]{:S(2)}) collective-permute-start(f32[32,256]{1,0:T(8,128)S(1)} %get-tuple-element.182), channel_id=1, source_target_pairs={{0,2},{1,3},{2,0},{3,1},{4,6},{5,7},{6,4},{7,5},{8,10},{9,11},{10,... | collective-permute-start | bytes 98312 | tf_op jit(solution)/shard_map/ppermute | solution.py:67
  27.0 1.9 %collective-permute-start.13 = (f32[128,256]{1,0:T(8,128)S(1)}, f32[128,256]{1,0:T(8,128)S(1)}, u32[]{:S(2)}, u32[]{:S(2)}) collective-permute-start(f32[128,256]{1,0:T(8,128)S(1)} %get-tuple-element.185), channel_id=1, source_target_pairs={{0,1},{1,0},{2,3},{3,2},{4,5},{5,4},{6,7},{7,6},{8,9},{9,8},{10,11... | collective-permute-start | bytes 393224 | tf_op jit(solution)/shard_map/ppermute | solution.py:67
  27.9 4.7 %collective-permute-start.14 = (f32[128,256]{1,0:T(8,128)S(1)}, f32[128,256]{1,0:T(8,128)S(1)}, u32[]{:S(2)}, u32[]{:S(2)}) collective-permute-start(f32[128,256]{1,0:T(8,128)S(1)} %get-tuple-element.187), channel_id=1, source_target_pairs={{0,16},{1,4},{2,18},{3,6},{4,1},{5,8},{6,3},{7,10},{8,5},{9,12},{1... | collective-permute-start | bytes 393224 | tf_op jit(solution)/shard_map/ppermute | solution.py:67
  28.7 3.5 %collective-permute-start.15 = (f32[72,256]{1,0:T(8,128)S(1)}, f32[72,256]{1,0:T(8,128)S(1)}, u32[]{:S(2)}, u32[]{:S(2)}) collective-permute-start(f32[72,256]{1,0:T(8,128)S(1)} %get-tuple-element.188), channel_id=1, source_target_pairs={{0,2},{1,3},{2,0},{3,1},{4,6},{5,7},{6,4},{7,5},{8,10},{9,11},{10,... | collective-permute-start | bytes 221192 | tf_op jit(solution)/shard_map/ppermute | solution.py:67
  32.8 2.5 %collective-permute-start.16 = (f32[2,128,256]{2,1,0:T(8,128)S(1)}, f32[2,128,256]{2,1,0:T(8,128)S(1)}, u32[]{:S(2)}, u32[]{:S(2)}) collective-permute-start(f32[2,128,256]{2,1,0:T(8,128)S(1)} %get-tuple-element.192), channel_id=1, source_target_pairs={{0,1},{1,0},{2,3},{3,2},{4,5},{5,4},{6,7},{7,6},{8,9},{9,8},{10,11... | collective-permute-start | bytes 786440 | tf_op jit(solution)/shard_map/ppermute | solution.py:67
  34.2 6.1 %collective-permute-start.17 = (f32[2,128,256]{2,1,0:T(8,128)S(1)}, f32[2,128,256]{2,1,0:T(8,128)S(1)}, u32[]{:S(2)}, u32[]{:S(2)}) collective-permute-start(f32[2,128,256]{2,1,0:T(8,128)S(1)} %get-tuple-element.194), channel_id=1, source_target_pairs={{0,16},{1,4},{2,18},{3,6},{4,1},{5,8},{6,3},{7,10},{8,5},{9,12},{1... | collective-permute-start | bytes 786440 | tf_op jit(solution)/shard_map/ppermute | solution.py:67
  34.4 3.4 %collective-permute-start.18 = (f32[2,32,256]{2,1,0:T(8,128)S(1)}, f32[2,32,256]{2,1,0:T(8,128)S(1)}, u32[]{:S(2)}, u32[]{:S(2)}) collective-permute-start(f32[2,32,256]{2,1,0:T(8,128)S(1)} %get-tuple-element.195), channel_id=1, source_target_pairs={{0,2},{1,3},{2,0},{3,1},{4,6},{5,7},{6,4},{7,5},{8,10},{9,11},{10,... | collective-permute-start | bytes 196616 | tf_op jit(solution)/shard_map/ppermute | solution.py:67
  40.9 4.7 %collective-permute-start.20 = (f32[128,256]{1,0:T(8,128)S(1)}, f32[128,256]{1,0:T(8,128)S(1)}, u32[]{:S(2)}, u32[]{:S(2)}) collective-permute-start(f32[128,256]{1,0:T(8,128)S(1)} %get-tuple-element.199), channel_id=1, source_target_pairs={{0,16},{1,4},{2,18},{3,6},{4,1},{5,8},{6,3},{7,10},{8,5},{9,12},{1... | collective-permute-start | bytes 393224 | tf_op jit(solution)/shard_map/ppermute | solution.py:67
  40.9 2.8 %collective-permute-start.21 = (f32[32,256]{1,0:T(8,128)S(1)}, f32[32,256]{1,0:T(8,128)S(1)}, u32[]{:S(2)}, u32[]{:S(2)}) collective-permute-start(f32[32,256]{1,0:T(8,128)S(1)} %get-tuple-element.200), channel_id=1, source_target_pairs={{0,2},{1,3},{2,0},{3,1},{4,6},{5,7},{6,4},{7,5},{8,10},{9,11},{10,... | collective-permute-start | bytes 98312 | tf_op jit(solution)/shard_map/ppermute | solution.py:67
  45.8 2.4 %collective-permute-start.22 = (f32[128,256]{1,0:T(8,128)S(1)}, f32[128,256]{1,0:T(8,128)S(1)}, u32[]{:S(2)}, u32[]{:S(2)}) collective-permute-start(f32[128,256]{1,0:T(8,128)S(1)} %get-tuple-element.202), channel_id=1, source_target_pairs={{0,1},{1,0},{2,3},{3,2},{4,5},{5,4},{6,7},{7,6},{8,9},{9,8},{10,11... | collective-permute-start | bytes 393224 | tf_op jit(solution)/shard_map/ppermute | solution.py:67
  46.3 4.7 %collective-permute-start.23 = (f32[128,256]{1,0:T(8,128)S(1)}, f32[128,256]{1,0:T(8,128)S(1)}, u32[]{:S(2)}, u32[]{:S(2)}) collective-permute-start(f32[128,256]{1,0:T(8,128)S(1)} %get-tuple-element.206), channel_id=1, source_target_pairs={{0,16},{1,4},{2,18},{3,6},{4,1},{5,8},{6,3},{7,10},{8,5},{9,12},{1... | collective-permute-start | bytes 393224 | tf_op jit(solution)/shard_map/ppermute | solution.py:67
  46.9 3.1 %collective-permute-start.24 = (f32[32,256]{1,0:T(8,128)S(1)}, f32[32,256]{1,0:T(8,128)S(1)}, u32[]{:S(2)}, u32[]{:S(2)}) collective-permute-start(f32[32,256]{1,0:T(8,128)S(1)} %get-tuple-element.207), channel_id=1, source_target_pairs={{0,2},{1,3},{2,0},{3,1},{4,6},{5,7},{6,4},{7,5},{8,10},{9,11},{10,... | collective-permute-start | bytes 98312 | tf_op jit(solution)/shard_map/ppermute | solution.py:67
  51.2 2.1 %collective-permute-start.25 = (f32[128,256]{1,0:T(8,128)S(1)}, f32[128,256]{1,0:T(8,128)S(1)}, u32[]{:S(2)}, u32[]{:S(2)}) collective-permute-start(f32[128,256]{1,0:T(8,128)S(1)} %get-tuple-element.209), channel_id=1, source_target_pairs={{0,1},{1,0},{2,3},{3,2},{4,5},{5,4},{6,7},{7,6},{8,9},{9,8},{10,11... | collective-permute-start | bytes 393224 | tf_op jit(solution)/shard_map/ppermute | solution.py:67
  51.7 4.7 %collective-permute-start.26 = (f32[128,256]{1,0:T(8,128)S(1)}, f32[128,256]{1,0:T(8,128)S(1)}, u32[]{:S(2)}, u32[]{:S(2)}) collective-permute-start(f32[128,256]{1,0:T(8,128)S(1)} %get-tuple-element.215), channel_id=1, source_target_pairs={{0,16},{1,4},{2,18},{3,6},{4,1},{5,8},{6,3},{7,10},{8,5},{9,12},{1... | collective-permute-start | bytes 393224 | tf_op jit(solution)/shard_map/ppermute | solution.py:67
  52.4 3.1 %collective-permute-start.27 = (f32[32,256]{1,0:T(8,128)S(1)}, f32[32,256]{1,0:T(8,128)S(1)}, u32[]{:S(2)}, u32[]{:S(2)}) collective-permute-start(f32[32,256]{1,0:T(8,128)S(1)} %get-tuple-element.216), channel_id=1, source_target_pairs={{0,2},{1,3},{2,0},{3,1},{4,6},{5,7},{6,4},{7,5},{8,10},{9,11},{10,... | collective-permute-start | bytes 98312 | tf_op jit(solution)/shard_map/ppermute | solution.py:67
  57.0 4.7 %collective-permute-start.29 = (f32[128,256]{1,0:T(8,128)S(1)}, f32[128,256]{1,0:T(8,128)S(1)}, u32[]{:S(2)}, u32[]{:S(2)}) collective-permute-start(f32[128,256]{1,0:T(8,128)S(1)} %get-tuple-element.220), channel_id=1, source_target_pairs={{0,16},{1,4},{2,18},{3,6},{4,1},{5,8},{6,3},{7,10},{8,5},{9,12},{1... | collective-permute-start | bytes 393224 | tf_op jit(solution)/shard_map/ppermute | solution.py:67
  57.7 3.1 %collective-permute-start.30 = (f32[32,256]{1,0:T(8,128)S(1)}, f32[32,256]{1,0:T(8,128)S(1)}, u32[]{:S(2)}, u32[]{:S(2)}) collective-permute-start(f32[32,256]{1,0:T(8,128)S(1)} %get-tuple-element.221), channel_id=1, source_target_pairs={{0,2},{1,3},{2,0},{3,1},{4,6},{5,7},{6,4},{7,5},{8,10},{9,11},{10,... | collective-permute-start | bytes 98312 | tf_op jit(solution)/shard_map/ppermute | solution.py:67
  63.0 4.7 %collective-permute-start.32 = (f32[128,256]{1,0:T(8,128)S(1)}, f32[128,256]{1,0:T(8,128)S(1)}, u32[]{:S(2)}, u32[]{:S(2)}) collective-permute-start(f32[128,256]{1,0:T(8,128)S(1)} %get-tuple-element.229), channel_id=1, source_target_pairs={{0,16},{1,4},{2,18},{3,6},{4,1},{5,8},{6,3},{7,10},{8,5},{9,12},{1... | collective-permute-start | bytes 393224 | tf_op jit(solution)/shard_map/ppermute | solution.py:67
  63.7 3.1 %collective-permute-start.33 = (f32[32,256]{1,0:T(8,128)S(1)}, f32[32,256]{1,0:T(8,128)S(1)}, u32[]{:S(2)}, u32[]{:S(2)}) collective-permute-start(f32[32,256]{1,0:T(8,128)S(1)} %get-tuple-element.230), channel_id=1, source_target_pairs={{0,2},{1,3},{2,0},{3,1},{4,6},{5,7},{6,4},{7,5},{8,10},{9,11},{10,... | collective-permute-start | bytes 98312 | tf_op jit(solution)/shard_map/ppermute | solution.py:67
  68.4 4.7 %collective-permute-start.35 = (f32[128,256]{1,0:T(8,128)S(1)}, f32[128,256]{1,0:T(8,128)S(1)}, u32[]{:S(2)}, u32[]{:S(2)}) collective-permute-start(f32[128,256]{1,0:T(8,128)S(1)} %get-tuple-element.236), channel_id=1, source_target_pairs={{0,16},{1,4},{2,18},{3,6},{4,1},{5,8},{6,3},{7,10},{8,5},{9,12},{1... | collective-permute-start | bytes 393224 | tf_op jit(solution)/shard_map/ppermute | solution.py:67
  69.1 3.1 %collective-permute-start.36 = (f32[32,256]{1,0:T(8,128)S(1)}, f32[32,256]{1,0:T(8,128)S(1)}, u32[]{:S(2)}, u32[]{:S(2)}) collective-permute-start(f32[32,256]{1,0:T(8,128)S(1)} %get-tuple-element.237), channel_id=1, source_target_pairs={{0,2},{1,3},{2,0},{3,1},{4,6},{5,7},{6,4},{7,5},{8,10},{9,11},{10,... | collective-permute-start | bytes 98312 | tf_op jit(solution)/shard_map/ppermute | solution.py:67
  73.8 4.7 %collective-permute-start.38 = (f32[128,256]{1,0:T(8,128)S(1)}, f32[128,256]{1,0:T(8,128)S(1)}, u32[]{:S(2)}, u32[]{:S(2)}) collective-permute-start(f32[128,256]{1,0:T(8,128)S(1)} %get-tuple-element.243), channel_id=1, source_target_pairs={{0,16},{1,4},{2,18},{3,6},{4,1},{5,8},{6,3},{7,10},{8,5},{9,12},{1... | collective-permute-start | bytes 393224 | tf_op jit(solution)/shard_map/ppermute | solution.py:67
  74.5 3.1 %collective-permute-start.39 = (f32[32,256]{1,0:T(8,128)S(1)}, f32[32,256]{1,0:T(8,128)S(1)}, u32[]{:S(2)}, u32[]{:S(2)}) collective-permute-start(f32[32,256]{1,0:T(8,128)S(1)} %get-tuple-element.244), channel_id=1, source_target_pairs={{0,2},{1,3},{2,0},{3,1},{4,6},{5,7},{6,4},{7,5},{8,10},{9,11},{10,... | collective-permute-start | bytes 98312 | tf_op jit(solution)/shard_map/ppermute | solution.py:67
  79.2 4.7 %collective-permute-start.41 = (f32[128,256]{1,0:T(8,128)S(1)}, f32[128,256]{1,0:T(8,128)S(1)}, u32[]{:S(2)}, u32[]{:S(2)}) collective-permute-start(f32[128,256]{1,0:T(8,128)S(1)} %get-tuple-element.250), channel_id=1, source_target_pairs={{0,16},{1,4},{2,18},{3,6},{4,1},{5,8},{6,3},{7,10},{8,5},{9,12},{1... | collective-permute-start | bytes 393224 | tf_op jit(solution)/shard_map/ppermute | solution.py:67
  79.9 3.1 %collective-permute-start.42 = (f32[32,256]{1,0:T(8,128)S(1)}, f32[32,256]{1,0:T(8,128)S(1)}, u32[]{:S(2)}, u32[]{:S(2)}) collective-permute-start(f32[32,256]{1,0:T(8,128)S(1)} %get-tuple-element.251), channel_id=1, source_target_pairs={{0,2},{1,3},{2,0},{3,1},{4,6},{5,7},{6,4},{7,5},{8,10},{9,11},{10,... | collective-permute-start | bytes 98312 | tf_op jit(solution)/shard_map/ppermute | solution.py:67
  84.8 4.7 %collective-permute-start.44 = (f32[128,256]{1,0:T(8,128)S(1)}, f32[128,256]{1,0:T(8,128)S(1)}, u32[]{:S(2)}, u32[]{:S(2)}) collective-permute-start(f32[128,256]{1,0:T(8,128)S(1)} %get-tuple-element.257), channel_id=1, source_target_pairs={{0,16},{1,4},{2,18},{3,6},{4,1},{5,8},{6,3},{7,10},{8,5},{9,12},{1... | collective-permute-start | bytes 393224 | tf_op jit(solution)/shard_map/ppermute | solution.py:67
  85.4 3.1 %collective-permute-start.45 = (f32[32,256]{1,0:T(8,128)S(1)}, f32[32,256]{1,0:T(8,128)S(1)}, u32[]{:S(2)}, u32[]{:S(2)}) collective-permute-start(f32[32,256]{1,0:T(8,128)S(1)} %get-tuple-element.258), channel_id=1, source_target_pairs={{0,2},{1,3},{2,0},{3,1},{4,6},{5,7},{6,4},{7,5},{8,10},{9,11},{10,... | collective-permute-start | bytes 98312 | tf_op jit(solution)/shard_map/ppermute | solution.py:67
  90.1 4.7 %collective-permute-start.47 = (f32[128,256]{1,0:T(8,128)S(1)}, f32[128,256]{1,0:T(8,128)S(1)}, u32[]{:S(2)}, u32[]{:S(2)}) collective-permute-start(f32[128,256]{1,0:T(8,128)S(1)} %get-tuple-element.264), channel_id=1, source_target_pairs={{0,16},{1,4},{2,18},{3,6},{4,1},{5,8},{6,3},{7,10},{8,5},{9,12},{1... | collective-permute-start | bytes 393224 | tf_op jit(solution)/shard_map/ppermute | solution.py:67
  90.8 3.1 %collective-permute-start.48 = (f32[32,256]{1,0:T(8,128)S(1)}, f32[32,256]{1,0:T(8,128)S(1)}, u32[]{:S(2)}, u32[]{:S(2)}) collective-permute-start(f32[32,256]{1,0:T(8,128)S(1)} %get-tuple-element.265), channel_id=1, source_target_pairs={{0,2},{1,3},{2,0},{3,1},{4,6},{5,7},{6,4},{7,5},{8,10},{9,11},{10,... | collective-permute-start | bytes 98312 | tf_op jit(solution)/shard_map/ppermute | solution.py:67
  95.5 4.7 %collective-permute-start.50 = (f32[128,256]{1,0:T(8,128)S(1)}, f32[128,256]{1,0:T(8,128)S(1)}, u32[]{:S(2)}, u32[]{:S(2)}) collective-permute-start(f32[128,256]{1,0:T(8,128)S(1)} %get-tuple-element.271), channel_id=1, source_target_pairs={{0,16},{1,4},{2,18},{3,6},{4,1},{5,8},{6,3},{7,10},{8,5},{9,12},{1... | collective-permute-start | bytes 393224 | tf_op jit(solution)/shard_map/ppermute | solution.py:67
  96.2 3.1 %collective-permute-start.51 = (f32[32,256]{1,0:T(8,128)S(1)}, f32[32,256]{1,0:T(8,128)S(1)}, u32[]{:S(2)}, u32[]{:S(2)}) collective-permute-start(f32[32,256]{1,0:T(8,128)S(1)} %get-tuple-element.272), channel_id=1, source_target_pairs={{0,2},{1,3},{2,0},{3,1},{4,6},{5,7},{6,4},{7,5},{8,10},{9,11},{10,... | collective-permute-start | bytes 98312 | tf_op jit(solution)/shard_map/ppermute | solution.py:67
  100.7 10.6 %collective-permute-start.54 = (f32[2,256,256]{2,1,0:T(8,128)S(1)}, f32[2,256,256]{2,1,0:T(8,128)S(1)}, u32[]{:S(2)}, u32[]{:S(2)}) collective-permute-start(f32[2,256,256]{2,1,0:T(8,128)S(1)} %get-tuple-element.278.own), channel_id=1, source_target_pairs={{0,16},{1,2},{2,1},{3,19},{4,20},{5,6},{6,5},{7,23},{8,24},{9,10},... | collective-permute-start | bytes 1572872 | tf_op jit(solution)/shard_map/ppermute | solution.py:67
  103.2 9.0 %collective-permute-start.53 = (f32[2,64,128]{2,1,0:T(8,128)S(1)}, f32[2,64,128]{2,1,0:T(8,128)S(1)}, u32[]{:S(2)}, u32[]{:S(2)}) collective-permute-start(f32[2,64,128]{2,1,0:T(8,128)S(1)} %get-tuple-element.277), channel_id=1, source_target_pairs={{0,12},{1,14},{2,13},{3,15},{4,8},{5,10},{6,9},{7,11},{8,4},{9,6},... | collective-permute-start | bytes 196616 | tf_op jit(solution)/shard_map/ppermute | solution.py:67
  104.6 7.9 %collective-permute-start.55 = (f32[2,64,128]{2,1,0:T(8,128)S(1)}, f32[2,64,128]{2,1,0:T(8,128)S(1)}, u32[]{:S(2)}, u32[]{:S(2)}) collective-permute-start(f32[2,64,128]{2,1,0:T(8,128)S(1)} %get-tuple-element.281), channel_id=1, source_target_pairs={{0,8},{1,10},{2,9},{3,11},{4,12},{5,14},{6,13},{7,15},{8,0},{9,2},... | collective-permute-start | bytes 196616 | tf_op jit(solution)/shard_map/ppermute | solution.py:67
  106.3 6.2 %collective-permute-start.56 = (f32[2,64,128]{2,1,0:T(8,128)S(1)}, f32[2,64,128]{2,1,0:T(8,128)S(1)}, u32[]{:S(2)}, u32[]{:S(2)}) collective-permute-start(f32[2,64,128]{2,1,0:T(8,128)S(1)} %get-tuple-element.282), channel_id=1, source_target_pairs={{0,4},{1,6},{2,5},{3,7},{4,0},{5,2},{6,1},{7,3},{8,12},{9,14},{10,... | collective-permute-start | bytes 196616 | tf_op jit(solution)/shard_map/ppermute | solution.py:67
  108.4 5.6 %collective-permute-start.57 = (f32[2,64,128]{2,1,0:T(8,128)S(1)}, f32[2,64,128]{2,1,0:T(8,128)S(1)}, u32[]{:S(2)}, u32[]{:S(2)}) collective-permute-start(f32[2,64,128]{2,1,0:T(8,128)S(1)} %get-tuple-element.283), channel_id=1, source_target_pairs={{0,0},{1,2},{2,1},{3,3},{4,4},{5,6},{6,5},{7,7},{8,8},{9,10},{10,9... | collective-permute-start | bytes 196616 | tf_op jit(solution)/shard_map/ppermute | solution.py:67
  (28 other events, 60.9 us)

commit v21 on v20

--- a/solution.py
+++ b/solution.py
@@ -656,9 +656,6 @@
     stacked = jnp.stack([velocity, fwd_before])
     got_model = send(stacked, swap_perm)
     full = nx * cols
-    inj, = call(functools.partial(source_kernel, 0, full), "source", [field], src_cell, wavelet,
-                weight=0.7, scalars=2)
-    got[0], inj = lax.optimization_barrier((got[0], inj))
     slots = subs * CAP
     entries, half_entries = shaped(subs, steps, 128), shaped(subs // 2, steps, 128)
     order = [*range(2, len(stages)), 0]
@@ -681,6 +678,8 @@
                                 [field, field] + [shaped(2, *r.shape) for r in rim],
                                 log_density, fwd_now, *got, far=2)
     zm, cm, ym = halo(*out)
+    inj, = call(functools.partial(source_kernel, 0, full), "source", [field], src_cell,
+                after(wavelet, density), weight=0.7, scalars=2)
     parts = call(first_inner_kernel, "first_inner", [field] * 7, density, p_now, cm,
                  near, deep, weight=1.3)
     got_adjoint = [send(after(v, parts[0]), swap_perm) for v in (adj_now, adj_before)]

time: 115 us -> 115 us (level)
  transfers between devices with their start and end apart: 58 -> 58, of which waited for: 35 -> 33; matrix products, arithmetic and copies ran while one was open for 1% -> 1% of each run, Pallas kernels for 18% -> 18%
where the time goes in v21:
time: 115 us
  starting transfers between devices  49 us (43%)
  waiting for transfers between devices  36 us (31%)
  Pallas kernels  26.8 us (23%)
  other arithmetic  1.26 us (1%)
  between operations  1.22 us (1%)
    ppermute x58, starting transfers between devices, send(): return lax.ppermute(value, ALL, pairs)  49 us
    ppermute x58, waiting for transfers between devices, send(): return lax.ppermute(value, ALL, pairs)  36 us
    pallas_call x42, Pallas kernels, call(): pl.pallas_call(functools.partial(kernel, Flags()), name=name, out_shape=o...  26.8 us
  transfers between devices with their start and end apart: 58, of which 33 were waited for; matrix products, arithmetic and copies ran while one was open for 1% of the time, Pallas kernels for 18%

profile of v21, /device:TPU:1, one launch (start us, length us, event | category | flops | bytes accessed | tf_op | source)
XLA Modules:
  0.0 115.3 jit_solution(7268185892057684980)
XLA Ops:
  0.6 2.7 %collective-permute-start.2 = (f32[256,256]{1,0:T(8,128)}, f32[256,256]{1,0:T(8,128)S(1)}, u32[]{:S(2)}, u32[]{:S(2)}) collective-permute-start(f32[256,256]{1,0:T(8,128)} %bitcast.16), channel_id=1, source_target_pairs={{0,16},{1,2},{2,1},{3,19},{4,20},{5,6},{6,5},{7,23},{8,24},{9,10},... | collective-permute-start | bytes 786440 | tf_op jit(solution)/shard_map/ppermute | solution.py:67
  3.4 1.1 pad_maximum_fusion
  4.6 1.7 %collective-permute-start.3 = (f32[2,256,256]{2,1,0:T(8,128)S(1)}, f32[2,256,256]{2,1,0:T(8,128)S(1)}, u32[]{:S(2)}, u32[]{:S(2)}) collective-permute-start(f32[2,256,256]{2,1,0:T(8,128)S(1)} %pad_maximum_fusion), channel_id=1, source_target_pairs={{0,16},{1,2},{2,1},{3,19},{4,20},{5,6},{6,5},{7,23},{8,24},{9,10},... | collective-permute-start | bytes 1572872 | tf_op jit(solution)/shard_map/ppermute | solution.py:67
  6.5 1.4 %collective-permute-start.1 = (f32[8,8,128]{2,1,0:T(8,128)S(1)}, f32[8,8,128]{2,1,0:T(8,128)S(1)}, u32[]{:S(2)}, u32[]{:S(2)}) collective-permute-start(f32[8,8,128]{2,1,0:T(8,128)S(1)} %get-tuple-element.145), channel_id=1, source_target_pairs={{0,4},{1,5},{2,6},{3,7},{4,0},{5,1},{6,2},{7,3},{8,12},{9,13},{10,... | collective-permute-start | bytes 98312 | tf_op jit(solution)/shard_map/ppermute | solution.py:67
  9.6 1.1 collective-permute-done.recv_a
  11.5 1.7 %collective-permute-start.5 = (f32[2,128,256]{2,1,0:T(8,128)S(1)}, f32[2,128,256]{2,1,0:T(8,128)S(1)}, u32[]{:S(2)}, u32[]{:S(2)}) collective-permute-start(f32[2,128,256]{2,1,0:T(8,128)S(1)} %get-tuple-element.161), channel_id=1, source_target_pairs={{0,16},{1,4},{2,18},{3,6},{4,1},{5,8},{6,3},{7,10},{8,5},{9,12},{1... | collective-permute-start | bytes 786440 | tf_op jit(solution)/shard_map/ppermute | solution.py:67
  13.2 2.4 %collective-permute-start.7 = (f32[8,8,128]{2,1,0:T(8,128)S(1)}, f32[8,8,128]{2,1,0:T(8,128)S(1)}, u32[]{:S(2)}, u32[]{:S(2)}) collective-permute-start(f32[8,8,128]{2,1,0:T(8,128)S(1)} %get-tuple-element.165), channel_id=1, source_target_pairs={{0,8},{1,9},{2,10},{3,11},{4,12},{5,13},{6,14},{7,15},{8,0},{9,1},... | collective-permute-start | bytes 98312 | tf_op jit(solution)/shard_map/ppermute | solution.py:67
  17.7 1.2 %collective-permute-start.10 = (f32[256,256]{1,0:T(8,128)S(1)}, f32[256,256]{1,0:T(8,128)S(1)}, u32[]{:S(2)}, u32[]{:S(2)}) collective-permute-start(f32[256,256]{1,0:T(8,128)S(1)} %bitcast.20), channel_id=1, source_target_pairs={{0,16},{1,2},{2,1},{3,19},{4,20},{5,6},{6,5},{7,23},{8,24},{9,10},... | collective-permute-start | bytes 786440 | tf_op jit(solution)/shard_map/ppermute | solution.py:67
  19.0 1.0 source.1.inj
  21.1 1.4 %collective-permute-start.11 = (f32[128,256]{1,0:T(8,128)S(1)}, f32[128,256]{1,0:T(8,128)S(1)}, u32[]{:S(2)}, u32[]{:S(2)}) collective-permute-start(f32[128,256]{1,0:T(8,128)S(1)} %get-tuple-element.179), channel_id=1, source_target_pairs={{0,16},{1,4},{2,18},{3,6},{4,1},{5,8},{6,3},{7,10},{8,5},{9,12},{1... | collective-permute-start | bytes 393224 | tf_op jit(solution)/shard_map/ppermute | solution.py:67
  23.0 1.4 %forward_inner.7 = (f32[256,256]{1,0:T(8,128)S(1)}, f32[256,256]{1,0:T(8,128)S(1)}) custom-call(s32[16]{0:T(128)S(1)} %copy-done.8, f32[8,16]{1,0:T(8,128)S(1)} %copy-done.3, f32[256,256]{1,0:T(8,128)S(1)} %get-tuple-element.168.cur.prev.before.state, f32[256,256]{1,0:T(8,128)S(1)} %get-tuple-element.148.cur.prev.before, ...), custom_call_target="tpu_custom_call" | custom-call | flops 1000 | bytes 4321000 | tf_op jit(solution)/shard_map/forward_inner/pallas_call | solution.py:600
  24.4 2.1 %collective-permute-done.10.rest_1_ = f32[256,256]{1,0:T(8,128)S(1)} collective-permute-done((f32[256,256]{1,0:T(8,128)S(1)}, f32[256,256]{1,0:T(8,128)S(1)}, u32[]{:S(2)}, u32[]{:S(2)}) %collective-permute-start.10) | collective-permute-done | bytes 262176 | tf_op jit(solution)/shard_map/ppermute | solution.py:67
  28.9 1.4 %forward_inner.8 = (f32[256,256]{1,0:T(8,128)S(1)}, f32[256,256]{1,0:T(8,128)S(1)}) custom-call(s32[16]{0:T(128)S(1)} %copy-done.8, f32[8,16]{1,0:T(8,128)S(1)} %copy-done.3, f32[256,256]{1,0:T(8,128)S(1)} %get-tuple-element.182.cur.prev.before.state, f32[256,256]{1,0:T(8,128)S(1)} %get-tuple-element.168.cur.prev.before.state, ...), custom_call_target="tpu_custom_call" | custom-call | flops 1000 | bytes 4321000 | tf_op jit(solution)/shard_map/forward_inner/pallas_call | solution.py:600
  30.3 1.9 %collective-permute-done.15.ym = f32[72,256]{1,0:T(8,128)S(1)} collective-permute-done((f32[72,256]{1,0:T(8,128)S(1)}, f32[72,256]{1,0:T(8,128)S(1)}, u32[]{:S(2)}, u32[]{:S(2)}) %collective-permute-start.15) | collective-permute-done | bytes 73760 | tf_op jit(solution)/shard_map/ppermute | solution.py:67
  32.8 1.3 %collective-permute-start.16 = (f32[2,128,256]{2,1,0:T(8,128)S(1)}, f32[2,128,256]{2,1,0:T(8,128)S(1)}, u32[]{:S(2)}, u32[]{:S(2)}) collective-permute-start(f32[2,128,256]{2,1,0:T(8,128)S(1)} %get-tuple-element.190), channel_id=1, source_target_pairs={{0,1},{1,0},{2,3},{3,2},{4,5},{5,4},{6,7},{7,6},{8,9},{9,8},{10,11... | collective-permute-start | bytes 786440 | tf_op jit(solution)/shard_map/ppermute | solution.py:67
  35.4 1.4 %forward_inner.9 = (f32[256,256]{1,0:T(8,128)S(1)}, f32[256,256]{1,0:T(8,128)S(1)}) custom-call(s32[16]{0:T(128)S(1)} %copy-done.8, f32[8,16]{1,0:T(8,128)S(1)} %copy-done.3, f32[256,256]{1,0:T(8,128)S(1)} %get-tuple-element.189.cur.prev.before.state, f32[256,256]{1,0:T(8,128)S(1)} %get-tuple-element.182.cur.prev.before.state, ...), custom_call_target="tpu_custom_call" | custom-call | flops 1000 | bytes 4321000 | tf_op jit(solution)/shard_map/forward_inner/pallas_call | solution.py:600
  36.8 2.0 %collective-permute-done.18.ym.u_ym = f32[2,32,256]{2,1,0:T(8,128)S(1)} collective-permute-done((f32[2,32,256]{2,1,0:T(8,128)S(1)}, f32[2,32,256]{2,1,0:T(8,128)S(1)}, u32[]{:S(2)}, u32[]{:S(2)}) %collective-permute-start.18) | collective-permute-done | bytes 65568 | tf_op jit(solution)/shard_map/ppermute | solution.py:67
  38.8 1.4 %collective-permute-done.17.zm.u_zm = f32[2,128,256]{2,1,0:T(8,128)S(1)} collective-permute-done((f32[2,128,256]{2,1,0:T(8,128)S(1)}, f32[2,128,256]{2,1,0:T(8,128)S(1)}, u32[]{:S(2)}, u32[]{:S(2)}) %collective-permute-start.17) | collective-permute-done | bytes 262176 | tf_op jit(solution)/shard_map/ppermute | solution.py:67
  41.9 1.4 %forward_inner.10 = (f32[256,256]{1,0:T(8,128)S(1)}, f32[256,256]{1,0:T(8,128)S(1)}) custom-call(s32[16]{0:T(128)S(1)} %copy-done.8, f32[8,16]{1,0:T(8,128)S(1)} %copy-done.3, f32[256,256]{1,0:T(8,128)S(1)} %get-tuple-element.194.cur.prev.before.state, f32[256,256]{1,0:T(8,128)S(1)} %get-tuple-element.189.cur.prev.before.state, ...), custom_call_target="tpu_custom_call" | custom-call | flops 1000 | bytes 4321000 | tf_op jit(solution)/shard_map/forward_inner/pallas_call | solution.py:600
  43.3 1.2 %collective-permute-done.21.ym = f32[32,256]{1,0:T(8,128)S(1)} collective-permute-done((f32[32,256]{1,0:T(8,128)S(1)}, f32[32,256]{1,0:T(8,128)S(1)}, u32[]{:S(2)}, u32[]{:S(2)}) %collective-permute-start.21) | collective-permute-done | bytes 32800 | tf_op jit(solution)/shard_map/ppermute | solution.py:67
  44.5 1.0 collective-permute-done.20.zm
  48.2 1.4 %forward_inner.11 = (f32[256,256]{1,0:T(8,128)S(1)}, f32[256,256]{1,0:T(8,128)S(1)}) custom-call(s32[16]{0:T(128)S(1)} %copy-done.8, f32[8,16]{1,0:T(8,128)S(1)} %copy-done.3, f32[256,256]{1,0:T(8,128)S(1)} %get-tuple-element.199.cur.prev.before.state, f32[256,256]{1,0:T(8,128)S(1)} %get-tuple-element.194.cur.prev.before.state, ...), custom_call_target="tpu_custom_call" | custom-call | flops 1000 | bytes 4321000 | tf_op jit(solution)/shard_map/forward_inner/pallas_call | solution.py:600
  50.0 1.0 collective-permute-done.23.zm
  53.3 1.4 %forward_inner.12 = (f32[256,256]{1,0:T(8,128)S(1)}, f32[256,256]{1,0:T(8,128)S(1)}) custom-call(s32[16]{0:T(128)S(1)} %copy-done.8, f32[8,16]{1,0:T(8,128)S(1)} %copy-done.3, f32[256,256]{1,0:T(8,128)S(1)} %get-tuple-element.206.cur.prev.rest_2_.state, f32[256,256]{1,0:T(8,128)S(1)} %get-tuple-element.199.cur.prev.before.state, ...), custom_call_target="tpu_custom_call" | custom-call | flops 1000 | bytes 4321000 | tf_op jit(solution)/shard_map/forward_inner/pallas_call | solution.py:600
  58.4 1.4 %forward_inner.13 = (f32[256,256]{1,0:T(8,128)S(1)}, f32[256,256]{1,0:T(8,128)S(1)}) custom-call(s32[16]{0:T(128)S(1)} %copy-done.8, f32[8,16]{1,0:T(8,128)S(1)} %copy-done.3, f32[256,256]{1,0:T(8,128)S(1)} %get-tuple-element.215.cur.state.rest_1_, f32[256,256]{1,0:T(8,128)S(1)} %get-tuple-element.206.cur.prev.rest_2_.state, ...), custom_call_target="tpu_custom_call" | custom-call | flops 1000 | bytes 4321000 | tf_op jit(solution)/shard_map/forward_inner/pallas_call | solution.py:600
  59.8 1.0 collective-permute-done.30.ym
  64.4 1.0 adjoint_inner.7
  65.5 1.3 %collective-permute-done.33.ym = f32[32,256]{1,0:T(8,128)S(1)} collective-permute-done((f32[32,256]{1,0:T(8,128)S(1)}, f32[32,256]{1,0:T(8,128)S(1)}, u32[]{:S(2)}, u32[]{:S(2)}) %collective-permute-start.33) | collective-permute-done | bytes 32800 | tf_op jit(solution)/shard_map/ppermute | solution.py:67
  69.8 1.0 adjoint_inner.8
  70.8 1.4 %collective-permute-done.36.ym = f32[32,256]{1,0:T(8,128)S(1)} collective-permute-done((f32[32,256]{1,0:T(8,128)S(1)}, f32[32,256]{1,0:T(8,128)S(1)}, u32[]{:S(2)}, u32[]{:S(2)}) %collective-permute-start.36) | collective-permute-done | bytes 32800 | tf_op jit(solution)/shard_map/ppermute | solution.py:67
  75.2 1.0 adjoint_inner.9
  76.2 1.4 %collective-permute-done.39.ym = f32[32,256]{1,0:T(8,128)S(1)} collective-permute-done((f32[32,256]{1,0:T(8,128)S(1)}, f32[32,256]{1,0:T(8,128)S(1)}, u32[]{:S(2)}, u32[]{:S(2)}) %collective-permute-start.39) | collective-permute-done | bytes 32800 | tf_op jit(solution)/shard_map/ppermute | solution.py:67
  80.6 1.0 adjoint_inner.10
  81.6 1.4 %collective-permute-done.42.ym = f32[32,256]{1,0:T(8,128)S(1)} collective-permute-done((f32[32,256]{1,0:T(8,128)S(1)}, f32[32,256]{1,0:T(8,128)S(1)}, u32[]{:S(2)}, u32[]{:S(2)}) %collective-permute-start.42) | collective-permute-done | bytes 32800 | tf_op jit(solution)/shard_map/ppermute | solution.py:67
  86.1 1.0 adjoint_inner.11
  87.1 1.4 %collective-permute-done.45.ym = f32[32,256]{1,0:T(8,128)S(1)} collective-permute-done((f32[32,256]{1,0:T(8,128)S(1)}, f32[32,256]{1,0:T(8,128)S(1)}, u32[]{:S(2)}, u32[]{:S(2)}) %collective-permute-start.45) | collective-permute-done | bytes 32800 | tf_op jit(solution)/shard_map/ppermute | solution.py:67
  91.5 1.0 adjoint_inner.12
  92.5 1.4 %collective-permute-done.48.ym = f32[32,256]{1,0:T(8,128)S(1)} collective-permute-done((f32[32,256]{1,0:T(8,128)S(1)}, f32[32,256]{1,0:T(8,128)S(1)}, u32[]{:S(2)}, u32[]{:S(2)}) %collective-permute-start.48) | collective-permute-done | bytes 32800 | tf_op jit(solution)/shard_map/ppermute | solution.py:67
  96.9 1.0 adjoint_inner.13
  97.9 1.4 %collective-permute-done.51.ym = f32[32,256]{1,0:T(8,128)S(1)} collective-permute-done((f32[32,256]{1,0:T(8,128)S(1)}, f32[32,256]{1,0:T(8,128)S(1)}, u32[]{:S(2)}, u32[]{:S(2)}) %collective-permute-start.51) | collective-permute-done | bytes 32800 | tf_op jit(solution)/shard_map/ppermute | solution.py:67
  100.7 1.0 collective-permute-start.54
  102.1 1.0 collective-permute-done.52.got
  103.1 1.4 %collective-permute-start.53 = (f32[2,64,128]{2,1,0:T(8,128)S(1)}, f32[2,64,128]{2,1,0:T(8,128)S(1)}, u32[]{:S(2)}, u32[]{:S(2)}) collective-permute-start(f32[2,64,128]{2,1,0:T(8,128)S(1)} %get-tuple-element.275), channel_id=1, source_target_pairs={{0,12},{1,14},{2,13},{3,15},{4,8},{5,10},{6,9},{7,11},{8,4},{9,6},... | collective-permute-start | bytes 196616 | tf_op jit(solution)/shard_map/ppermute | solution.py:67
  104.6 1.7 %collective-permute-start.55 = (f32[2,64,128]{2,1,0:T(8,128)S(1)}, f32[2,64,128]{2,1,0:T(8,128)S(1)}, u32[]{:S(2)}, u32[]{:S(2)}) collective-permute-start(f32[2,64,128]{2,1,0:T(8,128)S(1)} %get-tuple-element.279), channel_id=1, source_target_pairs={{0,8},{1,10},{2,9},{3,11},{4,12},{5,14},{6,13},{7,15},{8,0},{9,2},... | collective-permute-start | bytes 196616 | tf_op jit(solution)/shard_map/ppermute | solution.py:67
  106.3 2.1 %collective-permute-start.56 = (f32[2,64,128]{2,1,0:T(8,128)S(1)}, f32[2,64,128]{2,1,0:T(8,128)S(1)}, u32[]{:S(2)}, u32[]{:S(2)}) collective-permute-start(f32[2,64,128]{2,1,0:T(8,128)S(1)} %get-tuple-element.280), channel_id=1, source_target_pairs={{0,4},{1,6},{2,5},{3,7},{4,0},{5,2},{6,1},{7,3},{8,12},{9,14},{10,... | collective-permute-start | bytes 196616 | tf_op jit(solution)/shard_map/ppermute | solution.py:67
  108.4 2.9 %collective-permute-start.57 = (f32[2,64,128]{2,1,0:T(8,128)S(1)}, f32[2,64,128]{2,1,0:T(8,128)S(1)}, u32[]{:S(2)}, u32[]{:S(2)}) collective-permute-start(f32[2,64,128]{2,1,0:T(8,128)S(1)} %get-tuple-element.281), channel_id=1, source_target_pairs={{0,0},{1,2},{2,1},{3,3},{4,4},{5,6},{6,5},{7,7},{8,8},{9,10},{10,9... | collective-permute-start | bytes 196616 | tf_op jit(solution)/shard_map/ppermute | solution.py:67
  112.4 1.5 %collective-permute-done.57.refs_3_ = f32[2,64,128]{2,1,0:T(8,128)S(1)} collective-permute-done((f32[2,64,128]{2,1,0:T(8,128)S(1)}, f32[2,64,128]{2,1,0:T(8,128)S(1)}, u32[]{:S(2)}, u32[]{:S(2)}) %collective-permute-start.57) | collective-permute-done | bytes 65568 | tf_op jit(solution)/shard_map/ppermute | solution.py:67
  114.0 1.3 %filter.1 = f32[32,32,64]{2,1,0:T(8,128)} custom-call(f32[2,64,128]{2,1,0:T(8,128)S(1)} %collective-permute-done.53.refs_0_, f32[2,64,128]{2,1,0:T(8,128)S(1)} %collective-permute-done.55.refs_1_, f32[2,64,128]{2,1,0:T(8,128)S(1)} %collective-permute-done.56.refs_2_, f32[2,64,128]{2,1,0:T(8,128)S(1)} %collective-permute-done.57.refs_3_), custom_call_target="tpu_custom_call" | custom-call | flops 1000 | bytes 1000 | tf_op jit(solution)/shard_map/filter/pallas_call | solution.py:600
  (152 shorter events, 46.5 us)
Async XLA Ops:
  0.6 10.1 %collective-permute-start.2 = (f32[256,256]{1,0:T(8,128)}, f32[256,256]{1,0:T(8,128)S(1)}, u32[]{:S(2)}, u32[]{:S(2)}) collective-permute-start(f32[256,256]{1,0:T(8,128)} %bitcast.16), channel_id=1, source_target_pairs={{0,16},{1,2},{2,1},{3,19},{4,20},{5,6},{6,5},{7,23},{8,24},{9,10},... | collective-permute-start | bytes 786440 | tf_op jit(solution)/shard_map/ppermute | solution.py:67
  3.3 7.4 %collective-permute-start = (f32[256,256]{1,0:T(8,128)}, f32[256,256]{1,0:T(8,128)S(1)}, u32[]{:S(2)}, u32[]{:S(2)}) collective-permute-start(f32[256,256]{1,0:T(8,128)} %bitcast.14), channel_id=1, source_target_pairs={{0,16},{1,2},{2,1},{3,19},{4,20},{5,6},{6,5},{7,23},{8,24},{9,10},... | collective-permute-start | bytes 786440 | tf_op jit(solution)/shard_map/ppermute | solution.py:67
  4.6 13.2 %collective-permute-start.3 = (f32[2,256,256]{2,1,0:T(8,128)S(1)}, f32[2,256,256]{2,1,0:T(8,128)S(1)}, u32[]{:S(2)}, u32[]{:S(2)}) collective-permute-start(f32[2,256,256]{2,1,0:T(8,128)S(1)} %pad_maximum_fusion), channel_id=1, source_target_pairs={{0,16},{1,2},{2,1},{3,19},{4,20},{5,6},{6,5},{7,23},{8,24},{9,10},... | collective-permute-start | bytes 1572872 | tf_op jit(solution)/shard_map/ppermute | solution.py:67
  6.5 3.1 %collective-permute-start.1 = (f32[8,8,128]{2,1,0:T(8,128)S(1)}, f32[8,8,128]{2,1,0:T(8,128)S(1)}, u32[]{:S(2)}, u32[]{:S(2)}) collective-permute-start(f32[8,8,128]{2,1,0:T(8,128)S(1)} %get-tuple-element.145), channel_id=1, source_target_pairs={{0,4},{1,5},{2,6},{3,7},{4,0},{5,1},{6,2},{7,3},{8,12},{9,13},{10,... | collective-permute-start | bytes 98312 | tf_op jit(solution)/shard_map/ppermute | solution.py:67
  10.9 5.3 %collective-permute-start.4 = (f32[2,128,256]{2,1,0:T(8,128)S(1)}, f32[2,128,256]{2,1,0:T(8,128)S(1)}, u32[]{:S(2)}, u32[]{:S(2)}) collective-permute-start(f32[2,128,256]{2,1,0:T(8,128)S(1)} %get-tuple-element.152), channel_id=1, source_target_pairs={{0,1},{1,0},{2,3},{3,2},{4,5},{5,4},{6,7},{7,6},{8,9},{9,8},{10,11... | collective-permute-start | bytes 786440 | tf_op jit(solution)/shard_map/ppermute | solution.py:67
  11.5 8.7 %collective-permute-start.5 = (f32[2,128,256]{2,1,0:T(8,128)S(1)}, f32[2,128,256]{2,1,0:T(8,128)S(1)}, u32[]{:S(2)}, u32[]{:S(2)}) collective-permute-start(f32[2,128,256]{2,1,0:T(8,128)S(1)} %get-tuple-element.161), channel_id=1, source_target_pairs={{0,16},{1,4},{2,18},{3,6},{4,1},{5,8},{6,3},{7,10},{8,5},{9,12},{1... | collective-permute-start | bytes 786440 | tf_op jit(solution)/shard_map/ppermute | solution.py:67
  13.2 7.0 %collective-permute-start.7 = (f32[8,8,128]{2,1,0:T(8,128)S(1)}, f32[8,8,128]{2,1,0:T(8,128)S(1)}, u32[]{:S(2)}, u32[]{:S(2)}) collective-permute-start(f32[8,8,128]{2,1,0:T(8,128)S(1)} %get-tuple-element.165), channel_id=1, source_target_pairs={{0,8},{1,9},{2,10},{3,11},{4,12},{5,13},{6,14},{7,15},{8,0},{9,1},... | collective-permute-start | bytes 98312 | tf_op jit(solution)/shard_map/ppermute | solution.py:67
  15.6 4.6 %collective-permute-start.6 = (f32[2,32,256]{2,1,0:T(8,128)S(1)}, f32[2,32,256]{2,1,0:T(8,128)S(1)}, u32[]{:S(2)}, u32[]{:S(2)}) collective-permute-start(f32[2,32,256]{2,1,0:T(8,128)S(1)} %get-tuple-element.162), channel_id=1, source_target_pairs={{0,2},{1,3},{2,0},{3,1},{4,6},{5,7},{6,4},{7,5},{8,10},{9,11},{10,... | collective-permute-start | bytes 196616 | tf_op jit(solution)/shard_map/ppermute | solution.py:67
  17.2 7.2 %collective-permute-start.9 = (f32[256,256]{1,0:T(8,128)S(1)}, f32[256,256]{1,0:T(8,128)S(1)}, u32[]{:S(2)}, u32[]{:S(2)}) collective-permute-start(f32[256,256]{1,0:T(8,128)S(1)} %bitcast.18), channel_id=1, source_target_pairs={{0,16},{1,2},{2,1},{3,19},{4,20},{5,6},{6,5},{7,23},{8,24},{9,10},... | collective-permute-start | bytes 786440 | tf_op jit(solution)/shard_map/ppermute | solution.py:67
  17.7 8.7 %collective-permute-start.10 = (f32[256,256]{1,0:T(8,128)S(1)}, f32[256,256]{1,0:T(8,128)S(1)}, u32[]{:S(2)}, u32[]{:S(2)}) collective-permute-start(f32[256,256]{1,0:T(8,128)S(1)} %bitcast.20), channel_id=1, source_target_pairs={{0,16},{1,2},{2,1},{3,19},{4,20},{5,6},{6,5},{7,23},{8,24},{9,10},... | collective-permute-start | bytes 786440 | tf_op jit(solution)/shard_map/ppermute | solution.py:67
  20.7 2.2 %collective-permute-start.8 = (f32[168,256]{1,0:T(8,128)S(1)}, f32[168,256]{1,0:T(8,128)S(1)}, u32[]{:S(2)}, u32[]{:S(2)}) collective-permute-start(f32[168,256]{1,0:T(8,128)S(1)} %get-tuple-element.173), channel_id=1, source_target_pairs={{0,1},{1,0},{2,3},{3,2},{4,5},{5,4},{6,7},{7,6},{8,9},{9,8},{10,11... | collective-permute-start | bytes 516104 | tf_op jit(solution)/shard_map/ppermute | solution.py:67
  21.1 5.7 %collective-permute-start.11 = (f32[128,256]{1,0:T(8,128)S(1)}, f32[128,256]{1,0:T(8,128)S(1)}, u32[]{:S(2)}, u32[]{:S(2)}) collective-permute-start(f32[128,256]{1,0:T(8,128)S(1)} %get-tuple-element.179), channel_id=1, source_target_pairs={{0,16},{1,4},{2,18},{3,6},{4,1},{5,8},{6,3},{7,10},{8,5},{9,12},{1... | collective-permute-start | bytes 393224 | tf_op jit(solution)/shard_map/ppermute | solution.py:67
  22.4 4.3 %collective-permute-start.12 = (f32[32,256]{1,0:T(8,128)S(1)}, f32[32,256]{1,0:T(8,128)S(1)}, u32[]{:S(2)}, u32[]{:S(2)}) collective-permute-start(f32[32,256]{1,0:T(8,128)S(1)} %get-tuple-element.180), channel_id=1, source_target_pairs={{0,2},{1,3},{2,0},{3,1},{4,6},{5,7},{6,4},{7,5},{8,10},{9,11},{10,... | collective-permute-start | bytes 98312 | tf_op jit(solution)/shard_map/ppermute | solution.py:67
  27.0 1.9 %collective-permute-start.13 = (f32[128,256]{1,0:T(8,128)S(1)}, f32[128,256]{1,0:T(8,128)S(1)}, u32[]{:S(2)}, u32[]{:S(2)}) collective-permute-start(f32[128,256]{1,0:T(8,128)S(1)} %get-tuple-element.183), channel_id=1, source_target_pairs={{0,1},{1,0},{2,3},{3,2},{4,5},{5,4},{6,7},{7,6},{8,9},{9,8},{10,11... | collective-permute-start | bytes 393224 | tf_op jit(solution)/shard_map/ppermute | solution.py:67
  27.9 4.7 %collective-permute-start.14 = (f32[128,256]{1,0:T(8,128)S(1)}, f32[128,256]{1,0:T(8,128)S(1)}, u32[]{:S(2)}, u32[]{:S(2)}) collective-permute-start(f32[128,256]{1,0:T(8,128)S(1)} %get-tuple-element.185), channel_id=1, source_target_pairs={{0,16},{1,4},{2,18},{3,6},{4,1},{5,8},{6,3},{7,10},{8,5},{9,12},{1... | collective-permute-start | bytes 393224 | tf_op jit(solution)/shard_map/ppermute | solution.py:67
  28.7 3.5 %collective-permute-start.15 = (f32[72,256]{1,0:T(8,128)S(1)}, f32[72,256]{1,0:T(8,128)S(1)}, u32[]{:S(2)}, u32[]{:S(2)}) collective-permute-start(f32[72,256]{1,0:T(8,128)S(1)} %get-tuple-element.186), channel_id=1, source_target_pairs={{0,2},{1,3},{2,0},{3,1},{4,6},{5,7},{6,4},{7,5},{8,10},{9,11},{10,... | collective-permute-start | bytes 221192 | tf_op jit(solution)/shard_map/ppermute | solution.py:67
  32.8 2.6 %collective-permute-start.16 = (f32[2,128,256]{2,1,0:T(8,128)S(1)}, f32[2,128,256]{2,1,0:T(8,128)S(1)}, u32[]{:S(2)}, u32[]{:S(2)}) collective-permute-start(f32[2,128,256]{2,1,0:T(8,128)S(1)} %get-tuple-element.190), channel_id=1, source_target_pairs={{0,1},{1,0},{2,3},{3,2},{4,5},{5,4},{6,7},{7,6},{8,9},{9,8},{10,11... | collective-permute-start | bytes 786440 | tf_op jit(solution)/shard_map/ppermute | solution.py:67
  34.2 6.1 %collective-permute-start.17 = (f32[2,128,256]{2,1,0:T(8,128)S(1)}, f32[2,128,256]{2,1,0:T(8,128)S(1)}, u32[]{:S(2)}, u32[]{:S(2)}) collective-permute-start(f32[2,128,256]{2,1,0:T(8,128)S(1)} %get-tuple-element.192), channel_id=1, source_target_pairs={{0,16},{1,4},{2,18},{3,6},{4,1},{5,8},{6,3},{7,10},{8,5},{9,12},{1... | collective-permute-start | bytes 786440 | tf_op jit(solution)/shard_map/ppermute | solution.py:67
  35.0 3.8 %collective-permute-start.18 = (f32[2,32,256]{2,1,0:T(8,128)S(1)}, f32[2,32,256]{2,1,0:T(8,128)S(1)}, u32[]{:S(2)}, u32[]{:S(2)}) collective-permute-start(f32[2,32,256]{2,1,0:T(8,128)S(1)} %get-tuple-element.193), channel_id=1, source_target_pairs={{0,2},{1,3},{2,0},{3,1},{4,6},{5,7},{6,4},{7,5},{8,10},{9,11},{10,... | collective-permute-start | bytes 196616 | tf_op jit(solution)/shard_map/ppermute | solution.py:67
  40.9 4.7 %collective-permute-start.20 = (f32[128,256]{1,0:T(8,128)S(1)}, f32[128,256]{1,0:T(8,128)S(1)}, u32[]{:S(2)}, u32[]{:S(2)}) collective-permute-start(f32[128,256]{1,0:T(8,128)S(1)} %get-tuple-element.197), channel_id=1, source_target_pairs={{0,16},{1,4},{2,18},{3,6},{4,1},{5,8},{6,3},{7,10},{8,5},{9,12},{1... | collective-permute-start | bytes 393224 | tf_op jit(solution)/shard_map/ppermute | solution.py:67
  41.5 3.1 %collective-permute-start.21 = (f32[32,256]{1,0:T(8,128)S(1)}, f32[32,256]{1,0:T(8,128)S(1)}, u32[]{:S(2)}, u32[]{:S(2)}) collective-permute-start(f32[32,256]{1,0:T(8,128)S(1)} %get-tuple-element.198), channel_id=1, source_target_pairs={{0,2},{1,3},{2,0},{3,1},{4,6},{5,7},{6,4},{7,5},{8,10},{9,11},{10,... | collective-permute-start | bytes 98312 | tf_op jit(solution)/shard_map/ppermute | solution.py:67
  45.8 2.4 %collective-permute-start.22 = (f32[128,256]{1,0:T(8,128)S(1)}, f32[128,256]{1,0:T(8,128)S(1)}, u32[]{:S(2)}, u32[]{:S(2)}) collective-permute-start(f32[128,256]{1,0:T(8,128)S(1)} %get-tuple-element.200), channel_id=1, source_target_pairs={{0,1},{1,0},{2,3},{3,2},{4,5},{5,4},{6,7},{7,6},{8,9},{9,8},{10,11... | collective-permute-start | bytes 393224 | tf_op jit(solution)/shard_map/ppermute | solution.py:67
  46.3 4.7 %collective-permute-start.23 = (f32[128,256]{1,0:T(8,128)S(1)}, f32[128,256]{1,0:T(8,128)S(1)}, u32[]{:S(2)}, u32[]{:S(2)}) collective-permute-start(f32[128,256]{1,0:T(8,128)S(1)} %get-tuple-element.204), channel_id=1, source_target_pairs={{0,16},{1,4},{2,18},{3,6},{4,1},{5,8},{6,3},{7,10},{8,5},{9,12},{1... | collective-permute-start | bytes 393224 | tf_op jit(solution)/shard_map/ppermute | solution.py:67
  46.9 3.1 %collective-permute-start.24 = (f32[32,256]{1,0:T(8,128)S(1)}, f32[32,256]{1,0:T(8,128)S(1)}, u32[]{:S(2)}, u32[]{:S(2)}) collective-permute-start(f32[32,256]{1,0:T(8,128)S(1)} %get-tuple-element.205), channel_id=1, source_target_pairs={{0,2},{1,3},{2,0},{3,1},{4,6},{5,7},{6,4},{7,5},{8,10},{9,11},{10,... | collective-permute-start | bytes 98312 | tf_op jit(solution)/shard_map/ppermute | solution.py:67
  51.2 2.1 %collective-permute-start.25 = (f32[128,256]{1,0:T(8,128)S(1)}, f32[128,256]{1,0:T(8,128)S(1)}, u32[]{:S(2)}, u32[]{:S(2)}) collective-permute-start(f32[128,256]{1,0:T(8,128)S(1)} %get-tuple-element.207), channel_id=1, source_target_pairs={{0,1},{1,0},{2,3},{3,2},{4,5},{5,4},{6,7},{7,6},{8,9},{9,8},{10,11... | collective-permute-start | bytes 393224 | tf_op jit(solution)/shard_map/ppermute | solution.py:67
  51.6 4.7 %collective-permute-start.26 = (f32[128,256]{1,0:T(8,128)S(1)}, f32[128,256]{1,0:T(8,128)S(1)}, u32[]{:S(2)}, u32[]{:S(2)}) collective-permute-start(f32[128,256]{1,0:T(8,128)S(1)} %get-tuple-element.213), channel_id=1, source_target_pairs={{0,16},{1,4},{2,18},{3,6},{4,1},{5,8},{6,3},{7,10},{8,5},{9,12},{1... | collective-permute-start | bytes 393224 | tf_op jit(solution)/shard_map/ppermute | solution.py:67
  52.3 3.1 %collective-permute-start.27 = (f32[32,256]{1,0:T(8,128)S(1)}, f32[32,256]{1,0:T(8,128)S(1)}, u32[]{:S(2)}, u32[]{:S(2)}) collective-permute-start(f32[32,256]{1,0:T(8,128)S(1)} %get-tuple-element.214), channel_id=1, source_target_pairs={{0,2},{1,3},{2,0},{3,1},{4,6},{5,7},{6,4},{7,5},{8,10},{9,11},{10,... | collective-permute-start | bytes 98312 | tf_op jit(solution)/shard_map/ppermute | solution.py:67
  57.0 4.7 %collective-permute-start.29 = (f32[128,256]{1,0:T(8,128)S(1)}, f32[128,256]{1,0:T(8,128)S(1)}, u32[]{:S(2)}, u32[]{:S(2)}) collective-permute-start(f32[128,256]{1,0:T(8,128)S(1)} %get-tuple-element.218), channel_id=1, source_target_pairs={{0,16},{1,4},{2,18},{3,6},{4,1},{5,8},{6,3},{7,10},{8,5},{9,12},{1... | collective-permute-start | bytes 393224 | tf_op jit(solution)/shard_map/ppermute | solution.py:67
  57.7 3.1 %collective-permute-start.30 = (f32[32,256]{1,0:T(8,128)S(1)}, f32[32,256]{1,0:T(8,128)S(1)}, u32[]{:S(2)}, u32[]{:S(2)}) collective-permute-start(f32[32,256]{1,0:T(8,128)S(1)} %get-tuple-element.219), channel_id=1, source_target_pairs={{0,2},{1,3},{2,0},{3,1},{4,6},{5,7},{6,4},{7,5},{8,10},{9,11},{10,... | collective-permute-start | bytes 98312 | tf_op jit(solution)/shard_map/ppermute | solution.py:67
  63.0 4.7 %collective-permute-start.32 = (f32[128,256]{1,0:T(8,128)S(1)}, f32[128,256]{1,0:T(8,128)S(1)}, u32[]{:S(2)}, u32[]{:S(2)}) collective-permute-start(f32[128,256]{1,0:T(8,128)S(1)} %get-tuple-element.227), channel_id=1, source_target_pairs={{0,16},{1,4},{2,18},{3,6},{4,1},{5,8},{6,3},{7,10},{8,5},{9,12},{1... | collective-permute-start | bytes 393224 | tf_op jit(solution)/shard_map/ppermute | solution.py:67
  63.7 3.1 %collective-permute-start.33 = (f32[32,256]{1,0:T(8,128)S(1)}, f32[32,256]{1,0:T(8,128)S(1)}, u32[]{:S(2)}, u32[]{:S(2)}) collective-permute-start(f32[32,256]{1,0:T(8,128)S(1)} %get-tuple-element.228), channel_id=1, source_target_pairs={{0,2},{1,3},{2,0},{3,1},{4,6},{5,7},{6,4},{7,5},{8,10},{9,11},{10,... | collective-permute-start | bytes 98312 | tf_op jit(solution)/shard_map/ppermute | solution.py:67
  68.4 4.7 %collective-permute-start.35 = (f32[128,256]{1,0:T(8,128)S(1)}, f32[128,256]{1,0:T(8,128)S(1)}, u32[]{:S(2)}, u32[]{:S(2)}) collective-permute-start(f32[128,256]{1,0:T(8,128)S(1)} %get-tuple-element.234), channel_id=1, source_target_pairs={{0,16},{1,4},{2,18},{3,6},{4,1},{5,8},{6,3},{7,10},{8,5},{9,12},{1... | collective-permute-start | bytes 393224 | tf_op jit(solution)/shard_map/ppermute | solution.py:67
  69.1 3.1 %collective-permute-start.36 = (f32[32,256]{1,0:T(8,128)S(1)}, f32[32,256]{1,0:T(8,128)S(1)}, u32[]{:S(2)}, u32[]{:S(2)}) collective-permute-start(f32[32,256]{1,0:T(8,128)S(1)} %get-tuple-element.235), channel_id=1, source_target_pairs={{0,2},{1,3},{2,0},{3,1},{4,6},{5,7},{6,4},{7,5},{8,10},{9,11},{10,... | collective-permute-start | bytes 98312 | tf_op jit(solution)/shard_map/ppermute | solution.py:67
  73.8 4.7 %collective-permute-start.38 = (f32[128,256]{1,0:T(8,128)S(1)}, f32[128,256]{1,0:T(8,128)S(1)}, u32[]{:S(2)}, u32[]{:S(2)}) collective-permute-start(f32[128,256]{1,0:T(8,128)S(1)} %get-tuple-element.241), channel_id=1, source_target_pairs={{0,16},{1,4},{2,18},{3,6},{4,1},{5,8},{6,3},{7,10},{8,5},{9,12},{1... | collective-permute-start | bytes 393224 | tf_op jit(solution)/shard_map/ppermute | solution.py:67
  74.5 3.1 %collective-permute-start.39 = (f32[32,256]{1,0:T(8,128)S(1)}, f32[32,256]{1,0:T(8,128)S(1)}, u32[]{:S(2)}, u32[]{:S(2)}) collective-permute-start(f32[32,256]{1,0:T(8,128)S(1)} %get-tuple-element.242), channel_id=1, source_target_pairs={{0,2},{1,3},{2,0},{3,1},{4,6},{5,7},{6,4},{7,5},{8,10},{9,11},{10,... | collective-permute-start | bytes 98312 | tf_op jit(solution)/shard_map/ppermute | solution.py:67
  79.2 4.7 %collective-permute-start.41 = (f32[128,256]{1,0:T(8,128)S(1)}, f32[128,256]{1,0:T(8,128)S(1)}, u32[]{:S(2)}, u32[]{:S(2)}) collective-permute-start(f32[128,256]{1,0:T(8,128)S(1)} %get-tuple-element.248), channel_id=1, source_target_pairs={{0,16},{1,4},{2,18},{3,6},{4,1},{5,8},{6,3},{7,10},{8,5},{9,12},{1... | collective-permute-start | bytes 393224 | tf_op jit(solution)/shard_map/ppermute | solution.py:67
  79.9 3.1 %collective-permute-start.42 = (f32[32,256]{1,0:T(8,128)S(1)}, f32[32,256]{1,0:T(8,128)S(1)}, u32[]{:S(2)}, u32[]{:S(2)}) collective-permute-start(f32[32,256]{1,0:T(8,128)S(1)} %get-tuple-element.249), channel_id=1, source_target_pairs={{0,2},{1,3},{2,0},{3,1},{4,6},{5,7},{6,4},{7,5},{8,10},{9,11},{10,... | collective-permute-start | bytes 98312 | tf_op jit(solution)/shard_map/ppermute | solution.py:67
  84.7 4.7 %collective-permute-start.44 = (f32[128,256]{1,0:T(8,128)S(1)}, f32[128,256]{1,0:T(8,128)S(1)}, u32[]{:S(2)}, u32[]{:S(2)}) collective-permute-start(f32[128,256]{1,0:T(8,128)S(1)} %get-tuple-element.255), channel_id=1, source_target_pairs={{0,16},{1,4},{2,18},{3,6},{4,1},{5,8},{6,3},{7,10},{8,5},{9,12},{1... | collective-permute-start | bytes 393224 | tf_op jit(solution)/shard_map/ppermute | solution.py:67
  85.4 3.1 %collective-permute-start.45 = (f32[32,256]{1,0:T(8,128)S(1)}, f32[32,256]{1,0:T(8,128)S(1)}, u32[]{:S(2)}, u32[]{:S(2)}) collective-permute-start(f32[32,256]{1,0:T(8,128)S(1)} %get-tuple-element.256), channel_id=1, source_target_pairs={{0,2},{1,3},{2,0},{3,1},{4,6},{5,7},{6,4},{7,5},{8,10},{9,11},{10,... | collective-permute-start | bytes 98312 | tf_op jit(solution)/shard_map/ppermute | solution.py:67
  90.1 4.7 %collective-permute-start.47 = (f32[128,256]{1,0:T(8,128)S(1)}, f32[128,256]{1,0:T(8,128)S(1)}, u32[]{:S(2)}, u32[]{:S(2)}) collective-permute-start(f32[128,256]{1,0:T(8,128)S(1)} %get-tuple-element.262), channel_id=1, source_target_pairs={{0,16},{1,4},{2,18},{3,6},{4,1},{5,8},{6,3},{7,10},{8,5},{9,12},{1... | collective-permute-start | bytes 393224 | tf_op jit(solution)/shard_map/ppermute | solution.py:67
  90.8 3.1 %collective-permute-start.48 = (f32[32,256]{1,0:T(8,128)S(1)}, f32[32,256]{1,0:T(8,128)S(1)}, u32[]{:S(2)}, u32[]{:S(2)}) collective-permute-start(f32[32,256]{1,0:T(8,128)S(1)} %get-tuple-element.263), channel_id=1, source_target_pairs={{0,2},{1,3},{2,0},{3,1},{4,6},{5,7},{6,4},{7,5},{8,10},{9,11},{10,... | collective-permute-start | bytes 98312 | tf_op jit(solution)/shard_map/ppermute | solution.py:67
  95.5 4.7 %collective-permute-start.50 = (f32[128,256]{1,0:T(8,128)S(1)}, f32[128,256]{1,0:T(8,128)S(1)}, u32[]{:S(2)}, u32[]{:S(2)}) collective-permute-start(f32[128,256]{1,0:T(8,128)S(1)} %get-tuple-element.269), channel_id=1, source_target_pairs={{0,16},{1,4},{2,18},{3,6},{4,1},{5,8},{6,3},{7,10},{8,5},{9,12},{1... | collective-permute-start | bytes 393224 | tf_op jit(solution)/shard_map/ppermute | solution.py:67
  96.2 3.1 %collective-permute-start.51 = (f32[32,256]{1,0:T(8,128)S(1)}, f32[32,256]{1,0:T(8,128)S(1)}, u32[]{:S(2)}, u32[]{:S(2)}) collective-permute-start(f32[32,256]{1,0:T(8,128)S(1)} %get-tuple-element.270), channel_id=1, source_target_pairs={{0,2},{1,3},{2,0},{3,1},{4,6},{5,7},{6,4},{7,5},{8,10},{9,11},{10,... | collective-permute-start | bytes 98312 | tf_op jit(solution)/shard_map/ppermute | solution.py:67
  100.7 10.6 %collective-permute-start.54 = (f32[2,256,256]{2,1,0:T(8,128)S(1)}, f32[2,256,256]{2,1,0:T(8,128)S(1)}, u32[]{:S(2)}, u32[]{:S(2)}) collective-permute-start(f32[2,256,256]{2,1,0:T(8,128)S(1)} %get-tuple-element.276.own), channel_id=1, source_target_pairs={{0,16},{1,2},{2,1},{3,19},{4,20},{5,6},{6,5},{7,23},{8,24},{9,10},... | collective-permute-start | bytes 1572872 | tf_op jit(solution)/shard_map/ppermute | solution.py:67
  103.1 9.0 %collective-permute-start.53 = (f32[2,64,128]{2,1,0:T(8,128)S(1)}, f32[2,64,128]{2,1,0:T(8,128)S(1)}, u32[]{:S(2)}, u32[]{:S(2)}) collective-permute-start(f32[2,64,128]{2,1,0:T(8,128)S(1)} %get-tuple-element.275), channel_id=1, source_target_pairs={{0,12},{1,14},{2,13},{3,15},{4,8},{5,10},{6,9},{7,11},{8,4},{9,6},... | collective-permute-start | bytes 196616 | tf_op jit(solution)/shard_map/ppermute | solution.py:67
  104.6 7.9 %collective-permute-start.55 = (f32[2,64,128]{2,1,0:T(8,128)S(1)}, f32[2,64,128]{2,1,0:T(8,128)S(1)}, u32[]{:S(2)}, u32[]{:S(2)}) collective-permute-start(f32[2,64,128]{2,1,0:T(8,128)S(1)} %get-tuple-element.279), channel_id=1, source_target_pairs={{0,8},{1,10},{2,9},{3,11},{4,12},{5,14},{6,13},{7,15},{8,0},{9,2},... | collective-permute-start | bytes 196616 | tf_op jit(solution)/shard_map/ppermute | solution.py:67
  106.3 6.2 %collective-permute-start.56 = (f32[2,64,128]{2,1,0:T(8,128)S(1)}, f32[2,64,128]{2,1,0:T(8,128)S(1)}, u32[]{:S(2)}, u32[]{:S(2)}) collective-permute-start(f32[2,64,128]{2,1,0:T(8,128)S(1)} %get-tuple-element.280), channel_id=1, source_target_pairs={{0,4},{1,6},{2,5},{3,7},{4,0},{5,2},{6,1},{7,3},{8,12},{9,14},{10,... | collective-permute-start | bytes 196616 | tf_op jit(solution)/shard_map/ppermute | solution.py:67
  108.4 5.6 %collective-permute-start.57 = (f32[2,64,128]{2,1,0:T(8,128)S(1)}, f32[2,64,128]{2,1,0:T(8,128)S(1)}, u32[]{:S(2)}, u32[]{:S(2)}) collective-permute-start(f32[2,64,128]{2,1,0:T(8,128)S(1)} %get-tuple-element.281), channel_id=1, source_target_pairs={{0,0},{1,2},{2,1},{3,3},{4,4},{5,6},{6,5},{7,7},{8,8},{9,10},{10,9... | collective-permute-start | bytes 196616 | tf_op jit(solution)/shard_map/ppermute | solution.py:67
  (28 other events, 67.8 us)
